TPU v7x, 32 devices: a whole 2x2x4 slice. The times are simulated.
32 devices in a mesh: shots: 2 (over y), bfly: 4 (over z), sub: 2 (over x), tr: 2 (over core).
Axes of the slice: x: 2, y: 2, z: 4, core: 2. Of those that a mesh axis runs over, the one named last changes fastest.
Arguments:
- traces: bfloat16 [16384, 1024], P(('shots', 'tr'), ('bfly', 'sub')), parts along dimension 0, may hold values from -6 to 6
- sampling: bfloat16 [8, 128, 128], P(('bfly', 'sub')), may hold values from -0.5 to 0.5
- skeleton: int32 [8, 3, 64], P(('bfly', 'sub')), may hold values from 0 to 127, as said below
- compress: bfloat16 [8, 3, 64, 128], P(('bfly', 'sub'))
- evaluation: bfloat16 [8, 128, 128], P(('bfly', 'sub')), may hold values from -0.5 to 0.5
Outputs:
- migrated: bfloat16 [16384, 1024], P(('shots', 'tr'), ('bfly', 'sub')), parts along dimension 0
There are 2 independent parts, one for each index of `shots`. A program takes and returns all parts, laid end to end along the dimension named above; an argument that names none is the same for every part. Nothing has to cross between parts.
Inputs may be any that keep to these rules, and one draw needn't show every extreme that they name: The 64 entries of skeleton[b, s, :] are distinct; an entry below 64 picks a coefficient of box b, one of 64 or more a coefficient of its partner.
All inputs are finite; a program needn't handle non-finite values.
Results may differ from a plain program's by a relative error of at most 0.007.
Values may be sent and summed in bfloat16 or wider, within the bound.
No kernel may reach another device: no remote copies, remote signals or barrier semaphores. Data moves between devices by JAX's collectives and lax.ppermute only.
A program may use at most 64 MiB of HBM per device.

v0:
```python
import jax
import jax.numpy as jnp
from jax import lax
from jax.sharding import PartitionSpec as P


def from_partner(block, axis, apart):
    count = lax.axis_size(axis)
    route = []
    for low in range(count):
        high = low | 1 << apart
        if high != low and high < count:
            route += [(low, high), (high, low)]
    return lax.ppermute(block, axis, route)


def picked_tables(compress, skeleton):
    rank_size = skeleton.shape[-1]
    places = lax.broadcasted_iota(jnp.int32, (1, 2 * rank_size, 1), 1)
    chooser = (skeleton[:, None, :] == places).astype(jnp.bfloat16)
    real_part = jnp.einsum(
        "lik,ljk->lij", chooser, compress[:, :, :rank_size], preferred_element_type=jnp.float32
    )
    imag_part = jnp.einsum(
        "lik,ljk->lij", chooser, compress[:, :, rank_size:], preferred_element_type=jnp.float32
    )
    return jnp.concatenate([real_part, imag_part], -1).astype(jnp.bfloat16)


def expand(table):
    rank_size = table.shape[-1] // 2
    upper = table[..., :rank_size, :]
    bottom = table[..., rank_size:, :]

    def turned(blocked):
        return jnp.concatenate([-blocked[..., rank_size:], blocked[..., :rank_size]], -1)

    return jnp.concatenate([upper, turned(upper), bottom, turned(bottom)], -2)


def advance(coeffs, partner, matrix):
    joined = jnp.concatenate([coeffs, partner], -1)
    return jnp.dot(joined, matrix, preferred_element_type=jnp.float32).astype(jnp.bfloat16)


def local(traces, sampling, skeleton, compress, evaluation):
    coeffs = jnp.dot(traces, sampling[0], preferred_element_type=jnp.float32).astype(jnp.bfloat16)
    low_bits = lax.axis_size("sub").bit_length() - 1
    high_bits = lax.axis_size("bfly").bit_length() - 1
    tables = picked_tables(compress[0][:low_bits], skeleton[0][:low_bits])
    for bit_index in range(low_bits):
        partner = from_partner(coeffs, "sub", bit_index)
        coeffs = advance(coeffs, partner, expand(tables[bit_index]))
    high_tables = picked_tables(compress[0][low_bits:], skeleton[0][low_bits:])
    for bit_index in range(high_bits):
        partner = from_partner(coeffs, "bfly", bit_index)
        coeffs = advance(coeffs, partner, expand(high_tables[bit_index]))
    return jnp.dot(coeffs, evaluation[0], preferred_element_type=jnp.float32).astype(jnp.bfloat16)


def solution(mesh):
    placed = (
        P(("shots", "tr"), ("bfly", "sub")),
        P(("bfly", "sub"), None, None),
        P(("bfly", "sub"), None, None),
        P(("bfly", "sub"), None, None, None),
        P(("bfly", "sub"), None, None),
    )
    return jax.shard_map(
        local,
        mesh=mesh,
        in_specs=placed,
        out_specs=P(("shots", "tr"), ("bfly", "sub")),
        check_vma=False,
    )
```

profile of v0, /device:TPU:0, one launch (start us, length us, event | category | flops | bytes accessed | tf_op | source)
XLA Modules:
  0.0 103.2 jit_solution(366852498234597074)
XLA Ops:
  0.0 0.0 copy-start
  0.0 0.0 copy-start.2
  0.0 0.0 copy-start.1
  0.0 1.2 %copy-done = bf16[4096,128]{1,0:T(8,128)(2,1)S(1)} copy-done((bf16[4096,128]{1,0:T(8,128)(2,1)S(1)}, bf16[4096,128]{1,0:T(8,128)(2,1)}, u32[]{:S(2)}) %copy-start) | copy-done | bytes 1048600
  1.2 1.2 %convolution_convert_fusion.4 = bf16[4096,128]{0,1:T(8,128)(2,1)S(1)} fusion(bf16[4096,128]{1,0:T(8,128)(2,1)S(1)} %copy-done, bf16[1,128,128]{2,1,0:T(8,128)(2,1)} %param.6), kind=kOutput, calls=%fused_computation.4 | convolution fusion | flops 134742016 | bytes 2129920 | tf_op jit(solution)/shard_map/dot_general | solution.py:47
  2.5 3.0 %collective-permute-start = (bf16[4096,128]{0,1:T(8,128)(2,1)S(1)}, bf16[4096,128]{0,1:T(8,128)(2,1)S(1)}, u32[]{:S(2)}, u32[]{:S(2)}) collective-permute-start(bf16[4096,128]{0,1:T(8,128)(2,1)S(1)} %convolution_convert_fusion.4), channel_id=1, source_target_pairs={{0,2},{2,0},{1,3},{3,1},{4,6},{6,4},{5,7},{7,5},{8,10},{10,8},{9,1... | collective-permute-start | bytes 3145736 | tf_op jit(solution)/shard_map/ppermute | solution.py:14
  5.5 0.0 copy-done.2
  5.5 0.0 copy-done.1
  5.5 0.1 fusion.11
  5.6 0.2 fusion.12
  5.8 0.1 maximum_bitcast_fusion
  5.9 22.7 %collective-permute-done = bf16[4096,128]{0,1:T(8,128)(2,1)S(1)} collective-permute-done((bf16[4096,128]{0,1:T(8,128)(2,1)S(1)}, bf16[4096,128]{0,1:T(8,128)(2,1)S(1)}, u32[]{:S(2)}, u32[]{:S(2)}) %collective-permute-start) | collective-permute-done | bytes 1048608 | tf_op jit(solution)/shard_map/ppermute | solution.py:14
  28.6 0.5 convolution_convert_fusion.1
  29.1 1.9 %collective-permute-start.1 = (bf16[4096,128]{0,1:T(8,128)(2,1)S(1)}, bf16[4096,128]{0,1:T(8,128)(2,1)S(1)}, u32[]{:S(2)}, u32[]{:S(2)}) collective-permute-start(bf16[4096,128]{0,1:T(8,128)(2,1)S(1)} %convolution_convert_fusion.1), channel_id=1, source_target_pairs={{0,4},{4,0},{8,12},{12,8},{1,5},{5,1},{9,13},{13,9},{2,6},{6,2},{1... | collective-permute-start | bytes 3145736 | tf_op jit(solution)/shard_map/ppermute | solution.py:14
  31.0 0.2 convolution_convert_fusion.5
  31.2 0.2 convolution_convert_fusion.6
  31.5 0.1 fusion.58
  31.6 22.0 %collective-permute-done.1 = bf16[4096,128]{0,1:T(8,128)(2,1)S(1)} collective-permute-done((bf16[4096,128]{0,1:T(8,128)(2,1)S(1)}, bf16[4096,128]{0,1:T(8,128)(2,1)S(1)}, u32[]{:S(2)}, u32[]{:S(2)}) %collective-permute-start.1) | collective-permute-done | bytes 1048608 | tf_op jit(solution)/shard_map/ppermute | solution.py:14
  53.5 0.0 copy-start.3
  53.5 0.5 convolution_convert_fusion
  54.0 2.6 %collective-permute-start.2 = (bf16[4096,128]{0,1:T(8,128)(2,1)S(1)}, bf16[4096,128]{0,1:T(8,128)(2,1)S(1)}, u32[]{:S(2)}, u32[]{:S(2)}) collective-permute-start(bf16[4096,128]{0,1:T(8,128)(2,1)S(1)} %convolution_convert_fusion), channel_id=1, source_target_pairs={{0,8},{8,0},{4,12},{12,4},{1,9},{9,1},{5,13},{13,5},{2,10},{10,2},... | collective-permute-start | bytes 3145736 | tf_op jit(solution)/shard_map/ppermute | solution.py:14
  56.6 44.3 %collective-permute-done.2 = bf16[4096,128]{0,1:T(8,128)(2,1)S(1)} collective-permute-done((bf16[4096,128]{0,1:T(8,128)(2,1)S(1)}, bf16[4096,128]{0,1:T(8,128)(2,1)S(1)}, u32[]{:S(2)}, u32[]{:S(2)}) %collective-permute-start.2) | collective-permute-done | bytes 1048608 | tf_op jit(solution)/shard_map/ppermute | solution.py:14
  100.9 0.0 copy-done.3
  100.9 2.3 %convolution_convert_fusion.2 = bf16[4096,128]{1,0:T(8,128)(2,1)} fusion(bf16[4096,128]{0,1:T(8,128)(2,1)S(1)} %collective-permute-done.2, bf16[4096,128]{0,1:T(8,128)(2,1)S(1)} %convolution_convert_fusion, bf16[64,64]{0,1:T(8,128)(2,1)S(1)} %get-tuple-element.12, bf16[64,64]{0,1:T(8,128)(2,1)S(1)} %get-tuple-element.11, ...), kind=kOutput, calls=%fused_computation.2 | convolution fusion | flops 408289280 | bytes 3244032 | tf_op jit(solution)/shard_map/dot_general | solution.py:58
  (7 shorter events, 0.0 us)
Async XLA Ops:
  0.0 1.2 %copy-start = (bf16[4096,128]{1,0:T(8,128)(2,1)S(1)}, bf16[4096,128]{1,0:T(8,128)(2,1)}, u32[]{:S(2)}) copy-start(bf16[4096,128]{1,0:T(8,128)(2,1)} %param.5) | copy-start | bytes 3145732
  0.0 5.5 %copy-start.2 = (s32[1,3,64]{2,0,1:T(1,128)S(1)}, s32[1,3,64]{2,0,1:T(1,128)}, u32[]{:S(2)}) copy-start(s32[1,3,64]{2,0,1:T(1,128)} %param.7) | copy-start | bytes 2308
  0.0 5.5 %copy-start.1 = (bf16[1,3,64,128]{3,2,1,0:T(8,128)(2,1)S(1)}, bf16[1,3,64,128]{3,2,1,0:T(8,128)(2,1)}, u32[]{:S(2)}) copy-start(bf16[1,3,64,128]{3,2,1,0:T(8,128)(2,1)} %param.8) | copy-start | bytes 147460
  2.5 26.2 %collective-permute-start = (bf16[4096,128]{0,1:T(8,128)(2,1)S(1)}, bf16[4096,128]{0,1:T(8,128)(2,1)S(1)}, u32[]{:S(2)}, u32[]{:S(2)}) collective-permute-start(bf16[4096,128]{0,1:T(8,128)(2,1)S(1)} %convolution_convert_fusion.4), channel_id=1, source_target_pairs={{0,2},{2,0},{1,3},{3,1},{4,6},{6,4},{5,7},{7,5},{8,10},{10,8},{9,1... | collective-permute-start | bytes 3145736 | tf_op jit(solution)/shard_map/ppermute | solution.py:14
  29.1 24.4 %collective-permute-start.1 = (bf16[4096,128]{0,1:T(8,128)(2,1)S(1)}, bf16[4096,128]{0,1:T(8,128)(2,1)S(1)}, u32[]{:S(2)}, u32[]{:S(2)}) collective-permute-start(bf16[4096,128]{0,1:T(8,128)(2,1)S(1)} %convolution_convert_fusion.1), channel_id=1, source_target_pairs={{0,4},{4,0},{8,12},{12,8},{1,5},{5,1},{9,13},{13,9},{2,6},{6,2},{1... | collective-permute-start | bytes 3145736 | tf_op jit(solution)/shard_map/ppermute | solution.py:14
  53.5 47.4 %copy-start.3 = (bf16[1,128,128]{2,1,0:T(8,128)(2,1)S(1)}, bf16[1,128,128]{2,1,0:T(8,128)(2,1)}, u32[]{:S(2)}) copy-start(bf16[1,128,128]{2,1,0:T(8,128)(2,1)} %param.9) | copy-start | bytes 98308
  54.0 46.9 %collective-permute-start.2 = (bf16[4096,128]{0,1:T(8,128)(2,1)S(1)}, bf16[4096,128]{0,1:T(8,128)(2,1)S(1)}, u32[]{:S(2)}, u32[]{:S(2)}) collective-permute-start(bf16[4096,128]{0,1:T(8,128)(2,1)S(1)} %convolution_convert_fusion), channel_id=1, source_target_pairs={{0,8},{8,0},{4,12},{12,4},{1,9},{9,1},{5,13},{13,5},{2,10},{10,2},... | collective-permute-start | bytes 3145736 | tf_op jit(solution)/shard_map/ppermute | solution.py:14
where the time goes:
time: 103 us
  waiting for transfers between devices  89 us (86%)
  starting transfers between devices  7.49 us (7%)
  matrix products  5.22 us (5%)
  local copies, waits for them, and re-layouts  1.24 us (1%)
    ppermute x3, waiting for transfers between devices, from_partner(): return lax.ppermute(block, axis, route)  89 us
    ppermute x3, starting transfers between devices, from_partner(): return lax.ppermute(block, axis, route)  7.49 us
    dot_general x1, matrix products, local(): jnp.dot(coeffs, evaluation[0], preferred_element_type=jnp.float32)  2.27 us
  transfers between devices with their start and end apart: 3, of which 3 were waited for; matrix products, arithmetic and copies ran while one was open for 1% of the time, Pallas kernels for 0%

commit v1 on v0

v1 whole, which is shorter than its diff:
```python
import jax
import jax.numpy as jnp
from jax import lax
from jax.sharding import PartitionSpec as P

PIECES = 4


def from_partner(block, axis, apart):
    count = lax.axis_size(axis)
    route = []
    for low in range(count):
        high = low | 1 << apart
        if high != low and high < count:
            route += [(low, high), (high, low)]
    return lax.ppermute(block, axis, route)


def level_matrices(compress, skeleton):
    rank = skeleton.shape[-1]
    places = lax.broadcasted_iota(jnp.int32, (1, 2 * rank, 1), 1)
    chooser = (skeleton[:, None, :] == places).astype(jnp.bfloat16)
    both = jnp.einsum(
        "lik,ljk->lij",
        chooser,
        jnp.concatenate([compress[:, :, :rank], compress[:, :, rank:]], 1),
        preferred_element_type=jnp.float32,
    ).astype(jnp.bfloat16)
    real, imag = both[..., :rank], both[..., rank:]
    turned = jnp.concatenate([-imag, real], -1)
    return jnp.concatenate(
        [both[:, :rank], turned[:, :rank], both[:, rank:], turned[:, rank:]], 1
    )


def advance(coeffs, partner, matrix):
    joined = jnp.concatenate([coeffs, partner], -1)
    return jnp.dot(joined, matrix, preferred_element_type=jnp.float32).astype(jnp.bfloat16)


def local(traces, sampling, skeleton, compress, evaluation):
    low_bits = lax.axis_size("sub").bit_length() - 1
    high_bits = lax.axis_size("bfly").bit_length() - 1
    hops = [("sub", bit) for bit in range(low_bits)] + [("bfly", bit) for bit in range(high_bits)]
    matrices = level_matrices(compress[0], skeleton[0])
    rows = traces.shape[0] // PIECES
    coeffs = {}
    done = [None] * PIECES
    for step in range(PIECES + len(hops)):
        for level in range(len(hops), -1, -1):
            piece = step - level
            if not 0 <= piece < PIECES:
                continue
            if level == 0:
                block = traces[piece * rows : (piece + 1) * rows]
                coeffs[piece] = jnp.dot(
                    block, sampling[0], preferred_element_type=jnp.float32
                ).astype(jnp.bfloat16)
            if level < len(hops):
                axis, bit = hops[level]
                partner = from_partner(coeffs[piece], axis, bit)
                coeffs[piece] = advance(coeffs[piece], partner, matrices[level])
            else:
                done[piece] = jnp.dot(
                    coeffs[piece], evaluation[0], preferred_element_type=jnp.float32
                ).astype(jnp.bfloat16)
    return jnp.concatenate(done, 0)


def solution(mesh):
    placed = (
        P(("shots", "tr"), ("bfly", "sub")),
        P(("bfly", "sub"), None, None),
        P(("bfly", "sub"), None, None),
        P(("bfly", "sub"), None, None, None),
        P(("bfly", "sub"), None, None),
    )
    return jax.shard_map(
        local,
        mesh=mesh,
        in_specs=placed,
        out_specs=P(("shots", "tr"), ("bfly", "sub")),
        check_vma=False,
    )
```

time: 103 us -> 79.5 us (0.77)
  waiting for transfers between devices: 89 us -> 49.1 us
  starting transfers between devices: 7.49 us -> 20.4 us
  matrix products: 5.22 us -> 7.5 us
  other arithmetic: 0.23 us -> 1.32 us
    ppermute x3 -> x12, waiting for transfers between devices: 89 us -> 49.1 us  [from_partner(): return lax.ppermute(block, axis, route)]
    ppermute x3 -> x12, starting transfers between devices: 7.49 us -> 20.4 us  [from_partner(): return lax.ppermute(block, axis, route)]
    concatenate x0 -> x3, other arithmetic: none -> 1.22 us  [the longest x1 1.04 us: local(): return jnp.concatenate(done, 0)]
    dot_general x2 -> x8, matrix products: 0.98 us -> 2.12 us  [advance(): jnp.dot(joined, matrix, preferred_element_type=jnp.float32)]
    dot_general x6 -> x9, matrix products: 4.24 us -> 5.37 us  [the longest x4 2.95 us: local(): jnp.dot(block, sampling[0], preferred_element_type=jnp.float32)]
  transfers between devices with their start and end apart: 3 -> 12, of which waited for: 3 -> 9; matrix products, arithmetic and copies ran while one was open for 1% -> 8% of each run, Pallas kernels for 0% -> 0%
where the time goes in v1:
time: 79.5 us; the launch traced here: 79.4 us
  waiting for transfers between devices  49.1 us (62%)
  starting transfers between devices  20.4 us (26%)
  matrix products  7.5 us (9%)
  other arithmetic  1.32 us (2%)
  local copies, waits for them, and re-layouts  0.91 us (1%)
    ppermute x12, waiting for transfers between devices, from_partner(): return lax.ppermute(block, axis, route)  49.1 us
    ppermute x12, starting transfers between devices, from_partner(): return lax.ppermute(block, axis, route)  20.4 us
    dot_general x4, matrix products, local(): jnp.dot(block, sampling[0], preferred_element_type=jnp.float32)  2.95 us
    dot_general x8, matrix products, advance(): jnp.dot(joined, matrix, preferred_element_type=jnp.float32)  2.12 us
    dot_general x4, matrix products, local(): jnp.dot(coeffs[piece], evaluation[0], preferred_element_type=jnp.float32)  2.11 us
  transfers between devices with their start and end apart: 12, of which 9 were waited for; matrix products, arithmetic and copies ran while one was open for 8% of the time, Pallas kernels for 0%

profile of v1, /device:TPU:0, one launch (start us, length us, event | category | flops | bytes accessed | tf_op | source)
XLA Modules:
  0.0 79.4 jit_solution(18201959591617054087)
XLA Ops:
  0.0 0.7 copy-done
  0.8 1.2 %convolution_convert_fusion.9 = bf16[1024,128]{0,1:T(8,128)(2,1)S(1)} fusion(bf16[4096,128]{1,0:T(8,128)(2,1)} %param.5, bf16[1,128,128]{2,1,0:T(8,128)(2,1)S(1)} %copy-done), kind=kOutput, calls=%fused_computation.9 | convolution fusion | flops 33685504 | bytes 557056 | tf_op jit(solution)/shard_map/dot_general | solution.py:56
  2.0 3.0 %collective-permute-start.6 = (bf16[1024,128]{0,1:T(8,128)(2,1)S(1)}, bf16[1024,128]{0,1:T(8,128)(2,1)S(1)}, u32[]{:S(2)}, u32[]{:S(2)}) collective-permute-start(bf16[1024,128]{0,1:T(8,128)(2,1)S(1)} %convolution_convert_fusion.9), channel_id=1, source_target_pairs={{0,2},{2,0},{1,3},{3,1},{4,6},{6,4},{5,7},{7,5},{8,10},{10,8},{9,1... | collective-permute-start | bytes 786440 | tf_op jit(solution)/shard_map/ppermute | solution.py:16
  5.0 1.2 %convolution_convert_fusion.4 = bf16[1024,128]{0,1:T(8,128)(2,1)S(1)} fusion(bf16[4096,128]{1,0:T(8,128)(2,1)} %param.5, bf16[1,128,128]{2,1,0:T(8,128)(2,1)S(1)} %copy-done), kind=kOutput, calls=%fused_computation.4 | convolution fusion | flops 33685504 | bytes 557056 | tf_op jit(solution)/shard_map/dot_general | solution.py:56
  6.3 0.3 convolution_convert_fusion.19
  6.6 2.1 %collective-permute-start = (bf16[1024,128]{0,1:T(8,128)(2,1)S(1)}, bf16[1024,128]{0,1:T(8,128)(2,1)S(1)}, u32[]{:S(2)}, u32[]{:S(2)}) collective-permute-start(bf16[1024,128]{0,1:T(8,128)(2,1)S(1)} %convolution_convert_fusion.19), channel_id=1, source_target_pairs={{0,2},{2,0},{1,3},{3,1},{4,6},{6,4},{5,7},{7,5},{8,10},{10,8},{9,1... | collective-permute-start | bytes 786440 | tf_op jit(solution)/shard_map/ppermute | solution.py:16
  9.2 0.3 convolution_convert_fusion.20
  9.8 2.3 %collective-permute-done.6 = bf16[1024,128]{0,1:T(8,128)(2,1)S(1)} collective-permute-done((bf16[1024,128]{0,1:T(8,128)(2,1)S(1)}, bf16[1024,128]{0,1:T(8,128)(2,1)S(1)}, u32[]{:S(2)}, u32[]{:S(2)}) %collective-permute-start.6) | collective-permute-done | bytes 262176 | tf_op jit(solution)/shard_map/ppermute | solution.py:16
  12.4 2.2 %collective-permute-start.7 = (bf16[1024,128]{0,1:T(8,128)(2,1)S(1)}, bf16[1024,128]{0,1:T(8,128)(2,1)S(1)}, u32[]{:S(2)}, u32[]{:S(2)}) collective-permute-start(bf16[1024,128]{0,1:T(8,128)(2,1)S(1)} %convolution_convert_fusion.8), channel_id=1, source_target_pairs={{0,4},{4,0},{8,12},{12,8},{1,5},{5,1},{9,13},{13,9},{2,6},{6,2},{1... | collective-permute-start | bytes 786440 | tf_op jit(solution)/shard_map/ppermute | solution.py:16
  14.6 3.1 %collective-permute-done.9 = bf16[1024,128]{0,1:T(8,128)(2,1)S(1)} collective-permute-done((bf16[1024,128]{0,1:T(8,128)(2,1)S(1)}, bf16[1024,128]{0,1:T(8,128)(2,1)S(1)}, u32[]{:S(2)}, u32[]{:S(2)}) %collective-permute-start.9) | collective-permute-done | bytes 262176 | tf_op jit(solution)/shard_map/ppermute | solution.py:16
  18.0 2.2 %collective-permute-start.10 = (bf16[1024,128]{0,1:T(8,128)(2,1)S(1)}, bf16[1024,128]{0,1:T(8,128)(2,1)S(1)}, u32[]{:S(2)}, u32[]{:S(2)}) collective-permute-start(bf16[1024,128]{0,1:T(8,128)(2,1)S(1)} %convolution_convert_fusion.3), channel_id=1, source_target_pairs={{0,4},{4,0},{8,12},{12,8},{1,5},{5,1},{9,13},{13,9},{2,6},{6,2},{1... | collective-permute-start | bytes 786440 | tf_op jit(solution)/shard_map/ppermute | solution.py:16
  20.2 3.1 %collective-permute-done = bf16[1024,128]{0,1:T(8,128)(2,1)S(1)} collective-permute-done((bf16[1024,128]{0,1:T(8,128)(2,1)S(1)}, bf16[1024,128]{0,1:T(8,128)(2,1)S(1)}, u32[]{:S(2)}, u32[]{:S(2)}) %collective-permute-start) | collective-permute-done | bytes 262176 | tf_op jit(solution)/shard_map/ppermute | solution.py:16
  23.6 2.2 %collective-permute-start.1 = (bf16[1024,128]{0,1:T(8,128)(2,1)S(1)}, bf16[1024,128]{0,1:T(8,128)(2,1)S(1)}, u32[]{:S(2)}, u32[]{:S(2)}) collective-permute-start(bf16[1024,128]{0,1:T(8,128)(2,1)S(1)} %convolution_convert_fusion.18), channel_id=1, source_target_pairs={{0,4},{4,0},{8,12},{12,8},{1,5},{5,1},{9,13},{13,9},{2,6},{6,2},{1... | collective-permute-start | bytes 786440 | tf_op jit(solution)/shard_map/ppermute | solution.py:16
  25.8 2.3 %collective-permute-done.3 = bf16[1024,128]{0,1:T(8,128)(2,1)S(1)} collective-permute-done((bf16[1024,128]{0,1:T(8,128)(2,1)S(1)}, bf16[1024,128]{0,1:T(8,128)(2,1)S(1)}, u32[]{:S(2)}, u32[]{:S(2)}) %collective-permute-start.3) | collective-permute-done | bytes 262176 | tf_op jit(solution)/shard_map/ppermute | solution.py:16
  28.4 1.9 %collective-permute-start.4 = (bf16[1024,128]{0,1:T(8,128)(2,1)S(1)}, bf16[1024,128]{0,1:T(8,128)(2,1)S(1)}, u32[]{:S(2)}, u32[]{:S(2)}) collective-permute-start(bf16[1024,128]{0,1:T(8,128)(2,1)S(1)} %convolution_convert_fusion.13), channel_id=1, source_target_pairs={{0,4},{4,0},{8,12},{12,8},{1,5},{5,1},{9,13},{13,9},{2,6},{6,2},{1... | collective-permute-start | bytes 786440 | tf_op jit(solution)/shard_map/ppermute | solution.py:16
  30.3 0.3 convolution_convert_fusion.7
  30.6 2.7 %collective-permute-start.8 = (bf16[1024,128]{0,1:T(8,128)(2,1)S(1)}, bf16[1024,128]{0,1:T(8,128)(2,1)S(1)}, u32[]{:S(2)}, u32[]{:S(2)}) collective-permute-start(bf16[1024,128]{0,1:T(8,128)(2,1)S(1)} %convolution_convert_fusion.7), channel_id=1, source_target_pairs={{0,8},{8,0},{4,12},{12,4},{1,9},{9,1},{5,13},{13,5},{2,10},{10,2},... | collective-permute-start | bytes 786440 | tf_op jit(solution)/shard_map/ppermute | solution.py:16
  33.2 0.3 convolution_convert_fusion.2
  33.5 0.4 collective-permute-start.11
  33.9 0.3 convolution_convert_fusion.17
  34.2 2.7 %collective-permute-start.2 = (bf16[1024,128]{0,1:T(8,128)(2,1)S(1)}, bf16[1024,128]{0,1:T(8,128)(2,1)S(1)}, u32[]{:S(2)}, u32[]{:S(2)}) collective-permute-start(bf16[1024,128]{0,1:T(8,128)(2,1)S(1)} %convolution_convert_fusion.17), channel_id=1, source_target_pairs={{0,8},{8,0},{4,12},{12,4},{1,9},{9,1},{5,13},{13,5},{2,10},{10,2},... | collective-permute-start | bytes 786440 | tf_op jit(solution)/shard_map/ppermute | solution.py:16
  36.9 4.6 %collective-permute-done.4 = bf16[1024,128]{0,1:T(8,128)(2,1)S(1)} collective-permute-done((bf16[1024,128]{0,1:T(8,128)(2,1)S(1)}, bf16[1024,128]{0,1:T(8,128)(2,1)S(1)}, u32[]{:S(2)}, u32[]{:S(2)}) %collective-permute-start.4) | collective-permute-done | bytes 262176 | tf_op jit(solution)/shard_map/ppermute | solution.py:16
  41.8 0.9 %collective-permute-start.5 = (bf16[1024,128]{0,1:T(8,128)(2,1)S(1)}, bf16[1024,128]{0,1:T(8,128)(2,1)S(1)}, u32[]{:S(2)}, u32[]{:S(2)}) collective-permute-start(bf16[1024,128]{0,1:T(8,128)(2,1)S(1)} %convolution_convert_fusion.12), channel_id=1, source_target_pairs={{0,8},{8,0},{4,12},{12,4},{1,9},{9,1},{5,13},{13,5},{2,10},{10,2},... | collective-permute-start | bytes 786440 | tf_op jit(solution)/shard_map/ppermute | solution.py:16
  42.7 20.6 %collective-permute-done.8 = bf16[1024,128]{0,1:T(8,128)(2,1)S(1)} collective-permute-done((bf16[1024,128]{0,1:T(8,128)(2,1)S(1)}, bf16[1024,128]{0,1:T(8,128)(2,1)S(1)}, u32[]{:S(2)}, u32[]{:S(2)}) %collective-permute-start.8) | collective-permute-done | bytes 262176 | tf_op jit(solution)/shard_map/ppermute | solution.py:16
  63.3 0.5 convolution_convert_fusion.5
  63.8 5.1 %collective-permute-done.11 = bf16[1024,128]{0,1:T(8,128)(2,1)S(1)} collective-permute-done((bf16[1024,128]{0,1:T(8,128)(2,1)S(1)}, bf16[1024,128]{0,1:T(8,128)(2,1)S(1)}, u32[]{:S(2)}, u32[]{:S(2)}) %collective-permute-start.11) | collective-permute-done | bytes 262176 | tf_op jit(solution)/shard_map/ppermute | solution.py:16
  68.9 0.5 convolution_convert_fusion
  69.4 5.1 %collective-permute-done.2 = bf16[1024,128]{0,1:T(8,128)(2,1)S(1)} collective-permute-done((bf16[1024,128]{0,1:T(8,128)(2,1)S(1)}, bf16[1024,128]{0,1:T(8,128)(2,1)S(1)}, u32[]{:S(2)}, u32[]{:S(2)}) %collective-permute-start.2) | collective-permute-done | bytes 262176 | tf_op jit(solution)/shard_map/ppermute | solution.py:16
  74.5 0.5 convolution_convert_fusion.15
  75.0 2.8 %collective-permute-done.5 = bf16[1024,128]{0,1:T(8,128)(2,1)S(1)} collective-permute-done((bf16[1024,128]{0,1:T(8,128)(2,1)S(1)}, bf16[1024,128]{0,1:T(8,128)(2,1)S(1)}, u32[]{:S(2)}, u32[]{:S(2)}) %collective-permute-start.5) | collective-permute-done | bytes 262176 | tf_op jit(solution)/shard_map/ppermute | solution.py:16
  77.8 0.5 convolution_convert_fusion.10
  78.3 1.0 %pad_maximum_fusion = bf16[4096,128]{1,0:T(8,128)(2,1)} fusion(bf16[1024,128]{1,0:T(8,128)(2,1)S(1)} %convolution_convert_fusion, bf16[1024,128]{1,0:T(8,128)(2,1)S(1)} %convolution_convert_fusion.5, bf16[1024,128]{1,0:T(8,128)(2,1)S(1)} %convolution_convert_fusion.10, bf16[1024,128]{1,0:T(8,128)(2,1)S(1)} %convolution_convert_fusion.15), kind=kLoop, calls=%fused_computation.21 | loop fusion | flops 4194304 | bytes 2097152 | tf_op jit(solution)/shard_map/concatenate | solution.py:67
  (27 shorter events, 2.2 us)
Async XLA Ops:
  0.0 0.8 copy-start
  0.0 6.3 %copy-start.1 = (bf16[4096,128]{1,0:T(8,128)(2,1)S(1)}, bf16[4096,128]{1,0:T(8,128)(2,1)}, u32[]{:S(2)}) copy-start(bf16[4096,128]{1,0:T(8,128)(2,1)} %param.5) | copy-start | bytes 3145732
  0.0 9.0 %copy-start.3 = (s32[1,3,64]{2,0,1:T(1,128)S(1)}, s32[1,3,64]{2,0,1:T(1,128)}, u32[]{:S(2)}) copy-start(s32[1,3,64]{2,0,1:T(1,128)} %param.7) | copy-start | bytes 2308
  0.0 9.0 %copy-start.2 = (bf16[1,3,64,128]{3,2,1,0:T(8,128)(2,1)S(1)}, bf16[1,3,64,128]{3,2,1,0:T(8,128)(2,1)}, u32[]{:S(2)}) copy-start(bf16[1,3,64,128]{3,2,1,0:T(8,128)(2,1)} %param.8) | copy-start | bytes 147460
  2.0 10.1 %collective-permute-start.6 = (bf16[1024,128]{0,1:T(8,128)(2,1)S(1)}, bf16[1024,128]{0,1:T(8,128)(2,1)S(1)}, u32[]{:S(2)}, u32[]{:S(2)}) collective-permute-start(bf16[1024,128]{0,1:T(8,128)(2,1)S(1)} %convolution_convert_fusion.9), channel_id=1, source_target_pairs={{0,2},{2,0},{1,3},{3,1},{4,6},{6,4},{5,7},{7,5},{8,10},{10,8},{9,1... | collective-permute-start | bytes 786440 | tf_op jit(solution)/shard_map/ppermute | solution.py:16
  6.2 11.5 %collective-permute-start.9 = (bf16[1024,128]{0,1:T(8,128)(2,1)S(1)}, bf16[1024,128]{0,1:T(8,128)(2,1)S(1)}, u32[]{:S(2)}, u32[]{:S(2)}) collective-permute-start(bf16[1024,128]{0,1:T(8,128)(2,1)S(1)} %convolution_convert_fusion.4), channel_id=1, source_target_pairs={{0,2},{2,0},{1,3},{3,1},{4,6},{6,4},{5,7},{7,5},{8,10},{10,8},{9,1... | collective-permute-start | bytes 786440 | tf_op jit(solution)/shard_map/ppermute | solution.py:16
  6.6 16.8 %collective-permute-start = (bf16[1024,128]{0,1:T(8,128)(2,1)S(1)}, bf16[1024,128]{0,1:T(8,128)(2,1)S(1)}, u32[]{:S(2)}, u32[]{:S(2)}) collective-permute-start(bf16[1024,128]{0,1:T(8,128)(2,1)S(1)} %convolution_convert_fusion.19), channel_id=1, source_target_pairs={{0,2},{2,0},{1,3},{3,1},{4,6},{6,4},{5,7},{7,5},{8,10},{10,8},{9,1... | collective-permute-start | bytes 786440 | tf_op jit(solution)/shard_map/ppermute | solution.py:16
  8.9 19.2 %collective-permute-start.3 = (bf16[1024,128]{0,1:T(8,128)(2,1)S(1)}, bf16[1024,128]{0,1:T(8,128)(2,1)S(1)}, u32[]{:S(2)}, u32[]{:S(2)}) collective-permute-start(bf16[1024,128]{0,1:T(8,128)(2,1)S(1)} %convolution_convert_fusion.14), channel_id=1, source_target_pairs={{0,2},{2,0},{1,3},{3,1},{4,6},{6,4},{5,7},{7,5},{8,10},{10,8},{9,1... | collective-permute-start | bytes 786440 | tf_op jit(solution)/shard_map/ppermute | solution.py:16
  12.4 17.9 %collective-permute-start.7 = (bf16[1024,128]{0,1:T(8,128)(2,1)S(1)}, bf16[1024,128]{0,1:T(8,128)(2,1)S(1)}, u32[]{:S(2)}, u32[]{:S(2)}) collective-permute-start(bf16[1024,128]{0,1:T(8,128)(2,1)S(1)} %convolution_convert_fusion.8), channel_id=1, source_target_pairs={{0,4},{4,0},{8,12},{12,8},{1,5},{5,1},{9,13},{13,9},{2,6},{6,2},{1... | collective-permute-start | bytes 786440 | tf_op jit(solution)/shard_map/ppermute | solution.py:16
  18.0 15.2 %collective-permute-start.10 = (bf16[1024,128]{0,1:T(8,128)(2,1)S(1)}, bf16[1024,128]{0,1:T(8,128)(2,1)S(1)}, u32[]{:S(2)}, u32[]{:S(2)}) collective-permute-start(bf16[1024,128]{0,1:T(8,128)(2,1)S(1)} %convolution_convert_fusion.3), channel_id=1, source_target_pairs={{0,4},{4,0},{8,12},{12,8},{1,5},{5,1},{9,13},{13,9},{2,6},{6,2},{1... | collective-permute-start | bytes 786440 | tf_op jit(solution)/shard_map/ppermute | solution.py:16
  23.6 10.3 %collective-permute-start.1 = (bf16[1024,128]{0,1:T(8,128)(2,1)S(1)}, bf16[1024,128]{0,1:T(8,128)(2,1)S(1)}, u32[]{:S(2)}, u32[]{:S(2)}) collective-permute-start(bf16[1024,128]{0,1:T(8,128)(2,1)S(1)} %convolution_convert_fusion.18), channel_id=1, source_target_pairs={{0,4},{4,0},{8,12},{12,8},{1,5},{5,1},{9,13},{13,9},{2,6},{6,2},{1... | collective-permute-start | bytes 786440 | tf_op jit(solution)/shard_map/ppermute | solution.py:16
  28.4 13.1 %collective-permute-start.4 = (bf16[1024,128]{0,1:T(8,128)(2,1)S(1)}, bf16[1024,128]{0,1:T(8,128)(2,1)S(1)}, u32[]{:S(2)}, u32[]{:S(2)}) collective-permute-start(bf16[1024,128]{0,1:T(8,128)(2,1)S(1)} %convolution_convert_fusion.13), channel_id=1, source_target_pairs={{0,4},{4,0},{8,12},{12,8},{1,5},{5,1},{9,13},{13,9},{2,6},{6,2},{1... | collective-permute-start | bytes 786440 | tf_op jit(solution)/shard_map/ppermute | solution.py:16
  30.6 32.7 %collective-permute-start.8 = (bf16[1024,128]{0,1:T(8,128)(2,1)S(1)}, bf16[1024,128]{0,1:T(8,128)(2,1)S(1)}, u32[]{:S(2)}, u32[]{:S(2)}) collective-permute-start(bf16[1024,128]{0,1:T(8,128)(2,1)S(1)} %convolution_convert_fusion.7), channel_id=1, source_target_pairs={{0,8},{8,0},{4,12},{12,4},{1,9},{9,1},{5,13},{13,5},{2,10},{10,2},... | collective-permute-start | bytes 786440 | tf_op jit(solution)/shard_map/ppermute | solution.py:16
  33.5 29.7 %copy-start.4 = (bf16[1,128,128]{2,1,0:T(8,128)(2,1)S(1)}, bf16[1,128,128]{2,1,0:T(8,128)(2,1)}, u32[]{:S(2)}) copy-start(bf16[1,128,128]{2,1,0:T(8,128)(2,1)} %param.9) | copy-start | bytes 98308
  33.5 35.3 %collective-permute-start.11 = (bf16[1024,128]{0,1:T(8,128)(2,1)S(1)}, bf16[1024,128]{0,1:T(8,128)(2,1)S(1)}, u32[]{:S(2)}, u32[]{:S(2)}) collective-permute-start(bf16[1024,128]{0,1:T(8,128)(2,1)S(1)} %convolution_convert_fusion.2), channel_id=1, source_target_pairs={{0,8},{8,0},{4,12},{12,4},{1,9},{9,1},{5,13},{13,5},{2,10},{10,2},... | collective-permute-start | bytes 786440 | tf_op jit(solution)/shard_map/ppermute | solution.py:16
  34.2 40.3 %collective-permute-start.2 = (bf16[1024,128]{0,1:T(8,128)(2,1)S(1)}, bf16[1024,128]{0,1:T(8,128)(2,1)S(1)}, u32[]{:S(2)}, u32[]{:S(2)}) collective-permute-start(bf16[1024,128]{0,1:T(8,128)(2,1)S(1)} %convolution_convert_fusion.17), channel_id=1, source_target_pairs={{0,8},{8,0},{4,12},{12,4},{1,9},{9,1},{5,13},{13,5},{2,10},{10,2},... | collective-permute-start | bytes 786440 | tf_op jit(solution)/shard_map/ppermute | solution.py:16
  41.8 36.0 %collective-permute-start.5 = (bf16[1024,128]{0,1:T(8,128)(2,1)S(1)}, bf16[1024,128]{0,1:T(8,128)(2,1)S(1)}, u32[]{:S(2)}, u32[]{:S(2)}) collective-permute-start(bf16[1024,128]{0,1:T(8,128)(2,1)S(1)} %convolution_convert_fusion.12), channel_id=1, source_target_pairs={{0,8},{8,0},{4,12},{12,4},{1,9},{9,1},{5,13},{13,5},{2,10},{10,2},... | collective-permute-start | bytes 786440 | tf_op jit(solution)/shard_map/ppermute | solution.py:16

commit v2 on v1

--- a/solution.py
+++ b/solution.py
@@ -3,7 +3,7 @@
 from jax import lax
 from jax.sharding import PartitionSpec as P
 
-PIECES = 4
+SIXTEENTHS = (1, 3, 4, 4, 4)
 
 
 def from_partner(block, axis, apart):
@@ -43,26 +43,35 @@
     high_bits = lax.axis_size("bfly").bit_length() - 1
     hops = [("sub", bit) for bit in range(low_bits)] + [("bfly", bit) for bit in range(high_bits)]
     matrices = level_matrices(compress[0], skeleton[0])
-    rows = traces.shape[0] // PIECES
-    coeffs = {}
-    done = [None] * PIECES
-    for step in range(PIECES + len(hops)):
-        for level in range(len(hops), -1, -1):
+    unit = traces.shape[0] // sum(SIXTEENTHS)
+    pieces = len(SIXTEENTHS)
+    starts = [unit * sum(SIXTEENTHS[:i]) for i in range(pieces + 1)]
+    coeffs, partners, done = {}, {}, [None] * pieces
+    last_sent = None
+    for step in range(pieces + len(hops)):
+        for level in range(len(hops) + 1):
             piece = step - level
-            if not 0 <= piece < PIECES:
+            if not 0 <= piece < pieces:
                 continue
             if level == 0:
-                block = traces[piece * rows : (piece + 1) * rows]
-                coeffs[piece] = jnp.dot(
+                block = traces[starts[piece] : starts[piece + 1]]
+                value = jnp.dot(
                     block, sampling[0], preferred_element_type=jnp.float32
                 ).astype(jnp.bfloat16)
+            else:
+                arrived = partners[piece]
+                if last_sent is not None:
+                    arrived, _ = lax.optimization_barrier((arrived, last_sent))
+                value = advance(coeffs[piece], arrived, matrices[level - 1])
             if level < len(hops):
                 axis, bit = hops[level]
-                partner = from_partner(coeffs[piece], axis, bit)
-                coeffs[piece] = advance(coeffs[piece], partner, matrices[level])
+                coeffs[piece] = value
+                partners[piece] = from_partner(value, axis, bit)
+                if level > 0:
+                    last_sent = value
             else:
                 done[piece] = jnp.dot(
-                    coeffs[piece], evaluation[0], preferred_element_type=jnp.float32
+                    value, evaluation[0], preferred_element_type=jnp.float32
                 ).astype(jnp.bfloat16)
     return jnp.concatenate(done, 0)
 

time: 79.5 us -> 70.4 us (0.89)
  waiting for transfers between devices: 49.1 us -> 34.9 us
  matrix products: 7.5 us -> 12.7 us
  other arithmetic: 1.32 us -> 0.28 us
  starting transfers between devices: 20.4 us -> 21.3 us
    ppermute x12 -> x15, waiting for transfers between devices: 49.1 us -> 34.9 us  [from_partner(): return lax.ppermute(block, axis, route)]
    dot_general x4 -> x5, matrix products: 2.11 us -> 5.83 us  [local(): jnp.dot(value, evaluation[0], preferred_element_type=jnp.float32)]
    dot_general x4 -> x5, matrix products: 2.95 us -> 4.05 us  [local(): jnp.dot(block, sampling[0], preferred_element_type=jnp.float32)]
    concatenate x1 -> x0, other arithmetic: 1.04 us -> none  [local(): return jnp.concatenate(done, 0)]
    ppermute x12 -> x15, starting transfers between devices: 20.4 us -> 21.3 us  [from_partner(): return lax.ppermute(block, axis, route)]
    dot_general x8 -> x10, matrix products: 2.12 us -> 2.51 us  [advance(): jnp.dot(joined, matrix, preferred_element_type=jnp.float32)]
  transfers between devices with their start and end apart: 12 -> 15, of which waited for: 9 -> 6; matrix products, arithmetic and copies ran while one was open for 8% -> 15% of each run, Pallas kernels for 0% -> 0%
where the time goes in v2:
time: 70.4 us; the launch traced here: 70.2 us
  waiting for transfers between devices  34.9 us (50%)
  starting transfers between devices  21.3 us (30%)
  matrix products  12.7 us (18%)
  local copies, waits for them, and re-layouts  0.82 us (1%)
    ppermute x15, waiting for transfers between devices, from_partner(): return lax.ppermute(block, axis, route)  34.9 us
    ppermute x15, starting transfers between devices, from_partner(): return lax.ppermute(block, axis, route)  21.3 us
    dot_general x5, matrix products, local(): jnp.dot(value, evaluation[0], preferred_element_type=jnp.float32)  5.83 us
    dot_general x5, matrix products, local(): jnp.dot(block, sampling[0], preferred_element_type=jnp.float32)  4.05 us
    dot_general x10, matrix products, advance(): jnp.dot(joined, matrix, preferred_element_type=jnp.float32)  2.51 us
  transfers between devices with their start and end apart: 15, of which 6 were waited for; matrix products, arithmetic and copies ran while one was open for 15% of the time, Pallas kernels for 0%

profile of v2, /device:TPU:0, one launch (start us, length us, event | category | flops | bytes accessed | tf_op | source)
XLA Modules:
  0.0 70.2 jit_solution(14136346455048767428)
XLA Ops:
  0.0 1.1 %convolution_convert_fusion.22 = bf16[256,128]{0,1:T(8,128)(2,1)S(1)} fusion(bf16[4096,128]{1,0:T(8,128)(2,1)} %param.5, bf16[1,128,128]{2,1,0:T(8,128)(2,1)} %param.6), kind=kOutput, calls=%fused_computation.27 | convolution fusion | flops 8421376 | bytes 163840 | tf_op jit(solution)/shard_map/dot_general | solution.py:58
  1.2 3.0 %collective-permute-start = (bf16[256,128]{0,1:T(8,128)(2,1)S(1)}, bf16[256,128]{0,1:T(8,128)(2,1)S(1)}, u32[]{:S(2)}, u32[]{:S(2)}) collective-permute-start(bf16[256,128]{0,1:T(8,128)(2,1)S(1)} %convolution_convert_fusion.22), channel_id=1, source_target_pairs={{0,2},{2,0},{1,3},{3,1},{4,6},{6,4},{5,7},{7,5},{8,10},{10,8},{9,1... | collective-permute-start | bytes 196616 | tf_op jit(solution)/shard_map/ppermute | solution.py:16
  4.2 1.2 %convolution_convert_fusion.19 = bf16[768,128]{0,1:T(8,128)(2,1)S(1)} fusion(bf16[4096,128]{1,0:T(8,128)(2,1)} %param.5, bf16[1,128,128]{2,1,0:T(8,128)(2,1)} %param.6), kind=kOutput, calls=%fused_computation.23 | convolution fusion | flops 25264128 | bytes 425984 | tf_op jit(solution)/shard_map/dot_general | solution.py:58
  5.4 1.2 %convolution_convert_fusion.14 = bf16[1024,128]{0,1:T(8,128)(2,1)S(1)} fusion(bf16[4096,128]{1,0:T(8,128)(2,1)} %param.5, bf16[1,128,128]{2,1,0:T(8,128)(2,1)} %param.6), kind=kOutput, calls=%fused_computation.17 | convolution fusion | flops 33685504 | bytes 557056 | tf_op jit(solution)/shard_map/dot_general | solution.py:58
  6.7 2.1 %collective-permute-start.5 = (bf16[1024,128]{0,1:T(8,128)(2,1)S(1)}, bf16[1024,128]{0,1:T(8,128)(2,1)S(1)}, u32[]{:S(2)}, u32[]{:S(2)}) collective-permute-start(bf16[1024,128]{0,1:T(8,128)(2,1)S(1)} %convolution_convert_fusion.14), channel_id=1, source_target_pairs={{0,2},{2,0},{1,3},{3,1},{4,6},{6,4},{5,7},{7,5},{8,10},{10,8},{9,1... | collective-permute-start | bytes 786440 | tf_op jit(solution)/shard_map/ppermute | solution.py:16
  8.7 0.3 convolution_convert_fusion.12
  9.4 2.1 %collective-permute-start.11 = (bf16[1024,128]{0,1:T(8,128)(2,1)S(1)}, bf16[1024,128]{0,1:T(8,128)(2,1)S(1)}, u32[]{:S(2)}, u32[]{:S(2)}) collective-permute-start(bf16[1024,128]{0,1:T(8,128)(2,1)S(1)} %convolution_convert_fusion.9), channel_id=1, source_target_pairs={{0,2},{2,0},{1,3},{3,1},{4,6},{6,4},{5,7},{7,5},{8,10},{10,8},{9,1... | collective-permute-start | bytes 786440 | tf_op jit(solution)/shard_map/ppermute | solution.py:16
  11.6 0.7 copy-done.4
  12.3 0.3 convolution_convert_fusion.20
  13.1 1.6 %collective-permute-start.1 = (bf16[256,128]{0,1:T(8,128)(2,1)S(1)}, bf16[256,128]{0,1:T(8,128)(2,1)S(1)}, u32[]{:S(2)}, u32[]{:S(2)}) collective-permute-start(bf16[256,128]{0,1:T(8,128)(2,1)S(1)} %convolution_convert_fusion.25), channel_id=1, source_target_pairs={{0,4},{4,0},{8,12},{12,8},{1,5},{5,1},{9,13},{13,9},{2,6},{6,2},{1... | collective-permute-start | bytes 196616 | tf_op jit(solution)/shard_map/ppermute | solution.py:16
  15.0 0.5 collective-permute-start.4
  15.5 2.6 %collective-permute-done.1 = bf16[256,128]{0,1:T(8,128)(2,1)S(1)} collective-permute-done((bf16[256,128]{0,1:T(8,128)(2,1)S(1)}, bf16[256,128]{0,1:T(8,128)(2,1)S(1)}, u32[]{:S(2)}, u32[]{:S(2)}) %collective-permute-start.1) | collective-permute-done | bytes 65568 | tf_op jit(solution)/shard_map/ppermute | solution.py:16
  18.4 2.7 %collective-permute-start.3 = (bf16[256,128]{0,1:T(8,128)(2,1)S(1)}, bf16[256,128]{0,1:T(8,128)(2,1)S(1)}, u32[]{:S(2)}, u32[]{:S(2)}) collective-permute-start(bf16[256,128]{0,1:T(8,128)(2,1)S(1)} %convolution_convert_fusion.24), channel_id=1, source_target_pairs={{0,8},{8,0},{4,12},{12,4},{1,9},{9,1},{5,13},{13,5},{2,10},{10,2},... | collective-permute-start | bytes 196616 | tf_op jit(solution)/shard_map/ppermute | solution.py:16
  21.0 0.3 convolution_convert_fusion.13
  21.3 1.2 %collective-permute-start.7 = (bf16[1024,128]{0,1:T(8,128)(2,1)S(1)}, bf16[1024,128]{0,1:T(8,128)(2,1)S(1)}, u32[]{:S(2)}, u32[]{:S(2)}) collective-permute-start(bf16[1024,128]{0,1:T(8,128)(2,1)S(1)} %convolution_convert_fusion.13), channel_id=1, source_target_pairs={{0,4},{4,0},{8,12},{12,8},{1,5},{5,1},{9,13},{13,9},{2,6},{6,2},{1... | collective-permute-start | bytes 786440 | tf_op jit(solution)/shard_map/ppermute | solution.py:16
  22.8 3.1 %collective-permute-start.6 = (bf16[768,128]{0,1:T(8,128)(2,1)S(1)}, bf16[768,128]{0,1:T(8,128)(2,1)S(1)}, u32[]{:S(2)}, u32[]{:S(2)}) collective-permute-start(bf16[768,128]{0,1:T(8,128)(2,1)S(1)} %convolution_convert_fusion.17), channel_id=1, source_target_pairs={{0,8},{8,0},{4,12},{12,4},{1,9},{9,1},{5,13},{13,5},{2,10},{10,2},... | collective-permute-start | bytes 589832 | tf_op jit(solution)/shard_map/ppermute | solution.py:16
  25.8 0.3 convolution_convert_fusion.11
  26.1 2.0 %collective-permute-start.10 = (bf16[1024,128]{0,1:T(8,128)(2,1)S(1)}, bf16[1024,128]{0,1:T(8,128)(2,1)S(1)}, u32[]{:S(2)}, u32[]{:S(2)}) collective-permute-start(bf16[1024,128]{0,1:T(8,128)(2,1)S(1)} %convolution_convert_fusion.11), channel_id=1, source_target_pairs={{0,4},{4,0},{8,12},{12,8},{1,5},{5,1},{9,13},{13,9},{2,6},{6,2},{1... | collective-permute-start | bytes 786440 | tf_op jit(solution)/shard_map/ppermute | solution.py:16
  28.1 1.0 %fusion.4 = bf16[4096,128]{1,0:T(8,128)(2,1)} fusion(bf16[256,128]{0,1:T(8,128)(2,1)S(1)} %collective-permute-done.3, bf16[256,128]{0,1:T(8,128)(2,1)S(1)} %convolution_convert_fusion.24, bf16[3,256,128]{2,1,0:T(8,128)(2,1)S(1)} %fusion.59, bf16[1,128,128]{2,1,0:T(8,128)(2,1)S(1)} %copy-done), kind=kOutput, calls=%fused_computation.26 | convolution fusion | flops 25493504 | bytes 294912 | tf_op jit(solution)/shard_map/dot_general | solution.py:73
  29.1 4.7 %collective-permute-done.7 = bf16[1024,128]{0,1:T(8,128)(2,1)S(1)} collective-permute-done((bf16[1024,128]{0,1:T(8,128)(2,1)S(1)}, bf16[1024,128]{0,1:T(8,128)(2,1)S(1)}, u32[]{:S(2)}, u32[]{:S(2)}) %collective-permute-start.7) | collective-permute-done | bytes 262176 | tf_op jit(solution)/shard_map/ppermute | solution.py:16
  34.1 0.3 convolution_convert_fusion.8
  34.4 2.4 %collective-permute-start.13 = (bf16[1024,128]{0,1:T(8,128)(2,1)S(1)}, bf16[1024,128]{0,1:T(8,128)(2,1)S(1)}, u32[]{:S(2)}, u32[]{:S(2)}) collective-permute-start(bf16[1024,128]{0,1:T(8,128)(2,1)S(1)} %convolution_convert_fusion.8), channel_id=1, source_target_pairs={{0,4},{4,0},{8,12},{12,8},{1,5},{5,1},{9,13},{13,9},{2,6},{6,2},{1... | collective-permute-start | bytes 786440 | tf_op jit(solution)/shard_map/ppermute | solution.py:16
  36.8 1.1 %fusion.3 = bf16[4096,128]{1,0:T(8,128)(2,1)} fusion(bf16[4096,128]{1,0:T(8,128)(2,1)} %fusion.4, bf16[768,128]{0,1:T(8,128)(2,1)S(1)} %collective-permute-done.6, bf16[768,128]{0,1:T(8,128)(2,1)S(1)} %convolution_convert_fusion.17, bf16[3,256,128]{2,1,0:T(8,128)(2,1)S(1)} %fusion.59, bf16[1,128,128]{2,1,0:T(8,128)(2,1)S(1)} %copy-done), kind=kOutput, calls=%fused_computation.19 | convolution fusion | flops 76480512 | bytes 688128 | tf_op jit(solution)/shard_map/dot_general | solution.py:73
  37.9 6.3 %collective-permute-done.10 = bf16[1024,128]{0,1:T(8,128)(2,1)S(1)} collective-permute-done((bf16[1024,128]{0,1:T(8,128)(2,1)S(1)}, bf16[1024,128]{0,1:T(8,128)(2,1)S(1)}, u32[]{:S(2)}, u32[]{:S(2)}) %collective-permute-start.10) | collective-permute-done | bytes 262176 | tf_op jit(solution)/shard_map/ppermute | solution.py:16
  44.2 0.3 convolution_convert_fusion.7
  44.6 8.8 %collective-permute-done.13 = bf16[1024,128]{0,1:T(8,128)(2,1)S(1)} collective-permute-done((bf16[1024,128]{0,1:T(8,128)(2,1)S(1)}, bf16[1024,128]{0,1:T(8,128)(2,1)S(1)}, u32[]{:S(2)}, u32[]{:S(2)}) %collective-permute-start.13) | collective-permute-done | bytes 262176 | tf_op jit(solution)/shard_map/ppermute | solution.py:16
  53.7 0.3 collective-permute-start.14
  54.0 1.2 %fusion.2 = bf16[4096,128]{1,0:T(8,128)(2,1)} fusion(bf16[4096,128]{1,0:T(8,128)(2,1)} %fusion.3, bf16[1024,128]{0,1:T(8,128)(2,1)S(1)} %collective-permute-done.9, bf16[1024,128]{0,1:T(8,128)(2,1)S(1)} %convolution_convert_fusion.10, bf16[3,256,128]{2,1,0:T(8,128)(2,1)S(1)} %fusion.59, bf16[1,128,128]{2,1,0:T(8,128)(2,1)S(1)} %copy-done), kind=kOutput, calls=%fused_computation.8 | convolution fusion | flops 101974016 | bytes 884736 | tf_op jit(solution)/shard_map/dot_general | solution.py:73
  55.2 9.1 %collective-permute-done.12 = bf16[1024,128]{0,1:T(8,128)(2,1)S(1)} collective-permute-done((bf16[1024,128]{0,1:T(8,128)(2,1)S(1)}, bf16[1024,128]{0,1:T(8,128)(2,1)S(1)}, u32[]{:S(2)}, u32[]{:S(2)}) %collective-permute-start.12) | collective-permute-done | bytes 262176 | tf_op jit(solution)/shard_map/ppermute | solution.py:16
  64.3 1.2 %fusion.1 = bf16[4096,128]{1,0:T(8,128)(2,1)} fusion(bf16[4096,128]{1,0:T(8,128)(2,1)} %fusion.2, bf16[1024,128]{0,1:T(8,128)(2,1)S(1)} %collective-permute-done.12, bf16[1024,128]{0,1:T(8,128)(2,1)S(1)} %convolution_convert_fusion.7, bf16[3,256,128]{2,1,0:T(8,128)(2,1)S(1)} %fusion.59, bf16[1,128,128]{2,1,0:T(8,128)(2,1)S(1)} %copy-done), kind=kOutput, calls=%fused_computation.4 | convolution fusion | flops 101974016 | bytes 884736 | tf_op jit(solution)/shard_map/dot_general | solution.py:73
  65.6 3.4 %collective-permute-done.14 = bf16[1024,128]{0,1:T(8,128)(2,1)S(1)} collective-permute-done((bf16[1024,128]{0,1:T(8,128)(2,1)S(1)}, bf16[1024,128]{0,1:T(8,128)(2,1)S(1)}, u32[]{:S(2)}, u32[]{:S(2)}) %collective-permute-start.14) | collective-permute-done | bytes 262176 | tf_op jit(solution)/shard_map/ppermute | solution.py:16
  69.0 1.2 %fusion = bf16[4096,128]{1,0:T(8,128)(2,1)} fusion(bf16[4096,128]{1,0:T(8,128)(2,1)} %fusion.1, bf16[1024,128]{0,1:T(8,128)(2,1)S(1)} %collective-permute-done.14, bf16[1024,128]{0,1:T(8,128)(2,1)S(1)} %convolution_convert_fusion.4, bf16[3,256,128]{2,1,0:T(8,128)(2,1)S(1)} %fusion.59, bf16[1,128,128]{2,1,0:T(8,128)(2,1)S(1)} %copy-done), kind=kOutput, calls=%fused_computation.1 | convolution fusion | flops 101974016 | bytes 884736 | tf_op jit(solution)/shard_map/dot_general | solution.py:73
  (36 shorter events, 2.5 us)
Async XLA Ops:
  0.0 28.1 %copy-start = (bf16[1,128,128]{2,1,0:T(8,128)(2,1)S(1)}, bf16[1,128,128]{2,1,0:T(8,128)(2,1)}, u32[]{:S(2)}) copy-start(bf16[1,128,128]{2,1,0:T(8,128)(2,1)} %param.9) | copy-start | bytes 98308
  0.0 8.7 %copy-start.1 = (bf16[4096,128]{1,0:T(8,128)(2,1)S(1)}, bf16[4096,128]{1,0:T(8,128)(2,1)}, u32[]{:S(2)}) copy-start(bf16[4096,128]{1,0:T(8,128)(2,1)} %param.5) | copy-start | bytes 3145732
  1.2 11.7 %collective-permute-start = (bf16[256,128]{0,1:T(8,128)(2,1)S(1)}, bf16[256,128]{0,1:T(8,128)(2,1)S(1)}, u32[]{:S(2)}, u32[]{:S(2)}) collective-permute-start(bf16[256,128]{0,1:T(8,128)(2,1)S(1)} %convolution_convert_fusion.22), channel_id=1, source_target_pairs={{0,2},{2,0},{1,3},{3,1},{4,6},{6,4},{5,7},{7,5},{8,10},{10,8},{9,1... | collective-permute-start | bytes 196616 | tf_op jit(solution)/shard_map/ppermute | solution.py:16
  5.3 3.4 %copy-start.2 = (bf16[1,128,128]{2,1,0:T(8,128)(2,1)S(1)}, bf16[1,128,128]{2,1,0:T(8,128)(2,1)}, u32[]{:S(2)}) copy-start(bf16[1,128,128]{2,1,0:T(8,128)(2,1)} %param.6) | copy-start | bytes 98308
  5.3 9.4 %collective-permute-start.2 = (bf16[768,128]{0,1:T(8,128)(2,1)S(1)}, bf16[768,128]{0,1:T(8,128)(2,1)S(1)}, u32[]{:S(2)}, u32[]{:S(2)}) collective-permute-start(bf16[768,128]{0,1:T(8,128)(2,1)S(1)} %convolution_convert_fusion.19), channel_id=1, source_target_pairs={{0,2},{2,0},{1,3},{3,1},{4,6},{6,4},{5,7},{7,5},{8,10},{10,8},{9,1... | collective-permute-start | bytes 589832 | tf_op jit(solution)/shard_map/ppermute | solution.py:16
  6.7 14.4 %collective-permute-start.5 = (bf16[1024,128]{0,1:T(8,128)(2,1)S(1)}, bf16[1024,128]{0,1:T(8,128)(2,1)S(1)}, u32[]{:S(2)}, u32[]{:S(2)}) collective-permute-start(bf16[1024,128]{0,1:T(8,128)(2,1)S(1)} %convolution_convert_fusion.14), channel_id=1, source_target_pairs={{0,2},{2,0},{1,3},{3,1},{4,6},{6,4},{5,7},{7,5},{8,10},{10,8},{9,1... | collective-permute-start | bytes 786440 | tf_op jit(solution)/shard_map/ppermute | solution.py:16
  9.0 2.4 %copy-start.3 = (bf16[1,3,64,128]{3,2,1,0:T(8,128)(2,1)S(1)}, bf16[1,3,64,128]{3,2,1,0:T(8,128)(2,1)}, u32[]{:S(2)}) copy-start(bf16[1,3,64,128]{3,2,1,0:T(8,128)(2,1)} %param.8) | copy-start | bytes 147460
  9.0 16.8 %collective-permute-start.8 = (bf16[1024,128]{0,1:T(8,128)(2,1)S(1)}, bf16[1024,128]{0,1:T(8,128)(2,1)S(1)}, u32[]{:S(2)}, u32[]{:S(2)}) collective-permute-start(bf16[1024,128]{0,1:T(8,128)(2,1)S(1)} %convolution_convert_fusion.12), channel_id=1, source_target_pairs={{0,2},{2,0},{1,3},{3,1},{4,6},{6,4},{5,7},{7,5},{8,10},{10,8},{9,1... | collective-permute-start | bytes 786440 | tf_op jit(solution)/shard_map/ppermute | solution.py:16
  9.4 24.7 %collective-permute-start.11 = (bf16[1024,128]{0,1:T(8,128)(2,1)S(1)}, bf16[1024,128]{0,1:T(8,128)(2,1)S(1)}, u32[]{:S(2)}, u32[]{:S(2)}) collective-permute-start(bf16[1024,128]{0,1:T(8,128)(2,1)S(1)} %convolution_convert_fusion.9), channel_id=1, source_target_pairs={{0,2},{2,0},{1,3},{3,1},{4,6},{6,4},{5,7},{7,5},{8,10},{10,8},{9,1... | collective-permute-start | bytes 786440 | tf_op jit(solution)/shard_map/ppermute | solution.py:16
  11.6 0.7 copy-start.4
  13.1 5.0 %collective-permute-start.1 = (bf16[256,128]{0,1:T(8,128)(2,1)S(1)}, bf16[256,128]{0,1:T(8,128)(2,1)S(1)}, u32[]{:S(2)}, u32[]{:S(2)}) collective-permute-start(bf16[256,128]{0,1:T(8,128)(2,1)S(1)} %convolution_convert_fusion.25), channel_id=1, source_target_pairs={{0,4},{4,0},{8,12},{12,8},{1,5},{5,1},{9,13},{13,9},{2,6},{6,2},{1... | collective-permute-start | bytes 196616 | tf_op jit(solution)/shard_map/ppermute | solution.py:16
  15.0 7.5 %collective-permute-start.4 = (bf16[768,128]{0,1:T(8,128)(2,1)S(1)}, bf16[768,128]{0,1:T(8,128)(2,1)S(1)}, u32[]{:S(2)}, u32[]{:S(2)}) collective-permute-start(bf16[768,128]{0,1:T(8,128)(2,1)S(1)} %convolution_convert_fusion.18), channel_id=1, source_target_pairs={{0,4},{4,0},{8,12},{12,8},{1,5},{5,1},{9,13},{13,9},{2,6},{6,2},{1... | collective-permute-start | bytes 589832 | tf_op jit(solution)/shard_map/ppermute | solution.py:16
  18.4 7.8 %collective-permute-start.3 = (bf16[256,128]{0,1:T(8,128)(2,1)S(1)}, bf16[256,128]{0,1:T(8,128)(2,1)S(1)}, u32[]{:S(2)}, u32[]{:S(2)}) collective-permute-start(bf16[256,128]{0,1:T(8,128)(2,1)S(1)} %convolution_convert_fusion.24), channel_id=1, source_target_pairs={{0,8},{8,0},{4,12},{12,4},{1,9},{9,1},{5,13},{13,5},{2,10},{10,2},... | collective-permute-start | bytes 196616 | tf_op jit(solution)/shard_map/ppermute | solution.py:16
  21.3 12.5 %collective-permute-start.7 = (bf16[1024,128]{0,1:T(8,128)(2,1)S(1)}, bf16[1024,128]{0,1:T(8,128)(2,1)S(1)}, u32[]{:S(2)}, u32[]{:S(2)}) collective-permute-start(bf16[1024,128]{0,1:T(8,128)(2,1)S(1)} %convolution_convert_fusion.13), channel_id=1, source_target_pairs={{0,4},{4,0},{8,12},{12,8},{1,5},{5,1},{9,13},{13,9},{2,6},{6,2},{1... | collective-permute-start | bytes 786440 | tf_op jit(solution)/shard_map/ppermute | solution.py:16
  22.8 14.0 %collective-permute-start.6 = (bf16[768,128]{0,1:T(8,128)(2,1)S(1)}, bf16[768,128]{0,1:T(8,128)(2,1)S(1)}, u32[]{:S(2)}, u32[]{:S(2)}) collective-permute-start(bf16[768,128]{0,1:T(8,128)(2,1)S(1)} %convolution_convert_fusion.17), channel_id=1, source_target_pairs={{0,8},{8,0},{4,12},{12,4},{1,9},{9,1},{5,13},{13,5},{2,10},{10,2},... | collective-permute-start | bytes 589832 | tf_op jit(solution)/shard_map/ppermute | solution.py:16
  26.1 18.1 %collective-permute-start.10 = (bf16[1024,128]{0,1:T(8,128)(2,1)S(1)}, bf16[1024,128]{0,1:T(8,128)(2,1)S(1)}, u32[]{:S(2)}, u32[]{:S(2)}) collective-permute-start(bf16[1024,128]{0,1:T(8,128)(2,1)S(1)} %convolution_convert_fusion.11), channel_id=1, source_target_pairs={{0,4},{4,0},{8,12},{12,8},{1,5},{5,1},{9,13},{13,9},{2,6},{6,2},{1... | collective-permute-start | bytes 786440 | tf_op jit(solution)/shard_map/ppermute | solution.py:16
  34.0 19.6 %collective-permute-start.9 = (bf16[1024,128]{0,1:T(8,128)(2,1)S(1)}, bf16[1024,128]{0,1:T(8,128)(2,1)S(1)}, u32[]{:S(2)}, u32[]{:S(2)}) collective-permute-start(bf16[1024,128]{0,1:T(8,128)(2,1)S(1)} %convolution_convert_fusion.10), channel_id=1, source_target_pairs={{0,8},{8,0},{4,12},{12,4},{1,9},{9,1},{5,13},{13,5},{2,10},{10,2},... | collective-permute-start | bytes 786440 | tf_op jit(solution)/shard_map/ppermute | solution.py:16
  34.4 19.0 %collective-permute-start.13 = (bf16[1024,128]{0,1:T(8,128)(2,1)S(1)}, bf16[1024,128]{0,1:T(8,128)(2,1)S(1)}, u32[]{:S(2)}, u32[]{:S(2)}) collective-permute-start(bf16[1024,128]{0,1:T(8,128)(2,1)S(1)} %convolution_convert_fusion.8), channel_id=1, source_target_pairs={{0,4},{4,0},{8,12},{12,8},{1,5},{5,1},{9,13},{13,9},{2,6},{6,2},{1... | collective-permute-start | bytes 786440 | tf_op jit(solution)/shard_map/ppermute | solution.py:16
  44.5 19.8 %collective-permute-start.12 = (bf16[1024,128]{0,1:T(8,128)(2,1)S(1)}, bf16[1024,128]{0,1:T(8,128)(2,1)S(1)}, u32[]{:S(2)}, u32[]{:S(2)}) collective-permute-start(bf16[1024,128]{0,1:T(8,128)(2,1)S(1)} %convolution_convert_fusion.7), channel_id=1, source_target_pairs={{0,8},{8,0},{4,12},{12,4},{1,9},{9,1},{5,13},{13,5},{2,10},{10,2},... | collective-permute-start | bytes 786440 | tf_op jit(solution)/shard_map/ppermute | solution.py:16
  53.7 15.3 %collective-permute-start.14 = (bf16[1024,128]{0,1:T(8,128)(2,1)S(1)}, bf16[1024,128]{0,1:T(8,128)(2,1)S(1)}, u32[]{:S(2)}, u32[]{:S(2)}) collective-permute-start(bf16[1024,128]{0,1:T(8,128)(2,1)S(1)} %convolution_convert_fusion.4), channel_id=1, source_target_pairs={{0,8},{8,0},{4,12},{12,4},{1,9},{9,1},{5,13},{13,5},{2,10},{10,2},... | collective-permute-start | bytes 786440 | tf_op jit(solution)/shard_map/ppermute | solution.py:16

commit v3 on v2

v3 whole, which is shorter than its diff:
```python
import jax
import jax.numpy as jnp
from jax import lax
from jax.sharding import PartitionSpec as P

SIXTEENTHS = (1, 3, 4, 4, 4)
FIRST_COMPACT = 1
ROOM_EIGHTHS = 5


def route(axis, apart):
    count = lax.axis_size(axis)
    pairs = []
    for low in range(count):
        high = low | 1 << apart
        if high != low and high < count:
            pairs += [(low, high), (high, low)]
    return pairs


def from_partner(block, hop):
    return lax.ppermute(block, hop[0], route(*hop))


def real_form(both):
    rank = both.shape[-1] // 2
    turned = jnp.concatenate([-both[..., rank:], both[..., :rank]], -1)
    return jnp.concatenate([both, turned], -2)


def picked_rows(compress, skeleton):
    rank = skeleton.shape[-1]
    places = lax.broadcasted_iota(jnp.int32, (1, 2 * rank, 1), 1)
    chooser = (skeleton[:, None, :] == places).astype(jnp.bfloat16)
    stacked = jnp.concatenate([compress[:, :, :rank], compress[:, :, rank:]], 1)
    return jnp.einsum(
        "lik,ljk->lij", chooser, stacked, preferred_element_type=jnp.float32
    ).astype(jnp.bfloat16)


def slots(skeleton, room):
    rank = skeleton.shape[-1]
    places = rank + lax.broadcasted_iota(jnp.int32, (1, rank, 1), 1)
    picked = jnp.any(skeleton[:, None, :] == places, -1)
    before = lax.broadcasted_iota(jnp.int32, (rank, rank), 0) > lax.broadcasted_iota(
        jnp.int32, (rank, rank), 1
    )
    slot = jnp.sum(before[None] & picked[:, None, :], -1, dtype=jnp.int32)
    index = lax.broadcasted_iota(jnp.int32, (1, 1, room), 2)
    return (picked[..., None] & (slot[..., None] == index)).astype(jnp.bfloat16)


def compact_columns(matrix, slot):
    rank = slot.shape[1]
    parts = [
        jnp.einsum("lnr,lrj->lnj", half, slot, preferred_element_type=jnp.float32)
        for half in (matrix[..., :rank], matrix[..., rank:])
    ]
    return jnp.concatenate(parts, -1).astype(jnp.bfloat16)


def times(value, matrix):
    return jnp.dot(value, matrix, preferred_element_type=jnp.float32).astype(jnp.bfloat16)


def all_hops():
    low_bits = lax.axis_size("sub").bit_length() - 1
    high_bits = lax.axis_size("bfly").bit_length() - 1
    return [("sub", bit) for bit in range(low_bits)] + [("bfly", bit) for bit in range(high_bits)]


def full_width(traces, sampling, own_full, evaluation):
    coeffs = times(traces, sampling)
    for level, hop in enumerate(all_hops()):
        partner = from_partner(coeffs, hop)
        coeffs = times(jnp.concatenate([coeffs, partner], -1), own_full[level])
    return times(coeffs, evaluation)


def local(traces, sampling, skeleton, compress, evaluation):
    sampling, skeleton, compress, evaluation = sampling[0], skeleton[0], compress[0], evaluation[0]
    hops = all_hops()
    levels = len(hops)
    rank = skeleton.shape[-1]
    room = rank * ROOM_EIGHTHS // 8

    everyone = lax.all_gather(skeleton, ("bfly", "sub"))
    too_many = jnp.any(jnp.sum(everyone >= rank, -1) > room)
    box = lax.axis_index("bfly") * lax.axis_size("sub") + lax.axis_index("sub")
    partner_skeleton = jnp.stack([everyone[box ^ (1 << s), s] for s in range(levels)])

    rows = picked_rows(compress, skeleton)
    full = jnp.concatenate([real_form(rows[:, :rank]), real_form(rows[:, rank:])], 1)
    kept = jnp.einsum(
        "lrj,lrc->ljc", slots(skeleton, room), rows[:, rank:], preferred_element_type=jnp.float32
    ).astype(jnp.bfloat16)
    small = jnp.concatenate([real_form(rows[:, :rank]), real_form(kept)], 1)
    theirs = slots(partner_skeleton, room)
    sent_sampling = compact_columns(sampling[None], theirs[:1])[0]
    sent_full = compact_columns(full[:-1], theirs[1:])
    sent_small = compact_columns(small[:-1], theirs[1:])

    def is_compact(level, piece):
        return piece >= FIRST_COMPACT and level >= 0 and (level > 0 or piece > FIRST_COMPACT)

    unit = traces.shape[0] // sum(SIXTEENTHS)
    pieces = len(SIXTEENTHS)
    starts = [unit * sum(SIXTEENTHS[:i]) for i in range(pieces + 1)]
    inputs, partners, done = {}, {}, [None] * pieces
    last_sent = None
    for step in range(pieces + levels):
        for level in range(levels + 1):
            piece = step - level
            if not 0 <= piece < pieces:
                continue
            if level == 0:
                value = traces[starts[piece] : starts[piece + 1]]
                if piece >= 2:
                    value, _ = lax.optimization_barrier((value, last_sent))
                matrix, sending = sampling, sent_sampling
            else:
                arrived = partners[piece]
                if last_sent is not None:
                    arrived, _ = lax.optimization_barrier((arrived, last_sent))
                value = jnp.concatenate([inputs[piece], arrived], -1)
                if is_compact(level - 1, piece):
                    matrix = small[level - 1]
                    sending = sent_small[level - 1] if level < levels else None
                else:
                    matrix = full[level - 1]
                    sending = sent_full[level - 1] if level < levels else None
            own = times(value, matrix)
            if level < levels:
                outgoing = times(value, sending) if is_compact(level, piece) else own
                inputs[piece] = own
                partners[piece] = from_partner(outgoing, hops[level])
                if level > 0:
                    last_sent = outgoing
            else:
                done[piece] = times(own, evaluation)
    quick = jnp.concatenate(done, 0)
    return lax.cond(
        too_many,
        lambda: full_width(traces, sampling, full, evaluation),
        lambda: quick,
    )


def solution(mesh):
    placed = (
        P(("shots", "tr"), ("bfly", "sub")),
        P(("bfly", "sub"), None, None),
        P(("bfly", "sub"), None, None),
        P(("bfly", "sub"), None, None, None),
        P(("bfly", "sub"), None, None),
    )
    return jax.shard_map(
        local,
        mesh=mesh,
        in_specs=placed,
        out_specs=P(("shots", "tr"), ("bfly", "sub")),
        check_vma=False,
    )
```

time: 70.4 us -> 82.7 us (1.17)
  blocking collectives: 0 us -> 26.8 us
  waiting for transfers between devices: 34.9 us -> 8.53 us
  matrix products: 12.7 us -> 23.2 us
  starting transfers between devices: 21.3 us -> 19.2 us
  other arithmetic: 0.28 us -> 1.68 us
  local copies, waits for them, and re-layouts: 0.82 us -> 1.77 us
    all_gather x0 -> x1, blocking collectives: none -> 26.8 us  [local(): everyone = lax.all_gather(skeleton, ('bfly', 'sub'))]
    ppermute x15, waiting for transfers between devices: 34.9 us -> 8.53 us  [from_partner(): return lax.ppermute(block, hop[0], route(*hop))]
    dot_general x21 -> x39, matrix products: 12.7 us -> 23.2 us  [the longest x31 20.1 us: times(): jnp.dot(value, matrix, preferred_element_type=jnp.float32)]
    ppermute x15, starting transfers between devices: 21.3 us -> 19.2 us  [from_partner(): return lax.ppermute(block, hop[0], route(*hop))]
    reduce_or x0 -> x2, other arithmetic: none -> 0.89 us  [the longest x1 0.63 us: local(): too_many = jnp.any(jnp.sum(everyone >= rank, -1) > room)]
    unnamed x12 -> x22, local copies, waits for them, and re-layouts: 0.8 us -> 1.68 us
  transfers between devices with their start and end apart: 15 -> 15, of which waited for: 6 -> 4; matrix products, arithmetic and copies ran while one was open for 15% -> 30% of each run, Pallas kernels for 0% -> 0%
where the time goes in v3:
time: 82.7 us; the launch traced here: 82.3 us
  blocking collectives  26.8 us (32%)
  matrix products  23.2 us (28%)
  starting transfers between devices  19.2 us (23%)
  waiting for transfers between devices  8.53 us (10%)
  local copies, waits for them, and re-layouts  1.77 us (2%)
  other arithmetic  1.68 us (2%)
  between operations  1.04 us (1%)
    all_gather x1, blocking collectives, local(): everyone = lax.all_gather(skeleton, ('bfly', 'sub'))  26.8 us
    dot_general x31, matrix products, times(): jnp.dot(value, matrix, preferred_element_type=jnp.float32)  20.1 us
    ppermute x15, starting transfers between devices, from_partner(): return lax.ppermute(block, hop[0], route(*hop))  19.2 us
    ppermute x15, waiting for transfers between devices, from_partner(): return lax.ppermute(block, hop[0], route(*hop))  8.53 us
    dot_general x6, matrix products, compact_columns(): jnp.einsum('lnr,lrj->lnj', half, slot, preferred_element_type=jnp.float32)  2.64 us
    unnamed x22, local copies, waits for them, and re-layouts  1.68 us
  transfers between devices with their start and end apart: 15, of which 4 were waited for; matrix products, arithmetic and copies ran while one was open for 30% of the time, Pallas kernels for 0%

profile of v3, /device:TPU:0, one launch (start us, length us, event | category | flops | bytes accessed | tf_op | source)
XLA Modules:
  0.0 82.3 jit_solution(184394885547694031)
XLA Ops:
  0.0 1.0 %convolution_convert_fusion.38 = bf16[256,128]{0,1:T(8,128)(2,1)S(1)} fusion(bf16[4096,128]{1,0:T(8,128)(2,1)} %param.7, bf16[1,128,128]{2,1,0:T(8,128)(2,1)} %param.8), kind=kOutput, calls=%fused_computation.61 | convolution fusion | flops 8421376 | bytes 163840 | tf_op jit(solution)/shard_map/dot_general | solution.py:63
  1.1 3.0 %collective-permute-start.3 = (bf16[256,128]{0,1:T(8,128)(2,1)S(1)}, bf16[256,128]{0,1:T(8,128)(2,1)S(1)}, u32[]{:S(2)}, u32[]{:S(2)}) collective-permute-start(bf16[256,128]{0,1:T(8,128)(2,1)S(1)} %convolution_convert_fusion.38), channel_id=1, source_target_pairs={{0,2},{2,0},{1,3},{3,1},{4,6},{6,4},{5,7},{7,5},{8,10},{10,8},{9,1... | collective-permute-start | bytes 196616 | tf_op jit(solution)/shard_map/ppermute | solution.py:22
  4.1 1.2 %convolution_convert_fusion.24 = bf16[768,128]{0,1:T(8,128)(2,1)S(1)} fusion(bf16[4096,128]{1,0:T(8,128)(2,1)} %param.7, bf16[1,128,128]{2,1,0:T(8,128)(2,1)} %param.8), kind=kOutput, calls=%fused_computation.46 | convolution fusion | flops 25264128 | bytes 425984 | tf_op jit(solution)/shard_map/dot_general | solution.py:63
  5.4 0.7 copy.52
  6.1 26.8 %all_gather.3 = s32[8,3,64]{2,1,0:T(4,128)S(1)} all-gather(s32[1,3,64]{2,1,0:T(4,128)S(1)} %copy.52), channel_id=1, replica_groups=mesh['shots'=2,'bfly'=4,'sub'=2,'tr'=2] {'bfly','sub'}, dimensions={0}, use_global_device_ids=true | all-gather | bytes 6912 | tf_op jit(solution)/shard_map/all_gather | solution.py:87
  33.5 1.0 %fusion.29 = bf16[128,40]{0,1:T(8,128)(2,1)S(1)} fusion(bf16[1,128,128]{2,1,0:T(8,128)(2,1)} %param.8, pred[3,64,40]{1,2,0:T(8,128)(4,1)S(1)} %fusion.72), kind=kOutput, calls=%fused_computation.73 | convolution fusion | flops 660480 | bytes 48128 | tf_op jit(solution)/shard_map/lnr,lrj->lnj/dot_general | solution.py:56
  34.5 0.9 %fusion.28 = bf16[128,40]{0,1:T(8,128)(2,1)S(1)} fusion(bf16[1,128,128]{2,1,0:T(8,128)(2,1)} %param.8, pred[3,64,40]{1,2,0:T(8,128)(4,1)S(1)} %fusion.72), kind=kOutput, calls=%fused_computation.72 | convolution fusion | flops 660480 | bytes 48128 | tf_op jit(solution)/shard_map/lnr,lrj->lnj/dot_general | solution.py:56
  35.4 0.9 %copy.37 = bf16[1,3,64,128]{2,3,1,0:T(8,128)(2,1)S(1)} copy(bf16[1,3,64,128]{3,2,1,0:T(8,128)(2,1)} %param.10) | data formatting | bytes 98304 | tf_op args[3]
  38.2 0.6 compare_reduce_fusion.2
  40.2 1.6 %collective-permute-start.8 = (bf16[1024,80]{0,1:T(8,128)(2,1)S(1)}, bf16[1024,80]{0,1:T(8,128)(2,1)S(1)}, u32[]{:S(2)}, u32[]{:S(2)}) collective-permute-start(bf16[1024,80]{0,1:T(8,128)(2,1)S(1)} %convolution_convert_fusion.33), channel_id=1, source_target_pairs={{0,2},{2,0},{1,3},{3,1},{4,6},{6,4},{5,7},{7,5},{8,10},{10,8},{9,1... | collective-permute-start | bytes 491528 | tf_op jit(solution)/shard_map/ppermute | solution.py:22
  42.3 1.9 %collective-permute-start.7 = (bf16[768,80]{0,1:T(8,128)(2,1)S(1)}, bf16[768,80]{0,1:T(8,128)(2,1)S(1)}, u32[]{:S(2)}, u32[]{:S(2)}) collective-permute-start(bf16[768,80]{0,1:T(8,128)(2,1)S(1)} %convolution_convert_fusion.35), channel_id=1, source_target_pairs={{0,4},{4,0},{8,12},{12,8},{1,5},{5,1},{9,13},{13,9},{2,6},{6,2},{1... | collective-permute-start | bytes 368648 | tf_op jit(solution)/shard_map/ppermute | solution.py:22
  45.3 1.8 %collective-permute-start.11 = (bf16[1024,80]{0,1:T(8,128)(2,1)S(1)}, bf16[1024,80]{0,1:T(8,128)(2,1)S(1)}, u32[]{:S(2)}, u32[]{:S(2)}) collective-permute-start(bf16[1024,80]{0,1:T(8,128)(2,1)S(1)} %convolution_convert_fusion.32), channel_id=1, source_target_pairs={{0,2},{2,0},{1,3},{3,1},{4,6},{6,4},{5,7},{7,5},{8,10},{10,8},{9,1... | collective-permute-start | bytes 491528 | tf_op jit(solution)/shard_map/ppermute | solution.py:22
  47.6 2.4 %collective-permute-start.10 = (bf16[1024,80]{0,1:T(8,128)(2,1)S(1)}, bf16[1024,80]{0,1:T(8,128)(2,1)S(1)}, u32[]{:S(2)}, u32[]{:S(2)}) collective-permute-start(bf16[1024,80]{0,1:T(8,128)(2,1)S(1)} %convolution_convert_fusion.30), channel_id=1, source_target_pairs={{0,4},{4,0},{8,12},{12,8},{1,5},{5,1},{9,13},{13,9},{2,6},{6,2},{1... | collective-permute-start | bytes 491528 | tf_op jit(solution)/shard_map/ppermute | solution.py:22
  50.0 1.0 %convolution_convert_fusion.18 = bf16[1024,128]{0,1:T(8,128)(2,1)} fusion(bf16[1024,80]{0,1:T(8,128)(2,1)S(1)} %collective-permute-done.8, bf16[1024,128]{0,1:T(8,128)(2,1)S(1)} %convolution_convert_fusion.19, bf16[3,208,128]{2,1,0:T(8,128)(2,1)S(1)} %maximum_maximum_fusion.1), kind=kOutput, calls=%fused_computation.39 | convolution fusion | flops 55508992 | bytes 741376 | tf_op jit(solution)/shard_map/dot_general | solution.py:63
  51.0 0.8 %convolution_convert_fusion.34 = bf16[768,80]{0,1:T(8,128)(2,1)} fusion(bf16[208,80]{0,1:T(8,128)(2,1)S(1)} %fusion.80, bf16[768,80]{0,1:T(8,128)(2,1)S(1)} %collective-permute-done.7, bf16[768,128]{0,1:T(8,128)(2,1)S(1)} %convolution_convert_fusion.23), kind=kOutput, calls=%fused_computation.56 | convolution fusion | flops 26259456 | bytes 475648 | tf_op jit(solution)/shard_map/dot_general | solution.py:63
  51.8 0.6 collective-permute-start.9
  52.9 0.9 %convolution_convert_fusion.22 = bf16[768,128]{0,1:T(8,128)(2,1)} fusion(bf16[768,80]{0,1:T(8,128)(2,1)S(1)} %collective-permute-done.7, bf16[768,128]{0,1:T(8,128)(2,1)S(1)} %convolution_convert_fusion.23, bf16[3,208,128]{2,1,0:T(8,128)(2,1)S(1)} %maximum_maximum_fusion.1), kind=kOutput, calls=%fused_computation.44 | convolution fusion | flops 41631744 | bytes 569344 | tf_op jit(solution)/shard_map/dot_general | solution.py:63
  54.0 1.0 %fusion.27 = bf16[4096,128]{1,0:T(8,128)(2,1)} fusion(bf16[256,128]{0,1:T(8,128)(2,1)S(1)} %collective-permute-done.6, bf16[256,128]{0,1:T(8,128)(2,1)S(1)} %convolution_convert_fusion.40, bf16[3,256,128]{2,1,0:T(8,128)(2,1)S(1)} %maximum_maximum_fusion, bf16[1,128,128]{2,1,0:T(8,128)(2,1)S(1)} %copy-done.2), kind=kOutput, calls=%fused_computation.60 | convolution fusion | flops 25493504 | bytes 294912 | tf_op jit(solution)/shard_map/dot_general | solution.py:63
  55.2 2.1 %collective-permute-start.13 = (bf16[1024,80]{0,1:T(8,128)(2,1)S(1)}, bf16[1024,80]{0,1:T(8,128)(2,1)S(1)}, u32[]{:S(2)}, u32[]{:S(2)}) collective-permute-start(bf16[1024,80]{0,1:T(8,128)(2,1)S(1)} %convolution_convert_fusion.29), channel_id=1, source_target_pairs={{0,4},{4,0},{8,12},{12,8},{1,5},{5,1},{9,13},{13,9},{2,6},{6,2},{1... | collective-permute-start | bytes 491528 | tf_op jit(solution)/shard_map/ppermute | solution.py:22
  57.3 1.0 %convolution_convert_fusion.15 = bf16[1024,128]{0,1:T(8,128)(2,1)} fusion(bf16[1024,80]{0,1:T(8,128)(2,1)S(1)} %collective-permute-done.11, bf16[1024,128]{0,1:T(8,128)(2,1)S(1)} %convolution_convert_fusion.17, bf16[3,208,128]{2,1,0:T(8,128)(2,1)S(1)} %maximum_maximum_fusion.1), kind=kOutput, calls=%fused_computation.36 | convolution fusion | flops 55508992 | bytes 741376 | tf_op jit(solution)/shard_map/dot_general | solution.py:63
  58.7 1.0 %convolution_convert_fusion.16 = bf16[1024,128]{0,1:T(8,128)(2,1)} fusion(bf16[1024,80]{0,1:T(8,128)(2,1)S(1)} %collective-permute-done.10, bf16[1024,128]{0,1:T(8,128)(2,1)S(1)} %copy-done.4, bf16[3,208,128]{2,1,0:T(8,128)(2,1)S(1)} %maximum_maximum_fusion.1), kind=kOutput, calls=%fused_computation.37 | convolution fusion | flops 55508992 | bytes 741376 | tf_op jit(solution)/shard_map/dot_general | solution.py:63
  60.2 1.2 %fusion.26 = bf16[4096,128]{1,0:T(8,128)(2,1)} fusion(bf16[4096,128]{1,0:T(8,128)(2,1)} %fusion.27, bf16[768,80]{0,1:T(8,128)(2,1)S(1)} %collective-permute-done.9, bf16[768,128]{0,1:T(8,128)(2,1)S(1)} %copy-done.7, bf16[3,208,128]{2,1,0:T(8,128)(2,1)S(1)} %maximum_maximum_fusion.1, bf16[1,128,128]{2,1,0:T(8,128)(2,1)S(1)} %copy-done.3), kind=kOutput, calls=%fused_computation.42 | convolution fusion | flops 66895872 | bytes 602112 | tf_op jit(solution)/shard_map/dot_general | solution.py:63
  61.6 1.6 %collective-permute-start.16 = (bf16[1024,80]{0,1:T(8,128)(2,1)S(1)}, bf16[1024,80]{0,1:T(8,128)(2,1)S(1)}, u32[]{:S(2)}, u32[]{:S(2)}) collective-permute-start(bf16[1024,80]{0,1:T(8,128)(2,1)S(1)} %convolution_convert_fusion.27), channel_id=1, source_target_pairs={{0,4},{4,0},{8,12},{12,8},{1,5},{5,1},{9,13},{13,9},{2,6},{6,2},{1... | collective-permute-start | bytes 491528 | tf_op jit(solution)/shard_map/ppermute | solution.py:22
  63.1 1.0 %convolution_convert_fusion.10 = bf16[1024,128]{0,1:T(8,128)(2,1)} fusion(bf16[1024,80]{0,1:T(8,128)(2,1)S(1)} %collective-permute-done.14, bf16[1024,128]{0,1:T(8,128)(2,1)S(1)} %convolution_convert_fusion.14, bf16[3,208,128]{2,1,0:T(8,128)(2,1)S(1)} %maximum_maximum_fusion.1), kind=kOutput, calls=%fused_computation.30 | convolution fusion | flops 55508992 | bytes 741376 | tf_op jit(solution)/shard_map/dot_general | solution.py:63
  64.3 3.3 %collective-permute-start.15 = (bf16[1024,80]{0,1:T(8,128)(2,1)S(1)}, bf16[1024,80]{0,1:T(8,128)(2,1)S(1)}, u32[]{:S(2)}, u32[]{:S(2)}) collective-permute-start(bf16[1024,80]{0,1:T(8,128)(2,1)S(1)} %convolution_convert_fusion.26), channel_id=1, source_target_pairs={{0,8},{8,0},{4,12},{12,4},{1,9},{9,1},{5,13},{13,5},{2,10},{10,2},... | collective-permute-start | bytes 491528 | tf_op jit(solution)/shard_map/ppermute | solution.py:22
  67.6 1.0 %convolution_convert_fusion.11 = bf16[1024,128]{0,1:T(8,128)(2,1)} fusion(bf16[1024,80]{0,1:T(8,128)(2,1)S(1)} %collective-permute-done.13, bf16[1024,128]{0,1:T(8,128)(2,1)S(1)} %copy-done.5, bf16[3,208,128]{2,1,0:T(8,128)(2,1)S(1)} %maximum_maximum_fusion.1), kind=kOutput, calls=%fused_computation.31 | convolution fusion | flops 55508992 | bytes 741376 | tf_op jit(solution)/shard_map/dot_general | solution.py:63
  68.6 3.8 %collective-permute-done.12 = bf16[1024,80]{0,1:T(8,128)(2,1)S(1)} collective-permute-done((bf16[1024,80]{0,1:T(8,128)(2,1)S(1)}, bf16[1024,80]{0,1:T(8,128)(2,1)S(1)}, u32[]{:S(2)}, u32[]{:S(2)}) %collective-permute-start.12) | collective-permute-done | bytes 163872 | tf_op jit(solution)/shard_map/ppermute | solution.py:22
  72.3 2.2 %fusion.25 = bf16[4096,128]{1,0:T(8,128)(2,1)} fusion(bf16[4096,128]{1,0:T(8,128)(2,1)} %fusion.26, bf16[1024,80]{0,1:T(8,128)(2,1)S(1)} %collective-permute-done.12, bf16[1024,128]{0,1:T(8,128)(2,1)} %convolution_convert_fusion.16, bf16[3,208,128]{2,1,0:T(8,128)(2,1)S(1)} %maximum_maximum_fusion.1, bf16[1,128,128]{2,1,0:T(8,128)(2,1)S(1)} %copy-done.3), kind=kOutput, calls=%fused_computation.33 | convolution fusion | flops 89194496 | bytes 774144 | tf_op jit(solution)/shard_map/dot_general | solution.py:63
  74.8 1.0 %convolution_convert_fusion.7 = bf16[1024,128]{0,1:T(8,128)(2,1)} fusion(bf16[1024,80]{0,1:T(8,128)(2,1)S(1)} %collective-permute-done.16, bf16[1024,128]{0,1:T(8,128)(2,1)S(1)} %copy-done.6, bf16[3,208,128]{2,1,0:T(8,128)(2,1)S(1)} %maximum_maximum_fusion.1), kind=kOutput, calls=%fused_computation.26 | convolution fusion | flops 55508992 | bytes 741376 | tf_op jit(solution)/shard_map/dot_general | solution.py:63
  75.8 1.2 %fusion.24 = bf16[4096,128]{1,0:T(8,128)(2,1)} fusion(bf16[4096,128]{1,0:T(8,128)(2,1)} %fusion.25, bf16[1024,80]{0,1:T(8,128)(2,1)S(1)} %collective-permute-done.15, bf16[1024,128]{0,1:T(8,128)(2,1)S(1)} %copy-done.8, bf16[3,208,128]{2,1,0:T(8,128)(2,1)S(1)} %maximum_maximum_fusion.1, bf16[1,128,128]{2,1,0:T(8,128)(2,1)S(1)} %copy-done.3), kind=kOutput, calls=%fused_computation.28 | convolution fusion | flops 89194496 | bytes 774144 | tf_op jit(solution)/shard_map/dot_general | solution.py:63
  77.1 4.0 %collective-permute-done.17 = bf16[1024,80]{0,1:T(8,128)(2,1)S(1)} collective-permute-done((bf16[1024,80]{0,1:T(8,128)(2,1)S(1)}, bf16[1024,80]{0,1:T(8,128)(2,1)S(1)}, u32[]{:S(2)}, u32[]{:S(2)}) %collective-permute-start.17) | collective-permute-done | bytes 163872 | tf_op jit(solution)/shard_map/ppermute | solution.py:22
  81.0 1.2 %fusion.23 = bf16[4096,128]{1,0:T(8,128)(2,1)} fusion(bf16[4096,128]{1,0:T(8,128)(2,1)} %fusion.24, bf16[1024,80]{0,1:T(8,128)(2,1)S(1)} %collective-permute-done.17, bf16[1024,128]{0,1:T(8,128)(2,1)S(1)} %copy-done.9, bf16[3,208,128]{2,1,0:T(8,128)(2,1)S(1)} %maximum_maximum_fusion.1, bf16[1,128,128]{2,1,0:T(8,128)(2,1)S(1)} %copy-done.3), kind=kOutput, calls=%fused_computation.24 | convolution fusion | flops 89194496 | bytes 774144 | tf_op jit(solution)/shard_map/dot_general | solution.py:63
  (78 shorter events, 7.8 us)
Async XLA Ops:
  1.1 38.4 %collective-permute-start.3 = (bf16[256,128]{0,1:T(8,128)(2,1)S(1)}, bf16[256,128]{0,1:T(8,128)(2,1)S(1)}, u32[]{:S(2)}, u32[]{:S(2)}) collective-permute-start(bf16[256,128]{0,1:T(8,128)(2,1)S(1)} %convolution_convert_fusion.38), channel_id=1, source_target_pairs={{0,2},{2,0},{1,3},{3,1},{4,6},{6,4},{5,7},{7,5},{8,10},{10,8},{9,1... | collective-permute-start | bytes 196616 | tf_op jit(solution)/shard_map/ppermute | solution.py:22
  5.2 36.8 %collective-permute-start.5 = (bf16[768,128]{0,1:T(8,128)(2,1)S(1)}, bf16[768,128]{0,1:T(8,128)(2,1)S(1)}, u32[]{:S(2)}, u32[]{:S(2)}) collective-permute-start(bf16[768,128]{0,1:T(8,128)(2,1)S(1)} %convolution_convert_fusion.24), channel_id=1, source_target_pairs={{0,2},{2,0},{1,3},{3,1},{4,6},{6,4},{5,7},{7,5},{8,10},{10,8},{9,1... | collective-permute-start | bytes 589832 | tf_op jit(solution)/shard_map/ppermute | solution.py:22
  36.7 1.4 %copy-start = (bf16[4096,128]{1,0:T(8,128)(2,1)S(1)}, bf16[4096,128]{1,0:T(8,128)(2,1)}, u32[]{:S(2)}) copy-start(bf16[4096,128]{1,0:T(8,128)(2,1)} %param.7) | copy-start | bytes 3145732
  38.1 3.7 %copy-start.1 = (bf16[1,128,128]{2,1,0:T(8,128)(2,1)S(1)}, bf16[1,128,128]{2,1,0:T(8,128)(2,1)}, u32[]{:S(2)}) copy-start(bf16[1,128,128]{2,1,0:T(8,128)(2,1)} %param.8) | copy-start | bytes 98308
  39.7 4.7 %collective-permute-start.4 = (bf16[256,128]{0,1:T(8,128)(2,1)S(1)}, bf16[256,128]{0,1:T(8,128)(2,1)S(1)}, u32[]{:S(2)}, u32[]{:S(2)}) collective-permute-start(bf16[256,128]{0,1:T(8,128)(2,1)S(1)} %convolution_convert_fusion.41), channel_id=1, source_target_pairs={{0,4},{4,0},{8,12},{12,8},{1,5},{5,1},{9,13},{13,9},{2,6},{6,2},{1... | collective-permute-start | bytes 196616 | tf_op jit(solution)/shard_map/ppermute | solution.py:22
  40.2 7.1 %collective-permute-start.8 = (bf16[1024,80]{0,1:T(8,128)(2,1)S(1)}, bf16[1024,80]{0,1:T(8,128)(2,1)S(1)}, u32[]{:S(2)}, u32[]{:S(2)}) collective-permute-start(bf16[1024,80]{0,1:T(8,128)(2,1)S(1)} %convolution_convert_fusion.33), channel_id=1, source_target_pairs={{0,2},{2,0},{1,3},{3,1},{4,6},{6,4},{5,7},{7,5},{8,10},{10,8},{9,1... | collective-permute-start | bytes 491528 | tf_op jit(solution)/shard_map/ppermute | solution.py:22
  42.3 8.7 %collective-permute-start.7 = (bf16[768,80]{0,1:T(8,128)(2,1)S(1)}, bf16[768,80]{0,1:T(8,128)(2,1)S(1)}, u32[]{:S(2)}, u32[]{:S(2)}) collective-permute-start(bf16[768,80]{0,1:T(8,128)(2,1)S(1)} %convolution_convert_fusion.35), channel_id=1, source_target_pairs={{0,4},{4,0},{8,12},{12,8},{1,5},{5,1},{9,13},{13,9},{2,6},{6,2},{1... | collective-permute-start | bytes 368648 | tf_op jit(solution)/shard_map/ppermute | solution.py:22
  44.6 9.2 %collective-permute-start.6 = (bf16[256,128]{0,1:T(8,128)(2,1)S(1)}, bf16[256,128]{0,1:T(8,128)(2,1)S(1)}, u32[]{:S(2)}, u32[]{:S(2)}) collective-permute-start(bf16[256,128]{0,1:T(8,128)(2,1)S(1)} %convolution_convert_fusion.40), channel_id=1, source_target_pairs={{0,8},{8,0},{4,12},{12,4},{1,9},{9,1},{5,13},{13,5},{2,10},{10,2},... | collective-permute-start | bytes 196616 | tf_op jit(solution)/shard_map/ppermute | solution.py:22
  45.3 9.7 %collective-permute-start.11 = (bf16[1024,80]{0,1:T(8,128)(2,1)S(1)}, bf16[1024,80]{0,1:T(8,128)(2,1)S(1)}, u32[]{:S(2)}, u32[]{:S(2)}) collective-permute-start(bf16[1024,80]{0,1:T(8,128)(2,1)S(1)} %convolution_convert_fusion.32), channel_id=1, source_target_pairs={{0,2},{2,0},{1,3},{3,1},{4,6},{6,4},{5,7},{7,5},{8,10},{10,8},{9,1... | collective-permute-start | bytes 491528 | tf_op jit(solution)/shard_map/ppermute | solution.py:22
  47.6 10.7 %collective-permute-start.10 = (bf16[1024,80]{0,1:T(8,128)(2,1)S(1)}, bf16[1024,80]{0,1:T(8,128)(2,1)S(1)}, u32[]{:S(2)}, u32[]{:S(2)}) collective-permute-start(bf16[1024,80]{0,1:T(8,128)(2,1)S(1)} %convolution_convert_fusion.30), channel_id=1, source_target_pairs={{0,4},{4,0},{8,12},{12,8},{1,5},{5,1},{9,13},{13,9},{2,6},{6,2},{1... | collective-permute-start | bytes 491528 | tf_op jit(solution)/shard_map/ppermute | solution.py:22
  50.9 3.1 %copy-start.2 = (bf16[1,128,128]{2,1,0:T(8,128)(2,1)S(1)}, bf16[1,128,128]{2,1,0:T(8,128)(2,1)}, u32[]{:S(2)}) copy-start(bf16[1,128,128]{2,1,0:T(8,128)(2,1)} %param.11) | copy-start | bytes 98308
  51.8 8.4 %collective-permute-start.9 = (bf16[768,80]{0,1:T(8,128)(2,1)}, bf16[768,80]{0,1:T(8,128)(2,1)S(1)}, u32[]{:S(2)}, u32[]{:S(2)}) collective-permute-start(bf16[768,80]{0,1:T(8,128)(2,1)} %convolution_convert_fusion.34), channel_id=1, source_target_pairs={{0,8},{8,0},{4,12},{12,4},{1,9},{9,1},{5,13},{13,5},{2,10},{10,2},... | collective-permute-start | bytes 368648 | tf_op jit(solution)/shard_map/ppermute | solution.py:22
  53.8 7.5 %collective-permute-start.14 = (bf16[1024,80]{0,1:T(8,128)(2,1)S(1)}, bf16[1024,80]{0,1:T(8,128)(2,1)S(1)}, u32[]{:S(2)}, u32[]{:S(2)}) collective-permute-start(bf16[1024,80]{0,1:T(8,128)(2,1)S(1)} %convolution_convert_fusion.31), channel_id=1, source_target_pairs={{0,2},{2,0},{1,3},{3,1},{4,6},{6,4},{5,7},{7,5},{8,10},{10,8},{9,1... | collective-permute-start | bytes 491528 | tf_op jit(solution)/shard_map/ppermute | solution.py:22
  55.0 3.3 %copy-start.4 = (bf16[1024,128]{0,1:T(8,128)(2,1)S(1)}, bf16[1024,128]{0,1:T(8,128)(2,1)}, u32[]{:S(2)}) copy-start(bf16[1024,128]{0,1:T(8,128)(2,1)} %convolution_convert_fusion.18) | copy-start | bytes 786436
  55.2 8.9 %collective-permute-start.13 = (bf16[1024,80]{0,1:T(8,128)(2,1)S(1)}, bf16[1024,80]{0,1:T(8,128)(2,1)S(1)}, u32[]{:S(2)}, u32[]{:S(2)}) collective-permute-start(bf16[1024,80]{0,1:T(8,128)(2,1)S(1)} %convolution_convert_fusion.29), channel_id=1, source_target_pairs={{0,4},{4,0},{8,12},{12,8},{1,5},{5,1},{9,13},{13,9},{2,6},{6,2},{1... | collective-permute-start | bytes 491528 | tf_op jit(solution)/shard_map/ppermute | solution.py:22
  58.2 1.9 %copy-start.3 = (bf16[1,128,128]{2,1,0:T(8,128)(2,1)S(1)}, bf16[1,128,128]{2,1,0:T(8,128)(2,1)}, u32[]{:S(2)}) copy-start(bf16[1,128,128]{2,1,0:T(8,128)(2,1)} %param.11) | copy-start | bytes 98308
  58.2 1.9 %copy-start.7 = (bf16[768,128]{0,1:T(8,128)(2,1)S(1)}, bf16[768,128]{0,1:T(8,128)(2,1)}, u32[]{:S(2)}) copy-start(bf16[768,128]{0,1:T(8,128)(2,1)} %convolution_convert_fusion.22) | copy-start | bytes 589828
  58.5 13.9 %collective-permute-start.12 = (bf16[1024,80]{0,1:T(8,128)(2,1)S(1)}, bf16[1024,80]{0,1:T(8,128)(2,1)S(1)}, u32[]{:S(2)}, u32[]{:S(2)}) collective-permute-start(bf16[1024,80]{0,1:T(8,128)(2,1)S(1)} %convolution_convert_fusion.28), channel_id=1, source_target_pairs={{0,8},{8,0},{4,12},{12,4},{1,9},{9,1},{5,13},{13,5},{2,10},{10,2},... | collective-permute-start | bytes 491528 | tf_op jit(solution)/shard_map/ppermute | solution.py:22
  61.3 2.8 %copy-start.5 = (bf16[1024,128]{0,1:T(8,128)(2,1)S(1)}, bf16[1024,128]{0,1:T(8,128)(2,1)}, u32[]{:S(2)}) copy-start(bf16[1024,128]{0,1:T(8,128)(2,1)} %convolution_convert_fusion.15) | copy-start | bytes 786436
  61.6 13.0 %collective-permute-start.16 = (bf16[1024,80]{0,1:T(8,128)(2,1)S(1)}, bf16[1024,80]{0,1:T(8,128)(2,1)S(1)}, u32[]{:S(2)}, u32[]{:S(2)}) collective-permute-start(bf16[1024,80]{0,1:T(8,128)(2,1)S(1)} %convolution_convert_fusion.27), channel_id=1, source_target_pairs={{0,4},{4,0},{8,12},{12,8},{1,5},{5,1},{9,13},{13,9},{2,6},{6,2},{1... | collective-permute-start | bytes 491528 | tf_op jit(solution)/shard_map/ppermute | solution.py:22
  64.3 10.2 %copy-start.6 = (bf16[1024,128]{0,1:T(8,128)(2,1)S(1)}, bf16[1024,128]{0,1:T(8,128)(2,1)}, u32[]{:S(2)}) copy-start(bf16[1024,128]{0,1:T(8,128)(2,1)} %convolution_convert_fusion.10) | copy-start | bytes 786436
  64.3 11.5 %collective-permute-start.15 = (bf16[1024,80]{0,1:T(8,128)(2,1)S(1)}, bf16[1024,80]{0,1:T(8,128)(2,1)S(1)}, u32[]{:S(2)}, u32[]{:S(2)}) collective-permute-start(bf16[1024,80]{0,1:T(8,128)(2,1)S(1)} %convolution_convert_fusion.26), channel_id=1, source_target_pairs={{0,8},{8,0},{4,12},{12,4},{1,9},{9,1},{5,13},{13,5},{2,10},{10,2},... | collective-permute-start | bytes 491528 | tf_op jit(solution)/shard_map/ppermute | solution.py:22
  74.5 1.3 %copy-start.8 = (bf16[1024,128]{0,1:T(8,128)(2,1)S(1)}, bf16[1024,128]{0,1:T(8,128)(2,1)}, u32[]{:S(2)}) copy-start(bf16[1024,128]{0,1:T(8,128)(2,1)} %convolution_convert_fusion.11) | copy-start | bytes 786436
  74.8 6.3 %collective-permute-start.17 = (bf16[1024,80]{0,1:T(8,128)(2,1)S(1)}, bf16[1024,80]{0,1:T(8,128)(2,1)S(1)}, u32[]{:S(2)}, u32[]{:S(2)}) collective-permute-start(bf16[1024,80]{0,1:T(8,128)(2,1)S(1)} %convolution_convert_fusion.25), channel_id=1, source_target_pairs={{0,8},{8,0},{4,12},{12,4},{1,9},{9,1},{5,13},{13,5},{2,10},{10,2},... | collective-permute-start | bytes 491528 | tf_op jit(solution)/shard_map/ppermute | solution.py:22
  75.8 5.2 %copy-start.9 = (bf16[1024,128]{0,1:T(8,128)(2,1)S(1)}, bf16[1024,128]{0,1:T(8,128)(2,1)}, u32[]{:S(2)}) copy-start(bf16[1024,128]{0,1:T(8,128)(2,1)} %convolution_convert_fusion.7) | copy-start | bytes 786436

commit v4 on v0

v4 whole, which is shorter than its diff:
```python
import jax
import jax.numpy as jnp
from jax import lax
from jax.sharding import PartitionSpec as P

SIXTEENTHS = (1, 3, 4, 4, 4)
COUNT_PIECE = 2
ROOM_SIXTEENTHS = 12
EXTRA = 128


def route(axis, apart):
    count = lax.axis_size(axis)
    pairs = []
    for low in range(count):
        high = low | 1 << apart
        if high != low and high < count:
            pairs += [(low, high), (high, low)]
    return pairs


def from_partner(block, hop):
    return lax.ppermute(block, hop[0], route(*hop))


def real_form(both):
    rank = both.shape[1] // 2
    turned = jnp.concatenate([-both[:, rank:], both[:, :rank]], 1)
    return jnp.concatenate([both, turned], 2)


def picked_columns(compress, skeleton):
    rank = skeleton.shape[-1]
    places = lax.broadcasted_iota(jnp.int32, (1, 1, 2 * rank), 2)
    chooser = (skeleton[:, :, None] == places).astype(jnp.bfloat16)
    stacked = jnp.concatenate([compress[:, :, :rank], compress[:, :, rank:]], 1)
    return jnp.einsum(
        "ljk,lki->lji", stacked, chooser, preferred_element_type=jnp.float32
    ).astype(jnp.bfloat16)


def slots(skeleton, room):
    rank = skeleton.shape[-1]
    places = rank + lax.broadcasted_iota(jnp.int32, (1, 1, rank), 2)
    picked = jnp.any(skeleton[:, :, None] == places, 1)
    before = lax.broadcasted_iota(jnp.int32, (rank, rank), 0) < lax.broadcasted_iota(
        jnp.int32, (rank, rank), 1
    )
    slot = jnp.sum(before[None] & picked[:, :, None], 1, dtype=jnp.int32)
    index = lax.broadcasted_iota(jnp.int32, (1, room, 1), 1)
    return (picked[:, None] & (slot[:, None] == index)).astype(jnp.bfloat16)


def compact_rows(matrix, slot):
    rank = slot.shape[1]
    parts = [
        jnp.dot(slot, half, preferred_element_type=jnp.float32)
        for half in (matrix[:rank], matrix[rank:])
    ]
    return jnp.concatenate(parts, 0).astype(jnp.bfloat16)


def times(matrix, value):
    return jnp.dot(matrix, value, preferred_element_type=jnp.float32).astype(jnp.bfloat16)


def sampled(sampling, traces):
    return jnp.einsum(
        "pc,tp->ct", sampling, traces, preferred_element_type=jnp.float32
    ).astype(jnp.bfloat16)


def evaluated(coeffs, evaluation):
    return jnp.einsum(
        "ct,cp->tp", coeffs, evaluation, preferred_element_type=jnp.float32
    ).astype(jnp.bfloat16)


def after(value, earlier):
    return value if earlier is None else lax.optimization_barrier((value, earlier))[0]


def all_hops():
    low_bits = lax.axis_size("sub").bit_length() - 1
    high_bits = lax.axis_size("bfly").bit_length() - 1
    return [("sub", bit) for bit in range(low_bits)] + [("bfly", bit) for bit in range(high_bits)]


def full_width(traces, sampling, full, evaluation):
    coeffs = sampled(sampling, traces)
    for level, hop in enumerate(all_hops()):
        partner = from_partner(coeffs, hop)
        coeffs = times(full[level], jnp.concatenate([coeffs, partner], 0))
    return evaluated(coeffs, evaluation)


def sequence(pieces, levels):
    def turn(at):
        level, piece = at
        if level == 0:
            return max(0, 2 * piece - 1)
        return 2 * (level + piece + (piece > 0))

    return sorted(
        [(level, piece) for level in range(levels + 1) for piece in range(pieces)],
        key=lambda at: (turn(at), at),
    )


def local(traces, sampling, skeleton, compress, evaluation):
    sampling, skeleton, compress, evaluation = sampling[0], skeleton[0], compress[0], evaluation[0]
    hops = all_hops()
    levels = len(hops)
    wide = lax.axis_size("sub").bit_length() - 1
    rank = skeleton.shape[-1]
    room = rank * ROOM_SIXTEENTHS // 16

    columns = picked_columns(compress, skeleton)
    slot = slots(skeleton, room)
    full = jnp.concatenate([real_form(columns[..., :rank]), real_form(columns[..., rank:])], 2)
    kept = jnp.einsum(
        "lcr,ljr->lcj", columns[..., rank:], slot, preferred_element_type=jnp.float32
    ).astype(jnp.bfloat16)
    small = jnp.concatenate([real_form(columns[..., :rank]), real_form(kept)], 2)
    small = jnp.pad(small, ((0, 0), (0, 0), (0, full.shape[2] - small.shape[2])))
    most = jnp.max(jnp.sum(skeleton[wide:] >= rank, -1)).astype(jnp.bfloat16)

    def compact(level, piece):
        return piece > 0 and level >= wide

    unit = traces.shape[0] // sum(SIXTEENTHS)
    pieces = len(SIXTEENTHS)
    starts = [unit * sum(SIXTEENTHS[:i]) for i in range(pieces + 1)]
    inputs, partners, theirs, done = {}, {}, {}, [None] * pieces
    previous = None
    for level, piece in sequence(pieces, levels):
        count = starts[piece + 1] - starts[piece]
        if level == 0:
            block = traces[starts[piece] : starts[piece + 1]]
            if piece > 1:
                block = after(block, previous)
            own = sampled(sampling, block)
        else:
            arrived = after(partners[piece], previous)
            if piece == 0 and level - 1 >= wide:
                theirs[level - 1] = arrived[:room, count : count + rank]
            if piece == COUNT_PIECE:
                most = jnp.maximum(most, arrived[0, count])
            value = jnp.concatenate([inputs[piece], arrived[:, :count]], 0)
            matrix = full[level - 1]
            if compact(level - 1, piece):
                value = jnp.pad(value, ((0, full.shape[2] - value.shape[0]), (0, 0)))
                matrix = small[level - 1]
            own = times(matrix, value)
        if level == levels:
            done[piece] = evaluated(own, evaluation)
            continue
        outgoing = own
        if compact(level, piece):
            outgoing = times(compact_rows(matrix, theirs[level]), value)
        if piece == 0 and level >= wide:
            extra = jnp.pad(slot[level], ((0, 2 * rank - room), (0, EXTRA - rank)))
            outgoing = jnp.concatenate([outgoing, extra], 1)
        if piece == COUNT_PIECE:
            extra = jnp.broadcast_to(most, (outgoing.shape[0], EXTRA))
            outgoing = jnp.concatenate([outgoing, extra], 1)
        inputs[piece] = own
        partners[piece] = from_partner(outgoing, hops[level])
        previous = outgoing
    quick = jnp.concatenate(done, 0)
    return lax.cond(
        most > room,
        lambda: full_width(traces, sampling, full, evaluation),
        lambda: quick,
    )


def solution(mesh):
    placed = (
        P(("shots", "tr"), ("bfly", "sub")),
        P(("bfly", "sub"), None, None),
        P(("bfly", "sub"), None, None),
        P(("bfly", "sub"), None, None, None),
        P(("bfly", "sub"), None, None),
    )
    return jax.shard_map(
        local,
        mesh=mesh,
        in_specs=placed,
        out_specs=P(("shots", "tr"), ("bfly", "sub")),
        check_vma=False,
    )
```

time: 103 us -> 69.7 us (0.68)
  waiting for transfers between devices: 89 us -> 9.13 us
  matrix products: 5.22 us -> 30.1 us
  starting transfers between devices: 7.49 us -> 21.5 us
  between operations: 0.06 us -> 2.95 us
  local copies, waits for them, and re-layouts: 1.24 us -> 3.51 us
  other arithmetic: 0.23 us -> 2.01 us
    ppermute x3 -> x15, waiting for transfers between devices: 89 us -> 9.13 us  [from_partner(): return lax.ppermute(block, hop[0], route(*hop))]
    dot_general x8 -> x34, matrix products: 5.22 us -> 30.1 us  [the longest x18 18.2 us: times(): jnp.dot(matrix, value, preferred_element_type=jnp.float32)]
    ppermute x3 -> x15, starting transfers between devices: 7.49 us -> 21.5 us  [from_partner(): return lax.ppermute(block, hop[0], route(*hop))]
    slice x3 -> x11, local copies, waits for them, and re-layouts: 0.01 us -> 1.79 us  [the longest x3 1.64 us: local(): most = jnp.maximum(most, arrived[0, count])]
  transfers between devices with their start and end apart: 3 -> 15, of which waited for: 3 -> 6; matrix products, arithmetic and copies ran while one was open for 1% -> 48% of each run, Pallas kernels for 0% -> 0%
where the time goes in v4:
time: 69.7 us; the launch traced here: 69.1 us
  matrix products  30.1 us (43%)
  starting transfers between devices  21.5 us (31%)
  waiting for transfers between devices  9.13 us (13%)
  local copies, waits for them, and re-layouts  3.51 us (5%)
  between operations  2.95 us (4%)
  other arithmetic  2.01 us (3%)
    ppermute x15, starting transfers between devices, from_partner(): return lax.ppermute(block, hop[0], route(*hop))  21.5 us
    dot_general x18, matrix products, times(): jnp.dot(matrix, value, preferred_element_type=jnp.float32)  18.2 us
    ppermute x15, waiting for transfers between devices, from_partner(): return lax.ppermute(block, hop[0], route(*hop))  9.13 us
    dot_general x5, matrix products, evaluated(): jnp.einsum('ct,cp->tp', coeffs, evaluation, preferred_element_type=jnp.fl...  7.66 us
    dot_general x5, matrix products, sampled(): jnp.einsum('pc,tp->ct', sampling, traces, preferred_element_type=jnp.floa...  3.09 us
    unnamed x22, local copies, waits for them, and re-layouts  1.65 us
    slice x3, local copies, waits for them, and re-layouts, local(): most = jnp.maximum(most, arrived[0, count])  1.64 us
  transfers between devices with their start and end apart: 15, of which 6 were waited for; matrix products, arithmetic and copies ran while one was open for 48% of the time, Pallas kernels for 0%

profile of v4, /device:TPU:0, one launch (start us, length us, event | category | flops | bytes accessed | tf_op | source)
XLA Modules:
  0.0 69.1 jit_solution(8675209617438366660)
XLA Ops:
  0.0 1.1 %convolution_convert_fusion.35 = bf16[128,256]{1,0:T(8,128)(2,1)S(1)} fusion(bf16[4096,128]{1,0:T(8,128)(2,1)} %param.7, bf16[1,128,128]{2,1,0:T(8,128)(2,1)} %param.8), kind=kOutput, calls=%fused_computation.60 | convolution fusion | flops 8421376 | bytes 163840 | tf_op jit(solution)/shard_map/pc,tp->ct/dot_general | solution.py:68
  1.1 3.0 %collective-permute-start.3 = (bf16[128,256]{1,0:T(8,128)(2,1)S(1)}, bf16[128,256]{1,0:T(8,128)(2,1)S(1)}, u32[]{:S(2)}, u32[]{:S(2)}) collective-permute-start(bf16[128,256]{1,0:T(8,128)(2,1)S(1)} %convolution_convert_fusion.35), channel_id=1, source_target_pairs={{0,2},{2,0},{1,3},{3,1},{4,6},{6,4},{5,7},{7,5},{8,10},{10,8},{9,1... | collective-permute-start | bytes 196616 | tf_op jit(solution)/shard_map/ppermute | solution.py:23
  4.1 1.2 %convolution_convert_fusion.30 = bf16[128,768]{1,0:T(8,128)(2,1)S(1)} fusion(bf16[4096,128]{1,0:T(8,128)(2,1)} %param.7, bf16[1,128,128]{2,1,0:T(8,128)(2,1)} %param.8), kind=kOutput, calls=%fused_computation.51 | convolution fusion | flops 25264128 | bytes 425984 | tf_op jit(solution)/shard_map/pc,tp->ct/dot_general | solution.py:68
  10.5 2.2 %collective-permute-start.5 = (bf16[128,384]{1,0:T(8,128)(2,1)S(1)}, bf16[128,384]{1,0:T(8,128)(2,1)S(1)}, u32[]{:S(2)}, u32[]{:S(2)}) collective-permute-start(bf16[128,384]{1,0:T(8,128)(2,1)S(1)} %fusion.131), channel_id=1, source_target_pairs={{0,4},{4,0},{8,12},{12,8},{1,5},{5,1},{9,13},{13,9},{2,6},{6,2},{1... | collective-permute-start | bytes 294920 | tf_op jit(solution)/shard_map/ppermute | solution.py:23
  13.0 1.6 %collective-permute-start.4 = (bf16[128,1152]{1,0:T(8,128)(2,1)S(1)}, bf16[128,1152]{1,0:T(8,128)(2,1)S(1)}, u32[]{:S(2)}, u32[]{:S(2)}) collective-permute-start(bf16[128,1152]{1,0:T(8,128)(2,1)S(1)} %concatenate.114), channel_id=1, source_target_pairs={{0,2},{2,0},{1,3},{3,1},{4,6},{6,4},{5,7},{7,5},{8,10},{10,8},{9,1... | collective-permute-start | bytes 884744 | tf_op jit(solution)/shard_map/ppermute | solution.py:23
  15.7 3.1 %collective-permute-start.9 = (bf16[128,384]{1,0:T(8,128)(2,1)S(1)}, bf16[128,384]{1,0:T(8,128)(2,1)S(1)}, u32[]{:S(2)}, u32[]{:S(2)}) collective-permute-start(bf16[128,384]{1,0:T(8,128)(2,1)S(1)} %fusion.132), channel_id=1, source_target_pairs={{0,8},{8,0},{4,12},{12,4},{1,9},{9,1},{5,13},{13,5},{2,10},{10,2},... | collective-permute-start | bytes 294920 | tf_op jit(solution)/shard_map/ppermute | solution.py:23
  19.1 1.6 %collective-permute-start.8 = (bf16[128,1024]{1,0:T(8,128)(2,1)S(1)}, bf16[128,1024]{1,0:T(8,128)(2,1)}, u32[]{:S(2)}, u32[]{:S(2)}) collective-permute-start(bf16[128,1024]{1,0:T(8,128)(2,1)S(1)} %fusion.22), channel_id=1, source_target_pairs={{0,2},{2,0},{1,3},{3,1},{4,6},{6,4},{5,7},{7,5},{8,10},{10,8},{9,1... | collective-permute-start | bytes 786440 | tf_op jit(solution)/shard_map/ppermute | solution.py:23
  20.8 1.9 %convolution_convert_fusion.28 = bf16[128,768]{1,0:T(8,128)(2,1)} fusion(bf16[128,768]{1,0:T(8,128)(2,1)} %collective-permute-done.6, bf16[128,768]{1,0:T(8,128)(2,1)S(1)} %convolution_convert_fusion.30, bf16[3,128,256]{1,2,0:T(8,128)(2,1)S(1)} %get-tuple-element.70), kind=kOutput, calls=%fused_computation.49 | convolution fusion | flops 51216384 | bytes 655360 | tf_op jit(solution)/shard_map/dot_general | solution.py:64
  22.7 1.8 %convolution_convert_fusion.32 = bf16[96,768]{1,0:T(8,128)(2,1)} fusion(bf16[128,768]{1,0:T(8,128)(2,1)} %collective-permute-done.6, bf16[128,768]{1,0:T(8,128)(2,1)S(1)} %convolution_convert_fusion.30, bf16[48,256]{1,0:T(8,128)(2,1)S(1)} %convolution_convert_fusion.42, bf16[48,256]{1,0:T(8,128)(2,1)S(1)} %convolution_convert_fusion.43), kind=kOutput, calls=%fused_computation.56 | convolution fusion | flops 38707200 | bytes 589824 | tf_op jit(solution)/shard_map/dot_general | solution.py:64
  24.4 1.6 %collective-permute-start.10 = (bf16[96,768]{1,0:T(8,128)(2,1)}, bf16[96,768]{1,0:T(8,128)(2,1)}, u32[]{:S(2)}, u32[]{:S(2)}) collective-permute-start(bf16[96,768]{1,0:T(8,128)(2,1)} %convolution_convert_fusion.32), channel_id=1, source_target_pairs={{0,4},{4,0},{8,12},{12,8},{1,5},{5,1},{9,13},{13,9},{2,6},{6,2},{1... | collective-permute-start | bytes 442376 | tf_op jit(solution)/shard_map/ppermute | solution.py:23
  26.9 1.0 %fusion.24 = bf16[4096,128]{1,0:T(8,128)(2,1)} fusion(bf16[128,256]{1,0:T(8,128)(2,1)S(1)} %slice.204, bf16[128,256]{1,0:T(8,128)(2,1)S(1)} %convolution_convert_fusion.37, bf16[3,128,256]{1,2,0:T(8,128)(2,1)S(1)} %get-tuple-element.70, bf16[1,128,128]{2,1,0:T(8,128)(2,1)S(1)} %copy-done.2), kind=kOutput, calls=%fused_computation.59 | convolution fusion | flops 25493504 | bytes 294912 | tf_op jit(solution)/shard_map/ct,cp->tp/dot_general | solution.py:74
  30.5 1.9 %convolution_convert_fusion.23 = bf16[128,768]{1,0:T(8,128)(2,1)} fusion(bf16[96,768]{1,0:T(8,128)(2,1)} %collective-permute-done.10, bf16[128,768]{1,0:T(8,128)(2,1)} %convolution_convert_fusion.28, bf16[3,128,256]{1,2,0:T(8,128)(2,1)S(1)} %get-tuple-element.69), kind=kOutput, calls=%fused_computation.44 | convolution fusion | flops 51806208 | bytes 606208 | tf_op jit(solution)/shard_map/dot_general | solution.py:64
  32.4 1.1 %convolution_convert_fusion.31 = bf16[96,768]{1,0:T(8,128)(2,1)S(1)} fusion(bf16[96,768]{1,0:T(8,128)(2,1)} %collective-permute-done.10, bf16[128,768]{1,0:T(8,128)(2,1)S(1)} %copy-done.3, bf16[48,256]{1,0:T(8,128)(2,1)S(1)} %convolution_convert_fusion.40, bf16[48,256]{1,0:T(8,128)(2,1)S(1)} %convolution_convert_fusion.41), kind=kOutput, calls=%fused_computation.55 | convolution fusion | flops 39297024 | bytes 540672 | tf_op jit(solution)/shard_map/dot_general | solution.py:64
  34.2 1.3 %convolution_convert_fusion.27 = bf16[96,1024]{1,0:T(8,128)(2,1)S(1)} fusion(bf16[128,1024]{1,0:T(8,128)(2,1)} %collective-permute-done.8, bf16[128,1024]{1,0:T(8,128)(2,1)S(1)} %fusion.22, bf16[48,256]{1,0:T(8,128)(2,1)S(1)} %convolution_convert_fusion.42, bf16[48,256]{1,0:T(8,128)(2,1)S(1)} %convolution_convert_fusion.43), kind=kOutput, calls=%fused_computation.48 | convolution fusion | flops 51576832 | bytes 770048 | tf_op jit(solution)/shard_map/dot_general | solution.py:64
  35.5 2.6 %collective-permute-start.12 = (bf16[96,1024]{1,0:T(8,128)(2,1)S(1)}, bf16[96,1024]{1,0:T(8,128)(2,1)S(1)}, u32[]{:S(2)}, u32[]{:S(2)}) collective-permute-start(bf16[96,1024]{1,0:T(8,128)(2,1)S(1)} %convolution_convert_fusion.27), channel_id=1, source_target_pairs={{0,4},{4,0},{8,12},{12,8},{1,5},{5,1},{9,13},{13,9},{2,6},{6,2},{1... | collective-permute-start | bytes 589832 | tf_op jit(solution)/shard_map/ppermute | solution.py:23
  38.0 1.9 %convolution_convert_fusion.15 = bf16[128,1024]{1,0:T(8,128)(2,1)} fusion(bf16[128,1024]{1,0:T(8,128)(2,1)} %collective-permute-done.8, bf16[128,1024]{1,0:T(8,128)(2,1)S(1)} %fusion.22, bf16[3,128,256]{1,2,0:T(8,128)(2,1)S(1)} %get-tuple-element.70), kind=kOutput, calls=%fused_computation.35 | convolution fusion | flops 68288512 | bytes 851968 | tf_op jit(solution)/shard_map/dot_general | solution.py:64
  39.9 1.2 %collective-permute-done.7 = bf16[96,1152]{1,0:T(8,128)(2,1)S(1)} collective-permute-done((bf16[96,1152]{1,0:T(8,128)(2,1)S(1)}, bf16[96,1152]{1,0:T(8,128)(2,1)S(1)}, u32[]{:S(2)}, u32[]{:S(2)}) %collective-permute-start.7) | collective-permute-done | bytes 221216 | tf_op jit(solution)/shard_map/ppermute | solution.py:23
  42.6 1.4 %collective-permute-start.11 = (bf16[96,1152]{1,0:T(8,128)(2,1)S(1)}, bf16[96,1152]{1,0:T(8,128)(2,1)S(1)}, u32[]{:S(2)}, u32[]{:S(2)}) collective-permute-start(bf16[96,1152]{1,0:T(8,128)(2,1)S(1)} %concatenate.127), channel_id=1, source_target_pairs={{0,8},{8,0},{4,12},{12,4},{1,9},{9,1},{5,13},{13,5},{2,10},{10,2},... | collective-permute-start | bytes 663560 | tf_op jit(solution)/shard_map/ppermute | solution.py:23
  44.0 1.9 %convolution_convert_fusion.14 = bf16[128,1024]{1,0:T(8,128)(2,1)} fusion(bf16[96,1024]{1,0:T(8,128)(2,1)S(1)} %slice.201, bf16[128,1024]{1,0:T(8,128)(2,1)} %copy-done.7, bf16[3,128,256]{1,2,0:T(8,128)(2,1)S(1)} %get-tuple-element.69), kind=kOutput, calls=%fused_computation.34 | convolution fusion | flops 69074944 | bytes 786432 | tf_op jit(solution)/shard_map/dot_general | solution.py:64
  45.9 1.9 %convolution_convert_fusion.10 = bf16[128,1024]{1,0:T(8,128)(2,1)} fusion(bf16[128,1024]{1,0:T(8,128)(2,1)} %collective-permute-done.13, bf16[128,1024]{1,0:T(8,128)(2,1)S(1)} %fusion.23, bf16[3,128,256]{1,2,0:T(8,128)(2,1)S(1)} %get-tuple-element.70), kind=kOutput, calls=%fused_computation.29 | convolution fusion | flops 68288512 | bytes 851968 | tf_op jit(solution)/shard_map/dot_general | solution.py:64
  47.8 1.2 %convolution_convert_fusion.25 = bf16[96,1024]{1,0:T(8,128)(2,1)S(1)} fusion(bf16[128,1024]{1,0:T(8,128)(2,1)} %collective-permute-done.13, bf16[128,1024]{1,0:T(8,128)(2,1)S(1)} %fusion.23, bf16[48,256]{1,0:T(8,128)(2,1)S(1)} %convolution_convert_fusion.42, bf16[48,256]{1,0:T(8,128)(2,1)S(1)} %convolution_convert_fusion.43), kind=kOutput, calls=%fused_computation.46 | convolution fusion | flops 51576832 | bytes 770048 | tf_op jit(solution)/shard_map/dot_general | solution.py:64
  49.1 2.1 %fusion.20 = bf16[4096,128]{1,0:T(8,128)(2,1)} fusion(bf16[4096,128]{1,0:T(8,128)(2,1)} %fusion.24, bf16[96,768]{1,0:T(8,128)(2,1)S(1)} %collective-permute-done.14, bf16[128,768]{1,0:T(8,128)(2,1)} %convolution_convert_fusion.23, bf16[3,128,256]{1,2,0:T(8,128)(2,1)S(1)} %get-tuple-element.69, bf16[1,128,128]{2,1,0:T(8,128)(2,1)S(1)} %copy-done.2), kind=kOutput, calls=%fused_computation.42 | convolution fusion | flops 77070336 | bytes 638976 | tf_op jit(solution)/shard_map/ct,cp->tp/dot_general | solution.py:74
  51.4 1.7 %collective-permute-start.15 = (bf16[96,1024]{1,0:T(8,128)(2,1)S(1)}, bf16[96,1024]{1,0:T(8,128)(2,1)S(1)}, u32[]{:S(2)}, u32[]{:S(2)}) collective-permute-start(bf16[96,1024]{1,0:T(8,128)(2,1)S(1)} %convolution_convert_fusion.24), channel_id=1, source_target_pairs={{0,8},{8,0},{4,12},{12,4},{1,9},{9,1},{5,13},{13,5},{2,10},{10,2},... | collective-permute-start | bytes 589832 | tf_op jit(solution)/shard_map/ppermute | solution.py:23
  53.1 1.0 %convolution_convert_fusion.11 = bf16[128,1024]{1,0:T(8,128)(2,1)} fusion(bf16[96,1024]{1,0:T(8,128)(2,1)S(1)} %collective-permute-done.12, bf16[128,1024]{1,0:T(8,128)(2,1)S(1)} %copy-done.5, bf16[3,128,256]{1,2,0:T(8,128)(2,1)S(1)} %get-tuple-element.69), kind=kOutput, calls=%fused_computation.30 | convolution fusion | flops 69074944 | bytes 786432 | tf_op jit(solution)/shard_map/dot_general | solution.py:64
  54.0 3.1 %collective-permute-done.16 = bf16[96,1024]{1,0:T(8,128)(2,1)S(1)} collective-permute-done((bf16[96,1024]{1,0:T(8,128)(2,1)S(1)}, bf16[96,1024]{1,0:T(8,128)(2,1)S(1)}, u32[]{:S(2)}, u32[]{:S(2)}) %collective-permute-start.16) | collective-permute-done | bytes 196640 | tf_op jit(solution)/shard_map/ppermute | solution.py:23
  57.3 1.2 %collective-permute-start.17 = (bf16[96,1024]{1,0:T(8,128)(2,1)S(1)}, bf16[96,1024]{1,0:T(8,128)(2,1)S(1)}, u32[]{:S(2)}, u32[]{:S(2)}) collective-permute-start(bf16[96,1024]{1,0:T(8,128)(2,1)S(1)} %convolution_convert_fusion.20), channel_id=1, source_target_pairs={{0,8},{8,0},{4,12},{12,4},{1,9},{9,1},{5,13},{13,5},{2,10},{10,2},... | collective-permute-start | bytes 589832 | tf_op jit(solution)/shard_map/ppermute | solution.py:23
  58.5 0.9 %convolution_convert_fusion.7 = bf16[128,1024]{1,0:T(8,128)(2,1)} fusion(bf16[96,1024]{1,0:T(8,128)(2,1)S(1)} %collective-permute-done.16, bf16[128,1024]{1,0:T(8,128)(2,1)S(1)} %copy-done.6, bf16[3,128,256]{1,2,0:T(8,128)(2,1)S(1)} %get-tuple-element.69), kind=kOutput, calls=%fused_computation.25 | convolution fusion | flops 69074944 | bytes 786432 | tf_op jit(solution)/shard_map/dot_general | solution.py:64
  60.7 2.2 %fusion.19 = bf16[4096,128]{1,0:T(8,128)(2,1)} fusion(bf16[4096,128]{1,0:T(8,128)(2,1)} %fusion.20, bf16[96,1024]{1,0:T(8,128)(2,1)S(1)} %slice.207, bf16[128,1024]{1,0:T(8,128)(2,1)} %convolution_convert_fusion.14, bf16[3,128,256]{1,2,0:T(8,128)(2,1)S(1)} %get-tuple-element.69, bf16[1,128,128]{2,1,0:T(8,128)(2,1)S(1)} %copy-done.2), kind=kOutput, calls=%fused_computation.32 | convolution fusion | flops 102760448 | bytes 819200 | tf_op jit(solution)/shard_map/ct,cp->tp/dot_general | solution.py:74
  62.8 2.7 %collective-permute-done.15 = bf16[96,1024]{1,0:T(8,128)(2,1)S(1)} collective-permute-done((bf16[96,1024]{1,0:T(8,128)(2,1)S(1)}, bf16[96,1024]{1,0:T(8,128)(2,1)S(1)}, u32[]{:S(2)}, u32[]{:S(2)}) %collective-permute-start.15) | collective-permute-done | bytes 196640 | tf_op jit(solution)/shard_map/ppermute | solution.py:23
  65.5 1.2 %fusion.18 = bf16[4096,128]{1,0:T(8,128)(2,1)} fusion(bf16[4096,128]{1,0:T(8,128)(2,1)} %fusion.19, bf16[96,1024]{1,0:T(8,128)(2,1)S(1)} %collective-permute-done.15, bf16[128,1024]{1,0:T(8,128)(2,1)S(1)} %copy-done.8, bf16[3,128,256]{1,2,0:T(8,128)(2,1)S(1)} %get-tuple-element.69, bf16[1,128,128]{2,1,0:T(8,128)(2,1)S(1)} %copy-done.2), kind=kOutput, calls=%fused_computation.27 | convolution fusion | flops 102760448 | bytes 819200 | tf_op jit(solution)/shard_map/ct,cp->tp/dot_general | solution.py:74
  66.7 1.2 %collective-permute-done.17 = bf16[96,1024]{1,0:T(8,128)(2,1)S(1)} collective-permute-done((bf16[96,1024]{1,0:T(8,128)(2,1)S(1)}, bf16[96,1024]{1,0:T(8,128)(2,1)S(1)}, u32[]{:S(2)}, u32[]{:S(2)}) %collective-permute-start.17) | collective-permute-done | bytes 196640 | tf_op jit(solution)/shard_map/ppermute | solution.py:23
  67.9 1.2 %fusion.17 = bf16[4096,128]{1,0:T(8,128)(2,1)} fusion(bf16[4096,128]{1,0:T(8,128)(2,1)} %fusion.18, bf16[96,1024]{1,0:T(8,128)(2,1)S(1)} %collective-permute-done.17, bf16[128,1024]{1,0:T(8,128)(2,1)S(1)} %copy-done.9, bf16[3,128,256]{1,2,0:T(8,128)(2,1)S(1)} %get-tuple-element.69, bf16[1,128,128]{2,1,0:T(8,128)(2,1)S(1)} %copy-done.2), kind=kOutput, calls=%fused_computation.23 | convolution fusion | flops 102760448 | bytes 819200 | tf_op jit(solution)/shard_map/ct,cp->tp/dot_general | solution.py:74
  (82 shorter events, 11.6 us)
Async XLA Ops:
  0.0 8.7 %copy-start = (bf16[4096,128]{1,0:T(8,128)(2,1)S(1)}, bf16[4096,128]{1,0:T(8,128)(2,1)}, u32[]{:S(2)}) copy-start(bf16[4096,128]{1,0:T(8,128)(2,1)} %param.7) | copy-start | bytes 3145732
  1.1 9.2 %collective-permute-start.3 = (bf16[128,256]{1,0:T(8,128)(2,1)S(1)}, bf16[128,256]{1,0:T(8,128)(2,1)S(1)}, u32[]{:S(2)}, u32[]{:S(2)}) collective-permute-start(bf16[128,256]{1,0:T(8,128)(2,1)S(1)} %convolution_convert_fusion.35), channel_id=1, source_target_pairs={{0,2},{2,0},{1,3},{3,1},{4,6},{6,4},{5,7},{7,5},{8,10},{10,8},{9,1... | collective-permute-start | bytes 196616 | tf_op jit(solution)/shard_map/ppermute | solution.py:23
  5.3 15.5 %collective-permute-start.6 = (bf16[128,768]{1,0:T(8,128)(2,1)S(1)}, bf16[128,768]{1,0:T(8,128)(2,1)}, u32[]{:S(2)}, u32[]{:S(2)}) collective-permute-start(bf16[128,768]{1,0:T(8,128)(2,1)S(1)} %convolution_convert_fusion.30), channel_id=1, source_target_pairs={{0,2},{2,0},{1,3},{3,1},{4,6},{6,4},{5,7},{7,5},{8,10},{10,8},{9,1... | collective-permute-start | bytes 589832 | tf_op jit(solution)/shard_map/ppermute | solution.py:23
  8.8 3.9 %copy-start.1 = (bf16[1,128,128]{2,1,0:T(8,128)(2,1)S(1)}, bf16[1,128,128]{2,1,0:T(8,128)(2,1)}, u32[]{:S(2)}) copy-start(bf16[1,128,128]{2,1,0:T(8,128)(2,1)} %param.8) | copy-start | bytes 98308
  10.5 4.8 %collective-permute-start.5 = (bf16[128,384]{1,0:T(8,128)(2,1)S(1)}, bf16[128,384]{1,0:T(8,128)(2,1)S(1)}, u32[]{:S(2)}, u32[]{:S(2)}) collective-permute-start(bf16[128,384]{1,0:T(8,128)(2,1)S(1)} %fusion.131), channel_id=1, source_target_pairs={{0,4},{4,0},{8,12},{12,8},{1,5},{5,1},{9,13},{13,9},{2,6},{6,2},{1... | collective-permute-start | bytes 294920 | tf_op jit(solution)/shard_map/ppermute | solution.py:23
  13.0 15.3 %collective-permute-start.4 = (bf16[128,1152]{1,0:T(8,128)(2,1)S(1)}, bf16[128,1152]{1,0:T(8,128)(2,1)S(1)}, u32[]{:S(2)}, u32[]{:S(2)}) collective-permute-start(bf16[128,1152]{1,0:T(8,128)(2,1)S(1)} %concatenate.114), channel_id=1, source_target_pairs={{0,2},{2,0},{1,3},{3,1},{4,6},{6,4},{5,7},{7,5},{8,10},{10,8},{9,1... | collective-permute-start | bytes 884744 | tf_op jit(solution)/shard_map/ppermute | solution.py:23
  15.7 11.2 %collective-permute-start.9 = (bf16[128,384]{1,0:T(8,128)(2,1)S(1)}, bf16[128,384]{1,0:T(8,128)(2,1)S(1)}, u32[]{:S(2)}, u32[]{:S(2)}) collective-permute-start(bf16[128,384]{1,0:T(8,128)(2,1)S(1)} %fusion.132), channel_id=1, source_target_pairs={{0,8},{8,0},{4,12},{12,4},{1,9},{9,1},{5,13},{13,5},{2,10},{10,2},... | collective-permute-start | bytes 294920 | tf_op jit(solution)/shard_map/ppermute | solution.py:23
  19.1 15.1 %collective-permute-start.8 = (bf16[128,1024]{1,0:T(8,128)(2,1)S(1)}, bf16[128,1024]{1,0:T(8,128)(2,1)}, u32[]{:S(2)}, u32[]{:S(2)}) collective-permute-start(bf16[128,1024]{1,0:T(8,128)(2,1)S(1)} %fusion.22), channel_id=1, source_target_pairs={{0,2},{2,0},{1,3},{3,1},{4,6},{6,4},{5,7},{7,5},{8,10},{10,8},{9,1... | collective-permute-start | bytes 786440 | tf_op jit(solution)/shard_map/ppermute | solution.py:23
  20.8 6.1 %copy-start.2 = (bf16[1,128,128]{2,1,0:T(8,128)(2,1)S(1)}, bf16[1,128,128]{2,1,0:T(8,128)(2,1)}, u32[]{:S(2)}) copy-start(bf16[1,128,128]{2,1,0:T(8,128)(2,1)} %param.11) | copy-start | bytes 98308
  24.4 6.0 %collective-permute-start.10 = (bf16[96,768]{1,0:T(8,128)(2,1)}, bf16[96,768]{1,0:T(8,128)(2,1)}, u32[]{:S(2)}, u32[]{:S(2)}) collective-permute-start(bf16[96,768]{1,0:T(8,128)(2,1)} %convolution_convert_fusion.32), channel_id=1, source_target_pairs={{0,4},{4,0},{8,12},{12,8},{1,5},{5,1},{9,13},{13,9},{2,6},{6,2},{1... | collective-permute-start | bytes 442376 | tf_op jit(solution)/shard_map/ppermute | solution.py:23
  26.3 19.6 %collective-permute-start.13 = (bf16[128,1024]{1,0:T(8,128)(2,1)S(1)}, bf16[128,1024]{1,0:T(8,128)(2,1)}, u32[]{:S(2)}, u32[]{:S(2)}) collective-permute-start(bf16[128,1024]{1,0:T(8,128)(2,1)S(1)} %fusion.23), channel_id=1, source_target_pairs={{0,2},{2,0},{1,3},{3,1},{4,6},{6,4},{5,7},{7,5},{8,10},{10,8},{9,1... | collective-permute-start | bytes 786440 | tf_op jit(solution)/shard_map/ppermute | solution.py:23
  29.8 2.6 %copy-start.3 = (bf16[128,768]{1,0:T(8,128)(2,1)S(1)}, bf16[128,768]{1,0:T(8,128)(2,1)}, u32[]{:S(2)}) copy-start(bf16[128,768]{1,0:T(8,128)(2,1)} %convolution_convert_fusion.28) | copy-start | bytes 589828
  29.8 11.3 %collective-permute-start.7 = (bf16[96,1152]{1,0:T(8,128)(2,1)S(1)}, bf16[96,1152]{1,0:T(8,128)(2,1)S(1)}, u32[]{:S(2)}, u32[]{:S(2)}) collective-permute-start(bf16[96,1152]{1,0:T(8,128)(2,1)S(1)} %concatenate.120), channel_id=1, source_target_pairs={{0,4},{4,0},{8,12},{12,8},{1,5},{5,1},{9,13},{13,9},{2,6},{6,2},{1... | collective-permute-start | bytes 663560 | tf_op jit(solution)/shard_map/ppermute | solution.py:23
  33.5 15.5 %collective-permute-start.14 = (bf16[96,768]{1,0:T(8,128)(2,1)S(1)}, bf16[96,768]{1,0:T(8,128)(2,1)S(1)}, u32[]{:S(2)}, u32[]{:S(2)}) collective-permute-start(bf16[96,768]{1,0:T(8,128)(2,1)S(1)} %convolution_convert_fusion.31), channel_id=1, source_target_pairs={{0,8},{8,0},{4,12},{12,4},{1,9},{9,1},{5,13},{13,5},{2,10},{10,2},... | collective-permute-start | bytes 442376 | tf_op jit(solution)/shard_map/ppermute | solution.py:23
  34.2 7.0 %copy-start.7 = (bf16[128,1024]{1,0:T(8,128)(2,1)}, bf16[128,1024]{1,0:T(8,128)(2,1)S(1)}, u32[]{:S(2)}) copy-start(bf16[128,1024]{1,0:T(8,128)(2,1)S(1)} %convolution_convert_fusion.16) | copy-start | bytes 786436
  35.5 15.7 %collective-permute-start.12 = (bf16[96,1024]{1,0:T(8,128)(2,1)S(1)}, bf16[96,1024]{1,0:T(8,128)(2,1)S(1)}, u32[]{:S(2)}, u32[]{:S(2)}) collective-permute-start(bf16[96,1024]{1,0:T(8,128)(2,1)S(1)} %convolution_convert_fusion.27), channel_id=1, source_target_pairs={{0,4},{4,0},{8,12},{12,8},{1,5},{5,1},{9,13},{13,9},{2,6},{6,2},{1... | collective-permute-start | bytes 589832 | tf_op jit(solution)/shard_map/ppermute | solution.py:23
  42.6 16.8 %collective-permute-start.11 = (bf16[96,1152]{1,0:T(8,128)(2,1)S(1)}, bf16[96,1152]{1,0:T(8,128)(2,1)S(1)}, u32[]{:S(2)}, u32[]{:S(2)}) collective-permute-start(bf16[96,1152]{1,0:T(8,128)(2,1)S(1)} %concatenate.127), channel_id=1, source_target_pairs={{0,8},{8,0},{4,12},{12,4},{1,9},{9,1},{5,13},{13,5},{2,10},{10,2},... | collective-permute-start | bytes 663560 | tf_op jit(solution)/shard_map/ppermute | solution.py:23
  49.0 2.2 %copy-start.4 = (bf16[128,1024]{1,0:T(8,128)(2,1)S(1)}, bf16[128,1024]{1,0:T(8,128)(2,1)}, u32[]{:S(2)}) copy-start(bf16[128,1024]{1,0:T(8,128)(2,1)} %convolution_convert_fusion.15) | copy-start | bytes 786436
  49.0 8.1 %collective-permute-start.16 = (bf16[96,1024]{1,0:T(8,128)(2,1)S(1)}, bf16[96,1024]{1,0:T(8,128)(2,1)S(1)}, u32[]{:S(2)}, u32[]{:S(2)}) collective-permute-start(bf16[96,1024]{1,0:T(8,128)(2,1)S(1)} %convolution_convert_fusion.25), channel_id=1, source_target_pairs={{0,4},{4,0},{8,12},{12,8},{1,5},{5,1},{9,13},{13,9},{2,6},{6,2},{1... | collective-permute-start | bytes 589832 | tf_op jit(solution)/shard_map/ppermute | solution.py:23
  51.2 1.9 %copy-start.5 = (bf16[128,1024]{1,0:T(8,128)(2,1)S(1)}, bf16[128,1024]{1,0:T(8,128)(2,1)}, u32[]{:S(2)}) copy-start(bf16[128,1024]{1,0:T(8,128)(2,1)} %convolution_convert_fusion.15) | copy-start | bytes 786436
  51.4 5.7 %copy-start.6 = (bf16[128,1024]{1,0:T(8,128)(2,1)S(1)}, bf16[128,1024]{1,0:T(8,128)(2,1)}, u32[]{:S(2)}) copy-start(bf16[128,1024]{1,0:T(8,128)(2,1)} %convolution_convert_fusion.10) | copy-start | bytes 786436
  51.4 14.1 %collective-permute-start.15 = (bf16[96,1024]{1,0:T(8,128)(2,1)S(1)}, bf16[96,1024]{1,0:T(8,128)(2,1)S(1)}, u32[]{:S(2)}, u32[]{:S(2)}) collective-permute-start(bf16[96,1024]{1,0:T(8,128)(2,1)S(1)} %convolution_convert_fusion.24), channel_id=1, source_target_pairs={{0,8},{8,0},{4,12},{12,4},{1,9},{9,1},{5,13},{13,5},{2,10},{10,2},... | collective-permute-start | bytes 589832 | tf_op jit(solution)/shard_map/ppermute | solution.py:23
  57.3 10.6 %collective-permute-start.17 = (bf16[96,1024]{1,0:T(8,128)(2,1)S(1)}, bf16[96,1024]{1,0:T(8,128)(2,1)S(1)}, u32[]{:S(2)}, u32[]{:S(2)}) collective-permute-start(bf16[96,1024]{1,0:T(8,128)(2,1)S(1)} %convolution_convert_fusion.20), channel_id=1, source_target_pairs={{0,8},{8,0},{4,12},{12,4},{1,9},{9,1},{5,13},{13,5},{2,10},{10,2},... | collective-permute-start | bytes 589832 | tf_op jit(solution)/shard_map/ppermute | solution.py:23
  60.6 4.9 %copy-start.8 = (bf16[128,1024]{1,0:T(8,128)(2,1)S(1)}, bf16[128,1024]{1,0:T(8,128)(2,1)}, u32[]{:S(2)}) copy-start(bf16[128,1024]{1,0:T(8,128)(2,1)} %convolution_convert_fusion.11) | copy-start | bytes 786436
  62.8 5.1 %copy-start.9 = (bf16[128,1024]{1,0:T(8,128)(2,1)S(1)}, bf16[128,1024]{1,0:T(8,128)(2,1)}, u32[]{:S(2)}) copy-start(bf16[128,1024]{1,0:T(8,128)(2,1)} %convolution_convert_fusion.7) | copy-start | bytes 786436

commit v5 on v4

v5 whole, which is shorter than its diff:
```python
import jax
import jax.numpy as jnp
from jax import lax
from jax.experimental import pallas as pl
from jax.experimental.pallas import tpu as pltpu
from jax.sharding import PartitionSpec as P

SIXTEENTHS = (1, 3, 4, 4, 4)
ROOM_SIXTEENTHS = 12


def route(axis, apart):
    count = lax.axis_size(axis)
    pairs = []
    for low in range(count):
        high = low | 1 << apart
        if high != low and high < count:
            pairs += [(low, high), (high, low)]
    return pairs


def from_partner(block, hop):
    return lax.ppermute(block, hop[0], route(*hop))


def across(left, right):
    return lax.dot_general(left, right, (((1,), (1,)), ((), ())), preferred_element_type=jnp.float32)


def one_hot(condition):
    return jnp.where(condition, 1.0, 0.0).astype(jnp.bfloat16)


def tables_kernel(wide, room, skeleton_ref, compress_ref, full_ref, small_ref, extra_ref):
    levels, rank = skeleton_ref.shape[1:]
    width = 2 * rank
    f32, i32 = jnp.float32, jnp.int32
    k = lax.broadcasted_iota(i32, (width, width), 1)
    twice = one_hot(lax.broadcasted_iota(i32, (width, rank), 0) % rank == lax.broadcasted_iota(i32, (width, rank), 1))
    earlier = one_hot(
        (lax.broadcasted_iota(i32, (width, width), 1) < lax.broadcasted_iota(i32, (width, width), 0) % rank)
    )
    column = lax.broadcasted_iota(i32, (2 * width, width), 0)
    is_real_entry = lax.broadcasted_iota(i32, (2 * width, width), 1) < rank
    partner_column = column >= width
    imag_column = column % width >= rank
    coefficient = column % rank + jnp.where(partner_column, rank, 0)
    slot_column = column - width
    slot_imag = slot_column >= room
    slot_of_column = jnp.where(slot_imag, slot_column - room, slot_column)
    row = lax.broadcasted_iota(i32, (width, width), 0)
    most = jnp.zeros((1, 1), f32)
    for level in range(levels):
        entry = jnp.broadcast_to(skeleton_ref[0, level : level + 1].astype(f32), (8, rank)).astype(jnp.bfloat16)
        entry = across(entry, twice)[:1]
        picked = jnp.where(entry >= rank, 1.0, 0.0)
        slot = across(jnp.broadcast_to(picked, (8, width)).astype(jnp.bfloat16), earlier)[:1].astype(i32)
        entry = entry.astype(i32)
        from_partner_entry = entry >= rank
        matrix = compress_ref[0, level]

        def halves(match, imag):
            same = is_real_entry != imag
            real = jnp.where(match & same, jnp.where(imag, -1.0, 1.0), 0.0).astype(jnp.bfloat16)
            turned = one_hot(match & jnp.logical_not(same))
            return across(matrix, real).astype(jnp.bfloat16), across(matrix, turned).astype(jnp.bfloat16)

        match = entry == coefficient
        full_ref[level, :rank], full_ref[level, rank:] = halves(match, imag_column)
        compacted = (slot == slot_of_column) & from_partner_entry
        match = (match & jnp.logical_not(partner_column)) | (compacted & partner_column)
        imag = (imag_column & jnp.logical_not(partner_column)) | (slot_imag & partner_column)
        small_ref[level, :rank], small_ref[level, rank:] = halves(match, imag)
        once = (k < rank) & from_partner_entry
        places = across(one_hot(once & (slot == row)), one_hot(once & (entry - rank == row)))
        extra_ref[level] = places.astype(jnp.bfloat16)
        if level >= wide:
            most = jnp.maximum(most, jnp.sum(picked, axis=1, keepdims=True) * 0.5)
    for level in range(wide, levels):
        extra_ref[level] = jnp.where(k < rank, extra_ref[level].astype(f32), most).astype(jnp.bfloat16)


def tables(skeleton, compress, wide, room):
    levels, rank = skeleton.shape[1:]
    shape = (levels, 2 * rank, 4 * rank)
    whole = pl.BlockSpec(memory_space=pltpu.VMEM)
    return pl.pallas_call(
        lambda *refs: tables_kernel(wide, room, *refs),
        out_shape=[
            jax.ShapeDtypeStruct(shape, jnp.bfloat16),
            jax.ShapeDtypeStruct(shape, jnp.bfloat16),
            jax.ShapeDtypeStruct((levels, 2 * rank, 2 * rank), jnp.bfloat16),
        ],
        in_specs=[whole] * 2,
        out_specs=[whole] * 3,
        compiler_params=pltpu.CompilerParams(vmem_limit_bytes=16 * 1024 * 1024),
        cost_estimate=pl.CostEstimate(flops=50_000_000, bytes_accessed=600_000, transcendentals=0),
        name="tables",
    )(skeleton, compress)


def compact_rows(matrix, slot):
    rank = slot.shape[1]
    parts = [
        jnp.dot(slot, half, preferred_element_type=jnp.float32)
        for half in (matrix[:rank], matrix[rank:])
    ]
    return jnp.concatenate(parts, 0).astype(jnp.bfloat16)


def times(matrix, value):
    return jnp.dot(matrix, value, preferred_element_type=jnp.float32).astype(jnp.bfloat16)


def sampled(sampling, traces):
    return jnp.einsum(
        "pc,tp->ct", sampling, traces, preferred_element_type=jnp.float32
    ).astype(jnp.bfloat16)


def evaluated(coeffs, evaluation):
    return jnp.einsum(
        "ct,cp->tp", coeffs, evaluation, preferred_element_type=jnp.float32
    ).astype(jnp.bfloat16)


def after(value, earlier):
    return value if earlier is None else lax.optimization_barrier((value, earlier))[0]


def all_hops():
    low_bits = lax.axis_size("sub").bit_length() - 1
    high_bits = lax.axis_size("bfly").bit_length() - 1
    return [("sub", bit) for bit in range(low_bits)] + [("bfly", bit) for bit in range(high_bits)]


def full_width(traces, sampling, full, evaluation):
    coeffs = sampled(sampling, traces)
    for level, hop in enumerate(all_hops()):
        partner = from_partner(coeffs, hop)
        coeffs = times(full[level], jnp.concatenate([coeffs, partner], 0))
    return evaluated(coeffs, evaluation)


def sequence(pieces, levels):
    def turn(at):
        level, piece = at
        if level == 0:
            return max(0, 2 * piece - 1)
        return 2 * (level + piece + (piece > 0))

    return sorted(
        [(level, piece) for level in range(levels + 1) for piece in range(pieces)],
        key=lambda at: (turn(at), at),
    )


def local(traces, sampling, skeleton, compress, evaluation):
    sampling, evaluation = sampling[0], evaluation[0]
    hops = all_hops()
    levels = len(hops)
    wide = lax.axis_size("sub").bit_length() - 1
    rank = skeleton.shape[-1]
    room = rank * ROOM_SIXTEENTHS // 16
    full, small, extra = tables(skeleton, compress, wide, room)
    most_here = lax.broadcasted_iota(jnp.int32, extra.shape[1:], 1) >= rank

    def compact(level, piece):
        return piece > 0 and level >= wide

    unit = traces.shape[0] // sum(SIXTEENTHS)
    pieces = len(SIXTEENTHS)
    starts = [unit * sum(SIXTEENTHS[:i]) for i in range(pieces + 1)]
    inputs, partners, theirs, done = {}, {}, {}, [None] * pieces
    previous, known = None, None
    for level, piece in sequence(pieces, levels):
        count = starts[piece + 1] - starts[piece]
        if level == 0:
            own = sampled(
                after(sampling, previous) if piece > 1 else sampling,
                traces[starts[piece] : starts[piece + 1]],
            )
        else:
            arrived = after(partners[piece], previous)
            if piece == 0 and level - 1 >= wide:
                known = arrived[:, count:]
                theirs[level - 1] = known[:room, :rank]
            value = jnp.concatenate([inputs[piece], arrived[:, :count]], 0)
            matrix = full[level - 1]
            if compact(level - 1, piece):
                value = jnp.pad(value, ((0, full.shape[2] - value.shape[0]), (0, 0)))
                matrix = small[level - 1]
            own = times(matrix, value)
        if level == levels:
            done[piece] = evaluated(own, evaluation)
            continue
        outgoing = own
        if compact(level, piece):
            outgoing = times(compact_rows(matrix, theirs[level]), value)
        if piece == 0 and level >= wide:
            block = extra[level]
            if known is not None:
                block = jnp.where(most_here, jnp.maximum(block, known), block)
            outgoing = jnp.concatenate([outgoing, block], 1)
        inputs[piece] = own
        partners[piece] = from_partner(outgoing, hops[level])
        previous = outgoing
    most = after(jnp.maximum(extra[levels - 1], known)[:8, rank:], previous)
    for hop in hops[:wide]:
        most = jnp.maximum(most, from_partner(most, hop))
    quick = jnp.concatenate(done, 0)
    return lax.cond(
        most[0, 0] > room,
        lambda: full_width(traces, sampling, full, evaluation),
        lambda: quick,
    )


def solution(mesh):
    placed = (
        P(("shots", "tr"), ("bfly", "sub")),
        P(("bfly", "sub"), None, None),
        P(("bfly", "sub"), None, None),
        P(("bfly", "sub"), None, None, None),
        P(("bfly", "sub"), None, None),
    )
    return jax.shard_map(
        local,
        mesh=mesh,
        in_specs=placed,
        out_specs=P(("shots", "tr"), ("bfly", "sub")),
        check_vma=False,
    )
```

time: 69.7 us -> 62.9 us (0.902)
  matrix products: 30.1 us -> 21.4 us
  waiting for transfers between devices: 9.13 us -> 17.3 us
  starting transfers between devices: 21.5 us -> 19.2 us
  between operations: 2.95 us -> 0.83 us
  other arithmetic: 2.01 us -> 0.12 us
  Pallas kernels: 0 us -> 1.09 us
  local copies, waits for them, and re-layouts: 3.51 us -> 2.68 us
    dot_general x18, matrix products: 18.2 us -> 9.4 us  [times(): jnp.dot(matrix, value, preferred_element_type=jnp.float32)]
    ppermute x15 -> x16, waiting for transfers between devices: 9.13 us -> 17.3 us  [from_partner(): return lax.ppermute(block, hop[0], route(*hop))]
    ppermute x15 -> x16, starting transfers between devices: 21.5 us -> 19.2 us  [from_partner(): return lax.ppermute(block, hop[0], route(*hop))]
    slice x6 -> x2, local copies, waits for them, and re-layouts: 1.72 us -> 0.51 us  [the longest x1 0.51 us: local(): most[0, 0] > room]
    pallas_call x0 -> x1, Pallas kernels: none -> 1.09 us  [tables(): pl.pallas_call(lambda *refs: tables_kernel(wide, room, *refs), out_shape=...]
    reduce_sum x2 -> x0, other arithmetic: 0.91 us -> none  [the longest x1 0.8 us: local(): most = jnp.max(jnp.sum(skeleton[wide:] >= rank, -1)).astype(jnp.bfloat16)]
    dot_general x5, matrix products: 3.09 us -> 3.9 us  [sampled(): jnp.einsum('pc,tp->ct', sampling, traces, preferred_element_type=jnp.floa...]
    unnamed x22 -> x21, local copies, waits for them, and re-layouts: 1.65 us -> 2.15 us
  transfers between devices with their start and end apart: 15 -> 16, of which waited for: 6 -> 7; matrix products, arithmetic and copies ran while one was open for 48% -> 33% of each run, Pallas kernels for 0% -> 2%
where the time goes in v5:
time: 62.9 us; the launch traced here: 62.6 us
  matrix products  21.4 us (34%)
  starting transfers between devices  19.2 us (31%)
  waiting for transfers between devices  17.3 us (28%)
  local copies, waits for them, and re-layouts  2.68 us (4%)
  Pallas kernels  1.09 us (2%)
  between operations  0.83 us (1%)
    ppermute x16, starting transfers between devices, from_partner(): return lax.ppermute(block, hop[0], route(*hop))  19.2 us
    ppermute x16, waiting for transfers between devices, from_partner(): return lax.ppermute(block, hop[0], route(*hop))  17.3 us
    dot_general x18, matrix products, times(): jnp.dot(matrix, value, preferred_element_type=jnp.float32)  9.4 us
    dot_general x5, matrix products, evaluated(): jnp.einsum('ct,cp->tp', coeffs, evaluation, preferred_element_type=jnp.fl...  7.58 us
    dot_general x5, matrix products, sampled(): jnp.einsum('pc,tp->ct', sampling, traces, preferred_element_type=jnp.floa...  3.9 us
    unnamed x21, local copies, waits for them, and re-layouts  2.15 us
  transfers between devices with their start and end apart: 16, of which 7 were waited for; matrix products, arithmetic and copies ran while one was open for 33% of the time, Pallas kernels for 2%

profile of v5, /device:TPU:0, one launch (start us, length us, event | category | flops | bytes accessed | tf_op | source)
XLA Modules:
  0.0 62.6 jit_solution(14409496301518716268)
XLA Ops:
  0.0 1.1 %convolution_convert_fusion.34 = bf16[128,256]{1,0:T(8,128)(2,1)S(1)} fusion(bf16[4096,128]{1,0:T(8,128)(2,1)} %param.7, bf16[1,128,128]{2,1,0:T(8,128)(2,1)} %param.8), kind=kOutput, calls=%fused_computation.59 | convolution fusion | flops 8421376 | bytes 163840 | tf_op jit(solution)/shard_map/pc,tp->ct/dot_general | solution.py:116
  1.1 3.0 %collective-permute-start.3 = (bf16[128,256]{1,0:T(8,128)(2,1)S(1)}, bf16[128,256]{1,0:T(8,128)(2,1)S(1)}, u32[]{:S(2)}, u32[]{:S(2)}) collective-permute-start(bf16[128,256]{1,0:T(8,128)(2,1)S(1)} %convolution_convert_fusion.34), channel_id=1, source_target_pairs={{0,2},{2,0},{1,3},{3,1},{4,6},{6,4},{5,7},{7,5},{8,10},{10,8},{9,1... | collective-permute-start | bytes 196616 | tf_op jit(solution)/shard_map/ppermute | solution.py:23
  4.1 1.2 %convolution_convert_fusion.30 = bf16[128,768]{1,0:T(8,128)(2,1)S(1)} fusion(bf16[4096,128]{1,0:T(8,128)(2,1)} %param.7, bf16[1,128,128]{2,1,0:T(8,128)(2,1)} %param.8), kind=kOutput, calls=%fused_computation.54 | convolution fusion | flops 25264128 | bytes 425984 | tf_op jit(solution)/shard_map/pc,tp->ct/dot_general | solution.py:116
  6.8 1.1 %tables.1 = (bf16[3,128,256]{2,1,0:T(8,128)(2,1)S(1)}, bf16[3,128,256]{2,1,0:T(8,128)(2,1)S(1)}, bf16[3,128,128]{2,1,0:T(8,128)(2,1)S(1)}) custom-call(s32[1,3,64]{2,1,0:T(4,128)S(1)} %copy.8.refs_0_, bf16[1,3,64,128]{3,2,1,0:T(8,128)(2,1)S(1)} %copy-done), custom_call_target="tpu_custom_call" | custom-call | flops 50000000 | bytes 600000 | tf_op jit(solution)/shard_map/tables/pallas_call | solution.py:87
  8.1 2.2 %collective-permute-start.4 = (bf16[128,384]{1,0:T(8,128)(2,1)S(1)}, bf16[128,384]{1,0:T(8,128)(2,1)S(1)}, u32[]{:S(2)}, u32[]{:S(2)}) collective-permute-start(bf16[128,384]{1,0:T(8,128)(2,1)S(1)} %pad_maximum_fusion.12), channel_id=1, source_target_pairs={{0,4},{4,0},{8,12},{12,8},{1,5},{5,1},{9,13},{13,9},{2,6},{6,2},{1... | collective-permute-start | bytes 294920 | tf_op jit(solution)/shard_map/ppermute | solution.py:23
  10.3 1.2 %convolution_convert_fusion.19 = bf16[128,1024]{1,0:T(8,128)(2,1)S(1)} fusion(bf16[128,128]{1,0:T(8,128)(2,1)S(1)} %bitcast.95, bf16[4096,128]{1,0:T(8,128)(2,1)} %param.7), kind=kOutput, calls=%fused_computation.42 | convolution fusion | flops 33685504 | bytes 557056 | tf_op jit(solution)/shard_map/pc,tp->ct/dot_general | solution.py:116
  11.5 1.6 %collective-permute-start.8 = (bf16[128,1024]{1,0:T(8,128)(2,1)S(1)}, bf16[128,1024]{1,0:T(8,128)(2,1)S(1)}, u32[]{:S(2)}, u32[]{:S(2)}) collective-permute-start(bf16[128,1024]{1,0:T(8,128)(2,1)S(1)} %convolution_convert_fusion.19), channel_id=1, source_target_pairs={{0,2},{2,0},{1,3},{3,1},{4,6},{6,4},{5,7},{7,5},{8,10},{10,8},{9,1... | collective-permute-start | bytes 786440 | tf_op jit(solution)/shard_map/ppermute | solution.py:23
  13.4 2.9 %collective-permute-start.5 = (bf16[128,384]{1,0:T(8,128)(2,1)S(1)}, bf16[128,384]{1,0:T(8,128)(2,1)S(1)}, u32[]{:S(2)}, u32[]{:S(2)}) collective-permute-start(bf16[128,384]{1,0:T(8,128)(2,1)S(1)} %pad_maximum_fusion.13), channel_id=1, source_target_pairs={{0,8},{8,0},{4,12},{12,4},{1,9},{9,1},{5,13},{13,5},{2,10},{10,2},... | collective-permute-start | bytes 294920 | tf_op jit(solution)/shard_map/ppermute | solution.py:23
  16.6 1.6 %collective-permute-start.10 = (bf16[128,1024]{1,0:T(8,128)(2,1)S(1)}, bf16[128,1024]{1,0:T(8,128)(2,1)S(1)}, u32[]{:S(2)}, u32[]{:S(2)}) collective-permute-start(bf16[128,1024]{1,0:T(8,128)(2,1)S(1)} %convolution_convert_fusion.18), channel_id=1, source_target_pairs={{0,2},{2,0},{1,3},{3,1},{4,6},{6,4},{5,7},{7,5},{8,10},{10,8},{9,1... | collective-permute-start | bytes 786440 | tf_op jit(solution)/shard_map/ppermute | solution.py:23
  18.3 0.9 %convolution_convert_fusion.28 = bf16[128,768]{1,0:T(8,128)(2,1)} fusion(bf16[128,768]{1,0:T(8,128)(2,1)S(1)} %collective-permute-done.6, bf16[128,768]{1,0:T(8,128)(2,1)S(1)} %convolution_convert_fusion.30, bf16[3,128,256]{2,1,0:T(8,128)(2,1)S(1)} %get-tuple-element.44), kind=kOutput, calls=%fused_computation.52 | convolution fusion | flops 51216384 | bytes 655360 | tf_op jit(solution)/shard_map/dot_general | solution.py:112
  19.2 0.9 %convolution_convert_fusion.32 = bf16[96,768]{1,0:T(8,128)(2,1)} fusion(bf16[128,768]{1,0:T(8,128)(2,1)S(1)} %collective-permute-done.6, bf16[128,768]{1,0:T(8,128)(2,1)S(1)} %convolution_convert_fusion.30, bf16[48,256]{1,0:T(8,128)(2,1)S(1)} %convolution_convert_fusion.40, bf16[48,256]{1,0:T(8,128)(2,1)S(1)} %convolution_convert_fusion.41), kind=kOutput, calls=%fused_computation.56 | convolution fusion | flops 38707200 | bytes 589824 | tf_op jit(solution)/shard_map/dot_general | solution.py:112
  20.0 1.6 %collective-permute-start.11 = (bf16[96,768]{1,0:T(8,128)(2,1)}, bf16[96,768]{1,0:T(8,128)(2,1)S(1)}, u32[]{:S(2)}, u32[]{:S(2)}) collective-permute-start(bf16[96,768]{1,0:T(8,128)(2,1)} %convolution_convert_fusion.32), channel_id=1, source_target_pairs={{0,4},{4,0},{8,12},{12,8},{1,5},{5,1},{9,13},{13,9},{2,6},{6,2},{1... | collective-permute-start | bytes 442376 | tf_op jit(solution)/shard_map/ppermute | solution.py:23
  22.8 1.0 %fusion.29 = bf16[4096,128]{1,0:T(8,128)(2,1)} fusion(bf16[128,256]{1,0:T(8,128)(2,1)S(1)} %slice.147, bf16[128,256]{1,0:T(8,128)(2,1)S(1)} %convolution_convert_fusion.36, bf16[3,128,256]{2,1,0:T(8,128)(2,1)S(1)} %get-tuple-element.44, bf16[1,128,128]{2,1,0:T(8,128)(2,1)S(1)} %copy-done.3), kind=kOutput, calls=%fused_computation.58 | convolution fusion | flops 25493504 | bytes 294912 | tf_op jit(solution)/shard_map/ct,cp->tp/dot_general | solution.py:122
  24.8 3.5 %collective-permute-done.11 = bf16[96,768]{1,0:T(8,128)(2,1)S(1)} collective-permute-done((bf16[96,768]{1,0:T(8,128)(2,1)}, bf16[96,768]{1,0:T(8,128)(2,1)S(1)}, u32[]{:S(2)}, u32[]{:S(2)}) %collective-permute-start.11) | collective-permute-done | bytes 147488 | tf_op jit(solution)/shard_map/ppermute | solution.py:23
  28.6 0.9 %convolution_convert_fusion.22 = bf16[128,768]{1,0:T(8,128)(2,1)} fusion(bf16[96,768]{1,0:T(8,128)(2,1)S(1)} %collective-permute-done.11, bf16[128,768]{1,0:T(8,128)(2,1)S(1)} %copy-done.4, bf16[3,128,256]{2,1,0:T(8,128)(2,1)S(1)} %get-tuple-element.51), kind=kOutput, calls=%fused_computation.46 | convolution fusion | flops 51806208 | bytes 606208 | tf_op jit(solution)/shard_map/dot_general | solution.py:112
  30.2 0.9 %convolution_convert_fusion.14 = bf16[128,1024]{1,0:T(8,128)(2,1)} fusion(bf16[128,1024]{1,0:T(8,128)(2,1)S(1)} %collective-permute-done.10, bf16[128,1024]{1,0:T(8,128)(2,1)S(1)} %convolution_convert_fusion.18, bf16[3,128,256]{2,1,0:T(8,128)(2,1)S(1)} %get-tuple-element.44), kind=kOutput, calls=%fused_computation.37 | convolution fusion | flops 68288512 | bytes 851968 | tf_op jit(solution)/shard_map/dot_general | solution.py:112
  31.1 1.4 %collective-permute-done.9 = bf16[96,1024]{1,0:T(8,128)(2,1)S(1)} collective-permute-done((bf16[96,1024]{1,0:T(8,128)(2,1)S(1)}, bf16[96,1024]{1,0:T(8,128)(2,1)S(1)}, u32[]{:S(2)}, u32[]{:S(2)}) %collective-permute-start.9) | collective-permute-done | bytes 196640 | tf_op jit(solution)/shard_map/ppermute | solution.py:23
  32.8 2.0 %collective-permute-start.16 = (bf16[96,1024]{1,0:T(8,128)(2,1)S(1)}, bf16[96,1024]{1,0:T(8,128)(2,1)S(1)}, u32[]{:S(2)}, u32[]{:S(2)}) collective-permute-start(bf16[96,1024]{1,0:T(8,128)(2,1)S(1)} %convolution_convert_fusion.26), channel_id=1, source_target_pairs={{0,8},{8,0},{4,12},{12,4},{1,9},{9,1},{5,13},{13,5},{2,10},{10,2},... | collective-permute-start | bytes 589832 | tf_op jit(solution)/shard_map/ppermute | solution.py:23
  34.8 0.9 %convolution_convert_fusion.13 = bf16[128,1024]{1,0:T(8,128)(2,1)} fusion(bf16[96,1024]{1,0:T(8,128)(2,1)S(1)} %collective-permute-done.9, bf16[128,1024]{1,0:T(8,128)(2,1)S(1)} %convolution_convert_fusion.16, bf16[3,128,256]{2,1,0:T(8,128)(2,1)S(1)} %get-tuple-element.51), kind=kOutput, calls=%fused_computation.36 | convolution fusion | flops 69074944 | bytes 786432 | tf_op jit(solution)/shard_map/dot_general | solution.py:112
  35.7 0.9 %convolution_convert_fusion.15 = bf16[128,1024]{1,0:T(8,128)(2,1)} fusion(bf16[128,1024]{1,0:T(8,128)(2,1)S(1)} %collective-permute-done.7, bf16[128,1024]{1,0:T(8,128)(2,1)S(1)} %convolution_convert_fusion.17, bf16[3,128,256]{2,1,0:T(8,128)(2,1)S(1)} %get-tuple-element.44), kind=kOutput, calls=%fused_computation.38 | convolution fusion | flops 68288512 | bytes 851968 | tf_op jit(solution)/shard_map/dot_general | solution.py:112
  36.9 2.9 %collective-permute-done.15 = bf16[96,768]{1,0:T(8,128)(2,1)} collective-permute-done((bf16[96,768]{1,0:T(8,128)(2,1)S(1)}, bf16[96,768]{1,0:T(8,128)(2,1)}, u32[]{:S(2)}, u32[]{:S(2)}) %collective-permute-start.15) | collective-permute-done | bytes 147488 | tf_op jit(solution)/shard_map/ppermute | solution.py:23
  39.9 2.1 %fusion.28 = bf16[4096,128]{1,0:T(8,128)(2,1)} fusion(bf16[4096,128]{1,0:T(8,128)(2,1)} %fusion.29, bf16[96,768]{1,0:T(8,128)(2,1)} %collective-permute-done.15, bf16[128,768]{1,0:T(8,128)(2,1)} %convolution_convert_fusion.22, bf16[3,128,256]{2,1,0:T(8,128)(2,1)S(1)} %get-tuple-element.51, bf16[1,128,128]{2,1,0:T(8,128)(2,1)S(1)} %copy-done.3), kind=kOutput, calls=%fused_computation.44 | convolution fusion | flops 77070336 | bytes 638976 | tf_op jit(solution)/shard_map/ct,cp->tp/dot_general | solution.py:122
  43.0 0.9 %convolution_convert_fusion.10 = bf16[128,1024]{1,0:T(8,128)(2,1)} fusion(bf16[96,1024]{1,0:T(8,128)(2,1)S(1)} %collective-permute-done.13, bf16[128,1024]{1,0:T(8,128)(2,1)S(1)} %copy-done.6, bf16[3,128,256]{2,1,0:T(8,128)(2,1)S(1)} %get-tuple-element.51), kind=kOutput, calls=%fused_computation.32 | convolution fusion | flops 69074944 | bytes 786432 | tf_op jit(solution)/shard_map/dot_general | solution.py:112
  43.9 2.3 %collective-permute-done.12 = bf16[96,1024]{1,0:T(8,128)(2,1)S(1)} collective-permute-done((bf16[96,1024]{1,0:T(8,128)(2,1)S(1)}, bf16[96,1024]{1,0:T(8,128)(2,1)S(1)}, u32[]{:S(2)}, u32[]{:S(2)}) %collective-permute-start.12) | collective-permute-done | bytes 196640 | tf_op jit(solution)/shard_map/ppermute | solution.py:23
  46.4 2.2 %collective-permute-start.18 = (bf16[96,1024]{1,0:T(8,128)(2,1)S(1)}, bf16[96,1024]{1,0:T(8,128)(2,1)S(1)}, u32[]{:S(2)}, u32[]{:S(2)}) collective-permute-start(bf16[96,1024]{1,0:T(8,128)(2,1)S(1)} %convolution_convert_fusion.23), channel_id=1, source_target_pairs={{0,8},{8,0},{4,12},{12,4},{1,9},{9,1},{5,13},{13,5},{2,10},{10,2},... | collective-permute-start | bytes 589832 | tf_op jit(solution)/shard_map/ppermute | solution.py:23
  48.8 0.9 %convolution_convert_fusion.7 = bf16[128,1024]{1,0:T(8,128)(2,1)} fusion(bf16[96,1024]{1,0:T(8,128)(2,1)S(1)} %collective-permute-done.12, bf16[128,1024]{1,0:T(8,128)(2,1)S(1)} %copy-done.7, bf16[3,128,256]{2,1,0:T(8,128)(2,1)S(1)} %get-tuple-element.51), kind=kOutput, calls=%fused_computation.28 | convolution fusion | flops 69074944 | bytes 786432 | tf_op jit(solution)/shard_map/dot_general | solution.py:112
  49.8 2.4 %collective-permute-done.16 = bf16[96,1024]{1,0:T(8,128)(2,1)S(1)} collective-permute-done((bf16[96,1024]{1,0:T(8,128)(2,1)S(1)}, bf16[96,1024]{1,0:T(8,128)(2,1)S(1)}, u32[]{:S(2)}, u32[]{:S(2)}) %collective-permute-start.16) | collective-permute-done | bytes 196640 | tf_op jit(solution)/shard_map/ppermute | solution.py:23
  52.2 2.1 %fusion.27 = bf16[4096,128]{1,0:T(8,128)(2,1)} fusion(bf16[4096,128]{1,0:T(8,128)(2,1)} %fusion.28, bf16[96,1024]{1,0:T(8,128)(2,1)S(1)} %collective-permute-done.16, bf16[128,1024]{1,0:T(8,128)(2,1)} %convolution_convert_fusion.13, bf16[3,128,256]{2,1,0:T(8,128)(2,1)S(1)} %get-tuple-element.51, bf16[1,128,128]{2,1,0:T(8,128)(2,1)S(1)} %copy-done.3), kind=kOutput, calls=%fused_computation.34 | convolution fusion | flops 102760448 | bytes 819200 | tf_op jit(solution)/shard_map/ct,cp->tp/dot_general | solution.py:122
  55.4 3.1 %collective-permute-done.17 = bf16[96,1024]{1,0:T(8,128)(2,1)S(1)} collective-permute-done((bf16[96,1024]{1,0:T(8,128)(2,1)S(1)}, bf16[96,1024]{1,0:T(8,128)(2,1)S(1)}, u32[]{:S(2)}, u32[]{:S(2)}) %collective-permute-start.17) | collective-permute-done | bytes 196640 | tf_op jit(solution)/shard_map/ppermute | solution.py:23
  58.5 1.2 %fusion.26 = bf16[4096,128]{1,0:T(8,128)(2,1)} fusion(bf16[4096,128]{1,0:T(8,128)(2,1)} %fusion.27, bf16[96,1024]{1,0:T(8,128)(2,1)S(1)} %collective-permute-done.17, bf16[128,1024]{1,0:T(8,128)(2,1)S(1)} %copy-done.8, bf16[3,128,256]{2,1,0:T(8,128)(2,1)S(1)} %get-tuple-element.51, bf16[1,128,128]{2,1,0:T(8,128)(2,1)S(1)} %copy-done.3), kind=kOutput, calls=%fused_computation.30 | convolution fusion | flops 102760448 | bytes 819200 | tf_op jit(solution)/shard_map/ct,cp->tp/dot_general | solution.py:122
  59.7 1.7 %collective-permute-done.18 = bf16[96,1024]{1,0:T(8,128)(2,1)S(1)} collective-permute-done((bf16[96,1024]{1,0:T(8,128)(2,1)S(1)}, bf16[96,1024]{1,0:T(8,128)(2,1)S(1)}, u32[]{:S(2)}, u32[]{:S(2)}) %collective-permute-start.18) | collective-permute-done | bytes 196640 | tf_op jit(solution)/shard_map/ppermute | solution.py:23
  61.4 1.2 %fusion.25 = bf16[4096,128]{1,0:T(8,128)(2,1)} fusion(bf16[4096,128]{1,0:T(8,128)(2,1)} %fusion.26, bf16[96,1024]{1,0:T(8,128)(2,1)S(1)} %collective-permute-done.18, bf16[128,1024]{1,0:T(8,128)(2,1)S(1)} %copy-done.9, bf16[3,128,256]{2,1,0:T(8,128)(2,1)S(1)} %get-tuple-element.51, bf16[1,128,128]{2,1,0:T(8,128)(2,1)S(1)} %copy-done.3), kind=kOutput, calls=%fused_computation.26 | convolution fusion | flops 102760448 | bytes 819200 | tf_op jit(solution)/shard_map/ct,cp->tp/dot_general | solution.py:122
  (66 shorter events, 8.1 us)
Async XLA Ops:
  0.0 10.3 %copy-start.2 = (bf16[1,128,128]{2,1,0:T(8,128)(2,1)S(1)}, bf16[1,128,128]{2,1,0:T(8,128)(2,1)}, u32[]{:S(2)}) copy-start(bf16[1,128,128]{2,1,0:T(8,128)(2,1)} %param.8) | copy-start | bytes 98308
  1.1 6.9 %collective-permute-start.3 = (bf16[128,256]{1,0:T(8,128)(2,1)S(1)}, bf16[128,256]{1,0:T(8,128)(2,1)S(1)}, u32[]{:S(2)}, u32[]{:S(2)}) collective-permute-start(bf16[128,256]{1,0:T(8,128)(2,1)S(1)} %convolution_convert_fusion.34), channel_id=1, source_target_pairs={{0,2},{2,0},{1,3},{3,1},{4,6},{6,4},{5,7},{7,5},{8,10},{10,8},{9,1... | collective-permute-start | bytes 196616 | tf_op jit(solution)/shard_map/ppermute | solution.py:23
  5.2 13.0 %collective-permute-start.6 = (bf16[128,768]{1,0:T(8,128)(2,1)S(1)}, bf16[128,768]{1,0:T(8,128)(2,1)S(1)}, u32[]{:S(2)}, u32[]{:S(2)}) collective-permute-start(bf16[128,768]{1,0:T(8,128)(2,1)S(1)} %convolution_convert_fusion.30), channel_id=1, source_target_pairs={{0,2},{2,0},{1,3},{3,1},{4,6},{6,4},{5,7},{7,5},{8,10},{10,8},{9,1... | collective-permute-start | bytes 589832 | tf_op jit(solution)/shard_map/ppermute | solution.py:23
  6.0 0.8 %copy-start = (bf16[1,3,64,128]{3,2,1,0:T(8,128)(2,1)S(1)}, bf16[1,3,64,128]{3,2,1,0:T(8,128)(2,1)}, u32[]{:S(2)}) copy-start(bf16[1,3,64,128]{3,2,1,0:T(8,128)(2,1)} %refs_1_.1) | copy-start | bytes 147460
  7.9 8.4 %copy-start.1 = (bf16[4096,128]{1,0:T(8,128)(2,1)S(1)}, bf16[4096,128]{1,0:T(8,128)(2,1)}, u32[]{:S(2)}) copy-start(bf16[4096,128]{1,0:T(8,128)(2,1)} %param.7) | copy-start | bytes 3145732
  8.1 4.9 %collective-permute-start.4 = (bf16[128,384]{1,0:T(8,128)(2,1)S(1)}, bf16[128,384]{1,0:T(8,128)(2,1)S(1)}, u32[]{:S(2)}, u32[]{:S(2)}) collective-permute-start(bf16[128,384]{1,0:T(8,128)(2,1)S(1)} %pad_maximum_fusion.12), channel_id=1, source_target_pairs={{0,4},{4,0},{8,12},{12,8},{1,5},{5,1},{9,13},{13,9},{2,6},{6,2},{1... | collective-permute-start | bytes 294920 | tf_op jit(solution)/shard_map/ppermute | solution.py:23
  11.5 12.3 %collective-permute-start.8 = (bf16[128,1024]{1,0:T(8,128)(2,1)S(1)}, bf16[128,1024]{1,0:T(8,128)(2,1)S(1)}, u32[]{:S(2)}, u32[]{:S(2)}) collective-permute-start(bf16[128,1024]{1,0:T(8,128)(2,1)S(1)} %convolution_convert_fusion.19), channel_id=1, source_target_pairs={{0,2},{2,0},{1,3},{3,1},{4,6},{6,4},{5,7},{7,5},{8,10},{10,8},{9,1... | collective-permute-start | bytes 786440 | tf_op jit(solution)/shard_map/ppermute | solution.py:23
  13.4 9.1 %collective-permute-start.5 = (bf16[128,384]{1,0:T(8,128)(2,1)S(1)}, bf16[128,384]{1,0:T(8,128)(2,1)S(1)}, u32[]{:S(2)}, u32[]{:S(2)}) collective-permute-start(bf16[128,384]{1,0:T(8,128)(2,1)S(1)} %pad_maximum_fusion.13), channel_id=1, source_target_pairs={{0,8},{8,0},{4,12},{12,4},{1,9},{9,1},{5,13},{13,5},{2,10},{10,2},... | collective-permute-start | bytes 294920 | tf_op jit(solution)/shard_map/ppermute | solution.py:23
  16.6 13.0 %collective-permute-start.10 = (bf16[128,1024]{1,0:T(8,128)(2,1)S(1)}, bf16[128,1024]{1,0:T(8,128)(2,1)S(1)}, u32[]{:S(2)}, u32[]{:S(2)}) collective-permute-start(bf16[128,1024]{1,0:T(8,128)(2,1)S(1)} %convolution_convert_fusion.18), channel_id=1, source_target_pairs={{0,2},{2,0},{1,3},{3,1},{4,6},{6,4},{5,7},{7,5},{8,10},{10,8},{9,1... | collective-permute-start | bytes 786440 | tf_op jit(solution)/shard_map/ppermute | solution.py:23
  18.3 4.6 %copy-start.3 = (bf16[1,128,128]{2,1,0:T(8,128)(2,1)S(1)}, bf16[1,128,128]{2,1,0:T(8,128)(2,1)}, u32[]{:S(2)}) copy-start(bf16[1,128,128]{2,1,0:T(8,128)(2,1)} %param.11) | copy-start | bytes 98308
  20.0 8.3 %collective-permute-start.11 = (bf16[96,768]{1,0:T(8,128)(2,1)}, bf16[96,768]{1,0:T(8,128)(2,1)S(1)}, u32[]{:S(2)}, u32[]{:S(2)}) collective-permute-start(bf16[96,768]{1,0:T(8,128)(2,1)} %convolution_convert_fusion.32), channel_id=1, source_target_pairs={{0,4},{4,0},{8,12},{12,8},{1,5},{5,1},{9,13},{13,9},{2,6},{6,2},{1... | collective-permute-start | bytes 442376 | tf_op jit(solution)/shard_map/ppermute | solution.py:23
  21.9 13.8 %collective-permute-start.7 = (bf16[128,1024]{1,0:T(8,128)(2,1)S(1)}, bf16[128,1024]{1,0:T(8,128)(2,1)S(1)}, u32[]{:S(2)}, u32[]{:S(2)}) collective-permute-start(bf16[128,1024]{1,0:T(8,128)(2,1)S(1)} %convolution_convert_fusion.17), channel_id=1, source_target_pairs={{0,2},{2,0},{1,3},{3,1},{4,6},{6,4},{5,7},{7,5},{8,10},{10,8},{9,1... | collective-permute-start | bytes 786440 | tf_op jit(solution)/shard_map/ppermute | solution.py:23
  23.8 4.5 %copy-start.4 = (bf16[128,768]{1,0:T(8,128)(2,1)S(1)}, bf16[128,768]{1,0:T(8,128)(2,1)}, u32[]{:S(2)}) copy-start(bf16[128,768]{1,0:T(8,128)(2,1)} %convolution_convert_fusion.28) | copy-start | bytes 589828
  24.1 8.5 %collective-permute-start.9 = (bf16[96,1024]{1,0:T(8,128)(2,1)S(1)}, bf16[96,1024]{1,0:T(8,128)(2,1)S(1)}, u32[]{:S(2)}, u32[]{:S(2)}) collective-permute-start(bf16[96,1024]{1,0:T(8,128)(2,1)S(1)} %convolution_convert_fusion.29), channel_id=1, source_target_pairs={{0,4},{4,0},{8,12},{12,8},{1,5},{5,1},{9,13},{13,9},{2,6},{6,2},{1... | collective-permute-start | bytes 589832 | tf_op jit(solution)/shard_map/ppermute | solution.py:23
  28.5 11.2 %collective-permute-start.15 = (bf16[96,768]{1,0:T(8,128)(2,1)S(1)}, bf16[96,768]{1,0:T(8,128)(2,1)}, u32[]{:S(2)}, u32[]{:S(2)}) collective-permute-start(bf16[96,768]{1,0:T(8,128)(2,1)S(1)} %convolution_convert_fusion.31), channel_id=1, source_target_pairs={{0,8},{8,0},{4,12},{12,4},{1,9},{9,1},{5,13},{13,5},{2,10},{10,2},... | collective-permute-start | bytes 442376 | tf_op jit(solution)/shard_map/ppermute | solution.py:23
  29.8 12.3 %collective-permute-start.13 = (bf16[96,1024]{1,0:T(8,128)(2,1)S(1)}, bf16[96,1024]{1,0:T(8,128)(2,1)S(1)}, u32[]{:S(2)}, u32[]{:S(2)}) collective-permute-start(bf16[96,1024]{1,0:T(8,128)(2,1)S(1)} %convolution_convert_fusion.27), channel_id=1, source_target_pairs={{0,4},{4,0},{8,12},{12,8},{1,5},{5,1},{9,13},{13,9},{2,6},{6,2},{1... | collective-permute-start | bytes 589832 | tf_op jit(solution)/shard_map/ppermute | solution.py:23
  32.8 19.4 %collective-permute-start.16 = (bf16[96,1024]{1,0:T(8,128)(2,1)S(1)}, bf16[96,1024]{1,0:T(8,128)(2,1)S(1)}, u32[]{:S(2)}, u32[]{:S(2)}) collective-permute-start(bf16[96,1024]{1,0:T(8,128)(2,1)S(1)} %convolution_convert_fusion.26), channel_id=1, source_target_pairs={{0,8},{8,0},{4,12},{12,4},{1,9},{9,1},{5,13},{13,5},{2,10},{10,2},... | collective-permute-start | bytes 589832 | tf_op jit(solution)/shard_map/ppermute | solution.py:23
  36.9 5.2 %copy-start.5 = (bf16[128,1024]{1,0:T(8,128)(2,1)S(1)}, bf16[128,1024]{1,0:T(8,128)(2,1)}, u32[]{:S(2)}) copy-start(bf16[128,1024]{1,0:T(8,128)(2,1)} %convolution_convert_fusion.14) | copy-start | bytes 786436
  39.7 6.5 %collective-permute-start.12 = (bf16[96,1024]{1,0:T(8,128)(2,1)S(1)}, bf16[96,1024]{1,0:T(8,128)(2,1)S(1)}, u32[]{:S(2)}, u32[]{:S(2)}) collective-permute-start(bf16[96,1024]{1,0:T(8,128)(2,1)S(1)} %convolution_convert_fusion.25), channel_id=1, source_target_pairs={{0,4},{4,0},{8,12},{12,8},{1,5},{5,1},{9,13},{13,9},{2,6},{6,2},{1... | collective-permute-start | bytes 589832 | tf_op jit(solution)/shard_map/ppermute | solution.py:23
  42.0 0.9 %copy-start.6 = (bf16[128,1024]{1,0:T(8,128)(2,1)S(1)}, bf16[128,1024]{1,0:T(8,128)(2,1)}, u32[]{:S(2)}) copy-start(bf16[128,1024]{1,0:T(8,128)(2,1)} %convolution_convert_fusion.14) | copy-start | bytes 786436
  42.2 3.9 %copy-start.7 = (bf16[128,1024]{1,0:T(8,128)(2,1)S(1)}, bf16[128,1024]{1,0:T(8,128)(2,1)}, u32[]{:S(2)}) copy-start(bf16[128,1024]{1,0:T(8,128)(2,1)} %convolution_convert_fusion.15) | copy-start | bytes 786436
  42.3 16.3 %collective-permute-start.17 = (bf16[96,1024]{1,0:T(8,128)(2,1)S(1)}, bf16[96,1024]{1,0:T(8,128)(2,1)S(1)}, u32[]{:S(2)}, u32[]{:S(2)}) collective-permute-start(bf16[96,1024]{1,0:T(8,128)(2,1)S(1)} %convolution_convert_fusion.24), channel_id=1, source_target_pairs={{0,8},{8,0},{4,12},{12,4},{1,9},{9,1},{5,13},{13,5},{2,10},{10,2},... | collective-permute-start | bytes 589832 | tf_op jit(solution)/shard_map/ppermute | solution.py:23
  46.4 15.0 %collective-permute-start.18 = (bf16[96,1024]{1,0:T(8,128)(2,1)S(1)}, bf16[96,1024]{1,0:T(8,128)(2,1)S(1)}, u32[]{:S(2)}, u32[]{:S(2)}) collective-permute-start(bf16[96,1024]{1,0:T(8,128)(2,1)S(1)} %convolution_convert_fusion.23), channel_id=1, source_target_pairs={{0,8},{8,0},{4,12},{12,4},{1,9},{9,1},{5,13},{13,5},{2,10},{10,2},... | collective-permute-start | bytes 589832 | tf_op jit(solution)/shard_map/ppermute | solution.py:23
  48.6 5.7 %collective-permute-start.14 = (bf16[8,64]{1,0:T(8,128)(2,1)S(1)}, bf16[8,64]{1,0:T(8,128)(2,1)S(1)}, u32[]{:S(2)}, u32[]{:S(2)}) collective-permute-start(bf16[8,64]{1,0:T(8,128)(2,1)S(1)} %slice_maximum_fusion), channel_id=1, source_target_pairs={{0,2},{2,0},{1,3},{3,1},{4,6},{6,4},{5,7},{7,5},{8,10},{10,8},{9,1... | collective-permute-start | bytes 3080 | tf_op jit(solution)/shard_map/ppermute | solution.py:23
  49.8 8.7 %copy-start.8 = (bf16[128,1024]{1,0:T(8,128)(2,1)S(1)}, bf16[128,1024]{1,0:T(8,128)(2,1)}, u32[]{:S(2)}) copy-start(bf16[128,1024]{1,0:T(8,128)(2,1)} %convolution_convert_fusion.10) | copy-start | bytes 786436
  55.4 6.0 %copy-start.9 = (bf16[128,1024]{1,0:T(8,128)(2,1)S(1)}, bf16[128,1024]{1,0:T(8,128)(2,1)}, u32[]{:S(2)}) copy-start(bf16[128,1024]{1,0:T(8,128)(2,1)} %convolution_convert_fusion.7) | copy-start | bytes 786436

commit v6 on v5

--- a/solution.py
+++ b/solution.py
@@ -5,7 +5,7 @@
 from jax.experimental.pallas import tpu as pltpu
 from jax.sharding import PartitionSpec as P
 
-SIXTEENTHS = (1, 3, 4, 4, 4)
+SHARES = (2, 4, 8, 9, 9)
 ROOM_SIXTEENTHS = 12
 
 
@@ -31,8 +31,28 @@
     return jnp.where(condition, 1.0, 0.0).astype(jnp.bfloat16)
 
 
-def tables_kernel(wide, room, skeleton_ref, compress_ref, full_ref, small_ref, extra_ref):
-    levels, rank = skeleton_ref.shape[1:]
+def sampled_block(sampling, rows):
+    turned = sampling.astype(jnp.float32).T.astype(jnp.bfloat16)
+    return across(turned, rows).astype(jnp.bfloat16)
+
+
+def first_kernel(
+    wide, room, count, skeleton_hbm, compress_hbm, sampling_hbm, traces_hbm,
+    full_ref, small_ref, extra_ref, coeffs_ref,
+    skeleton_ref, compress_ref, sampling_ref, rows_ref, arrived,
+):
+    loads = [
+        pltpu.make_async_copy(skeleton_hbm, skeleton_ref, arrived.at[0]),
+        pltpu.make_async_copy(compress_hbm, compress_ref, arrived.at[1]),
+        pltpu.make_async_copy(sampling_hbm, sampling_ref, arrived.at[2]),
+        pltpu.make_async_copy(traces_hbm.at[pl.ds(0, count)], rows_ref, arrived.at[3]),
+    ]
+    for load in loads:
+        load.start()
+    for load in loads:
+        load.wait()
+    coeffs_ref[...] = sampled_block(sampling_ref[0], rows_ref[...])
+    levels, rank = skeleton_ref.shape[0], skeleton_ref.shape[-1]
     width = 2 * rank
     f32, i32 = jnp.float32, jnp.int32
     k = lax.broadcasted_iota(i32, (width, width), 1)
@@ -51,7 +71,7 @@
     row = lax.broadcasted_iota(i32, (width, width), 0)
     most = jnp.zeros((1, 1), f32)
     for level in range(levels):
-        entry = jnp.broadcast_to(skeleton_ref[0, level : level + 1].astype(f32), (8, rank)).astype(jnp.bfloat16)
+        entry = jnp.broadcast_to(skeleton_ref[level].astype(f32), (8, rank)).astype(jnp.bfloat16)
         entry = across(entry, twice)[:1]
         picked = jnp.where(entry >= rank, 1.0, 0.0)
         slot = across(jnp.broadcast_to(picked, (8, width)).astype(jnp.bfloat16), earlier)[:1].astype(i32)
@@ -80,23 +100,74 @@
         extra_ref[level] = jnp.where(k < rank, extra_ref[level].astype(f32), most).astype(jnp.bfloat16)
 
 
-def tables(skeleton, compress, wide, room):
+def first(skeleton, compress, sampling, traces, wide, room, count):
     levels, rank = skeleton.shape[1:]
     shape = (levels, 2 * rank, 4 * rank)
+    width = sampling.shape[-1]
     whole = pl.BlockSpec(memory_space=pltpu.VMEM)
     return pl.pallas_call(
-        lambda *refs: tables_kernel(wide, room, *refs),
+        lambda *refs: first_kernel(wide, room, count, *refs),
         out_shape=[
             jax.ShapeDtypeStruct(shape, jnp.bfloat16),
             jax.ShapeDtypeStruct(shape, jnp.bfloat16),
             jax.ShapeDtypeStruct((levels, 2 * rank, 2 * rank), jnp.bfloat16),
+            jax.ShapeDtypeStruct((width, count), jnp.bfloat16),
         ],
-        in_specs=[whole] * 2,
-        out_specs=[whole] * 3,
+        in_specs=[pl.BlockSpec(memory_space=pl.ANY)] * 4,
+        out_specs=[whole] * 4,
+        scratch_shapes=[
+            pltpu.VMEM((levels, 1, rank), jnp.int32),
+            pltpu.VMEM(compress.shape, jnp.bfloat16),
+            pltpu.VMEM(sampling.shape, jnp.bfloat16),
+            pltpu.VMEM((count, traces.shape[1]), jnp.bfloat16),
+            pltpu.SemaphoreType.DMA((4,)),
+        ],
         compiler_params=pltpu.CompilerParams(vmem_limit_bytes=16 * 1024 * 1024),
         cost_estimate=pl.CostEstimate(flops=50_000_000, bytes_accessed=600_000, transcendentals=0),
-        name="tables",
-    )(skeleton, compress)
+        name="first",
+    )(skeleton.transpose(1, 0, 2), compress, sampling, traces)
+
+
+def rest_kernel(starts, sampling_hbm, traces_hbm, *refs):
+    pieces = len(starts) - 1
+    outs, (sampling_ref, rows_ref, arrived) = refs[:pieces], refs[pieces:]
+    base = starts[0]
+    loads = [pltpu.make_async_copy(sampling_hbm, sampling_ref, arrived.at[pieces])]
+    for i in range(pieces):
+        span = pl.ds(starts[i], starts[i + 1] - starts[i])
+        here = pl.ds(starts[i] - base, starts[i + 1] - starts[i])
+        loads.append(pltpu.make_async_copy(traces_hbm.at[span], rows_ref.at[here], arrived.at[i]))
+    for load in loads:
+        load.start()
+    loads[0].wait()
+    for i in range(pieces):
+        loads[i + 1].wait()
+        here = pl.ds(starts[i] - base, starts[i + 1] - starts[i])
+        outs[i][...] = sampled_block(sampling_ref[0], rows_ref[here])
+
+
+def rest(sampling, traces, starts):
+    pieces = len(starts) - 1
+    width = sampling.shape[-1]
+    total = starts[-1] - starts[0]
+    return pl.pallas_call(
+        lambda *refs: rest_kernel(starts, *refs),
+        out_shape=[
+            jax.ShapeDtypeStruct((width, starts[i + 1] - starts[i]), jnp.bfloat16) for i in range(pieces)
+        ],
+        in_specs=[pl.BlockSpec(memory_space=pl.ANY)] * 2,
+        out_specs=[pl.BlockSpec(memory_space=pltpu.VMEM)] * pieces,
+        scratch_shapes=[
+            pltpu.VMEM(sampling.shape, jnp.bfloat16),
+            pltpu.VMEM((total, traces.shape[1]), jnp.bfloat16),
+            pltpu.SemaphoreType.DMA((pieces + 1,)),
+        ],
+        compiler_params=pltpu.CompilerParams(vmem_limit_bytes=16 * 1024 * 1024),
+        cost_estimate=pl.CostEstimate(
+            flops=2 * total * width * width, bytes_accessed=4 * total * width, transcendentals=0
+        ),
+        name="rest",
+    )(sampling, traces)
 
 
 def compact_rows(matrix, slot):
@@ -146,7 +217,7 @@
     def turn(at):
         level, piece = at
         if level == 0:
-            return max(0, 2 * piece - 1)
+            return 0 if piece < 2 else 3 if piece == 2 else 2 * piece + 1
         return 2 * (level + piece + (piece > 0))
 
     return sorted(
@@ -156,30 +227,28 @@
 
 
 def local(traces, sampling, skeleton, compress, evaluation):
-    sampling, evaluation = sampling[0], evaluation[0]
     hops = all_hops()
     levels = len(hops)
     wide = lax.axis_size("sub").bit_length() - 1
     rank = skeleton.shape[-1]
     room = rank * ROOM_SIXTEENTHS // 16
-    full, small, extra = tables(skeleton, compress, wide, room)
+    unit = traces.shape[0] // sum(SHARES)
+    pieces = len(SHARES)
+    starts = [unit * sum(SHARES[:i]) for i in range(pieces + 1)]
+    full, small, extra, coeffs = first(skeleton, compress, sampling, traces, wide, room, starts[1])
+    sampling, evaluation = after(sampling, coeffs), evaluation[0]
+    coeffs = [coeffs] + list(rest(sampling, traces, starts[1:]))
     most_here = lax.broadcasted_iota(jnp.int32, extra.shape[1:], 1) >= rank
 
     def compact(level, piece):
         return piece > 0 and level >= wide
 
-    unit = traces.shape[0] // sum(SIXTEENTHS)
-    pieces = len(SIXTEENTHS)
-    starts = [unit * sum(SIXTEENTHS[:i]) for i in range(pieces + 1)]
     inputs, partners, theirs, done = {}, {}, {}, [None] * pieces
     previous, known = None, None
     for level, piece in sequence(pieces, levels):
         count = starts[piece + 1] - starts[piece]
         if level == 0:
-            own = sampled(
-                after(sampling, previous) if piece > 1 else sampling,
-                traces[starts[piece] : starts[piece + 1]],
-            )
+            own = after(coeffs[piece], previous if piece > 1 else None)
         else:
             arrived = after(partners[piece], previous)
             if piece == 0 and level - 1 >= wide:
@@ -211,7 +280,7 @@
     quick = jnp.concatenate(done, 0)
     return lax.cond(
         most[0, 0] > room,
-        lambda: full_width(traces, sampling, full, evaluation),
+        lambda: full_width(traces, sampling[0], full, evaluation),
         lambda: quick,
     )
 

time: 62.9 us -> 72.3 us (1.15)
  waiting for transfers between devices: 17.3 us -> 11.7 us
  starting transfers between devices: 19.2 us -> 23.3 us
  local copies, waits for them, and re-layouts: 2.68 us -> 6.42 us
  matrix products: 21.4 us -> 25 us
  Pallas kernels: 1.09 us -> 3.59 us
    ppermute x16, waiting for transfers between devices: 17.3 us -> 11.7 us  [from_partner(): return lax.ppermute(block, hop[0], route(*hop))]
    ppermute x16, starting transfers between devices: 19.2 us -> 23.3 us  [from_partner(): return lax.ppermute(block, hop[0], route(*hop))]
    dot_general x18, matrix products: 9.4 us -> 13.4 us  [times(): jnp.dot(matrix, value, preferred_element_type=jnp.float32)]
    dot_general x5 -> x0, matrix products: 3.9 us -> none  [sampled(): jnp.einsum('pc,tp->ct', sampling, traces, preferred_element_type=jnp.floa...]
    concatenate x0 -> x4, local copies, waits for them, and re-layouts: none -> 3 us  [local(): value = jnp.concatenate([inputs[piece], arrived[:, :count]], 0)]
    pallas_call x1 -> x2, Pallas kernels: 1.09 us -> 3.59 us  [the longest x1 2.13 us: first(): pl.pallas_call(lambda *refs: first_kernel(wide, room, count, *refs), out_...]
    dot_general x5, matrix products: 7.58 us -> 9.84 us  [evaluated(): jnp.einsum('ct,cp->tp', coeffs, evaluation, preferred_element_type=jnp.fl...]
    dot_general x4, matrix products: 0.49 us -> 1.71 us  [compact_rows(): jnp.dot(slot, half, preferred_element_type=jnp.float32)]
  transfers between devices with their start and end apart: 16 -> 16, of which waited for: 7 -> 5; matrix products, arithmetic and copies ran while one was open for 33% -> 39% of each run, Pallas kernels for 2% -> 2%
where the time goes in v6:
time: 72.3 us; the launch traced here: 71.6 us
  matrix products  25 us (35%)
  starting transfers between devices  23.3 us (32%)
  waiting for transfers between devices  11.7 us (16%)
  local copies, waits for them, and re-layouts  6.42 us (9%)
  Pallas kernels  3.59 us (5%)
  between operations  0.96 us (1%)
    ppermute x16, starting transfers between devices, from_partner(): return lax.ppermute(block, hop[0], route(*hop))  23.3 us
    dot_general x18, matrix products, times(): jnp.dot(matrix, value, preferred_element_type=jnp.float32)  13.4 us
    ppermute x16, waiting for transfers between devices, from_partner(): return lax.ppermute(block, hop[0], route(*hop))  11.7 us
    dot_general x5, matrix products, evaluated(): jnp.einsum('ct,cp->tp', coeffs, evaluation, preferred_element_type=jnp.fl...  9.84 us
    concatenate x4, local copies, waits for them, and re-layouts, local(): value = jnp.concatenate([inputs[piece], arrived[:, :count]], 0)  3 us
    unnamed x40, local copies, waits for them, and re-layouts  2.24 us
    pallas_call x1, Pallas kernels, first(): pl.pallas_call(lambda *refs: first_kernel(wide, room, count, *refs), out_...  2.13 us
    dot_general x4, matrix products, compact_rows(): jnp.dot(slot, half, preferred_element_type=jnp.float32)  1.71 us
  transfers between devices with their start and end apart: 16, of which 5 were waited for; matrix products, arithmetic and copies ran while one was open for 39% of the time, Pallas kernels for 2%

profile of v6, /device:TPU:0, one launch (start us, length us, event | category | flops | bytes accessed | tf_op | source)
XLA Modules:
  0.0 71.6 jit_solution(8943465140040491302)
XLA Ops:
  1.5 2.1 %first.1 = (bf16[3,128,256]{2,1,0:T(8,128)(2,1)S(1)}, bf16[3,128,256]{2,1,0:T(8,128)(2,1)S(1)}, bf16[3,128,128]{2,1,0:T(8,128)(2,1)S(1)}, bf16[128,256]{1,0:T(8,128)(2,1)S(1)}) custom-call(s32[3,1,64]{2,1,0:T(1,128)S(1)} %bitcast.98, bf16[1,3,64,128]{3,2,1,0:T(8,128)(2,1)S(1)} %copy-done, bf16[1,128,128]{2,1,0:T(8,128)(2,1)} %refs_0_, bf16[4096,128]{1,0:T(8,128)(2,1)} %refs_1_.3), custom_call_target="tpu_custom_call" | custom-call | flops 50000000 | bytes 600000 | tf_op jit(solution)/shard_map/first/pallas_call | solution.py:108
  3.6 3.0 %collective-permute-start.3 = (bf16[128,256]{1,0:T(8,128)(2,1)S(1)}, bf16[128,256]{1,0:T(8,128)(2,1)S(1)}, u32[]{:S(2)}, u32[]{:S(2)}) collective-permute-start(bf16[128,256]{1,0:T(8,128)(2,1)S(1)} %get-tuple-element.51), channel_id=1, source_target_pairs={{0,2},{2,0},{1,3},{3,1},{4,6},{6,4},{5,7},{7,5},{8,10},{10,8},{9,1... | collective-permute-start | bytes 196616 | tf_op jit(solution)/shard_map/ppermute | solution.py:23
  6.6 1.5 %rest.1 = (bf16[128,512]{1,0:T(8,128)(2,1)S(1)}, bf16[128,1024]{1,0:T(8,128)(2,1)S(1)}, bf16[128,1152]{1,0:T(8,128)(2,1)S(1)}, bf16[128,1152]{1,0:T(8,128)(2,1)S(1)}) custom-call(bf16[1,128,128]{2,1,0:T(8,128)(2,1)S(1)} %copy-done.5, bf16[4096,128]{1,0:T(8,128)(2,1)S(1)} %copy-done.2), custom_call_target="tpu_custom_call" | custom-call | flops 125829120 | bytes 1966080 | tf_op jit(solution)/shard_map/rest/pallas_call | solution.py:153
  9.1 2.2 %collective-permute-start.4 = (bf16[128,384]{1,0:T(8,128)(2,1)S(1)}, bf16[128,384]{1,0:T(8,128)(2,1)S(1)}, u32[]{:S(2)}, u32[]{:S(2)}) collective-permute-start(bf16[128,384]{1,0:T(8,128)(2,1)S(1)} %pad_maximum_fusion), channel_id=1, source_target_pairs={{0,4},{4,0},{8,12},{12,8},{1,5},{5,1},{9,13},{13,9},{2,6},{6,2},{1... | collective-permute-start | bytes 294920 | tf_op jit(solution)/shard_map/ppermute | solution.py:23
  11.2 1.6 %collective-permute-start.8 = (bf16[128,1024]{1,0:T(8,128)(2,1)S(1)}, bf16[128,1024]{1,0:T(8,128)(2,1)}, u32[]{:S(2)}, u32[]{:S(2)}) collective-permute-start(bf16[128,1024]{1,0:T(8,128)(2,1)S(1)} %get-tuple-element.56), channel_id=1, source_target_pairs={{0,2},{2,0},{1,3},{3,1},{4,6},{6,4},{5,7},{7,5},{8,10},{10,8},{9,1... | collective-permute-start | bytes 786440 | tf_op jit(solution)/shard_map/ppermute | solution.py:23
  12.8 1.0 %collective-permute-done.4 = bf16[128,384]{1,0:T(8,128)(2,1)S(1)} collective-permute-done((bf16[128,384]{1,0:T(8,128)(2,1)S(1)}, bf16[128,384]{1,0:T(8,128)(2,1)S(1)}, u32[]{:S(2)}, u32[]{:S(2)}) %collective-permute-start.4) | collective-permute-done | bytes 98336 | tf_op jit(solution)/shard_map/ppermute | solution.py:23
  14.8 3.1 %collective-permute-start.5 = (bf16[128,384]{1,0:T(8,128)(2,1)S(1)}, bf16[128,384]{1,0:T(8,128)(2,1)S(1)}, u32[]{:S(2)}, u32[]{:S(2)}) collective-permute-start(bf16[128,384]{1,0:T(8,128)(2,1)S(1)} %pad_maximum_fusion.1), channel_id=1, source_target_pairs={{0,8},{8,0},{4,12},{12,4},{1,9},{9,1},{5,13},{13,5},{2,10},{10,2},... | collective-permute-start | bytes 294920 | tf_op jit(solution)/shard_map/ppermute | solution.py:23
  18.9 1.6 %collective-permute-start.7 = (bf16[96,512]{1,0:T(8,128)(2,1)}, bf16[96,512]{1,0:T(8,128)(2,1)}, u32[]{:S(2)}, u32[]{:S(2)}) collective-permute-start(bf16[96,512]{1,0:T(8,128)(2,1)} %convolution_convert_fusion.28), channel_id=1, source_target_pairs={{0,4},{4,0},{8,12},{12,8},{1,5},{5,1},{9,13},{13,9},{2,6},{6,2},{1... | collective-permute-start | bytes 294920 | tf_op jit(solution)/shard_map/ppermute | solution.py:23
  20.4 1.6 %collective-permute-start.11 = (bf16[128,1152]{1,0:T(8,128)(2,1)S(1)}, bf16[128,1152]{1,0:T(8,128)(2,1)}, u32[]{:S(2)}, u32[]{:S(2)}) collective-permute-start(bf16[128,1152]{1,0:T(8,128)(2,1)S(1)} %get-tuple-element.63), channel_id=1, source_target_pairs={{0,2},{2,0},{1,3},{3,1},{4,6},{6,4},{5,7},{7,5},{8,10},{10,8},{9,1... | collective-permute-start | bytes 884744 | tf_op jit(solution)/shard_map/ppermute | solution.py:23
  25.6 1.8 %fusion.38 = bf16[4096,128]{1,0:T(8,128)(2,1)} fusion(bf16[128,256]{1,0:T(8,128)(2,1)} %slice.127, bf16[128,256]{1,0:T(8,128)(2,1)S(1)} %copy-done.8, bf16[3,128,256]{2,1,0:T(8,128)(2,1)S(1)} %get-tuple-element.50, bf16[1,128,128]{2,1,0:T(8,128)(2,1)} %param.11), kind=kOutput, calls=%fused_computation.64 | convolution fusion | flops 25493504 | bytes 294912 | tf_op jit(solution)/shard_map/ct,cp->tp/dot_general | solution.py:193
  27.5 1.0 %constant_dynamic-update-slice_fusion.2 = bf16[256,1024]{1,0:T(8,128)(2,1)S(1)} fusion(bf16[256,1024]{1,0:T(8,128)(2,1)S(1)} %constant_dynamic-update-slice_fusion.3, bf16[128,1024]{1,0:T(8,128)(2,1)} %collective-permute-done.8), kind=kLoop, calls=%fused_computation.162 | loop fusion | bytes 524288 | tf_op jit(solution)/shard_map/concatenate | solution.py:257
  29.3 1.1 %convolution_convert_fusion.27 = bf16[96,512]{1,0:T(8,128)(2,1)S(1)} fusion(bf16[96,512]{1,0:T(8,128)(2,1)} %collective-permute-done.7, bf16[128,512]{1,0:T(8,128)(2,1)S(1)} %copy-done.6, bf16[48,256]{1,0:T(8,128)(2,1)S(1)} %copy-done.9, bf16[48,256]{1,0:T(8,128)(2,1)S(1)} %copy-done.11), kind=kOutput, calls=%fused_computation.61 | convolution fusion | flops 26230784 | bytes 376832 | tf_op jit(solution)/shard_map/dot_general | solution.py:183
  30.4 2.8 %collective-permute-start.15 = (bf16[96,512]{1,0:T(8,128)(2,1)S(1)}, bf16[96,512]{1,0:T(8,128)(2,1)}, u32[]{:S(2)}, u32[]{:S(2)}) collective-permute-start(bf16[96,512]{1,0:T(8,128)(2,1)S(1)} %convolution_convert_fusion.27), channel_id=1, source_target_pairs={{0,8},{8,0},{4,12},{12,4},{1,9},{9,1},{5,13},{13,5},{2,10},{10,2},... | collective-permute-start | bytes 294920 | tf_op jit(solution)/shard_map/ppermute | solution.py:23
  33.1 1.6 %collective-permute-start.9 = (bf16[128,1152]{1,0:T(8,128)(2,1)S(1)}, bf16[128,1152]{1,0:T(8,128)(2,1)}, u32[]{:S(2)}, u32[]{:S(2)}) collective-permute-start(bf16[128,1152]{1,0:T(8,128)(2,1)S(1)} %get-tuple-element.66), channel_id=1, source_target_pairs={{0,2},{2,0},{1,3},{3,1},{4,6},{6,4},{5,7},{7,5},{8,10},{10,8},{9,1... | collective-permute-start | bytes 884744 | tf_op jit(solution)/shard_map/ppermute | solution.py:23
  34.7 1.8 %convolution_convert_fusion.25 = bf16[128,512]{1,0:T(8,128)(2,1)} fusion(bf16[96,512]{1,0:T(8,128)(2,1)} %collective-permute-done.7, bf16[128,512]{1,0:T(8,128)(2,1)S(1)} %copy-done.6, bf16[3,128,256]{2,1,0:T(8,128)(2,1)S(1)} %get-tuple-element.60), kind=kOutput, calls=%fused_computation.59 | convolution fusion | flops 34537472 | bytes 425984 | tf_op jit(solution)/shard_map/dot_general | solution.py:183
  36.8 1.0 %constant_dynamic-update-slice_fusion.4 = bf16[256,1152]{1,0:T(8,128)(2,1)S(1)} fusion(bf16[256,1152]{1,0:T(8,128)(2,1)S(1)} %constant_dynamic-update-slice_fusion.5, bf16[128,1152]{1,0:T(8,128)(2,1)} %collective-permute-done.11), kind=kLoop, calls=%fused_computation.164 | loop fusion | bytes 589824 | tf_op jit(solution)/shard_map/concatenate | solution.py:257
  37.8 0.9 %convolution_convert_fusion.16 = bf16[96,1152]{1,0:T(8,128)(2,1)} fusion(bf16[256,1152]{1,0:T(8,128)(2,1)S(1)} %constant_dynamic-update-slice_fusion.4, bf16[48,256]{1,0:T(8,128)(2,1)S(1)} %convolution_convert_fusion.35, bf16[48,256]{1,0:T(8,128)(2,1)S(1)} %convolution_convert_fusion.36), kind=kOutput, calls=%fused_computation.39 | convolution fusion | flops 56832000 | bytes 860160 | tf_op jit(solution)/shard_map/dot_general | solution.py:183
  39.9 1.0 %collective-permute-start.16 = (bf16[96,1024]{1,0:T(8,128)(2,1)}, bf16[96,1024]{1,0:T(8,128)(2,1)}, u32[]{:S(2)}, u32[]{:S(2)}) collective-permute-start(bf16[96,1024]{1,0:T(8,128)(2,1)} %convolution_convert_fusion.21), channel_id=1, source_target_pairs={{0,8},{8,0},{4,12},{12,4},{1,9},{9,1},{5,13},{13,5},{2,10},{10,2},... | collective-permute-start | bytes 589832 | tf_op jit(solution)/shard_map/ppermute | solution.py:23
  40.9 2.0 %fusion.37 = bf16[4096,128]{1,0:T(8,128)(2,1)} fusion(bf16[4096,128]{1,0:T(8,128)(2,1)} %fusion.38, bf16[96,512]{1,0:T(8,128)(2,1)} %collective-permute-done.15, bf16[128,512]{1,0:T(8,128)(2,1)S(1)} %copy-done.16, bf16[3,128,256]{2,1,0:T(8,128)(2,1)S(1)} %get-tuple-element.60, bf16[1,128,128]{2,1,0:T(8,128)(2,1)} %param.11), kind=kOutput, calls=%fused_computation.57 | convolution fusion | flops 51380224 | bytes 458752 | tf_op jit(solution)/shard_map/ct,cp->tp/dot_general | solution.py:193
  42.9 0.9 %convolution_convert_fusion.19 = bf16[128,1024]{1,0:T(8,128)(2,1)} fusion(bf16[96,1024]{1,0:T(8,128)(2,1)S(1)} %copy-done.15, bf16[128,1024]{1,0:T(8,128)(2,1)S(1)} %convolution_convert_fusion.20, bf16[3,128,256]{2,1,0:T(8,128)(2,1)S(1)} %get-tuple-element.60), kind=kOutput, calls=%fused_computation.43 | convolution fusion | flops 69074944 | bytes 786432 | tf_op jit(solution)/shard_map/dot_general | solution.py:183
  43.8 1.0 %constant_dynamic-update-slice_fusion.6 = bf16[256,1152]{1,0:T(8,128)(2,1)S(1)} fusion(bf16[256,1152]{1,0:T(8,128)(2,1)S(1)} %constant_dynamic-update-slice_fusion.7, bf16[128,1152]{1,0:T(8,128)(2,1)} %collective-permute-done.9), kind=kLoop, calls=%fused_computation.166 | loop fusion | bytes 589824 | tf_op jit(solution)/shard_map/concatenate | solution.py:257
  45.1 1.2 %collective-permute-start.12 = (bf16[96,1152]{1,0:T(8,128)(2,1)S(1)}, bf16[96,1152]{1,0:T(8,128)(2,1)}, u32[]{:S(2)}, u32[]{:S(2)}) collective-permute-start(bf16[96,1152]{1,0:T(8,128)(2,1)S(1)} %convolution_convert_fusion.15), channel_id=1, source_target_pairs={{0,4},{4,0},{8,12},{12,8},{1,5},{5,1},{9,13},{13,9},{2,6},{6,2},{1... | collective-permute-start | bytes 663560 | tf_op jit(solution)/shard_map/ppermute | solution.py:23
  46.5 4.3 %collective-permute-done.13 = bf16[96,1152]{1,0:T(8,128)(2,1)} collective-permute-done((bf16[96,1152]{1,0:T(8,128)(2,1)}, bf16[96,1152]{1,0:T(8,128)(2,1)}, u32[]{:S(2)}, u32[]{:S(2)}) %collective-permute-start.13) | collective-permute-done | bytes 221216 | tf_op jit(solution)/shard_map/ppermute | solution.py:23
  50.8 1.2 %convolution_convert_fusion.14 = bf16[96,1152]{1,0:T(8,128)(2,1)S(1)} fusion(bf16[96,1152]{1,0:T(8,128)(2,1)} %collective-permute-done.13, bf16[128,1152]{1,0:T(8,128)(2,1)S(1)} %convolution_convert_fusion.11, bf16[48,256]{1,0:T(8,128)(2,1)S(1)} %copy-done.10, bf16[48,256]{1,0:T(8,128)(2,1)S(1)} %copy-done.12), kind=kOutput, calls=%fused_computation.37 | convolution fusion | flops 58896384 | bytes 786432 | tf_op jit(solution)/shard_map/dot_general | solution.py:183
  52.0 1.2 %convolution_convert_fusion.10 = bf16[128,1152]{1,0:T(8,128)(2,1)S(1)} fusion(bf16[96,1152]{1,0:T(8,128)(2,1)} %collective-permute-done.13, bf16[128,1152]{1,0:T(8,128)(2,1)S(1)} %convolution_convert_fusion.11, bf16[3,128,256]{2,1,0:T(8,128)(2,1)S(1)} %get-tuple-element.60), kind=kOutput, calls=%fused_computation.33 | convolution fusion | flops 77709312 | bytes 876544 | tf_op jit(solution)/shard_map/dot_general | solution.py:183
  53.2 2.1 %fusion.28 = bf16[4096,128]{1,0:T(8,128)(2,1)} fusion(bf16[4096,128]{1,0:T(8,128)(2,1)} %fusion.37, bf16[96,1024]{1,0:T(8,128)(2,1)} %collective-permute-done.16, bf16[128,1024]{1,0:T(8,128)(2,1)S(1)} %copy-done.17, bf16[3,128,256]{2,1,0:T(8,128)(2,1)S(1)} %get-tuple-element.60, bf16[1,128,128]{2,1,0:T(8,128)(2,1)} %param.11), kind=kOutput, calls=%fused_computation.41 | convolution fusion | flops 102760448 | bytes 819200 | tf_op jit(solution)/shard_map/ct,cp->tp/dot_general | solution.py:193
  55.3 1.2 %convolution_convert_fusion.13 = bf16[96,1152]{1,0:T(8,128)(2,1)S(1)} fusion(bf16[96,1152]{1,0:T(8,128)(2,1)} %collective-permute-done.12, bf16[128,1152]{1,0:T(8,128)(2,1)S(1)} %convolution_convert_fusion.12, bf16[48,256]{1,0:T(8,128)(2,1)S(1)} %copy-done.10, bf16[48,256]{1,0:T(8,128)(2,1)S(1)} %copy-done.12), kind=kOutput, calls=%fused_computation.36 | convolution fusion | flops 58896384 | bytes 786432 | tf_op jit(solution)/shard_map/dot_general | solution.py:183
  56.7 1.2 %convolution_convert_fusion.7 = bf16[128,1152]{1,0:T(8,128)(2,1)S(1)} fusion(bf16[96,1152]{1,0:T(8,128)(2,1)} %collective-permute-done.12, bf16[128,1152]{1,0:T(8,128)(2,1)S(1)} %convolution_convert_fusion.12, bf16[3,128,256]{2,1,0:T(8,128)(2,1)S(1)} %get-tuple-element.60), kind=kOutput, calls=%fused_computation.29 | convolution fusion | flops 77709312 | bytes 876544 | tf_op jit(solution)/shard_map/dot_general | solution.py:183
  57.8 2.9 %collective-permute-start.18 = (bf16[96,1152]{1,0:T(8,128)(2,1)S(1)}, bf16[96,1152]{1,0:T(8,128)(2,1)S(1)}, u32[]{:S(2)}, u32[]{:S(2)}) collective-permute-start(bf16[96,1152]{1,0:T(8,128)(2,1)S(1)} %convolution_convert_fusion.13), channel_id=1, source_target_pairs={{0,8},{8,0},{4,12},{12,4},{1,9},{9,1},{5,13},{13,5},{2,10},{10,2},... | collective-permute-start | bytes 663560 | tf_op jit(solution)/shard_map/ppermute | solution.py:23
  62.0 5.2 %collective-permute-done.17 = bf16[96,1152]{1,0:T(8,128)(2,1)S(1)} collective-permute-done((bf16[96,1152]{1,0:T(8,128)(2,1)S(1)}, bf16[96,1152]{1,0:T(8,128)(2,1)S(1)}, u32[]{:S(2)}, u32[]{:S(2)}) %collective-permute-start.17) | collective-permute-done | bytes 221216 | tf_op jit(solution)/shard_map/ppermute | solution.py:23
  67.2 2.0 %fusion.27 = bf16[4096,128]{1,0:T(8,128)(2,1)} fusion(bf16[4096,128]{1,0:T(8,128)(2,1)} %fusion.28, bf16[96,1152]{1,0:T(8,128)(2,1)S(1)} %collective-permute-done.17, bf16[128,1152]{1,0:T(8,128)(2,1)S(1)} %convolution_convert_fusion.10, bf16[3,128,256]{2,1,0:T(8,128)(2,1)S(1)} %get-tuple-element.60, bf16[1,128,128]{2,1,0:T(8,128)(2,1)} %param.11), kind=kOutput, calls=%fused_computation.31 | convolution fusion | flops 115605504 | bytes 909312 | tf_op jit(solution)/shard_map/ct,cp->tp/dot_general | solution.py:193
  69.7 2.0 %fusion.26 = bf16[4096,128]{1,0:T(8,128)(2,1)} fusion(bf16[4096,128]{1,0:T(8,128)(2,1)} %fusion.27, bf16[96,1152]{1,0:T(8,128)(2,1)S(1)} %collective-permute-done.18, bf16[128,1152]{1,0:T(8,128)(2,1)S(1)} %convolution_convert_fusion.7, bf16[3,128,256]{2,1,0:T(8,128)(2,1)S(1)} %get-tuple-element.60, bf16[1,128,128]{2,1,0:T(8,128)(2,1)} %param.11), kind=kOutput, calls=%fused_computation.27 | convolution fusion | flops 115605504 | bytes 909312 | tf_op jit(solution)/shard_map/ct,cp->tp/dot_general | solution.py:193
  (85 shorter events, 11.9 us)
Async XLA Ops:
  0.0 0.8 %copy-start = (bf16[1,3,64,128]{3,2,1,0:T(8,128)(2,1)S(1)}, bf16[1,3,64,128]{3,2,1,0:T(8,128)(2,1)}, u32[]{:S(2)}) copy-start(bf16[1,3,64,128]{3,2,1,0:T(8,128)(2,1)} %refs_1_.2) | copy-start | bytes 147460
  1.5 5.2 %copy-start.2 = (bf16[4096,128]{1,0:T(8,128)(2,1)S(1)}, bf16[4096,128]{1,0:T(8,128)(2,1)}, u32[]{:S(2)}) copy-start(bf16[4096,128]{1,0:T(8,128)(2,1)} %refs_1_.3) | copy-start | bytes 3145732
  1.5 5.2 %copy-start.5 = (bf16[1,128,128]{2,1,0:T(8,128)(2,1)S(1)}, bf16[1,128,128]{2,1,0:T(8,128)(2,1)}, u32[]{:S(2)}) copy-start(bf16[1,128,128]{2,1,0:T(8,128)(2,1)} %refs_0_) | copy-start | bytes 98308
  3.6 5.2 %collective-permute-start.3 = (bf16[128,256]{1,0:T(8,128)(2,1)S(1)}, bf16[128,256]{1,0:T(8,128)(2,1)S(1)}, u32[]{:S(2)}, u32[]{:S(2)}) collective-permute-start(bf16[128,256]{1,0:T(8,128)(2,1)S(1)} %get-tuple-element.51), channel_id=1, source_target_pairs={{0,2},{2,0},{1,3},{3,1},{4,6},{6,4},{5,7},{7,5},{8,10},{10,8},{9,1... | collective-permute-start | bytes 196616 | tf_op jit(solution)/shard_map/ppermute | solution.py:23
  8.1 9.9 %collective-permute-start.6 = (bf16[128,512]{1,0:T(8,128)(2,1)S(1)}, bf16[128,512]{1,0:T(8,128)(2,1)S(1)}, u32[]{:S(2)}, u32[]{:S(2)}) collective-permute-start(bf16[128,512]{1,0:T(8,128)(2,1)S(1)} %get-tuple-element.53), channel_id=1, source_target_pairs={{0,2},{2,0},{1,3},{3,1},{4,6},{6,4},{5,7},{7,5},{8,10},{10,8},{9,1... | collective-permute-start | bytes 393224 | tf_op jit(solution)/shard_map/ppermute | solution.py:23
  9.1 4.8 %collective-permute-start.4 = (bf16[128,384]{1,0:T(8,128)(2,1)S(1)}, bf16[128,384]{1,0:T(8,128)(2,1)S(1)}, u32[]{:S(2)}, u32[]{:S(2)}) collective-permute-start(bf16[128,384]{1,0:T(8,128)(2,1)S(1)} %pad_maximum_fusion), channel_id=1, source_target_pairs={{0,4},{4,0},{8,12},{12,8},{1,5},{5,1},{9,13},{13,9},{2,6},{6,2},{1... | collective-permute-start | bytes 294920 | tf_op jit(solution)/shard_map/ppermute | solution.py:23
  11.2 16.3 %collective-permute-start.8 = (bf16[128,1024]{1,0:T(8,128)(2,1)S(1)}, bf16[128,1024]{1,0:T(8,128)(2,1)}, u32[]{:S(2)}, u32[]{:S(2)}) collective-permute-start(bf16[128,1024]{1,0:T(8,128)(2,1)S(1)} %get-tuple-element.56), channel_id=1, source_target_pairs={{0,2},{2,0},{1,3},{3,1},{4,6},{6,4},{5,7},{7,5},{8,10},{10,8},{9,1... | collective-permute-start | bytes 786440 | tf_op jit(solution)/shard_map/ppermute | solution.py:23
  14.8 8.1 %collective-permute-start.5 = (bf16[128,384]{1,0:T(8,128)(2,1)S(1)}, bf16[128,384]{1,0:T(8,128)(2,1)S(1)}, u32[]{:S(2)}, u32[]{:S(2)}) collective-permute-start(bf16[128,384]{1,0:T(8,128)(2,1)S(1)} %pad_maximum_fusion.1), channel_id=1, source_target_pairs={{0,8},{8,0},{4,12},{12,4},{1,9},{9,1},{5,13},{13,5},{2,10},{10,2},... | collective-permute-start | bytes 294920 | tf_op jit(solution)/shard_map/ppermute | solution.py:23
  18.0 7.6 %copy-start.8 = (bf16[128,256]{1,0:T(8,128)(2,1)S(1)}, bf16[128,256]{1,0:T(8,128)(2,1)}, u32[]{:S(2)}) copy-start(bf16[128,256]{1,0:T(8,128)(2,1)} %copy-done.7) | copy-start | bytes 196612
  18.9 10.4 %collective-permute-start.7 = (bf16[96,512]{1,0:T(8,128)(2,1)}, bf16[96,512]{1,0:T(8,128)(2,1)}, u32[]{:S(2)}, u32[]{:S(2)}) collective-permute-start(bf16[96,512]{1,0:T(8,128)(2,1)} %convolution_convert_fusion.28), channel_id=1, source_target_pairs={{0,4},{4,0},{8,12},{12,8},{1,5},{5,1},{9,13},{13,9},{2,6},{6,2},{1... | collective-permute-start | bytes 294920 | tf_op jit(solution)/shard_map/ppermute | solution.py:23
  20.4 16.3 %collective-permute-start.11 = (bf16[128,1152]{1,0:T(8,128)(2,1)S(1)}, bf16[128,1152]{1,0:T(8,128)(2,1)}, u32[]{:S(2)}, u32[]{:S(2)}) collective-permute-start(bf16[128,1152]{1,0:T(8,128)(2,1)S(1)} %get-tuple-element.63), channel_id=1, source_target_pairs={{0,2},{2,0},{1,3},{3,1},{4,6},{6,4},{5,7},{7,5},{8,10},{10,8},{9,1... | collective-permute-start | bytes 884744 | tf_op jit(solution)/shard_map/ppermute | solution.py:23
  27.5 1.8 %copy-start.6 = (bf16[128,512]{1,0:T(8,128)(2,1)S(1)}, bf16[128,512]{1,0:T(8,128)(2,1)}, u32[]{:S(2)}) copy-start(bf16[128,512]{1,0:T(8,128)(2,1)} %convolution_convert_fusion.26) | copy-start | bytes 393220
  27.5 1.8 %copy-start.9 = (bf16[48,256]{1,0:T(8,128)(2,1)S(1)}, bf16[48,256]{1,0:T(8,128)(2,1)}, u32[]{:S(2)}) copy-start(bf16[48,256]{1,0:T(8,128)(2,1)} %convolution_convert_fusion.33) | copy-start | bytes 73732
  27.5 1.8 %copy-start.11 = (bf16[48,256]{1,0:T(8,128)(2,1)S(1)}, bf16[48,256]{1,0:T(8,128)(2,1)}, u32[]{:S(2)}) copy-start(bf16[48,256]{1,0:T(8,128)(2,1)} %convolution_convert_fusion.34) | copy-start | bytes 73732
  28.5 4.6 %copy-start.3 = (bf16[256,1024]{1,0:T(8,128)(2,1)}, bf16[256,1024]{1,0:T(8,128)(2,1)S(1)}, u32[]{:S(2)}) copy-start(bf16[256,1024]{1,0:T(8,128)(2,1)S(1)} %constant_dynamic-update-slice_fusion.2) | copy-start | bytes 1572868
  28.7 10.3 %collective-permute-start.10 = (bf16[96,1024]{1,0:T(8,128)(2,1)S(1)}, bf16[96,1024]{1,0:T(8,128)(2,1)S(1)}, u32[]{:S(2)}, u32[]{:S(2)}) collective-permute-start(bf16[96,1024]{1,0:T(8,128)(2,1)S(1)} %convolution_convert_fusion.22), channel_id=1, source_target_pairs={{0,4},{4,0},{8,12},{12,8},{1,5},{5,1},{9,13},{13,9},{2,6},{6,2},{1... | collective-permute-start | bytes 589832 | tf_op jit(solution)/shard_map/ppermute | solution.py:23
  30.4 10.5 %collective-permute-start.15 = (bf16[96,512]{1,0:T(8,128)(2,1)S(1)}, bf16[96,512]{1,0:T(8,128)(2,1)}, u32[]{:S(2)}, u32[]{:S(2)}) collective-permute-start(bf16[96,512]{1,0:T(8,128)(2,1)S(1)} %convolution_convert_fusion.27), channel_id=1, source_target_pairs={{0,8},{8,0},{4,12},{12,4},{1,9},{9,1},{5,13},{13,5},{2,10},{10,2},... | collective-permute-start | bytes 294920 | tf_op jit(solution)/shard_map/ppermute | solution.py:23
  33.1 10.7 %collective-permute-start.9 = (bf16[128,1152]{1,0:T(8,128)(2,1)S(1)}, bf16[128,1152]{1,0:T(8,128)(2,1)}, u32[]{:S(2)}, u32[]{:S(2)}) collective-permute-start(bf16[128,1152]{1,0:T(8,128)(2,1)S(1)} %get-tuple-element.66), channel_id=1, source_target_pairs={{0,2},{2,0},{1,3},{3,1},{4,6},{6,4},{5,7},{7,5},{8,10},{10,8},{9,1... | collective-permute-start | bytes 884744 | tf_op jit(solution)/shard_map/ppermute | solution.py:23
  34.7 1.8 %copy-start.4 = (bf16[256,1024]{1,0:T(8,128)(2,1)S(1)}, bf16[256,1024]{1,0:T(8,128)(2,1)}, u32[]{:S(2)}) copy-start(bf16[256,1024]{1,0:T(8,128)(2,1)} %copy-done.3) | copy-start | bytes 1572868
  38.7 12.1 %collective-permute-start.13 = (bf16[96,1152]{1,0:T(8,128)(2,1)}, bf16[96,1152]{1,0:T(8,128)(2,1)}, u32[]{:S(2)}, u32[]{:S(2)}) collective-permute-start(bf16[96,1152]{1,0:T(8,128)(2,1)} %convolution_convert_fusion.16), channel_id=1, source_target_pairs={{0,4},{4,0},{8,12},{12,8},{1,5},{5,1},{9,13},{13,9},{2,6},{6,2},{1... | collective-permute-start | bytes 663560 | tf_op jit(solution)/shard_map/ppermute | solution.py:23
  39.0 1.9 %copy-start.16 = (bf16[128,512]{1,0:T(8,128)(2,1)S(1)}, bf16[128,512]{1,0:T(8,128)(2,1)}, u32[]{:S(2)}) copy-start(bf16[128,512]{1,0:T(8,128)(2,1)} %convolution_convert_fusion.25) | copy-start | bytes 393220
  39.0 0.9 %copy-start.14 = (bf16[96,1024]{1,0:T(8,128)(2,1)}, bf16[96,1024]{1,0:T(8,128)(2,1)S(1)}, u32[]{:S(2)}) copy-start(bf16[96,1024]{1,0:T(8,128)(2,1)S(1)} %collective-permute-done.10) | copy-start | bytes 589828
  39.9 13.3 %collective-permute-start.16 = (bf16[96,1024]{1,0:T(8,128)(2,1)}, bf16[96,1024]{1,0:T(8,128)(2,1)}, u32[]{:S(2)}, u32[]{:S(2)}) collective-permute-start(bf16[96,1024]{1,0:T(8,128)(2,1)} %convolution_convert_fusion.21), channel_id=1, source_target_pairs={{0,8},{8,0},{4,12},{12,4},{1,9},{9,1},{5,13},{13,5},{2,10},{10,2},... | collective-permute-start | bytes 589832 | tf_op jit(solution)/shard_map/ppermute | solution.py:23
  40.9 2.0 %copy-start.15 = (bf16[96,1024]{1,0:T(8,128)(2,1)S(1)}, bf16[96,1024]{1,0:T(8,128)(2,1)}, u32[]{:S(2)}) copy-start(bf16[96,1024]{1,0:T(8,128)(2,1)} %copy-done.14) | copy-start | bytes 589828
  44.8 6.0 %copy-start.10 = (bf16[48,256]{1,0:T(8,128)(2,1)S(1)}, bf16[48,256]{1,0:T(8,128)(2,1)}, u32[]{:S(2)}) copy-start(bf16[48,256]{1,0:T(8,128)(2,1)} %convolution_convert_fusion.33) | copy-start | bytes 73732
  44.8 6.0 %copy-start.12 = (bf16[48,256]{1,0:T(8,128)(2,1)S(1)}, bf16[48,256]{1,0:T(8,128)(2,1)}, u32[]{:S(2)}) copy-start(bf16[48,256]{1,0:T(8,128)(2,1)} %convolution_convert_fusion.34) | copy-start | bytes 73732
  45.1 10.3 %collective-permute-start.12 = (bf16[96,1152]{1,0:T(8,128)(2,1)S(1)}, bf16[96,1152]{1,0:T(8,128)(2,1)}, u32[]{:S(2)}, u32[]{:S(2)}) collective-permute-start(bf16[96,1152]{1,0:T(8,128)(2,1)S(1)} %convolution_convert_fusion.15), channel_id=1, source_target_pairs={{0,4},{4,0},{8,12},{12,8},{1,5},{5,1},{9,13},{13,9},{2,6},{6,2},{1... | collective-permute-start | bytes 663560 | tf_op jit(solution)/shard_map/ppermute | solution.py:23
  51.9 1.3 %copy-start.17 = (bf16[128,1024]{1,0:T(8,128)(2,1)S(1)}, bf16[128,1024]{1,0:T(8,128)(2,1)}, u32[]{:S(2)}) copy-start(bf16[128,1024]{1,0:T(8,128)(2,1)} %convolution_convert_fusion.19) | copy-start | bytes 786436
  52.0 15.2 %collective-permute-start.17 = (bf16[96,1152]{1,0:T(8,128)(2,1)S(1)}, bf16[96,1152]{1,0:T(8,128)(2,1)S(1)}, u32[]{:S(2)}, u32[]{:S(2)}) collective-permute-start(bf16[96,1152]{1,0:T(8,128)(2,1)S(1)} %convolution_convert_fusion.14), channel_id=1, source_target_pairs={{0,8},{8,0},{4,12},{12,4},{1,9},{9,1},{5,13},{13,5},{2,10},{10,2},... | collective-permute-start | bytes 663560 | tf_op jit(solution)/shard_map/ppermute | solution.py:23
  55.3 1.2 %copy-start.13 = (bf16[8,64]{1,0:T(8,128)(2,1)S(1)}, bf16[8,64]{1,0:T(8,128)(2,1)}, u32[]{:S(2)}) copy-start(bf16[8,64]{1,0:T(8,128)(2,1)} %slice_maximum_fusion) | copy-start | bytes 3076
  56.5 4.2 %collective-permute-start.14 = (bf16[8,64]{1,0:T(8,128)(2,1)S(1)}, bf16[8,64]{1,0:T(8,128)(2,1)S(1)}, u32[]{:S(2)}, u32[]{:S(2)}) collective-permute-start(bf16[8,64]{1,0:T(8,128)(2,1)S(1)} %copy-done.13), channel_id=1, source_target_pairs={{0,2},{2,0},{1,3},{3,1},{4,6},{6,4},{5,7},{7,5},{8,10},{10,8},{9,1... | collective-permute-start | bytes 3080 | tf_op jit(solution)/shard_map/ppermute | solution.py:23
  57.8 11.8 %collective-permute-start.18 = (bf16[96,1152]{1,0:T(8,128)(2,1)S(1)}, bf16[96,1152]{1,0:T(8,128)(2,1)S(1)}, u32[]{:S(2)}, u32[]{:S(2)}) collective-permute-start(bf16[96,1152]{1,0:T(8,128)(2,1)S(1)} %convolution_convert_fusion.13), channel_id=1, source_target_pairs={{0,8},{8,0},{4,12},{12,4},{1,9},{9,1},{5,13},{13,5},{2,10},{10,2},... | collective-permute-start | bytes 663560 | tf_op jit(solution)/shard_map/ppermute | solution.py:23
  (2 other events, 1.3 us)

commit v7 on v6

--- a/solution.py
+++ b/solution.py
@@ -5,7 +5,9 @@
 from jax.experimental.pallas import tpu as pltpu
 from jax.sharding import PartitionSpec as P
 
-SHARES = (2, 4, 8, 9, 9)
+SHARES = (1, 3, 8, 10, 10)
+FULL_PIECES = 2
+KERNEL_VMEM = 60 * 1024 * 1024
 ROOM_SIXTEENTHS = 12
 
 
@@ -122,52 +124,47 @@
             pltpu.VMEM((count, traces.shape[1]), jnp.bfloat16),
             pltpu.SemaphoreType.DMA((4,)),
         ],
-        compiler_params=pltpu.CompilerParams(vmem_limit_bytes=16 * 1024 * 1024),
+        compiler_params=pltpu.CompilerParams(vmem_limit_bytes=KERNEL_VMEM),
         cost_estimate=pl.CostEstimate(flops=50_000_000, bytes_accessed=600_000, transcendentals=0),
         name="first",
     )(skeleton.transpose(1, 0, 2), compress, sampling, traces)
 
 
-def rest_kernel(starts, sampling_hbm, traces_hbm, *refs):
-    pieces = len(starts) - 1
-    outs, (sampling_ref, rows_ref, arrived) = refs[:pieces], refs[pieces:]
-    base = starts[0]
-    loads = [pltpu.make_async_copy(sampling_hbm, sampling_ref, arrived.at[pieces])]
-    for i in range(pieces):
-        span = pl.ds(starts[i], starts[i + 1] - starts[i])
-        here = pl.ds(starts[i] - base, starts[i + 1] - starts[i])
-        loads.append(pltpu.make_async_copy(traces_hbm.at[span], rows_ref.at[here], arrived.at[i]))
-    for load in loads:
-        load.start()
-    loads[0].wait()
-    for i in range(pieces):
-        loads[i + 1].wait()
-        here = pl.ds(starts[i] - base, starts[i + 1] - starts[i])
-        outs[i][...] = sampled_block(sampling_ref[0], rows_ref[here])
-
-
-def rest(sampling, traces, starts):
-    pieces = len(starts) - 1
-    width = sampling.shape[-1]
-    total = starts[-1] - starts[0]
+def sampled_apart(sampling, traces):
+    count, width = traces.shape
+    block = count // 8
+
+    def kernel(sampling_ref, rows_ref, coeffs_ref):
+        coeffs_ref[...] = sampled_block(sampling_ref[...], rows_ref[...])
+
     return pl.pallas_call(
-        lambda *refs: rest_kernel(starts, *refs),
-        out_shape=[
-            jax.ShapeDtypeStruct((width, starts[i + 1] - starts[i]), jnp.bfloat16) for i in range(pieces)
+        kernel,
+        grid=(count // block,),
+        out_shape=jax.ShapeDtypeStruct((sampling.shape[1], count), jnp.bfloat16),
+        in_specs=[
+            pl.BlockSpec(sampling.shape, lambda i: (0, 0)),
+            pl.BlockSpec((block, width), lambda i: (i, 0)),
         ],
-        in_specs=[pl.BlockSpec(memory_space=pl.ANY)] * 2,
-        out_specs=[pl.BlockSpec(memory_space=pltpu.VMEM)] * pieces,
-        scratch_shapes=[
-            pltpu.VMEM(sampling.shape, jnp.bfloat16),
-            pltpu.VMEM((total, traces.shape[1]), jnp.bfloat16),
-            pltpu.SemaphoreType.DMA((pieces + 1,)),
-        ],
-        compiler_params=pltpu.CompilerParams(vmem_limit_bytes=16 * 1024 * 1024),
-        cost_estimate=pl.CostEstimate(
-            flops=2 * total * width * width, bytes_accessed=4 * total * width, transcendentals=0
-        ),
-        name="rest",
+        out_specs=pl.BlockSpec((sampling.shape[1], block), lambda i: (0, i)),
+        compiler_params=pltpu.CompilerParams(vmem_limit_bytes=63 * 1024 * 1024),
+        name="sampled_apart",
     )(sampling, traces)
+
+
+def picked_columns(compress, skeleton):
+    rank = skeleton.shape[-1]
+    places = lax.broadcasted_iota(jnp.int32, (1, 1, 2 * rank), 2)
+    chooser = (skeleton[:, :, None] == places).astype(jnp.bfloat16)
+    stacked = jnp.concatenate([compress[:, :, :rank], compress[:, :, rank:]], 1)
+    return jnp.einsum(
+        "ljk,lki->lji", stacked, chooser, preferred_element_type=jnp.float32
+    ).astype(jnp.bfloat16)
+
+
+def real_form(both):
+    rank = both.shape[1] // 2
+    turned = jnp.concatenate([-both[:, rank:], both[:, :rank]], 1)
+    return jnp.concatenate([both, turned], 2)
 
 
 def compact_rows(matrix, slot):
@@ -205,8 +202,11 @@
     return [("sub", bit) for bit in range(low_bits)] + [("bfly", bit) for bit in range(high_bits)]
 
 
-def full_width(traces, sampling, full, evaluation):
-    coeffs = sampled(sampling, traces)
+def full_width(traces, sampling, skeleton, compress, evaluation):
+    rank = skeleton.shape[-1]
+    columns = picked_columns(compress, skeleton)
+    full = jnp.concatenate([real_form(columns[..., :rank]), real_form(columns[..., rank:])], 2)
+    coeffs = sampled_apart(sampling, traces)
     for level, hop in enumerate(all_hops()):
         partner = from_partner(coeffs, hop)
         coeffs = times(full[level], jnp.concatenate([coeffs, partner], 0))
@@ -216,13 +216,16 @@
 def sequence(pieces, levels):
     def turn(at):
         level, piece = at
+        if piece < FULL_PIECES:
+            late = 1.5 if level == levels and piece else 0
+            return 2 * level + 0.5 * piece + late
         if level == 0:
-            return 0 if piece < 2 else 3 if piece == 2 else 2 * piece + 1
-        return 2 * (level + piece + (piece > 0))
+            return 2.2 if piece == 2 else 5.5 if piece == 3 else 7.05 + 2.1 * (piece - 4)
+        late = 2.15 if level == levels else 0
+        return 2 * level + 3 + 2.1 * (piece - 2) + late
 
     return sorted(
-        [(level, piece) for level in range(levels + 1) for piece in range(pieces)],
-        key=lambda at: (turn(at), at),
+        [(level, piece) for level in range(levels + 1) for piece in range(pieces)], key=turn
     )
 
 
@@ -236,19 +239,21 @@
     pieces = len(SHARES)
     starts = [unit * sum(SHARES[:i]) for i in range(pieces + 1)]
     full, small, extra, coeffs = first(skeleton, compress, sampling, traces, wide, room, starts[1])
-    sampling, evaluation = after(sampling, coeffs), evaluation[0]
-    coeffs = [coeffs] + list(rest(sampling, traces, starts[1:]))
+    sampling, evaluation = sampling[0], evaluation[0]
     most_here = lax.broadcasted_iota(jnp.int32, extra.shape[1:], 1) >= rank
 
     def compact(level, piece):
-        return piece > 0 and level >= wide
+        return piece >= FULL_PIECES and level >= wide
 
     inputs, partners, theirs, done = {}, {}, {}, [None] * pieces
     previous, known = None, None
     for level, piece in sequence(pieces, levels):
         count = starts[piece + 1] - starts[piece]
         if level == 0:
-            own = after(coeffs[piece], previous if piece > 1 else None)
+            own = coeffs
+            if piece > 0:
+                block = traces[starts[piece] : starts[piece + 1]]
+                own = sampled(after(sampling, coeffs if piece == 1 else previous), block)
         else:
             arrived = after(partners[piece], previous)
             if piece == 0 and level - 1 >= wide:
@@ -280,7 +285,7 @@
     quick = jnp.concatenate(done, 0)
     return lax.cond(
         most[0, 0] > room,
-        lambda: full_width(traces, sampling[0], full, evaluation),
+        lambda: full_width(traces, sampling, skeleton[0], compress[0], evaluation),
         lambda: quick,
     )
 

time: 72.3 us -> 66.5 us (0.920)
  waiting for transfers between devices: 11.7 us -> 22.4 us
  matrix products: 25 us -> 16 us
  local copies, waits for them, and re-layouts: 6.42 us -> 1.33 us
  starting transfers between devices: 23.3 us -> 22 us
  Pallas kernels: 3.59 us -> 2.64 us
    ppermute x16, waiting for transfers between devices: 11.7 us -> 22.4 us  [from_partner(): return lax.ppermute(block, hop[0], route(*hop))]
    dot_general x18 -> x16, matrix products: 13.4 us -> 5.1 us  [times(): jnp.dot(matrix, value, preferred_element_type=jnp.float32)]
    dot_general x0 -> x4, matrix products: none -> 4.76 us  [sampled(): jnp.einsum('pc,tp->ct', sampling, traces, preferred_element_type=jnp.floa...]
    dot_general x5, matrix products: 9.84 us -> 5.62 us  [evaluated(): jnp.einsum('ct,cp->tp', coeffs, evaluation, preferred_element_type=jnp.fl...]
    concatenate x4 -> x0, local copies, waits for them, and re-layouts: 3 us -> none  [local(): value = jnp.concatenate([inputs[piece], arrived[:, :count]], 0)]
    unnamed x40 -> x14, local copies, waits for them, and re-layouts: 2.24 us -> 0.04 us
    pallas_call x1 -> x0, Pallas kernels: 1.46 us -> none  [rest(): pl.pallas_call(lambda *refs: rest_kernel(starts, *refs), out_shape=[jax.S...]
    ppermute x16, starting transfers between devices: 23.3 us -> 22 us  [from_partner(): return lax.ppermute(block, hop[0], route(*hop))]
  transfers between devices with their start and end apart: 16 -> 16, of which waited for: 5 -> 8; matrix products, arithmetic and copies ran while one was open for 39% -> 26% of each run, Pallas kernels for 2% -> 0%
where the time goes in v7:
time: 66.5 us; the launch traced here: 66 us
  waiting for transfers between devices  22.4 us (34%)
  starting transfers between devices  22 us (33%)
  matrix products  16 us (24%)
  Pallas kernels  2.64 us (4%)
  local copies, waits for them, and re-layouts  1.33 us (2%)
  other arithmetic  0.88 us (1%)
  between operations  0.85 us (1%)
    ppermute x16, waiting for transfers between devices, from_partner(): return lax.ppermute(block, hop[0], route(*hop))  22.4 us
    ppermute x16, starting transfers between devices, from_partner(): return lax.ppermute(block, hop[0], route(*hop))  22 us
    dot_general x5, matrix products, evaluated(): jnp.einsum('ct,cp->tp', coeffs, evaluation, preferred_element_type=jnp.fl...  5.62 us
    dot_general x16, matrix products, times(): jnp.dot(matrix, value, preferred_element_type=jnp.float32)  5.1 us
    dot_general x4, matrix products, sampled(): jnp.einsum('pc,tp->ct', sampling, traces, preferred_element_type=jnp.floa...  4.76 us
    pallas_call x1, Pallas kernels, first(): pl.pallas_call(lambda *refs: first_kernel(wide, room, count, *refs), out_...  2.64 us
  transfers between devices with their start and end apart: 16, of which 8 were waited for; matrix products, arithmetic and copies ran while one was open for 26% of the time, Pallas kernels for 0%

profile of v7, /device:TPU:0, one launch (start us, length us, event | category | flops | bytes accessed | tf_op | source)
XLA Modules:
  0.0 66.0 jit_solution(352878920456417933)
XLA Ops:
  0.0 2.6 %first.1 = (bf16[3,128,256]{2,1,0:T(8,128)(2,1)}, bf16[3,128,256]{2,1,0:T(8,128)(2,1)}, bf16[3,128,128]{2,1,0:T(8,128)(2,1)}, bf16[128,128]{1,0:T(8,128)(2,1)}) custom-call(s32[3,1,64]{2,1,0:T(1,128)} %bitcast.98, bf16[1,3,64,128]{3,2,1,0:T(8,128)(2,1)} %refs_1_.1, bf16[1,128,128]{2,1,0:T(8,128)(2,1)} %refs_2_.1, bf16[4096,128]{1,0:T(8,128)(2,1)} %refs_3_.1), custom_call_target="tpu_custom_call" | custom-call | flops 50000000 | bytes 600000 | tf_op jit(solution)/shard_map/first/pallas_call | solution.py:110
  2.7 3.0 %collective-permute-start.3 = (bf16[128,128]{1,0:T(8,128)(2,1)}, bf16[128,128]{1,0:T(8,128)(2,1)S(1)}, u32[]{:S(2)}, u32[]{:S(2)}) collective-permute-start(bf16[128,128]{1,0:T(8,128)(2,1)} %get-tuple-element.50), channel_id=1, source_target_pairs={{0,2},{2,0},{1,3},{3,1},{4,6},{6,4},{5,7},{7,5},{8,10},{10,8},{9,1... | collective-permute-start | bytes 98312 | tf_op jit(solution)/shard_map/ppermute | solution.py:25
  5.7 1.1 %convolution_convert_fusion.30 = bf16[128,384]{1,0:T(8,128)(2,1)S(1)} fusion(bf16[128,128]{1,0:T(8,128)(2,1)S(1)} %bitcast.91, bf16[4096,128]{1,0:T(8,128)(2,1)} %refs_3_.1), kind=kOutput, calls=%fused_computation.68 | convolution fusion | flops 12632064 | bytes 229376 | tf_op jit(solution)/shard_map/pc,tp->ct/dot_general | solution.py:184
  6.9 0.8 %slice_bitcast_fusion.8 = (bf16[128,128]{1,0:T(8,128)(2,1)S(1)}, bf16[128,128]{1,0:T(8,128)(2,1)S(1)}) fusion(bf16[3,128,128]{2,1,0:T(8,128)(2,1)} %get-tuple-element.48), kind=kLoop, calls=%fused_computation.170 | loop fusion | bytes 131072 | tf_op jit(solution)/shard_map/squeeze | solution.py:282
  7.8 1.0 %convolution_convert_fusion.34 = bf16[128,128]{1,0:T(8,128)(2,1)S(1)} fusion(bf16[128,128]{1,0:T(8,128)(2,1)S(1)} %collective-permute-done.3, bf16[128,128]{1,0:T(8,128)(2,1)} %get-tuple-element.50, bf16[3,128,256]{2,1,0:T(8,128)(2,1)} %get-tuple-element.49), kind=kOutput, calls=%fused_computation.73 | convolution fusion | flops 8536064 | bytes 163840 | tf_op jit(solution)/shard_map/dot_general | solution.py:180
  8.8 2.2 %collective-permute-start.4 = (bf16[128,256]{1,0:T(8,128)(2,1)S(1)}, bf16[128,256]{1,0:T(8,128)(2,1)S(1)}, u32[]{:S(2)}, u32[]{:S(2)}) collective-permute-start(bf16[128,256]{1,0:T(8,128)(2,1)S(1)} %pad_maximum_fusion.9), channel_id=1, source_target_pairs={{0,4},{4,0},{8,12},{12,8},{1,5},{5,1},{9,13},{13,9},{2,6},{6,2},{1... | collective-permute-start | bytes 196616 | tf_op jit(solution)/shard_map/ppermute | solution.py:25
  11.0 1.2 %convolution_convert_fusion.23 = bf16[128,1024]{1,0:T(8,128)(2,1)S(1)} fusion(bf16[128,128]{1,0:T(8,128)(2,1)S(1)} %bitcast.92, bf16[4096,128]{1,0:T(8,128)(2,1)} %refs_3_.1), kind=kOutput, calls=%fused_computation.60 | convolution fusion | flops 33685504 | bytes 557056 | tf_op jit(solution)/shard_map/pc,tp->ct/dot_general | solution.py:184
  12.1 1.8 %collective-permute-start.7 = (bf16[128,1024]{1,0:T(8,128)(2,1)S(1)}, bf16[128,1024]{1,0:T(8,128)(2,1)S(1)}, u32[]{:S(2)}, u32[]{:S(2)}) collective-permute-start(bf16[128,1024]{1,0:T(8,128)(2,1)S(1)} %convolution_convert_fusion.23), channel_id=1, source_target_pairs={{0,2},{2,0},{1,3},{3,1},{4,6},{6,4},{5,7},{7,5},{8,10},{10,8},{9,1... | collective-permute-start | bytes 786440 | tf_op jit(solution)/shard_map/ppermute | solution.py:25
  14.4 1.0 %collective-permute-start.8 = (bf16[128,384]{1,0:T(8,128)(2,1)S(1)}, bf16[128,384]{1,0:T(8,128)(2,1)S(1)}, u32[]{:S(2)}, u32[]{:S(2)}) collective-permute-start(bf16[128,384]{1,0:T(8,128)(2,1)S(1)} %convolution_convert_fusion.29), channel_id=1, source_target_pairs={{0,4},{4,0},{8,12},{12,8},{1,5},{5,1},{9,13},{13,9},{2,6},{6,2},{1... | collective-permute-start | bytes 294920 | tf_op jit(solution)/shard_map/ppermute | solution.py:25
  15.5 0.8 %fusion.223 = (bf16[128,128]{1,0:T(8,128)(2,1)S(1)}, bf16[128,128]{1,0:T(8,128)(2,1)S(1)}) fusion(bf16[128,256]{1,0:T(8,128)(2,1)S(1)} %collective-permute-done.4, bf16[3,128,128]{2,1,0:T(8,128)(2,1)} %get-tuple-element.48, pred[128]{0:T(512)(128)(4,1)S(1)} %iota_compare_fusion.4), kind=kLoop, calls=%fused_computation.224 | loop fusion | flops 32768 | bytes 163968 | tf_op jit(solution)/shard_map/slice | solution.py:262
  16.4 2.7 %collective-permute-start.6 = (bf16[128,256]{1,0:T(8,128)(2,1)S(1)}, bf16[128,256]{1,0:T(8,128)(2,1)S(1)}, u32[]{:S(2)}, u32[]{:S(2)}) collective-permute-start(bf16[128,256]{1,0:T(8,128)(2,1)S(1)} %pad_maximum_fusion.10), channel_id=1, source_target_pairs={{0,8},{8,0},{4,12},{12,4},{1,9},{9,1},{5,13},{13,5},{2,10},{10,2},... | collective-permute-start | bytes 196616 | tf_op jit(solution)/shard_map/ppermute | solution.py:25
  19.6 2.4 %collective-permute-start.15 = (bf16[128,384]{1,0:T(8,128)(2,1)S(1)}, bf16[128,384]{1,0:T(8,128)(2,1)S(1)}, u32[]{:S(2)}, u32[]{:S(2)}) collective-permute-start(bf16[128,384]{1,0:T(8,128)(2,1)S(1)} %convolution_convert_fusion.28), channel_id=1, source_target_pairs={{0,8},{8,0},{4,12},{12,4},{1,9},{9,1},{5,13},{13,5},{2,10},{10,2},... | collective-permute-start | bytes 294920 | tf_op jit(solution)/shard_map/ppermute | solution.py:25
  22.5 1.7 %collective-permute-start.9 = (bf16[96,1024]{1,0:T(8,128)(2,1)S(1)}, bf16[96,1024]{1,0:T(8,128)(2,1)S(1)}, u32[]{:S(2)}, u32[]{:S(2)}) collective-permute-start(bf16[96,1024]{1,0:T(8,128)(2,1)S(1)} %convolution_convert_fusion.25), channel_id=1, source_target_pairs={{0,4},{4,0},{8,12},{12,8},{1,5},{5,1},{9,13},{13,9},{2,6},{6,2},{1... | collective-permute-start | bytes 589832 | tf_op jit(solution)/shard_map/ppermute | solution.py:25
  24.2 1.2 %convolution_convert_fusion.14 = bf16[128,1280]{1,0:T(8,128)(2,1)S(1)} fusion(bf16[128,128]{1,0:T(8,128)(2,1)S(1)} %bitcast.93, bf16[4096,128]{1,0:T(8,128)(2,1)} %refs_3_.1), kind=kOutput, calls=%fused_computation.41 | convolution fusion | flops 42106880 | bytes 688128 | tf_op jit(solution)/shard_map/pc,tp->ct/dot_general | solution.py:184
  25.7 1.2 %collective-permute-start.11 = (bf16[128,1280]{1,0:T(8,128)(2,1)S(1)}, bf16[128,1280]{1,0:T(8,128)(2,1)S(1)}, u32[]{:S(2)}, u32[]{:S(2)}) collective-permute-start(bf16[128,1280]{1,0:T(8,128)(2,1)S(1)} %convolution_convert_fusion.14), channel_id=1, source_target_pairs={{0,2},{2,0},{1,3},{3,1},{4,6},{6,4},{5,7},{7,5},{8,10},{10,8},{9,1... | collective-permute-start | bytes 983048 | tf_op jit(solution)/shard_map/ppermute | solution.py:25
  26.9 1.0 %fusion.32 = bf16[4096,128]{1,0:T(8,128)(2,1)} fusion(bf16[128,128]{1,0:T(8,128)(2,1)S(1)} %get-tuple-element.88, bf16[128,128]{1,0:T(8,128)(2,1)S(1)} %convolution_convert_fusion.33, bf16[3,128,256]{2,1,0:T(8,128)(2,1)S(1)} %copy-done.4, bf16[1,128,128]{2,1,0:T(8,128)(2,1)S(1)} %copy-done.6), kind=kOutput, calls=%fused_computation.70 | convolution fusion | flops 12746751 | bytes 196608 | tf_op jit(solution)/shard_map/ct,cp->tp/dot_general | solution.py:190
  27.9 0.5 collective-permute-done.9
  28.7 0.8 %collective-permute-start.16 = (bf16[96,1024]{1,0:T(8,128)(2,1)S(1)}, bf16[96,1024]{1,0:T(8,128)(2,1)S(1)}, u32[]{:S(2)}, u32[]{:S(2)}) collective-permute-start(bf16[96,1024]{1,0:T(8,128)(2,1)S(1)} %convolution_convert_fusion.24), channel_id=1, source_target_pairs={{0,8},{8,0},{4,12},{12,4},{1,9},{9,1},{5,13},{13,5},{2,10},{10,2},... | collective-permute-start | bytes 589832 | tf_op jit(solution)/shard_map/ppermute | solution.py:25
  29.4 1.2 %convolution_convert_fusion.13 = bf16[128,1280]{1,0:T(8,128)(2,1)S(1)} fusion(bf16[128,128]{1,0:T(8,128)(2,1)S(1)} %bitcast.94, bf16[4096,128]{1,0:T(8,128)(2,1)} %refs_3_.1), kind=kOutput, calls=%fused_computation.40 | convolution fusion | flops 42106880 | bytes 688128 | tf_op jit(solution)/shard_map/pc,tp->ct/dot_general | solution.py:184
  30.7 1.8 %collective-permute-start.10 = (bf16[128,1280]{1,0:T(8,128)(2,1)S(1)}, bf16[128,1280]{1,0:T(8,128)(2,1)S(1)}, u32[]{:S(2)}, u32[]{:S(2)}) collective-permute-start(bf16[128,1280]{1,0:T(8,128)(2,1)S(1)} %convolution_convert_fusion.13), channel_id=1, source_target_pairs={{0,2},{2,0},{1,3},{3,1},{4,6},{6,4},{5,7},{7,5},{8,10},{10,8},{9,1... | collective-permute-start | bytes 983048 | tf_op jit(solution)/shard_map/ppermute | solution.py:25
  32.7 2.5 %collective-permute-done.11 = bf16[128,1280]{1,0:T(8,128)(2,1)S(1)} collective-permute-done((bf16[128,1280]{1,0:T(8,128)(2,1)S(1)}, bf16[128,1280]{1,0:T(8,128)(2,1)S(1)}, u32[]{:S(2)}, u32[]{:S(2)}) %collective-permute-start.11) | collective-permute-done | bytes 327712 | tf_op jit(solution)/shard_map/ppermute | solution.py:25
  35.6 1.0 %fusion.31 = bf16[4096,128]{1,0:T(8,128)(2,1)} fusion(bf16[4096,128]{1,0:T(8,128)(2,1)} %fusion.32, bf16[128,384]{1,0:T(8,128)(2,1)S(1)} %collective-permute-done.15, bf16[128,384]{1,0:T(8,128)(2,1)S(1)} %convolution_convert_fusion.28, bf16[3,128,256]{2,1,0:T(8,128)(2,1)S(1)} %copy-done.4, bf16[1,128,128]{2,1,0:T(8,128)(2,1)S(1)} %copy-done.6), kind=kOutput, calls=%fused_computation.64 | convolution fusion | flops 38240256 | bytes 393216 | tf_op jit(solution)/shard_map/ct,cp->tp/dot_general | solution.py:190
  36.9 4.8 %collective-permute-done.12 = bf16[96,1280]{1,0:T(8,128)(2,1)S(1)} collective-permute-done((bf16[96,1280]{1,0:T(8,128)(2,1)S(1)}, bf16[96,1280]{1,0:T(8,128)(2,1)S(1)}, u32[]{:S(2)}, u32[]{:S(2)}) %collective-permute-start.12) | collective-permute-done | bytes 245792 | tf_op jit(solution)/shard_map/ppermute | solution.py:25
  41.9 1.0 %convolution_convert_fusion.10 = bf16[128,1280]{1,0:T(8,128)(2,1)} fusion(bf16[96,1280]{1,0:T(8,128)(2,1)S(1)} %collective-permute-done.12, bf16[128,1280]{1,0:T(8,128)(2,1)S(1)} %convolution_convert_fusion.12, bf16[3,128,256]{2,1,0:T(8,128)(2,1)S(1)} %copy-done.3), kind=kOutput, calls=%fused_computation.37 | convolution fusion | flops 86343680 | bytes 966656 | tf_op jit(solution)/shard_map/dot_general | solution.py:180
  43.6 1.3 %collective-permute-start.17 = (bf16[96,1280]{1,0:T(8,128)(2,1)S(1)}, bf16[96,1280]{1,0:T(8,128)(2,1)S(1)}, u32[]{:S(2)}, u32[]{:S(2)}) collective-permute-start(bf16[96,1280]{1,0:T(8,128)(2,1)S(1)} %convolution_convert_fusion.17), channel_id=1, source_target_pairs={{0,8},{8,0},{4,12},{12,4},{1,9},{9,1},{5,13},{13,5},{2,10},{10,2},... | collective-permute-start | bytes 737288 | tf_op jit(solution)/shard_map/ppermute | solution.py:25
  44.9 1.2 %fusion.30 = bf16[4096,128]{1,0:T(8,128)(2,1)} fusion(bf16[4096,128]{1,0:T(8,128)(2,1)} %fusion.31, bf16[96,1024]{1,0:T(8,128)(2,1)S(1)} %collective-permute-done.16, bf16[128,1024]{1,0:T(8,128)(2,1)S(1)} %convolution_convert_fusion.21, bf16[3,128,256]{2,1,0:T(8,128)(2,1)S(1)} %copy-done.3, bf16[1,128,128]{2,1,0:T(8,128)(2,1)S(1)} %copy-done.6), kind=kOutput, calls=%fused_computation.56 | convolution fusion | flops 102760448 | bytes 819200 | tf_op jit(solution)/shard_map/ct,cp->tp/dot_general | solution.py:190
  46.1 5.6 %collective-permute-done.13 = bf16[96,1280]{1,0:T(8,128)(2,1)S(1)} collective-permute-done((bf16[96,1280]{1,0:T(8,128)(2,1)S(1)}, bf16[96,1280]{1,0:T(8,128)(2,1)S(1)}, u32[]{:S(2)}, u32[]{:S(2)}) %collective-permute-start.13) | collective-permute-done | bytes 245792 | tf_op jit(solution)/shard_map/ppermute | solution.py:25
  52.0 1.7 %collective-permute-start.14 = (bf16[8,64]{1,0:T(8,128)(2,1)S(1)}, bf16[8,64]{1,0:T(8,128)(2,1)S(1)}, u32[]{:S(2)}, u32[]{:S(2)}) collective-permute-start(bf16[8,64]{1,0:T(8,128)(2,1)S(1)} %slice_maximum_fusion), channel_id=1, source_target_pairs={{0,2},{2,0},{1,3},{3,1},{4,6},{6,4},{5,7},{7,5},{8,10},{10,8},{9,1... | collective-permute-start | bytes 3080 | tf_op jit(solution)/shard_map/ppermute | solution.py:25
  53.7 7.7 %collective-permute-done.17 = bf16[96,1280]{1,0:T(8,128)(2,1)S(1)} collective-permute-done((bf16[96,1280]{1,0:T(8,128)(2,1)S(1)}, bf16[96,1280]{1,0:T(8,128)(2,1)S(1)}, u32[]{:S(2)}, u32[]{:S(2)}) %collective-permute-start.17) | collective-permute-done | bytes 245792 | tf_op jit(solution)/shard_map/ppermute | solution.py:25
  61.4 1.2 %fusion.21 = bf16[4096,128]{1,0:T(8,128)(2,1)} fusion(bf16[4096,128]{1,0:T(8,128)(2,1)} %fusion.30, bf16[96,1280]{1,0:T(8,128)(2,1)S(1)} %collective-permute-done.17, bf16[128,1280]{1,0:T(8,128)(2,1)S(1)} %copy-done.7, bf16[3,128,256]{2,1,0:T(8,128)(2,1)S(1)} %copy-done.3, bf16[1,128,128]{2,1,0:T(8,128)(2,1)S(1)} %copy-done.6), kind=kOutput, calls=%fused_computation.35 | convolution fusion | flops 128450560 | bytes 999424 | tf_op jit(solution)/shard_map/ct,cp->tp/dot_general | solution.py:190
  64.0 0.8 %collective-permute-done.18 = bf16[96,1280]{1,0:T(8,128)(2,1)S(1)} collective-permute-done((bf16[96,1280]{1,0:T(8,128)(2,1)S(1)}, bf16[96,1280]{1,0:T(8,128)(2,1)S(1)}, u32[]{:S(2)}, u32[]{:S(2)}) %collective-permute-start.18) | collective-permute-done | bytes 245792 | tf_op jit(solution)/shard_map/ppermute | solution.py:25
  64.8 1.2 %fusion.20 = bf16[4096,128]{1,0:T(8,128)(2,1)} fusion(bf16[4096,128]{1,0:T(8,128)(2,1)} %fusion.21, bf16[96,1280]{1,0:T(8,128)(2,1)S(1)} %collective-permute-done.18, bf16[128,1280]{1,0:T(8,128)(2,1)S(1)} %convolution_convert_fusion.7, bf16[3,128,256]{2,1,0:T(8,128)(2,1)S(1)} %copy-done.3, bf16[1,128,128]{2,1,0:T(8,128)(2,1)S(1)} %copy-done.6), kind=kOutput, calls=%fused_computation.31 | convolution fusion | flops 128450560 | bytes 999424 | tf_op jit(solution)/shard_map/ct,cp->tp/dot_general | solution.py:190
  (54 shorter events, 5.4 us)
Async XLA Ops:
  0.0 5.7 %copy-start = (bf16[1,128,128]{2,1,0:T(8,128)(2,1)S(1)}, bf16[1,128,128]{2,1,0:T(8,128)(2,1)}, u32[]{:S(2)}) copy-start(bf16[1,128,128]{2,1,0:T(8,128)(2,1)} %refs_2_.1) | copy-start | bytes 98308
  2.7 11.3 %copy-start.4 = (bf16[3,128,256]{2,1,0:T(8,128)(2,1)S(1)}, bf16[3,128,256]{2,1,0:T(8,128)(2,1)}, u32[]{:S(2)}) copy-start(bf16[3,128,256]{2,1,0:T(8,128)(2,1)} %get-tuple-element.49) | copy-start | bytes 589828
  2.7 5.1 %collective-permute-start.3 = (bf16[128,128]{1,0:T(8,128)(2,1)}, bf16[128,128]{1,0:T(8,128)(2,1)S(1)}, u32[]{:S(2)}, u32[]{:S(2)}) collective-permute-start(bf16[128,128]{1,0:T(8,128)(2,1)} %get-tuple-element.50), channel_id=1, source_target_pairs={{0,2},{2,0},{1,3},{3,1},{4,6},{6,4},{5,7},{7,5},{8,10},{10,8},{9,1... | collective-permute-start | bytes 98312 | tf_op jit(solution)/shard_map/ppermute | solution.py:25
  6.8 7.2 %collective-permute-start.5 = (bf16[128,384]{1,0:T(8,128)(2,1)S(1)}, bf16[128,384]{1,0:T(8,128)(2,1)S(1)}, u32[]{:S(2)}, u32[]{:S(2)}) collective-permute-start(bf16[128,384]{1,0:T(8,128)(2,1)S(1)} %convolution_convert_fusion.30), channel_id=1, source_target_pairs={{0,2},{2,0},{1,3},{3,1},{4,6},{6,4},{5,7},{7,5},{8,10},{10,8},{9,1... | collective-permute-start | bytes 294920 | tf_op jit(solution)/shard_map/ppermute | solution.py:25
  8.8 5.4 %collective-permute-start.4 = (bf16[128,256]{1,0:T(8,128)(2,1)S(1)}, bf16[128,256]{1,0:T(8,128)(2,1)S(1)}, u32[]{:S(2)}, u32[]{:S(2)}) collective-permute-start(bf16[128,256]{1,0:T(8,128)(2,1)S(1)} %pad_maximum_fusion.9), channel_id=1, source_target_pairs={{0,4},{4,0},{8,12},{12,8},{1,5},{5,1},{9,13},{13,9},{2,6},{6,2},{1... | collective-permute-start | bytes 196616 | tf_op jit(solution)/shard_map/ppermute | solution.py:25
  12.1 9.8 %collective-permute-start.7 = (bf16[128,1024]{1,0:T(8,128)(2,1)S(1)}, bf16[128,1024]{1,0:T(8,128)(2,1)S(1)}, u32[]{:S(2)}, u32[]{:S(2)}) collective-permute-start(bf16[128,1024]{1,0:T(8,128)(2,1)S(1)} %convolution_convert_fusion.23), channel_id=1, source_target_pairs={{0,2},{2,0},{1,3},{3,1},{4,6},{6,4},{5,7},{7,5},{8,10},{10,8},{9,1... | collective-permute-start | bytes 786440 | tf_op jit(solution)/shard_map/ppermute | solution.py:25
  14.4 5.0 %collective-permute-start.8 = (bf16[128,384]{1,0:T(8,128)(2,1)S(1)}, bf16[128,384]{1,0:T(8,128)(2,1)S(1)}, u32[]{:S(2)}, u32[]{:S(2)}) collective-permute-start(bf16[128,384]{1,0:T(8,128)(2,1)S(1)} %convolution_convert_fusion.29), channel_id=1, source_target_pairs={{0,4},{4,0},{8,12},{12,8},{1,5},{5,1},{9,13},{13,9},{2,6},{6,2},{1... | collective-permute-start | bytes 294920 | tf_op jit(solution)/shard_map/ppermute | solution.py:25
  16.4 9.0 %collective-permute-start.6 = (bf16[128,256]{1,0:T(8,128)(2,1)S(1)}, bf16[128,256]{1,0:T(8,128)(2,1)S(1)}, u32[]{:S(2)}, u32[]{:S(2)}) collective-permute-start(bf16[128,256]{1,0:T(8,128)(2,1)S(1)} %pad_maximum_fusion.10), channel_id=1, source_target_pairs={{0,8},{8,0},{4,12},{12,4},{1,9},{9,1},{5,13},{13,5},{2,10},{10,2},... | collective-permute-start | bytes 196616 | tf_op jit(solution)/shard_map/ppermute | solution.py:25
  19.6 16.0 %collective-permute-start.15 = (bf16[128,384]{1,0:T(8,128)(2,1)S(1)}, bf16[128,384]{1,0:T(8,128)(2,1)S(1)}, u32[]{:S(2)}, u32[]{:S(2)}) collective-permute-start(bf16[128,384]{1,0:T(8,128)(2,1)S(1)} %convolution_convert_fusion.28), channel_id=1, source_target_pairs={{0,8},{8,0},{4,12},{12,4},{1,9},{9,1},{5,13},{13,5},{2,10},{10,2},... | collective-permute-start | bytes 294920 | tf_op jit(solution)/shard_map/ppermute | solution.py:25
  22.2 3.2 %copy-start.3 = (bf16[3,128,256]{2,1,0:T(8,128)(2,1)S(1)}, bf16[3,128,256]{2,1,0:T(8,128)(2,1)}, u32[]{:S(2)}) copy-start(bf16[3,128,256]{2,1,0:T(8,128)(2,1)} %get-tuple-element.60) | copy-start | bytes 589828
  22.2 4.6 %copy-start.6 = (bf16[1,128,128]{2,1,0:T(8,128)(2,1)S(1)}, bf16[1,128,128]{2,1,0:T(8,128)(2,1)}, u32[]{:S(2)}) copy-start(bf16[1,128,128]{2,1,0:T(8,128)(2,1)} %param.11) | copy-start | bytes 98308
  22.5 5.9 %collective-permute-start.9 = (bf16[96,1024]{1,0:T(8,128)(2,1)S(1)}, bf16[96,1024]{1,0:T(8,128)(2,1)S(1)}, u32[]{:S(2)}, u32[]{:S(2)}) collective-permute-start(bf16[96,1024]{1,0:T(8,128)(2,1)S(1)} %convolution_convert_fusion.25), channel_id=1, source_target_pairs={{0,4},{4,0},{8,12},{12,8},{1,5},{5,1},{9,13},{13,9},{2,6},{6,2},{1... | collective-permute-start | bytes 589832 | tf_op jit(solution)/shard_map/ppermute | solution.py:25
  25.7 9.4 %collective-permute-start.11 = (bf16[128,1280]{1,0:T(8,128)(2,1)S(1)}, bf16[128,1280]{1,0:T(8,128)(2,1)S(1)}, u32[]{:S(2)}, u32[]{:S(2)}) collective-permute-start(bf16[128,1280]{1,0:T(8,128)(2,1)S(1)} %convolution_convert_fusion.14), channel_id=1, source_target_pairs={{0,2},{2,0},{1,3},{3,1},{4,6},{6,4},{5,7},{7,5},{8,10},{10,8},{9,1... | collective-permute-start | bytes 983048 | tf_op jit(solution)/shard_map/ppermute | solution.py:25
  28.7 16.3 %collective-permute-start.16 = (bf16[96,1024]{1,0:T(8,128)(2,1)S(1)}, bf16[96,1024]{1,0:T(8,128)(2,1)S(1)}, u32[]{:S(2)}, u32[]{:S(2)}) collective-permute-start(bf16[96,1024]{1,0:T(8,128)(2,1)S(1)} %convolution_convert_fusion.24), channel_id=1, source_target_pairs={{0,8},{8,0},{4,12},{12,4},{1,9},{9,1},{5,13},{13,5},{2,10},{10,2},... | collective-permute-start | bytes 589832 | tf_op jit(solution)/shard_map/ppermute | solution.py:25
  30.7 12.2 %collective-permute-start.10 = (bf16[128,1280]{1,0:T(8,128)(2,1)S(1)}, bf16[128,1280]{1,0:T(8,128)(2,1)S(1)}, u32[]{:S(2)}, u32[]{:S(2)}) collective-permute-start(bf16[128,1280]{1,0:T(8,128)(2,1)S(1)} %convolution_convert_fusion.13), channel_id=1, source_target_pairs={{0,2},{2,0},{1,3},{3,1},{4,6},{6,4},{5,7},{7,5},{8,10},{10,8},{9,1... | collective-permute-start | bytes 983048 | tf_op jit(solution)/shard_map/ppermute | solution.py:25
  35.4 6.3 %collective-permute-start.12 = (bf16[96,1280]{1,0:T(8,128)(2,1)S(1)}, bf16[96,1280]{1,0:T(8,128)(2,1)S(1)}, u32[]{:S(2)}, u32[]{:S(2)}) collective-permute-start(bf16[96,1280]{1,0:T(8,128)(2,1)S(1)} %convolution_convert_fusion.18), channel_id=1, source_target_pairs={{0,4},{4,0},{8,12},{12,8},{1,5},{5,1},{9,13},{13,9},{2,6},{6,2},{1... | collective-permute-start | bytes 737288 | tf_op jit(solution)/shard_map/ppermute | solution.py:25
  43.1 8.5 %collective-permute-start.13 = (bf16[96,1280]{1,0:T(8,128)(2,1)S(1)}, bf16[96,1280]{1,0:T(8,128)(2,1)S(1)}, u32[]{:S(2)}, u32[]{:S(2)}) collective-permute-start(bf16[96,1280]{1,0:T(8,128)(2,1)S(1)} %convolution_convert_fusion.16), channel_id=1, source_target_pairs={{0,4},{4,0},{8,12},{12,8},{1,5},{5,1},{9,13},{13,9},{2,6},{6,2},{1... | collective-permute-start | bytes 737288 | tf_op jit(solution)/shard_map/ppermute | solution.py:25
  43.6 17.8 %collective-permute-start.17 = (bf16[96,1280]{1,0:T(8,128)(2,1)S(1)}, bf16[96,1280]{1,0:T(8,128)(2,1)S(1)}, u32[]{:S(2)}, u32[]{:S(2)}) collective-permute-start(bf16[96,1280]{1,0:T(8,128)(2,1)S(1)} %convolution_convert_fusion.17), channel_id=1, source_target_pairs={{0,8},{8,0},{4,12},{12,4},{1,9},{9,1},{5,13},{13,5},{2,10},{10,2},... | collective-permute-start | bytes 737288 | tf_op jit(solution)/shard_map/ppermute | solution.py:25
  46.1 15.3 %copy-start.7 = (bf16[128,1280]{1,0:T(8,128)(2,1)S(1)}, bf16[128,1280]{1,0:T(8,128)(2,1)}, u32[]{:S(2)}) copy-start(bf16[128,1280]{1,0:T(8,128)(2,1)} %convolution_convert_fusion.10) | copy-start | bytes 983044
  51.9 12.9 %collective-permute-start.18 = (bf16[96,1280]{1,0:T(8,128)(2,1)S(1)}, bf16[96,1280]{1,0:T(8,128)(2,1)S(1)}, u32[]{:S(2)}, u32[]{:S(2)}) collective-permute-start(bf16[96,1280]{1,0:T(8,128)(2,1)S(1)} %convolution_convert_fusion.15), channel_id=1, source_target_pairs={{0,8},{8,0},{4,12},{12,4},{1,9},{9,1},{5,13},{13,5},{2,10},{10,2},... | collective-permute-start | bytes 737288 | tf_op jit(solution)/shard_map/ppermute | solution.py:25
  52.0 10.9 %collective-permute-start.14 = (bf16[8,64]{1,0:T(8,128)(2,1)S(1)}, bf16[8,64]{1,0:T(8,128)(2,1)S(1)}, u32[]{:S(2)}, u32[]{:S(2)}) collective-permute-start(bf16[8,64]{1,0:T(8,128)(2,1)S(1)} %slice_maximum_fusion), channel_id=1, source_target_pairs={{0,2},{2,0},{1,3},{3,1},{4,6},{6,4},{5,7},{7,5},{8,10},{10,8},{9,1... | collective-permute-start | bytes 3080 | tf_op jit(solution)/shard_map/ppermute | solution.py:25
  64.0 2.0 %copy-start.2 = (bf16[1,3,64,128]{3,2,1,0:T(8,128)(2,1)S(1)}, bf16[1,3,64,128]{3,2,1,0:T(8,128)(2,1)}, u32[]{:S(2)}) copy-start(bf16[1,3,64,128]{3,2,1,0:T(8,128)(2,1)} %refs_1_.1) | copy-start | bytes 147460
  64.0 2.0 %copy-start.5 = (s32[1,3,64]{2,0,1:T(1,128)S(1)}, s32[1,3,64]{2,0,1:T(1,128)}, u32[]{:S(2)}) copy-start(s32[1,3,64]{2,0,1:T(1,128)} %param.9) | copy-start | bytes 2308

commit v8 on v7

--- a/solution.py
+++ b/solution.py
@@ -5,9 +5,9 @@
 from jax.experimental.pallas import tpu as pltpu
 from jax.sharding import PartitionSpec as P
 
-SHARES = (1, 3, 8, 10, 10)
+SHARES = (1, 3, 8, 9, 11)
 FULL_PIECES = 2
-KERNEL_VMEM = 60 * 1024 * 1024
+KERNEL_VMEM = 16 * 1024 * 1024
 ROOM_SIXTEENTHS = 12
 
 
@@ -115,7 +115,7 @@
             jax.ShapeDtypeStruct((levels, 2 * rank, 2 * rank), jnp.bfloat16),
             jax.ShapeDtypeStruct((width, count), jnp.bfloat16),
         ],
-        in_specs=[pl.BlockSpec(memory_space=pl.ANY)] * 4,
+        in_specs=[pl.BlockSpec(memory_space=pltpu.HBM)] * 4,
         out_specs=[whole] * 4,
         scratch_shapes=[
             pltpu.VMEM((levels, 1, rank), jnp.int32),
@@ -217,12 +217,14 @@
     def turn(at):
         level, piece = at
         if piece < FULL_PIECES:
-            late = 1.5 if level == levels and piece else 0
-            return 2 * level + 0.5 * piece + late
+            if level == 0:
+                return piece
+            late = 2 if level == levels and piece else 0
+            return 3 * level + 1.5 * piece + late
         if level == 0:
-            return 2.2 if piece == 2 else 5.5 if piece == 3 else 7.05 + 2.1 * (piece - 4)
-        late = 2.15 if level == levels else 0
-        return 2 * level + 3 + 2.1 * (piece - 2) + late
+            return 3.5 if piece == 2 else 6.5 if piece == 3 else 11.02 + 3.05 * (piece - 4)
+        late = 3 if level == levels else 0
+        return 3 * level + 5 + 3.05 * (piece - 2) + late
 
     return sorted(
         [(level, piece) for level in range(levels + 1) for piece in range(pieces)], key=turn

time: 66.5 us -> 69.3 us (1.042)
  starting transfers between devices: 22 us -> 31.9 us
  waiting for transfers between devices: 22.4 us -> 18.3 us
  matrix products: 16 us -> 15.1 us
  other arithmetic: 0.88 us -> 0.12 us
  local copies, waits for them, and re-layouts: 1.33 us -> 0.63 us
    ppermute x16, starting transfers between devices: 22 us -> 31.9 us  [from_partner(): return lax.ppermute(block, hop[0], route(*hop))]
    ppermute x16, waiting for transfers between devices: 22.4 us -> 18.3 us  [from_partner(): return lax.ppermute(block, hop[0], route(*hop))]
    dot_general x16, matrix products: 5.1 us -> 4.26 us  [times(): jnp.dot(matrix, value, preferred_element_type=jnp.float32)]
    squeeze x1, local copies, waits for them, and re-layouts: 0.78 us -> 0.01 us  [local(): most = after(jnp.maximum(extra[levels - 1], known)[:8, rank:], previous)]
    slice x1, other arithmetic: 0.77 us -> 0.02 us  [local(): value = jnp.concatenate([inputs[piece], arrived[:, :count]], 0)]
  transfers between devices with their start and end apart: 16 -> 16, of which waited for: 8 -> 7; matrix products, arithmetic and copies ran while one was open for 26% -> 21% of each run, Pallas kernels for 0% -> 0%
where the time goes in v8:
time: 69.3 us; the launch traced here: 69 us
  starting transfers between devices  31.9 us (46%)
  waiting for transfers between devices  18.3 us (26%)
  matrix products  15.1 us (22%)
  Pallas kernels  1.98 us (3%)
  between operations  0.9 us (1%)
    ppermute x16, starting transfers between devices, from_partner(): return lax.ppermute(block, hop[0], route(*hop))  31.9 us
    ppermute x16, waiting for transfers between devices, from_partner(): return lax.ppermute(block, hop[0], route(*hop))  18.3 us
    dot_general x5, matrix products, evaluated(): jnp.einsum('ct,cp->tp', coeffs, evaluation, preferred_element_type=jnp.fl...  5.59 us
    dot_general x4, matrix products, sampled(): jnp.einsum('pc,tp->ct', sampling, traces, preferred_element_type=jnp.floa...  4.77 us
    dot_general x16, matrix products, times(): jnp.dot(matrix, value, preferred_element_type=jnp.float32)  4.26 us
    pallas_call x1, Pallas kernels, first(): pl.pallas_call(lambda *refs: first_kernel(wide, room, count, *refs), out_...  1.98 us
  transfers between devices with their start and end apart: 16, of which 7 were waited for; matrix products, arithmetic and copies ran while one was open for 21% of the time, Pallas kernels for 0%

profile of v8, /device:TPU:0, one launch (start us, length us, event | category | flops | bytes accessed | tf_op | source)
XLA Modules:
  0.0 69.0 jit_solution(304924401754716578)
XLA Ops:
  0.0 2.0 %first.1 = (bf16[3,128,256]{2,1,0:T(8,128)(2,1)S(1)}, bf16[3,128,256]{2,1,0:T(8,128)(2,1)S(1)}, bf16[3,128,128]{2,1,0:T(8,128)(2,1)S(1)}, bf16[128,128]{1,0:T(8,128)(2,1)S(1)}) custom-call(s32[3,1,64]{2,1,0:T(1,128)} %bitcast.98, bf16[1,3,64,128]{3,2,1,0:T(8,128)(2,1)} %refs_1_.1, bf16[1,128,128]{2,1,0:T(8,128)(2,1)} %refs_2_.1, bf16[4096,128]{1,0:T(8,128)(2,1)} %refs_3_.1), custom_call_target="tpu_custom_call" | custom-call | flops 50000000 | bytes 600000 | tf_op jit(solution)/shard_map/first/pallas_call | solution.py:110
  2.0 3.0 %collective-permute-start.3 = (bf16[128,128]{1,0:T(8,128)(2,1)S(1)}, bf16[128,128]{1,0:T(8,128)(2,1)S(1)}, u32[]{:S(2)}, u32[]{:S(2)}) collective-permute-start(bf16[128,128]{1,0:T(8,128)(2,1)S(1)} %get-tuple-element.50), channel_id=1, source_target_pairs={{0,2},{2,0},{1,3},{3,1},{4,6},{6,4},{5,7},{7,5},{8,10},{10,8},{9,1... | collective-permute-start | bytes 98312 | tf_op jit(solution)/shard_map/ppermute | solution.py:25
  5.0 1.1 %convolution_convert_fusion.30 = bf16[128,384]{1,0:T(8,128)(2,1)S(1)} fusion(bf16[128,128]{1,0:T(8,128)(2,1)S(1)} %bitcast.91, bf16[4096,128]{1,0:T(8,128)(2,1)} %refs_3_.1), kind=kOutput, calls=%fused_computation.69 | convolution fusion | flops 12632064 | bytes 229376 | tf_op jit(solution)/shard_map/pc,tp->ct/dot_general | solution.py:184
  6.2 0.7 collective-permute-done.3
  7.1 2.2 %collective-permute-start.4 = (bf16[128,256]{1,0:T(8,128)(2,1)S(1)}, bf16[128,256]{1,0:T(8,128)(2,1)S(1)}, u32[]{:S(2)}, u32[]{:S(2)}) collective-permute-start(bf16[128,256]{1,0:T(8,128)(2,1)S(1)} %pad_maximum_fusion.9), channel_id=1, source_target_pairs={{0,4},{4,0},{8,12},{12,8},{1,5},{5,1},{9,13},{13,9},{2,6},{6,2},{1... | collective-permute-start | bytes 196616 | tf_op jit(solution)/shard_map/ppermute | solution.py:25
  9.2 1.2 %convolution_convert_fusion.23 = bf16[128,1024]{1,0:T(8,128)(2,1)S(1)} fusion(bf16[128,128]{1,0:T(8,128)(2,1)S(1)} %bitcast.92, bf16[4096,128]{1,0:T(8,128)(2,1)} %refs_3_.1), kind=kOutput, calls=%fused_computation.56 | convolution fusion | flops 33685504 | bytes 557056 | tf_op jit(solution)/shard_map/pc,tp->ct/dot_general | solution.py:184
  10.4 1.6 %collective-permute-start.7 = (bf16[128,1024]{1,0:T(8,128)(2,1)S(1)}, bf16[128,1024]{1,0:T(8,128)(2,1)S(1)}, u32[]{:S(2)}, u32[]{:S(2)}) collective-permute-start(bf16[128,1024]{1,0:T(8,128)(2,1)S(1)} %convolution_convert_fusion.23), channel_id=1, source_target_pairs={{0,2},{2,0},{1,3},{3,1},{4,6},{6,4},{5,7},{7,5},{8,10},{10,8},{9,1... | collective-permute-start | bytes 786440 | tf_op jit(solution)/shard_map/ppermute | solution.py:25
  12.7 2.6 %collective-permute-start.6 = (bf16[128,256]{1,0:T(8,128)(2,1)S(1)}, bf16[128,256]{1,0:T(8,128)(2,1)S(1)}, u32[]{:S(2)}, u32[]{:S(2)}) collective-permute-start(bf16[128,256]{1,0:T(8,128)(2,1)S(1)} %pad_maximum_fusion.10), channel_id=1, source_target_pairs={{0,8},{8,0},{4,12},{12,4},{1,9},{9,1},{5,13},{13,5},{2,10},{10,2},... | collective-permute-start | bytes 196616 | tf_op jit(solution)/shard_map/ppermute | solution.py:25
  15.3 1.2 %collective-permute-start.8 = (bf16[128,384]{1,0:T(8,128)(2,1)S(1)}, bf16[128,384]{1,0:T(8,128)(2,1)S(1)}, u32[]{:S(2)}, u32[]{:S(2)}) collective-permute-start(bf16[128,384]{1,0:T(8,128)(2,1)S(1)} %convolution_convert_fusion.29), channel_id=1, source_target_pairs={{0,4},{4,0},{8,12},{12,8},{1,5},{5,1},{9,13},{13,9},{2,6},{6,2},{1... | collective-permute-start | bytes 294920 | tf_op jit(solution)/shard_map/ppermute | solution.py:25
  16.6 1.2 %convolution_convert_fusion.14 = bf16[128,1152]{1,0:T(8,128)(2,1)S(1)} fusion(bf16[128,128]{1,0:T(8,128)(2,1)S(1)} %bitcast.93, bf16[4096,128]{1,0:T(8,128)(2,1)} %refs_3_.1), kind=kOutput, calls=%fused_computation.41 | convolution fusion | flops 37896192 | bytes 622592 | tf_op jit(solution)/shard_map/pc,tp->ct/dot_general | solution.py:184
  17.8 1.6 %collective-permute-start.11 = (bf16[128,1152]{1,0:T(8,128)(2,1)S(1)}, bf16[128,1152]{1,0:T(8,128)(2,1)S(1)}, u32[]{:S(2)}, u32[]{:S(2)}) collective-permute-start(bf16[128,1152]{1,0:T(8,128)(2,1)S(1)} %convolution_convert_fusion.14), channel_id=1, source_target_pairs={{0,2},{2,0},{1,3},{3,1},{4,6},{6,4},{5,7},{7,5},{8,10},{10,8},{9,1... | collective-permute-start | bytes 884744 | tf_op jit(solution)/shard_map/ppermute | solution.py:25
  21.3 2.0 %collective-permute-start.9 = (bf16[96,1024]{1,0:T(8,128)(2,1)S(1)}, bf16[96,1024]{1,0:T(8,128)(2,1)S(1)}, u32[]{:S(2)}, u32[]{:S(2)}) collective-permute-start(bf16[96,1024]{1,0:T(8,128)(2,1)S(1)} %convolution_convert_fusion.25), channel_id=1, source_target_pairs={{0,4},{4,0},{8,12},{12,8},{1,5},{5,1},{9,13},{13,9},{2,6},{6,2},{1... | collective-permute-start | bytes 589832 | tf_op jit(solution)/shard_map/ppermute | solution.py:25
  23.4 1.0 %fusion.32 = bf16[4096,128]{1,0:T(8,128)(2,1)} fusion(bf16[128,128]{1,0:T(8,128)(2,1)S(1)} %get-tuple-element.88, bf16[128,128]{1,0:T(8,128)(2,1)S(1)} %convolution_convert_fusion.33, bf16[3,128,256]{2,1,0:T(8,128)(2,1)S(1)} %get-tuple-element.49, bf16[1,128,128]{2,1,0:T(8,128)(2,1)S(1)} %copy-done.4), kind=kOutput, calls=%fused_computation.71 | convolution fusion | flops 12746751 | bytes 196608 | tf_op jit(solution)/shard_map/ct,cp->tp/dot_general | solution.py:190
  24.4 3.7 %collective-permute-done.9 = bf16[96,1024]{1,0:T(8,128)(2,1)S(1)} collective-permute-done((bf16[96,1024]{1,0:T(8,128)(2,1)S(1)}, bf16[96,1024]{1,0:T(8,128)(2,1)S(1)}, u32[]{:S(2)}, u32[]{:S(2)}) %collective-permute-start.9) | collective-permute-done | bytes 196640 | tf_op jit(solution)/shard_map/ppermute | solution.py:25
  28.3 3.9 %collective-permute-start.16 = (bf16[96,1024]{1,0:T(8,128)(2,1)S(1)}, bf16[96,1024]{1,0:T(8,128)(2,1)S(1)}, u32[]{:S(2)}, u32[]{:S(2)}) collective-permute-start(bf16[96,1024]{1,0:T(8,128)(2,1)S(1)} %convolution_convert_fusion.24), channel_id=1, source_target_pairs={{0,8},{8,0},{4,12},{12,4},{1,9},{9,1},{5,13},{13,5},{2,10},{10,2},... | collective-permute-start | bytes 589832 | tf_op jit(solution)/shard_map/ppermute | solution.py:25
  32.2 1.3 %convolution_convert_fusion.13 = bf16[128,1408]{1,0:T(8,128)(2,1)S(1)} fusion(bf16[128,128]{1,0:T(8,128)(2,1)S(1)} %bitcast.94, bf16[4096,128]{1,0:T(8,128)(2,1)} %refs_3_.1), kind=kOutput, calls=%fused_computation.40 | convolution fusion | flops 46317568 | bytes 753664 | tf_op jit(solution)/shard_map/pc,tp->ct/dot_general | solution.py:184
  33.5 1.8 %collective-permute-start.10 = (bf16[128,1408]{1,0:T(8,128)(2,1)S(1)}, bf16[128,1408]{1,0:T(8,128)(2,1)S(1)}, u32[]{:S(2)}, u32[]{:S(2)}) collective-permute-start(bf16[128,1408]{1,0:T(8,128)(2,1)S(1)} %convolution_convert_fusion.13), channel_id=1, source_target_pairs={{0,2},{2,0},{1,3},{3,1},{4,6},{6,4},{5,7},{7,5},{8,10},{10,8},{9,1... | collective-permute-start | bytes 1081352 | tf_op jit(solution)/shard_map/ppermute | solution.py:25
  36.0 2.6 %collective-permute-start.12 = (bf16[96,1152]{1,0:T(8,128)(2,1)S(1)}, bf16[96,1152]{1,0:T(8,128)(2,1)S(1)}, u32[]{:S(2)}, u32[]{:S(2)}) collective-permute-start(bf16[96,1152]{1,0:T(8,128)(2,1)S(1)} %convolution_convert_fusion.18), channel_id=1, source_target_pairs={{0,4},{4,0},{8,12},{12,8},{1,5},{5,1},{9,13},{13,9},{2,6},{6,2},{1... | collective-permute-start | bytes 663560 | tf_op jit(solution)/shard_map/ppermute | solution.py:25
  38.5 1.0 %fusion.31 = bf16[4096,128]{1,0:T(8,128)(2,1)} fusion(bf16[4096,128]{1,0:T(8,128)(2,1)} %fusion.32, bf16[128,384]{1,0:T(8,128)(2,1)S(1)} %collective-permute-done.15, bf16[128,384]{1,0:T(8,128)(2,1)S(1)} %convolution_convert_fusion.28, bf16[3,128,256]{2,1,0:T(8,128)(2,1)S(1)} %get-tuple-element.49, bf16[1,128,128]{2,1,0:T(8,128)(2,1)S(1)} %copy-done.4), kind=kOutput, calls=%fused_computation.65 | convolution fusion | flops 38240256 | bytes 393216 | tf_op jit(solution)/shard_map/ct,cp->tp/dot_general | solution.py:190
  39.6 6.3 %collective-permute-done.12 = bf16[96,1152]{1,0:T(8,128)(2,1)S(1)} collective-permute-done((bf16[96,1152]{1,0:T(8,128)(2,1)S(1)}, bf16[96,1152]{1,0:T(8,128)(2,1)S(1)}, u32[]{:S(2)}, u32[]{:S(2)}) %collective-permute-start.12) | collective-permute-done | bytes 221216 | tf_op jit(solution)/shard_map/ppermute | solution.py:25
  45.9 1.0 %convolution_convert_fusion.10 = bf16[128,1152]{1,0:T(8,128)(2,1)} fusion(bf16[96,1152]{1,0:T(8,128)(2,1)S(1)} %collective-permute-done.12, bf16[128,1152]{1,0:T(8,128)(2,1)S(1)} %convolution_convert_fusion.12, bf16[3,128,256]{2,1,0:T(8,128)(2,1)S(1)} %get-tuple-element.60), kind=kOutput, calls=%fused_computation.37 | convolution fusion | flops 77709312 | bytes 876544 | tf_op jit(solution)/shard_map/dot_general | solution.py:180
  47.1 2.3 %collective-permute-start.17 = (bf16[96,1152]{1,0:T(8,128)(2,1)S(1)}, bf16[96,1152]{1,0:T(8,128)(2,1)S(1)}, u32[]{:S(2)}, u32[]{:S(2)}) collective-permute-start(bf16[96,1152]{1,0:T(8,128)(2,1)S(1)} %convolution_convert_fusion.17), channel_id=1, source_target_pairs={{0,8},{8,0},{4,12},{12,4},{1,9},{9,1},{5,13},{13,5},{2,10},{10,2},... | collective-permute-start | bytes 663560 | tf_op jit(solution)/shard_map/ppermute | solution.py:25
  49.6 2.6 %collective-permute-start.13 = (bf16[96,1408]{1,0:T(8,128)(2,1)S(1)}, bf16[96,1408]{1,0:T(8,128)(2,1)S(1)}, u32[]{:S(2)}, u32[]{:S(2)}) collective-permute-start(bf16[96,1408]{1,0:T(8,128)(2,1)S(1)} %convolution_convert_fusion.16), channel_id=1, source_target_pairs={{0,4},{4,0},{8,12},{12,8},{1,5},{5,1},{9,13},{13,9},{2,6},{6,2},{1... | collective-permute-start | bytes 811016 | tf_op jit(solution)/shard_map/ppermute | solution.py:25
  52.2 1.2 %fusion.26 = bf16[4096,128]{1,0:T(8,128)(2,1)} fusion(bf16[4096,128]{1,0:T(8,128)(2,1)} %fusion.31, bf16[96,1024]{1,0:T(8,128)(2,1)S(1)} %collective-permute-done.16, bf16[128,1024]{1,0:T(8,128)(2,1)S(1)} %convolution_convert_fusion.21, bf16[3,128,256]{2,1,0:T(8,128)(2,1)S(1)} %get-tuple-element.60, bf16[1,128,128]{2,1,0:T(8,128)(2,1)S(1)} %copy-done.4), kind=kOutput, calls=%fused_computation.52 | convolution fusion | flops 102760448 | bytes 819200 | tf_op jit(solution)/shard_map/ct,cp->tp/dot_general | solution.py:190
  53.6 3.5 %collective-permute-done.13 = bf16[96,1408]{1,0:T(8,128)(2,1)S(1)} collective-permute-done((bf16[96,1408]{1,0:T(8,128)(2,1)S(1)}, bf16[96,1408]{1,0:T(8,128)(2,1)S(1)}, u32[]{:S(2)}, u32[]{:S(2)}) %collective-permute-start.13) | collective-permute-done | bytes 270368 | tf_op jit(solution)/shard_map/ppermute | solution.py:25
  57.4 3.0 %collective-permute-start.18 = (bf16[96,1408]{1,0:T(8,128)(2,1)S(1)}, bf16[96,1408]{1,0:T(8,128)(2,1)S(1)}, u32[]{:S(2)}, u32[]{:S(2)}) collective-permute-start(bf16[96,1408]{1,0:T(8,128)(2,1)S(1)} %convolution_convert_fusion.15), channel_id=1, source_target_pairs={{0,8},{8,0},{4,12},{12,4},{1,9},{9,1},{5,13},{13,5},{2,10},{10,2},... | collective-permute-start | bytes 811016 | tf_op jit(solution)/shard_map/ppermute | solution.py:25
  60.7 1.0 %collective-permute-start.14 = (bf16[8,64]{1,0:T(8,128)(2,1)S(1)}, bf16[8,64]{1,0:T(8,128)(2,1)S(1)}, u32[]{:S(2)}, u32[]{:S(2)}) collective-permute-start(bf16[8,64]{1,0:T(8,128)(2,1)S(1)} %slice_maximum_fusion), channel_id=1, source_target_pairs={{0,2},{2,0},{1,3},{3,1},{4,6},{6,4},{5,7},{7,5},{8,10},{10,8},{9,1... | collective-permute-start | bytes 3080 | tf_op jit(solution)/shard_map/ppermute | solution.py:25
  61.7 1.2 %fusion.21 = bf16[4096,128]{1,0:T(8,128)(2,1)} fusion(bf16[4096,128]{1,0:T(8,128)(2,1)} %fusion.26, bf16[96,1152]{1,0:T(8,128)(2,1)S(1)} %collective-permute-done.17, bf16[128,1152]{1,0:T(8,128)(2,1)S(1)} %copy-done.5, bf16[3,128,256]{2,1,0:T(8,128)(2,1)S(1)} %get-tuple-element.60, bf16[1,128,128]{2,1,0:T(8,128)(2,1)S(1)} %copy-done.4), kind=kOutput, calls=%fused_computation.35 | convolution fusion | flops 115605504 | bytes 909312 | tf_op jit(solution)/shard_map/ct,cp->tp/dot_general | solution.py:190
  62.9 1.5 %collective-permute-done.14 = bf16[8,64]{1,0:T(8,128)(2,1)S(1)} collective-permute-done((bf16[8,64]{1,0:T(8,128)(2,1)S(1)}, bf16[8,64]{1,0:T(8,128)(2,1)S(1)}, u32[]{:S(2)}, u32[]{:S(2)}) %collective-permute-start.14) | collective-permute-done | bytes 1056 | tf_op jit(solution)/shard_map/ppermute | solution.py:25
  64.4 0.6 slice.165
  65.6 2.1 %collective-permute-done.18 = bf16[96,1408]{1,0:T(8,128)(2,1)S(1)} collective-permute-done((bf16[96,1408]{1,0:T(8,128)(2,1)S(1)}, bf16[96,1408]{1,0:T(8,128)(2,1)S(1)}, u32[]{:S(2)}, u32[]{:S(2)}) %collective-permute-start.18) | collective-permute-done | bytes 270368 | tf_op jit(solution)/shard_map/ppermute | solution.py:25
  67.7 1.2 %fusion.20 = bf16[4096,128]{1,0:T(8,128)(2,1)} fusion(bf16[4096,128]{1,0:T(8,128)(2,1)} %fusion.21, bf16[96,1408]{1,0:T(8,128)(2,1)S(1)} %collective-permute-done.18, bf16[128,1408]{1,0:T(8,128)(2,1)S(1)} %convolution_convert_fusion.7, bf16[3,128,256]{2,1,0:T(8,128)(2,1)S(1)} %get-tuple-element.60, bf16[1,128,128]{2,1,0:T(8,128)(2,1)S(1)} %copy-done.4), kind=kOutput, calls=%fused_computation.31 | convolution fusion | flops 141295616 | bytes 1089536 | tf_op jit(solution)/shard_map/ct,cp->tp/dot_general | solution.py:190
  (50 shorter events, 5.0 us)
Async XLA Ops:
  0.0 5.0 %copy-start = (bf16[1,128,128]{2,1,0:T(8,128)(2,1)S(1)}, bf16[1,128,128]{2,1,0:T(8,128)(2,1)}, u32[]{:S(2)}) copy-start(bf16[1,128,128]{2,1,0:T(8,128)(2,1)} %refs_2_.1) | copy-start | bytes 98308
  2.0 4.9 %collective-permute-start.3 = (bf16[128,128]{1,0:T(8,128)(2,1)S(1)}, bf16[128,128]{1,0:T(8,128)(2,1)S(1)}, u32[]{:S(2)}, u32[]{:S(2)}) collective-permute-start(bf16[128,128]{1,0:T(8,128)(2,1)S(1)} %get-tuple-element.50), channel_id=1, source_target_pairs={{0,2},{2,0},{1,3},{3,1},{4,6},{6,4},{5,7},{7,5},{8,10},{10,8},{9,1... | collective-permute-start | bytes 98312 | tf_op jit(solution)/shard_map/ppermute | solution.py:25
  6.1 5.9 %collective-permute-start.5 = (bf16[128,384]{1,0:T(8,128)(2,1)S(1)}, bf16[128,384]{1,0:T(8,128)(2,1)S(1)}, u32[]{:S(2)}, u32[]{:S(2)}) collective-permute-start(bf16[128,384]{1,0:T(8,128)(2,1)S(1)} %convolution_convert_fusion.30), channel_id=1, source_target_pairs={{0,2},{2,0},{1,3},{3,1},{4,6},{6,4},{5,7},{7,5},{8,10},{10,8},{9,1... | collective-permute-start | bytes 294920 | tf_op jit(solution)/shard_map/ppermute | solution.py:25
  7.1 5.2 %collective-permute-start.4 = (bf16[128,256]{1,0:T(8,128)(2,1)S(1)}, bf16[128,256]{1,0:T(8,128)(2,1)S(1)}, u32[]{:S(2)}, u32[]{:S(2)}) collective-permute-start(bf16[128,256]{1,0:T(8,128)(2,1)S(1)} %pad_maximum_fusion.9), channel_id=1, source_target_pairs={{0,4},{4,0},{8,12},{12,8},{1,5},{5,1},{9,13},{13,9},{2,6},{6,2},{1... | collective-permute-start | bytes 196616 | tf_op jit(solution)/shard_map/ppermute | solution.py:25
  10.4 10.1 %collective-permute-start.7 = (bf16[128,1024]{1,0:T(8,128)(2,1)S(1)}, bf16[128,1024]{1,0:T(8,128)(2,1)S(1)}, u32[]{:S(2)}, u32[]{:S(2)}) collective-permute-start(bf16[128,1024]{1,0:T(8,128)(2,1)S(1)} %convolution_convert_fusion.23), channel_id=1, source_target_pairs={{0,2},{2,0},{1,3},{3,1},{4,6},{6,4},{5,7},{7,5},{8,10},{10,8},{9,1... | collective-permute-start | bytes 786440 | tf_op jit(solution)/shard_map/ppermute | solution.py:25
  12.7 8.4 %collective-permute-start.6 = (bf16[128,256]{1,0:T(8,128)(2,1)S(1)}, bf16[128,256]{1,0:T(8,128)(2,1)S(1)}, u32[]{:S(2)}, u32[]{:S(2)}) collective-permute-start(bf16[128,256]{1,0:T(8,128)(2,1)S(1)} %pad_maximum_fusion.10), channel_id=1, source_target_pairs={{0,8},{8,0},{4,12},{12,4},{1,9},{9,1},{5,13},{13,5},{2,10},{10,2},... | collective-permute-start | bytes 196616 | tf_op jit(solution)/shard_map/ppermute | solution.py:25
  15.3 4.6 %collective-permute-start.8 = (bf16[128,384]{1,0:T(8,128)(2,1)S(1)}, bf16[128,384]{1,0:T(8,128)(2,1)S(1)}, u32[]{:S(2)}, u32[]{:S(2)}) collective-permute-start(bf16[128,384]{1,0:T(8,128)(2,1)S(1)} %convolution_convert_fusion.29), channel_id=1, source_target_pairs={{0,4},{4,0},{8,12},{12,8},{1,5},{5,1},{9,13},{13,9},{2,6},{6,2},{1... | collective-permute-start | bytes 294920 | tf_op jit(solution)/shard_map/ppermute | solution.py:25
  17.8 17.7 %collective-permute-start.11 = (bf16[128,1152]{1,0:T(8,128)(2,1)S(1)}, bf16[128,1152]{1,0:T(8,128)(2,1)S(1)}, u32[]{:S(2)}, u32[]{:S(2)}) collective-permute-start(bf16[128,1152]{1,0:T(8,128)(2,1)S(1)} %convolution_convert_fusion.14), channel_id=1, source_target_pairs={{0,2},{2,0},{1,3},{3,1},{4,6},{6,4},{5,7},{7,5},{8,10},{10,8},{9,1... | collective-permute-start | bytes 884744 | tf_op jit(solution)/shard_map/ppermute | solution.py:25
  20.1 3.2 %copy-start.4 = (bf16[1,128,128]{2,1,0:T(8,128)(2,1)S(1)}, bf16[1,128,128]{2,1,0:T(8,128)(2,1)}, u32[]{:S(2)}) copy-start(bf16[1,128,128]{2,1,0:T(8,128)(2,1)} %param.11) | copy-start | bytes 98308
  20.2 18.4 %collective-permute-start.15 = (bf16[128,384]{1,0:T(8,128)(2,1)S(1)}, bf16[128,384]{1,0:T(8,128)(2,1)S(1)}, u32[]{:S(2)}, u32[]{:S(2)}) collective-permute-start(bf16[128,384]{1,0:T(8,128)(2,1)S(1)} %convolution_convert_fusion.28), channel_id=1, source_target_pairs={{0,8},{8,0},{4,12},{12,4},{1,9},{9,1},{5,13},{13,5},{2,10},{10,2},... | collective-permute-start | bytes 294920 | tf_op jit(solution)/shard_map/ppermute | solution.py:25
  21.3 6.8 %collective-permute-start.9 = (bf16[96,1024]{1,0:T(8,128)(2,1)S(1)}, bf16[96,1024]{1,0:T(8,128)(2,1)S(1)}, u32[]{:S(2)}, u32[]{:S(2)}) collective-permute-start(bf16[96,1024]{1,0:T(8,128)(2,1)S(1)} %convolution_convert_fusion.25), channel_id=1, source_target_pairs={{0,4},{4,0},{8,12},{12,8},{1,5},{5,1},{9,13},{13,9},{2,6},{6,2},{1... | collective-permute-start | bytes 589832 | tf_op jit(solution)/shard_map/ppermute | solution.py:25
  28.3 23.8 %collective-permute-start.16 = (bf16[96,1024]{1,0:T(8,128)(2,1)S(1)}, bf16[96,1024]{1,0:T(8,128)(2,1)S(1)}, u32[]{:S(2)}, u32[]{:S(2)}) collective-permute-start(bf16[96,1024]{1,0:T(8,128)(2,1)S(1)} %convolution_convert_fusion.24), channel_id=1, source_target_pairs={{0,8},{8,0},{4,12},{12,4},{1,9},{9,1},{5,13},{13,5},{2,10},{10,2},... | collective-permute-start | bytes 589832 | tf_op jit(solution)/shard_map/ppermute | solution.py:25
  33.5 15.9 %collective-permute-start.10 = (bf16[128,1408]{1,0:T(8,128)(2,1)S(1)}, bf16[128,1408]{1,0:T(8,128)(2,1)S(1)}, u32[]{:S(2)}, u32[]{:S(2)}) collective-permute-start(bf16[128,1408]{1,0:T(8,128)(2,1)S(1)} %convolution_convert_fusion.13), channel_id=1, source_target_pairs={{0,2},{2,0},{1,3},{3,1},{4,6},{6,4},{5,7},{7,5},{8,10},{10,8},{9,1... | collective-permute-start | bytes 1081352 | tf_op jit(solution)/shard_map/ppermute | solution.py:25
  36.0 9.9 %collective-permute-start.12 = (bf16[96,1152]{1,0:T(8,128)(2,1)S(1)}, bf16[96,1152]{1,0:T(8,128)(2,1)S(1)}, u32[]{:S(2)}, u32[]{:S(2)}) collective-permute-start(bf16[96,1152]{1,0:T(8,128)(2,1)S(1)} %convolution_convert_fusion.18), channel_id=1, source_target_pairs={{0,4},{4,0},{8,12},{12,8},{1,5},{5,1},{9,13},{13,9},{2,6},{6,2},{1... | collective-permute-start | bytes 663560 | tf_op jit(solution)/shard_map/ppermute | solution.py:25
  47.1 13.6 %collective-permute-start.17 = (bf16[96,1152]{1,0:T(8,128)(2,1)S(1)}, bf16[96,1152]{1,0:T(8,128)(2,1)S(1)}, u32[]{:S(2)}, u32[]{:S(2)}) collective-permute-start(bf16[96,1152]{1,0:T(8,128)(2,1)S(1)} %convolution_convert_fusion.17), channel_id=1, source_target_pairs={{0,8},{8,0},{4,12},{12,4},{1,9},{9,1},{5,13},{13,5},{2,10},{10,2},... | collective-permute-start | bytes 663560 | tf_op jit(solution)/shard_map/ppermute | solution.py:25
  49.6 7.5 %collective-permute-start.13 = (bf16[96,1408]{1,0:T(8,128)(2,1)S(1)}, bf16[96,1408]{1,0:T(8,128)(2,1)S(1)}, u32[]{:S(2)}, u32[]{:S(2)}) collective-permute-start(bf16[96,1408]{1,0:T(8,128)(2,1)S(1)} %convolution_convert_fusion.16), channel_id=1, source_target_pairs={{0,4},{4,0},{8,12},{12,8},{1,5},{5,1},{9,13},{13,9},{2,6},{6,2},{1... | collective-permute-start | bytes 811016 | tf_op jit(solution)/shard_map/ppermute | solution.py:25
  57.4 4.3 %copy-start.5 = (bf16[128,1152]{1,0:T(8,128)(2,1)S(1)}, bf16[128,1152]{1,0:T(8,128)(2,1)}, u32[]{:S(2)}) copy-start(bf16[128,1152]{1,0:T(8,128)(2,1)} %convolution_convert_fusion.10) | copy-start | bytes 884740
  57.4 10.4 %collective-permute-start.18 = (bf16[96,1408]{1,0:T(8,128)(2,1)S(1)}, bf16[96,1408]{1,0:T(8,128)(2,1)S(1)}, u32[]{:S(2)}, u32[]{:S(2)}) collective-permute-start(bf16[96,1408]{1,0:T(8,128)(2,1)S(1)} %convolution_convert_fusion.15), channel_id=1, source_target_pairs={{0,8},{8,0},{4,12},{12,4},{1,9},{9,1},{5,13},{13,5},{2,10},{10,2},... | collective-permute-start | bytes 811016 | tf_op jit(solution)/shard_map/ppermute | solution.py:25
  60.7 3.7 %collective-permute-start.14 = (bf16[8,64]{1,0:T(8,128)(2,1)S(1)}, bf16[8,64]{1,0:T(8,128)(2,1)S(1)}, u32[]{:S(2)}, u32[]{:S(2)}) collective-permute-start(bf16[8,64]{1,0:T(8,128)(2,1)S(1)} %slice_maximum_fusion), channel_id=1, source_target_pairs={{0,2},{2,0},{1,3},{3,1},{4,6},{6,4},{5,7},{7,5},{8,10},{10,8},{9,1... | collective-permute-start | bytes 3080 | tf_op jit(solution)/shard_map/ppermute | solution.py:25
  65.6 3.4 %copy-start.2 = (bf16[1,3,64,128]{3,2,1,0:T(8,128)(2,1)S(1)}, bf16[1,3,64,128]{3,2,1,0:T(8,128)(2,1)}, u32[]{:S(2)}) copy-start(bf16[1,3,64,128]{3,2,1,0:T(8,128)(2,1)} %refs_1_.1) | copy-start | bytes 147460
  65.6 3.4 %copy-start.3 = (s32[1,3,64]{2,0,1:T(1,128)S(1)}, s32[1,3,64]{2,0,1:T(1,128)}, u32[]{:S(2)}) copy-start(s32[1,3,64]{2,0,1:T(1,128)} %param.9) | copy-start | bytes 2308

commit v9 on v8

v9 whole, which is shorter than its diff:
```python
import jax
import jax.numpy as jnp
from jax import lax
from jax.experimental import pallas as pl
from jax.experimental.pallas import tpu as pltpu
from jax.sharding import PartitionSpec as P

SHARES = (2, 6, 8, 9, 7)
POOL_EIGHTHS = 5

UP = [(0, 1), (3, 2)]
MIDDLE = [(1, 2), (2, 1)]
DOWN = [(1, 0), (2, 3)]


def route(axis, apart):
    count = lax.axis_size(axis)
    pairs = []
    for low in range(count):
        high = low | 1 << apart
        if high != low and high < count:
            pairs += [(low, high), (high, low)]
    return pairs


def from_partner(block, hop):
    return lax.ppermute(block, hop[0], route(*hop))


def across(left, right):
    return lax.dot_general(left, right, (((1,), (1,)), ((), ())), preferred_element_type=jnp.float32)


def one_hot(condition):
    return jnp.where(condition, 1.0, 0.0).astype(jnp.bfloat16)


def sampled_block(sampling, rows):
    turned = sampling.astype(jnp.float32).T.astype(jnp.bfloat16)
    return across(turned, rows).astype(jnp.bfloat16)


def tables_kernel(
    wide, pool, own_skeleton_hbm, own_compress_hbm, out_skeleton_hbm, out_compress_hbm,
    low_ref, both_ref, last_ref, last_full_ref, extra_ref,
    own_skeleton, own_compress, out_skeleton, out_compress, arrived,
):
    loads = [
        pltpu.make_async_copy(own_skeleton_hbm, own_skeleton, arrived.at[0]),
        pltpu.make_async_copy(own_compress_hbm, own_compress, arrived.at[1]),
        pltpu.make_async_copy(out_skeleton_hbm, out_skeleton, arrived.at[2]),
        pltpu.make_async_copy(out_compress_hbm, out_compress, arrived.at[3]),
    ]
    for load in loads:
        load.start()
    for load in loads:
        load.wait()
    rank = own_skeleton.shape[-1]
    width = 2 * rank
    f32, i32 = jnp.float32, jnp.int32
    twice = one_hot(
        lax.broadcasted_iota(i32, (width, rank), 0) % rank == lax.broadcasted_iota(i32, (width, rank), 1)
    )
    square_row = lax.broadcasted_iota(i32, (width, width), 0)
    square_lane = lax.broadcasted_iota(i32, (width, width), 1)
    earlier = one_hot(square_lane < square_row % rank)
    column = lax.broadcasted_iota(i32, (2 * width, width), 0)
    real_entry = lax.broadcasted_iota(i32, (2 * width, width), 1) < rank
    coefficient = column % rank

    def entries(skeleton, level):
        row = jnp.broadcast_to(skeleton[level].astype(f32), (8, rank)).astype(jnp.bfloat16)
        return across(row, twice)[:1].astype(i32)

    def halves(matrix, match, imag):
        same = real_entry != imag
        real = jnp.where(match & same, jnp.where(imag, -1.0, 1.0), 0.0).astype(jnp.bfloat16)
        turned = one_hot(match & jnp.logical_not(same))
        return across(matrix, real).astype(jnp.bfloat16), across(matrix, turned).astype(jnp.bfloat16)

    by_box_imag = column % width >= rank
    second_box = column >= width
    for level in range(wide):
        match = entries(own_skeleton, level) == coefficient + jnp.where(second_box, rank, 0)
        low_ref[level, :rank], low_ref[level, rank:] = halves(own_compress[0, level], match, by_box_imag)

    boxes = ((own_skeleton, own_compress), (out_skeleton, out_compress))
    for box, (skeleton, compress) in enumerate(boxes):
        partner = second_box if box == 0 else jnp.logical_not(second_box)
        match = entries(skeleton, wide) == coefficient + jnp.where(partner, rank, 0)
        real, imag = halves(compress[0, wide], match, by_box_imag)
        both_ref[box * rank : (box + 1) * rank] = real
        both_ref[width + box * rank : width + (box + 1) * rank] = imag

    by_part_imag = column >= width
    column_box = column % width // rank
    slot_imag = column >= pool
    slot_column = jnp.where(slot_imag, column - pool, column)
    used = jnp.zeros((1, 1), f32)
    places = jnp.zeros((width, width), f32)
    for box, (skeleton, compress) in enumerate(boxes):
        entry = entries(skeleton, wide + 1)
        matrix = compress[0, wide + 1]
        picked = jnp.where(entry >= rank, 1.0, 0.0)
        slot = across(jnp.broadcast_to(picked, (8, width)).astype(jnp.bfloat16), earlier)[:1]
        slot = jnp.where(entry >= rank, slot + used, -1.0).astype(i32)
        used = used + jnp.sum(picked, axis=1, keepdims=True) * 0.5
        rows = slice(box * width, box * width + rank)
        turned_rows = slice(box * width + rank, (box + 1) * width)
        match = (entry == coefficient) & (column_box == box)
        real, imag = halves(matrix, match, by_part_imag)
        last_ref[rows, : 2 * width] = real
        last_ref[turned_rows, : 2 * width] = imag
        last_full_ref[rows, : 2 * width] = real
        last_full_ref[turned_rows, : 2 * width] = imag
        real, imag = halves(matrix, slot == slot_column, slot_imag)
        last_ref[rows, 2 * width :] = real
        last_ref[turned_rows, 2 * width :] = imag
        match = (entry - rank == coefficient) & (column_box == 1 - box)
        real, imag = halves(matrix, match, by_part_imag)
        last_full_ref[rows, 2 * width :] = real
        last_full_ref[turned_rows, 2 * width :] = imag
        once = square_lane < rank
        here = entry - rank == square_row - (1 - box) * rank
        here = here & (entry >= rank) & (square_row // rank == 1 - box)
        places = places + across(one_hot(once & (slot == square_row)), one_hot(once & here))
    extra_ref[:width] = places.astype(jnp.bfloat16)
    extra_ref[width:] = jnp.broadcast_to(used, (width, width)).astype(jnp.bfloat16)


def tables(skeleton, compress, out_skeleton, out_compress, wide, pool):
    levels, rank = skeleton.shape[1:]
    width = 2 * rank
    out_shape = [
        jax.ShapeDtypeStruct(shape, jnp.bfloat16)
        for shape in (
            (wide, width, 2 * width),
            (2 * width, 2 * width),
            (2 * width, 4 * width),
            (2 * width, 4 * width),
            (2 * width, width),
        )
    ]
    small = [pltpu.VMEM((levels, 1, rank), jnp.int32), pltpu.VMEM(compress.shape, jnp.bfloat16)]
    return pl.pallas_call(
        lambda *refs: tables_kernel(wide, pool, *refs),
        out_shape=out_shape,
        in_specs=[pl.BlockSpec(memory_space=pltpu.HBM)] * 4,
        out_specs=[pl.BlockSpec(memory_space=pltpu.VMEM)] * 5,
        scratch_shapes=small + small + [pltpu.SemaphoreType.DMA((4,))],
        compiler_params=pltpu.CompilerParams(vmem_limit_bytes=16 * 1024 * 1024),
        cost_estimate=pl.CostEstimate(flops=50_000_000, bytes_accessed=1_000_000, transcendentals=0),
        name="tables",
    )(skeleton.transpose(1, 0, 2), compress, out_skeleton.transpose(1, 0, 2), out_compress)


def sampled_apart(sampling, traces):
    count, width = traces.shape
    block = count // 8

    def kernel(sampling_ref, rows_ref, coeffs_ref):
        coeffs_ref[...] = sampled_block(sampling_ref[...], rows_ref[...])

    return pl.pallas_call(
        kernel,
        grid=(count // block,),
        out_shape=jax.ShapeDtypeStruct((sampling.shape[1], count), jnp.bfloat16),
        in_specs=[
            pl.BlockSpec(sampling.shape, lambda i: (0, 0)),
            pl.BlockSpec((block, width), lambda i: (i, 0)),
        ],
        out_specs=pl.BlockSpec((sampling.shape[1], block), lambda i: (0, i)),
        compiler_params=pltpu.CompilerParams(vmem_limit_bytes=63 * 1024 * 1024),
        name="sampled_apart",
    )(sampling, traces)


def picked_columns(compress, skeleton):
    rank = skeleton.shape[-1]
    places = lax.broadcasted_iota(jnp.int32, (1, 1, 2 * rank), 2)
    chooser = (skeleton[:, :, None] == places).astype(jnp.bfloat16)
    stacked = jnp.concatenate([compress[:, :, :rank], compress[:, :, rank:]], 1)
    return jnp.einsum(
        "ljk,lki->lji", stacked, chooser, preferred_element_type=jnp.float32
    ).astype(jnp.bfloat16)


def real_form(both):
    rank = both.shape[1] // 2
    turned = jnp.concatenate([-both[:, rank:], both[:, :rank]], 1)
    return jnp.concatenate([both, turned], 2)


def times(matrix, value):
    return jnp.dot(matrix, value, preferred_element_type=jnp.float32).astype(jnp.bfloat16)


def sampled(sampling, traces):
    return jnp.einsum(
        "pc,tp->ct", sampling, traces, preferred_element_type=jnp.float32
    ).astype(jnp.bfloat16)


def evaluated(coeffs, evaluation):
    return jnp.einsum(
        "ct,cp->tp", coeffs, evaluation, preferred_element_type=jnp.float32
    ).astype(jnp.bfloat16)


def after(value, earlier):
    return value if earlier is None else lax.optimization_barrier((value, earlier))[0]


def all_hops():
    low_bits = lax.axis_size("sub").bit_length() - 1
    high_bits = lax.axis_size("bfly").bit_length() - 1
    return [("sub", bit) for bit in range(low_bits)] + [("bfly", bit) for bit in range(high_bits)]


def full_width(traces, sampling, skeleton, compress, evaluation):
    rank = skeleton.shape[-1]
    columns = picked_columns(compress, skeleton)
    full = jnp.concatenate([real_form(columns[..., :rank]), real_form(columns[..., rank:])], 2)
    coeffs = sampled_apart(sampling, traces)
    for level, hop in enumerate(all_hops()):
        partner = from_partner(coeffs, hop)
        coeffs = times(full[level], jnp.concatenate([coeffs, partner], 0))
    return evaluated(coeffs, evaluation)


def sequence(pieces, middle):
    def turn(at):
        stage, piece = at
        if stage == 0:
            return max(0, 2 * piece - 1.5)
        ahead = 0.45 if stage == middle and piece > 1 else 0
        late = 2.05 if stage == middle + 2 else 0
        return 2 * stage + 2.1 * piece - ahead + late

    return sorted(
        [(stage, piece) for stage in range(middle + 3) for piece in range(pieces)], key=turn
    )


def local(traces, sampling, skeleton, compress, evaluation):
    if lax.axis_size("bfly") != 4:
        return full_width(traces, sampling[0], skeleton[0], compress[0], evaluation[0])
    hops = all_hops()
    wide = len(hops) - 2
    middle = wide + 1
    rank = skeleton.shape[-1]
    width = 2 * rank
    pool = width * POOL_EIGHTHS // 8
    unit = traces.shape[0] // sum(SHARES)
    pieces = len(SHARES)
    starts = [unit * sum(SHARES[:i]) for i in range(pieces + 1)]
    place = lax.axis_index("bfly")
    inner = (place == 1) | (place == 2)

    out_compress = lax.ppermute(compress, "bfly", UP)
    out_skeleton = lax.ppermute(skeleton, "bfly", UP)
    low, both, last, last_full, extra = tables(
        skeleton, compress, out_skeleton, out_compress, wide, pool
    )
    sampling, evaluation = sampling[0], evaluation[0]

    inputs, arrivals, done = {}, {}, [None] * pieces
    previous, sending, most = None, None, None
    for stage, piece in sequence(pieces, middle):
        count = starts[piece + 1] - starts[piece]
        arrived = after(arrivals[piece], previous) if stage else None
        if stage == 0:
            block = traces[starts[piece] : starts[piece + 1]]
            own = outgoing = sampled(after(sampling, previous if piece > 1 else None), block)
        elif stage <= wide:
            own = outgoing = times(low[stage - 1], jnp.concatenate([inputs[piece], arrived], 0))
        elif stage == middle:
            value = jnp.concatenate([inputs[piece], arrived], 0)
            own = times(both, value)
            if piece == 0:
                outgoing = jnp.concatenate([own, extra], 1)
            else:
                outgoing = times(sending, value)
        elif stage == middle + 1:
            if piece == 0:
                theirs = arrived[:pool, count:]
                sending = jnp.concatenate(
                    [
                        jnp.dot(theirs, half, preferred_element_type=jnp.float32)
                        for half in (both[:width], both[width:])
                    ],
                    0,
                ).astype(jnp.bfloat16)
                most = jnp.maximum(extra[width : width + 8], arrived[width : width + 8, count:])
                value = jnp.concatenate([inputs[piece], arrived[:, :count]], 0)
                matrix = last_full
            else:
                value = jnp.concatenate([inputs[piece], arrived], 0)
                value = jnp.pad(value, ((0, 4 * width - value.shape[0]), (0, 0)))
                matrix = last
            outgoing = times(matrix[width:], value)
            own = times(matrix[:width], value)
        else:
            done[piece] = evaluated(jnp.where(inner, inputs[piece], arrived), evaluation)
            continue
        inputs[piece] = own
        if stage < wide:
            arrivals[piece] = from_partner(outgoing, hops[stage])
        else:
            arrivals[piece] = lax.ppermute(outgoing, "bfly", (UP, MIDDLE, DOWN)[stage - wide])
        previous = outgoing
        if stage == middle and piece == pieces - 1:
            most = after(most, previous)
            for hop in hops[:wide]:
                most = jnp.maximum(most, from_partner(most, hop))
            most = jnp.where(inner, most, lax.ppermute(most, "bfly", DOWN))
    quick = jnp.concatenate(done, 0)
    return lax.cond(
        most[0, 0] > pool,
        lambda: full_width(traces, sampling, skeleton[0], compress[0], evaluation),
        lambda: quick,
    )


def solution(mesh):
    placed = (
        P(("shots", "tr"), ("bfly", "sub")),
        P(("bfly", "sub"), None, None),
        P(("bfly", "sub"), None, None),
        P(("bfly", "sub"), None, None, None),
        P(("bfly", "sub"), None, None),
    )
    return jax.shard_map(
        local,
        mesh=mesh,
        in_specs=placed,
        out_specs=P(("shots", "tr"), ("bfly", "sub")),
        check_vma=False,
    )
```

time: 69.3 us -> 98.6 us (1.42)
  starting transfers between devices: 31.9 us -> 55.6 us
  matrix products: 15.1 us -> 24.4 us
  waiting for transfers between devices: 18.3 us -> 13.5 us
    ppermute x0 -> x18, starting transfers between devices: none -> 48.2 us  [the longest x15 40.5 us: local(): lax.ppermute(outgoing, 'bfly', (UP, MIDDLE, DOWN)[stage - wide])]
    ppermute x16 -> x6, starting transfers between devices: 31.9 us -> 7.43 us  [from_partner(): return lax.ppermute(block, hop[0], route(*hop))]
    ppermute x16 -> x6, waiting for transfers between devices: 18.3 us -> 1.05 us  [from_partner(): return lax.ppermute(block, hop[0], route(*hop))]
    ppermute x0 -> x18, waiting for transfers between devices: none -> 12.5 us  [the longest x15 8.81 us: local(): lax.ppermute(outgoing, 'bfly', (UP, MIDDLE, DOWN)[stage - wide])]
    dot_general x16 -> x19, matrix products: 4.26 us -> 10.1 us  [times(): jnp.dot(matrix, value, preferred_element_type=jnp.float32)]
    dot_general x5, matrix products: 5.59 us -> 8.03 us  [evaluated(): jnp.einsum('ct,cp->tp', coeffs, evaluation, preferred_element_type=jnp.fl...]
    dot_general x4 -> x5, matrix products: 4.77 us -> 5.98 us  [sampled(): jnp.einsum('pc,tp->ct', sampling, traces, preferred_element_type=jnp.floa...]
  transfers between devices with their start and end apart: 16 -> 24, of which waited for: 7 -> 7; matrix products, arithmetic and copies ran while one was open for 21% -> 24% of each run, Pallas kernels for 0% -> 2%
where the time goes in v9:
time: 98.6 us; the launch traced here: 97.7 us
  starting transfers between devices  55.6 us (56%)
  matrix products  24.4 us (25%)
  waiting for transfers between devices  13.5 us (14%)
  Pallas kernels  2.36 us (2%)
  between operations  1.1 us (1%)
    ppermute x15, starting transfers between devices, local(): lax.ppermute(outgoing, 'bfly', (UP, MIDDLE, DOWN)[stage - wide])  40.5 us
    dot_general x19, matrix products, times(): jnp.dot(matrix, value, preferred_element_type=jnp.float32)  10.1 us
    ppermute x15, waiting for transfers between devices, local(): lax.ppermute(outgoing, 'bfly', (UP, MIDDLE, DOWN)[stage - wide])  8.81 us
    dot_general x5, matrix products, evaluated(): jnp.einsum('ct,cp->tp', coeffs, evaluation, preferred_element_type=jnp.fl...  8.03 us
    ppermute x6, starting transfers between devices, from_partner(): return lax.ppermute(block, hop[0], route(*hop))  7.43 us
    dot_general x5, matrix products, sampled(): jnp.einsum('pc,tp->ct', sampling, traces, preferred_element_type=jnp.floa...  5.98 us
    ppermute x1, starting transfers between devices, local(): out_skeleton = lax.ppermute(skeleton, 'bfly', UP)  5.05 us
    ppermute x1, waiting for transfers between devices, local(): most = jnp.where(inner, most, lax.ppermute(most, 'bfly', DOWN))  3.68 us
  transfers between devices with their start and end apart: 24, of which 7 were waited for; matrix products, arithmetic and copies ran while one was open for 24% of the time, Pallas kernels for 2%

profile of v9, /device:TPU:0, one launch (start us, length us, event | category | flops | bytes accessed | tf_op | source)
XLA Modules:
  0.0 97.7 jit_solution(6107014147600306767)
XLA Ops:
  0.0 5.0 %collective-permute-start.3 = (s32[1,3,64]{2,0,1:T(1,128)}, s32[1,3,64]{2,0,1:T(1,128)S(1)}, u32[]{:S(2)}, u32[]{:S(2)}) collective-permute-start(s32[1,3,64]{2,0,1:T(1,128)} %param.9), channel_id=1, source_target_pairs={{0,4},{12,8},{1,5},{13,9},{2,6},{14,10},{3,7},{15,11},{16,20},{28,... | collective-permute-start | bytes 2312 | tf_op jit(solution)/shard_map/ppermute | solution.py:261
  5.1 1.3 %collective-permute-start.4 = (bf16[1,3,64,128]{3,2,1,0:T(8,128)(2,1)}, bf16[1,3,64,128]{3,2,1,0:T(8,128)(2,1)S(1)}, u32[]{:S(2)}, u32[]{:S(2)}) collective-permute-start(bf16[1,3,64,128]{3,2,1,0:T(8,128)(2,1)} %refs_1_.1), channel_id=1, source_target_pairs={{0,4},{12,8},{1,5},{13,9},{2,6},{14,10},{3,7},{15,11},{16,20},{28,... | collective-permute-start | bytes 147464 | tf_op jit(solution)/shard_map/ppermute | solution.py:260
  7.4 1.6 %collective-permute-start.5 = (bf16[128,256]{1,0:T(8,128)(2,1)S(1)}, bf16[128,256]{1,0:T(8,128)(2,1)S(1)}, u32[]{:S(2)}, u32[]{:S(2)}) collective-permute-start(bf16[128,256]{1,0:T(8,128)(2,1)S(1)} %convolution_convert_fusion.37), channel_id=1, source_target_pairs={{0,2},{2,0},{1,3},{3,1},{4,6},{6,4},{5,7},{7,5},{8,10},{10,8},{9,1... | collective-permute-start | bytes 196616 | tf_op jit(solution)/shard_map/ppermute | solution.py:27
  10.8 2.4 %tables.1 = (bf16[1,128,256]{2,1,0:T(8,128)(2,1)S(1)}, bf16[256,256]{1,0:T(8,128)(2,1)S(1)}, bf16[256,512]{1,0:T(8,128)(2,1)S(1)}, bf16[256,512]{1,0:T(8,128)(2,1)S(1)}, bf16[256,128]{1,0:T(8,128)(2,1)S(1)}) custom-call(s32[3,1,64]{2,1,0:T(1,128)} %bitcast.60, bf16[1,3,64,128]{3,2,1,0:T(8,128)(2,1)} %refs_1_.1, s32[3,1,64]{2,1,0:T(1,128)S(1)} %bitcast.53, ...), custom_call_target="tpu_custom_call" | custom-call | flops 50000000 | bytes 1000000 | tf_op jit(solution)/shard_map/tables/pallas_call | solution.py:145
  13.3 1.8 %collective-permute-start.6 = (bf16[128,256]{1,0:T(8,128)(2,1)S(1)}, bf16[128,256]{1,0:T(8,128)(2,1)S(1)}, u32[]{:S(2)}, u32[]{:S(2)}) collective-permute-start(bf16[128,256]{1,0:T(8,128)(2,1)S(1)} %convolution_convert_fusion.38), channel_id=1, source_target_pairs={{0,4},{12,8},{1,5},{13,9},{2,6},{14,10},{3,7},{15,11},{16,20},{28,... | collective-permute-start | bytes 196616 | tf_op jit(solution)/shard_map/ppermute | solution.py:310
  15.1 1.2 %convolution_convert_fusion.21 = bf16[128,1024]{1,0:T(8,128)(2,1)S(1)} fusion(bf16[128,128]{1,0:T(8,128)(2,1)S(1)} %bitcast.54, bf16[4096,128]{1,0:T(8,128)(2,1)} %param.7), kind=kOutput, calls=%fused_computation.61 | convolution fusion | flops 33685504 | bytes 557056 | tf_op jit(solution)/shard_map/pc,tp->ct/dot_general | solution.py:199
  16.3 1.6 %collective-permute-start.9 = (bf16[128,1024]{1,0:T(8,128)(2,1)S(1)}, bf16[128,1024]{1,0:T(8,128)(2,1)S(1)}, u32[]{:S(2)}, u32[]{:S(2)}) collective-permute-start(bf16[128,1024]{1,0:T(8,128)(2,1)S(1)} %convolution_convert_fusion.21), channel_id=1, source_target_pairs={{0,2},{2,0},{1,3},{3,1},{4,6},{6,4},{5,7},{7,5},{8,10},{10,8},{9,1... | collective-permute-start | bytes 786440 | tf_op jit(solution)/shard_map/ppermute | solution.py:27
  19.0 6.2 %collective-permute-start.10 = (bf16[128,768]{1,0:T(8,128)(2,1)S(1)}, bf16[128,768]{1,0:T(8,128)(2,1)S(1)}, u32[]{:S(2)}, u32[]{:S(2)}) collective-permute-start(bf16[128,768]{1,0:T(8,128)(2,1)S(1)} %convolution_convert_fusion.29), channel_id=1, source_target_pairs={{0,4},{12,8},{1,5},{13,9},{2,6},{14,10},{3,7},{15,11},{16,20},{28,... | collective-permute-start | bytes 589832 | tf_op jit(solution)/shard_map/ppermute | solution.py:310
  25.2 1.2 %convolution_convert_fusion.11 = bf16[128,1152]{1,0:T(8,128)(2,1)S(1)} fusion(bf16[128,128]{1,0:T(8,128)(2,1)S(1)} %bitcast.55, bf16[4096,128]{1,0:T(8,128)(2,1)} %param.7), kind=kOutput, calls=%fused_computation.37 | convolution fusion | flops 37896192 | bytes 622592 | tf_op jit(solution)/shard_map/pc,tp->ct/dot_general | solution.py:199
  26.5 1.6 %collective-permute-start.14 = (bf16[128,1152]{1,0:T(8,128)(2,1)S(1)}, bf16[128,1152]{1,0:T(8,128)(2,1)S(1)}, u32[]{:S(2)}, u32[]{:S(2)}) collective-permute-start(bf16[128,1152]{1,0:T(8,128)(2,1)S(1)} %convolution_convert_fusion.11), channel_id=1, source_target_pairs={{0,2},{2,0},{1,3},{3,1},{4,6},{6,4},{5,7},{7,5},{8,10},{10,8},{9,1... | collective-permute-start | bytes 884744 | tf_op jit(solution)/shard_map/ppermute | solution.py:27
  29.7 5.9 %collective-permute-start.12 = (bf16[128,1024]{1,0:T(8,128)(2,1)S(1)}, bf16[128,1024]{1,0:T(8,128)(2,1)S(1)}, u32[]{:S(2)}, u32[]{:S(2)}) collective-permute-start(bf16[128,1024]{1,0:T(8,128)(2,1)S(1)} %convolution_convert_fusion.20), channel_id=1, source_target_pairs={{0,4},{12,8},{1,5},{13,9},{2,6},{14,10},{3,7},{15,11},{16,20},{28,... | collective-permute-start | bytes 786440 | tf_op jit(solution)/shard_map/ppermute | solution.py:310
  35.9 1.3 %convolution_convert_fusion.25 = bf16[128,896]{1,0:T(8,128)(2,1)S(1)} fusion(bf16[128,128]{1,0:T(8,128)(2,1)S(1)} %bitcast.56, bf16[4096,128]{1,0:T(8,128)(2,1)} %param.7), kind=kOutput, calls=%fused_computation.66 | convolution fusion | flops 29474816 | bytes 491520 | tf_op jit(solution)/shard_map/pc,tp->ct/dot_general | solution.py:199
  37.3 2.2 %collective-permute-done.12 = bf16[128,1024]{1,0:T(8,128)(2,1)S(1)} collective-permute-done((bf16[128,1024]{1,0:T(8,128)(2,1)S(1)}, bf16[128,1024]{1,0:T(8,128)(2,1)S(1)}, u32[]{:S(2)}, u32[]{:S(2)}) %collective-permute-start.12) | collective-permute-done | bytes 262176 | tf_op jit(solution)/shard_map/ppermute | solution.py:310
  41.0 4.4 %collective-permute-start.16 = (bf16[128,1152]{1,0:T(8,128)(2,1)S(1)}, bf16[128,1152]{1,0:T(8,128)(2,1)S(1)}, u32[]{:S(2)}, u32[]{:S(2)}) collective-permute-start(bf16[128,1152]{1,0:T(8,128)(2,1)S(1)} %convolution_convert_fusion.10), channel_id=1, source_target_pairs={{0,4},{12,8},{1,5},{13,9},{2,6},{14,10},{3,7},{15,11},{16,20},{28,... | collective-permute-start | bytes 884744 | tf_op jit(solution)/shard_map/ppermute | solution.py:310
  45.4 1.3 %collective-permute-start.20 = (bf16[128,256]{1,0:T(8,128)(2,1)S(1)}, bf16[128,256]{1,0:T(8,128)(2,1)S(1)}, u32[]{:S(2)}, u32[]{:S(2)}) collective-permute-start(bf16[128,256]{1,0:T(8,128)(2,1)S(1)} %convolution_convert_fusion.36), channel_id=1, source_target_pairs={{4,0},{8,12},{5,1},{9,13},{6,2},{10,14},{7,3},{11,15},{20,16},{24,... | collective-permute-start | bytes 196616 | tf_op jit(solution)/shard_map/ppermute | solution.py:310
  46.7 1.6 %collective-permute-start.11 = (bf16[128,896]{1,0:T(8,128)(2,1)S(1)}, bf16[128,896]{1,0:T(8,128)(2,1)S(1)}, u32[]{:S(2)}, u32[]{:S(2)}) collective-permute-start(bf16[128,896]{1,0:T(8,128)(2,1)S(1)} %convolution_convert_fusion.25), channel_id=1, source_target_pairs={{0,2},{2,0},{1,3},{3,1},{4,6},{6,4},{5,7},{7,5},{8,10},{10,8},{9,1... | collective-permute-start | bytes 688136 | tf_op jit(solution)/shard_map/ppermute | solution.py:27
  49.0 1.3 %collective-permute-start.21 = (bf16[128,768]{1,0:T(8,128)(2,1)}, bf16[128,768]{1,0:T(8,128)(2,1)}, u32[]{:S(2)}, u32[]{:S(2)}) collective-permute-start(bf16[128,768]{1,0:T(8,128)(2,1)} %convolution_convert_fusion.32), channel_id=1, source_target_pairs={{4,0},{8,12},{5,1},{9,13},{6,2},{10,14},{7,3},{11,15},{20,16},{24,... | collective-permute-start | bytes 589832 | tf_op jit(solution)/shard_map/ppermute | solution.py:310
  54.0 12.3 %collective-permute-start.17 = (bf16[128,896]{1,0:T(8,128)(2,1)S(1)}, bf16[128,896]{1,0:T(8,128)(2,1)}, u32[]{:S(2)}, u32[]{:S(2)}) collective-permute-start(bf16[128,896]{1,0:T(8,128)(2,1)S(1)} %convolution_convert_fusion.24), channel_id=1, source_target_pairs={{0,4},{12,8},{1,5},{13,9},{2,6},{14,10},{3,7},{15,11},{16,20},{28,... | collective-permute-start | bytes 688136 | tf_op jit(solution)/shard_map/ppermute | solution.py:310
  67.3 1.3 %collective-permute-start.22 = (bf16[128,1024]{1,0:T(8,128)(2,1)S(1)}, bf16[128,1024]{1,0:T(8,128)(2,1)S(1)}, u32[]{:S(2)}, u32[]{:S(2)}) collective-permute-start(bf16[128,1024]{1,0:T(8,128)(2,1)S(1)} %convolution_convert_fusion.19), channel_id=1, source_target_pairs={{4,0},{8,12},{5,1},{9,13},{6,2},{10,14},{7,3},{11,15},{20,16},{24,... | collective-permute-start | bytes 786440 | tf_op jit(solution)/shard_map/ppermute | solution.py:310
  69.1 1.2 %convolution_convert_fusion.16 = bf16[160,896]{1,0:T(8,128)(2,1)S(1)} fusion(bf16[128,896]{1,0:T(8,128)(2,1)} %collective-permute-done.17, bf16[128,896]{1,0:T(8,128)(2,1)S(1)} %convolution_convert_fusion.24, bf16[80,256]{1,0:T(8,128)(2,1)S(1)} %convolution_convert_fusion.39, bf16[80,256]{1,0:T(8,128)(2,1)S(1)} %convolution_convert_fusion.40), kind=kOutput, calls=%fused_computation.55 | convolution fusion | flops 74625024 | bytes 827392 | tf_op jit(solution)/shard_map/dot_general | solution.py:195
  71.6 2.0 %convolution_convert_fusion.13 = bf16[256,896]{1,0:T(8,128)(2,1)} fusion(bf16[256,256]{1,0:T(8,128)(2,1)S(1)} %get-tuple-element.54, bf16[128,896]{1,0:T(8,128)(2,1)} %collective-permute-done.17, bf16[128,896]{1,0:T(8,128)(2,1)S(1)} %convolution_convert_fusion.24), kind=kOutput, calls=%fused_computation.52 | convolution fusion | flops 118587392 | bytes 1048576 | tf_op jit(solution)/shard_map/dot_general | solution.py:195
  74.6 1.3 %collective-permute-start.19 = (bf16[8,128]{1,0:T(8,128)(2,1)S(1)}, bf16[8,128]{1,0:T(8,128)(2,1)S(1)}, u32[]{:S(2)}, u32[]{:S(2)}) collective-permute-start(bf16[8,128]{1,0:T(8,128)(2,1)S(1)} %max.7), channel_id=1, source_target_pairs={{4,0},{8,12},{5,1},{9,13},{6,2},{10,14},{7,3},{11,15},{20,16},{24,... | collective-permute-start | bytes 6152 | tf_op jit(solution)/shard_map/ppermute | solution.py:316
  75.9 2.2 %fusion.33 = bf16[4096,128]{1,0:T(8,128)(2,1)} fusion(bf16[4096,128]{1,0:T(8,128)(2,1)} %fusion.37, bf16[128,768]{1,0:T(8,128)(2,1)} %collective-permute-done.21, bf16[160,768]{1,0:T(8,128)(2,1)S(1)} %collective-permute-done.15, bf16[256,768]{1,0:T(8,128)(2,1)} %copy-done.5, pred[]{:T(512)S(6)} %or.3, bf16[256,512]{1,0:T(8,128)(2,1)S(1)} %get-tuple-element.66, ...), kind=kOutput, calls=%fused_computation.71 | convolution fusion | flops 128876544 | bytes 1196033 | tf_op jit(solution)/shard_map/ct,cp->tp/dot_general | solution.py:205
  78.1 3.7 %collective-permute-done.19 = bf16[8,128]{1,0:T(8,128)(2,1)S(1)} collective-permute-done((bf16[8,128]{1,0:T(8,128)(2,1)S(1)}, bf16[8,128]{1,0:T(8,128)(2,1)S(1)}, u32[]{:S(2)}, u32[]{:S(2)}) %collective-permute-start.19) | collective-permute-done | bytes 2080 | tf_op jit(solution)/shard_map/ppermute | solution.py:316
  83.0 1.4 %convolution_convert_fusion.9 = bf16[128,1152]{1,0:T(8,128)(2,1)S(1)} fusion(bf16[160,1152]{1,0:T(8,128)(2,1)S(1)} %collective-permute-done.23, bf16[256,1152]{1,0:T(8,128)(2,1)} %convolution_convert_fusion.5, bf16[256,512]{1,0:T(8,128)(2,1)S(1)} %get-tuple-element.66), kind=kOutput, calls=%fused_computation.35 | convolution fusion | flops 155271168 | bytes 1384448 | tf_op jit(solution)/shard_map/dot_general | solution.py:195
  84.5 1.4 %collective-permute-start.24 = (bf16[128,1152]{1,0:T(8,128)(2,1)S(1)}, bf16[128,1152]{1,0:T(8,128)(2,1)S(1)}, u32[]{:S(2)}, u32[]{:S(2)}) collective-permute-start(bf16[128,1152]{1,0:T(8,128)(2,1)S(1)} %convolution_convert_fusion.9), channel_id=1, source_target_pairs={{4,0},{8,12},{5,1},{9,13},{6,2},{10,14},{7,3},{11,15},{20,16},{24,... | collective-permute-start | bytes 884744 | tf_op jit(solution)/shard_map/ppermute | solution.py:310
  85.9 2.3 %fusion.30 = bf16[4096,128]{1,0:T(8,128)(2,1)} fusion(bf16[4096,128]{1,0:T(8,128)(2,1)} %fusion.33, bf16[128,1024]{1,0:T(8,128)(2,1)S(1)} %collective-permute-done.22, bf16[160,1024]{1,0:T(8,128)(2,1)S(1)} %collective-permute-done.13, bf16[256,1024]{1,0:T(8,128)(2,1)} %copy-done.7, pred[]{:T(512)S(6)} %or.3, bf16[256,512]{1,0:T(8,128)(2,1)S(1)} %get-tuple-element.66, ...), kind=kOutput, calls=%fused_computation.57 | convolution fusion | flops 171835392 | bytes 1540097 | tf_op jit(solution)/shard_map/ct,cp->tp/dot_general | solution.py:205
  88.5 1.3 %collective-permute-start.26 = (bf16[128,896]{1,0:T(8,128)(2,1)S(1)}, bf16[128,896]{1,0:T(8,128)(2,1)S(1)}, u32[]{:S(2)}, u32[]{:S(2)}) collective-permute-start(bf16[128,896]{1,0:T(8,128)(2,1)S(1)} %convolution_convert_fusion.27), channel_id=1, source_target_pairs={{4,0},{8,12},{5,1},{9,13},{6,2},{10,14},{7,3},{11,15},{20,16},{24,... | collective-permute-start | bytes 688136 | tf_op jit(solution)/shard_map/ppermute | solution.py:310
  89.8 3.4 %collective-permute-done.24 = bf16[128,1152]{1,0:T(8,128)(2,1)S(1)} collective-permute-done((bf16[128,1152]{1,0:T(8,128)(2,1)S(1)}, bf16[128,1152]{1,0:T(8,128)(2,1)S(1)}, u32[]{:S(2)}, u32[]{:S(2)}) %collective-permute-start.24) | collective-permute-done | bytes 294944 | tf_op jit(solution)/shard_map/ppermute | solution.py:310
  93.2 1.3 %fusion.20 = bf16[4096,128]{1,0:T(8,128)(2,1)} fusion(bf16[4096,128]{1,0:T(8,128)(2,1)} %fusion.30, bf16[128,1152]{1,0:T(8,128)(2,1)S(1)} %collective-permute-done.24, bf16[160,1152]{1,0:T(8,128)(2,1)S(1)} %collective-permute-done.23, bf16[256,1152]{1,0:T(8,128)(2,1)S(1)} %copy-done.8, pred[]{:T(512)S(6)} %or.3, ...), kind=kOutput, calls=%fused_computation.33 | convolution fusion | flops 193314816 | bytes 1712129 | tf_op jit(solution)/shard_map/ct,cp->tp/dot_general | solution.py:205
  94.5 1.9 %collective-permute-done.26 = bf16[128,896]{1,0:T(8,128)(2,1)S(1)} collective-permute-done((bf16[128,896]{1,0:T(8,128)(2,1)S(1)}, bf16[128,896]{1,0:T(8,128)(2,1)S(1)}, u32[]{:S(2)}, u32[]{:S(2)}) %collective-permute-start.26) | collective-permute-done | bytes 229408 | tf_op jit(solution)/shard_map/ppermute | solution.py:310
  96.4 1.2 %fusion.31 = bf16[4096,128]{1,0:T(8,128)(2,1)} fusion(bf16[4096,128]{1,0:T(8,128)(2,1)} %fusion.20, bf16[128,896]{1,0:T(8,128)(2,1)S(1)} %collective-permute-done.26, bf16[160,896]{1,0:T(8,128)(2,1)S(1)} %collective-permute-done.25, bf16[256,896]{1,0:T(8,128)(2,1)S(1)} %copy-done.6, pred[]{:T(512)S(6)} %or.3, bf16[256,512]{1,0:T(8,128)(2,1)S(1)} %get-tuple-element.66, ...), kind=kOutput, calls=%fused_computation.64 | convolution fusion | flops 150355968 | bytes 1368065 | tf_op jit(solution)/shard_map/ct,cp->tp/dot_general | solution.py:205
  (71 shorter events, 16.6 us)
Async XLA Ops:
  0.0 15.1 %copy-start = (bf16[1,128,128]{2,1,0:T(8,128)(2,1)S(1)}, bf16[1,128,128]{2,1,0:T(8,128)(2,1)}, u32[]{:S(2)}) copy-start(bf16[1,128,128]{2,1,0:T(8,128)(2,1)} %param.8) | copy-start | bytes 98308
  0.0 10.8 %collective-permute-start.3 = (s32[1,3,64]{2,0,1:T(1,128)}, s32[1,3,64]{2,0,1:T(1,128)S(1)}, u32[]{:S(2)}, u32[]{:S(2)}) collective-permute-start(s32[1,3,64]{2,0,1:T(1,128)} %param.9), channel_id=1, source_target_pairs={{0,4},{12,8},{1,5},{13,9},{2,6},{14,10},{3,7},{15,11},{16,20},{28,... | collective-permute-start | bytes 2312 | tf_op jit(solution)/shard_map/ppermute | solution.py:261
  5.1 5.7 %collective-permute-start.4 = (bf16[1,3,64,128]{3,2,1,0:T(8,128)(2,1)}, bf16[1,3,64,128]{3,2,1,0:T(8,128)(2,1)S(1)}, u32[]{:S(2)}, u32[]{:S(2)}) collective-permute-start(bf16[1,3,64,128]{3,2,1,0:T(8,128)(2,1)} %refs_1_.1), channel_id=1, source_target_pairs={{0,4},{12,8},{1,5},{13,9},{2,6},{14,10},{3,7},{15,11},{16,20},{28,... | collective-permute-start | bytes 147464 | tf_op jit(solution)/shard_map/ppermute | solution.py:260
  7.4 5.7 %collective-permute-start.5 = (bf16[128,256]{1,0:T(8,128)(2,1)S(1)}, bf16[128,256]{1,0:T(8,128)(2,1)S(1)}, u32[]{:S(2)}, u32[]{:S(2)}) collective-permute-start(bf16[128,256]{1,0:T(8,128)(2,1)S(1)} %convolution_convert_fusion.37), channel_id=1, source_target_pairs={{0,2},{2,0},{1,3},{3,1},{4,6},{6,4},{5,7},{7,5},{8,10},{10,8},{9,1... | collective-permute-start | bytes 196616 | tf_op jit(solution)/shard_map/ppermute | solution.py:27
  10.2 8.6 %collective-permute-start.8 = (bf16[128,768]{1,0:T(8,128)(2,1)S(1)}, bf16[128,768]{1,0:T(8,128)(2,1)S(1)}, u32[]{:S(2)}, u32[]{:S(2)}) collective-permute-start(bf16[128,768]{1,0:T(8,128)(2,1)S(1)} %convolution_convert_fusion.30), channel_id=1, source_target_pairs={{0,2},{2,0},{1,3},{3,1},{4,6},{6,4},{5,7},{7,5},{8,10},{10,8},{9,1... | collective-permute-start | bytes 589832 | tf_op jit(solution)/shard_map/ppermute | solution.py:27
  13.3 4.6 %collective-permute-start.6 = (bf16[128,256]{1,0:T(8,128)(2,1)S(1)}, bf16[128,256]{1,0:T(8,128)(2,1)S(1)}, u32[]{:S(2)}, u32[]{:S(2)}) collective-permute-start(bf16[128,256]{1,0:T(8,128)(2,1)S(1)} %convolution_convert_fusion.38), channel_id=1, source_target_pairs={{0,4},{12,8},{1,5},{13,9},{2,6},{14,10},{3,7},{15,11},{16,20},{28,... | collective-permute-start | bytes 196616 | tf_op jit(solution)/shard_map/ppermute | solution.py:310
  16.3 13.1 %collective-permute-start.9 = (bf16[128,1024]{1,0:T(8,128)(2,1)S(1)}, bf16[128,1024]{1,0:T(8,128)(2,1)S(1)}, u32[]{:S(2)}, u32[]{:S(2)}) collective-permute-start(bf16[128,1024]{1,0:T(8,128)(2,1)S(1)} %convolution_convert_fusion.21), channel_id=1, source_target_pairs={{0,2},{2,0},{1,3},{3,1},{4,6},{6,4},{5,7},{7,5},{8,10},{10,8},{9,1... | collective-permute-start | bytes 786440 | tf_op jit(solution)/shard_map/ppermute | solution.py:27
  18.1 9.9 %collective-permute-start.7 = (bf16[256,384]{1,0:T(8,128)(2,1)S(1)}, bf16[256,384]{1,0:T(8,128)(2,1)S(1)}, u32[]{:S(2)}, u32[]{:S(2)}) collective-permute-start(bf16[256,384]{1,0:T(8,128)(2,1)S(1)} %pad_maximum_fusion.13), channel_id=1, source_target_pairs={{4,8},{8,4},{5,9},{9,5},{6,10},{10,6},{7,11},{11,7},{20,24},{24,20... | collective-permute-start | bytes 589832 | tf_op jit(solution)/shard_map/ppermute | solution.py:310
  19.0 9.5 %collective-permute-start.10 = (bf16[128,768]{1,0:T(8,128)(2,1)S(1)}, bf16[128,768]{1,0:T(8,128)(2,1)S(1)}, u32[]{:S(2)}, u32[]{:S(2)}) collective-permute-start(bf16[128,768]{1,0:T(8,128)(2,1)S(1)} %convolution_convert_fusion.29), channel_id=1, source_target_pairs={{0,4},{12,8},{1,5},{13,9},{2,6},{14,10},{3,7},{15,11},{16,20},{28,... | collective-permute-start | bytes 589832 | tf_op jit(solution)/shard_map/ppermute | solution.py:310
  26.5 14.3 %collective-permute-start.14 = (bf16[128,1152]{1,0:T(8,128)(2,1)S(1)}, bf16[128,1152]{1,0:T(8,128)(2,1)S(1)}, u32[]{:S(2)}, u32[]{:S(2)}) collective-permute-start(bf16[128,1152]{1,0:T(8,128)(2,1)S(1)} %convolution_convert_fusion.11), channel_id=1, source_target_pairs={{0,2},{2,0},{1,3},{3,1},{4,6},{6,4},{5,7},{7,5},{8,10},{10,8},{9,1... | collective-permute-start | bytes 884744 | tf_op jit(solution)/shard_map/ppermute | solution.py:27
  28.8 11.0 %collective-permute-start.15 = (bf16[160,768]{1,0:T(8,128)(2,1)S(1)}, bf16[160,768]{1,0:T(8,128)(2,1)S(1)}, u32[]{:S(2)}, u32[]{:S(2)}) collective-permute-start(bf16[160,768]{1,0:T(8,128)(2,1)S(1)} %convolution_convert_fusion.22), channel_id=1, source_target_pairs={{4,8},{8,4},{5,9},{9,5},{6,10},{10,6},{7,11},{11,7},{20,24},{24,20... | collective-permute-start | bytes 737288 | tf_op jit(solution)/shard_map/ppermute | solution.py:310
  29.7 9.8 %collective-permute-start.12 = (bf16[128,1024]{1,0:T(8,128)(2,1)S(1)}, bf16[128,1024]{1,0:T(8,128)(2,1)S(1)}, u32[]{:S(2)}, u32[]{:S(2)}) collective-permute-start(bf16[128,1024]{1,0:T(8,128)(2,1)S(1)} %convolution_convert_fusion.20), channel_id=1, source_target_pairs={{0,4},{12,8},{1,5},{13,9},{2,6},{14,10},{3,7},{15,11},{16,20},{28,... | collective-permute-start | bytes 786440 | tf_op jit(solution)/shard_map/ppermute | solution.py:310
  35.9 10.8 %copy-start.5 = (bf16[256,768]{1,0:T(8,128)(2,1)}, bf16[256,768]{1,0:T(8,128)(2,1)S(1)}, u32[]{:S(2)}) copy-start(bf16[256,768]{1,0:T(8,128)(2,1)S(1)} %convolution_convert_fusion.14) | copy-start | bytes 1179652
  41.0 9.6 %collective-permute-start.16 = (bf16[128,1152]{1,0:T(8,128)(2,1)S(1)}, bf16[128,1152]{1,0:T(8,128)(2,1)S(1)}, u32[]{:S(2)}, u32[]{:S(2)}) collective-permute-start(bf16[128,1152]{1,0:T(8,128)(2,1)S(1)} %convolution_convert_fusion.10), channel_id=1, source_target_pairs={{0,4},{12,8},{1,5},{13,9},{2,6},{14,10},{3,7},{15,11},{16,20},{28,... | collective-permute-start | bytes 884744 | tf_op jit(solution)/shard_map/ppermute | solution.py:310
  45.4 6.9 %collective-permute-start.20 = (bf16[128,256]{1,0:T(8,128)(2,1)S(1)}, bf16[128,256]{1,0:T(8,128)(2,1)S(1)}, u32[]{:S(2)}, u32[]{:S(2)}) collective-permute-start(bf16[128,256]{1,0:T(8,128)(2,1)S(1)} %convolution_convert_fusion.36), channel_id=1, source_target_pairs={{4,0},{8,12},{5,1},{9,13},{6,2},{10,14},{7,3},{11,15},{20,16},{24,... | collective-permute-start | bytes 196616 | tf_op jit(solution)/shard_map/ppermute | solution.py:310
  46.7 7.0 %collective-permute-start.11 = (bf16[128,896]{1,0:T(8,128)(2,1)S(1)}, bf16[128,896]{1,0:T(8,128)(2,1)S(1)}, u32[]{:S(2)}, u32[]{:S(2)}) collective-permute-start(bf16[128,896]{1,0:T(8,128)(2,1)S(1)} %convolution_convert_fusion.25), channel_id=1, source_target_pairs={{0,2},{2,0},{1,3},{3,1},{4,6},{6,4},{5,7},{7,5},{8,10},{10,8},{9,1... | collective-permute-start | bytes 688136 | tf_op jit(solution)/shard_map/ppermute | solution.py:27
  48.3 5.1 %collective-permute-start.13 = (bf16[160,1024]{1,0:T(8,128)(2,1)S(1)}, bf16[160,1024]{1,0:T(8,128)(2,1)S(1)}, u32[]{:S(2)}, u32[]{:S(2)}) collective-permute-start(bf16[160,1024]{1,0:T(8,128)(2,1)S(1)} %convolution_convert_fusion.15), channel_id=1, source_target_pairs={{4,8},{8,4},{5,9},{9,5},{6,10},{10,6},{7,11},{11,7},{20,24},{24,20... | collective-permute-start | bytes 983048 | tf_op jit(solution)/shard_map/ppermute | solution.py:310
  49.0 24.6 %collective-permute-start.21 = (bf16[128,768]{1,0:T(8,128)(2,1)}, bf16[128,768]{1,0:T(8,128)(2,1)}, u32[]{:S(2)}, u32[]{:S(2)}) collective-permute-start(bf16[128,768]{1,0:T(8,128)(2,1)} %convolution_convert_fusion.32), channel_id=1, source_target_pairs={{4,0},{8,12},{5,1},{9,13},{6,2},{10,14},{7,3},{11,15},{20,16},{24,... | collective-permute-start | bytes 589832 | tf_op jit(solution)/shard_map/ppermute | solution.py:310
  50.6 3.2 %copy-start.7 = (bf16[256,1024]{1,0:T(8,128)(2,1)}, bf16[256,1024]{1,0:T(8,128)(2,1)S(1)}, u32[]{:S(2)}) copy-start(bf16[256,1024]{1,0:T(8,128)(2,1)S(1)} %convolution_convert_fusion.12) | copy-start | bytes 1572868
  50.9 32.2 %collective-permute-start.23 = (bf16[160,1152]{1,0:T(8,128)(2,1)S(1)}, bf16[160,1152]{1,0:T(8,128)(2,1)S(1)}, u32[]{:S(2)}, u32[]{:S(2)}) collective-permute-start(bf16[160,1152]{1,0:T(8,128)(2,1)S(1)} %convolution_convert_fusion.6), channel_id=1, source_target_pairs={{4,8},{8,4},{5,9},{9,5},{6,10},{10,6},{7,11},{11,7},{20,24},{24,20... | collective-permute-start | bytes 1105928 | tf_op jit(solution)/shard_map/ppermute | solution.py:310
  53.4 12.8 %copy-start.4 = (bf16[1,128,128]{2,1,0:T(8,128)(2,1)S(1)}, bf16[1,128,128]{2,1,0:T(8,128)(2,1)}, u32[]{:S(2)}) copy-start(bf16[1,128,128]{2,1,0:T(8,128)(2,1)} %param.11) | copy-start | bytes 98308
  54.0 15.1 %collective-permute-start.17 = (bf16[128,896]{1,0:T(8,128)(2,1)S(1)}, bf16[128,896]{1,0:T(8,128)(2,1)}, u32[]{:S(2)}, u32[]{:S(2)}) collective-permute-start(bf16[128,896]{1,0:T(8,128)(2,1)S(1)} %convolution_convert_fusion.24), channel_id=1, source_target_pairs={{0,4},{12,8},{1,5},{13,9},{2,6},{14,10},{3,7},{15,11},{16,20},{28,... | collective-permute-start | bytes 688136 | tf_op jit(solution)/shard_map/ppermute | solution.py:310
  67.3 18.6 %collective-permute-start.22 = (bf16[128,1024]{1,0:T(8,128)(2,1)S(1)}, bf16[128,1024]{1,0:T(8,128)(2,1)S(1)}, u32[]{:S(2)}, u32[]{:S(2)}) collective-permute-start(bf16[128,1024]{1,0:T(8,128)(2,1)S(1)} %convolution_convert_fusion.19), channel_id=1, source_target_pairs={{4,0},{8,12},{5,1},{9,13},{6,2},{10,14},{7,3},{11,15},{20,16},{24,... | collective-permute-start | bytes 786440 | tf_op jit(solution)/shard_map/ppermute | solution.py:310
  70.3 17.9 %collective-permute-start.25 = (bf16[160,896]{1,0:T(8,128)(2,1)S(1)}, bf16[160,896]{1,0:T(8,128)(2,1)S(1)}, u32[]{:S(2)}, u32[]{:S(2)}) collective-permute-start(bf16[160,896]{1,0:T(8,128)(2,1)S(1)} %convolution_convert_fusion.16), channel_id=1, source_target_pairs={{4,8},{8,4},{5,9},{9,5},{6,10},{10,6},{7,11},{11,7},{20,24},{24,20... | collective-permute-start | bytes 860168 | tf_op jit(solution)/shard_map/ppermute | solution.py:310
  71.0 3.7 %collective-permute-start.18 = (bf16[8,128]{1,0:T(8,128)(2,1)S(1)}, bf16[8,128]{1,0:T(8,128)(2,1)S(1)}, u32[]{:S(2)}, u32[]{:S(2)}) collective-permute-start(bf16[8,128]{1,0:T(8,128)(2,1)S(1)} %slice_maximum_fusion), channel_id=1, source_target_pairs={{0,2},{2,0},{1,3},{3,1},{4,6},{6,4},{5,7},{7,5},{8,10},{10,8},{9,1... | collective-permute-start | bytes 6152 | tf_op jit(solution)/shard_map/ppermute | solution.py:27
  74.6 7.2 %collective-permute-start.19 = (bf16[8,128]{1,0:T(8,128)(2,1)S(1)}, bf16[8,128]{1,0:T(8,128)(2,1)S(1)}, u32[]{:S(2)}, u32[]{:S(2)}) collective-permute-start(bf16[8,128]{1,0:T(8,128)(2,1)S(1)} %max.7), channel_id=1, source_target_pairs={{4,0},{8,12},{5,1},{9,13},{6,2},{10,14},{7,3},{11,15},{20,16},{24,... | collective-permute-start | bytes 6152 | tf_op jit(solution)/shard_map/ppermute | solution.py:316
  84.5 3.7 %copy-start.6 = (bf16[256,896]{1,0:T(8,128)(2,1)S(1)}, bf16[256,896]{1,0:T(8,128)(2,1)}, u32[]{:S(2)}) copy-start(bf16[256,896]{1,0:T(8,128)(2,1)} %convolution_convert_fusion.13) | copy-start | bytes 1376260
  84.5 8.7 %collective-permute-start.24 = (bf16[128,1152]{1,0:T(8,128)(2,1)S(1)}, bf16[128,1152]{1,0:T(8,128)(2,1)S(1)}, u32[]{:S(2)}, u32[]{:S(2)}) collective-permute-start(bf16[128,1152]{1,0:T(8,128)(2,1)S(1)} %convolution_convert_fusion.9), channel_id=1, source_target_pairs={{4,0},{8,12},{5,1},{9,13},{6,2},{10,14},{7,3},{11,15},{20,16},{24,... | collective-permute-start | bytes 884744 | tf_op jit(solution)/shard_map/ppermute | solution.py:310
  88.2 5.0 %copy-start.8 = (bf16[256,1152]{1,0:T(8,128)(2,1)S(1)}, bf16[256,1152]{1,0:T(8,128)(2,1)}, u32[]{:S(2)}) copy-start(bf16[256,1152]{1,0:T(8,128)(2,1)} %convolution_convert_fusion.5) | copy-start | bytes 1769476
  88.5 7.9 %collective-permute-start.26 = (bf16[128,896]{1,0:T(8,128)(2,1)S(1)}, bf16[128,896]{1,0:T(8,128)(2,1)S(1)}, u32[]{:S(2)}, u32[]{:S(2)}) collective-permute-start(bf16[128,896]{1,0:T(8,128)(2,1)S(1)} %convolution_convert_fusion.27), channel_id=1, source_target_pairs={{4,0},{8,12},{5,1},{9,13},{6,2},{10,14},{7,3},{11,15},{20,16},{24,... | collective-permute-start | bytes 688136 | tf_op jit(solution)/shard_map/ppermute | solution.py:310
  94.5 3.2 %copy-start.2 = (bf16[1,3,64,128]{3,2,1,0:T(8,128)(2,1)S(1)}, bf16[1,3,64,128]{3,2,1,0:T(8,128)(2,1)}, u32[]{:S(2)}) copy-start(bf16[1,3,64,128]{3,2,1,0:T(8,128)(2,1)} %refs_1_.1) | copy-start | bytes 147460
  94.5 3.2 %copy-start.3 = (s32[1,3,64]{2,0,1:T(1,128)S(1)}, s32[1,3,64]{2,0,1:T(1,128)}, u32[]{:S(2)}) copy-start(s32[1,3,64]{2,0,1:T(1,128)} %param.9) | copy-start | bytes 2308

commit v10 on v8

--- a/solution.py
+++ b/solution.py
@@ -5,10 +5,14 @@
 from jax.experimental.pallas import tpu as pltpu
 from jax.sharding import PartitionSpec as P
 
-SHARES = (1, 3, 8, 9, 11)
-FULL_PIECES = 2
+SHARES = (2, 7, 11, 8, 4)
+FULL_PIECES = 1
+ORDER = (
+    (0, 0), (0, 1), (1, 0), (0, 2), (2, 0), (1, 1), (0, 3), (3, 0), (1, 2), (2, 1), (1, 3), (2, 2),
+    (0, 4), (3, 1), (1, 4), (2, 3), (2, 4), (3, 2), (3, 3), (3, 4),
+)
 KERNEL_VMEM = 16 * 1024 * 1024
-ROOM_SIXTEENTHS = 12
+ROOM_SIXTEENTHS = 11
 
 
 def route(axis, apart):
@@ -213,27 +217,11 @@
     return evaluated(coeffs, evaluation)
 
 
-def sequence(pieces, levels):
-    def turn(at):
-        level, piece = at
-        if piece < FULL_PIECES:
-            if level == 0:
-                return piece
-            late = 2 if level == levels and piece else 0
-            return 3 * level + 1.5 * piece + late
-        if level == 0:
-            return 3.5 if piece == 2 else 6.5 if piece == 3 else 11.02 + 3.05 * (piece - 4)
-        late = 3 if level == levels else 0
-        return 3 * level + 5 + 3.05 * (piece - 2) + late
-
-    return sorted(
-        [(level, piece) for level in range(levels + 1) for piece in range(pieces)], key=turn
-    )
-
-
 def local(traces, sampling, skeleton, compress, evaluation):
     hops = all_hops()
     levels = len(hops)
+    if levels != max(level for level, _ in ORDER):
+        return full_width(traces, sampling[0], skeleton[0], compress[0], evaluation[0])
     wide = lax.axis_size("sub").bit_length() - 1
     rank = skeleton.shape[-1]
     room = rank * ROOM_SIXTEENTHS // 16
@@ -249,7 +237,7 @@
 
     inputs, partners, theirs, done = {}, {}, {}, [None] * pieces
     previous, known = None, None
-    for level, piece in sequence(pieces, levels):
+    for level, piece in ORDER:
         count = starts[piece + 1] - starts[piece]
         if level == 0:
             own = coeffs
@@ -268,7 +256,7 @@
                 matrix = small[level - 1]
             own = times(matrix, value)
         if level == levels:
-            done[piece] = evaluated(own, evaluation)
+            done[piece] = previous = evaluated(own, evaluation)
             continue
         outgoing = own
         if compact(level, piece):

time: 69.3 us -> 63.7 us (0.919)
  starting transfers between devices: 31.9 us -> 23.5 us
  waiting for transfers between devices: 18.3 us -> 20.2 us
  matrix products: 15.1 us -> 16.1 us
    ppermute x16, starting transfers between devices: 31.9 us -> 23.5 us  [from_partner(): return lax.ppermute(block, hop[0], route(*hop))]
    ppermute x16, waiting for transfers between devices: 18.3 us -> 20.2 us  [from_partner(): return lax.ppermute(block, hop[0], route(*hop))]
    dot_general x16 -> x18, matrix products: 4.26 us -> 5.27 us  [times(): jnp.dot(matrix, value, preferred_element_type=jnp.float32)]
  transfers between devices with their start and end apart: 16 -> 16, of which waited for: 7 -> 7; matrix products, arithmetic and copies ran while one was open for 21% -> 24% of each run, Pallas kernels for 0% -> 0%
where the time goes in v10:
time: 63.7 us; the launch traced here: 63.5 us
  starting transfers between devices  23.5 us (37%)
  waiting for transfers between devices  20.2 us (32%)
  matrix products  16.1 us (25%)
  Pallas kernels  2.05 us (3%)
  between operations  0.86 us (1%)
    ppermute x16, starting transfers between devices, from_partner(): return lax.ppermute(block, hop[0], route(*hop))  23.5 us
    ppermute x16, waiting for transfers between devices, from_partner(): return lax.ppermute(block, hop[0], route(*hop))  20.2 us
    dot_general x5, matrix products, evaluated(): jnp.einsum('ct,cp->tp', coeffs, evaluation, preferred_element_type=jnp.fl...  5.62 us
    dot_general x18, matrix products, times(): jnp.dot(matrix, value, preferred_element_type=jnp.float32)  5.27 us
    dot_general x4, matrix products, sampled(): jnp.einsum('pc,tp->ct', sampling, traces, preferred_element_type=jnp.floa...  4.74 us
    pallas_call x1, Pallas kernels, first(): pl.pallas_call(lambda *refs: first_kernel(wide, room, count, *refs), out_...  2.05 us
  transfers between devices with their start and end apart: 16, of which 7 were waited for; matrix products, arithmetic and copies ran while one was open for 24% of the time, Pallas kernels for 0%

profile of v10, /device:TPU:0, one launch (start us, length us, event | category | flops | bytes accessed | tf_op | source)
XLA Modules:
  0.0 63.5 jit_solution(1337332673180872368)
XLA Ops:
  0.0 2.0 %first.1 = (bf16[3,128,256]{2,1,0:T(8,128)(2,1)S(1)}, bf16[3,128,256]{2,1,0:T(8,128)(2,1)S(1)}, bf16[3,128,128]{2,1,0:T(8,128)(2,1)S(1)}, bf16[128,256]{1,0:T(8,128)(2,1)S(1)}) custom-call(s32[3,1,64]{2,1,0:T(1,128)} %bitcast.118, bf16[1,3,64,128]{3,2,1,0:T(8,128)(2,1)} %refs_1_.1, bf16[1,128,128]{2,1,0:T(8,128)(2,1)} %refs_2_.1, bf16[4096,128]{1,0:T(8,128)(2,1)} %refs_3_.1), custom_call_target="tpu_custom_call" | custom-call | flops 50000000 | bytes 600000 | tf_op jit(solution)/shard_map/first/pallas_call | solution.py:114
  2.1 3.0 %collective-permute-start.3 = (bf16[128,256]{1,0:T(8,128)(2,1)S(1)}, bf16[128,256]{1,0:T(8,128)(2,1)S(1)}, u32[]{:S(2)}, u32[]{:S(2)}) collective-permute-start(bf16[128,256]{1,0:T(8,128)(2,1)S(1)} %get-tuple-element.50), channel_id=1, source_target_pairs={{0,2},{2,0},{1,3},{3,1},{4,6},{6,4},{5,7},{7,5},{8,10},{10,8},{9,1... | collective-permute-start | bytes 196616 | tf_op jit(solution)/shard_map/ppermute | solution.py:29
  5.1 1.2 %convolution_convert_fusion.21 = bf16[128,896]{1,0:T(8,128)(2,1)S(1)} fusion(bf16[128,128]{1,0:T(8,128)(2,1)S(1)} %bitcast.111, bf16[4096,128]{1,0:T(8,128)(2,1)} %refs_3_.1), kind=kOutput, calls=%fused_computation.51 | convolution fusion | flops 29474816 | bytes 491520 | tf_op jit(solution)/shard_map/pc,tp->ct/dot_general | solution.py:188
  6.4 1.0 %collective-permute-done.3 = bf16[128,256]{1,0:T(8,128)(2,1)S(1)} collective-permute-done((bf16[128,256]{1,0:T(8,128)(2,1)S(1)}, bf16[128,256]{1,0:T(8,128)(2,1)S(1)}, u32[]{:S(2)}, u32[]{:S(2)}) %collective-permute-start.3) | collective-permute-done | bytes 65568 | tf_op jit(solution)/shard_map/ppermute | solution.py:29
  7.6 2.1 %collective-permute-start.4 = (bf16[128,384]{1,0:T(8,128)(2,1)S(1)}, bf16[128,384]{1,0:T(8,128)(2,1)S(1)}, u32[]{:S(2)}, u32[]{:S(2)}) collective-permute-start(bf16[128,384]{1,0:T(8,128)(2,1)S(1)} %pad_maximum_fusion.12), channel_id=1, source_target_pairs={{0,4},{4,0},{8,12},{12,8},{1,5},{5,1},{9,13},{13,9},{2,6},{6,2},{1... | collective-permute-start | bytes 294920 | tf_op jit(solution)/shard_map/ppermute | solution.py:29
  9.7 1.3 %convolution_convert_fusion.9 = bf16[128,1408]{1,0:T(8,128)(2,1)S(1)} fusion(bf16[128,128]{1,0:T(8,128)(2,1)S(1)} %bitcast.112, bf16[4096,128]{1,0:T(8,128)(2,1)} %refs_3_.1), kind=kOutput, calls=%fused_computation.34 | convolution fusion | flops 46317568 | bytes 753664 | tf_op jit(solution)/shard_map/pc,tp->ct/dot_general | solution.py:188
  10.9 2.0 %collective-permute-start.7 = (bf16[128,1408]{1,0:T(8,128)(2,1)S(1)}, bf16[128,1408]{1,0:T(8,128)(2,1)S(1)}, u32[]{:S(2)}, u32[]{:S(2)}) collective-permute-start(bf16[128,1408]{1,0:T(8,128)(2,1)S(1)} %convolution_convert_fusion.9), channel_id=1, source_target_pairs={{0,2},{2,0},{1,3},{3,1},{4,6},{6,4},{5,7},{7,5},{8,10},{10,8},{9,1... | collective-permute-start | bytes 1081352 | tf_op jit(solution)/shard_map/ppermute | solution.py:29
  13.3 2.6 %collective-permute-start.5 = (bf16[128,384]{1,0:T(8,128)(2,1)S(1)}, bf16[128,384]{1,0:T(8,128)(2,1)S(1)}, u32[]{:S(2)}, u32[]{:S(2)}) collective-permute-start(bf16[128,384]{1,0:T(8,128)(2,1)S(1)} %pad_maximum_fusion.13), channel_id=1, source_target_pairs={{0,8},{8,0},{4,12},{12,4},{1,9},{9,1},{5,13},{13,5},{2,10},{10,2},... | collective-permute-start | bytes 294920 | tf_op jit(solution)/shard_map/ppermute | solution.py:29
  16.5 1.4 %collective-permute-start.10 = (bf16[88,896]{1,0:T(8,128)(2,1)S(1)}, bf16[88,896]{1,0:T(8,128)(2,1)S(1)}, u32[]{:S(2)}, u32[]{:S(2)}) collective-permute-start(bf16[88,896]{1,0:T(8,128)(2,1)S(1)} %convolution_convert_fusion.25), channel_id=1, source_target_pairs={{0,4},{4,0},{8,12},{12,8},{1,5},{5,1},{9,13},{13,9},{2,6},{6,2},{1... | collective-permute-start | bytes 473096 | tf_op jit(solution)/shard_map/ppermute | solution.py:29
  18.0 1.2 %convolution_convert_fusion.16 = bf16[128,1024]{1,0:T(8,128)(2,1)S(1)} fusion(bf16[128,128]{1,0:T(8,128)(2,1)S(1)} %bitcast.113, bf16[4096,128]{1,0:T(8,128)(2,1)} %refs_3_.1), kind=kOutput, calls=%fused_computation.46 | convolution fusion | flops 33685504 | bytes 557056 | tf_op jit(solution)/shard_map/pc,tp->ct/dot_general | solution.py:188
  19.2 2.0 %collective-permute-start.9 = (bf16[128,1024]{1,0:T(8,128)(2,1)S(1)}, bf16[128,1024]{1,0:T(8,128)(2,1)S(1)}, u32[]{:S(2)}, u32[]{:S(2)}) collective-permute-start(bf16[128,1024]{1,0:T(8,128)(2,1)S(1)} %convolution_convert_fusion.16), channel_id=1, source_target_pairs={{0,2},{2,0},{1,3},{3,1},{4,6},{6,4},{5,7},{7,5},{8,10},{10,8},{9,1... | collective-permute-start | bytes 786440 | tf_op jit(solution)/shard_map/ppermute | solution.py:29
  21.3 1.0 %constant_dynamic-update-slice_fusion.4 = bf16[4096,128]{1,0:T(8,128)(2,1)} fusion(bf16[1,128,128]{2,1,0:T(8,128)(2,1)S(1)} %copy-done.4, bf16[128,256]{1,0:T(8,128)(2,1)S(1)} %slice.171, bf16[128,256]{1,0:T(8,128)(2,1)S(1)} %convolution_convert_fusion.35, bf16[3,128,256]{2,1,0:T(8,128)(2,1)S(1)} %get-tuple-element.49), kind=kOutput, calls=%fused_computation.176 | convolution fusion | flops 25493504 | bytes 294912 | tf_op jit(solution)/shard_map/ct,cp->tp/dot_general | solution.py:194
  22.7 1.7 %collective-permute-start.8 = (bf16[88,1408]{1,0:T(8,128)(2,1)S(1)}, bf16[88,1408]{1,0:T(8,128)(2,1)S(1)}, u32[]{:S(2)}, u32[]{:S(2)}) collective-permute-start(bf16[88,1408]{1,0:T(8,128)(2,1)S(1)} %convolution_convert_fusion.11), channel_id=1, source_target_pairs={{0,4},{4,0},{8,12},{12,8},{1,5},{5,1},{9,13},{13,9},{2,6},{6,2},{1... | collective-permute-start | bytes 743432 | tf_op jit(solution)/shard_map/ppermute | solution.py:29
  24.5 0.9 %convolution_convert_fusion.19 = bf16[128,896]{1,0:T(8,128)(2,1)} fusion(bf16[88,896]{1,0:T(8,128)(2,1)S(1)} %collective-permute-done.10, bf16[128,896]{1,0:T(8,128)(2,1)S(1)} %convolution_convert_fusion.20, bf16[3,128,256]{2,1,0:T(8,128)(2,1)S(1)} %get-tuple-element.58), kind=kOutput, calls=%fused_computation.49 | convolution fusion | flops 60440576 | bytes 681984 | tf_op jit(solution)/shard_map/dot_general | solution.py:184
  25.6 2.7 %collective-permute-start.12 = (bf16[88,896]{1,0:T(8,128)(2,1)S(1)}, bf16[88,896]{1,0:T(8,128)(2,1)S(1)}, u32[]{:S(2)}, u32[]{:S(2)}) collective-permute-start(bf16[88,896]{1,0:T(8,128)(2,1)S(1)} %convolution_convert_fusion.24), channel_id=1, source_target_pairs={{0,8},{8,0},{4,12},{12,4},{1,9},{9,1},{5,13},{13,5},{2,10},{10,2},... | collective-permute-start | bytes 473096 | tf_op jit(solution)/shard_map/ppermute | solution.py:29
  29.4 6.6 %collective-permute-done.8 = bf16[88,1408]{1,0:T(8,128)(2,1)S(1)} collective-permute-done((bf16[88,1408]{1,0:T(8,128)(2,1)S(1)}, bf16[88,1408]{1,0:T(8,128)(2,1)S(1)}, u32[]{:S(2)}, u32[]{:S(2)}) %collective-permute-start.8) | collective-permute-done | bytes 247840 | tf_op jit(solution)/shard_map/ppermute | solution.py:29
  36.3 0.4 collective-permute-start.17
  36.7 1.1 %convolution_convert_fusion.30 = bf16[128,512]{1,0:T(8,128)(2,1)S(1)} fusion(bf16[128,128]{1,0:T(8,128)(2,1)S(1)} %bitcast.114, bf16[4096,128]{1,0:T(8,128)(2,1)} %refs_3_.1), kind=kOutput, calls=%fused_computation.60 | convolution fusion | flops 16842752 | bytes 294912 | tf_op jit(solution)/shard_map/pc,tp->ct/dot_general | solution.py:188
  37.8 1.0 %collective-permute-start.11 = (bf16[128,512]{1,0:T(8,128)(2,1)S(1)}, bf16[128,512]{1,0:T(8,128)(2,1)S(1)}, u32[]{:S(2)}, u32[]{:S(2)}) collective-permute-start(bf16[128,512]{1,0:T(8,128)(2,1)S(1)} %convolution_convert_fusion.30), channel_id=1, source_target_pairs={{0,2},{2,0},{1,3},{3,1},{4,6},{6,4},{5,7},{7,5},{8,10},{10,8},{9,1... | collective-permute-start | bytes 393224 | tf_op jit(solution)/shard_map/ppermute | solution.py:29
  38.8 1.2 %constant_dynamic-update-slice_fusion.3 = bf16[4096,128]{1,0:T(8,128)(2,1)} fusion(bf16[4096,128]{1,0:T(8,128)(2,1)} %constant_dynamic-update-slice_fusion.4, bf16[1,128,128]{2,1,0:T(8,128)(2,1)S(1)} %copy-done.4, bf16[88,896]{1,0:T(8,128)(2,1)S(1)} %collective-permute-done.12, bf16[128,896]{1,0:T(8,128)(2,1)S(1)} %copy-done.5, ...), kind=kOutput, calls=%fused_computation.175 | convolution fusion | flops 89915392 | bytes 714752 | tf_op jit(solution)/shard_map/ct,cp->tp/dot_general | solution.py:194
  40.0 1.0 %convolution_convert_fusion.7 = bf16[128,1408]{1,0:T(8,128)(2,1)} fusion(bf16[88,1408]{1,0:T(8,128)(2,1)S(1)} %collective-permute-done.8, bf16[128,1408]{1,0:T(8,128)(2,1)S(1)} %convolution_convert_fusion.8, bf16[3,128,256]{2,1,0:T(8,128)(2,1)S(1)} %get-tuple-element.58), kind=kOutput, calls=%fused_computation.32 | convolution fusion | flops 94978048 | bytes 1034240 | tf_op jit(solution)/shard_map/dot_general | solution.py:184
  41.0 1.8 %collective-permute-done.11 = bf16[128,512]{1,0:T(8,128)(2,1)S(1)} collective-permute-done((bf16[128,512]{1,0:T(8,128)(2,1)S(1)}, bf16[128,512]{1,0:T(8,128)(2,1)S(1)}, u32[]{:S(2)}, u32[]{:S(2)}) %collective-permute-start.11) | collective-permute-done | bytes 131104 | tf_op jit(solution)/shard_map/ppermute | solution.py:29
  43.0 2.5 %collective-permute-start.13 = (bf16[88,512]{1,0:T(8,128)(2,1)S(1)}, bf16[88,512]{1,0:T(8,128)(2,1)S(1)}, u32[]{:S(2)}, u32[]{:S(2)}) collective-permute-start(bf16[88,512]{1,0:T(8,128)(2,1)S(1)} %convolution_convert_fusion.32), channel_id=1, source_target_pairs={{0,4},{4,0},{8,12},{12,8},{1,5},{5,1},{9,13},{13,9},{2,6},{6,2},{1... | collective-permute-start | bytes 270344 | tf_op jit(solution)/shard_map/ppermute | solution.py:29
  46.4 4.8 %collective-permute-done.13 = bf16[88,512]{1,0:T(8,128)(2,1)S(1)} collective-permute-done((bf16[88,512]{1,0:T(8,128)(2,1)S(1)}, bf16[88,512]{1,0:T(8,128)(2,1)S(1)}, u32[]{:S(2)}, u32[]{:S(2)}) %collective-permute-start.13) | collective-permute-done | bytes 90144 | tf_op jit(solution)/shard_map/ppermute | solution.py:29
  51.6 1.8 %collective-permute-done.17 = bf16[88,1408]{1,0:T(8,128)(2,1)S(1)} collective-permute-done((bf16[88,1408]{1,0:T(8,128)(2,1)S(1)}, bf16[88,1408]{1,0:T(8,128)(2,1)S(1)}, u32[]{:S(2)}, u32[]{:S(2)}) %collective-permute-start.17) | collective-permute-done | bytes 247840 | tf_op jit(solution)/shard_map/ppermute | solution.py:29
  53.5 1.2 %constant_dynamic-update-slice_fusion.2 = bf16[4096,128]{1,0:T(8,128)(2,1)} fusion(bf16[4096,128]{1,0:T(8,128)(2,1)} %constant_dynamic-update-slice_fusion.3, bf16[1,128,128]{2,1,0:T(8,128)(2,1)S(1)} %copy-done.4, bf16[88,1408]{1,0:T(8,128)(2,1)S(1)} %collective-permute-done.17, bf16[128,1408]{1,0:T(8,128)(2,1)S(1)} %copy-done.6, ...), kind=kOutput, calls=%fused_computation.174 | convolution fusion | flops 141295616 | bytes 1067008 | tf_op jit(solution)/shard_map/ct,cp->tp/dot_general | solution.py:194
  54.7 1.8 %collective-permute-done.16 = bf16[88,1024]{1,0:T(8,128)(2,1)S(1)} collective-permute-done((bf16[88,1024]{1,0:T(8,128)(2,1)S(1)}, bf16[88,1024]{1,0:T(8,128)(2,1)S(1)}, u32[]{:S(2)}, u32[]{:S(2)}) %collective-permute-start.16) | collective-permute-done | bytes 180256 | tf_op jit(solution)/shard_map/ppermute | solution.py:29
  56.5 1.2 %constant_dynamic-update-slice_fusion.1 = bf16[4096,128]{1,0:T(8,128)(2,1)} fusion(bf16[4096,128]{1,0:T(8,128)(2,1)} %constant_dynamic-update-slice_fusion.2, bf16[1,128,128]{2,1,0:T(8,128)(2,1)S(1)} %copy-done.4, bf16[88,1024]{1,0:T(8,128)(2,1)S(1)} %collective-permute-done.16, bf16[128,1024]{1,0:T(8,128)(2,1)S(1)} %convolution_convert_fusion.14, ...), kind=kOutput, calls=%fused_computation.173 | convolution fusion | flops 102760448 | bytes 802816 | tf_op jit(solution)/shard_map/ct,cp->tp/dot_general | solution.py:194
  57.7 1.1 %constant_dynamic-update-slice_fusion = bf16[4096,128]{1,0:T(8,128)(2,1)} fusion(bf16[4096,128]{1,0:T(8,128)(2,1)} %constant_dynamic-update-slice_fusion.1, bf16[1,128,128]{2,1,0:T(8,128)(2,1)S(1)} %copy-done.4, bf16[88,512]{1,0:T(8,128)(2,1)S(1)} %collective-permute-done.15, bf16[128,512]{1,0:T(8,128)(2,1)S(1)} %convolution_convert_fusion.28, ...), kind=kOutput, calls=%fused_computation.172 | convolution fusion | flops 51380224 | bytes 450560 | tf_op jit(solution)/shard_map/ct,cp->tp/dot_general | solution.py:194
  58.8 1.3 %collective-permute-start.18 = (bf16[8,64]{1,0:T(8,128)(2,1)S(1)}, bf16[8,64]{1,0:T(8,128)(2,1)S(1)}, u32[]{:S(2)}, u32[]{:S(2)}) collective-permute-start(bf16[8,64]{1,0:T(8,128)(2,1)S(1)} %slice_maximum_fusion), channel_id=1, source_target_pairs={{0,2},{2,0},{1,3},{3,1},{4,6},{6,4},{5,7},{7,5},{8,10},{10,8},{9,1... | collective-permute-start | bytes 3080 | tf_op jit(solution)/shard_map/ppermute | solution.py:29
  60.1 2.3 %collective-permute-done.18 = bf16[8,64]{1,0:T(8,128)(2,1)S(1)} collective-permute-done((bf16[8,64]{1,0:T(8,128)(2,1)S(1)}, bf16[8,64]{1,0:T(8,128)(2,1)S(1)}, u32[]{:S(2)}, u32[]{:S(2)}) %collective-permute-start.18) | collective-permute-done | bytes 1056 | tf_op jit(solution)/shard_map/ppermute | solution.py:29
  62.4 0.5 slice.173
  (56 shorter events, 4.8 us)
Async XLA Ops:
  0.0 5.1 %copy-start = (bf16[1,128,128]{2,1,0:T(8,128)(2,1)S(1)}, bf16[1,128,128]{2,1,0:T(8,128)(2,1)}, u32[]{:S(2)}) copy-start(bf16[1,128,128]{2,1,0:T(8,128)(2,1)} %refs_2_.1) | copy-start | bytes 98308
  2.1 5.3 %collective-permute-start.3 = (bf16[128,256]{1,0:T(8,128)(2,1)S(1)}, bf16[128,256]{1,0:T(8,128)(2,1)S(1)}, u32[]{:S(2)}, u32[]{:S(2)}) collective-permute-start(bf16[128,256]{1,0:T(8,128)(2,1)S(1)} %get-tuple-element.50), channel_id=1, source_target_pairs={{0,2},{2,0},{1,3},{3,1},{4,6},{6,4},{5,7},{7,5},{8,10},{10,8},{9,1... | collective-permute-start | bytes 196616 | tf_op jit(solution)/shard_map/ppermute | solution.py:29
  6.3 9.8 %collective-permute-start.6 = (bf16[128,896]{1,0:T(8,128)(2,1)S(1)}, bf16[128,896]{1,0:T(8,128)(2,1)S(1)}, u32[]{:S(2)}, u32[]{:S(2)}) collective-permute-start(bf16[128,896]{1,0:T(8,128)(2,1)S(1)} %convolution_convert_fusion.21), channel_id=1, source_target_pairs={{0,2},{2,0},{1,3},{3,1},{4,6},{6,4},{5,7},{7,5},{8,10},{10,8},{9,1... | collective-permute-start | bytes 688136 | tf_op jit(solution)/shard_map/ppermute | solution.py:29
  7.6 5.3 %collective-permute-start.4 = (bf16[128,384]{1,0:T(8,128)(2,1)S(1)}, bf16[128,384]{1,0:T(8,128)(2,1)S(1)}, u32[]{:S(2)}, u32[]{:S(2)}) collective-permute-start(bf16[128,384]{1,0:T(8,128)(2,1)S(1)} %pad_maximum_fusion.12), channel_id=1, source_target_pairs={{0,4},{4,0},{8,12},{12,8},{1,5},{5,1},{9,13},{13,9},{2,6},{6,2},{1... | collective-permute-start | bytes 294920 | tf_op jit(solution)/shard_map/ppermute | solution.py:29
  10.9 11.5 %collective-permute-start.7 = (bf16[128,1408]{1,0:T(8,128)(2,1)S(1)}, bf16[128,1408]{1,0:T(8,128)(2,1)S(1)}, u32[]{:S(2)}, u32[]{:S(2)}) collective-permute-start(bf16[128,1408]{1,0:T(8,128)(2,1)S(1)} %convolution_convert_fusion.9), channel_id=1, source_target_pairs={{0,2},{2,0},{1,3},{3,1},{4,6},{6,4},{5,7},{7,5},{8,10},{10,8},{9,1... | collective-permute-start | bytes 1081352 | tf_op jit(solution)/shard_map/ppermute | solution.py:29
  13.3 7.9 %collective-permute-start.5 = (bf16[128,384]{1,0:T(8,128)(2,1)S(1)}, bf16[128,384]{1,0:T(8,128)(2,1)S(1)}, u32[]{:S(2)}, u32[]{:S(2)}) collective-permute-start(bf16[128,384]{1,0:T(8,128)(2,1)S(1)} %pad_maximum_fusion.13), channel_id=1, source_target_pairs={{0,8},{8,0},{4,12},{12,4},{1,9},{9,1},{5,13},{13,5},{2,10},{10,2},... | collective-permute-start | bytes 294920 | tf_op jit(solution)/shard_map/ppermute | solution.py:29
  16.3 5.0 %copy-start.4 = (bf16[1,128,128]{2,1,0:T(8,128)(2,1)S(1)}, bf16[1,128,128]{2,1,0:T(8,128)(2,1)}, u32[]{:S(2)}) copy-start(bf16[1,128,128]{2,1,0:T(8,128)(2,1)} %param.11) | copy-start | bytes 98308
  16.5 8.0 %collective-permute-start.10 = (bf16[88,896]{1,0:T(8,128)(2,1)S(1)}, bf16[88,896]{1,0:T(8,128)(2,1)S(1)}, u32[]{:S(2)}, u32[]{:S(2)}) collective-permute-start(bf16[88,896]{1,0:T(8,128)(2,1)S(1)} %convolution_convert_fusion.25), channel_id=1, source_target_pairs={{0,4},{4,0},{8,12},{12,8},{1,5},{5,1},{9,13},{13,9},{2,6},{6,2},{1... | collective-permute-start | bytes 473096 | tf_op jit(solution)/shard_map/ppermute | solution.py:29
  19.2 9.4 %collective-permute-start.9 = (bf16[128,1024]{1,0:T(8,128)(2,1)S(1)}, bf16[128,1024]{1,0:T(8,128)(2,1)S(1)}, u32[]{:S(2)}, u32[]{:S(2)}) collective-permute-start(bf16[128,1024]{1,0:T(8,128)(2,1)S(1)} %convolution_convert_fusion.16), channel_id=1, source_target_pairs={{0,2},{2,0},{1,3},{3,1},{4,6},{6,4},{5,7},{7,5},{8,10},{10,8},{9,1... | collective-permute-start | bytes 786440 | tf_op jit(solution)/shard_map/ppermute | solution.py:29
  22.7 13.3 %collective-permute-start.8 = (bf16[88,1408]{1,0:T(8,128)(2,1)S(1)}, bf16[88,1408]{1,0:T(8,128)(2,1)S(1)}, u32[]{:S(2)}, u32[]{:S(2)}) collective-permute-start(bf16[88,1408]{1,0:T(8,128)(2,1)S(1)} %convolution_convert_fusion.11), channel_id=1, source_target_pairs={{0,4},{4,0},{8,12},{12,8},{1,5},{5,1},{9,13},{13,9},{2,6},{6,2},{1... | collective-permute-start | bytes 743432 | tf_op jit(solution)/shard_map/ppermute | solution.py:29
  25.6 13.2 %collective-permute-start.12 = (bf16[88,896]{1,0:T(8,128)(2,1)S(1)}, bf16[88,896]{1,0:T(8,128)(2,1)S(1)}, u32[]{:S(2)}, u32[]{:S(2)}) collective-permute-start(bf16[88,896]{1,0:T(8,128)(2,1)S(1)} %convolution_convert_fusion.24), channel_id=1, source_target_pairs={{0,8},{8,0},{4,12},{12,4},{1,9},{9,1},{5,13},{13,5},{2,10},{10,2},... | collective-permute-start | bytes 473096 | tf_op jit(solution)/shard_map/ppermute | solution.py:29
  28.8 16.9 %collective-permute-start.14 = (bf16[88,1024]{1,0:T(8,128)(2,1)S(1)}, bf16[88,1024]{1,0:T(8,128)(2,1)S(1)}, u32[]{:S(2)}, u32[]{:S(2)}) collective-permute-start(bf16[88,1024]{1,0:T(8,128)(2,1)S(1)} %convolution_convert_fusion.23), channel_id=1, source_target_pairs={{0,4},{4,0},{8,12},{12,8},{1,5},{5,1},{9,13},{13,9},{2,6},{6,2},{1... | collective-permute-start | bytes 540680 | tf_op jit(solution)/shard_map/ppermute | solution.py:29
  29.4 9.4 %copy-start.5 = (bf16[128,896]{1,0:T(8,128)(2,1)S(1)}, bf16[128,896]{1,0:T(8,128)(2,1)}, u32[]{:S(2)}) copy-start(bf16[128,896]{1,0:T(8,128)(2,1)} %convolution_convert_fusion.19) | copy-start | bytes 688132
  36.3 17.2 %collective-permute-start.17 = (bf16[88,1408]{1,0:T(8,128)(2,1)S(1)}, bf16[88,1408]{1,0:T(8,128)(2,1)S(1)}, u32[]{:S(2)}, u32[]{:S(2)}) collective-permute-start(bf16[88,1408]{1,0:T(8,128)(2,1)S(1)} %convolution_convert_fusion.10), channel_id=1, source_target_pairs={{0,8},{8,0},{4,12},{12,4},{1,9},{9,1},{5,13},{13,5},{2,10},{10,2},... | collective-permute-start | bytes 743432 | tf_op jit(solution)/shard_map/ppermute | solution.py:29
  37.8 5.0 %collective-permute-start.11 = (bf16[128,512]{1,0:T(8,128)(2,1)S(1)}, bf16[128,512]{1,0:T(8,128)(2,1)S(1)}, u32[]{:S(2)}, u32[]{:S(2)}) collective-permute-start(bf16[128,512]{1,0:T(8,128)(2,1)S(1)} %convolution_convert_fusion.30), channel_id=1, source_target_pairs={{0,2},{2,0},{1,3},{3,1},{4,6},{6,4},{5,7},{7,5},{8,10},{10,8},{9,1... | collective-permute-start | bytes 393224 | tf_op jit(solution)/shard_map/ppermute | solution.py:29
  43.0 8.2 %collective-permute-start.13 = (bf16[88,512]{1,0:T(8,128)(2,1)S(1)}, bf16[88,512]{1,0:T(8,128)(2,1)S(1)}, u32[]{:S(2)}, u32[]{:S(2)}) collective-permute-start(bf16[88,512]{1,0:T(8,128)(2,1)S(1)} %convolution_convert_fusion.32), channel_id=1, source_target_pairs={{0,4},{4,0},{8,12},{12,8},{1,5},{5,1},{9,13},{13,9},{2,6},{6,2},{1... | collective-permute-start | bytes 270344 | tf_op jit(solution)/shard_map/ppermute | solution.py:29
  46.2 7.3 %copy-start.6 = (bf16[128,1408]{1,0:T(8,128)(2,1)S(1)}, bf16[128,1408]{1,0:T(8,128)(2,1)}, u32[]{:S(2)}) copy-start(bf16[128,1408]{1,0:T(8,128)(2,1)} %convolution_convert_fusion.7) | copy-start | bytes 1081348
  46.2 10.3 %collective-permute-start.16 = (bf16[88,1024]{1,0:T(8,128)(2,1)S(1)}, bf16[88,1024]{1,0:T(8,128)(2,1)S(1)}, u32[]{:S(2)}, u32[]{:S(2)}) collective-permute-start(bf16[88,1024]{1,0:T(8,128)(2,1)S(1)} %convolution_convert_fusion.22), channel_id=1, source_target_pairs={{0,8},{8,0},{4,12},{12,4},{1,9},{9,1},{5,13},{13,5},{2,10},{10,2},... | collective-permute-start | bytes 540680 | tf_op jit(solution)/shard_map/ppermute | solution.py:29
  51.4 6.3 %collective-permute-start.15 = (bf16[88,512]{1,0:T(8,128)(2,1)S(1)}, bf16[88,512]{1,0:T(8,128)(2,1)S(1)}, u32[]{:S(2)}, u32[]{:S(2)}) collective-permute-start(bf16[88,512]{1,0:T(8,128)(2,1)S(1)} %convolution_convert_fusion.31), channel_id=1, source_target_pairs={{0,8},{8,0},{4,12},{12,4},{1,9},{9,1},{5,13},{13,5},{2,10},{10,2},... | collective-permute-start | bytes 270344 | tf_op jit(solution)/shard_map/ppermute | solution.py:29
  57.7 5.7 %copy-start.2 = (bf16[1,3,64,128]{3,2,1,0:T(8,128)(2,1)S(1)}, bf16[1,3,64,128]{3,2,1,0:T(8,128)(2,1)}, u32[]{:S(2)}) copy-start(bf16[1,3,64,128]{3,2,1,0:T(8,128)(2,1)} %refs_1_.1) | copy-start | bytes 147460
  57.7 5.8 %copy-start.3 = (s32[1,3,64]{2,0,1:T(1,128)S(1)}, s32[1,3,64]{2,0,1:T(1,128)}, u32[]{:S(2)}) copy-start(s32[1,3,64]{2,0,1:T(1,128)} %param.9) | copy-start | bytes 2308
  58.8 3.6 %collective-permute-start.18 = (bf16[8,64]{1,0:T(8,128)(2,1)S(1)}, bf16[8,64]{1,0:T(8,128)(2,1)S(1)}, u32[]{:S(2)}, u32[]{:S(2)}) collective-permute-start(bf16[8,64]{1,0:T(8,128)(2,1)S(1)} %slice_maximum_fusion), channel_id=1, source_target_pairs={{0,2},{2,0},{1,3},{3,1},{4,6},{6,4},{5,7},{7,5},{8,10},{10,8},{9,1... | collective-permute-start | bytes 3080 | tf_op jit(solution)/shard_map/ppermute | solution.py:29

commit v11 on v10

--- a/solution.py
+++ b/solution.py
@@ -5,11 +5,13 @@
 from jax.experimental.pallas import tpu as pltpu
 from jax.sharding import PartitionSpec as P
 
-SHARES = (2, 7, 11, 8, 4)
-FULL_PIECES = 1
+SHARES = (2, 5, 9, 10, 6)
+FULL_PIECES = 2
+EARLY_PIECES = 3
+COUNT_PIECE = 2
 ORDER = (
-    (0, 0), (0, 1), (1, 0), (0, 2), (2, 0), (1, 1), (0, 3), (3, 0), (1, 2), (2, 1), (1, 3), (2, 2),
-    (0, 4), (3, 1), (1, 4), (2, 3), (2, 4), (3, 2), (3, 3), (3, 4),
+    (0, 0), (0, 1), (0, 2), (1, 0), (0, 3), (1, 1), (2, 0), (1, 2), (2, 1), (3, 0), (0, 4), (1, 3),
+    (2, 2), (1, 4), (2, 3), (3, 1), (2, 4), (3, 2), (3, 3), (3, 4),
 )
 KERNEL_VMEM = 16 * 1024 * 1024
 ROOM_SIXTEENTHS = 11
@@ -42,22 +44,58 @@
     return across(turned, rows).astype(jnp.bfloat16)
 
 
-def first_kernel(
-    wide, room, count, skeleton_hbm, compress_hbm, sampling_hbm, traces_hbm,
-    full_ref, small_ref, extra_ref, coeffs_ref,
-    skeleton_ref, compress_ref, sampling_ref, rows_ref, arrived,
+def early_kernel(starts, sampling_hbm, traces_hbm, *refs):
+    pieces = len(starts) - 1
+    outs, (sampling_ref, rows_ref, arrived) = refs[:pieces], refs[pieces:]
+    loads = [pltpu.make_async_copy(sampling_hbm, sampling_ref, arrived.at[pieces])]
+    for i in range(pieces):
+        span = pl.ds(starts[i], starts[i + 1] - starts[i])
+        loads.append(pltpu.make_async_copy(traces_hbm.at[span], rows_ref.at[span], arrived.at[i]))
+    for load in loads:
+        load.start()
+    loads[0].wait()
+    for i in range(pieces):
+        loads[i + 1].wait()
+        span = pl.ds(starts[i], starts[i + 1] - starts[i])
+        outs[i][...] = sampled_block(sampling_ref[0], rows_ref[span])
+
+
+def early(sampling, traces, starts):
+    pieces = len(starts) - 1
+    width = sampling.shape[-1]
+    total = starts[-1]
+    return pl.pallas_call(
+        lambda *refs: early_kernel(starts, *refs),
+        out_shape=[
+            jax.ShapeDtypeStruct((width, starts[i + 1] - starts[i]), jnp.bfloat16) for i in range(pieces)
+        ],
+        in_specs=[pl.BlockSpec(memory_space=pltpu.HBM)] * 2,
+        out_specs=[pl.BlockSpec(memory_space=pltpu.VMEM)] * pieces,
+        scratch_shapes=[
+            pltpu.VMEM(sampling.shape, jnp.bfloat16),
+            pltpu.VMEM((total, traces.shape[1]), jnp.bfloat16),
+            pltpu.SemaphoreType.DMA((pieces + 1,)),
+        ],
+        compiler_params=pltpu.CompilerParams(vmem_limit_bytes=KERNEL_VMEM),
+        cost_estimate=pl.CostEstimate(
+            flops=2 * total * width * width, bytes_accessed=4 * total * width, transcendentals=0
+        ),
+        name="early",
+    )(sampling, traces)
+
+
+def tables_kernel(
+    wide, room, skeleton_hbm, compress_hbm, full_ref, small_ref, extra_ref,
+    skeleton_ref, compress_ref, arrived,
 ):
     loads = [
         pltpu.make_async_copy(skeleton_hbm, skeleton_ref, arrived.at[0]),
         pltpu.make_async_copy(compress_hbm, compress_ref, arrived.at[1]),
-        pltpu.make_async_copy(sampling_hbm, sampling_ref, arrived.at[2]),
-        pltpu.make_async_copy(traces_hbm.at[pl.ds(0, count)], rows_ref, arrived.at[3]),
     ]
     for load in loads:
         load.start()
     for load in loads:
         load.wait()
-    coeffs_ref[...] = sampled_block(sampling_ref[0], rows_ref[...])
     levels, rank = skeleton_ref.shape[0], skeleton_ref.shape[-1]
     width = 2 * rank
     f32, i32 = jnp.float32, jnp.int32
@@ -106,32 +144,27 @@
         extra_ref[level] = jnp.where(k < rank, extra_ref[level].astype(f32), most).astype(jnp.bfloat16)
 
 
-def first(skeleton, compress, sampling, traces, wide, room, count):
+def tables(skeleton, compress, wide, room):
     levels, rank = skeleton.shape[1:]
     shape = (levels, 2 * rank, 4 * rank)
-    width = sampling.shape[-1]
-    whole = pl.BlockSpec(memory_space=pltpu.VMEM)
     return pl.pallas_call(
-        lambda *refs: first_kernel(wide, room, count, *refs),
+        lambda *refs: tables_kernel(wide, room, *refs),
         out_shape=[
             jax.ShapeDtypeStruct(shape, jnp.bfloat16),
             jax.ShapeDtypeStruct(shape, jnp.bfloat16),
             jax.ShapeDtypeStruct((levels, 2 * rank, 2 * rank), jnp.bfloat16),
-            jax.ShapeDtypeStruct((width, count), jnp.bfloat16),
-        ],
-        in_specs=[pl.BlockSpec(memory_space=pltpu.HBM)] * 4,
-        out_specs=[whole] * 4,
+        ],
+        in_specs=[pl.BlockSpec(memory_space=pltpu.HBM)] * 2,
+        out_specs=[pl.BlockSpec(memory_space=pltpu.VMEM)] * 3,
         scratch_shapes=[
             pltpu.VMEM((levels, 1, rank), jnp.int32),
             pltpu.VMEM(compress.shape, jnp.bfloat16),
-            pltpu.VMEM(sampling.shape, jnp.bfloat16),
-            pltpu.VMEM((count, traces.shape[1]), jnp.bfloat16),
-            pltpu.SemaphoreType.DMA((4,)),
+            pltpu.SemaphoreType.DMA((2,)),
         ],
         compiler_params=pltpu.CompilerParams(vmem_limit_bytes=KERNEL_VMEM),
         cost_estimate=pl.CostEstimate(flops=50_000_000, bytes_accessed=600_000, transcendentals=0),
-        name="first",
-    )(skeleton.transpose(1, 0, 2), compress, sampling, traces)
+        name="tables",
+    )(skeleton.transpose(1, 0, 2), compress)
 
 
 def sampled_apart(sampling, traces):
@@ -228,7 +261,8 @@
     unit = traces.shape[0] // sum(SHARES)
     pieces = len(SHARES)
     starts = [unit * sum(SHARES[:i]) for i in range(pieces + 1)]
-    full, small, extra, coeffs = first(skeleton, compress, sampling, traces, wide, room, starts[1])
+    coeffs = early(sampling, traces, starts[: EARLY_PIECES + 1])
+    full, small, extra = tables(after(skeleton, coeffs[0]), compress, wide, room)
     sampling, evaluation = sampling[0], evaluation[0]
     most_here = lax.broadcasted_iota(jnp.int32, extra.shape[1:], 1) >= rank
 
@@ -240,10 +274,11 @@
     for level, piece in ORDER:
         count = starts[piece + 1] - starts[piece]
         if level == 0:
-            own = coeffs
-            if piece > 0:
+            if piece < EARLY_PIECES:
+                own = coeffs[piece]
+            else:
                 block = traces[starts[piece] : starts[piece + 1]]
-                own = sampled(after(sampling, coeffs if piece == 1 else previous), block)
+                own = sampled(after(sampling, previous), block)
         else:
             arrived = after(partners[piece], previous)
             if piece == 0 and level - 1 >= wide:
@@ -257,6 +292,10 @@
             own = times(matrix, value)
         if level == levels:
             done[piece] = previous = evaluated(own, evaluation)
+            if piece == COUNT_PIECE:
+                most = after(jnp.maximum(extra[levels - 1], known)[:8, rank:], previous)
+                for hop in hops[:wide]:
+                    most = jnp.maximum(most, from_partner(most, hop))
             continue
         outgoing = own
         if compact(level, piece):
@@ -269,9 +308,6 @@
         inputs[piece] = own
         partners[piece] = from_partner(outgoing, hops[level])
         previous = outgoing
-    most = after(jnp.maximum(extra[levels - 1], known)[:8, rank:], previous)
-    for hop in hops[:wide]:
-        most = jnp.maximum(most, from_partner(most, hop))
     quick = jnp.concatenate(done, 0)
     return lax.cond(
         most[0, 0] > room,

time: 63.7 us -> 56.2 us (0.88)
  waiting for transfers between devices: 20.2 us -> 13.1 us
  matrix products: 16.1 us -> 12.8 us
  starting transfers between devices: 23.5 us -> 25.7 us
  Pallas kernels: 2.05 us -> 2.85 us
    ppermute x16, waiting for transfers between devices: 20.2 us -> 13.1 us  [from_partner(): return lax.ppermute(block, hop[0], route(*hop))]
    dot_general x4 -> x2, matrix products: 4.74 us -> 2.39 us  [sampled(): jnp.einsum('pc,tp->ct', sampling, traces, preferred_element_type=jnp.floa...]
    ppermute x16, starting transfers between devices: 23.5 us -> 25.7 us  [from_partner(): return lax.ppermute(block, hop[0], route(*hop))]
    dot_general x18 -> x16, matrix products: 5.27 us -> 4.23 us  [times(): jnp.dot(matrix, value, preferred_element_type=jnp.float32)]
    pallas_call x1 -> x2, Pallas kernels: 2.05 us -> 2.85 us  [the longest x1 1.66 us: early(): pl.pallas_call(lambda *refs: early_kernel(starts, *refs), out_shape=[jax....]
  transfers between devices with their start and end apart: 16 -> 16, of which waited for: 7 -> 7; matrix products, arithmetic and copies ran while one was open for 24% -> 22% of each run, Pallas kernels for 0% -> 2%
where the time goes in v11:
time: 56.2 us; the launch traced here: 56 us
  starting transfers between devices  25.7 us (46%)
  waiting for transfers between devices  13.1 us (23%)
  matrix products  12.8 us (23%)
  Pallas kernels  2.85 us (5%)
  between operations  0.88 us (2%)
  local copies, waits for them, and re-layouts  0.6 us (1%)
    ppermute x16, starting transfers between devices, from_partner(): return lax.ppermute(block, hop[0], route(*hop))  25.7 us
    ppermute x16, waiting for transfers between devices, from_partner(): return lax.ppermute(block, hop[0], route(*hop))  13.1 us
    dot_general x5, matrix products, evaluated(): jnp.einsum('ct,cp->tp', coeffs, evaluation, preferred_element_type=jnp.fl...  5.67 us
    dot_general x16, matrix products, times(): jnp.dot(matrix, value, preferred_element_type=jnp.float32)  4.23 us
    dot_general x2, matrix products, sampled(): jnp.einsum('pc,tp->ct', sampling, traces, preferred_element_type=jnp.floa...  2.39 us
    pallas_call x1, Pallas kernels, early(): pl.pallas_call(lambda *refs: early_kernel(starts, *refs), out_shape=[jax....  1.66 us
    pallas_call x1, Pallas kernels, tables(): pl.pallas_call(lambda *refs: tables_kernel(wide, room, *refs), out_shape=...  1.19 us
  transfers between devices with their start and end apart: 16, of which 7 were waited for; matrix products, arithmetic and copies ran while one was open for 22% of the time, Pallas kernels for 2%

profile of v11, /device:TPU:0, one launch (start us, length us, event | category | flops | bytes accessed | tf_op | source)
XLA Modules:
  0.0 56.0 jit_solution(4816699780986780140)
XLA Ops:
  0.0 1.7 %early.1 = (bf16[128,256]{1,0:T(8,128)(2,1)S(1)}, bf16[128,640]{1,0:T(8,128)(2,1)S(1)}, bf16[128,1152]{1,0:T(8,128)(2,1)S(1)}) custom-call(bf16[1,128,128]{2,1,0:T(8,128)(2,1)} %refs_0_.1, bf16[4096,128]{1,0:T(8,128)(2,1)} %refs_1_.2), custom_call_target="tpu_custom_call" | custom-call | flops 67108864 | bytes 1048576 | tf_op jit(solution)/shard_map/early/pallas_call | solution.py:67
  1.7 3.0 %collective-permute-start.3 = (bf16[128,256]{1,0:T(8,128)(2,1)S(1)}, bf16[128,256]{1,0:T(8,128)(2,1)S(1)}, u32[]{:S(2)}, u32[]{:S(2)}) collective-permute-start(bf16[128,256]{1,0:T(8,128)(2,1)S(1)} %get-tuple-element.49), channel_id=1, source_target_pairs={{0,2},{2,0},{1,3},{3,1},{4,6},{6,4},{5,7},{7,5},{8,10},{10,8},{9,1... | collective-permute-start | bytes 196616 | tf_op jit(solution)/shard_map/ppermute | solution.py:31
  4.8 1.9 %collective-permute-start.8 = (bf16[128,1152]{1,0:T(8,128)(2,1)S(1)}, bf16[128,1152]{1,0:T(8,128)(2,1)S(1)}, u32[]{:S(2)}, u32[]{:S(2)}) collective-permute-start(bf16[128,1152]{1,0:T(8,128)(2,1)S(1)} %get-tuple-element.53), channel_id=1, source_target_pairs={{0,2},{2,0},{1,3},{3,1},{4,6},{6,4},{5,7},{7,5},{8,10},{10,8},{9,1... | collective-permute-start | bytes 884744 | tf_op jit(solution)/shard_map/ppermute | solution.py:31
  6.8 1.2 %tables.1 = (bf16[3,128,256]{2,1,0:T(8,128)(2,1)S(1)}, bf16[3,128,256]{2,1,0:T(8,128)(2,1)S(1)}, bf16[3,128,128]{2,1,0:T(8,128)(2,1)S(1)}) custom-call(s32[3,1,64]{2,1,0:T(1,128)S(1)} %bitcast.112, bf16[1,3,64,128]{3,2,1,0:T(8,128)(2,1)S(1)} %copy-done.2), custom_call_target="tpu_custom_call" | custom-call | flops 50000000 | bytes 600000 | tf_op jit(solution)/shard_map/tables/pallas_call | solution.py:150
  8.2 1.7 %collective-permute-start.4 = (bf16[128,384]{1,0:T(8,128)(2,1)S(1)}, bf16[128,384]{1,0:T(8,128)(2,1)S(1)}, u32[]{:S(2)}, u32[]{:S(2)}) collective-permute-start(bf16[128,384]{1,0:T(8,128)(2,1)S(1)} %pad_maximum_fusion.6), channel_id=1, source_target_pairs={{0,4},{4,0},{8,12},{12,8},{1,5},{5,1},{9,13},{13,9},{2,6},{6,2},{1... | collective-permute-start | bytes 294920 | tf_op jit(solution)/shard_map/ppermute | solution.py:31
  9.9 1.2 %convolution_convert_fusion.13 = bf16[128,1280]{1,0:T(8,128)(2,1)S(1)} fusion(bf16[128,128]{1,0:T(8,128)(2,1)S(1)} %bitcast.107, bf16[4096,128]{1,0:T(8,128)(2,1)} %refs_1_.2), kind=kOutput, calls=%fused_computation.38 | convolution fusion | flops 42106880 | bytes 688128 | tf_op jit(solution)/shard_map/pc,tp->ct/dot_general | solution.py:221
  11.2 1.6 %collective-permute-start.10 = (bf16[128,1280]{1,0:T(8,128)(2,1)S(1)}, bf16[128,1280]{1,0:T(8,128)(2,1)S(1)}, u32[]{:S(2)}, u32[]{:S(2)}) collective-permute-start(bf16[128,1280]{1,0:T(8,128)(2,1)S(1)} %convolution_convert_fusion.13), channel_id=1, source_target_pairs={{0,2},{2,0},{1,3},{3,1},{4,6},{6,4},{5,7},{7,5},{8,10},{10,8},{9,1... | collective-permute-start | bytes 983048 | tf_op jit(solution)/shard_map/ppermute | solution.py:31
  13.2 1.6 %collective-permute-start.7 = (bf16[128,640]{1,0:T(8,128)(2,1)S(1)}, bf16[128,640]{1,0:T(8,128)(2,1)S(1)}, u32[]{:S(2)}, u32[]{:S(2)}) collective-permute-start(bf16[128,640]{1,0:T(8,128)(2,1)S(1)} %convolution_convert_fusion.25), channel_id=1, source_target_pairs={{0,4},{4,0},{8,12},{12,8},{1,5},{5,1},{9,13},{13,9},{2,6},{6,2},{1... | collective-permute-start | bytes 491528 | tf_op jit(solution)/shard_map/ppermute | solution.py:31
  14.9 2.7 %collective-permute-start.6 = (bf16[128,384]{1,0:T(8,128)(2,1)S(1)}, bf16[128,384]{1,0:T(8,128)(2,1)S(1)}, u32[]{:S(2)}, u32[]{:S(2)}) collective-permute-start(bf16[128,384]{1,0:T(8,128)(2,1)S(1)} %pad_maximum_fusion.7), channel_id=1, source_target_pairs={{0,8},{8,0},{4,12},{12,4},{1,9},{9,1},{5,13},{13,5},{2,10},{10,2},... | collective-permute-start | bytes 294920 | tf_op jit(solution)/shard_map/ppermute | solution.py:31
  17.7 0.4 collective-permute-done.8
  18.4 1.6 %collective-permute-start.9 = (bf16[88,1152]{1,0:T(8,128)(2,1)S(1)}, bf16[88,1152]{1,0:T(8,128)(2,1)S(1)}, u32[]{:S(2)}, u32[]{:S(2)}) collective-permute-start(bf16[88,1152]{1,0:T(8,128)(2,1)S(1)} %convolution_convert_fusion.17), channel_id=1, source_target_pairs={{0,4},{4,0},{8,12},{12,8},{1,5},{5,1},{9,13},{13,9},{2,6},{6,2},{1... | collective-permute-start | bytes 608264 | tf_op jit(solution)/shard_map/ppermute | solution.py:31
  20.8 3.5 %collective-permute-start.14 = (bf16[128,640]{1,0:T(8,128)(2,1)S(1)}, bf16[128,640]{1,0:T(8,128)(2,1)S(1)}, u32[]{:S(2)}, u32[]{:S(2)}) collective-permute-start(bf16[128,640]{1,0:T(8,128)(2,1)S(1)} %convolution_convert_fusion.24), channel_id=1, source_target_pairs={{0,8},{8,0},{4,12},{12,4},{1,9},{9,1},{5,13},{13,5},{2,10},{10,2},... | collective-permute-start | bytes 491528 | tf_op jit(solution)/shard_map/ppermute | solution.py:31
  24.4 1.0 %constant_dynamic-update-slice_fusion.5 = bf16[4096,128]{1,0:T(8,128)(2,1)} fusion(bf16[1,128,128]{2,1,0:T(8,128)(2,1)S(1)} %copy-done.4, bf16[128,256]{1,0:T(8,128)(2,1)S(1)} %slice.154, bf16[128,256]{1,0:T(8,128)(2,1)S(1)} %convolution_convert_fusion.31, bf16[3,128,256]{2,1,0:T(8,128)(2,1)S(1)} %get-tuple-element.52), kind=kOutput, calls=%fused_computation.168 | convolution fusion | flops 25493504 | bytes 294912 | tf_op jit(solution)/shard_map/ct,cp->tp/dot_general | solution.py:227
  25.4 1.2 %convolution_convert_fusion.22 = bf16[128,768]{1,0:T(8,128)(2,1)S(1)} fusion(bf16[128,128]{1,0:T(8,128)(2,1)S(1)} %bitcast.108, bf16[4096,128]{1,0:T(8,128)(2,1)} %refs_1_.2), kind=kOutput, calls=%fused_computation.58 | convolution fusion | flops 25264128 | bytes 425984 | tf_op jit(solution)/shard_map/pc,tp->ct/dot_general | solution.py:221
  26.5 1.7 %collective-permute-start.12 = (bf16[128,768]{1,0:T(8,128)(2,1)S(1)}, bf16[128,768]{1,0:T(8,128)(2,1)S(1)}, u32[]{:S(2)}, u32[]{:S(2)}) collective-permute-start(bf16[128,768]{1,0:T(8,128)(2,1)S(1)} %convolution_convert_fusion.22), channel_id=1, source_target_pairs={{0,2},{2,0},{1,3},{3,1},{4,6},{6,4},{5,7},{7,5},{8,10},{10,8},{9,1... | collective-permute-start | bytes 589832 | tf_op jit(solution)/shard_map/ppermute | solution.py:31
  28.5 0.3 convolution_convert_fusion.16
  28.8 0.3 convolution_convert_fusion.10
  29.3 1.7 %collective-permute-start.11 = (bf16[88,1152]{1,0:T(8,128)(2,1)S(1)}, bf16[88,1152]{1,0:T(8,128)(2,1)S(1)}, u32[]{:S(2)}, u32[]{:S(2)}) collective-permute-start(bf16[88,1152]{1,0:T(8,128)(2,1)S(1)} %convolution_convert_fusion.15), channel_id=1, source_target_pairs={{0,8},{8,0},{4,12},{12,4},{1,9},{9,1},{5,13},{13,5},{2,10},{10,2},... | collective-permute-start | bytes 608264 | tf_op jit(solution)/shard_map/ppermute | solution.py:31
  31.0 1.0 %convolution_convert_fusion.11 = bf16[128,1152]{1,0:T(8,128)(2,1)} fusion(bf16[88,1152]{1,0:T(8,128)(2,1)S(1)} %collective-permute-done.9, bf16[128,1152]{1,0:T(8,128)(2,1)S(1)} %convolution_convert_fusion.12, bf16[3,128,256]{2,1,0:T(8,128)(2,1)S(1)} %get-tuple-element.62), kind=kOutput, calls=%fused_computation.36 | convolution fusion | flops 77709312 | bytes 858112 | tf_op jit(solution)/shard_map/dot_general | solution.py:217
  31.9 0.3 collective-permute-done.12
  32.5 0.5 collective-permute-start.13
  33.2 6.5 %collective-permute-done.15 = bf16[88,1280]{1,0:T(8,128)(2,1)S(1)} collective-permute-done((bf16[88,1280]{1,0:T(8,128)(2,1)S(1)}, bf16[88,1280]{1,0:T(8,128)(2,1)S(1)}, u32[]{:S(2)}, u32[]{:S(2)}) %collective-permute-start.15) | collective-permute-done | bytes 225312 | tf_op jit(solution)/shard_map/ppermute | solution.py:31
  39.9 0.4 collective-permute-start.17
  40.6 1.1 %constant_dynamic-update-slice_fusion.4 = bf16[4096,128]{1,0:T(8,128)(2,1)} fusion(bf16[4096,128]{1,0:T(8,128)(2,1)} %constant_dynamic-update-slice_fusion.5, bf16[1,128,128]{2,1,0:T(8,128)(2,1)S(1)} %copy-done.4, bf16[128,640]{1,0:T(8,128)(2,1)S(1)} %collective-permute-done.14, bf16[128,640]{1,0:T(8,128)(2,1)S(1)} %convolution_convert_fusion.24, ...), kind=kOutput, calls=%fused_computation.167 | convolution fusion | flops 63733760 | bytes 589824 | tf_op jit(solution)/shard_map/ct,cp->tp/dot_general | solution.py:227
  41.7 0.3 collective-permute-done.13
  42.3 1.2 %constant_dynamic-update-slice_fusion.3 = bf16[4096,128]{1,0:T(8,128)(2,1)} fusion(bf16[4096,128]{1,0:T(8,128)(2,1)} %constant_dynamic-update-slice_fusion.4, bf16[1,128,128]{2,1,0:T(8,128)(2,1)S(1)} %copy-done.4, bf16[88,1152]{1,0:T(8,128)(2,1)S(1)} %collective-permute-done.11, bf16[128,1152]{1,0:T(8,128)(2,1)S(1)} %copy-done.5, ...), kind=kOutput, calls=%fused_computation.166 | convolution fusion | flops 115605504 | bytes 890880 | tf_op jit(solution)/shard_map/ct,cp->tp/dot_general | solution.py:227
  43.5 1.4 %collective-permute-start.16 = (bf16[8,64]{1,0:T(8,128)(2,1)S(1)}, bf16[8,64]{1,0:T(8,128)(2,1)S(1)}, u32[]{:S(2)}, u32[]{:S(2)}) collective-permute-start(bf16[8,64]{1,0:T(8,128)(2,1)S(1)} %slice_maximum_fusion), channel_id=1, source_target_pairs={{0,2},{2,0},{1,3},{3,1},{4,6},{6,4},{5,7},{7,5},{8,10},{10,8},{9,1... | collective-permute-start | bytes 3080 | tf_op jit(solution)/shard_map/ppermute | solution.py:31
  45.1 2.2 %collective-permute-start.18 = (bf16[88,768]{1,0:T(8,128)(2,1)S(1)}, bf16[88,768]{1,0:T(8,128)(2,1)S(1)}, u32[]{:S(2)}, u32[]{:S(2)}) collective-permute-start(bf16[88,768]{1,0:T(8,128)(2,1)S(1)} %convolution_convert_fusion.27), channel_id=1, source_target_pairs={{0,8},{8,0},{4,12},{12,4},{1,9},{9,1},{5,13},{13,5},{2,10},{10,2},... | collective-permute-start | bytes 405512 | tf_op jit(solution)/shard_map/ppermute | solution.py:31
  47.3 0.5 slice.161
  48.4 5.0 %collective-permute-done.17 = bf16[88,1280]{1,0:T(8,128)(2,1)S(1)} collective-permute-done((bf16[88,1280]{1,0:T(8,128)(2,1)S(1)}, bf16[88,1280]{1,0:T(8,128)(2,1)S(1)}, u32[]{:S(2)}, u32[]{:S(2)}) %collective-permute-start.17) | collective-permute-done | bytes 225312 | tf_op jit(solution)/shard_map/ppermute | solution.py:31
  53.4 1.2 %constant_dynamic-update-slice_fusion.2 = bf16[4096,128]{1,0:T(8,128)(2,1)} fusion(bf16[4096,128]{1,0:T(8,128)(2,1)} %constant_dynamic-update-slice_fusion.3, bf16[1,128,128]{2,1,0:T(8,128)(2,1)S(1)} %copy-done.4, bf16[88,1280]{1,0:T(8,128)(2,1)S(1)} %collective-permute-done.17, bf16[128,1280]{1,0:T(8,128)(2,1)S(1)} %convolution_convert_fusion.7, ...), kind=kOutput, calls=%fused_computation.165 | convolution fusion | flops 128450560 | bytes 978944 | tf_op jit(solution)/shard_map/ct,cp->tp/dot_general | solution.py:227
  54.9 1.1 %fusion.28 = bf16[4096,128]{1,0:T(8,128)(2,1)} fusion(bf16[4096,128]{1,0:T(8,128)(2,1)} %constant_dynamic-update-slice_fusion.2, bf16[88,768]{1,0:T(8,128)(2,1)S(1)} %collective-permute-done.18, bf16[128,768]{1,0:T(8,128)(2,1)S(1)} %convolution_convert_fusion.20, bf16[3,128,256]{2,1,0:T(8,128)(2,1)S(1)} %get-tuple-element.62, ...), kind=kOutput, calls=%fused_computation.54 | convolution fusion | flops 77070336 | bytes 626688 | tf_op jit(solution)/shard_map/ct,cp->tp/dot_general | solution.py:227
  (53 shorter events, 4.1 us)
Async XLA Ops:
  0.0 9.9 %copy-start.1 = (bf16[1,128,128]{2,1,0:T(8,128)(2,1)S(1)}, bf16[1,128,128]{2,1,0:T(8,128)(2,1)}, u32[]{:S(2)}) copy-start(bf16[1,128,128]{2,1,0:T(8,128)(2,1)} %refs_0_.1) | copy-start | bytes 98308
  0.0 6.7 %copy-start.3 = (s32[1,3,64]{2,0,1:T(1,128)S(1)}, s32[1,3,64]{2,0,1:T(1,128)}, u32[]{:S(2)}) copy-start(s32[1,3,64]{2,0,1:T(1,128)} %param.9) | copy-start | bytes 2308
  0.0 6.8 %copy-start.2 = (bf16[1,3,64,128]{3,2,1,0:T(8,128)(2,1)S(1)}, bf16[1,3,64,128]{3,2,1,0:T(8,128)(2,1)}, u32[]{:S(2)}) copy-start(bf16[1,3,64,128]{3,2,1,0:T(8,128)(2,1)} %refs_1_.3) | copy-start | bytes 147460
  1.7 6.3 %collective-permute-start.3 = (bf16[128,256]{1,0:T(8,128)(2,1)S(1)}, bf16[128,256]{1,0:T(8,128)(2,1)S(1)}, u32[]{:S(2)}, u32[]{:S(2)}) collective-permute-start(bf16[128,256]{1,0:T(8,128)(2,1)S(1)} %get-tuple-element.49), channel_id=1, source_target_pairs={{0,2},{2,0},{1,3},{3,1},{4,6},{6,4},{5,7},{7,5},{8,10},{10,8},{9,1... | collective-permute-start | bytes 196616 | tf_op jit(solution)/shard_map/ppermute | solution.py:31
  4.7 8.1 %collective-permute-start.5 = (bf16[128,640]{1,0:T(8,128)(2,1)S(1)}, bf16[128,640]{1,0:T(8,128)(2,1)S(1)}, u32[]{:S(2)}, u32[]{:S(2)}) collective-permute-start(bf16[128,640]{1,0:T(8,128)(2,1)S(1)} %get-tuple-element.55), channel_id=1, source_target_pairs={{0,2},{2,0},{1,3},{3,1},{4,6},{6,4},{5,7},{7,5},{8,10},{10,8},{9,1... | collective-permute-start | bytes 491528 | tf_op jit(solution)/shard_map/ppermute | solution.py:31
  4.8 13.4 %collective-permute-start.8 = (bf16[128,1152]{1,0:T(8,128)(2,1)S(1)}, bf16[128,1152]{1,0:T(8,128)(2,1)S(1)}, u32[]{:S(2)}, u32[]{:S(2)}) collective-permute-start(bf16[128,1152]{1,0:T(8,128)(2,1)S(1)} %get-tuple-element.53), channel_id=1, source_target_pairs={{0,2},{2,0},{1,3},{3,1},{4,6},{6,4},{5,7},{7,5},{8,10},{10,8},{9,1... | collective-permute-start | bytes 884744 | tf_op jit(solution)/shard_map/ppermute | solution.py:31
  8.2 4.8 %collective-permute-start.4 = (bf16[128,384]{1,0:T(8,128)(2,1)S(1)}, bf16[128,384]{1,0:T(8,128)(2,1)S(1)}, u32[]{:S(2)}, u32[]{:S(2)}) collective-permute-start(bf16[128,384]{1,0:T(8,128)(2,1)S(1)} %pad_maximum_fusion.6), channel_id=1, source_target_pairs={{0,4},{4,0},{8,12},{12,8},{1,5},{5,1},{9,13},{13,9},{2,6},{6,2},{1... | collective-permute-start | bytes 294920 | tf_op jit(solution)/shard_map/ppermute | solution.py:31
  11.2 17.3 %collective-permute-start.10 = (bf16[128,1280]{1,0:T(8,128)(2,1)S(1)}, bf16[128,1280]{1,0:T(8,128)(2,1)S(1)}, u32[]{:S(2)}, u32[]{:S(2)}) collective-permute-start(bf16[128,1280]{1,0:T(8,128)(2,1)S(1)} %convolution_convert_fusion.13), channel_id=1, source_target_pairs={{0,2},{2,0},{1,3},{3,1},{4,6},{6,4},{5,7},{7,5},{8,10},{10,8},{9,1... | collective-permute-start | bytes 983048 | tf_op jit(solution)/shard_map/ppermute | solution.py:31
  13.2 7.1 %collective-permute-start.7 = (bf16[128,640]{1,0:T(8,128)(2,1)S(1)}, bf16[128,640]{1,0:T(8,128)(2,1)S(1)}, u32[]{:S(2)}, u32[]{:S(2)}) collective-permute-start(bf16[128,640]{1,0:T(8,128)(2,1)S(1)} %convolution_convert_fusion.25), channel_id=1, source_target_pairs={{0,4},{4,0},{8,12},{12,8},{1,5},{5,1},{9,13},{13,9},{2,6},{6,2},{1... | collective-permute-start | bytes 491528 | tf_op jit(solution)/shard_map/ppermute | solution.py:31
  14.9 5.8 %collective-permute-start.6 = (bf16[128,384]{1,0:T(8,128)(2,1)S(1)}, bf16[128,384]{1,0:T(8,128)(2,1)S(1)}, u32[]{:S(2)}, u32[]{:S(2)}) collective-permute-start(bf16[128,384]{1,0:T(8,128)(2,1)S(1)} %pad_maximum_fusion.7), channel_id=1, source_target_pairs={{0,8},{8,0},{4,12},{12,4},{1,9},{9,1},{5,13},{13,5},{2,10},{10,2},... | collective-permute-start | bytes 294920 | tf_op jit(solution)/shard_map/ppermute | solution.py:31
  18.4 6.0 %copy-start.4 = (bf16[1,128,128]{2,1,0:T(8,128)(2,1)S(1)}, bf16[1,128,128]{2,1,0:T(8,128)(2,1)}, u32[]{:S(2)}) copy-start(bf16[1,128,128]{2,1,0:T(8,128)(2,1)} %param.11) | copy-start | bytes 98308
  18.4 10.6 %collective-permute-start.9 = (bf16[88,1152]{1,0:T(8,128)(2,1)S(1)}, bf16[88,1152]{1,0:T(8,128)(2,1)S(1)}, u32[]{:S(2)}, u32[]{:S(2)}) collective-permute-start(bf16[88,1152]{1,0:T(8,128)(2,1)S(1)} %convolution_convert_fusion.17), channel_id=1, source_target_pairs={{0,4},{4,0},{8,12},{12,8},{1,5},{5,1},{9,13},{13,9},{2,6},{6,2},{1... | collective-permute-start | bytes 608264 | tf_op jit(solution)/shard_map/ppermute | solution.py:31
  20.8 19.8 %collective-permute-start.14 = (bf16[128,640]{1,0:T(8,128)(2,1)S(1)}, bf16[128,640]{1,0:T(8,128)(2,1)S(1)}, u32[]{:S(2)}, u32[]{:S(2)}) collective-permute-start(bf16[128,640]{1,0:T(8,128)(2,1)S(1)} %convolution_convert_fusion.24), channel_id=1, source_target_pairs={{0,8},{8,0},{4,12},{12,4},{1,9},{9,1},{5,13},{13,5},{2,10},{10,2},... | collective-permute-start | bytes 491528 | tf_op jit(solution)/shard_map/ppermute | solution.py:31
  26.5 5.7 %collective-permute-start.12 = (bf16[128,768]{1,0:T(8,128)(2,1)S(1)}, bf16[128,768]{1,0:T(8,128)(2,1)S(1)}, u32[]{:S(2)}, u32[]{:S(2)}) collective-permute-start(bf16[128,768]{1,0:T(8,128)(2,1)S(1)} %convolution_convert_fusion.22), channel_id=1, source_target_pairs={{0,2},{2,0},{1,3},{3,1},{4,6},{6,4},{5,7},{7,5},{8,10},{10,8},{9,1... | collective-permute-start | bytes 589832 | tf_op jit(solution)/shard_map/ppermute | solution.py:31
  28.7 11.0 %collective-permute-start.15 = (bf16[88,1280]{1,0:T(8,128)(2,1)S(1)}, bf16[88,1280]{1,0:T(8,128)(2,1)S(1)}, u32[]{:S(2)}, u32[]{:S(2)}) collective-permute-start(bf16[88,1280]{1,0:T(8,128)(2,1)S(1)} %convolution_convert_fusion.16), channel_id=1, source_target_pairs={{0,4},{4,0},{8,12},{12,8},{1,5},{5,1},{9,13},{13,9},{2,6},{6,2},{1... | collective-permute-start | bytes 675848 | tf_op jit(solution)/shard_map/ppermute | solution.py:31
  29.3 12.9 %collective-permute-start.11 = (bf16[88,1152]{1,0:T(8,128)(2,1)S(1)}, bf16[88,1152]{1,0:T(8,128)(2,1)S(1)}, u32[]{:S(2)}, u32[]{:S(2)}) collective-permute-start(bf16[88,1152]{1,0:T(8,128)(2,1)S(1)} %convolution_convert_fusion.15), channel_id=1, source_target_pairs={{0,8},{8,0},{4,12},{12,4},{1,9},{9,1},{5,13},{13,5},{2,10},{10,2},... | collective-permute-start | bytes 608264 | tf_op jit(solution)/shard_map/ppermute | solution.py:31
  32.5 9.6 %collective-permute-start.13 = (bf16[88,768]{1,0:T(8,128)(2,1)S(1)}, bf16[88,768]{1,0:T(8,128)(2,1)S(1)}, u32[]{:S(2)}, u32[]{:S(2)}) collective-permute-start(bf16[88,768]{1,0:T(8,128)(2,1)S(1)} %convolution_convert_fusion.28), channel_id=1, source_target_pairs={{0,4},{4,0},{8,12},{12,8},{1,5},{5,1},{9,13},{13,9},{2,6},{6,2},{1... | collective-permute-start | bytes 405512 | tf_op jit(solution)/shard_map/ppermute | solution.py:31
  39.9 13.5 %collective-permute-start.17 = (bf16[88,1280]{1,0:T(8,128)(2,1)S(1)}, bf16[88,1280]{1,0:T(8,128)(2,1)S(1)}, u32[]{:S(2)}, u32[]{:S(2)}) collective-permute-start(bf16[88,1280]{1,0:T(8,128)(2,1)S(1)} %convolution_convert_fusion.14), channel_id=1, source_target_pairs={{0,8},{8,0},{4,12},{12,4},{1,9},{9,1},{5,13},{13,5},{2,10},{10,2},... | collective-permute-start | bytes 675848 | tf_op jit(solution)/shard_map/ppermute | solution.py:31
  40.6 1.7 %copy-start.5 = (bf16[128,1152]{1,0:T(8,128)(2,1)S(1)}, bf16[128,1152]{1,0:T(8,128)(2,1)}, u32[]{:S(2)}) copy-start(bf16[128,1152]{1,0:T(8,128)(2,1)} %convolution_convert_fusion.11) | copy-start | bytes 884740
  43.5 3.8 %collective-permute-start.16 = (bf16[8,64]{1,0:T(8,128)(2,1)S(1)}, bf16[8,64]{1,0:T(8,128)(2,1)S(1)}, u32[]{:S(2)}, u32[]{:S(2)}) collective-permute-start(bf16[8,64]{1,0:T(8,128)(2,1)S(1)} %slice_maximum_fusion), channel_id=1, source_target_pairs={{0,2},{2,0},{1,3},{3,1},{4,6},{6,4},{5,7},{7,5},{8,10},{10,8},{9,1... | collective-permute-start | bytes 3080 | tf_op jit(solution)/shard_map/ppermute | solution.py:31
  45.1 9.8 %collective-permute-start.18 = (bf16[88,768]{1,0:T(8,128)(2,1)S(1)}, bf16[88,768]{1,0:T(8,128)(2,1)S(1)}, u32[]{:S(2)}, u32[]{:S(2)}) collective-permute-start(bf16[88,768]{1,0:T(8,128)(2,1)S(1)} %convolution_convert_fusion.27), channel_id=1, source_target_pairs={{0,8},{8,0},{4,12},{12,4},{1,9},{9,1},{5,13},{13,5},{2,10},{10,2},... | collective-permute-start | bytes 405512 | tf_op jit(solution)/shard_map/ppermute | solution.py:31

commit v12 on v11

--- a/solution.py
+++ b/solution.py
@@ -5,13 +5,14 @@
 from jax.experimental.pallas import tpu as pltpu
 from jax.sharding import PartitionSpec as P
 
-SHARES = (2, 5, 9, 10, 6)
-FULL_PIECES = 2
+SHARES = (2, 5, 7, 10, 8)
+FULL_PIECES = (2, 1)
 EARLY_PIECES = 3
 COUNT_PIECE = 2
+LOOK = (3, -1)
 ORDER = (
-    (0, 0), (0, 1), (0, 2), (1, 0), (0, 3), (1, 1), (2, 0), (1, 2), (2, 1), (3, 0), (0, 4), (1, 3),
-    (2, 2), (1, 4), (2, 3), (3, 1), (2, 4), (3, 2), (3, 3), (3, 4),
+    (0, 0), (0, 1), (1, 0), (0, 2), (1, 1), (2, 0), (0, 3), (1, 2), LOOK, (2, 1), (0, 4), (1, 3),
+    (2, 2), (3, 0), (1, 4), (2, 3), (3, 1), (2, 4), (3, 2), (3, 3), (3, 4),
 )
 KERNEL_VMEM = 16 * 1024 * 1024
 ROOM_SIXTEENTHS = 11
@@ -267,11 +268,15 @@
     most_here = lax.broadcasted_iota(jnp.int32, extra.shape[1:], 1) >= rank
 
     def compact(level, piece):
-        return piece >= FULL_PIECES and level >= wide
+        return level >= wide and piece >= FULL_PIECES[level - wide]
 
     inputs, partners, theirs, done = {}, {}, {}, [None] * pieces
-    previous, known = None, None
+    previous, finished, known = None, None, None
     for level, piece in ORDER:
+        if (level, piece) == LOOK:
+            known = after(partners[0], previous)[:, starts[1] :]
+            theirs[levels - 1] = known[:room, :rank]
+            continue
         count = starts[piece + 1] - starts[piece]
         if level == 0:
             if piece < EARLY_PIECES:
@@ -281,7 +286,9 @@
                 own = sampled(after(sampling, previous), block)
         else:
             arrived = after(partners[piece], previous)
-            if piece == 0 and level - 1 >= wide:
+            if level == levels:
+                arrived = after(arrived, finished)
+            elif piece == 0 and level - 1 >= wide:
                 known = arrived[:, count:]
                 theirs[level - 1] = known[:room, :rank]
             value = jnp.concatenate([inputs[piece], arrived[:, :count]], 0)
@@ -291,13 +298,15 @@
                 matrix = small[level - 1]
             own = times(matrix, value)
         if level == levels:
-            done[piece] = previous = evaluated(own, evaluation)
+            done[piece] = finished = evaluated(own, evaluation)
             if piece == COUNT_PIECE:
-                most = after(jnp.maximum(extra[levels - 1], known)[:8, rank:], previous)
+                most = after(jnp.maximum(extra[levels - 1], known)[:8, rank:], finished)
                 for hop in hops[:wide]:
                     most = jnp.maximum(most, from_partner(most, hop))
             continue
         outgoing = own
+        if level == 0 and 1 < piece < EARLY_PIECES:
+            outgoing = after(own, previous)
         if compact(level, piece):
             outgoing = times(compact_rows(matrix, theirs[level]), value)
         if piece == 0 and level >= wide:

time: 56.2 us -> 57.3 us (1.020)
  waiting for transfers between devices: 13.1 us -> 15.4 us
  matrix products: 12.8 us -> 11.3 us
    ppermute x16, waiting for transfers between devices: 13.1 us -> 15.4 us  [from_partner(): return lax.ppermute(block, hop[0], route(*hop))]
    dot_general x2, matrix products: 2.39 us -> 0.51 us  [sampled(): jnp.einsum('pc,tp->ct', sampling, traces, preferred_element_type=jnp.floa...]
    dot_general x16 -> x17, matrix products: 4.23 us -> 4.38 us  [times(): jnp.dot(matrix, value, preferred_element_type=jnp.float32)]
  transfers between devices with their start and end apart: 16 -> 16, of which waited for: 7 -> 7; matrix products, arithmetic and copies ran while one was open for 22% -> 19% of each run, Pallas kernels for 2% -> 2%
where the time goes in v12:
time: 57.3 us; the launch traced here: 57.1 us
  starting transfers between devices  25.8 us (45%)
  waiting for transfers between devices  15.4 us (27%)
  matrix products  11.3 us (20%)
  Pallas kernels  2.84 us (5%)
  between operations  0.96 us (2%)
  local copies, waits for them, and re-layouts  0.69 us (1%)
    ppermute x16, starting transfers between devices, from_partner(): return lax.ppermute(block, hop[0], route(*hop))  25.8 us
    ppermute x16, waiting for transfers between devices, from_partner(): return lax.ppermute(block, hop[0], route(*hop))  15.4 us
    dot_general x5, matrix products, evaluated(): jnp.einsum('ct,cp->tp', coeffs, evaluation, preferred_element_type=jnp.fl...  5.66 us
    dot_general x17, matrix products, times(): jnp.dot(matrix, value, preferred_element_type=jnp.float32)  4.38 us
    pallas_call x1, Pallas kernels, early(): pl.pallas_call(lambda *refs: early_kernel(starts, *refs), out_shape=[jax....  1.65 us
    pallas_call x1, Pallas kernels, tables(): pl.pallas_call(lambda *refs: tables_kernel(wide, room, *refs), out_shape=...  1.19 us
  transfers between devices with their start and end apart: 16, of which 7 were waited for; matrix products, arithmetic and copies ran while one was open for 19% of the time, Pallas kernels for 2%

profile of v12, /device:TPU:0, one launch (start us, length us, event | category | flops | bytes accessed | tf_op | source)
XLA Modules:
  0.0 57.1 jit_solution(406054881198208075)
XLA Ops:
  0.0 1.7 %early.1 = (bf16[128,256]{1,0:T(8,128)(2,1)S(1)}, bf16[128,640]{1,0:T(8,128)(2,1)S(1)}, bf16[128,896]{1,0:T(8,128)(2,1)S(1)}) custom-call(bf16[1,128,128]{2,1,0:T(8,128)(2,1)} %refs_0_.1, bf16[4096,128]{1,0:T(8,128)(2,1)} %refs_1_.2), custom_call_target="tpu_custom_call" | custom-call | flops 58720256 | bytes 917504 | tf_op jit(solution)/shard_map/early/pallas_call | solution.py:68
  1.7 3.0 %collective-permute-start.3 = (bf16[128,256]{1,0:T(8,128)(2,1)S(1)}, bf16[128,256]{1,0:T(8,128)(2,1)S(1)}, u32[]{:S(2)}, u32[]{:S(2)}) collective-permute-start(bf16[128,256]{1,0:T(8,128)(2,1)S(1)} %get-tuple-element.55), channel_id=1, source_target_pairs={{0,2},{2,0},{1,3},{3,1},{4,6},{6,4},{5,7},{7,5},{8,10},{10,8},{9,1... | collective-permute-start | bytes 196616 | tf_op jit(solution)/shard_map/ppermute | solution.py:32
  4.8 1.2 %tables.1 = (bf16[3,128,256]{2,1,0:T(8,128)(2,1)S(1)}, bf16[3,128,256]{2,1,0:T(8,128)(2,1)S(1)}, bf16[3,128,128]{2,1,0:T(8,128)(2,1)S(1)}) custom-call(s32[3,1,64]{2,1,0:T(1,128)S(1)} %bitcast.118, bf16[1,3,64,128]{3,2,1,0:T(8,128)(2,1)S(1)} %copy-done.3), custom_call_target="tpu_custom_call" | custom-call | flops 50000000 | bytes 600000 | tf_op jit(solution)/shard_map/tables/pallas_call | solution.py:151
  6.0 1.1 %collective-permute-done.3 = bf16[128,256]{1,0:T(8,128)(2,1)S(1)} collective-permute-done((bf16[128,256]{1,0:T(8,128)(2,1)S(1)}, bf16[128,256]{1,0:T(8,128)(2,1)S(1)}, u32[]{:S(2)}, u32[]{:S(2)}) %collective-permute-start.3) | collective-permute-done | bytes 65568 | tf_op jit(solution)/shard_map/ppermute | solution.py:32
  7.4 2.5 %collective-permute-start.4 = (bf16[128,384]{1,0:T(8,128)(2,1)S(1)}, bf16[128,384]{1,0:T(8,128)(2,1)S(1)}, u32[]{:S(2)}, u32[]{:S(2)}) collective-permute-start(bf16[128,384]{1,0:T(8,128)(2,1)S(1)} %pad_maximum_fusion.9), channel_id=1, source_target_pairs={{0,4},{4,0},{8,12},{12,8},{1,5},{5,1},{9,13},{13,9},{2,6},{6,2},{1... | collective-permute-start | bytes 294920 | tf_op jit(solution)/shard_map/ppermute | solution.py:32
  9.9 1.6 %collective-permute-start.7 = (bf16[128,896]{1,0:T(8,128)(2,1)S(1)}, bf16[128,896]{1,0:T(8,128)(2,1)S(1)}, u32[]{:S(2)}, u32[]{:S(2)}) collective-permute-start(bf16[128,896]{1,0:T(8,128)(2,1)S(1)} %get-tuple-element.62), channel_id=1, source_target_pairs={{0,2},{2,0},{1,3},{3,1},{4,6},{6,4},{5,7},{7,5},{8,10},{10,8},{9,1... | collective-permute-start | bytes 688136 | tf_op jit(solution)/shard_map/ppermute | solution.py:32
  11.7 0.8 %collective-permute-done.4 = bf16[128,384]{1,0:T(8,128)(2,1)S(1)} collective-permute-done((bf16[128,384]{1,0:T(8,128)(2,1)S(1)}, bf16[128,384]{1,0:T(8,128)(2,1)S(1)}, u32[]{:S(2)}, u32[]{:S(2)}) %collective-permute-start.4) | collective-permute-done | bytes 98336 | tf_op jit(solution)/shard_map/ppermute | solution.py:32
  12.8 3.1 %collective-permute-start.6 = (bf16[128,384]{1,0:T(8,128)(2,1)S(1)}, bf16[128,384]{1,0:T(8,128)(2,1)S(1)}, u32[]{:S(2)}, u32[]{:S(2)}) collective-permute-start(bf16[128,384]{1,0:T(8,128)(2,1)S(1)} %pad_maximum_fusion.10), channel_id=1, source_target_pairs={{0,8},{8,0},{4,12},{12,4},{1,9},{9,1},{5,13},{13,5},{2,10},{10,2},... | collective-permute-start | bytes 294920 | tf_op jit(solution)/shard_map/ppermute | solution.py:32
  15.9 1.6 %collective-permute-start.10 = (bf16[128,640]{1,0:T(8,128)(2,1)S(1)}, bf16[128,640]{1,0:T(8,128)(2,1)S(1)}, u32[]{:S(2)}, u32[]{:S(2)}) collective-permute-start(bf16[128,640]{1,0:T(8,128)(2,1)S(1)} %convolution_convert_fusion.25), channel_id=1, source_target_pairs={{0,4},{4,0},{8,12},{12,8},{1,5},{5,1},{9,13},{13,9},{2,6},{6,2},{1... | collective-permute-start | bytes 491528 | tf_op jit(solution)/shard_map/ppermute | solution.py:32
  17.5 0.3 convolution_convert_fusion.9
  17.8 1.7 %collective-permute-start.9 = (bf16[128,1280]{1,0:T(8,128)(2,1)S(1)}, bf16[128,1280]{1,0:T(8,128)(2,1)S(1)}, u32[]{:S(2)}, u32[]{:S(2)}) collective-permute-start(bf16[128,1280]{1,0:T(8,128)(2,1)S(1)} %convolution_convert_fusion.9), channel_id=1, source_target_pairs={{0,2},{2,0},{1,3},{3,1},{4,6},{6,4},{5,7},{7,5},{8,10},{10,8},{9,1... | collective-permute-start | bytes 983048 | tf_op jit(solution)/shard_map/ppermute | solution.py:32
  20.6 0.6 %collective-permute-start.8 = (bf16[88,896]{1,0:T(8,128)(2,1)S(1)}, bf16[88,896]{1,0:T(8,128)(2,1)S(1)}, u32[]{:S(2)}, u32[]{:S(2)}) collective-permute-start(bf16[88,896]{1,0:T(8,128)(2,1)S(1)} %convolution_convert_fusion.28), channel_id=1, source_target_pairs={{0,4},{4,0},{8,12},{12,8},{1,5},{5,1},{9,13},{13,9},{2,6},{6,2},{1... | collective-permute-start | bytes 473096 | tf_op jit(solution)/shard_map/ppermute | solution.py:32
  21.3 2.9 %collective-permute-done.10 = bf16[128,640]{1,0:T(8,128)(2,1)S(1)} collective-permute-done((bf16[128,640]{1,0:T(8,128)(2,1)S(1)}, bf16[128,640]{1,0:T(8,128)(2,1)S(1)}, u32[]{:S(2)}, u32[]{:S(2)}) %collective-permute-start.10) | collective-permute-done | bytes 163872 | tf_op jit(solution)/shard_map/ppermute | solution.py:32
  24.6 0.7 %collective-permute-start.15 = (bf16[88,640]{1,0:T(8,128)(2,1)S(1)}, bf16[88,640]{1,0:T(8,128)(2,1)S(1)}, u32[]{:S(2)}, u32[]{:S(2)}) collective-permute-start(bf16[88,640]{1,0:T(8,128)(2,1)S(1)} %convolution_convert_fusion.29), channel_id=1, source_target_pairs={{0,8},{8,0},{4,12},{12,4},{1,9},{9,1},{5,13},{13,5},{2,10},{10,2},... | collective-permute-start | bytes 337928 | tf_op jit(solution)/shard_map/ppermute | solution.py:32
  25.5 1.6 %collective-permute-start.12 = (bf16[128,1024]{1,0:T(8,128)(2,1)S(1)}, bf16[128,1024]{1,0:T(8,128)(2,1)S(1)}, u32[]{:S(2)}, u32[]{:S(2)}) collective-permute-start(bf16[128,1024]{1,0:T(8,128)(2,1)S(1)} %convolution_convert_fusion.16), channel_id=1, source_target_pairs={{0,2},{2,0},{1,3},{3,1},{4,6},{6,4},{5,7},{7,5},{8,10},{10,8},{9,1... | collective-permute-start | bytes 786440 | tf_op jit(solution)/shard_map/ppermute | solution.py:32
  27.4 0.9 %convolution_convert_fusion.19 = bf16[128,896]{1,0:T(8,128)(2,1)} fusion(bf16[88,896]{1,0:T(8,128)(2,1)S(1)} %collective-permute-done.8, bf16[128,896]{1,0:T(8,128)(2,1)S(1)} %convolution_convert_fusion.20, bf16[3,128,256]{2,1,0:T(8,128)(2,1)S(1)} %get-tuple-element.68), kind=kOutput, calls=%fused_computation.50 | convolution fusion | flops 60440576 | bytes 681984 | tf_op jit(solution)/shard_map/dot_general | solution.py:218
  28.6 3.0 %collective-permute-start.11 = (bf16[88,896]{1,0:T(8,128)(2,1)S(1)}, bf16[88,896]{1,0:T(8,128)(2,1)S(1)}, u32[]{:S(2)}, u32[]{:S(2)}) collective-permute-start(bf16[88,896]{1,0:T(8,128)(2,1)S(1)} %convolution_convert_fusion.27), channel_id=1, source_target_pairs={{0,8},{8,0},{4,12},{12,4},{1,9},{9,1},{5,13},{13,5},{2,10},{10,2},... | collective-permute-start | bytes 473096 | tf_op jit(solution)/shard_map/ppermute | solution.py:32
  31.6 1.0 %constant_dynamic-update-slice_fusion.5 = bf16[4096,128]{1,0:T(8,128)(2,1)} fusion(bf16[1,128,128]{2,1,0:T(8,128)(2,1)S(1)} %copy-done.5, bf16[128,256]{1,0:T(8,128)(2,1)S(1)} %slice.178, bf16[128,256]{1,0:T(8,128)(2,1)S(1)} %convolution_convert_fusion.32, bf16[3,128,256]{2,1,0:T(8,128)(2,1)S(1)} %get-tuple-element.58), kind=kOutput, calls=%fused_computation.181 | convolution fusion | flops 25493504 | bytes 294912 | tf_op jit(solution)/shard_map/ct,cp->tp/dot_general | solution.py:228
  32.6 0.3 convolution_convert_fusion.8
  33.1 2.7 %collective-permute-start.13 = (bf16[88,1024]{1,0:T(8,128)(2,1)S(1)}, bf16[88,1024]{1,0:T(8,128)(2,1)S(1)}, u32[]{:S(2)}, u32[]{:S(2)}) collective-permute-start(bf16[88,1024]{1,0:T(8,128)(2,1)S(1)} %convolution_convert_fusion.22), channel_id=1, source_target_pairs={{0,4},{4,0},{8,12},{12,8},{1,5},{5,1},{9,13},{13,9},{2,6},{6,2},{1... | collective-permute-start | bytes 540680 | tf_op jit(solution)/shard_map/ppermute | solution.py:32
  36.0 3.4 %collective-permute-done.14 = bf16[88,1280]{1,0:T(8,128)(2,1)S(1)} collective-permute-done((bf16[88,1280]{1,0:T(8,128)(2,1)S(1)}, bf16[88,1280]{1,0:T(8,128)(2,1)S(1)}, u32[]{:S(2)}, u32[]{:S(2)}) %collective-permute-start.14) | collective-permute-done | bytes 225312 | tf_op jit(solution)/shard_map/ppermute | solution.py:32
  39.4 0.2 convolution_convert_fusion.7
  40.0 1.1 %constant_dynamic-update-slice_fusion.4 = bf16[4096,128]{1,0:T(8,128)(2,1)} fusion(bf16[4096,128]{1,0:T(8,128)(2,1)} %constant_dynamic-update-slice_fusion.5, bf16[1,128,128]{2,1,0:T(8,128)(2,1)S(1)} %copy-done.5, bf16[88,640]{1,0:T(8,128)(2,1)S(1)} %collective-permute-done.15, bf16[128,640]{1,0:T(8,128)(2,1)S(1)} %convolution_convert_fusion.24, ...), kind=kOutput, calls=%fused_computation.180 | convolution fusion | flops 64225280 | bytes 538624 | tf_op jit(solution)/shard_map/ct,cp->tp/dot_general | solution.py:228
  41.1 0.9 %collective-permute-done.13 = bf16[88,1024]{1,0:T(8,128)(2,1)S(1)} collective-permute-done((bf16[88,1024]{1,0:T(8,128)(2,1)S(1)}, bf16[88,1024]{1,0:T(8,128)(2,1)S(1)}, u32[]{:S(2)}, u32[]{:S(2)}) %collective-permute-start.13) | collective-permute-done | bytes 180256 | tf_op jit(solution)/shard_map/ppermute | solution.py:32
  42.2 1.2 %constant_dynamic-update-slice_fusion.3 = bf16[4096,128]{1,0:T(8,128)(2,1)} fusion(bf16[4096,128]{1,0:T(8,128)(2,1)} %constant_dynamic-update-slice_fusion.4, bf16[1,128,128]{2,1,0:T(8,128)(2,1)S(1)} %copy-done.5, bf16[88,896]{1,0:T(8,128)(2,1)S(1)} %collective-permute-done.11, bf16[128,896]{1,0:T(8,128)(2,1)S(1)} %copy-done.6, ...), kind=kOutput, calls=%fused_computation.179 | convolution fusion | flops 89915392 | bytes 714752 | tf_op jit(solution)/shard_map/ct,cp->tp/dot_general | solution.py:228
  43.4 1.1 %collective-permute-start.16 = (bf16[8,64]{1,0:T(8,128)(2,1)S(1)}, bf16[8,64]{1,0:T(8,128)(2,1)S(1)}, u32[]{:S(2)}, u32[]{:S(2)}) collective-permute-start(bf16[8,64]{1,0:T(8,128)(2,1)S(1)} %slice_maximum_fusion), channel_id=1, source_target_pairs={{0,2},{2,0},{1,3},{3,1},{4,6},{6,4},{5,7},{7,5},{8,10},{10,8},{9,1... | collective-permute-start | bytes 3080 | tf_op jit(solution)/shard_map/ppermute | solution.py:32
  44.7 2.5 %collective-permute-start.18 = (bf16[88,1024]{1,0:T(8,128)(2,1)S(1)}, bf16[88,1024]{1,0:T(8,128)(2,1)S(1)}, u32[]{:S(2)}, u32[]{:S(2)}) collective-permute-start(bf16[88,1024]{1,0:T(8,128)(2,1)S(1)} %convolution_convert_fusion.21), channel_id=1, source_target_pairs={{0,8},{8,0},{4,12},{12,4},{1,9},{9,1},{5,13},{13,5},{2,10},{10,2},... | collective-permute-start | bytes 540680 | tf_op jit(solution)/shard_map/ppermute | solution.py:32
  47.2 0.6 %slice.179 = bf16[1,1]{1,0:T(2,128)(2,1)} slice(bf16[8,64]{1,0:T(8,128)(2,1)S(1)} %max.11), slice={[0:1], [0:1]} | slice | bytes 4 | tf_op jit(solution)/shard_map/slice | solution.py:322
  48.5 5.5 %collective-permute-done.17 = bf16[88,1280]{1,0:T(8,128)(2,1)S(1)} collective-permute-done((bf16[88,1280]{1,0:T(8,128)(2,1)S(1)}, bf16[88,1280]{1,0:T(8,128)(2,1)S(1)}, u32[]{:S(2)}, u32[]{:S(2)}) %collective-permute-start.17) | collective-permute-done | bytes 225312 | tf_op jit(solution)/shard_map/ppermute | solution.py:32
  54.0 1.2 %constant_dynamic-update-slice_fusion.2 = bf16[4096,128]{1,0:T(8,128)(2,1)} fusion(bf16[4096,128]{1,0:T(8,128)(2,1)} %constant_dynamic-update-slice_fusion.3, bf16[1,128,128]{2,1,0:T(8,128)(2,1)S(1)} %copy-done.5, bf16[88,1280]{1,0:T(8,128)(2,1)S(1)} %collective-permute-done.17, bf16[128,1280]{1,0:T(8,128)(2,1)S(1)} %convolution_convert_fusion.7, ...), kind=kOutput, calls=%fused_computation.178 | convolution fusion | flops 128450560 | bytes 978944 | tf_op jit(solution)/shard_map/ct,cp->tp/dot_general | solution.py:228
  55.3 0.7 %collective-permute-done.18 = bf16[88,1024]{1,0:T(8,128)(2,1)S(1)} collective-permute-done((bf16[88,1024]{1,0:T(8,128)(2,1)S(1)}, bf16[88,1024]{1,0:T(8,128)(2,1)S(1)}, u32[]{:S(2)}, u32[]{:S(2)}) %collective-permute-start.18) | collective-permute-done | bytes 180256 | tf_op jit(solution)/shard_map/ppermute | solution.py:32
  56.0 1.2 %fusion.24 = bf16[4096,128]{1,0:T(8,128)(2,1)} fusion(bf16[4096,128]{1,0:T(8,128)(2,1)} %constant_dynamic-update-slice_fusion.2, bf16[88,1024]{1,0:T(8,128)(2,1)S(1)} %collective-permute-done.18, bf16[128,1024]{1,0:T(8,128)(2,1)S(1)} %convolution_convert_fusion.14, bf16[3,128,256]{2,1,0:T(8,128)(2,1)S(1)} %get-tuple-element.68, ...), kind=kOutput, calls=%fused_computation.43 | convolution fusion | flops 102760448 | bytes 802816 | tf_op jit(solution)/shard_map/ct,cp->tp/dot_general | solution.py:228
  (58 shorter events, 4.5 us)
Async XLA Ops:
  0.0 4.8 %copy-start.4 = (s32[1,3,64]{2,0,1:T(1,128)S(1)}, s32[1,3,64]{2,0,1:T(1,128)}, u32[]{:S(2)}) copy-start(s32[1,3,64]{2,0,1:T(1,128)} %param.9) | copy-start | bytes 2308
  0.0 4.8 %copy-start.3 = (bf16[1,3,64,128]{3,2,1,0:T(8,128)(2,1)S(1)}, bf16[1,3,64,128]{3,2,1,0:T(8,128)(2,1)}, u32[]{:S(2)}) copy-start(bf16[1,3,64,128]{3,2,1,0:T(8,128)(2,1)} %refs_1_.3) | copy-start | bytes 147460
  1.7 5.5 %collective-permute-start.3 = (bf16[128,256]{1,0:T(8,128)(2,1)S(1)}, bf16[128,256]{1,0:T(8,128)(2,1)S(1)}, u32[]{:S(2)}, u32[]{:S(2)}) collective-permute-start(bf16[128,256]{1,0:T(8,128)(2,1)S(1)} %get-tuple-element.55), channel_id=1, source_target_pairs={{0,2},{2,0},{1,3},{3,1},{4,6},{6,4},{5,7},{7,5},{8,10},{10,8},{9,1... | collective-permute-start | bytes 196616 | tf_op jit(solution)/shard_map/ppermute | solution.py:32
  4.7 6.8 %collective-permute-start.5 = (bf16[128,640]{1,0:T(8,128)(2,1)S(1)}, bf16[128,640]{1,0:T(8,128)(2,1)S(1)}, u32[]{:S(2)}, u32[]{:S(2)}) collective-permute-start(bf16[128,640]{1,0:T(8,128)(2,1)S(1)} %get-tuple-element.59), channel_id=1, source_target_pairs={{0,2},{2,0},{1,3},{3,1},{4,6},{6,4},{5,7},{7,5},{8,10},{10,8},{9,1... | collective-permute-start | bytes 491528 | tf_op jit(solution)/shard_map/ppermute | solution.py:32
  6.0 11.5 %copy-start = (bf16[4096,128]{1,0:T(8,128)(2,1)S(1)}, bf16[4096,128]{1,0:T(8,128)(2,1)}, u32[]{:S(2)}) copy-start(bf16[4096,128]{1,0:T(8,128)(2,1)} %refs_1_.2) | copy-start | bytes 3145732
  6.0 11.5 %copy-start.2 = (bf16[1,128,128]{2,1,0:T(8,128)(2,1)S(1)}, bf16[1,128,128]{2,1,0:T(8,128)(2,1)}, u32[]{:S(2)}) copy-start(bf16[1,128,128]{2,1,0:T(8,128)(2,1)} %refs_0_.1) | copy-start | bytes 98308
  7.4 5.1 %collective-permute-start.4 = (bf16[128,384]{1,0:T(8,128)(2,1)S(1)}, bf16[128,384]{1,0:T(8,128)(2,1)S(1)}, u32[]{:S(2)}, u32[]{:S(2)}) collective-permute-start(bf16[128,384]{1,0:T(8,128)(2,1)S(1)} %pad_maximum_fusion.9), channel_id=1, source_target_pairs={{0,4},{4,0},{8,12},{12,8},{1,5},{5,1},{9,13},{13,9},{2,6},{6,2},{1... | collective-permute-start | bytes 294920 | tf_op jit(solution)/shard_map/ppermute | solution.py:32
  9.9 9.7 %collective-permute-start.7 = (bf16[128,896]{1,0:T(8,128)(2,1)S(1)}, bf16[128,896]{1,0:T(8,128)(2,1)S(1)}, u32[]{:S(2)}, u32[]{:S(2)}) collective-permute-start(bf16[128,896]{1,0:T(8,128)(2,1)S(1)} %get-tuple-element.62), channel_id=1, source_target_pairs={{0,2},{2,0},{1,3},{3,1},{4,6},{6,4},{5,7},{7,5},{8,10},{10,8},{9,1... | collective-permute-start | bytes 688136 | tf_op jit(solution)/shard_map/ppermute | solution.py:32
  12.8 7.2 %collective-permute-start.6 = (bf16[128,384]{1,0:T(8,128)(2,1)S(1)}, bf16[128,384]{1,0:T(8,128)(2,1)S(1)}, u32[]{:S(2)}, u32[]{:S(2)}) collective-permute-start(bf16[128,384]{1,0:T(8,128)(2,1)S(1)} %pad_maximum_fusion.10), channel_id=1, source_target_pairs={{0,8},{8,0},{4,12},{12,4},{1,9},{9,1},{5,13},{13,5},{2,10},{10,2},... | collective-permute-start | bytes 294920 | tf_op jit(solution)/shard_map/ppermute | solution.py:32
  15.9 8.2 %collective-permute-start.10 = (bf16[128,640]{1,0:T(8,128)(2,1)S(1)}, bf16[128,640]{1,0:T(8,128)(2,1)S(1)}, u32[]{:S(2)}, u32[]{:S(2)}) collective-permute-start(bf16[128,640]{1,0:T(8,128)(2,1)S(1)} %convolution_convert_fusion.25), channel_id=1, source_target_pairs={{0,4},{4,0},{8,12},{12,8},{1,5},{5,1},{9,13},{13,9},{2,6},{6,2},{1... | collective-permute-start | bytes 491528 | tf_op jit(solution)/shard_map/ppermute | solution.py:32
  17.8 9.3 %collective-permute-start.9 = (bf16[128,1280]{1,0:T(8,128)(2,1)S(1)}, bf16[128,1280]{1,0:T(8,128)(2,1)S(1)}, u32[]{:S(2)}, u32[]{:S(2)}) collective-permute-start(bf16[128,1280]{1,0:T(8,128)(2,1)S(1)} %convolution_convert_fusion.9), channel_id=1, source_target_pairs={{0,2},{2,0},{1,3},{3,1},{4,6},{6,4},{5,7},{7,5},{8,10},{10,8},{9,1... | collective-permute-start | bytes 983048 | tf_op jit(solution)/shard_map/ppermute | solution.py:32
  20.6 6.8 %collective-permute-start.8 = (bf16[88,896]{1,0:T(8,128)(2,1)S(1)}, bf16[88,896]{1,0:T(8,128)(2,1)S(1)}, u32[]{:S(2)}, u32[]{:S(2)}) collective-permute-start(bf16[88,896]{1,0:T(8,128)(2,1)S(1)} %convolution_convert_fusion.28), channel_id=1, source_target_pairs={{0,4},{4,0},{8,12},{12,8},{1,5},{5,1},{9,13},{13,9},{2,6},{6,2},{1... | collective-permute-start | bytes 473096 | tf_op jit(solution)/shard_map/ppermute | solution.py:32
  24.6 15.4 %collective-permute-start.15 = (bf16[88,640]{1,0:T(8,128)(2,1)S(1)}, bf16[88,640]{1,0:T(8,128)(2,1)S(1)}, u32[]{:S(2)}, u32[]{:S(2)}) collective-permute-start(bf16[88,640]{1,0:T(8,128)(2,1)S(1)} %convolution_convert_fusion.29), channel_id=1, source_target_pairs={{0,8},{8,0},{4,12},{12,4},{1,9},{9,1},{5,13},{13,5},{2,10},{10,2},... | collective-permute-start | bytes 337928 | tf_op jit(solution)/shard_map/ppermute | solution.py:32
  25.5 7.4 %collective-permute-start.12 = (bf16[128,1024]{1,0:T(8,128)(2,1)S(1)}, bf16[128,1024]{1,0:T(8,128)(2,1)S(1)}, u32[]{:S(2)}, u32[]{:S(2)}) collective-permute-start(bf16[128,1024]{1,0:T(8,128)(2,1)S(1)} %convolution_convert_fusion.16), channel_id=1, source_target_pairs={{0,2},{2,0},{1,3},{3,1},{4,6},{6,4},{5,7},{7,5},{8,10},{10,8},{9,1... | collective-permute-start | bytes 786440 | tf_op jit(solution)/shard_map/ppermute | solution.py:32
  27.3 12.0 %collective-permute-start.14 = (bf16[88,1280]{1,0:T(8,128)(2,1)S(1)}, bf16[88,1280]{1,0:T(8,128)(2,1)S(1)}, u32[]{:S(2)}, u32[]{:S(2)}) collective-permute-start(bf16[88,1280]{1,0:T(8,128)(2,1)S(1)} %convolution_convert_fusion.11), channel_id=1, source_target_pairs={{0,4},{4,0},{8,12},{12,8},{1,5},{5,1},{9,13},{13,9},{2,6},{6,2},{1... | collective-permute-start | bytes 675848 | tf_op jit(solution)/shard_map/ppermute | solution.py:32
  28.4 3.2 %copy-start.5 = (bf16[1,128,128]{2,1,0:T(8,128)(2,1)S(1)}, bf16[1,128,128]{2,1,0:T(8,128)(2,1)}, u32[]{:S(2)}) copy-start(bf16[1,128,128]{2,1,0:T(8,128)(2,1)} %param.11) | copy-start | bytes 98308
  28.6 13.6 %collective-permute-start.11 = (bf16[88,896]{1,0:T(8,128)(2,1)S(1)}, bf16[88,896]{1,0:T(8,128)(2,1)S(1)}, u32[]{:S(2)}, u32[]{:S(2)}) collective-permute-start(bf16[88,896]{1,0:T(8,128)(2,1)S(1)} %convolution_convert_fusion.27), channel_id=1, source_target_pairs={{0,8},{8,0},{4,12},{12,4},{1,9},{9,1},{5,13},{13,5},{2,10},{10,2},... | collective-permute-start | bytes 473096 | tf_op jit(solution)/shard_map/ppermute | solution.py:32
  33.1 8.9 %collective-permute-start.13 = (bf16[88,1024]{1,0:T(8,128)(2,1)S(1)}, bf16[88,1024]{1,0:T(8,128)(2,1)S(1)}, u32[]{:S(2)}, u32[]{:S(2)}) collective-permute-start(bf16[88,1024]{1,0:T(8,128)(2,1)S(1)} %convolution_convert_fusion.22), channel_id=1, source_target_pairs={{0,4},{4,0},{8,12},{12,8},{1,5},{5,1},{9,13},{13,9},{2,6},{6,2},{1... | collective-permute-start | bytes 540680 | tf_op jit(solution)/shard_map/ppermute | solution.py:32
  39.9 14.1 %collective-permute-start.17 = (bf16[88,1280]{1,0:T(8,128)(2,1)S(1)}, bf16[88,1280]{1,0:T(8,128)(2,1)S(1)}, u32[]{:S(2)}, u32[]{:S(2)}) collective-permute-start(bf16[88,1280]{1,0:T(8,128)(2,1)S(1)} %convolution_convert_fusion.10), channel_id=1, source_target_pairs={{0,8},{8,0},{4,12},{12,4},{1,9},{9,1},{5,13},{13,5},{2,10},{10,2},... | collective-permute-start | bytes 675848 | tf_op jit(solution)/shard_map/ppermute | solution.py:32
  41.1 1.1 %copy-start.6 = (bf16[128,896]{1,0:T(8,128)(2,1)S(1)}, bf16[128,896]{1,0:T(8,128)(2,1)}, u32[]{:S(2)}) copy-start(bf16[128,896]{1,0:T(8,128)(2,1)} %convolution_convert_fusion.19) | copy-start | bytes 688132
  43.4 3.9 %collective-permute-start.16 = (bf16[8,64]{1,0:T(8,128)(2,1)S(1)}, bf16[8,64]{1,0:T(8,128)(2,1)S(1)}, u32[]{:S(2)}, u32[]{:S(2)}) collective-permute-start(bf16[8,64]{1,0:T(8,128)(2,1)S(1)} %slice_maximum_fusion), channel_id=1, source_target_pairs={{0,2},{2,0},{1,3},{3,1},{4,6},{6,4},{5,7},{7,5},{8,10},{10,8},{9,1... | collective-permute-start | bytes 3080 | tf_op jit(solution)/shard_map/ppermute | solution.py:32
  44.7 11.3 %collective-permute-start.18 = (bf16[88,1024]{1,0:T(8,128)(2,1)S(1)}, bf16[88,1024]{1,0:T(8,128)(2,1)S(1)}, u32[]{:S(2)}, u32[]{:S(2)}) collective-permute-start(bf16[88,1024]{1,0:T(8,128)(2,1)S(1)} %convolution_convert_fusion.21), channel_id=1, source_target_pairs={{0,8},{8,0},{4,12},{12,4},{1,9},{9,1},{5,13},{13,5},{2,10},{10,2},... | collective-permute-start | bytes 540680 | tf_op jit(solution)/shard_map/ppermute | solution.py:32

commit v13 on v12

--- a/solution.py
+++ b/solution.py
@@ -5,13 +5,13 @@
 from jax.experimental.pallas import tpu as pltpu
 from jax.sharding import PartitionSpec as P
 
-SHARES = (2, 5, 7, 10, 8)
+SHARES = (1, 5, 8, 10, 8)
 FULL_PIECES = (2, 1)
 EARLY_PIECES = 3
 COUNT_PIECE = 2
 LOOK = (3, -1)
 ORDER = (
-    (0, 0), (0, 1), (1, 0), (0, 2), (1, 1), (2, 0), (0, 3), (1, 2), LOOK, (2, 1), (0, 4), (1, 3),
+    (0, 0), (0, 1), (0, 2), (1, 0), (0, 3), (1, 1), (2, 0), (1, 2), LOOK, (2, 1), (0, 4), (1, 3),
     (2, 2), (3, 0), (1, 4), (2, 3), (3, 1), (2, 4), (3, 2), (3, 3), (3, 4),
 )
 KERNEL_VMEM = 16 * 1024 * 1024
@@ -305,8 +305,6 @@
                     most = jnp.maximum(most, from_partner(most, hop))
             continue
         outgoing = own
-        if level == 0 and 1 < piece < EARLY_PIECES:
-            outgoing = after(own, previous)
         if compact(level, piece):
             outgoing = times(compact_rows(matrix, theirs[level]), value)
         if piece == 0 and level >= wide:

time: 57.3 us -> 57.7 us (level)
  starting transfers between devices: 25.8 us -> 23.9 us
  matrix products: 11.3 us -> 12.7 us
  waiting for transfers between devices: 15.4 us -> 16 us
    ppermute x16, starting transfers between devices: 25.8 us -> 23.9 us  [from_partner(): return lax.ppermute(block, hop[0], route(*hop))]
    dot_general x17, matrix products: 4.38 us -> 5.84 us  [times(): jnp.dot(matrix, value, preferred_element_type=jnp.float32)]
    ppermute x16, waiting for transfers between devices: 15.4 us -> 16 us  [from_partner(): return lax.ppermute(block, hop[0], route(*hop))]
  transfers between devices with their start and end apart: 16 -> 16, of which waited for: 7 -> 8; matrix products, arithmetic and copies ran while one was open for 19% -> 21% of each run, Pallas kernels for 2% -> 2%
where the time goes in v13:
time: 57.7 us; the launch traced here: 57.6 us
  starting transfers between devices  23.9 us (41%)
  waiting for transfers between devices  16 us (28%)
  matrix products  12.7 us (22%)
  Pallas kernels  2.82 us (5%)
  local copies, waits for them, and re-layouts  1.08 us (2%)
  between operations  0.95 us (2%)
    ppermute x16, starting transfers between devices, from_partner(): return lax.ppermute(block, hop[0], route(*hop))  23.9 us
    ppermute x16, waiting for transfers between devices, from_partner(): return lax.ppermute(block, hop[0], route(*hop))  16 us
    dot_general x17, matrix products, times(): jnp.dot(matrix, value, preferred_element_type=jnp.float32)  5.84 us
    dot_general x5, matrix products, evaluated(): jnp.einsum('ct,cp->tp', coeffs, evaluation, preferred_element_type=jnp.fl...  5.63 us
    pallas_call x1, Pallas kernels, early(): pl.pallas_call(lambda *refs: early_kernel(starts, *refs), out_shape=[jax....  1.63 us
    pallas_call x1, Pallas kernels, tables(): pl.pallas_call(lambda *refs: tables_kernel(wide, room, *refs), out_shape=...  1.19 us
  transfers between devices with their start and end apart: 16, of which 8 were waited for; matrix products, arithmetic and copies ran while one was open for 21% of the time, Pallas kernels for 2%

profile of v13, /device:TPU:0, one launch (start us, length us, event | category | flops | bytes accessed | tf_op | source)
XLA Modules:
  0.0 57.6 jit_solution(17045305818872559069)
XLA Ops:
  0.0 1.6 %early.1 = (bf16[128,128]{1,0:T(8,128)(2,1)S(1)}, bf16[128,640]{1,0:T(8,128)(2,1)S(1)}, bf16[128,1024]{1,0:T(8,128)(2,1)S(1)}) custom-call(bf16[1,128,128]{2,1,0:T(8,128)(2,1)} %refs_0_.1, bf16[4096,128]{1,0:T(8,128)(2,1)} %refs_1_.2), custom_call_target="tpu_custom_call" | custom-call | flops 58720256 | bytes 917504 | tf_op jit(solution)/shard_map/early/pallas_call | solution.py:68
  1.6 3.0 %collective-permute-start.3 = (bf16[128,128]{1,0:T(8,128)(2,1)S(1)}, bf16[128,128]{1,0:T(8,128)(2,1)S(1)}, u32[]{:S(2)}, u32[]{:S(2)}) collective-permute-start(bf16[128,128]{1,0:T(8,128)(2,1)S(1)} %get-tuple-element.54), channel_id=1, source_target_pairs={{0,2},{2,0},{1,3},{3,1},{4,6},{6,4},{5,7},{7,5},{8,10},{10,8},{9,1... | collective-permute-start | bytes 98312 | tf_op jit(solution)/shard_map/ppermute | solution.py:32
  4.7 1.9 %collective-permute-start.7 = (bf16[128,1024]{1,0:T(8,128)(2,1)S(1)}, bf16[128,1024]{1,0:T(8,128)(2,1)S(1)}, u32[]{:S(2)}, u32[]{:S(2)}) collective-permute-start(bf16[128,1024]{1,0:T(8,128)(2,1)S(1)} %get-tuple-element.58), channel_id=1, source_target_pairs={{0,2},{2,0},{1,3},{3,1},{4,6},{6,4},{5,7},{7,5},{8,10},{10,8},{9,1... | collective-permute-start | bytes 786440 | tf_op jit(solution)/shard_map/ppermute | solution.py:32
  6.7 1.2 %tables.1 = (bf16[3,128,256]{2,1,0:T(8,128)(2,1)S(1)}, bf16[3,128,256]{2,1,0:T(8,128)(2,1)S(1)}, bf16[3,128,128]{2,1,0:T(8,128)(2,1)S(1)}) custom-call(s32[3,1,64]{2,1,0:T(1,128)S(1)} %bitcast.118, bf16[1,3,64,128]{3,2,1,0:T(8,128)(2,1)S(1)} %copy-done.3), custom_call_target="tpu_custom_call" | custom-call | flops 50000000 | bytes 600000 | tf_op jit(solution)/shard_map/tables/pallas_call | solution.py:151
  8.1 1.6 %collective-permute-start.4 = (bf16[128,256]{1,0:T(8,128)(2,1)S(1)}, bf16[128,256]{1,0:T(8,128)(2,1)S(1)}, u32[]{:S(2)}, u32[]{:S(2)}) collective-permute-start(bf16[128,256]{1,0:T(8,128)(2,1)S(1)} %pad_maximum_fusion.9), channel_id=1, source_target_pairs={{0,4},{4,0},{8,12},{12,8},{1,5},{5,1},{9,13},{13,9},{2,6},{6,2},{1... | collective-permute-start | bytes 196616 | tf_op jit(solution)/shard_map/ppermute | solution.py:32
  10.1 1.0 %collective-permute-start.9 = (bf16[128,1280]{1,0:T(8,128)(2,1)S(1)}, bf16[128,1280]{1,0:T(8,128)(2,1)S(1)}, u32[]{:S(2)}, u32[]{:S(2)}) collective-permute-start(bf16[128,1280]{1,0:T(8,128)(2,1)S(1)} %convolution_convert_fusion.9), channel_id=1, source_target_pairs={{0,2},{2,0},{1,3},{3,1},{4,6},{6,4},{5,7},{7,5},{8,10},{10,8},{9,1... | collective-permute-start | bytes 983048 | tf_op jit(solution)/shard_map/ppermute | solution.py:32
  11.1 0.7 %collective-permute-done.5 = bf16[128,640]{1,0:T(8,128)(2,1)S(1)} collective-permute-done((bf16[128,640]{1,0:T(8,128)(2,1)S(1)}, bf16[128,640]{1,0:T(8,128)(2,1)S(1)}, u32[]{:S(2)}, u32[]{:S(2)}) %collective-permute-start.5) | collective-permute-done | bytes 163872 | tf_op jit(solution)/shard_map/ppermute | solution.py:32
  12.0 1.6 %collective-permute-start.10 = (bf16[128,640]{1,0:T(8,128)(2,1)S(1)}, bf16[128,640]{1,0:T(8,128)(2,1)S(1)}, u32[]{:S(2)}, u32[]{:S(2)}) collective-permute-start(bf16[128,640]{1,0:T(8,128)(2,1)S(1)} %convolution_convert_fusion.27), channel_id=1, source_target_pairs={{0,4},{4,0},{8,12},{12,8},{1,5},{5,1},{9,13},{13,9},{2,6},{6,2},{1... | collective-permute-start | bytes 491528 | tf_op jit(solution)/shard_map/ppermute | solution.py:32
  14.0 2.6 %collective-permute-start.6 = (bf16[128,256]{1,0:T(8,128)(2,1)S(1)}, bf16[128,256]{1,0:T(8,128)(2,1)S(1)}, u32[]{:S(2)}, u32[]{:S(2)}) collective-permute-start(bf16[128,256]{1,0:T(8,128)(2,1)S(1)} %pad_maximum_fusion.10), channel_id=1, source_target_pairs={{0,8},{8,0},{4,12},{12,4},{1,9},{9,1},{5,13},{13,5},{2,10},{10,2},... | collective-permute-start | bytes 196616 | tf_op jit(solution)/shard_map/ppermute | solution.py:32
  16.7 0.7 %collective-permute-done.7 = bf16[128,1024]{1,0:T(8,128)(2,1)S(1)} collective-permute-done((bf16[128,1024]{1,0:T(8,128)(2,1)S(1)}, bf16[128,1024]{1,0:T(8,128)(2,1)S(1)}, u32[]{:S(2)}, u32[]{:S(2)}) %collective-permute-start.7) | collective-permute-done | bytes 262176 | tf_op jit(solution)/shard_map/ppermute | solution.py:32
  17.9 1.3 %collective-permute-done.6 = bf16[128,256]{1,0:T(8,128)(2,1)S(1)} collective-permute-done((bf16[128,256]{1,0:T(8,128)(2,1)S(1)}, bf16[128,256]{1,0:T(8,128)(2,1)S(1)}, u32[]{:S(2)}, u32[]{:S(2)}) %collective-permute-start.6) | collective-permute-done | bytes 65568 | tf_op jit(solution)/shard_map/ppermute | solution.py:32
  19.8 1.5 %collective-permute-start.8 = (bf16[88,1024]{1,0:T(8,128)(2,1)S(1)}, bf16[88,1024]{1,0:T(8,128)(2,1)S(1)}, u32[]{:S(2)}, u32[]{:S(2)}) collective-permute-start(bf16[88,1024]{1,0:T(8,128)(2,1)S(1)} %convolution_convert_fusion.24), channel_id=1, source_target_pairs={{0,4},{4,0},{8,12},{12,8},{1,5},{5,1},{9,13},{13,9},{2,6},{6,2},{1... | collective-permute-start | bytes 540680 | tf_op jit(solution)/shard_map/ppermute | solution.py:32
  21.6 1.8 %collective-permute-start.15 = (bf16[88,640]{1,0:T(8,128)(2,1)S(1)}, bf16[88,640]{1,0:T(8,128)(2,1)S(1)}, u32[]{:S(2)}, u32[]{:S(2)}) collective-permute-start(bf16[88,640]{1,0:T(8,128)(2,1)S(1)} %convolution_convert_fusion.29), channel_id=1, source_target_pairs={{0,8},{8,0},{4,12},{12,4},{1,9},{9,1},{5,13},{13,5},{2,10},{10,2},... | collective-permute-start | bytes 337928 | tf_op jit(solution)/shard_map/ppermute | solution.py:32
  23.6 2.0 %collective-permute-start.12 = (bf16[128,1024]{1,0:T(8,128)(2,1)S(1)}, bf16[128,1024]{1,0:T(8,128)(2,1)S(1)}, u32[]{:S(2)}, u32[]{:S(2)}) collective-permute-start(bf16[128,1024]{1,0:T(8,128)(2,1)S(1)} %convolution_convert_fusion.19), channel_id=1, source_target_pairs={{0,2},{2,0},{1,3},{3,1},{4,6},{6,4},{5,7},{7,5},{8,10},{10,8},{9,1... | collective-permute-start | bytes 786440 | tf_op jit(solution)/shard_map/ppermute | solution.py:32
  26.4 1.0 %convolution_convert_fusion.8 = bf16[128,1280]{1,0:T(8,128)(2,1)} fusion(bf16[128,1280]{1,0:T(8,128)(2,1)S(1)} %collective-permute-done.9, bf16[128,1280]{1,0:T(8,128)(2,1)S(1)} %convolution_convert_fusion.9, bf16[3,128,256]{2,1,0:T(8,128)(2,1)S(1)} %get-tuple-element.57), kind=kOutput, calls=%fused_computation.33 | convolution fusion | flops 85360640 | bytes 1048576 | tf_op jit(solution)/shard_map/dot_general | solution.py:218
  27.4 0.9 %convolution_convert_fusion.18 = bf16[128,1024]{1,0:T(8,128)(2,1)} fusion(bf16[88,1024]{1,0:T(8,128)(2,1)S(1)} %collective-permute-done.8, bf16[128,1024]{1,0:T(8,128)(2,1)S(1)} %convolution_convert_fusion.20, bf16[3,128,256]{2,1,0:T(8,128)(2,1)S(1)} %get-tuple-element.66), kind=kOutput, calls=%fused_computation.49 | convolution fusion | flops 69074944 | bytes 770048 | tf_op jit(solution)/shard_map/dot_general | solution.py:218
  28.5 2.6 %collective-permute-start.11 = (bf16[88,1024]{1,0:T(8,128)(2,1)S(1)}, bf16[88,1024]{1,0:T(8,128)(2,1)S(1)}, u32[]{:S(2)}, u32[]{:S(2)}) collective-permute-start(bf16[88,1024]{1,0:T(8,128)(2,1)S(1)} %convolution_convert_fusion.23), channel_id=1, source_target_pairs={{0,8},{8,0},{4,12},{12,4},{1,9},{9,1},{5,13},{13,5},{2,10},{10,2},... | collective-permute-start | bytes 540680 | tf_op jit(solution)/shard_map/ppermute | solution.py:32
  31.1 0.9 %constant_dynamic-update-slice_fusion.5 = bf16[4096,128]{1,0:T(8,128)(2,1)} fusion(bf16[1,128,128]{2,1,0:T(8,128)(2,1)S(1)} %copy-done.5, bf16[128,128]{1,0:T(8,128)(2,1)S(1)} %slice.178, bf16[128,128]{1,0:T(8,128)(2,1)S(1)} %convolution_convert_fusion.32, bf16[3,128,256]{2,1,0:T(8,128)(2,1)S(1)} %get-tuple-element.57), kind=kOutput, calls=%fused_computation.180 | convolution fusion | flops 12746751 | bytes 196608 | tf_op jit(solution)/shard_map/ct,cp->tp/dot_general | solution.py:228
  32.3 0.5 collective-permute-start.13
  32.8 5.0 %collective-permute-done.14 = bf16[88,1280]{1,0:T(8,128)(2,1)S(1)} collective-permute-done((bf16[88,1280]{1,0:T(8,128)(2,1)S(1)}, bf16[88,1280]{1,0:T(8,128)(2,1)S(1)}, u32[]{:S(2)}, u32[]{:S(2)}) %collective-permute-start.14) | collective-permute-done | bytes 225312 | tf_op jit(solution)/shard_map/ppermute | solution.py:32
  37.8 1.0 %convolution_convert_fusion.7 = bf16[128,1280]{1,0:T(8,128)(2,1)} fusion(bf16[88,1280]{1,0:T(8,128)(2,1)S(1)} %collective-permute-done.14, bf16[128,1280]{1,0:T(8,128)(2,1)S(1)} %copy-done.6, bf16[3,128,256]{2,1,0:T(8,128)(2,1)S(1)} %get-tuple-element.66), kind=kOutput, calls=%fused_computation.32 | convolution fusion | flops 86343680 | bytes 946176 | tf_op jit(solution)/shard_map/dot_general | solution.py:218
  39.1 1.4 %collective-permute-start.17 = (bf16[88,1280]{1,0:T(8,128)(2,1)S(1)}, bf16[88,1280]{1,0:T(8,128)(2,1)S(1)}, u32[]{:S(2)}, u32[]{:S(2)}) collective-permute-start(bf16[88,1280]{1,0:T(8,128)(2,1)S(1)} %convolution_convert_fusion.10), channel_id=1, source_target_pairs={{0,8},{8,0},{4,12},{12,4},{1,9},{9,1},{5,13},{13,5},{2,10},{10,2},... | collective-permute-start | bytes 675848 | tf_op jit(solution)/shard_map/ppermute | solution.py:32
  40.5 1.1 %constant_dynamic-update-slice_fusion.4 = bf16[4096,128]{1,0:T(8,128)(2,1)} fusion(bf16[4096,128]{1,0:T(8,128)(2,1)} %constant_dynamic-update-slice_fusion.5, bf16[1,128,128]{2,1,0:T(8,128)(2,1)S(1)} %copy-done.5, bf16[88,640]{1,0:T(8,128)(2,1)S(1)} %collective-permute-done.15, bf16[128,640]{1,0:T(8,128)(2,1)S(1)} %convolution_convert_fusion.26, ...), kind=kOutput, calls=%fused_computation.179 | convolution fusion | flops 64225280 | bytes 538624 | tf_op jit(solution)/shard_map/ct,cp->tp/dot_general | solution.py:228
  42.4 0.4 copy-done.7
  42.8 1.2 %constant_dynamic-update-slice_fusion.3 = bf16[4096,128]{1,0:T(8,128)(2,1)} fusion(bf16[4096,128]{1,0:T(8,128)(2,1)} %constant_dynamic-update-slice_fusion.4, bf16[1,128,128]{2,1,0:T(8,128)(2,1)S(1)} %copy-done.5, bf16[88,1024]{1,0:T(8,128)(2,1)S(1)} %collective-permute-done.11, bf16[128,1024]{1,0:T(8,128)(2,1)S(1)} %copy-done.7, ...), kind=kOutput, calls=%fused_computation.178 | convolution fusion | flops 102760448 | bytes 802816 | tf_op jit(solution)/shard_map/ct,cp->tp/dot_general | solution.py:228
  44.2 1.7 %collective-permute-start.18 = (bf16[88,1024]{1,0:T(8,128)(2,1)S(1)}, bf16[88,1024]{1,0:T(8,128)(2,1)S(1)}, u32[]{:S(2)}, u32[]{:S(2)}) collective-permute-start(bf16[88,1024]{1,0:T(8,128)(2,1)S(1)} %convolution_convert_fusion.21), channel_id=1, source_target_pairs={{0,8},{8,0},{4,12},{12,4},{1,9},{9,1},{5,13},{13,5},{2,10},{10,2},... | collective-permute-start | bytes 540680 | tf_op jit(solution)/shard_map/ppermute | solution.py:32
  45.9 1.7 %collective-permute-done.16 = bf16[8,64]{1,0:T(8,128)(2,1)S(1)} collective-permute-done((bf16[8,64]{1,0:T(8,128)(2,1)S(1)}, bf16[8,64]{1,0:T(8,128)(2,1)S(1)}, u32[]{:S(2)}, u32[]{:S(2)}) %collective-permute-start.16) | collective-permute-done | bytes 1056 | tf_op jit(solution)/shard_map/ppermute | solution.py:32
  47.6 0.6 %slice.179 = bf16[1,1]{1,0:T(2,128)(2,1)} slice(bf16[8,64]{1,0:T(8,128)(2,1)S(1)} %max.11), slice={[0:1], [0:1]} | slice | bytes 4 | tf_op jit(solution)/shard_map/slice | solution.py:320
  48.8 5.6 %collective-permute-done.17 = bf16[88,1280]{1,0:T(8,128)(2,1)S(1)} collective-permute-done((bf16[88,1280]{1,0:T(8,128)(2,1)S(1)}, bf16[88,1280]{1,0:T(8,128)(2,1)S(1)}, u32[]{:S(2)}, u32[]{:S(2)}) %collective-permute-start.17) | collective-permute-done | bytes 225312 | tf_op jit(solution)/shard_map/ppermute | solution.py:32
  54.5 1.2 %constant_dynamic-update-slice_fusion.2 = bf16[4096,128]{1,0:T(8,128)(2,1)} fusion(bf16[4096,128]{1,0:T(8,128)(2,1)} %constant_dynamic-update-slice_fusion.3, bf16[1,128,128]{2,1,0:T(8,128)(2,1)S(1)} %copy-done.5, bf16[88,1280]{1,0:T(8,128)(2,1)S(1)} %collective-permute-done.17, bf16[128,1280]{1,0:T(8,128)(2,1)S(1)} %copy-done.8, ...), kind=kOutput, calls=%fused_computation.177 | convolution fusion | flops 128450560 | bytes 978944 | tf_op jit(solution)/shard_map/ct,cp->tp/dot_general | solution.py:228
  55.7 0.7 %collective-permute-done.18 = bf16[88,1024]{1,0:T(8,128)(2,1)S(1)} collective-permute-done((bf16[88,1024]{1,0:T(8,128)(2,1)S(1)}, bf16[88,1024]{1,0:T(8,128)(2,1)S(1)}, u32[]{:S(2)}, u32[]{:S(2)}) %collective-permute-start.18) | collective-permute-done | bytes 180256 | tf_op jit(solution)/shard_map/ppermute | solution.py:32
  56.4 1.2 %fusion.24 = bf16[4096,128]{1,0:T(8,128)(2,1)} fusion(bf16[4096,128]{1,0:T(8,128)(2,1)} %constant_dynamic-update-slice_fusion.2, bf16[88,1024]{1,0:T(8,128)(2,1)S(1)} %collective-permute-done.18, bf16[128,1024]{1,0:T(8,128)(2,1)S(1)} %convolution_convert_fusion.14, bf16[3,128,256]{2,1,0:T(8,128)(2,1)S(1)} %get-tuple-element.66, ...), kind=kOutput, calls=%fused_computation.43 | convolution fusion | flops 102760448 | bytes 802816 | tf_op jit(solution)/shard_map/ct,cp->tp/dot_general | solution.py:228
  (61 shorter events, 5.1 us)
Async XLA Ops:
  0.0 9.8 %copy-start = (bf16[4096,128]{1,0:T(8,128)(2,1)S(1)}, bf16[4096,128]{1,0:T(8,128)(2,1)}, u32[]{:S(2)}) copy-start(bf16[4096,128]{1,0:T(8,128)(2,1)} %refs_1_.2) | copy-start | bytes 3145732
  0.0 9.8 %copy-start.2 = (bf16[1,128,128]{2,1,0:T(8,128)(2,1)S(1)}, bf16[1,128,128]{2,1,0:T(8,128)(2,1)}, u32[]{:S(2)}) copy-start(bf16[1,128,128]{2,1,0:T(8,128)(2,1)} %refs_0_.1) | copy-start | bytes 98308
  0.0 6.7 %copy-start.4 = (s32[1,3,64]{2,0,1:T(1,128)S(1)}, s32[1,3,64]{2,0,1:T(1,128)}, u32[]{:S(2)}) copy-start(s32[1,3,64]{2,0,1:T(1,128)} %param.9) | copy-start | bytes 2308
  0.0 6.7 %copy-start.3 = (bf16[1,3,64,128]{3,2,1,0:T(8,128)(2,1)S(1)}, bf16[1,3,64,128]{3,2,1,0:T(8,128)(2,1)}, u32[]{:S(2)}) copy-start(bf16[1,3,64,128]{3,2,1,0:T(8,128)(2,1)} %refs_1_.3) | copy-start | bytes 147460
  1.6 6.3 %collective-permute-start.3 = (bf16[128,128]{1,0:T(8,128)(2,1)S(1)}, bf16[128,128]{1,0:T(8,128)(2,1)S(1)}, u32[]{:S(2)}, u32[]{:S(2)}) collective-permute-start(bf16[128,128]{1,0:T(8,128)(2,1)S(1)} %get-tuple-element.54), channel_id=1, source_target_pairs={{0,2},{2,0},{1,3},{3,1},{4,6},{6,4},{5,7},{7,5},{8,10},{10,8},{9,1... | collective-permute-start | bytes 98312 | tf_op jit(solution)/shard_map/ppermute | solution.py:32
  4.7 7.1 %collective-permute-start.5 = (bf16[128,640]{1,0:T(8,128)(2,1)S(1)}, bf16[128,640]{1,0:T(8,128)(2,1)S(1)}, u32[]{:S(2)}, u32[]{:S(2)}) collective-permute-start(bf16[128,640]{1,0:T(8,128)(2,1)S(1)} %get-tuple-element.60), channel_id=1, source_target_pairs={{0,2},{2,0},{1,3},{3,1},{4,6},{6,4},{5,7},{7,5},{8,10},{10,8},{9,1... | collective-permute-start | bytes 491528 | tf_op jit(solution)/shard_map/ppermute | solution.py:32
  4.7 12.7 %collective-permute-start.7 = (bf16[128,1024]{1,0:T(8,128)(2,1)S(1)}, bf16[128,1024]{1,0:T(8,128)(2,1)S(1)}, u32[]{:S(2)}, u32[]{:S(2)}) collective-permute-start(bf16[128,1024]{1,0:T(8,128)(2,1)S(1)} %get-tuple-element.58), channel_id=1, source_target_pairs={{0,2},{2,0},{1,3},{3,1},{4,6},{6,4},{5,7},{7,5},{8,10},{10,8},{9,1... | collective-permute-start | bytes 786440 | tf_op jit(solution)/shard_map/ppermute | solution.py:32
  8.1 5.5 %collective-permute-start.4 = (bf16[128,256]{1,0:T(8,128)(2,1)S(1)}, bf16[128,256]{1,0:T(8,128)(2,1)S(1)}, u32[]{:S(2)}, u32[]{:S(2)}) collective-permute-start(bf16[128,256]{1,0:T(8,128)(2,1)S(1)} %pad_maximum_fusion.9), channel_id=1, source_target_pairs={{0,4},{4,0},{8,12},{12,8},{1,5},{5,1},{9,13},{13,9},{2,6},{6,2},{1... | collective-permute-start | bytes 196616 | tf_op jit(solution)/shard_map/ppermute | solution.py:32
  10.1 15.8 %collective-permute-start.9 = (bf16[128,1280]{1,0:T(8,128)(2,1)S(1)}, bf16[128,1280]{1,0:T(8,128)(2,1)S(1)}, u32[]{:S(2)}, u32[]{:S(2)}) collective-permute-start(bf16[128,1280]{1,0:T(8,128)(2,1)S(1)} %convolution_convert_fusion.9), channel_id=1, source_target_pairs={{0,2},{2,0},{1,3},{3,1},{4,6},{6,4},{5,7},{7,5},{8,10},{10,8},{9,1... | collective-permute-start | bytes 983048 | tf_op jit(solution)/shard_map/ppermute | solution.py:32
  12.0 9.3 %collective-permute-start.10 = (bf16[128,640]{1,0:T(8,128)(2,1)S(1)}, bf16[128,640]{1,0:T(8,128)(2,1)S(1)}, u32[]{:S(2)}, u32[]{:S(2)}) collective-permute-start(bf16[128,640]{1,0:T(8,128)(2,1)S(1)} %convolution_convert_fusion.27), channel_id=1, source_target_pairs={{0,4},{4,0},{8,12},{12,8},{1,5},{5,1},{9,13},{13,9},{2,6},{6,2},{1... | collective-permute-start | bytes 491528 | tf_op jit(solution)/shard_map/ppermute | solution.py:32
  14.0 5.3 %collective-permute-start.6 = (bf16[128,256]{1,0:T(8,128)(2,1)S(1)}, bf16[128,256]{1,0:T(8,128)(2,1)S(1)}, u32[]{:S(2)}, u32[]{:S(2)}) collective-permute-start(bf16[128,256]{1,0:T(8,128)(2,1)S(1)} %pad_maximum_fusion.10), channel_id=1, source_target_pairs={{0,8},{8,0},{4,12},{12,4},{1,9},{9,1},{5,13},{13,5},{2,10},{10,2},... | collective-permute-start | bytes 196616 | tf_op jit(solution)/shard_map/ppermute | solution.py:32
  19.8 7.6 %collective-permute-start.8 = (bf16[88,1024]{1,0:T(8,128)(2,1)S(1)}, bf16[88,1024]{1,0:T(8,128)(2,1)S(1)}, u32[]{:S(2)}, u32[]{:S(2)}) collective-permute-start(bf16[88,1024]{1,0:T(8,128)(2,1)S(1)} %convolution_convert_fusion.24), channel_id=1, source_target_pairs={{0,4},{4,0},{8,12},{12,8},{1,5},{5,1},{9,13},{13,9},{2,6},{6,2},{1... | collective-permute-start | bytes 540680 | tf_op jit(solution)/shard_map/ppermute | solution.py:32
  21.6 18.9 %collective-permute-start.15 = (bf16[88,640]{1,0:T(8,128)(2,1)S(1)}, bf16[88,640]{1,0:T(8,128)(2,1)S(1)}, u32[]{:S(2)}, u32[]{:S(2)}) collective-permute-start(bf16[88,640]{1,0:T(8,128)(2,1)S(1)} %convolution_convert_fusion.29), channel_id=1, source_target_pairs={{0,8},{8,0},{4,12},{12,4},{1,9},{9,1},{5,13},{13,5},{2,10},{10,2},... | collective-permute-start | bytes 337928 | tf_op jit(solution)/shard_map/ppermute | solution.py:32
  23.6 8.5 %collective-permute-start.12 = (bf16[128,1024]{1,0:T(8,128)(2,1)S(1)}, bf16[128,1024]{1,0:T(8,128)(2,1)S(1)}, u32[]{:S(2)}, u32[]{:S(2)}) collective-permute-start(bf16[128,1024]{1,0:T(8,128)(2,1)S(1)} %convolution_convert_fusion.19), channel_id=1, source_target_pairs={{0,2},{2,0},{1,3},{3,1},{4,6},{6,4},{5,7},{7,5},{8,10},{10,8},{9,1... | collective-permute-start | bytes 786440 | tf_op jit(solution)/shard_map/ppermute | solution.py:32
  26.1 11.8 %collective-permute-start.14 = (bf16[88,1280]{1,0:T(8,128)(2,1)S(1)}, bf16[88,1280]{1,0:T(8,128)(2,1)S(1)}, u32[]{:S(2)}, u32[]{:S(2)}) collective-permute-start(bf16[88,1280]{1,0:T(8,128)(2,1)S(1)} %convolution_convert_fusion.11), channel_id=1, source_target_pairs={{0,4},{4,0},{8,12},{12,8},{1,5},{5,1},{9,13},{13,9},{2,6},{6,2},{1... | collective-permute-start | bytes 675848 | tf_op jit(solution)/shard_map/ppermute | solution.py:32
  28.3 2.8 %copy-start.5 = (bf16[1,128,128]{2,1,0:T(8,128)(2,1)S(1)}, bf16[1,128,128]{2,1,0:T(8,128)(2,1)}, u32[]{:S(2)}) copy-start(bf16[1,128,128]{2,1,0:T(8,128)(2,1)} %param.11) | copy-start | bytes 98308
  28.5 9.3 %copy-start.6 = (bf16[128,1280]{1,0:T(8,128)(2,1)S(1)}, bf16[128,1280]{1,0:T(8,128)(2,1)}, u32[]{:S(2)}) copy-start(bf16[128,1280]{1,0:T(8,128)(2,1)} %convolution_convert_fusion.8) | copy-start | bytes 983044
  28.5 13.8 %collective-permute-start.11 = (bf16[88,1024]{1,0:T(8,128)(2,1)S(1)}, bf16[88,1024]{1,0:T(8,128)(2,1)S(1)}, u32[]{:S(2)}, u32[]{:S(2)}) collective-permute-start(bf16[88,1024]{1,0:T(8,128)(2,1)S(1)} %convolution_convert_fusion.23), channel_id=1, source_target_pairs={{0,8},{8,0},{4,12},{12,4},{1,9},{9,1},{5,13},{13,5},{2,10},{10,2},... | collective-permute-start | bytes 540680 | tf_op jit(solution)/shard_map/ppermute | solution.py:32
  32.3 9.8 %collective-permute-start.13 = (bf16[88,1024]{1,0:T(8,128)(2,1)S(1)}, bf16[88,1024]{1,0:T(8,128)(2,1)S(1)}, u32[]{:S(2)}, u32[]{:S(2)}) collective-permute-start(bf16[88,1024]{1,0:T(8,128)(2,1)S(1)} %convolution_convert_fusion.22), channel_id=1, source_target_pairs={{0,4},{4,0},{8,12},{12,8},{1,5},{5,1},{9,13},{13,9},{2,6},{6,2},{1... | collective-permute-start | bytes 540680 | tf_op jit(solution)/shard_map/ppermute | solution.py:32
  39.1 15.4 %collective-permute-start.17 = (bf16[88,1280]{1,0:T(8,128)(2,1)S(1)}, bf16[88,1280]{1,0:T(8,128)(2,1)S(1)}, u32[]{:S(2)}, u32[]{:S(2)}) collective-permute-start(bf16[88,1280]{1,0:T(8,128)(2,1)S(1)} %convolution_convert_fusion.10), channel_id=1, source_target_pairs={{0,8},{8,0},{4,12},{12,4},{1,9},{9,1},{5,13},{13,5},{2,10},{10,2},... | collective-permute-start | bytes 675848 | tf_op jit(solution)/shard_map/ppermute | solution.py:32
  41.8 1.0 %copy-start.7 = (bf16[128,1024]{1,0:T(8,128)(2,1)S(1)}, bf16[128,1024]{1,0:T(8,128)(2,1)}, u32[]{:S(2)}) copy-start(bf16[128,1024]{1,0:T(8,128)(2,1)} %convolution_convert_fusion.18) | copy-start | bytes 786436
  44.0 10.5 %copy-start.8 = (bf16[128,1280]{1,0:T(8,128)(2,1)S(1)}, bf16[128,1280]{1,0:T(8,128)(2,1)}, u32[]{:S(2)}) copy-start(bf16[128,1280]{1,0:T(8,128)(2,1)} %convolution_convert_fusion.7) | copy-start | bytes 983044
  44.0 3.6 %collective-permute-start.16 = (bf16[8,64]{1,0:T(8,128)(2,1)S(1)}, bf16[8,64]{1,0:T(8,128)(2,1)S(1)}, u32[]{:S(2)}, u32[]{:S(2)}) collective-permute-start(bf16[8,64]{1,0:T(8,128)(2,1)S(1)} %slice_maximum_fusion), channel_id=1, source_target_pairs={{0,2},{2,0},{1,3},{3,1},{4,6},{6,4},{5,7},{7,5},{8,10},{10,8},{9,1... | collective-permute-start | bytes 3080 | tf_op jit(solution)/shard_map/ppermute | solution.py:32
  44.2 12.1 %collective-permute-start.18 = (bf16[88,1024]{1,0:T(8,128)(2,1)S(1)}, bf16[88,1024]{1,0:T(8,128)(2,1)S(1)}, u32[]{:S(2)}, u32[]{:S(2)}) collective-permute-start(bf16[88,1024]{1,0:T(8,128)(2,1)S(1)} %convolution_convert_fusion.21), channel_id=1, source_target_pairs={{0,8},{8,0},{4,12},{12,4},{1,9},{9,1},{5,13},{13,5},{2,10},{10,2},... | collective-permute-start | bytes 540680 | tf_op jit(solution)/shard_map/ppermute | solution.py:32

commit v14 on v13

--- a/solution.py
+++ b/solution.py
@@ -5,9 +5,9 @@
 from jax.experimental.pallas import tpu as pltpu
 from jax.sharding import PartitionSpec as P
 
-SHARES = (1, 5, 8, 10, 8)
+SHARES = (2, 5, 9, 9, 7)
 FULL_PIECES = (2, 1)
-EARLY_PIECES = 3
+EARLY_PIECES = 2
 COUNT_PIECE = 2
 LOOK = (3, -1)
 ORDER = (
@@ -296,7 +296,11 @@
             if compact(level - 1, piece):
                 value = jnp.pad(value, ((0, full.shape[2] - value.shape[0]), (0, 0)))
                 matrix = small[level - 1]
-            own = times(matrix, value)
+            if level < levels and compact(level, piece):
+                outgoing = times(compact_rows(matrix, theirs[level]), value)
+                own = times(after(matrix, outgoing), value)
+            else:
+                own = outgoing = times(matrix, value)
         if level == levels:
             done[piece] = finished = evaluated(own, evaluation)
             if piece == COUNT_PIECE:
@@ -304,9 +308,8 @@
                 for hop in hops[:wide]:
                     most = jnp.maximum(most, from_partner(most, hop))
             continue
-        outgoing = own
-        if compact(level, piece):
-            outgoing = times(compact_rows(matrix, theirs[level]), value)
+        if level == 0:
+            outgoing = own
         if piece == 0 and level >= wide:
             block = extra[level]
             if known is not None:

time: 57.7 us -> 58.5 us (1.014)
  starting transfers between devices: 23.9 us -> 30.1 us
  waiting for transfers between devices: 16 us -> 10.9 us
    ppermute x16, starting transfers between devices: 23.9 us -> 30.1 us  [from_partner(): return lax.ppermute(block, hop[0], route(*hop))]
    ppermute x16, waiting for transfers between devices: 16 us -> 10.9 us  [from_partner(): return lax.ppermute(block, hop[0], route(*hop))]
  transfers between devices with their start and end apart: 16 -> 16, of which waited for: 8 -> 7; matrix products, arithmetic and copies ran while one was open for 21% -> 22% of each run, Pallas kernels for 2% -> 2%
where the time goes in v14:
time: 58.5 us; the launch traced here: 58.3 us
  starting transfers between devices  30.1 us (51%)
  matrix products  13.1 us (22%)
  waiting for transfers between devices  10.9 us (19%)
  Pallas kernels  2.63 us (4%)
  between operations  0.94 us (2%)
  local copies, waits for them, and re-layouts  0.62 us (1%)
    ppermute x16, starting transfers between devices, from_partner(): return lax.ppermute(block, hop[0], route(*hop))  30.1 us
    ppermute x16, waiting for transfers between devices, from_partner(): return lax.ppermute(block, hop[0], route(*hop))  10.9 us
    dot_general x17, matrix products, times(): jnp.dot(matrix, value, preferred_element_type=jnp.float32)  5.9 us
    dot_general x5, matrix products, evaluated(): jnp.einsum('ct,cp->tp', coeffs, evaluation, preferred_element_type=jnp.fl...  5.65 us
    pallas_call x1, Pallas kernels, early(): pl.pallas_call(lambda *refs: early_kernel(starts, *refs), out_shape=[jax....  1.45 us
    pallas_call x1, Pallas kernels, tables(): pl.pallas_call(lambda *refs: tables_kernel(wide, room, *refs), out_shape=...  1.18 us
  transfers between devices with their start and end apart: 16, of which 7 were waited for; matrix products, arithmetic and copies ran while one was open for 22% of the time, Pallas kernels for 2%

profile of v14, /device:TPU:0, one launch (start us, length us, event | category | flops | bytes accessed | tf_op | source)
XLA Modules:
  0.0 58.3 jit_solution(11098629854954124124)
XLA Ops:
  0.0 1.4 %early.1 = (bf16[128,256]{1,0:T(8,128)(2,1)S(1)}, bf16[128,640]{1,0:T(8,128)(2,1)S(1)}) custom-call(bf16[1,128,128]{2,1,0:T(8,128)(2,1)} %refs_0_.1, bf16[4096,128]{1,0:T(8,128)(2,1)} %refs_1_.2), custom_call_target="tpu_custom_call" | custom-call | flops 29360128 | bytes 458752 | tf_op jit(solution)/shard_map/early/pallas_call | solution.py:68
  1.5 3.0 %collective-permute-start.3 = (bf16[128,256]{1,0:T(8,128)(2,1)S(1)}, bf16[128,256]{1,0:T(8,128)(2,1)S(1)}, u32[]{:S(2)}, u32[]{:S(2)}) collective-permute-start(bf16[128,256]{1,0:T(8,128)(2,1)S(1)} %get-tuple-element.61), channel_id=1, source_target_pairs={{0,2},{2,0},{1,3},{3,1},{4,6},{6,4},{5,7},{7,5},{8,10},{10,8},{9,1... | collective-permute-start | bytes 196616 | tf_op jit(solution)/shard_map/ppermute | solution.py:32
  4.8 2.0 %collective-permute-start.7 = (bf16[128,1152]{1,0:T(8,128)(2,1)S(1)}, bf16[128,1152]{1,0:T(8,128)(2,1)S(1)}, u32[]{:S(2)}, u32[]{:S(2)}) collective-permute-start(bf16[128,1152]{1,0:T(8,128)(2,1)S(1)} %convolution_convert_fusion.14), channel_id=1, source_target_pairs={{0,2},{2,0},{1,3},{3,1},{4,6},{6,4},{5,7},{7,5},{8,10},{10,8},{9,1... | collective-permute-start | bytes 884744 | tf_op jit(solution)/shard_map/ppermute | solution.py:32
  6.8 1.2 %tables.1 = (bf16[3,128,256]{2,1,0:T(8,128)(2,1)S(1)}, bf16[3,128,256]{2,1,0:T(8,128)(2,1)S(1)}, bf16[3,128,128]{2,1,0:T(8,128)(2,1)S(1)}) custom-call(s32[3,1,64]{2,1,0:T(1,128)S(1)} %bitcast.111, bf16[1,3,64,128]{3,2,1,0:T(8,128)(2,1)S(1)} %copy-done.4), custom_call_target="tpu_custom_call" | custom-call | flops 50000000 | bytes 600000 | tf_op jit(solution)/shard_map/tables/pallas_call | solution.py:151
  8.3 1.6 %collective-permute-start.4 = (bf16[128,384]{1,0:T(8,128)(2,1)S(1)}, bf16[128,384]{1,0:T(8,128)(2,1)S(1)}, u32[]{:S(2)}, u32[]{:S(2)}) collective-permute-start(bf16[128,384]{1,0:T(8,128)(2,1)S(1)} %pad_maximum_fusion.12), channel_id=1, source_target_pairs={{0,4},{4,0},{8,12},{12,8},{1,5},{5,1},{9,13},{13,9},{2,6},{6,2},{1... | collective-permute-start | bytes 294920 | tf_op jit(solution)/shard_map/ppermute | solution.py:32
  10.2 1.4 %collective-permute-start.9 = (bf16[128,1152]{1,0:T(8,128)(2,1)S(1)}, bf16[128,1152]{1,0:T(8,128)(2,1)S(1)}, u32[]{:S(2)}, u32[]{:S(2)}) collective-permute-start(bf16[128,1152]{1,0:T(8,128)(2,1)S(1)} %convolution_convert_fusion.13), channel_id=1, source_target_pairs={{0,2},{2,0},{1,3},{3,1},{4,6},{6,4},{5,7},{7,5},{8,10},{10,8},{9,1... | collective-permute-start | bytes 884744 | tf_op jit(solution)/shard_map/ppermute | solution.py:32
  11.8 1.1 %collective-permute-done.4 = bf16[128,384]{1,0:T(8,128)(2,1)S(1)} collective-permute-done((bf16[128,384]{1,0:T(8,128)(2,1)S(1)}, bf16[128,384]{1,0:T(8,128)(2,1)S(1)}, u32[]{:S(2)}, u32[]{:S(2)}) %collective-permute-start.4) | collective-permute-done | bytes 98336 | tf_op jit(solution)/shard_map/ppermute | solution.py:32
  13.1 1.6 %collective-permute-start.10 = (bf16[128,640]{1,0:T(8,128)(2,1)S(1)}, bf16[128,640]{1,0:T(8,128)(2,1)S(1)}, u32[]{:S(2)}, u32[]{:S(2)}) collective-permute-start(bf16[128,640]{1,0:T(8,128)(2,1)S(1)} %convolution_convert_fusion.26), channel_id=1, source_target_pairs={{0,4},{4,0},{8,12},{12,8},{1,5},{5,1},{9,13},{13,9},{2,6},{6,2},{1... | collective-permute-start | bytes 491528 | tf_op jit(solution)/shard_map/ppermute | solution.py:32
  14.9 2.6 %collective-permute-start.6 = (bf16[128,384]{1,0:T(8,128)(2,1)S(1)}, bf16[128,384]{1,0:T(8,128)(2,1)S(1)}, u32[]{:S(2)}, u32[]{:S(2)}) collective-permute-start(bf16[128,384]{1,0:T(8,128)(2,1)S(1)} %pad_maximum_fusion.13), channel_id=1, source_target_pairs={{0,8},{8,0},{4,12},{12,4},{1,9},{9,1},{5,13},{13,5},{2,10},{10,2},... | collective-permute-start | bytes 294920 | tf_op jit(solution)/shard_map/ppermute | solution.py:32
  18.2 2.4 %collective-permute-done.6 = bf16[128,384]{1,0:T(8,128)(2,1)S(1)} collective-permute-done((bf16[128,384]{1,0:T(8,128)(2,1)S(1)}, bf16[128,384]{1,0:T(8,128)(2,1)S(1)}, u32[]{:S(2)}, u32[]{:S(2)}) %collective-permute-start.6) | collective-permute-done | bytes 98336 | tf_op jit(solution)/shard_map/ppermute | solution.py:32
  21.1 1.7 %collective-permute-start.8 = (bf16[88,1152]{1,0:T(8,128)(2,1)S(1)}, bf16[88,1152]{1,0:T(8,128)(2,1)S(1)}, u32[]{:S(2)}, u32[]{:S(2)}) collective-permute-start(bf16[88,1152]{1,0:T(8,128)(2,1)S(1)} %convolution_convert_fusion.18), channel_id=1, source_target_pairs={{0,4},{4,0},{8,12},{12,8},{1,5},{5,1},{9,13},{13,9},{2,6},{6,2},{1... | collective-permute-start | bytes 608264 | tf_op jit(solution)/shard_map/ppermute | solution.py:32
  23.3 1.6 %collective-permute-start.15 = (bf16[88,640]{1,0:T(8,128)(2,1)S(1)}, bf16[88,640]{1,0:T(8,128)(2,1)S(1)}, u32[]{:S(2)}, u32[]{:S(2)}) collective-permute-start(bf16[88,640]{1,0:T(8,128)(2,1)S(1)} %convolution_convert_fusion.30), channel_id=1, source_target_pairs={{0,8},{8,0},{4,12},{12,4},{1,9},{9,1},{5,13},{13,5},{2,10},{10,2},... | collective-permute-start | bytes 337928 | tf_op jit(solution)/shard_map/ppermute | solution.py:32
  25.1 1.6 %collective-permute-start.12 = (bf16[128,896]{1,0:T(8,128)(2,1)S(1)}, bf16[128,896]{1,0:T(8,128)(2,1)S(1)}, u32[]{:S(2)}, u32[]{:S(2)}) collective-permute-start(bf16[128,896]{1,0:T(8,128)(2,1)S(1)} %convolution_convert_fusion.23), channel_id=1, source_target_pairs={{0,2},{2,0},{1,3},{3,1},{4,6},{6,4},{5,7},{7,5},{8,10},{10,8},{9,1... | collective-permute-start | bytes 688136 | tf_op jit(solution)/shard_map/ppermute | solution.py:32
  27.2 2.1 %collective-permute-start.14 = (bf16[88,1152]{1,0:T(8,128)(2,1)S(1)}, bf16[88,1152]{1,0:T(8,128)(2,1)S(1)}, u32[]{:S(2)}, u32[]{:S(2)}) collective-permute-start(bf16[88,1152]{1,0:T(8,128)(2,1)S(1)} %convolution_convert_fusion.17), channel_id=1, source_target_pairs={{0,4},{4,0},{8,12},{12,8},{1,5},{5,1},{9,13},{13,9},{2,6},{6,2},{1... | collective-permute-start | bytes 608264 | tf_op jit(solution)/shard_map/ppermute | solution.py:32
  29.3 1.0 %convolution_convert_fusion.10 = bf16[128,1152]{1,0:T(8,128)(2,1)} fusion(bf16[128,256]{1,0:T(8,128)(2,1)S(1)} %get-tuple-element.81, bf16[128,1152]{1,0:T(8,128)(2,1)S(1)} %collective-permute-done.9, bf16[128,1152]{1,0:T(8,128)(2,1)S(1)} %convolution_convert_fusion.13), kind=kOutput, calls=%fused_computation.35 | convolution fusion | flops 76824576 | bytes 950272 | tf_op jit(solution)/shard_map/dot_general | solution.py:218
  30.2 1.4 %collective-permute-done.8 = bf16[88,1152]{1,0:T(8,128)(2,1)S(1)} collective-permute-done((bf16[88,1152]{1,0:T(8,128)(2,1)S(1)}, bf16[88,1152]{1,0:T(8,128)(2,1)S(1)}, u32[]{:S(2)}, u32[]{:S(2)}) %collective-permute-start.8) | collective-permute-done | bytes 202784 | tf_op jit(solution)/shard_map/ppermute | solution.py:32
  31.9 0.5 collective-permute-start.11
  32.3 1.0 %convolution_convert_fusion.11 = bf16[128,1152]{1,0:T(8,128)(2,1)} fusion(bf16[128,256]{1,0:T(8,128)(2,1)S(1)} %slice_bitcast_fusion.7, bf16[88,1152]{1,0:T(8,128)(2,1)S(1)} %collective-permute-done.8, bf16[128,1152]{1,0:T(8,128)(2,1)S(1)} %convolution_convert_fusion.12), kind=kOutput, calls=%fused_computation.36 | convolution fusion | flops 77709312 | bytes 858112 | tf_op jit(solution)/shard_map/dot_general | solution.py:218
  33.3 1.0 %constant_dynamic-update-slice_fusion.3 = bf16[4096,128]{1,0:T(8,128)(2,1)} fusion(bf16[1,128,128]{2,1,0:T(8,128)(2,1)S(1)} %copy-done.6, bf16[128,256]{1,0:T(8,128)(2,1)S(1)} %slice-done, bf16[128,256]{1,0:T(8,128)(2,1)S(1)} %convolution_convert_fusion.33, bf16[3,128,256]{2,1,0:T(8,128)(2,1)S(1)} %get-tuple-element.64), kind=kOutput, calls=%fused_computation.164 | convolution fusion | flops 25493504 | bytes 294912 | tf_op jit(solution)/shard_map/ct,cp->tp/dot_general | solution.py:228
  34.5 2.7 %collective-permute-start.13 = (bf16[88,896]{1,0:T(8,128)(2,1)S(1)}, bf16[88,896]{1,0:T(8,128)(2,1)S(1)}, u32[]{:S(2)}, u32[]{:S(2)}) collective-permute-start(bf16[88,896]{1,0:T(8,128)(2,1)S(1)} %convolution_convert_fusion.29), channel_id=1, source_target_pairs={{0,4},{4,0},{8,12},{12,8},{1,5},{5,1},{9,13},{13,9},{2,6},{6,2},{1... | collective-permute-start | bytes 473096 | tf_op jit(solution)/shard_map/ppermute | solution.py:32
  37.7 0.8 %collective-permute-start.17 = (bf16[88,1152]{1,0:T(8,128)(2,1)S(1)}, bf16[88,1152]{1,0:T(8,128)(2,1)S(1)}, u32[]{:S(2)}, u32[]{:S(2)}) collective-permute-start(bf16[88,1152]{1,0:T(8,128)(2,1)S(1)} %convolution_convert_fusion.15), channel_id=1, source_target_pairs={{0,8},{8,0},{4,12},{12,4},{1,9},{9,1},{5,13},{13,5},{2,10},{10,2},... | collective-permute-start | bytes 608264 | tf_op jit(solution)/shard_map/ppermute | solution.py:32
  38.5 1.1 %constant_dynamic-update-slice_fusion.2 = bf16[4096,128]{1,0:T(8,128)(2,1)} fusion(bf16[4096,128]{1,0:T(8,128)(2,1)} %constant_dynamic-update-slice_fusion.3, bf16[1,128,128]{2,1,0:T(8,128)(2,1)S(1)} %copy-done.6, bf16[88,640]{1,0:T(8,128)(2,1)S(1)} %collective-permute-done.15, bf16[128,640]{1,0:T(8,128)(2,1)S(1)} %convolution_convert_fusion.25, ...), kind=kOutput, calls=%fused_computation.163 | convolution fusion | flops 64225280 | bytes 538624 | tf_op jit(solution)/shard_map/ct,cp->tp/dot_general | solution.py:228
  39.6 1.0 %convolution_convert_fusion.7 = bf16[128,1152]{1,0:T(8,128)(2,1)} fusion(bf16[128,256]{1,0:T(8,128)(2,1)S(1)} %slice_bitcast_fusion.7, bf16[88,1152]{1,0:T(8,128)(2,1)S(1)} %collective-permute-done.14, bf16[128,1152]{1,0:T(8,128)(2,1)S(1)} %copy-done.8), kind=kOutput, calls=%fused_computation.32 | convolution fusion | flops 77709312 | bytes 858112 | tf_op jit(solution)/shard_map/dot_general | solution.py:218
  40.6 1.8 %collective-permute-done.13 = bf16[88,896]{1,0:T(8,128)(2,1)S(1)} collective-permute-done((bf16[88,896]{1,0:T(8,128)(2,1)S(1)}, bf16[88,896]{1,0:T(8,128)(2,1)S(1)}, u32[]{:S(2)}, u32[]{:S(2)}) %collective-permute-start.13) | collective-permute-done | bytes 157728 | tf_op jit(solution)/shard_map/ppermute | solution.py:32
  42.5 3.2 %collective-permute-start.18 = (bf16[88,896]{1,0:T(8,128)(2,1)S(1)}, bf16[88,896]{1,0:T(8,128)(2,1)S(1)}, u32[]{:S(2)}, u32[]{:S(2)}) collective-permute-start(bf16[88,896]{1,0:T(8,128)(2,1)S(1)} %convolution_convert_fusion.28), channel_id=1, source_target_pairs={{0,8},{8,0},{4,12},{12,4},{1,9},{9,1},{5,13},{13,5},{2,10},{10,2},... | collective-permute-start | bytes 473096 | tf_op jit(solution)/shard_map/ppermute | solution.py:32
  45.8 2.6 %collective-permute-done.11 = bf16[88,1152]{1,0:T(8,128)(2,1)S(1)} collective-permute-done((bf16[88,1152]{1,0:T(8,128)(2,1)S(1)}, bf16[88,1152]{1,0:T(8,128)(2,1)S(1)}, u32[]{:S(2)}, u32[]{:S(2)}) %collective-permute-start.11) | collective-permute-done | bytes 202784 | tf_op jit(solution)/shard_map/ppermute | solution.py:32
  48.4 1.2 %constant_dynamic-update-slice_fusion.1 = bf16[4096,128]{1,0:T(8,128)(2,1)} fusion(bf16[4096,128]{1,0:T(8,128)(2,1)} %constant_dynamic-update-slice_fusion.2, bf16[1,128,128]{2,1,0:T(8,128)(2,1)S(1)} %copy-done.6, bf16[88,1152]{1,0:T(8,128)(2,1)S(1)} %collective-permute-done.11, bf16[128,1152]{1,0:T(8,128)(2,1)S(1)} %copy-done.9, ...), kind=kOutput, calls=%fused_computation.162 | convolution fusion | flops 115605504 | bytes 890880 | tf_op jit(solution)/shard_map/ct,cp->tp/dot_general | solution.py:228
  49.6 3.6 %collective-permute-start.16 = (bf16[8,64]{1,0:T(8,128)(2,1)S(1)}, bf16[8,64]{1,0:T(8,128)(2,1)S(1)}, u32[]{:S(2)}, u32[]{:S(2)}) collective-permute-start(bf16[8,64]{1,0:T(8,128)(2,1)S(1)} %slice_maximum_fusion), channel_id=1, source_target_pairs={{0,2},{2,0},{1,3},{3,1},{4,6},{6,4},{5,7},{7,5},{8,10},{10,8},{9,1... | collective-permute-start | bytes 3080 | tf_op jit(solution)/shard_map/ppermute | solution.py:32
  53.4 1.3 %collective-permute-done.16 = bf16[8,64]{1,0:T(8,128)(2,1)S(1)} collective-permute-done((bf16[8,64]{1,0:T(8,128)(2,1)S(1)}, bf16[8,64]{1,0:T(8,128)(2,1)S(1)}, u32[]{:S(2)}, u32[]{:S(2)}) %collective-permute-start.16) | collective-permute-done | bytes 1056 | tf_op jit(solution)/shard_map/ppermute | solution.py:32
  54.8 0.5 slice.183
  56.0 1.2 %constant_dynamic-update-slice_fusion = bf16[4096,128]{1,0:T(8,128)(2,1)} fusion(bf16[4096,128]{1,0:T(8,128)(2,1)} %constant_dynamic-update-slice_fusion.1, bf16[1,128,128]{2,1,0:T(8,128)(2,1)S(1)} %copy-done.6, bf16[88,1152]{1,0:T(8,128)(2,1)S(1)} %collective-permute-done.17, bf16[128,1152]{1,0:T(8,128)(2,1)S(1)} %copy-done.10, ...), kind=kOutput, calls=%fused_computation.161 | convolution fusion | flops 115605504 | bytes 890880 | tf_op jit(solution)/shard_map/ct,cp->tp/dot_general | solution.py:228
  57.2 1.1 %fusion.20 = bf16[4096,128]{1,0:T(8,128)(2,1)} fusion(bf16[4096,128]{1,0:T(8,128)(2,1)} %constant_dynamic-update-slice_fusion, bf16[88,896]{1,0:T(8,128)(2,1)S(1)} %collective-permute-done.18, bf16[128,896]{1,0:T(8,128)(2,1)S(1)} %convolution_convert_fusion.21, bf16[3,128,256]{2,1,0:T(8,128)(2,1)S(1)} %get-tuple-element.73, ...), kind=kOutput, calls=%fused_computation.45 | convolution fusion | flops 89915392 | bytes 714752 | tf_op jit(solution)/shard_map/ct,cp->tp/dot_general | solution.py:228
  (68 shorter events, 5.0 us)
Async XLA Ops:
  0.0 4.6 %copy-start = (bf16[4096,128]{1,0:T(8,128)(2,1)S(1)}, bf16[4096,128]{1,0:T(8,128)(2,1)}, u32[]{:S(2)}) copy-start(bf16[4096,128]{1,0:T(8,128)(2,1)} %refs_1_.2) | copy-start | bytes 3145732
  0.0 4.6 %copy-start.2 = (bf16[1,128,128]{2,1,0:T(8,128)(2,1)S(1)}, bf16[1,128,128]{2,1,0:T(8,128)(2,1)}, u32[]{:S(2)}) copy-start(bf16[1,128,128]{2,1,0:T(8,128)(2,1)} %refs_0_.1) | copy-start | bytes 98308
  0.0 6.8 %copy-start.5 = (s32[1,3,64]{2,0,1:T(1,128)S(1)}, s32[1,3,64]{2,0,1:T(1,128)}, u32[]{:S(2)}) copy-start(s32[1,3,64]{2,0,1:T(1,128)} %param.9) | copy-start | bytes 2308
  0.0 6.8 %copy-start.4 = (bf16[1,3,64,128]{3,2,1,0:T(8,128)(2,1)S(1)}, bf16[1,3,64,128]{3,2,1,0:T(8,128)(2,1)}, u32[]{:S(2)}) copy-start(bf16[1,3,64,128]{3,2,1,0:T(8,128)(2,1)} %refs_1_.3) | copy-start | bytes 147460
  1.5 6.6 %collective-permute-start.3 = (bf16[128,256]{1,0:T(8,128)(2,1)S(1)}, bf16[128,256]{1,0:T(8,128)(2,1)S(1)}, u32[]{:S(2)}, u32[]{:S(2)}) collective-permute-start(bf16[128,256]{1,0:T(8,128)(2,1)S(1)} %get-tuple-element.61), channel_id=1, source_target_pairs={{0,2},{2,0},{1,3},{3,1},{4,6},{6,4},{5,7},{7,5},{8,10},{10,8},{9,1... | collective-permute-start | bytes 196616 | tf_op jit(solution)/shard_map/ppermute | solution.py:32
  4.5 7.1 %collective-permute-start.5 = (bf16[128,640]{1,0:T(8,128)(2,1)S(1)}, bf16[128,640]{1,0:T(8,128)(2,1)S(1)}, u32[]{:S(2)}, u32[]{:S(2)}) collective-permute-start(bf16[128,640]{1,0:T(8,128)(2,1)S(1)} %get-tuple-element.65), channel_id=1, source_target_pairs={{0,2},{2,0},{1,3},{3,1},{4,6},{6,4},{5,7},{7,5},{8,10},{10,8},{9,1... | collective-permute-start | bytes 491528 | tf_op jit(solution)/shard_map/ppermute | solution.py:32
  4.8 13.1 %collective-permute-start.7 = (bf16[128,1152]{1,0:T(8,128)(2,1)S(1)}, bf16[128,1152]{1,0:T(8,128)(2,1)S(1)}, u32[]{:S(2)}, u32[]{:S(2)}) collective-permute-start(bf16[128,1152]{1,0:T(8,128)(2,1)S(1)} %convolution_convert_fusion.14), channel_id=1, source_target_pairs={{0,2},{2,0},{1,3},{3,1},{4,6},{6,4},{5,7},{7,5},{8,10},{10,8},{9,1... | collective-permute-start | bytes 884744 | tf_op jit(solution)/shard_map/ppermute | solution.py:32
  8.3 4.7 %collective-permute-start.4 = (bf16[128,384]{1,0:T(8,128)(2,1)S(1)}, bf16[128,384]{1,0:T(8,128)(2,1)S(1)}, u32[]{:S(2)}, u32[]{:S(2)}) collective-permute-start(bf16[128,384]{1,0:T(8,128)(2,1)S(1)} %pad_maximum_fusion.12), channel_id=1, source_target_pairs={{0,4},{4,0},{8,12},{12,8},{1,5},{5,1},{9,13},{13,9},{2,6},{6,2},{1... | collective-permute-start | bytes 294920 | tf_op jit(solution)/shard_map/ppermute | solution.py:32
  10.2 16.7 %collective-permute-start.9 = (bf16[128,1152]{1,0:T(8,128)(2,1)S(1)}, bf16[128,1152]{1,0:T(8,128)(2,1)S(1)}, u32[]{:S(2)}, u32[]{:S(2)}) collective-permute-start(bf16[128,1152]{1,0:T(8,128)(2,1)S(1)} %convolution_convert_fusion.13), channel_id=1, source_target_pairs={{0,2},{2,0},{1,3},{3,1},{4,6},{6,4},{5,7},{7,5},{8,10},{10,8},{9,1... | collective-permute-start | bytes 884744 | tf_op jit(solution)/shard_map/ppermute | solution.py:32
  13.1 10.0 %collective-permute-start.10 = (bf16[128,640]{1,0:T(8,128)(2,1)S(1)}, bf16[128,640]{1,0:T(8,128)(2,1)S(1)}, u32[]{:S(2)}, u32[]{:S(2)}) collective-permute-start(bf16[128,640]{1,0:T(8,128)(2,1)S(1)} %convolution_convert_fusion.26), channel_id=1, source_target_pairs={{0,4},{4,0},{8,12},{12,8},{1,5},{5,1},{9,13},{13,9},{2,6},{6,2},{1... | collective-permute-start | bytes 491528 | tf_op jit(solution)/shard_map/ppermute | solution.py:32
  14.9 5.6 %collective-permute-start.6 = (bf16[128,384]{1,0:T(8,128)(2,1)S(1)}, bf16[128,384]{1,0:T(8,128)(2,1)S(1)}, u32[]{:S(2)}, u32[]{:S(2)}) collective-permute-start(bf16[128,384]{1,0:T(8,128)(2,1)S(1)} %pad_maximum_fusion.13), channel_id=1, source_target_pairs={{0,8},{8,0},{4,12},{12,4},{1,9},{9,1},{5,13},{13,5},{2,10},{10,2},... | collective-permute-start | bytes 294920 | tf_op jit(solution)/shard_map/ppermute | solution.py:32
  20.5 11.8 %copy-start.3 = (bf16[128,384]{1,0:T(8,128)(2,1)}, bf16[128,384]{1,0:T(8,128)(2,1)S(1)}, u32[]{:S(2)}) copy-start(bf16[128,384]{1,0:T(8,128)(2,1)S(1)} %collective-permute-done.6) | copy-start | bytes 294916
  21.1 10.6 %collective-permute-start.8 = (bf16[88,1152]{1,0:T(8,128)(2,1)S(1)}, bf16[88,1152]{1,0:T(8,128)(2,1)S(1)}, u32[]{:S(2)}, u32[]{:S(2)}) collective-permute-start(bf16[88,1152]{1,0:T(8,128)(2,1)S(1)} %convolution_convert_fusion.18), channel_id=1, source_target_pairs={{0,4},{4,0},{8,12},{12,8},{1,5},{5,1},{9,13},{13,9},{2,6},{6,2},{1... | collective-permute-start | bytes 608264 | tf_op jit(solution)/shard_map/ppermute | solution.py:32
  23.3 15.2 %collective-permute-start.15 = (bf16[88,640]{1,0:T(8,128)(2,1)S(1)}, bf16[88,640]{1,0:T(8,128)(2,1)S(1)}, u32[]{:S(2)}, u32[]{:S(2)}) collective-permute-start(bf16[88,640]{1,0:T(8,128)(2,1)S(1)} %convolution_convert_fusion.30), channel_id=1, source_target_pairs={{0,8},{8,0},{4,12},{12,4},{1,9},{9,1},{5,13},{13,5},{2,10},{10,2},... | collective-permute-start | bytes 337928 | tf_op jit(solution)/shard_map/ppermute | solution.py:32
  25.1 9.2 %collective-permute-start.12 = (bf16[128,896]{1,0:T(8,128)(2,1)S(1)}, bf16[128,896]{1,0:T(8,128)(2,1)S(1)}, u32[]{:S(2)}, u32[]{:S(2)}) collective-permute-start(bf16[128,896]{1,0:T(8,128)(2,1)S(1)} %convolution_convert_fusion.23), channel_id=1, source_target_pairs={{0,2},{2,0},{1,3},{3,1},{4,6},{6,4},{5,7},{7,5},{8,10},{10,8},{9,1... | collective-permute-start | bytes 688136 | tf_op jit(solution)/shard_map/ppermute | solution.py:32
  27.2 10.3 %collective-permute-start.14 = (bf16[88,1152]{1,0:T(8,128)(2,1)S(1)}, bf16[88,1152]{1,0:T(8,128)(2,1)S(1)}, u32[]{:S(2)}, u32[]{:S(2)}) collective-permute-start(bf16[88,1152]{1,0:T(8,128)(2,1)S(1)} %convolution_convert_fusion.17), channel_id=1, source_target_pairs={{0,4},{4,0},{8,12},{12,8},{1,5},{5,1},{9,13},{13,9},{2,6},{6,2},{1... | collective-permute-start | bytes 608264 | tf_op jit(solution)/shard_map/ppermute | solution.py:32
  31.9 16.5 %collective-permute-start.11 = (bf16[88,1152]{1,0:T(8,128)(2,1)S(1)}, bf16[88,1152]{1,0:T(8,128)(2,1)S(1)}, u32[]{:S(2)}, u32[]{:S(2)}) collective-permute-start(bf16[88,1152]{1,0:T(8,128)(2,1)S(1)} %convolution_convert_fusion.16), channel_id=1, source_target_pairs={{0,8},{8,0},{4,12},{12,4},{1,9},{9,1},{5,13},{13,5},{2,10},{10,2},... | collective-permute-start | bytes 608264 | tf_op jit(solution)/shard_map/ppermute | solution.py:32
  32.3 1.0 %slice-start = ((bf16[128,384]{1,0:T(8,128)(2,1)}), bf16[128,256]{1,0:T(8,128)(2,1)S(1)}, s32[]{:S(2)}) async-start(bf16[128,384]{1,0:T(8,128)(2,1)} %copy-done.3), calls=%async_computation | async-start | bytes 131072 | tf_op jit(solution)/shard_map/slice | solution.py:294
  32.3 1.0 %copy-start.6 = (bf16[1,128,128]{2,1,0:T(8,128)(2,1)S(1)}, bf16[1,128,128]{2,1,0:T(8,128)(2,1)}, u32[]{:S(2)}) copy-start(bf16[1,128,128]{2,1,0:T(8,128)(2,1)} %param.11) | copy-start | bytes 98308
  34.3 3.2 %copy-start.7 = (bf16[128,1152]{1,0:T(8,128)(2,1)S(1)}, bf16[128,1152]{1,0:T(8,128)(2,1)}, u32[]{:S(2)}) copy-start(bf16[128,1152]{1,0:T(8,128)(2,1)} %convolution_convert_fusion.10) | copy-start | bytes 884740
  34.5 7.8 %collective-permute-start.13 = (bf16[88,896]{1,0:T(8,128)(2,1)S(1)}, bf16[88,896]{1,0:T(8,128)(2,1)S(1)}, u32[]{:S(2)}, u32[]{:S(2)}) collective-permute-start(bf16[88,896]{1,0:T(8,128)(2,1)S(1)} %convolution_convert_fusion.29), channel_id=1, source_target_pairs={{0,4},{4,0},{8,12},{12,8},{1,5},{5,1},{9,13},{13,9},{2,6},{6,2},{1... | collective-permute-start | bytes 473096 | tf_op jit(solution)/shard_map/ppermute | solution.py:32
  37.7 1.9 %copy-start.8 = (bf16[128,1152]{1,0:T(8,128)(2,1)S(1)}, bf16[128,1152]{1,0:T(8,128)(2,1)}, u32[]{:S(2)}) copy-start(bf16[128,1152]{1,0:T(8,128)(2,1)} %convolution_convert_fusion.10) | copy-start | bytes 884740
  37.7 18.2 %collective-permute-start.17 = (bf16[88,1152]{1,0:T(8,128)(2,1)S(1)}, bf16[88,1152]{1,0:T(8,128)(2,1)S(1)}, u32[]{:S(2)}, u32[]{:S(2)}) collective-permute-start(bf16[88,1152]{1,0:T(8,128)(2,1)S(1)} %convolution_convert_fusion.15), channel_id=1, source_target_pairs={{0,8},{8,0},{4,12},{12,4},{1,9},{9,1},{5,13},{13,5},{2,10},{10,2},... | collective-permute-start | bytes 608264 | tf_op jit(solution)/shard_map/ppermute | solution.py:32
  40.6 7.8 %copy-start.9 = (bf16[128,1152]{1,0:T(8,128)(2,1)S(1)}, bf16[128,1152]{1,0:T(8,128)(2,1)}, u32[]{:S(2)}) copy-start(bf16[128,1152]{1,0:T(8,128)(2,1)} %convolution_convert_fusion.11) | copy-start | bytes 884740
  42.5 14.6 %collective-permute-start.18 = (bf16[88,896]{1,0:T(8,128)(2,1)S(1)}, bf16[88,896]{1,0:T(8,128)(2,1)S(1)}, u32[]{:S(2)}, u32[]{:S(2)}) collective-permute-start(bf16[88,896]{1,0:T(8,128)(2,1)S(1)} %convolution_convert_fusion.28), channel_id=1, source_target_pairs={{0,8},{8,0},{4,12},{12,4},{1,9},{9,1},{5,13},{13,5},{2,10},{10,2},... | collective-permute-start | bytes 473096 | tf_op jit(solution)/shard_map/ppermute | solution.py:32
  49.6 6.4 %copy-start.10 = (bf16[128,1152]{1,0:T(8,128)(2,1)S(1)}, bf16[128,1152]{1,0:T(8,128)(2,1)}, u32[]{:S(2)}) copy-start(bf16[128,1152]{1,0:T(8,128)(2,1)} %convolution_convert_fusion.7) | copy-start | bytes 884740
  49.6 5.1 %collective-permute-start.16 = (bf16[8,64]{1,0:T(8,128)(2,1)S(1)}, bf16[8,64]{1,0:T(8,128)(2,1)S(1)}, u32[]{:S(2)}, u32[]{:S(2)}) collective-permute-start(bf16[8,64]{1,0:T(8,128)(2,1)S(1)} %slice_maximum_fusion), channel_id=1, source_target_pairs={{0,2},{2,0},{1,3},{3,1},{4,6},{6,4},{5,7},{7,5},{8,10},{10,8},{9,1... | collective-permute-start | bytes 3080 | tf_op jit(solution)/shard_map/ppermute | solution.py:32

commit v15 on v14

--- a/solution.py
+++ b/solution.py
@@ -9,10 +9,11 @@
 FULL_PIECES = (2, 1)
 EARLY_PIECES = 2
 COUNT_PIECE = 2
+COUNT_READ = 2
 LOOK = (3, -1)
 ORDER = (
-    (0, 0), (0, 1), (0, 2), (1, 0), (0, 3), (1, 1), (2, 0), (1, 2), LOOK, (2, 1), (0, 4), (1, 3),
-    (2, 2), (3, 0), (1, 4), (2, 3), (3, 1), (2, 4), (3, 2), (3, 3), (3, 4),
+    (0, 0), (0, 1), (0, 2), (1, 0), (1, 1), (0, 3), (2, 0), (0, 4), (1, 2), LOOK, (2, 1), (1, 3),
+    (2, 2), (1, 4), (2, 3), (3, 0), (3, 1), (2, 4), (3, 2), (3, 3), (3, 4),
 )
 KERNEL_VMEM = 16 * 1024 * 1024
 ROOM_SIXTEENTHS = 11
@@ -274,7 +275,7 @@
     previous, finished, known = None, None, None
     for level, piece in ORDER:
         if (level, piece) == LOOK:
-            known = after(partners[0], previous)[:, starts[1] :]
+            known = after(after(partners[0], previous), partners[1])[:, starts[1] :]
             theirs[levels - 1] = known[:room, :rank]
             continue
         count = starts[piece + 1] - starts[piece]
@@ -302,11 +303,9 @@
             else:
                 own = outgoing = times(matrix, value)
         if level == levels:
-            done[piece] = finished = evaluated(own, evaluation)
-            if piece == COUNT_PIECE:
-                most = after(jnp.maximum(extra[levels - 1], known)[:8, rank:], finished)
-                for hop in hops[:wide]:
-                    most = jnp.maximum(most, from_partner(most, hop))
+            done[piece] = finished = previous = evaluated(own, evaluation)
+            if piece == COUNT_READ:
+                most = jnp.maximum(most, after(counted, finished))
             continue
         if level == 0:
             outgoing = own
@@ -318,6 +317,11 @@
         inputs[piece] = own
         partners[piece] = from_partner(outgoing, hops[level])
         previous = outgoing
+        if (level, piece) == (levels - 1, COUNT_PIECE):
+            most = after(jnp.maximum(extra[levels - 1], known)[:8, rank:], outgoing)
+            for hop in hops[: wide - 1]:
+                most = jnp.maximum(most, from_partner(most, hop))
+            counted = from_partner(most, hops[wide - 1])
     quick = jnp.concatenate(done, 0)
     return lax.cond(
         most[0, 0] > room,

time: 58.5 us -> 58.1 us (level)
  waiting for transfers between devices: 10.9 us -> 17 us
  starting transfers between devices: 30.1 us -> 25.6 us
  matrix products: 13.1 us -> 10.9 us
    ppermute x16, waiting for transfers between devices: 10.9 us -> 17 us  [from_partner(): return lax.ppermute(block, hop[0], route(*hop))]
    ppermute x16, starting transfers between devices: 30.1 us -> 25.6 us  [from_partner(): return lax.ppermute(block, hop[0], route(*hop))]
    dot_general x17, matrix products: 5.9 us -> 3.76 us  [times(): jnp.dot(matrix, value, preferred_element_type=jnp.float32)]
  transfers between devices with their start and end apart: 16 -> 16, of which waited for: 7 -> 8; matrix products, arithmetic and copies ran while one was open for 22% -> 18% of each run, Pallas kernels for 2% -> 2%
where the time goes in v15:
time: 58.1 us; the launch traced here: 57.9 us
  starting transfers between devices  25.6 us (44%)
  waiting for transfers between devices  17 us (29%)
  matrix products  10.9 us (19%)
  Pallas kernels  2.63 us (5%)
  between operations  0.96 us (2%)
  local copies, waits for them, and re-layouts  0.65 us (1%)
    ppermute x16, starting transfers between devices, from_partner(): return lax.ppermute(block, hop[0], route(*hop))  25.6 us
    ppermute x16, waiting for transfers between devices, from_partner(): return lax.ppermute(block, hop[0], route(*hop))  17 us
    dot_general x5, matrix products, evaluated(): jnp.einsum('ct,cp->tp', coeffs, evaluation, preferred_element_type=jnp.fl...  5.65 us
    dot_general x17, matrix products, times(): jnp.dot(matrix, value, preferred_element_type=jnp.float32)  3.76 us
    pallas_call x1, Pallas kernels, early(): pl.pallas_call(lambda *refs: early_kernel(starts, *refs), out_shape=[jax....  1.45 us
    pallas_call x1, Pallas kernels, tables(): pl.pallas_call(lambda *refs: tables_kernel(wide, room, *refs), out_shape=...  1.18 us
  transfers between devices with their start and end apart: 16, of which 8 were waited for; matrix products, arithmetic and copies ran while one was open for 18% of the time, Pallas kernels for 2%

profile of v15, /device:TPU:0, one launch (start us, length us, event | category | flops | bytes accessed | tf_op | source)
XLA Modules:
  0.0 57.9 jit_solution(10773319679070568084)
XLA Ops:
  0.0 1.4 %early.1 = (bf16[128,256]{1,0:T(8,128)(2,1)S(1)}, bf16[128,640]{1,0:T(8,128)(2,1)S(1)}) custom-call(bf16[1,128,128]{2,1,0:T(8,128)(2,1)} %refs_0_.1, bf16[4096,128]{1,0:T(8,128)(2,1)} %refs_1_.2), custom_call_target="tpu_custom_call" | custom-call | flops 29360128 | bytes 458752 | tf_op jit(solution)/shard_map/early/pallas_call | solution.py:69
  1.5 3.0 %collective-permute-start.3 = (bf16[128,256]{1,0:T(8,128)(2,1)S(1)}, bf16[128,256]{1,0:T(8,128)(2,1)S(1)}, u32[]{:S(2)}, u32[]{:S(2)}) collective-permute-start(bf16[128,256]{1,0:T(8,128)(2,1)S(1)} %get-tuple-element.63), channel_id=1, source_target_pairs={{0,2},{2,0},{1,3},{3,1},{4,6},{6,4},{5,7},{7,5},{8,10},{10,8},{9,1... | collective-permute-start | bytes 196616 | tf_op jit(solution)/shard_map/ppermute | solution.py:33
  4.6 0.3 convolution_convert_fusion.14
  4.8 2.0 %collective-permute-start.7 = (bf16[128,1152]{1,0:T(8,128)(2,1)S(1)}, bf16[128,1152]{1,0:T(8,128)(2,1)S(1)}, u32[]{:S(2)}, u32[]{:S(2)}) collective-permute-start(bf16[128,1152]{1,0:T(8,128)(2,1)S(1)} %convolution_convert_fusion.14), channel_id=1, source_target_pairs={{0,2},{2,0},{1,3},{3,1},{4,6},{6,4},{5,7},{7,5},{8,10},{10,8},{9,1... | collective-permute-start | bytes 884744 | tf_op jit(solution)/shard_map/ppermute | solution.py:33
  6.8 1.2 %tables.1 = (bf16[3,128,256]{2,1,0:T(8,128)(2,1)S(1)}, bf16[3,128,256]{2,1,0:T(8,128)(2,1)S(1)}, bf16[3,128,128]{2,1,0:T(8,128)(2,1)S(1)}) custom-call(s32[3,1,64]{2,1,0:T(1,128)S(1)} %bitcast.111, bf16[1,3,64,128]{3,2,1,0:T(8,128)(2,1)S(1)} %copy-done.3), custom_call_target="tpu_custom_call" | custom-call | flops 50000000 | bytes 600000 | tf_op jit(solution)/shard_map/tables/pallas_call | solution.py:152
  8.3 1.6 %collective-permute-start.4 = (bf16[128,384]{1,0:T(8,128)(2,1)S(1)}, bf16[128,384]{1,0:T(8,128)(2,1)S(1)}, u32[]{:S(2)}, u32[]{:S(2)}) collective-permute-start(bf16[128,384]{1,0:T(8,128)(2,1)S(1)} %pad_maximum_fusion.12), channel_id=1, source_target_pairs={{0,4},{4,0},{8,12},{12,8},{1,5},{5,1},{9,13},{13,9},{2,6},{6,2},{1... | collective-permute-start | bytes 294920 | tf_op jit(solution)/shard_map/ppermute | solution.py:33
  9.9 1.7 %collective-permute-done.5 = bf16[128,640]{1,0:T(8,128)(2,1)S(1)} collective-permute-done((bf16[128,640]{1,0:T(8,128)(2,1)S(1)}, bf16[128,640]{1,0:T(8,128)(2,1)S(1)}, u32[]{:S(2)}, u32[]{:S(2)}) %collective-permute-start.5) | collective-permute-done | bytes 163872 | tf_op jit(solution)/shard_map/ppermute | solution.py:33
  11.8 1.6 %collective-permute-start.8 = (bf16[128,640]{1,0:T(8,128)(2,1)S(1)}, bf16[128,640]{1,0:T(8,128)(2,1)S(1)}, u32[]{:S(2)}, u32[]{:S(2)}) collective-permute-start(bf16[128,640]{1,0:T(8,128)(2,1)S(1)} %convolution_convert_fusion.26), channel_id=1, source_target_pairs={{0,4},{4,0},{8,12},{12,8},{1,5},{5,1},{9,13},{13,9},{2,6},{6,2},{1... | collective-permute-start | bytes 491528 | tf_op jit(solution)/shard_map/ppermute | solution.py:33
  13.5 0.3 convolution_convert_fusion.13
  14.1 2.7 %collective-permute-start.6 = (bf16[128,384]{1,0:T(8,128)(2,1)S(1)}, bf16[128,384]{1,0:T(8,128)(2,1)S(1)}, u32[]{:S(2)}, u32[]{:S(2)}) collective-permute-start(bf16[128,384]{1,0:T(8,128)(2,1)S(1)} %pad_maximum_fusion.13), channel_id=1, source_target_pairs={{0,8},{8,0},{4,12},{12,4},{1,9},{9,1},{5,13},{13,5},{2,10},{10,2},... | collective-permute-start | bytes 294920 | tf_op jit(solution)/shard_map/ppermute | solution.py:33
  16.7 1.4 %collective-permute-start.10 = (bf16[128,1152]{1,0:T(8,128)(2,1)S(1)}, bf16[128,1152]{1,0:T(8,128)(2,1)S(1)}, u32[]{:S(2)}, u32[]{:S(2)}) collective-permute-start(bf16[128,1152]{1,0:T(8,128)(2,1)S(1)} %convolution_convert_fusion.13), channel_id=1, source_target_pairs={{0,2},{2,0},{1,3},{3,1},{4,6},{6,4},{5,7},{7,5},{8,10},{10,8},{9,1... | collective-permute-start | bytes 884744 | tf_op jit(solution)/shard_map/ppermute | solution.py:33
  18.3 0.7 %collective-permute-start.13 = (bf16[128,896]{1,0:T(8,128)(2,1)S(1)}, bf16[128,896]{1,0:T(8,128)(2,1)S(1)}, u32[]{:S(2)}, u32[]{:S(2)}) collective-permute-start(bf16[128,896]{1,0:T(8,128)(2,1)S(1)} %convolution_convert_fusion.23), channel_id=1, source_target_pairs={{0,2},{2,0},{1,3},{3,1},{4,6},{6,4},{5,7},{7,5},{8,10},{10,8},{9,1... | collective-permute-start | bytes 688136 | tf_op jit(solution)/shard_map/ppermute | solution.py:33
  19.5 1.0 %collective-permute-start.9 = (bf16[88,1152]{1,0:T(8,128)(2,1)S(1)}, bf16[88,1152]{1,0:T(8,128)(2,1)S(1)}, u32[]{:S(2)}, u32[]{:S(2)}) collective-permute-start(bf16[88,1152]{1,0:T(8,128)(2,1)S(1)} %convolution_convert_fusion.18), channel_id=1, source_target_pairs={{0,4},{4,0},{8,12},{12,8},{1,5},{5,1},{9,13},{13,9},{2,6},{6,2},{1... | collective-permute-start | bytes 608264 | tf_op jit(solution)/shard_map/ppermute | solution.py:33
  21.4 2.5 %collective-permute-start.15 = (bf16[88,640]{1,0:T(8,128)(2,1)S(1)}, bf16[88,640]{1,0:T(8,128)(2,1)S(1)}, u32[]{:S(2)}, u32[]{:S(2)}) collective-permute-start(bf16[88,640]{1,0:T(8,128)(2,1)S(1)} %convolution_convert_fusion.30), channel_id=1, source_target_pairs={{0,8},{8,0},{4,12},{12,4},{1,9},{9,1},{5,13},{13,5},{2,10},{10,2},... | collective-permute-start | bytes 337928 | tf_op jit(solution)/shard_map/ppermute | solution.py:33
  24.2 1.8 %collective-permute-done.10 = bf16[128,1152]{1,0:T(8,128)(2,1)S(1)} collective-permute-done((bf16[128,1152]{1,0:T(8,128)(2,1)S(1)}, bf16[128,1152]{1,0:T(8,128)(2,1)S(1)}, u32[]{:S(2)}, u32[]{:S(2)}) %collective-permute-start.10) | collective-permute-done | bytes 294944 | tf_op jit(solution)/shard_map/ppermute | solution.py:33
  26.2 1.5 %collective-permute-start.16 = (bf16[88,1152]{1,0:T(8,128)(2,1)S(1)}, bf16[88,1152]{1,0:T(8,128)(2,1)S(1)}, u32[]{:S(2)}, u32[]{:S(2)}) collective-permute-start(bf16[88,1152]{1,0:T(8,128)(2,1)S(1)} %convolution_convert_fusion.17), channel_id=1, source_target_pairs={{0,4},{4,0},{8,12},{12,8},{1,5},{5,1},{9,13},{13,9},{2,6},{6,2},{1... | collective-permute-start | bytes 608264 | tf_op jit(solution)/shard_map/ppermute | solution.py:33
  28.0 0.4 collective-permute-done.9
  28.9 1.3 %collective-permute-start.14 = (bf16[88,896]{1,0:T(8,128)(2,1)S(1)}, bf16[88,896]{1,0:T(8,128)(2,1)S(1)}, u32[]{:S(2)}, u32[]{:S(2)}) collective-permute-start(bf16[88,896]{1,0:T(8,128)(2,1)S(1)} %convolution_convert_fusion.29), channel_id=1, source_target_pairs={{0,4},{4,0},{8,12},{12,8},{1,5},{5,1},{9,13},{13,9},{2,6},{6,2},{1... | collective-permute-start | bytes 473096 | tf_op jit(solution)/shard_map/ppermute | solution.py:33
  30.2 2.6 %collective-permute-start.12 = (bf16[88,1152]{1,0:T(8,128)(2,1)S(1)}, bf16[88,1152]{1,0:T(8,128)(2,1)S(1)}, u32[]{:S(2)}, u32[]{:S(2)}) collective-permute-start(bf16[88,1152]{1,0:T(8,128)(2,1)S(1)} %convolution_convert_fusion.16), channel_id=1, source_target_pairs={{0,8},{8,0},{4,12},{12,4},{1,9},{9,1},{5,13},{13,5},{2,10},{10,2},... | collective-permute-start | bytes 608264 | tf_op jit(solution)/shard_map/ppermute | solution.py:33
  33.0 1.1 %collective-permute-start.11 = (bf16[8,64]{1,0:T(8,128)(2,1)S(1)}, bf16[8,64]{1,0:T(8,128)(2,1)S(1)}, u32[]{:S(2)}, u32[]{:S(2)}) collective-permute-start(bf16[8,64]{1,0:T(8,128)(2,1)S(1)} %slice_maximum_fusion), channel_id=1, source_target_pairs={{0,2},{2,0},{1,3},{3,1},{4,6},{6,4},{5,7},{7,5},{8,10},{10,8},{9,1... | collective-permute-start | bytes 3080 | tf_op jit(solution)/shard_map/ppermute | solution.py:33
  34.4 0.7 %collective-permute-done.16 = bf16[88,1152]{1,0:T(8,128)(2,1)S(1)} collective-permute-done((bf16[88,1152]{1,0:T(8,128)(2,1)S(1)}, bf16[88,1152]{1,0:T(8,128)(2,1)S(1)}, u32[]{:S(2)}, u32[]{:S(2)}) %collective-permute-start.16) | collective-permute-done | bytes 202784 | tf_op jit(solution)/shard_map/ppermute | solution.py:33
  35.4 1.0 %constant_dynamic-update-slice_fusion.3 = bf16[4096,128]{1,0:T(8,128)(2,1)} fusion(bf16[1,128,128]{2,1,0:T(8,128)(2,1)S(1)} %copy-done.5, bf16[128,256]{1,0:T(8,128)(2,1)S(1)} %slice.182, bf16[128,256]{1,0:T(8,128)(2,1)S(1)} %convolution_convert_fusion.33, bf16[3,128,256]{2,1,0:T(8,128)(2,1)S(1)} %get-tuple-element.66), kind=kOutput, calls=%fused_computation.164 | convolution fusion | flops 25493504 | bytes 294912 | tf_op jit(solution)/shard_map/ct,cp->tp/dot_general | solution.py:229
  36.4 1.1 %constant_dynamic-update-slice_fusion.2 = bf16[4096,128]{1,0:T(8,128)(2,1)} fusion(bf16[4096,128]{1,0:T(8,128)(2,1)} %constant_dynamic-update-slice_fusion.3, bf16[1,128,128]{2,1,0:T(8,128)(2,1)S(1)} %copy-done.5, bf16[88,640]{1,0:T(8,128)(2,1)S(1)} %collective-permute-done.15, bf16[128,640]{1,0:T(8,128)(2,1)S(1)} %convolution_convert_fusion.25, ...), kind=kOutput, calls=%fused_computation.163 | convolution fusion | flops 64225280 | bytes 538624 | tf_op jit(solution)/shard_map/ct,cp->tp/dot_general | solution.py:229
  37.5 0.5 collective-permute-done.14
  38.3 2.4 %collective-permute-start.18 = (bf16[88,896]{1,0:T(8,128)(2,1)S(1)}, bf16[88,896]{1,0:T(8,128)(2,1)S(1)}, u32[]{:S(2)}, u32[]{:S(2)}) collective-permute-start(bf16[88,896]{1,0:T(8,128)(2,1)S(1)} %convolution_convert_fusion.28), channel_id=1, source_target_pairs={{0,8},{8,0},{4,12},{12,4},{1,9},{9,1},{5,13},{13,5},{2,10},{10,2},... | collective-permute-start | bytes 473096 | tf_op jit(solution)/shard_map/ppermute | solution.py:33
  41.2 9.7 %collective-permute-done.12 = bf16[88,1152]{1,0:T(8,128)(2,1)S(1)} collective-permute-done((bf16[88,1152]{1,0:T(8,128)(2,1)S(1)}, bf16[88,1152]{1,0:T(8,128)(2,1)S(1)}, u32[]{:S(2)}, u32[]{:S(2)}) %collective-permute-start.12) | collective-permute-done | bytes 202784 | tf_op jit(solution)/shard_map/ppermute | solution.py:33
  50.9 1.2 %constant_dynamic-update-slice_fusion.1 = bf16[4096,128]{1,0:T(8,128)(2,1)} fusion(bf16[4096,128]{1,0:T(8,128)(2,1)} %constant_dynamic-update-slice_fusion.2, bf16[1,128,128]{2,1,0:T(8,128)(2,1)S(1)} %copy-done.5, bf16[88,1152]{1,0:T(8,128)(2,1)S(1)} %collective-permute-done.12, bf16[128,1152]{1,0:T(8,128)(2,1)S(1)} %convolution_convert_fusion.11, ...), kind=kOutput, calls=%fused_computation.162 | convolution fusion | flops 115605504 | bytes 890880 | tf_op jit(solution)/shard_map/ct,cp->tp/dot_general | solution.py:229
  52.1 0.6 %slice.183 = bf16[1,1]{1,0:T(2,128)(2,1)} slice(bf16[8,64]{1,0:T(8,128)(2,1)S(1)} %max.11), slice={[0:1], [0:1]} | slice | bytes 4 | tf_op jit(solution)/shard_map/slice | solution.py:327
  53.3 1.8 %collective-permute-done.17 = bf16[88,1152]{1,0:T(8,128)(2,1)S(1)} collective-permute-done((bf16[88,1152]{1,0:T(8,128)(2,1)S(1)}, bf16[88,1152]{1,0:T(8,128)(2,1)S(1)}, u32[]{:S(2)}, u32[]{:S(2)}) %collective-permute-start.17) | collective-permute-done | bytes 202784 | tf_op jit(solution)/shard_map/ppermute | solution.py:33
  55.1 1.2 %constant_dynamic-update-slice_fusion = bf16[4096,128]{1,0:T(8,128)(2,1)} fusion(bf16[4096,128]{1,0:T(8,128)(2,1)} %constant_dynamic-update-slice_fusion.1, bf16[1,128,128]{2,1,0:T(8,128)(2,1)S(1)} %copy-done.5, bf16[88,1152]{1,0:T(8,128)(2,1)S(1)} %collective-permute-done.17, bf16[128,1152]{1,0:T(8,128)(2,1)S(1)} %convolution_convert_fusion.7, ...), kind=kOutput, calls=%fused_computation.161 | convolution fusion | flops 115605504 | bytes 890880 | tf_op jit(solution)/shard_map/ct,cp->tp/dot_general | solution.py:229
  56.3 0.5 collective-permute-done.18
  56.8 1.1 %fusion.20 = bf16[4096,128]{1,0:T(8,128)(2,1)} fusion(bf16[4096,128]{1,0:T(8,128)(2,1)} %constant_dynamic-update-slice_fusion, bf16[88,896]{1,0:T(8,128)(2,1)S(1)} %collective-permute-done.18, bf16[128,896]{1,0:T(8,128)(2,1)S(1)} %convolution_convert_fusion.21, bf16[3,128,256]{2,1,0:T(8,128)(2,1)S(1)} %get-tuple-element.77, ...), kind=kOutput, calls=%fused_computation.45 | convolution fusion | flops 89915392 | bytes 714752 | tf_op jit(solution)/shard_map/ct,cp->tp/dot_general | solution.py:229
  (57 shorter events, 5.1 us)
Async XLA Ops:
  0.0 4.6 %copy-start = (bf16[4096,128]{1,0:T(8,128)(2,1)S(1)}, bf16[4096,128]{1,0:T(8,128)(2,1)}, u32[]{:S(2)}) copy-start(bf16[4096,128]{1,0:T(8,128)(2,1)} %refs_1_.2) | copy-start | bytes 3145732
  0.0 4.6 %copy-start.2 = (bf16[1,128,128]{2,1,0:T(8,128)(2,1)S(1)}, bf16[1,128,128]{2,1,0:T(8,128)(2,1)}, u32[]{:S(2)}) copy-start(bf16[1,128,128]{2,1,0:T(8,128)(2,1)} %refs_0_.1) | copy-start | bytes 98308
  0.0 6.8 %copy-start.4 = (s32[1,3,64]{2,0,1:T(1,128)S(1)}, s32[1,3,64]{2,0,1:T(1,128)}, u32[]{:S(2)}) copy-start(s32[1,3,64]{2,0,1:T(1,128)} %param.9) | copy-start | bytes 2308
  0.0 6.8 %copy-start.3 = (bf16[1,3,64,128]{3,2,1,0:T(8,128)(2,1)S(1)}, bf16[1,3,64,128]{3,2,1,0:T(8,128)(2,1)}, u32[]{:S(2)}) copy-start(bf16[1,3,64,128]{3,2,1,0:T(8,128)(2,1)} %refs_1_.3) | copy-start | bytes 147460
  1.5 6.6 %collective-permute-start.3 = (bf16[128,256]{1,0:T(8,128)(2,1)S(1)}, bf16[128,256]{1,0:T(8,128)(2,1)S(1)}, u32[]{:S(2)}, u32[]{:S(2)}) collective-permute-start(bf16[128,256]{1,0:T(8,128)(2,1)S(1)} %get-tuple-element.63), channel_id=1, source_target_pairs={{0,2},{2,0},{1,3},{3,1},{4,6},{6,4},{5,7},{7,5},{8,10},{10,8},{9,1... | collective-permute-start | bytes 196616 | tf_op jit(solution)/shard_map/ppermute | solution.py:33
  4.5 7.1 %collective-permute-start.5 = (bf16[128,640]{1,0:T(8,128)(2,1)S(1)}, bf16[128,640]{1,0:T(8,128)(2,1)S(1)}, u32[]{:S(2)}, u32[]{:S(2)}) collective-permute-start(bf16[128,640]{1,0:T(8,128)(2,1)S(1)} %get-tuple-element.67), channel_id=1, source_target_pairs={{0,2},{2,0},{1,3},{3,1},{4,6},{6,4},{5,7},{7,5},{8,10},{10,8},{9,1... | collective-permute-start | bytes 491528 | tf_op jit(solution)/shard_map/ppermute | solution.py:33
  4.8 14.4 %collective-permute-start.7 = (bf16[128,1152]{1,0:T(8,128)(2,1)S(1)}, bf16[128,1152]{1,0:T(8,128)(2,1)S(1)}, u32[]{:S(2)}, u32[]{:S(2)}) collective-permute-start(bf16[128,1152]{1,0:T(8,128)(2,1)S(1)} %convolution_convert_fusion.14), channel_id=1, source_target_pairs={{0,2},{2,0},{1,3},{3,1},{4,6},{6,4},{5,7},{7,5},{8,10},{10,8},{9,1... | collective-permute-start | bytes 884744 | tf_op jit(solution)/shard_map/ppermute | solution.py:33
  8.3 5.4 %collective-permute-start.4 = (bf16[128,384]{1,0:T(8,128)(2,1)S(1)}, bf16[128,384]{1,0:T(8,128)(2,1)S(1)}, u32[]{:S(2)}, u32[]{:S(2)}) collective-permute-start(bf16[128,384]{1,0:T(8,128)(2,1)S(1)} %pad_maximum_fusion.12), channel_id=1, source_target_pairs={{0,4},{4,0},{8,12},{12,8},{1,5},{5,1},{9,13},{13,9},{2,6},{6,2},{1... | collective-permute-start | bytes 294920 | tf_op jit(solution)/shard_map/ppermute | solution.py:33
  11.8 8.9 %collective-permute-start.8 = (bf16[128,640]{1,0:T(8,128)(2,1)S(1)}, bf16[128,640]{1,0:T(8,128)(2,1)S(1)}, u32[]{:S(2)}, u32[]{:S(2)}) collective-permute-start(bf16[128,640]{1,0:T(8,128)(2,1)S(1)} %convolution_convert_fusion.26), channel_id=1, source_target_pairs={{0,4},{4,0},{8,12},{12,8},{1,5},{5,1},{9,13},{13,9},{2,6},{6,2},{1... | collective-permute-start | bytes 491528 | tf_op jit(solution)/shard_map/ppermute | solution.py:33
  14.1 6.3 %collective-permute-start.6 = (bf16[128,384]{1,0:T(8,128)(2,1)S(1)}, bf16[128,384]{1,0:T(8,128)(2,1)S(1)}, u32[]{:S(2)}, u32[]{:S(2)}) collective-permute-start(bf16[128,384]{1,0:T(8,128)(2,1)S(1)} %pad_maximum_fusion.13), channel_id=1, source_target_pairs={{0,8},{8,0},{4,12},{12,4},{1,9},{9,1},{5,13},{13,5},{2,10},{10,2},... | collective-permute-start | bytes 294920 | tf_op jit(solution)/shard_map/ppermute | solution.py:33
  16.7 9.2 %collective-permute-start.10 = (bf16[128,1152]{1,0:T(8,128)(2,1)S(1)}, bf16[128,1152]{1,0:T(8,128)(2,1)S(1)}, u32[]{:S(2)}, u32[]{:S(2)}) collective-permute-start(bf16[128,1152]{1,0:T(8,128)(2,1)S(1)} %convolution_convert_fusion.13), channel_id=1, source_target_pairs={{0,2},{2,0},{1,3},{3,1},{4,6},{6,4},{5,7},{7,5},{8,10},{10,8},{9,1... | collective-permute-start | bytes 884744 | tf_op jit(solution)/shard_map/ppermute | solution.py:33
  18.3 10.3 %collective-permute-start.13 = (bf16[128,896]{1,0:T(8,128)(2,1)S(1)}, bf16[128,896]{1,0:T(8,128)(2,1)S(1)}, u32[]{:S(2)}, u32[]{:S(2)}) collective-permute-start(bf16[128,896]{1,0:T(8,128)(2,1)S(1)} %convolution_convert_fusion.23), channel_id=1, source_target_pairs={{0,2},{2,0},{1,3},{3,1},{4,6},{6,4},{5,7},{7,5},{8,10},{10,8},{9,1... | collective-permute-start | bytes 688136 | tf_op jit(solution)/shard_map/ppermute | solution.py:33
  19.5 8.9 %collective-permute-start.9 = (bf16[88,1152]{1,0:T(8,128)(2,1)S(1)}, bf16[88,1152]{1,0:T(8,128)(2,1)S(1)}, u32[]{:S(2)}, u32[]{:S(2)}) collective-permute-start(bf16[88,1152]{1,0:T(8,128)(2,1)S(1)} %convolution_convert_fusion.18), channel_id=1, source_target_pairs={{0,4},{4,0},{8,12},{12,8},{1,5},{5,1},{9,13},{13,9},{2,6},{6,2},{1... | collective-permute-start | bytes 608264 | tf_op jit(solution)/shard_map/ppermute | solution.py:33
  21.4 15.0 %collective-permute-start.15 = (bf16[88,640]{1,0:T(8,128)(2,1)S(1)}, bf16[88,640]{1,0:T(8,128)(2,1)S(1)}, u32[]{:S(2)}, u32[]{:S(2)}) collective-permute-start(bf16[88,640]{1,0:T(8,128)(2,1)S(1)} %convolution_convert_fusion.30), channel_id=1, source_target_pairs={{0,8},{8,0},{4,12},{12,4},{1,9},{9,1},{5,13},{13,5},{2,10},{10,2},... | collective-permute-start | bytes 337928 | tf_op jit(solution)/shard_map/ppermute | solution.py:33
  26.2 8.9 %collective-permute-start.16 = (bf16[88,1152]{1,0:T(8,128)(2,1)S(1)}, bf16[88,1152]{1,0:T(8,128)(2,1)S(1)}, u32[]{:S(2)}, u32[]{:S(2)}) collective-permute-start(bf16[88,1152]{1,0:T(8,128)(2,1)S(1)} %convolution_convert_fusion.17), channel_id=1, source_target_pairs={{0,4},{4,0},{8,12},{12,8},{1,5},{5,1},{9,13},{13,9},{2,6},{6,2},{1... | collective-permute-start | bytes 608264 | tf_op jit(solution)/shard_map/ppermute | solution.py:33
  28.9 9.2 %collective-permute-start.14 = (bf16[88,896]{1,0:T(8,128)(2,1)S(1)}, bf16[88,896]{1,0:T(8,128)(2,1)S(1)}, u32[]{:S(2)}, u32[]{:S(2)}) collective-permute-start(bf16[88,896]{1,0:T(8,128)(2,1)S(1)} %convolution_convert_fusion.29), channel_id=1, source_target_pairs={{0,4},{4,0},{8,12},{12,8},{1,5},{5,1},{9,13},{13,9},{2,6},{6,2},{1... | collective-permute-start | bytes 473096 | tf_op jit(solution)/shard_map/ppermute | solution.py:33
  30.2 20.7 %collective-permute-start.12 = (bf16[88,1152]{1,0:T(8,128)(2,1)S(1)}, bf16[88,1152]{1,0:T(8,128)(2,1)S(1)}, u32[]{:S(2)}, u32[]{:S(2)}) collective-permute-start(bf16[88,1152]{1,0:T(8,128)(2,1)S(1)} %convolution_convert_fusion.16), channel_id=1, source_target_pairs={{0,8},{8,0},{4,12},{12,4},{1,9},{9,1},{5,13},{13,5},{2,10},{10,2},... | collective-permute-start | bytes 608264 | tf_op jit(solution)/shard_map/ppermute | solution.py:33
  33.0 19.0 %collective-permute-start.11 = (bf16[8,64]{1,0:T(8,128)(2,1)S(1)}, bf16[8,64]{1,0:T(8,128)(2,1)S(1)}, u32[]{:S(2)}, u32[]{:S(2)}) collective-permute-start(bf16[8,64]{1,0:T(8,128)(2,1)S(1)} %slice_maximum_fusion), channel_id=1, source_target_pairs={{0,2},{2,0},{1,3},{3,1},{4,6},{6,4},{5,7},{7,5},{8,10},{10,8},{9,1... | collective-permute-start | bytes 3080 | tf_op jit(solution)/shard_map/ppermute | solution.py:33
  34.4 1.0 %copy-start.5 = (bf16[1,128,128]{2,1,0:T(8,128)(2,1)S(1)}, bf16[1,128,128]{2,1,0:T(8,128)(2,1)}, u32[]{:S(2)}) copy-start(bf16[1,128,128]{2,1,0:T(8,128)(2,1)} %param.11) | copy-start | bytes 98308
  35.3 19.8 %collective-permute-start.17 = (bf16[88,1152]{1,0:T(8,128)(2,1)S(1)}, bf16[88,1152]{1,0:T(8,128)(2,1)S(1)}, u32[]{:S(2)}, u32[]{:S(2)}) collective-permute-start(bf16[88,1152]{1,0:T(8,128)(2,1)S(1)} %convolution_convert_fusion.15), channel_id=1, source_target_pairs={{0,8},{8,0},{4,12},{12,4},{1,9},{9,1},{5,13},{13,5},{2,10},{10,2},... | collective-permute-start | bytes 608264 | tf_op jit(solution)/shard_map/ppermute | solution.py:33
  38.3 18.5 %collective-permute-start.18 = (bf16[88,896]{1,0:T(8,128)(2,1)S(1)}, bf16[88,896]{1,0:T(8,128)(2,1)S(1)}, u32[]{:S(2)}, u32[]{:S(2)}) collective-permute-start(bf16[88,896]{1,0:T(8,128)(2,1)S(1)} %convolution_convert_fusion.28), channel_id=1, source_target_pairs={{0,8},{8,0},{4,12},{12,4},{1,9},{9,1},{5,13},{13,5},{2,10},{10,2},... | collective-permute-start | bytes 473096 | tf_op jit(solution)/shard_map/ppermute | solution.py:33

commit v16 on v15

--- a/solution.py
+++ b/solution.py
@@ -12,8 +12,8 @@
 COUNT_READ = 2
 LOOK = (3, -1)
 ORDER = (
-    (0, 0), (0, 1), (0, 2), (1, 0), (1, 1), (0, 3), (2, 0), (0, 4), (1, 2), LOOK, (2, 1), (1, 3),
-    (2, 2), (1, 4), (2, 3), (3, 0), (3, 1), (2, 4), (3, 2), (3, 3), (3, 4),
+    (0, 0), (0, 1), (0, 2), (1, 0), (1, 1), (0, 3), (2, 0), (1, 2), LOOK, (2, 1), (0, 4), (1, 3),
+    (2, 2), (3, 0), (1, 4), (2, 3), (3, 1), (2, 4), (3, 2), (3, 3), (3, 4),
 )
 KERNEL_VMEM = 16 * 1024 * 1024
 ROOM_SIXTEENTHS = 11

time: 58.1 us -> 55.9 us (0.962)
  waiting for transfers between devices: 17 us -> 10.6 us
  matrix products: 10.9 us -> 14 us
  starting transfers between devices: 25.6 us -> 26.6 us
    ppermute x16, waiting for transfers between devices: 17 us -> 10.6 us  [from_partner(): return lax.ppermute(block, hop[0], route(*hop))]
    dot_general x17, matrix products: 3.76 us -> 6.84 us  [times(): jnp.dot(matrix, value, preferred_element_type=jnp.float32)]
    ppermute x16, starting transfers between devices: 25.6 us -> 26.6 us  [from_partner(): return lax.ppermute(block, hop[0], route(*hop))]
  transfers between devices with their start and end apart: 16 -> 16, of which waited for: 8 -> 6; matrix products, arithmetic and copies ran while one was open for 18% -> 24% of each run, Pallas kernels for 2% -> 2%
where the time goes in v16:
time: 55.9 us; the launch traced here: 55.8 us
  starting transfers between devices  26.6 us (48%)
  matrix products  14 us (25%)
  waiting for transfers between devices  10.6 us (19%)
  Pallas kernels  2.63 us (5%)
  between operations  0.91 us (2%)
  local copies, waits for them, and re-layouts  0.86 us (2%)
    ppermute x16, starting transfers between devices, from_partner(): return lax.ppermute(block, hop[0], route(*hop))  26.6 us
    ppermute x16, waiting for transfers between devices, from_partner(): return lax.ppermute(block, hop[0], route(*hop))  10.6 us
    dot_general x17, matrix products, times(): jnp.dot(matrix, value, preferred_element_type=jnp.float32)  6.84 us
    dot_general x5, matrix products, evaluated(): jnp.einsum('ct,cp->tp', coeffs, evaluation, preferred_element_type=jnp.fl...  5.65 us
    pallas_call x1, Pallas kernels, early(): pl.pallas_call(lambda *refs: early_kernel(starts, *refs), out_shape=[jax....  1.45 us
    pallas_call x1, Pallas kernels, tables(): pl.pallas_call(lambda *refs: tables_kernel(wide, room, *refs), out_shape=...  1.18 us
  transfers between devices with their start and end apart: 16, of which 6 were waited for; matrix products, arithmetic and copies ran while one was open for 24% of the time, Pallas kernels for 2%

profile of v16, /device:TPU:0, one launch (start us, length us, event | category | flops | bytes accessed | tf_op | source)
XLA Modules:
  0.0 55.8 jit_solution(1452195724909600416)
XLA Ops:
  0.0 1.4 %early.1 = (bf16[128,256]{1,0:T(8,128)(2,1)S(1)}, bf16[128,640]{1,0:T(8,128)(2,1)S(1)}) custom-call(bf16[1,128,128]{2,1,0:T(8,128)(2,1)} %refs_0_.1, bf16[4096,128]{1,0:T(8,128)(2,1)} %refs_1_.2), custom_call_target="tpu_custom_call" | custom-call | flops 29360128 | bytes 458752 | tf_op jit(solution)/shard_map/early/pallas_call | solution.py:69
  1.5 3.0 %collective-permute-start.3 = (bf16[128,256]{1,0:T(8,128)(2,1)S(1)}, bf16[128,256]{1,0:T(8,128)(2,1)S(1)}, u32[]{:S(2)}, u32[]{:S(2)}) collective-permute-start(bf16[128,256]{1,0:T(8,128)(2,1)S(1)} %get-tuple-element.63), channel_id=1, source_target_pairs={{0,2},{2,0},{1,3},{3,1},{4,6},{6,4},{5,7},{7,5},{8,10},{10,8},{9,1... | collective-permute-start | bytes 196616 | tf_op jit(solution)/shard_map/ppermute | solution.py:33
  4.8 2.0 %collective-permute-start.7 = (bf16[128,1152]{1,0:T(8,128)(2,1)S(1)}, bf16[128,1152]{1,0:T(8,128)(2,1)S(1)}, u32[]{:S(2)}, u32[]{:S(2)}) collective-permute-start(bf16[128,1152]{1,0:T(8,128)(2,1)S(1)} %convolution_convert_fusion.14), channel_id=1, source_target_pairs={{0,2},{2,0},{1,3},{3,1},{4,6},{6,4},{5,7},{7,5},{8,10},{10,8},{9,1... | collective-permute-start | bytes 884744 | tf_op jit(solution)/shard_map/ppermute | solution.py:33
  6.8 1.2 %tables.1 = (bf16[3,128,256]{2,1,0:T(8,128)(2,1)S(1)}, bf16[3,128,256]{2,1,0:T(8,128)(2,1)S(1)}, bf16[3,128,128]{2,1,0:T(8,128)(2,1)S(1)}) custom-call(s32[3,1,64]{2,1,0:T(1,128)S(1)} %bitcast.111, bf16[1,3,64,128]{3,2,1,0:T(8,128)(2,1)S(1)} %copy-done.4), custom_call_target="tpu_custom_call" | custom-call | flops 50000000 | bytes 600000 | tf_op jit(solution)/shard_map/tables/pallas_call | solution.py:152
  8.3 1.6 %collective-permute-start.4 = (bf16[128,384]{1,0:T(8,128)(2,1)S(1)}, bf16[128,384]{1,0:T(8,128)(2,1)S(1)}, u32[]{:S(2)}, u32[]{:S(2)}) collective-permute-start(bf16[128,384]{1,0:T(8,128)(2,1)S(1)} %pad_maximum_fusion.12), channel_id=1, source_target_pairs={{0,4},{4,0},{8,12},{12,8},{1,5},{5,1},{9,13},{13,9},{2,6},{6,2},{1... | collective-permute-start | bytes 294920 | tf_op jit(solution)/shard_map/ppermute | solution.py:33
  9.9 1.7 %collective-permute-done.5 = bf16[128,640]{1,0:T(8,128)(2,1)S(1)} collective-permute-done((bf16[128,640]{1,0:T(8,128)(2,1)S(1)}, bf16[128,640]{1,0:T(8,128)(2,1)S(1)}, u32[]{:S(2)}, u32[]{:S(2)}) %collective-permute-start.5) | collective-permute-done | bytes 163872 | tf_op jit(solution)/shard_map/ppermute | solution.py:33
  11.8 1.6 %collective-permute-start.8 = (bf16[128,640]{1,0:T(8,128)(2,1)S(1)}, bf16[128,640]{1,0:T(8,128)(2,1)S(1)}, u32[]{:S(2)}, u32[]{:S(2)}) collective-permute-start(bf16[128,640]{1,0:T(8,128)(2,1)S(1)} %convolution_convert_fusion.26), channel_id=1, source_target_pairs={{0,4},{4,0},{8,12},{12,8},{1,5},{5,1},{9,13},{13,9},{2,6},{6,2},{1... | collective-permute-start | bytes 491528 | tf_op jit(solution)/shard_map/ppermute | solution.py:33
  13.9 1.4 %collective-permute-start.10 = (bf16[128,1152]{1,0:T(8,128)(2,1)S(1)}, bf16[128,1152]{1,0:T(8,128)(2,1)S(1)}, u32[]{:S(2)}, u32[]{:S(2)}) collective-permute-start(bf16[128,1152]{1,0:T(8,128)(2,1)S(1)} %convolution_convert_fusion.13), channel_id=1, source_target_pairs={{0,2},{2,0},{1,3},{3,1},{4,6},{6,4},{5,7},{7,5},{8,10},{10,8},{9,1... | collective-permute-start | bytes 884744 | tf_op jit(solution)/shard_map/ppermute | solution.py:33
  15.5 2.6 %collective-permute-start.6 = (bf16[128,384]{1,0:T(8,128)(2,1)S(1)}, bf16[128,384]{1,0:T(8,128)(2,1)S(1)}, u32[]{:S(2)}, u32[]{:S(2)}) collective-permute-start(bf16[128,384]{1,0:T(8,128)(2,1)S(1)} %pad_maximum_fusion.13), channel_id=1, source_target_pairs={{0,8},{8,0},{4,12},{12,4},{1,9},{9,1},{5,13},{13,5},{2,10},{10,2},... | collective-permute-start | bytes 294920 | tf_op jit(solution)/shard_map/ppermute | solution.py:33
  18.5 1.6 %collective-permute-start.9 = (bf16[88,1152]{1,0:T(8,128)(2,1)S(1)}, bf16[88,1152]{1,0:T(8,128)(2,1)S(1)}, u32[]{:S(2)}, u32[]{:S(2)}) collective-permute-start(bf16[88,1152]{1,0:T(8,128)(2,1)S(1)} %convolution_convert_fusion.18), channel_id=1, source_target_pairs={{0,4},{4,0},{8,12},{12,8},{1,5},{5,1},{9,13},{13,9},{2,6},{6,2},{1... | collective-permute-start | bytes 608264 | tf_op jit(solution)/shard_map/ppermute | solution.py:33
  20.1 1.2 %collective-permute-done.6 = bf16[128,384]{1,0:T(8,128)(2,1)S(1)} collective-permute-done((bf16[128,384]{1,0:T(8,128)(2,1)S(1)}, bf16[128,384]{1,0:T(8,128)(2,1)S(1)}, u32[]{:S(2)}, u32[]{:S(2)}) %collective-permute-start.6) | collective-permute-done | bytes 98336 | tf_op jit(solution)/shard_map/ppermute | solution.py:33
  22.3 3.4 %collective-permute-start.15 = (bf16[88,640]{1,0:T(8,128)(2,1)S(1)}, bf16[88,640]{1,0:T(8,128)(2,1)S(1)}, u32[]{:S(2)}, u32[]{:S(2)}) collective-permute-start(bf16[88,640]{1,0:T(8,128)(2,1)S(1)} %convolution_convert_fusion.30), channel_id=1, source_target_pairs={{0,8},{8,0},{4,12},{12,4},{1,9},{9,1},{5,13},{13,5},{2,10},{10,2},... | collective-permute-start | bytes 337928 | tf_op jit(solution)/shard_map/ppermute | solution.py:33
  26.0 0.7 %collective-permute-start.13 = (bf16[128,896]{1,0:T(8,128)(2,1)S(1)}, bf16[128,896]{1,0:T(8,128)(2,1)S(1)}, u32[]{:S(2)}, u32[]{:S(2)}) collective-permute-start(bf16[128,896]{1,0:T(8,128)(2,1)S(1)} %convolution_convert_fusion.23), channel_id=1, source_target_pairs={{0,2},{2,0},{1,3},{3,1},{4,6},{6,4},{5,7},{7,5},{8,10},{10,8},{9,1... | collective-permute-start | bytes 688136 | tf_op jit(solution)/shard_map/ppermute | solution.py:33
  27.3 1.4 %collective-permute-start.16 = (bf16[88,1152]{1,0:T(8,128)(2,1)S(1)}, bf16[88,1152]{1,0:T(8,128)(2,1)S(1)}, u32[]{:S(2)}, u32[]{:S(2)}) collective-permute-start(bf16[88,1152]{1,0:T(8,128)(2,1)S(1)} %convolution_convert_fusion.17), channel_id=1, source_target_pairs={{0,4},{4,0},{8,12},{12,8},{1,5},{5,1},{9,13},{13,9},{2,6},{6,2},{1... | collective-permute-start | bytes 608264 | tf_op jit(solution)/shard_map/ppermute | solution.py:33
  28.6 1.0 %convolution_convert_fusion.10 = bf16[128,1152]{1,0:T(8,128)(2,1)} fusion(bf16[128,256]{1,0:T(8,128)(2,1)S(1)} %get-tuple-element.86, bf16[128,1152]{1,0:T(8,128)(2,1)S(1)} %collective-permute-done.10, bf16[128,1152]{1,0:T(8,128)(2,1)S(1)} %convolution_convert_fusion.13), kind=kOutput, calls=%fused_computation.35 | convolution fusion | flops 76824576 | bytes 950272 | tf_op jit(solution)/shard_map/dot_general | solution.py:219
  30.0 1.0 %convolution_convert_fusion.11 = bf16[128,1152]{1,0:T(8,128)(2,1)} fusion(bf16[128,256]{1,0:T(8,128)(2,1)S(1)} %slice_bitcast_fusion.7, bf16[88,1152]{1,0:T(8,128)(2,1)S(1)} %collective-permute-done.9, bf16[128,1152]{1,0:T(8,128)(2,1)S(1)} %convolution_convert_fusion.12), kind=kOutput, calls=%fused_computation.36 | convolution fusion | flops 77709312 | bytes 858112 | tf_op jit(solution)/shard_map/dot_general | solution.py:219
  31.0 2.0 %collective-permute-start.11 = (bf16[8,64]{1,0:T(8,128)(2,1)S(1)}, bf16[8,64]{1,0:T(8,128)(2,1)S(1)}, u32[]{:S(2)}, u32[]{:S(2)}) collective-permute-start(bf16[8,64]{1,0:T(8,128)(2,1)S(1)} %slice_maximum_fusion), channel_id=1, source_target_pairs={{0,2},{2,0},{1,3},{3,1},{4,6},{6,4},{5,7},{7,5},{8,10},{10,8},{9,1... | collective-permute-start | bytes 3080 | tf_op jit(solution)/shard_map/ppermute | solution.py:33
  32.9 1.0 %constant_dynamic-update-slice_fusion.3 = bf16[4096,128]{1,0:T(8,128)(2,1)} fusion(bf16[1,128,128]{2,1,0:T(8,128)(2,1)S(1)} %copy-done.6, bf16[128,256]{1,0:T(8,128)(2,1)S(1)} %slice-done, bf16[128,256]{1,0:T(8,128)(2,1)S(1)} %convolution_convert_fusion.33, bf16[3,128,256]{2,1,0:T(8,128)(2,1)S(1)} %get-tuple-element.66), kind=kOutput, calls=%fused_computation.164 | convolution fusion | flops 25493504 | bytes 294912 | tf_op jit(solution)/shard_map/ct,cp->tp/dot_general | solution.py:229
  34.3 0.9 %convolution_convert_fusion.22 = bf16[128,896]{1,0:T(8,128)(2,1)} fusion(bf16[128,256]{1,0:T(8,128)(2,1)S(1)} %get-tuple-element.86, bf16[128,896]{1,0:T(8,128)(2,1)S(1)} %collective-permute-done.13, bf16[128,896]{1,0:T(8,128)(2,1)S(1)} %convolution_convert_fusion.23), kind=kOutput, calls=%fused_computation.48 | convolution fusion | flops 59752448 | bytes 753664 | tf_op jit(solution)/shard_map/dot_general | solution.py:219
  35.3 0.9 %collective-permute-done.16 = bf16[88,1152]{1,0:T(8,128)(2,1)S(1)} collective-permute-done((bf16[88,1152]{1,0:T(8,128)(2,1)S(1)}, bf16[88,1152]{1,0:T(8,128)(2,1)S(1)}, u32[]{:S(2)}, u32[]{:S(2)}) %collective-permute-start.16) | collective-permute-done | bytes 202784 | tf_op jit(solution)/shard_map/ppermute | solution.py:33
  36.2 1.2 %convolution_convert_fusion.15 = bf16[88,1152]{1,0:T(8,128)(2,1)S(1)} fusion(bf16[88,1152]{1,0:T(8,128)(2,1)S(1)} %collective-permute-done.16, bf16[128,1152]{1,0:T(8,128)(2,1)} %convolution_convert_fusion.10, bf16[44,256]{1,0:T(8,128)(2,1)S(1)} %convolution_convert_fusion.37, bf16[44,256]{1,0:T(8,128)(2,1)S(1)} %convolution_convert_fusion.38), kind=kOutput, calls=%fused_computation.40 | convolution fusion | flops 54160384 | bytes 745472 | tf_op jit(solution)/shard_map/dot_general | solution.py:219
  37.4 2.0 %collective-permute-start.17 = (bf16[88,1152]{1,0:T(8,128)(2,1)S(1)}, bf16[88,1152]{1,0:T(8,128)(2,1)S(1)}, u32[]{:S(2)}, u32[]{:S(2)}) collective-permute-start(bf16[88,1152]{1,0:T(8,128)(2,1)S(1)} %convolution_convert_fusion.15), channel_id=1, source_target_pairs={{0,8},{8,0},{4,12},{12,4},{1,9},{9,1},{5,13},{13,5},{2,10},{10,2},... | collective-permute-start | bytes 608264 | tf_op jit(solution)/shard_map/ppermute | solution.py:33
  39.4 1.1 %constant_dynamic-update-slice_fusion.2 = bf16[4096,128]{1,0:T(8,128)(2,1)} fusion(bf16[4096,128]{1,0:T(8,128)(2,1)} %constant_dynamic-update-slice_fusion.3, bf16[1,128,128]{2,1,0:T(8,128)(2,1)S(1)} %copy-done.6, bf16[88,640]{1,0:T(8,128)(2,1)S(1)} %collective-permute-done.15, bf16[128,640]{1,0:T(8,128)(2,1)S(1)} %convolution_convert_fusion.25, ...), kind=kOutput, calls=%fused_computation.163 | convolution fusion | flops 64225280 | bytes 538624 | tf_op jit(solution)/shard_map/ct,cp->tp/dot_general | solution.py:229
  40.8 0.4 collective-permute-done.14
  41.2 0.3 copy-done.7
  41.7 2.7 %collective-permute-start.18 = (bf16[88,896]{1,0:T(8,128)(2,1)S(1)}, bf16[88,896]{1,0:T(8,128)(2,1)S(1)}, u32[]{:S(2)}, u32[]{:S(2)}) collective-permute-start(bf16[88,896]{1,0:T(8,128)(2,1)S(1)} %convolution_convert_fusion.28), channel_id=1, source_target_pairs={{0,8},{8,0},{4,12},{12,4},{1,9},{9,1},{5,13},{13,5},{2,10},{10,2},... | collective-permute-start | bytes 473096 | tf_op jit(solution)/shard_map/ppermute | solution.py:33
  44.4 1.2 %constant_dynamic-update-slice_fusion.1 = bf16[4096,128]{1,0:T(8,128)(2,1)} fusion(bf16[4096,128]{1,0:T(8,128)(2,1)} %constant_dynamic-update-slice_fusion.2, bf16[1,128,128]{2,1,0:T(8,128)(2,1)S(1)} %copy-done.6, bf16[88,1152]{1,0:T(8,128)(2,1)S(1)} %collective-permute-done.12, bf16[128,1152]{1,0:T(8,128)(2,1)S(1)} %copy-done.9, ...), kind=kOutput, calls=%fused_computation.162 | convolution fusion | flops 115605504 | bytes 890880 | tf_op jit(solution)/shard_map/ct,cp->tp/dot_general | solution.py:229
  45.6 0.5 slice.183
  47.0 5.2 %collective-permute-done.17 = bf16[88,1152]{1,0:T(8,128)(2,1)S(1)} collective-permute-done((bf16[88,1152]{1,0:T(8,128)(2,1)S(1)}, bf16[88,1152]{1,0:T(8,128)(2,1)S(1)}, u32[]{:S(2)}, u32[]{:S(2)}) %collective-permute-start.17) | collective-permute-done | bytes 202784 | tf_op jit(solution)/shard_map/ppermute | solution.py:33
  52.2 1.2 %constant_dynamic-update-slice_fusion = bf16[4096,128]{1,0:T(8,128)(2,1)} fusion(bf16[4096,128]{1,0:T(8,128)(2,1)} %constant_dynamic-update-slice_fusion.1, bf16[1,128,128]{2,1,0:T(8,128)(2,1)S(1)} %copy-done.6, bf16[88,1152]{1,0:T(8,128)(2,1)S(1)} %collective-permute-done.17, bf16[128,1152]{1,0:T(8,128)(2,1)S(1)} %convolution_convert_fusion.7, ...), kind=kOutput, calls=%fused_computation.161 | convolution fusion | flops 115605504 | bytes 890880 | tf_op jit(solution)/shard_map/ct,cp->tp/dot_general | solution.py:229
  53.4 1.2 %collective-permute-done.18 = bf16[88,896]{1,0:T(8,128)(2,1)S(1)} collective-permute-done((bf16[88,896]{1,0:T(8,128)(2,1)S(1)}, bf16[88,896]{1,0:T(8,128)(2,1)S(1)}, u32[]{:S(2)}, u32[]{:S(2)}) %collective-permute-start.18) | collective-permute-done | bytes 157728 | tf_op jit(solution)/shard_map/ppermute | solution.py:33
  54.6 1.1 %fusion.20 = bf16[4096,128]{1,0:T(8,128)(2,1)} fusion(bf16[4096,128]{1,0:T(8,128)(2,1)} %constant_dynamic-update-slice_fusion, bf16[88,896]{1,0:T(8,128)(2,1)S(1)} %collective-permute-done.18, bf16[128,896]{1,0:T(8,128)(2,1)S(1)} %convolution_convert_fusion.21, bf16[3,128,256]{2,1,0:T(8,128)(2,1)S(1)} %get-tuple-element.76, ...), kind=kOutput, calls=%fused_computation.45 | convolution fusion | flops 89915392 | bytes 714752 | tf_op jit(solution)/shard_map/ct,cp->tp/dot_general | solution.py:229
  (66 shorter events, 4.9 us)
Async XLA Ops:
  0.0 4.6 %copy-start = (bf16[4096,128]{1,0:T(8,128)(2,1)S(1)}, bf16[4096,128]{1,0:T(8,128)(2,1)}, u32[]{:S(2)}) copy-start(bf16[4096,128]{1,0:T(8,128)(2,1)} %refs_1_.2) | copy-start | bytes 3145732
  0.0 4.6 %copy-start.2 = (bf16[1,128,128]{2,1,0:T(8,128)(2,1)S(1)}, bf16[1,128,128]{2,1,0:T(8,128)(2,1)}, u32[]{:S(2)}) copy-start(bf16[1,128,128]{2,1,0:T(8,128)(2,1)} %refs_0_.1) | copy-start | bytes 98308
  0.0 6.8 %copy-start.5 = (s32[1,3,64]{2,0,1:T(1,128)S(1)}, s32[1,3,64]{2,0,1:T(1,128)}, u32[]{:S(2)}) copy-start(s32[1,3,64]{2,0,1:T(1,128)} %param.9) | copy-start | bytes 2308
  0.0 6.8 %copy-start.4 = (bf16[1,3,64,128]{3,2,1,0:T(8,128)(2,1)S(1)}, bf16[1,3,64,128]{3,2,1,0:T(8,128)(2,1)}, u32[]{:S(2)}) copy-start(bf16[1,3,64,128]{3,2,1,0:T(8,128)(2,1)} %refs_1_.3) | copy-start | bytes 147460
  1.5 6.6 %collective-permute-start.3 = (bf16[128,256]{1,0:T(8,128)(2,1)S(1)}, bf16[128,256]{1,0:T(8,128)(2,1)S(1)}, u32[]{:S(2)}, u32[]{:S(2)}) collective-permute-start(bf16[128,256]{1,0:T(8,128)(2,1)S(1)} %get-tuple-element.63), channel_id=1, source_target_pairs={{0,2},{2,0},{1,3},{3,1},{4,6},{6,4},{5,7},{7,5},{8,10},{10,8},{9,1... | collective-permute-start | bytes 196616 | tf_op jit(solution)/shard_map/ppermute | solution.py:33
  4.5 7.1 %collective-permute-start.5 = (bf16[128,640]{1,0:T(8,128)(2,1)S(1)}, bf16[128,640]{1,0:T(8,128)(2,1)S(1)}, u32[]{:S(2)}, u32[]{:S(2)}) collective-permute-start(bf16[128,640]{1,0:T(8,128)(2,1)S(1)} %get-tuple-element.67), channel_id=1, source_target_pairs={{0,2},{2,0},{1,3},{3,1},{4,6},{6,4},{5,7},{7,5},{8,10},{10,8},{9,1... | collective-permute-start | bytes 491528 | tf_op jit(solution)/shard_map/ppermute | solution.py:33
  4.8 13.4 %collective-permute-start.7 = (bf16[128,1152]{1,0:T(8,128)(2,1)S(1)}, bf16[128,1152]{1,0:T(8,128)(2,1)S(1)}, u32[]{:S(2)}, u32[]{:S(2)}) collective-permute-start(bf16[128,1152]{1,0:T(8,128)(2,1)S(1)} %convolution_convert_fusion.14), channel_id=1, source_target_pairs={{0,2},{2,0},{1,3},{3,1},{4,6},{6,4},{5,7},{7,5},{8,10},{10,8},{9,1... | collective-permute-start | bytes 884744 | tf_op jit(solution)/shard_map/ppermute | solution.py:33
  8.3 5.4 %collective-permute-start.4 = (bf16[128,384]{1,0:T(8,128)(2,1)S(1)}, bf16[128,384]{1,0:T(8,128)(2,1)S(1)}, u32[]{:S(2)}, u32[]{:S(2)}) collective-permute-start(bf16[128,384]{1,0:T(8,128)(2,1)S(1)} %pad_maximum_fusion.12), channel_id=1, source_target_pairs={{0,4},{4,0},{8,12},{12,8},{1,5},{5,1},{9,13},{13,9},{2,6},{6,2},{1... | collective-permute-start | bytes 294920 | tf_op jit(solution)/shard_map/ppermute | solution.py:33
  11.8 9.8 %collective-permute-start.8 = (bf16[128,640]{1,0:T(8,128)(2,1)S(1)}, bf16[128,640]{1,0:T(8,128)(2,1)S(1)}, u32[]{:S(2)}, u32[]{:S(2)}) collective-permute-start(bf16[128,640]{1,0:T(8,128)(2,1)S(1)} %convolution_convert_fusion.26), channel_id=1, source_target_pairs={{0,4},{4,0},{8,12},{12,8},{1,5},{5,1},{9,13},{13,9},{2,6},{6,2},{1... | collective-permute-start | bytes 491528 | tf_op jit(solution)/shard_map/ppermute | solution.py:33
  13.9 13.2 %collective-permute-start.10 = (bf16[128,1152]{1,0:T(8,128)(2,1)S(1)}, bf16[128,1152]{1,0:T(8,128)(2,1)S(1)}, u32[]{:S(2)}, u32[]{:S(2)}) collective-permute-start(bf16[128,1152]{1,0:T(8,128)(2,1)S(1)} %convolution_convert_fusion.13), channel_id=1, source_target_pairs={{0,2},{2,0},{1,3},{3,1},{4,6},{6,4},{5,7},{7,5},{8,10},{10,8},{9,1... | collective-permute-start | bytes 884744 | tf_op jit(solution)/shard_map/ppermute | solution.py:33
  15.5 5.8 %collective-permute-start.6 = (bf16[128,384]{1,0:T(8,128)(2,1)S(1)}, bf16[128,384]{1,0:T(8,128)(2,1)S(1)}, u32[]{:S(2)}, u32[]{:S(2)}) collective-permute-start(bf16[128,384]{1,0:T(8,128)(2,1)S(1)} %pad_maximum_fusion.13), channel_id=1, source_target_pairs={{0,8},{8,0},{4,12},{12,4},{1,9},{9,1},{5,13},{13,5},{2,10},{10,2},... | collective-permute-start | bytes 294920 | tf_op jit(solution)/shard_map/ppermute | solution.py:33
  18.5 11.1 %collective-permute-start.9 = (bf16[88,1152]{1,0:T(8,128)(2,1)S(1)}, bf16[88,1152]{1,0:T(8,128)(2,1)S(1)}, u32[]{:S(2)}, u32[]{:S(2)}) collective-permute-start(bf16[88,1152]{1,0:T(8,128)(2,1)S(1)} %convolution_convert_fusion.18), channel_id=1, source_target_pairs={{0,4},{4,0},{8,12},{12,8},{1,5},{5,1},{9,13},{13,9},{2,6},{6,2},{1... | collective-permute-start | bytes 608264 | tf_op jit(solution)/shard_map/ppermute | solution.py:33
  21.3 8.7 %copy-start.3 = (bf16[128,384]{1,0:T(8,128)(2,1)}, bf16[128,384]{1,0:T(8,128)(2,1)S(1)}, u32[]{:S(2)}) copy-start(bf16[128,384]{1,0:T(8,128)(2,1)S(1)} %collective-permute-done.6) | copy-start | bytes 294916
  22.3 17.1 %collective-permute-start.15 = (bf16[88,640]{1,0:T(8,128)(2,1)S(1)}, bf16[88,640]{1,0:T(8,128)(2,1)S(1)}, u32[]{:S(2)}, u32[]{:S(2)}) collective-permute-start(bf16[88,640]{1,0:T(8,128)(2,1)S(1)} %convolution_convert_fusion.30), channel_id=1, source_target_pairs={{0,8},{8,0},{4,12},{12,4},{1,9},{9,1},{5,13},{13,5},{2,10},{10,2},... | collective-permute-start | bytes 337928 | tf_op jit(solution)/shard_map/ppermute | solution.py:33
  26.0 7.9 %collective-permute-start.13 = (bf16[128,896]{1,0:T(8,128)(2,1)S(1)}, bf16[128,896]{1,0:T(8,128)(2,1)S(1)}, u32[]{:S(2)}, u32[]{:S(2)}) collective-permute-start(bf16[128,896]{1,0:T(8,128)(2,1)S(1)} %convolution_convert_fusion.23), channel_id=1, source_target_pairs={{0,2},{2,0},{1,3},{3,1},{4,6},{6,4},{5,7},{7,5},{8,10},{10,8},{9,1... | collective-permute-start | bytes 688136 | tf_op jit(solution)/shard_map/ppermute | solution.py:33
  27.3 8.9 %collective-permute-start.16 = (bf16[88,1152]{1,0:T(8,128)(2,1)S(1)}, bf16[88,1152]{1,0:T(8,128)(2,1)S(1)}, u32[]{:S(2)}, u32[]{:S(2)}) collective-permute-start(bf16[88,1152]{1,0:T(8,128)(2,1)S(1)} %convolution_convert_fusion.17), channel_id=1, source_target_pairs={{0,4},{4,0},{8,12},{12,8},{1,5},{5,1},{9,13},{13,9},{2,6},{6,2},{1... | collective-permute-start | bytes 608264 | tf_op jit(solution)/shard_map/ppermute | solution.py:33
  29.8 14.6 %collective-permute-start.12 = (bf16[88,1152]{1,0:T(8,128)(2,1)S(1)}, bf16[88,1152]{1,0:T(8,128)(2,1)S(1)}, u32[]{:S(2)}, u32[]{:S(2)}) collective-permute-start(bf16[88,1152]{1,0:T(8,128)(2,1)S(1)} %convolution_convert_fusion.16), channel_id=1, source_target_pairs={{0,8},{8,0},{4,12},{12,4},{1,9},{9,1},{5,13},{13,5},{2,10},{10,2},... | collective-permute-start | bytes 608264 | tf_op jit(solution)/shard_map/ppermute | solution.py:33
  30.0 3.0 %slice-start = ((bf16[128,384]{1,0:T(8,128)(2,1)}), bf16[128,256]{1,0:T(8,128)(2,1)S(1)}, s32[]{:S(2)}) async-start(bf16[128,384]{1,0:T(8,128)(2,1)} %copy-done.3), calls=%async_computation | async-start | bytes 131072 | tf_op jit(solution)/shard_map/slice | solution.py:295
  30.0 3.0 %copy-start.6 = (bf16[1,128,128]{2,1,0:T(8,128)(2,1)S(1)}, bf16[1,128,128]{2,1,0:T(8,128)(2,1)}, u32[]{:S(2)}) copy-start(bf16[1,128,128]{2,1,0:T(8,128)(2,1)} %param.11) | copy-start | bytes 98308
  31.0 14.7 %collective-permute-start.11 = (bf16[8,64]{1,0:T(8,128)(2,1)S(1)}, bf16[8,64]{1,0:T(8,128)(2,1)S(1)}, u32[]{:S(2)}, u32[]{:S(2)}) collective-permute-start(bf16[8,64]{1,0:T(8,128)(2,1)S(1)} %slice_maximum_fusion), channel_id=1, source_target_pairs={{0,2},{2,0},{1,3},{3,1},{4,6},{6,4},{5,7},{7,5},{8,10},{10,8},{9,1... | collective-permute-start | bytes 3080 | tf_op jit(solution)/shard_map/ppermute | solution.py:33
  34.2 7.0 %collective-permute-start.14 = (bf16[88,896]{1,0:T(8,128)(2,1)S(1)}, bf16[88,896]{1,0:T(8,128)(2,1)S(1)}, u32[]{:S(2)}, u32[]{:S(2)}) collective-permute-start(bf16[88,896]{1,0:T(8,128)(2,1)S(1)} %convolution_convert_fusion.29), channel_id=1, source_target_pairs={{0,4},{4,0},{8,12},{12,8},{1,5},{5,1},{9,13},{13,9},{2,6},{6,2},{1... | collective-permute-start | bytes 473096 | tf_op jit(solution)/shard_map/ppermute | solution.py:33
  37.4 3.1 %copy-start.8 = (bf16[128,1152]{1,0:T(8,128)(2,1)S(1)}, bf16[128,1152]{1,0:T(8,128)(2,1)}, u32[]{:S(2)}) copy-start(bf16[128,1152]{1,0:T(8,128)(2,1)} %convolution_convert_fusion.10) | copy-start | bytes 884740
  37.4 14.8 %collective-permute-start.17 = (bf16[88,1152]{1,0:T(8,128)(2,1)S(1)}, bf16[88,1152]{1,0:T(8,128)(2,1)S(1)}, u32[]{:S(2)}, u32[]{:S(2)}) collective-permute-start(bf16[88,1152]{1,0:T(8,128)(2,1)S(1)} %convolution_convert_fusion.15), channel_id=1, source_target_pairs={{0,8},{8,0},{4,12},{12,4},{1,9},{9,1},{5,13},{13,5},{2,10},{10,2},... | collective-permute-start | bytes 608264 | tf_op jit(solution)/shard_map/ppermute | solution.py:33
  40.5 0.9 %copy-start.7 = (bf16[128,896]{1,0:T(8,128)(2,1)S(1)}, bf16[128,896]{1,0:T(8,128)(2,1)}, u32[]{:S(2)}) copy-start(bf16[128,896]{1,0:T(8,128)(2,1)} %convolution_convert_fusion.22) | copy-start | bytes 688132
  40.8 3.6 %copy-start.9 = (bf16[128,1152]{1,0:T(8,128)(2,1)S(1)}, bf16[128,1152]{1,0:T(8,128)(2,1)}, u32[]{:S(2)}) copy-start(bf16[128,1152]{1,0:T(8,128)(2,1)} %convolution_convert_fusion.11) | copy-start | bytes 884740
  41.7 12.9 %collective-permute-start.18 = (bf16[88,896]{1,0:T(8,128)(2,1)S(1)}, bf16[88,896]{1,0:T(8,128)(2,1)S(1)}, u32[]{:S(2)}, u32[]{:S(2)}) collective-permute-start(bf16[88,896]{1,0:T(8,128)(2,1)S(1)} %convolution_convert_fusion.28), channel_id=1, source_target_pairs={{0,8},{8,0},{4,12},{12,4},{1,9},{9,1},{5,13},{13,5},{2,10},{10,2},... | collective-permute-start | bytes 473096 | tf_op jit(solution)/shard_map/ppermute | solution.py:33

commit v17 on v16

--- a/solution.py
+++ b/solution.py
@@ -5,14 +5,15 @@
 from jax.experimental.pallas import tpu as pltpu
 from jax.sharding import PartitionSpec as P
 
-SHARES = (2, 5, 9, 9, 7)
+SHARES = (2, 5, 7, 9, 9)
 FULL_PIECES = (2, 1)
 EARLY_PIECES = 2
 COUNT_PIECE = 2
 COUNT_READ = 2
 LOOK = (3, -1)
+MAKE = (0, -1)
 ORDER = (
-    (0, 0), (0, 1), (0, 2), (1, 0), (1, 1), (0, 3), (2, 0), (1, 2), LOOK, (2, 1), (0, 4), (1, 3),
+    (0, 0), (0, 1), (0, 2), (1, 0), (1, 1), MAKE, (2, 0), (0, 3), (1, 2), LOOK, (2, 1), (0, 4), (1, 3),
     (2, 2), (3, 0), (1, 4), (2, 3), (3, 1), (2, 4), (3, 2), (3, 3), (3, 4),
 )
 KERNEL_VMEM = 16 * 1024 * 1024
@@ -263,7 +264,7 @@
     unit = traces.shape[0] // sum(SHARES)
     pieces = len(SHARES)
     starts = [unit * sum(SHARES[:i]) for i in range(pieces + 1)]
-    coeffs = early(sampling, traces, starts[: EARLY_PIECES + 1])
+    coeffs = list(early(sampling, traces, starts[: EARLY_PIECES + 1]))
     full, small, extra = tables(after(skeleton, coeffs[0]), compress, wide, room)
     sampling, evaluation = sampling[0], evaluation[0]
     most_here = lax.broadcasted_iota(jnp.int32, extra.shape[1:], 1) >= rank
@@ -274,17 +275,21 @@
     inputs, partners, theirs, done = {}, {}, {}, [None] * pieces
     previous, finished, known = None, None, None
     for level, piece in ORDER:
+        if (level, piece) == MAKE:
+            waiting = after(sampling, previous)
+            for late in range(len(coeffs), pieces):
+                coeffs.append(sampled(waiting, traces[starts[late] : starts[late + 1]]))
+            previous = coeffs[-1]
+            continue
         if (level, piece) == LOOK:
             known = after(after(partners[0], previous), partners[1])[:, starts[1] :]
             theirs[levels - 1] = known[:room, :rank]
             continue
         count = starts[piece + 1] - starts[piece]
         if level == 0:
-            if piece < EARLY_PIECES:
-                own = coeffs[piece]
-            else:
-                block = traces[starts[piece] : starts[piece + 1]]
-                own = sampled(after(sampling, previous), block)
+            if piece == len(coeffs):
+                coeffs.append(sampled(after(sampling, previous), traces[starts[piece] : starts[piece + 1]]))
+            own = coeffs[piece]
         else:
             arrived = after(partners[piece], previous)
             if level == levels:
@@ -308,7 +313,7 @@
                 most = jnp.maximum(most, after(counted, finished))
             continue
         if level == 0:
-            outgoing = own
+            outgoing = after(own, previous) if piece > EARLY_PIECES else own
         if piece == 0 and level >= wide:
             block = extra[level]
             if known is not None:

time: 55.9 us -> 57.5 us (1.029)
  matrix products: 14 us -> 17.6 us
  starting transfers between devices: 26.6 us -> 23.9 us
  waiting for transfers between devices: 10.6 us -> 11.3 us
    dot_general x5, matrix products: 5.65 us -> 9.56 us  [evaluated(): jnp.einsum('ct,cp->tp', coeffs, evaluation, preferred_element_type=jnp.fl...]
    ppermute x16, starting transfers between devices: 26.6 us -> 23.9 us  [from_partner(): return lax.ppermute(block, hop[0], route(*hop))]
    ppermute x16, waiting for transfers between devices: 10.6 us -> 11.3 us  [from_partner(): return lax.ppermute(block, hop[0], route(*hop))]
  transfers between devices with their start and end apart: 16 -> 16, of which waited for: 6 -> 7; matrix products, arithmetic and copies ran while one was open for 24% -> 29% of each run, Pallas kernels for 2% -> 2%
where the time goes in v17:
time: 57.5 us; the launch traced here: 57 us
  starting transfers between devices  23.9 us (42%)
  matrix products  17.6 us (31%)
  waiting for transfers between devices  11.3 us (20%)
  Pallas kernels  2.63 us (5%)
  between operations  0.94 us (2%)
  local copies, waits for them, and re-layouts  0.62 us (1%)
    ppermute x16, starting transfers between devices, from_partner(): return lax.ppermute(block, hop[0], route(*hop))  23.9 us
    ppermute x16, waiting for transfers between devices, from_partner(): return lax.ppermute(block, hop[0], route(*hop))  11.3 us
    dot_general x5, matrix products, evaluated(): jnp.einsum('ct,cp->tp', coeffs, evaluation, preferred_element_type=jnp.fl...  9.56 us
    dot_general x17, matrix products, times(): jnp.dot(matrix, value, preferred_element_type=jnp.float32)  6.51 us
    pallas_call x1, Pallas kernels, early(): pl.pallas_call(lambda *refs: early_kernel(starts, *refs), out_shape=[jax....  1.45 us
    pallas_call x1, Pallas kernels, tables(): pl.pallas_call(lambda *refs: tables_kernel(wide, room, *refs), out_shape=...  1.18 us
  transfers between devices with their start and end apart: 16, of which 7 were waited for; matrix products, arithmetic and copies ran while one was open for 29% of the time, Pallas kernels for 2%

profile of v17, /device:TPU:0, one launch (start us, length us, event | category | flops | bytes accessed | tf_op | source)
XLA Modules:
  0.0 57.0 jit_solution(5868397493602186995)
XLA Ops:
  0.0 1.4 %early.1 = (bf16[128,256]{1,0:T(8,128)(2,1)S(1)}, bf16[128,640]{1,0:T(8,128)(2,1)S(1)}) custom-call(bf16[1,128,128]{2,1,0:T(8,128)(2,1)} %refs_0_.1, bf16[4096,128]{1,0:T(8,128)(2,1)} %refs_1_.2), custom_call_target="tpu_custom_call" | custom-call | flops 29360128 | bytes 458752 | tf_op jit(solution)/shard_map/early/pallas_call | solution.py:70
  1.5 3.0 %collective-permute-start.3 = (bf16[128,256]{1,0:T(8,128)(2,1)S(1)}, bf16[128,256]{1,0:T(8,128)(2,1)S(1)}, u32[]{:S(2)}, u32[]{:S(2)}) collective-permute-start(bf16[128,256]{1,0:T(8,128)(2,1)S(1)} %get-tuple-element.64), channel_id=1, source_target_pairs={{0,2},{2,0},{1,3},{3,1},{4,6},{6,4},{5,7},{7,5},{8,10},{10,8},{9,1... | collective-permute-start | bytes 196616 | tf_op jit(solution)/shard_map/ppermute | solution.py:34
  4.8 2.0 %collective-permute-start.7 = (bf16[128,896]{1,0:T(8,128)(2,1)S(1)}, bf16[128,896]{1,0:T(8,128)(2,1)S(1)}, u32[]{:S(2)}, u32[]{:S(2)}) collective-permute-start(bf16[128,896]{1,0:T(8,128)(2,1)S(1)} %convolution_convert_fusion.23), channel_id=1, source_target_pairs={{0,2},{2,0},{1,3},{3,1},{4,6},{6,4},{5,7},{7,5},{8,10},{10,8},{9,1... | collective-permute-start | bytes 688136 | tf_op jit(solution)/shard_map/ppermute | solution.py:34
  6.8 1.2 %tables.1 = (bf16[3,128,256]{2,1,0:T(8,128)(2,1)S(1)}, bf16[3,128,256]{2,1,0:T(8,128)(2,1)S(1)}, bf16[3,128,128]{2,1,0:T(8,128)(2,1)S(1)}) custom-call(s32[3,1,64]{2,1,0:T(1,128)S(1)} %bitcast.111, bf16[1,3,64,128]{3,2,1,0:T(8,128)(2,1)S(1)} %copy-done.4), custom_call_target="tpu_custom_call" | custom-call | flops 50000000 | bytes 600000 | tf_op jit(solution)/shard_map/tables/pallas_call | solution.py:153
  8.3 1.6 %collective-permute-start.4 = (bf16[128,384]{1,0:T(8,128)(2,1)S(1)}, bf16[128,384]{1,0:T(8,128)(2,1)S(1)}, u32[]{:S(2)}, u32[]{:S(2)}) collective-permute-start(bf16[128,384]{1,0:T(8,128)(2,1)S(1)} %pad_maximum_fusion.12), channel_id=1, source_target_pairs={{0,4},{4,0},{8,12},{12,8},{1,5},{5,1},{9,13},{13,9},{2,6},{6,2},{1... | collective-permute-start | bytes 294920 | tf_op jit(solution)/shard_map/ppermute | solution.py:34
  9.9 1.7 %collective-permute-done.5 = bf16[128,640]{1,0:T(8,128)(2,1)S(1)} collective-permute-done((bf16[128,640]{1,0:T(8,128)(2,1)S(1)}, bf16[128,640]{1,0:T(8,128)(2,1)S(1)}, u32[]{:S(2)}, u32[]{:S(2)}) %collective-permute-start.5) | collective-permute-done | bytes 163872 | tf_op jit(solution)/shard_map/ppermute | solution.py:34
  11.8 1.6 %collective-permute-start.8 = (bf16[128,640]{1,0:T(8,128)(2,1)S(1)}, bf16[128,640]{1,0:T(8,128)(2,1)S(1)}, u32[]{:S(2)}, u32[]{:S(2)}) collective-permute-start(bf16[128,640]{1,0:T(8,128)(2,1)S(1)} %convolution_convert_fusion.26), channel_id=1, source_target_pairs={{0,4},{4,0},{8,12},{12,8},{1,5},{5,1},{9,13},{13,9},{2,6},{6,2},{1... | collective-permute-start | bytes 491528 | tf_op jit(solution)/shard_map/ppermute | solution.py:34
  13.9 0.3 convolution_convert_fusion.13
  14.3 2.7 %collective-permute-start.6 = (bf16[128,384]{1,0:T(8,128)(2,1)S(1)}, bf16[128,384]{1,0:T(8,128)(2,1)S(1)}, u32[]{:S(2)}, u32[]{:S(2)}) collective-permute-start(bf16[128,384]{1,0:T(8,128)(2,1)S(1)} %pad_maximum_fusion.13), channel_id=1, source_target_pairs={{0,8},{8,0},{4,12},{12,4},{1,9},{9,1},{5,13},{13,5},{2,10},{10,2},... | collective-permute-start | bytes 294920 | tf_op jit(solution)/shard_map/ppermute | solution.py:34
  17.0 1.4 %collective-permute-start.10 = (bf16[128,1152]{1,0:T(8,128)(2,1)S(1)}, bf16[128,1152]{1,0:T(8,128)(2,1)S(1)}, u32[]{:S(2)}, u32[]{:S(2)}) collective-permute-start(bf16[128,1152]{1,0:T(8,128)(2,1)S(1)} %convolution_convert_fusion.13), channel_id=1, source_target_pairs={{0,2},{2,0},{1,3},{3,1},{4,6},{6,4},{5,7},{7,5},{8,10},{10,8},{9,1... | collective-permute-start | bytes 884744 | tf_op jit(solution)/shard_map/ppermute | solution.py:34
  18.7 1.6 %collective-permute-start.9 = (bf16[88,896]{1,0:T(8,128)(2,1)S(1)}, bf16[88,896]{1,0:T(8,128)(2,1)S(1)}, u32[]{:S(2)}, u32[]{:S(2)}) collective-permute-start(bf16[88,896]{1,0:T(8,128)(2,1)S(1)} %convolution_convert_fusion.29), channel_id=1, source_target_pairs={{0,4},{4,0},{8,12},{12,8},{1,5},{5,1},{9,13},{13,9},{2,6},{6,2},{1... | collective-permute-start | bytes 473096 | tf_op jit(solution)/shard_map/ppermute | solution.py:34
  21.3 2.9 %collective-permute-start.15 = (bf16[88,640]{1,0:T(8,128)(2,1)S(1)}, bf16[88,640]{1,0:T(8,128)(2,1)}, u32[]{:S(2)}, u32[]{:S(2)}) collective-permute-start(bf16[88,640]{1,0:T(8,128)(2,1)S(1)} %convolution_convert_fusion.30), channel_id=1, source_target_pairs={{0,8},{8,0},{4,12},{12,4},{1,9},{9,1},{5,13},{13,5},{2,10},{10,2},... | collective-permute-start | bytes 337928 | tf_op jit(solution)/shard_map/ppermute | solution.py:34
  24.1 0.9 %convolution_convert_fusion.25 = bf16[128,640]{1,0:T(8,128)(2,1)} fusion(bf16[128,256]{1,0:T(8,128)(2,1)S(1)} %get-tuple-element.89, bf16[128,640]{1,0:T(8,128)(2,1)S(1)} %collective-permute-done.8, bf16[128,640]{1,0:T(8,128)(2,1)S(1)} %convolution_convert_fusion.26), kind=kOutput, calls=%fused_computation.60 | convolution fusion | flops 42680320 | bytes 557056 | tf_op jit(solution)/shard_map/dot_general | solution.py:220
  25.1 1.5 %collective-permute-start.13 = (bf16[128,1152]{1,0:T(8,128)(2,1)S(1)}, bf16[128,1152]{1,0:T(8,128)(2,1)S(1)}, u32[]{:S(2)}, u32[]{:S(2)}) collective-permute-start(bf16[128,1152]{1,0:T(8,128)(2,1)S(1)} %convolution_convert_fusion.14), channel_id=1, source_target_pairs={{0,2},{2,0},{1,3},{3,1},{4,6},{6,4},{5,7},{7,5},{8,10},{10,8},{9,1... | collective-permute-start | bytes 884744 | tf_op jit(solution)/shard_map/ppermute | solution.py:34
  27.0 2.0 %collective-permute-start.16 = (bf16[88,1152]{1,0:T(8,128)(2,1)S(1)}, bf16[88,1152]{1,0:T(8,128)(2,1)S(1)}, u32[]{:S(2)}, u32[]{:S(2)}) collective-permute-start(bf16[88,1152]{1,0:T(8,128)(2,1)S(1)} %convolution_convert_fusion.18), channel_id=1, source_target_pairs={{0,4},{4,0},{8,12},{12,8},{1,5},{5,1},{9,13},{13,9},{2,6},{6,2},{1... | collective-permute-start | bytes 608264 | tf_op jit(solution)/shard_map/ppermute | solution.py:34
  29.0 0.9 %convolution_convert_fusion.28 = bf16[88,896]{1,0:T(8,128)(2,1)} fusion(bf16[88,896]{1,0:T(8,128)(2,1)S(1)} %collective-permute-done.9, bf16[128,896]{1,0:T(8,128)(2,1)S(1)} %convolution_convert_fusion.22, bf16[44,256]{1,0:T(8,128)(2,1)S(1)} %convolution_convert_fusion.37, bf16[44,256]{1,0:T(8,128)(2,1)S(1)} %convolution_convert_fusion.38), kind=kOutput, calls=%fused_computation.63 | convolution fusion | flops 42144768 | bytes 589824 | tf_op jit(solution)/shard_map/dot_general | solution.py:220
  29.9 0.9 %convolution_convert_fusion.21 = bf16[128,896]{1,0:T(8,128)(2,1)} fusion(bf16[128,256]{1,0:T(8,128)(2,1)S(1)} %slice_bitcast_fusion.7, bf16[88,896]{1,0:T(8,128)(2,1)S(1)} %collective-permute-done.9, bf16[128,896]{1,0:T(8,128)(2,1)S(1)} %convolution_convert_fusion.22), kind=kOutput, calls=%fused_computation.47 | convolution fusion | flops 60440576 | bytes 681984 | tf_op jit(solution)/shard_map/dot_general | solution.py:220
  30.9 1.8 %constant_dynamic-update-slice_fusion.3 = bf16[4096,128]{1,0:T(8,128)(2,1)} fusion(bf16[1,128,128]{2,1,0:T(8,128)(2,1)} %param.11, bf16[128,256]{1,0:T(8,128)(2,1)S(1)} %slice-done, bf16[128,256]{1,0:T(8,128)(2,1)S(1)} %convolution_convert_fusion.33, bf16[3,128,256]{2,1,0:T(8,128)(2,1)S(1)} %get-tuple-element.67), kind=kOutput, calls=%fused_computation.164 | convolution fusion | flops 25493504 | bytes 294912 | tf_op jit(solution)/shard_map/ct,cp->tp/dot_general | solution.py:230
  33.1 1.2 %collective-permute-start.14 = (bf16[88,1152]{1,0:T(8,128)(2,1)S(1)}, bf16[88,1152]{1,0:T(8,128)(2,1)S(1)}, u32[]{:S(2)}, u32[]{:S(2)}) collective-permute-start(bf16[88,1152]{1,0:T(8,128)(2,1)S(1)} %convolution_convert_fusion.17), channel_id=1, source_target_pairs={{0,4},{4,0},{8,12},{12,8},{1,5},{5,1},{9,13},{13,9},{2,6},{6,2},{1... | collective-permute-start | bytes 608264 | tf_op jit(solution)/shard_map/ppermute | solution.py:34
  34.6 2.0 %collective-permute-done.16 = bf16[88,1152]{1,0:T(8,128)(2,1)S(1)} collective-permute-done((bf16[88,1152]{1,0:T(8,128)(2,1)S(1)}, bf16[88,1152]{1,0:T(8,128)(2,1)S(1)}, u32[]{:S(2)}, u32[]{:S(2)}) %collective-permute-start.16) | collective-permute-done | bytes 202784 | tf_op jit(solution)/shard_map/ppermute | solution.py:34
  36.8 1.0 %collective-permute-start.17 = (bf16[88,1152]{1,0:T(8,128)(2,1)S(1)}, bf16[88,1152]{1,0:T(8,128)(2,1)S(1)}, u32[]{:S(2)}, u32[]{:S(2)}) collective-permute-start(bf16[88,1152]{1,0:T(8,128)(2,1)S(1)} %convolution_convert_fusion.16), channel_id=1, source_target_pairs={{0,8},{8,0},{4,12},{12,4},{1,9},{9,1},{5,13},{13,5},{2,10},{10,2},... | collective-permute-start | bytes 608264 | tf_op jit(solution)/shard_map/ppermute | solution.py:34
  37.8 2.0 %constant_dynamic-update-slice_fusion.2 = bf16[4096,128]{1,0:T(8,128)(2,1)} fusion(bf16[4096,128]{1,0:T(8,128)(2,1)} %constant_dynamic-update-slice_fusion.3, bf16[1,128,128]{2,1,0:T(8,128)(2,1)} %param.11, bf16[88,640]{1,0:T(8,128)(2,1)} %collective-permute-done.15, bf16[128,640]{1,0:T(8,128)(2,1)S(1)} %copy-done.6, ...), kind=kOutput, calls=%fused_computation.163 | convolution fusion | flops 64225280 | bytes 538624 | tf_op jit(solution)/shard_map/ct,cp->tp/dot_general | solution.py:230
  39.8 1.0 %convolution_convert_fusion.10 = bf16[128,1152]{1,0:T(8,128)(2,1)} fusion(bf16[128,256]{1,0:T(8,128)(2,1)S(1)} %slice_bitcast_fusion.7, bf16[88,1152]{1,0:T(8,128)(2,1)S(1)} %collective-permute-done.16, bf16[128,1152]{1,0:T(8,128)(2,1)S(1)} %copy-done.8), kind=kOutput, calls=%fused_computation.36 | convolution fusion | flops 77709312 | bytes 858112 | tf_op jit(solution)/shard_map/dot_general | solution.py:220
  40.8 0.8 %collective-permute-done.14 = bf16[88,1152]{1,0:T(8,128)(2,1)S(1)} collective-permute-done((bf16[88,1152]{1,0:T(8,128)(2,1)S(1)}, bf16[88,1152]{1,0:T(8,128)(2,1)S(1)}, u32[]{:S(2)}, u32[]{:S(2)}) %collective-permute-start.14) | collective-permute-done | bytes 202784 | tf_op jit(solution)/shard_map/ppermute | solution.py:34
  41.8 1.3 %collective-permute-start.18 = (bf16[88,1152]{1,0:T(8,128)(2,1)S(1)}, bf16[88,1152]{1,0:T(8,128)(2,1)S(1)}, u32[]{:S(2)}, u32[]{:S(2)}) collective-permute-start(bf16[88,1152]{1,0:T(8,128)(2,1)S(1)} %convolution_convert_fusion.15), channel_id=1, source_target_pairs={{0,8},{8,0},{4,12},{12,4},{1,9},{9,1},{5,13},{13,5},{2,10},{10,2},... | collective-permute-start | bytes 608264 | tf_op jit(solution)/shard_map/ppermute | solution.py:34
  43.1 0.8 %collective-permute-done.12 = bf16[88,896]{1,0:T(8,128)(2,1)S(1)} collective-permute-done((bf16[88,896]{1,0:T(8,128)(2,1)}, bf16[88,896]{1,0:T(8,128)(2,1)S(1)}, u32[]{:S(2)}, u32[]{:S(2)}) %collective-permute-start.12) | collective-permute-done | bytes 157728 | tf_op jit(solution)/shard_map/ppermute | solution.py:34
  43.8 1.9 %constant_dynamic-update-slice_fusion.1 = bf16[4096,128]{1,0:T(8,128)(2,1)} fusion(bf16[4096,128]{1,0:T(8,128)(2,1)} %constant_dynamic-update-slice_fusion.2, bf16[1,128,128]{2,1,0:T(8,128)(2,1)} %param.11, bf16[88,896]{1,0:T(8,128)(2,1)S(1)} %collective-permute-done.12, bf16[128,896]{1,0:T(8,128)(2,1)S(1)} %copy-done.9, ...), kind=kOutput, calls=%fused_computation.162 | convolution fusion | flops 89915392 | bytes 714752 | tf_op jit(solution)/shard_map/ct,cp->tp/dot_general | solution.py:230
  45.7 0.5 slice.183
  47.2 5.3 %collective-permute-done.17 = bf16[88,1152]{1,0:T(8,128)(2,1)S(1)} collective-permute-done((bf16[88,1152]{1,0:T(8,128)(2,1)S(1)}, bf16[88,1152]{1,0:T(8,128)(2,1)S(1)}, u32[]{:S(2)}, u32[]{:S(2)}) %collective-permute-start.17) | collective-permute-done | bytes 202784 | tf_op jit(solution)/shard_map/ppermute | solution.py:34
  52.5 2.0 %constant_dynamic-update-slice_fusion = bf16[4096,128]{1,0:T(8,128)(2,1)} fusion(bf16[4096,128]{1,0:T(8,128)(2,1)} %constant_dynamic-update-slice_fusion.1, bf16[1,128,128]{2,1,0:T(8,128)(2,1)} %param.11, bf16[88,1152]{1,0:T(8,128)(2,1)S(1)} %collective-permute-done.17, bf16[128,1152]{1,0:T(8,128)(2,1)S(1)} %copy-done.10, ...), kind=kOutput, calls=%fused_computation.161 | convolution fusion | flops 115605504 | bytes 890880 | tf_op jit(solution)/shard_map/ct,cp->tp/dot_general | solution.py:230
  54.5 0.6 %collective-permute-done.18 = bf16[88,1152]{1,0:T(8,128)(2,1)S(1)} collective-permute-done((bf16[88,1152]{1,0:T(8,128)(2,1)S(1)}, bf16[88,1152]{1,0:T(8,128)(2,1)S(1)}, u32[]{:S(2)}, u32[]{:S(2)}) %collective-permute-start.18) | collective-permute-done | bytes 202784 | tf_op jit(solution)/shard_map/ppermute | solution.py:34
  55.1 2.0 %fusion.20 = bf16[4096,128]{1,0:T(8,128)(2,1)} fusion(bf16[4096,128]{1,0:T(8,128)(2,1)} %constant_dynamic-update-slice_fusion, bf16[88,1152]{1,0:T(8,128)(2,1)S(1)} %collective-permute-done.18, bf16[128,1152]{1,0:T(8,128)(2,1)S(1)} %convolution_convert_fusion.7, bf16[3,128,256]{2,1,0:T(8,128)(2,1)S(1)} %get-tuple-element.78, bf16[1,128,128]{2,1,0:T(8,128)(2,1)} %param.11), kind=kOutput, calls=%fused_computation.31 | convolution fusion | flops 115605504 | bytes 890880 | tf_op jit(solution)/shard_map/ct,cp->tp/dot_general | solution.py:230
  (68 shorter events, 4.5 us)
Async XLA Ops:
  0.0 4.6 %copy-start = (bf16[4096,128]{1,0:T(8,128)(2,1)S(1)}, bf16[4096,128]{1,0:T(8,128)(2,1)}, u32[]{:S(2)}) copy-start(bf16[4096,128]{1,0:T(8,128)(2,1)} %refs_1_.2) | copy-start | bytes 3145732
  0.0 4.6 %copy-start.2 = (bf16[1,128,128]{2,1,0:T(8,128)(2,1)S(1)}, bf16[1,128,128]{2,1,0:T(8,128)(2,1)}, u32[]{:S(2)}) copy-start(bf16[1,128,128]{2,1,0:T(8,128)(2,1)} %refs_0_.1) | copy-start | bytes 98308
  0.0 6.8 %copy-start.5 = (s32[1,3,64]{2,0,1:T(1,128)S(1)}, s32[1,3,64]{2,0,1:T(1,128)}, u32[]{:S(2)}) copy-start(s32[1,3,64]{2,0,1:T(1,128)} %param.9) | copy-start | bytes 2308
  0.0 6.8 %copy-start.4 = (bf16[1,3,64,128]{3,2,1,0:T(8,128)(2,1)S(1)}, bf16[1,3,64,128]{3,2,1,0:T(8,128)(2,1)}, u32[]{:S(2)}) copy-start(bf16[1,3,64,128]{3,2,1,0:T(8,128)(2,1)} %refs_1_.3) | copy-start | bytes 147460
  1.5 6.6 %collective-permute-start.3 = (bf16[128,256]{1,0:T(8,128)(2,1)S(1)}, bf16[128,256]{1,0:T(8,128)(2,1)S(1)}, u32[]{:S(2)}, u32[]{:S(2)}) collective-permute-start(bf16[128,256]{1,0:T(8,128)(2,1)S(1)} %get-tuple-element.64), channel_id=1, source_target_pairs={{0,2},{2,0},{1,3},{3,1},{4,6},{6,4},{5,7},{7,5},{8,10},{10,8},{9,1... | collective-permute-start | bytes 196616 | tf_op jit(solution)/shard_map/ppermute | solution.py:34
  4.5 7.1 %collective-permute-start.5 = (bf16[128,640]{1,0:T(8,128)(2,1)S(1)}, bf16[128,640]{1,0:T(8,128)(2,1)S(1)}, u32[]{:S(2)}, u32[]{:S(2)}) collective-permute-start(bf16[128,640]{1,0:T(8,128)(2,1)S(1)} %get-tuple-element.68), channel_id=1, source_target_pairs={{0,2},{2,0},{1,3},{3,1},{4,6},{6,4},{5,7},{7,5},{8,10},{10,8},{9,1... | collective-permute-start | bytes 491528 | tf_op jit(solution)/shard_map/ppermute | solution.py:34
  4.8 13.7 %collective-permute-start.7 = (bf16[128,896]{1,0:T(8,128)(2,1)S(1)}, bf16[128,896]{1,0:T(8,128)(2,1)S(1)}, u32[]{:S(2)}, u32[]{:S(2)}) collective-permute-start(bf16[128,896]{1,0:T(8,128)(2,1)S(1)} %convolution_convert_fusion.23), channel_id=1, source_target_pairs={{0,2},{2,0},{1,3},{3,1},{4,6},{6,4},{5,7},{7,5},{8,10},{10,8},{9,1... | collective-permute-start | bytes 688136 | tf_op jit(solution)/shard_map/ppermute | solution.py:34
  8.3 5.4 %collective-permute-start.4 = (bf16[128,384]{1,0:T(8,128)(2,1)S(1)}, bf16[128,384]{1,0:T(8,128)(2,1)S(1)}, u32[]{:S(2)}, u32[]{:S(2)}) collective-permute-start(bf16[128,384]{1,0:T(8,128)(2,1)S(1)} %pad_maximum_fusion.12), channel_id=1, source_target_pairs={{0,4},{4,0},{8,12},{12,8},{1,5},{5,1},{9,13},{13,9},{2,6},{6,2},{1... | collective-permute-start | bytes 294920 | tf_op jit(solution)/shard_map/ppermute | solution.py:34
  11.8 8.8 %collective-permute-start.8 = (bf16[128,640]{1,0:T(8,128)(2,1)S(1)}, bf16[128,640]{1,0:T(8,128)(2,1)S(1)}, u32[]{:S(2)}, u32[]{:S(2)}) collective-permute-start(bf16[128,640]{1,0:T(8,128)(2,1)S(1)} %convolution_convert_fusion.26), channel_id=1, source_target_pairs={{0,4},{4,0},{8,12},{12,8},{1,5},{5,1},{9,13},{13,9},{2,6},{6,2},{1... | collective-permute-start | bytes 491528 | tf_op jit(solution)/shard_map/ppermute | solution.py:34
  14.3 6.3 %collective-permute-start.6 = (bf16[128,384]{1,0:T(8,128)(2,1)S(1)}, bf16[128,384]{1,0:T(8,128)(2,1)S(1)}, u32[]{:S(2)}, u32[]{:S(2)}) collective-permute-start(bf16[128,384]{1,0:T(8,128)(2,1)S(1)} %pad_maximum_fusion.13), channel_id=1, source_target_pairs={{0,8},{8,0},{4,12},{12,4},{1,9},{9,1},{5,13},{13,5},{2,10},{10,2},... | collective-permute-start | bytes 294920 | tf_op jit(solution)/shard_map/ppermute | solution.py:34
  17.0 9.8 %collective-permute-start.10 = (bf16[128,1152]{1,0:T(8,128)(2,1)S(1)}, bf16[128,1152]{1,0:T(8,128)(2,1)S(1)}, u32[]{:S(2)}, u32[]{:S(2)}) collective-permute-start(bf16[128,1152]{1,0:T(8,128)(2,1)S(1)} %convolution_convert_fusion.13), channel_id=1, source_target_pairs={{0,2},{2,0},{1,3},{3,1},{4,6},{6,4},{5,7},{7,5},{8,10},{10,8},{9,1... | collective-permute-start | bytes 884744 | tf_op jit(solution)/shard_map/ppermute | solution.py:34
  18.7 10.3 %collective-permute-start.9 = (bf16[88,896]{1,0:T(8,128)(2,1)S(1)}, bf16[88,896]{1,0:T(8,128)(2,1)S(1)}, u32[]{:S(2)}, u32[]{:S(2)}) collective-permute-start(bf16[88,896]{1,0:T(8,128)(2,1)S(1)} %convolution_convert_fusion.29), channel_id=1, source_target_pairs={{0,4},{4,0},{8,12},{12,8},{1,5},{5,1},{9,13},{13,9},{2,6},{6,2},{1... | collective-permute-start | bytes 473096 | tf_op jit(solution)/shard_map/ppermute | solution.py:34
  20.6 9.3 %copy-start.3 = (bf16[128,384]{1,0:T(8,128)(2,1)}, bf16[128,384]{1,0:T(8,128)(2,1)S(1)}, u32[]{:S(2)}) copy-start(bf16[128,384]{1,0:T(8,128)(2,1)S(1)} %collective-permute-done.6) | copy-start | bytes 294916
  21.3 16.5 %collective-permute-start.15 = (bf16[88,640]{1,0:T(8,128)(2,1)S(1)}, bf16[88,640]{1,0:T(8,128)(2,1)}, u32[]{:S(2)}, u32[]{:S(2)}) collective-permute-start(bf16[88,640]{1,0:T(8,128)(2,1)S(1)} %convolution_convert_fusion.30), channel_id=1, source_target_pairs={{0,8},{8,0},{4,12},{12,4},{1,9},{9,1},{5,13},{13,5},{2,10},{10,2},... | collective-permute-start | bytes 337928 | tf_op jit(solution)/shard_map/ppermute | solution.py:34
  25.1 7.7 %collective-permute-start.13 = (bf16[128,1152]{1,0:T(8,128)(2,1)S(1)}, bf16[128,1152]{1,0:T(8,128)(2,1)S(1)}, u32[]{:S(2)}, u32[]{:S(2)}) collective-permute-start(bf16[128,1152]{1,0:T(8,128)(2,1)S(1)} %convolution_convert_fusion.14), channel_id=1, source_target_pairs={{0,2},{2,0},{1,3},{3,1},{4,6},{6,4},{5,7},{7,5},{8,10},{10,8},{9,1... | collective-permute-start | bytes 884744 | tf_op jit(solution)/shard_map/ppermute | solution.py:34
  27.0 9.5 %collective-permute-start.16 = (bf16[88,1152]{1,0:T(8,128)(2,1)S(1)}, bf16[88,1152]{1,0:T(8,128)(2,1)S(1)}, u32[]{:S(2)}, u32[]{:S(2)}) collective-permute-start(bf16[88,1152]{1,0:T(8,128)(2,1)S(1)} %convolution_convert_fusion.18), channel_id=1, source_target_pairs={{0,4},{4,0},{8,12},{12,8},{1,5},{5,1},{9,13},{13,9},{2,6},{6,2},{1... | collective-permute-start | bytes 608264 | tf_op jit(solution)/shard_map/ppermute | solution.py:34
  29.9 13.9 %collective-permute-start.12 = (bf16[88,896]{1,0:T(8,128)(2,1)}, bf16[88,896]{1,0:T(8,128)(2,1)S(1)}, u32[]{:S(2)}, u32[]{:S(2)}) collective-permute-start(bf16[88,896]{1,0:T(8,128)(2,1)} %convolution_convert_fusion.28), channel_id=1, source_target_pairs={{0,8},{8,0},{4,12},{12,4},{1,9},{9,1},{5,13},{13,5},{2,10},{10,2},... | collective-permute-start | bytes 473096 | tf_op jit(solution)/shard_map/ppermute | solution.py:34
  29.9 0.9 %slice-start = ((bf16[128,384]{1,0:T(8,128)(2,1)}), bf16[128,256]{1,0:T(8,128)(2,1)S(1)}, s32[]{:S(2)}) async-start(bf16[128,384]{1,0:T(8,128)(2,1)} %copy-done.3), calls=%async_computation | async-start | bytes 131072 | tf_op jit(solution)/shard_map/slice | solution.py:300
  30.8 14.9 %collective-permute-start.11 = (bf16[8,64]{1,0:T(8,128)(2,1)S(1)}, bf16[8,64]{1,0:T(8,128)(2,1)S(1)}, u32[]{:S(2)}, u32[]{:S(2)}) collective-permute-start(bf16[8,64]{1,0:T(8,128)(2,1)S(1)} %slice_maximum_fusion), channel_id=1, source_target_pairs={{0,2},{2,0},{1,3},{3,1},{4,6},{6,4},{5,7},{7,5},{8,10},{10,8},{9,1... | collective-permute-start | bytes 3080 | tf_op jit(solution)/shard_map/ppermute | solution.py:34
  32.9 3.7 %copy-start.7 = (bf16[128,1152]{1,0:T(8,128)(2,1)}, bf16[128,1152]{1,0:T(8,128)(2,1)S(1)}, u32[]{:S(2)}) copy-start(bf16[128,1152]{1,0:T(8,128)(2,1)S(1)} %convolution_convert_fusion.11) | copy-start | bytes 884740
  33.1 8.4 %collective-permute-start.14 = (bf16[88,1152]{1,0:T(8,128)(2,1)S(1)}, bf16[88,1152]{1,0:T(8,128)(2,1)S(1)}, u32[]{:S(2)}, u32[]{:S(2)}) collective-permute-start(bf16[88,1152]{1,0:T(8,128)(2,1)S(1)} %convolution_convert_fusion.17), channel_id=1, source_target_pairs={{0,4},{4,0},{8,12},{12,8},{1,5},{5,1},{9,13},{13,9},{2,6},{6,2},{1... | collective-permute-start | bytes 608264 | tf_op jit(solution)/shard_map/ppermute | solution.py:34
  34.6 3.2 %copy-start.6 = (bf16[128,640]{1,0:T(8,128)(2,1)S(1)}, bf16[128,640]{1,0:T(8,128)(2,1)}, u32[]{:S(2)}) copy-start(bf16[128,640]{1,0:T(8,128)(2,1)} %convolution_convert_fusion.25) | copy-start | bytes 491524
  36.8 3.0 %copy-start.8 = (bf16[128,1152]{1,0:T(8,128)(2,1)S(1)}, bf16[128,1152]{1,0:T(8,128)(2,1)}, u32[]{:S(2)}) copy-start(bf16[128,1152]{1,0:T(8,128)(2,1)} %copy-done.7) | copy-start | bytes 884740
  36.8 15.7 %collective-permute-start.17 = (bf16[88,1152]{1,0:T(8,128)(2,1)S(1)}, bf16[88,1152]{1,0:T(8,128)(2,1)S(1)}, u32[]{:S(2)}, u32[]{:S(2)}) collective-permute-start(bf16[88,1152]{1,0:T(8,128)(2,1)S(1)} %convolution_convert_fusion.16), channel_id=1, source_target_pairs={{0,8},{8,0},{4,12},{12,4},{1,9},{9,1},{5,13},{13,5},{2,10},{10,2},... | collective-permute-start | bytes 608264 | tf_op jit(solution)/shard_map/ppermute | solution.py:34
  40.8 3.1 %copy-start.9 = (bf16[128,896]{1,0:T(8,128)(2,1)S(1)}, bf16[128,896]{1,0:T(8,128)(2,1)}, u32[]{:S(2)}) copy-start(bf16[128,896]{1,0:T(8,128)(2,1)} %convolution_convert_fusion.21) | copy-start | bytes 688132
  41.8 13.3 %collective-permute-start.18 = (bf16[88,1152]{1,0:T(8,128)(2,1)S(1)}, bf16[88,1152]{1,0:T(8,128)(2,1)S(1)}, u32[]{:S(2)}, u32[]{:S(2)}) collective-permute-start(bf16[88,1152]{1,0:T(8,128)(2,1)S(1)} %convolution_convert_fusion.15), channel_id=1, source_target_pairs={{0,8},{8,0},{4,12},{12,4},{1,9},{9,1},{5,13},{13,5},{2,10},{10,2},... | collective-permute-start | bytes 608264 | tf_op jit(solution)/shard_map/ppermute | solution.py:34
  46.9 5.6 %copy-start.10 = (bf16[128,1152]{1,0:T(8,128)(2,1)S(1)}, bf16[128,1152]{1,0:T(8,128)(2,1)}, u32[]{:S(2)}) copy-start(bf16[128,1152]{1,0:T(8,128)(2,1)} %convolution_convert_fusion.10) | copy-start | bytes 884740

commit v18 on v16

--- a/solution.py
+++ b/solution.py
@@ -16,7 +16,7 @@
     (2, 2), (3, 0), (1, 4), (2, 3), (3, 1), (2, 4), (3, 2), (3, 3), (3, 4),
 )
 KERNEL_VMEM = 16 * 1024 * 1024
-ROOM_SIXTEENTHS = 11
+ROOM_SIXTEENTHS = (11, 10)
 
 
 def route(axis, apart):
@@ -87,7 +87,7 @@
 
 
 def tables_kernel(
-    wide, room, skeleton_hbm, compress_hbm, full_ref, small_ref, extra_ref,
+    wide, rooms, skeleton_hbm, compress_hbm, full_ref, small_ref, extra_ref,
     skeleton_ref, compress_ref, arrived,
 ):
     loads = [
@@ -112,10 +112,8 @@
     imag_column = column % width >= rank
     coefficient = column % rank + jnp.where(partner_column, rank, 0)
     slot_column = column - width
-    slot_imag = slot_column >= room
-    slot_of_column = jnp.where(slot_imag, slot_column - room, slot_column)
     row = lax.broadcasted_iota(i32, (width, width), 0)
-    most = jnp.zeros((1, 1), f32)
+    most = jnp.full((1, 1), -float(rank), f32)
     for level in range(levels):
         entry = jnp.broadcast_to(skeleton_ref[level].astype(f32), (8, rank)).astype(jnp.bfloat16)
         entry = across(entry, twice)[:1]
@@ -133,28 +131,33 @@
 
         match = entry == coefficient
         full_ref[level, :rank], full_ref[level, rank:] = halves(match, imag_column)
+        if level < wide:
+            continue
+        high = level - wide
+        room = rooms[high]
+        slot_imag = slot_column >= room
+        slot_of_column = jnp.where(slot_imag, slot_column - room, slot_column)
         compacted = (slot == slot_of_column) & from_partner_entry
         match = (match & jnp.logical_not(partner_column)) | (compacted & partner_column)
         imag = (imag_column & jnp.logical_not(partner_column)) | (slot_imag & partner_column)
-        small_ref[level, :rank], small_ref[level, rank:] = halves(match, imag)
+        small_ref[high, :rank], small_ref[high, rank:] = halves(match, imag)
         once = (k < rank) & from_partner_entry
         places = across(one_hot(once & (slot == row)), one_hot(once & (entry - rank == row)))
-        extra_ref[level] = places.astype(jnp.bfloat16)
-        if level >= wide:
-            most = jnp.maximum(most, jnp.sum(picked, axis=1, keepdims=True) * 0.5)
-    for level in range(wide, levels):
-        extra_ref[level] = jnp.where(k < rank, extra_ref[level].astype(f32), most).astype(jnp.bfloat16)
-
-
-def tables(skeleton, compress, wide, room):
+        extra_ref[high] = places.astype(jnp.bfloat16)
+        most = jnp.maximum(most, jnp.sum(picked, axis=1, keepdims=True) * 0.5 - room)
+    for high in range(levels - wide):
+        extra_ref[high] = jnp.where(k < rank, extra_ref[high].astype(f32), most).astype(jnp.bfloat16)
+
+
+def tables(skeleton, compress, wide, rooms):
     levels, rank = skeleton.shape[1:]
     shape = (levels, 2 * rank, 4 * rank)
     return pl.pallas_call(
-        lambda *refs: tables_kernel(wide, room, *refs),
+        lambda *refs: tables_kernel(wide, rooms, *refs),
         out_shape=[
             jax.ShapeDtypeStruct(shape, jnp.bfloat16),
-            jax.ShapeDtypeStruct(shape, jnp.bfloat16),
-            jax.ShapeDtypeStruct((levels, 2 * rank, 2 * rank), jnp.bfloat16),
+            jax.ShapeDtypeStruct((levels - wide,) + shape[1:], jnp.bfloat16),
+            jax.ShapeDtypeStruct((levels - wide, 2 * rank, 2 * rank), jnp.bfloat16),
         ],
         in_specs=[pl.BlockSpec(memory_space=pltpu.HBM)] * 2,
         out_specs=[pl.BlockSpec(memory_space=pltpu.VMEM)] * 3,
@@ -255,16 +258,16 @@
 def local(traces, sampling, skeleton, compress, evaluation):
     hops = all_hops()
     levels = len(hops)
-    if levels != max(level for level, _ in ORDER):
+    if (lax.axis_size("sub"), lax.axis_size("bfly")) != (2, 4):
         return full_width(traces, sampling[0], skeleton[0], compress[0], evaluation[0])
     wide = lax.axis_size("sub").bit_length() - 1
     rank = skeleton.shape[-1]
-    room = rank * ROOM_SIXTEENTHS // 16
+    rooms = [rank * share // 16 for share in ROOM_SIXTEENTHS]
     unit = traces.shape[0] // sum(SHARES)
     pieces = len(SHARES)
     starts = [unit * sum(SHARES[:i]) for i in range(pieces + 1)]
     coeffs = early(sampling, traces, starts[: EARLY_PIECES + 1])
-    full, small, extra = tables(after(skeleton, coeffs[0]), compress, wide, room)
+    full, small, extra = tables(after(skeleton, coeffs[0]), compress, wide, rooms)
     sampling, evaluation = sampling[0], evaluation[0]
     most_here = lax.broadcasted_iota(jnp.int32, extra.shape[1:], 1) >= rank
 
@@ -276,7 +279,7 @@
     for level, piece in ORDER:
         if (level, piece) == LOOK:
             known = after(after(partners[0], previous), partners[1])[:, starts[1] :]
-            theirs[levels - 1] = known[:room, :rank]
+            theirs[levels - 1] = known[: rooms[levels - 1 - wide], :rank]
             continue
         count = starts[piece + 1] - starts[piece]
         if level == 0:
@@ -291,12 +294,12 @@
                 arrived = after(arrived, finished)
             elif piece == 0 and level - 1 >= wide:
                 known = arrived[:, count:]
-                theirs[level - 1] = known[:room, :rank]
+                theirs[level - 1] = known[: rooms[level - 1 - wide], :rank]
             value = jnp.concatenate([inputs[piece], arrived[:, :count]], 0)
             matrix = full[level - 1]
             if compact(level - 1, piece):
                 value = jnp.pad(value, ((0, full.shape[2] - value.shape[0]), (0, 0)))
-                matrix = small[level - 1]
+                matrix = small[level - 1 - wide]
             if level < levels and compact(level, piece):
                 outgoing = times(compact_rows(matrix, theirs[level]), value)
                 own = times(after(matrix, outgoing), value)
@@ -310,7 +313,7 @@
         if level == 0:
             outgoing = own
         if piece == 0 and level >= wide:
-            block = extra[level]
+            block = extra[level - wide]
             if known is not None:
                 block = jnp.where(most_here, jnp.maximum(block, known), block)
             outgoing = jnp.concatenate([outgoing, block], 1)
@@ -318,13 +321,13 @@
         partners[piece] = from_partner(outgoing, hops[level])
         previous = outgoing
         if (level, piece) == (levels - 1, COUNT_PIECE):
-            most = after(jnp.maximum(extra[levels - 1], known)[:8, rank:], outgoing)
+            most = after(jnp.maximum(extra[levels - 1 - wide], known)[:8, rank:], outgoing)
             for hop in hops[: wide - 1]:
                 most = jnp.maximum(most, from_partner(most, hop))
             counted = from_partner(most, hops[wide - 1])
     quick = jnp.concatenate(done, 0)
     return lax.cond(
-        most[0, 0] > room,
+        most[0, 0] > 0,
         lambda: full_width(traces, sampling, skeleton[0], compress[0], evaluation),
         lambda: quick,
     )

time: 55.9 us -> 53.9 us (0.964)
  waiting for transfers between devices: 10.6 us -> 8.87 us
  starting transfers between devices: 26.6 us -> 27.5 us
  matrix products: 14 us -> 13.3 us
    ppermute x16, waiting for transfers between devices: 10.6 us -> 8.87 us  [from_partner(): return lax.ppermute(block, hop[0], route(*hop))]
    ppermute x16, starting transfers between devices: 26.6 us -> 27.5 us  [from_partner(): return lax.ppermute(block, hop[0], route(*hop))]
    dot_general x17, matrix products: 6.84 us -> 6.12 us  [times(): jnp.dot(matrix, value, preferred_element_type=jnp.float32)]
where the time goes in v18:
time: 53.9 us; the launch traced here: 53.7 us
  starting transfers between devices  27.5 us (51%)
  matrix products  13.3 us (25%)
  waiting for transfers between devices  8.87 us (16%)
  Pallas kernels  2.51 us (5%)
  between operations  0.87 us (2%)
  local copies, waits for them, and re-layouts  0.58 us (1%)
    ppermute x16, starting transfers between devices, from_partner(): return lax.ppermute(block, hop[0], route(*hop))  27.5 us
    ppermute x16, waiting for transfers between devices, from_partner(): return lax.ppermute(block, hop[0], route(*hop))  8.87 us
    dot_general x17, matrix products, times(): jnp.dot(matrix, value, preferred_element_type=jnp.float32)  6.12 us
    dot_general x5, matrix products, evaluated(): jnp.einsum('ct,cp->tp', coeffs, evaluation, preferred_element_type=jnp.fl...  5.63 us
    pallas_call x1, Pallas kernels, early(): pl.pallas_call(lambda *refs: early_kernel(starts, *refs), out_shape=[jax....  1.45 us
  transfers between devices with their start and end apart: 16, of which 6 were waited for; matrix products, arithmetic and copies ran while one was open for 24% of the time, Pallas kernels for 2%

profile of v18, /device:TPU:0, one launch (start us, length us, event | category | flops | bytes accessed | tf_op | source)
XLA Modules:
  0.0 53.7 jit_solution(8173524697288585006)
XLA Ops:
  0.0 1.4 %early.1 = (bf16[128,256]{1,0:T(8,128)(2,1)S(1)}, bf16[128,640]{1,0:T(8,128)(2,1)S(1)}) custom-call(bf16[1,128,128]{2,1,0:T(8,128)(2,1)} %refs_0_.1, bf16[4096,128]{1,0:T(8,128)(2,1)} %refs_1_.2), custom_call_target="tpu_custom_call" | custom-call | flops 29360128 | bytes 458752 | tf_op jit(solution)/shard_map/early/pallas_call | solution.py:69
  1.5 3.0 %collective-permute-start.3 = (bf16[128,256]{1,0:T(8,128)(2,1)S(1)}, bf16[128,256]{1,0:T(8,128)(2,1)S(1)}, u32[]{:S(2)}, u32[]{:S(2)}) collective-permute-start(bf16[128,256]{1,0:T(8,128)(2,1)S(1)} %get-tuple-element.63), channel_id=1, source_target_pairs={{0,2},{2,0},{1,3},{3,1},{4,6},{6,4},{5,7},{7,5},{8,10},{10,8},{9,1... | collective-permute-start | bytes 196616 | tf_op jit(solution)/shard_map/ppermute | solution.py:33
  4.6 0.3 convolution_convert_fusion.14
  4.8 2.0 %collective-permute-start.7 = (bf16[128,1152]{1,0:T(8,128)(2,1)S(1)}, bf16[128,1152]{1,0:T(8,128)(2,1)S(1)}, u32[]{:S(2)}, u32[]{:S(2)}) collective-permute-start(bf16[128,1152]{1,0:T(8,128)(2,1)S(1)} %convolution_convert_fusion.14), channel_id=1, source_target_pairs={{0,2},{2,0},{1,3},{3,1},{4,6},{6,4},{5,7},{7,5},{8,10},{10,8},{9,1... | collective-permute-start | bytes 884744 | tf_op jit(solution)/shard_map/ppermute | solution.py:33
  6.8 1.1 %tables.1 = (bf16[3,128,256]{2,1,0:T(8,128)(2,1)S(1)}, bf16[2,128,256]{2,1,0:T(8,128)(2,1)S(1)}, bf16[2,128,128]{2,1,0:T(8,128)(2,1)S(1)}) custom-call(s32[3,1,64]{2,1,0:T(1,128)S(1)} %bitcast.111, bf16[1,3,64,128]{3,2,1,0:T(8,128)(2,1)S(1)} %copy-done.4), custom_call_target="tpu_custom_call" | custom-call | flops 50000000 | bytes 600000 | tf_op jit(solution)/shard_map/tables/pallas_call | solution.py:155
  8.2 1.6 %collective-permute-start.4 = (bf16[128,384]{1,0:T(8,128)(2,1)S(1)}, bf16[128,384]{1,0:T(8,128)(2,1)S(1)}, u32[]{:S(2)}, u32[]{:S(2)}) collective-permute-start(bf16[128,384]{1,0:T(8,128)(2,1)S(1)} %pad_maximum_fusion.12), channel_id=1, source_target_pairs={{0,4},{4,0},{8,12},{12,8},{1,5},{5,1},{9,13},{13,9},{2,6},{6,2},{1... | collective-permute-start | bytes 294920 | tf_op jit(solution)/shard_map/ppermute | solution.py:33
  9.8 1.8 %collective-permute-done.5 = bf16[128,640]{1,0:T(8,128)(2,1)S(1)} collective-permute-done((bf16[128,640]{1,0:T(8,128)(2,1)S(1)}, bf16[128,640]{1,0:T(8,128)(2,1)S(1)}, u32[]{:S(2)}, u32[]{:S(2)}) %collective-permute-start.5) | collective-permute-done | bytes 163872 | tf_op jit(solution)/shard_map/ppermute | solution.py:33
  11.8 1.6 %collective-permute-start.8 = (bf16[128,640]{1,0:T(8,128)(2,1)S(1)}, bf16[128,640]{1,0:T(8,128)(2,1)S(1)}, u32[]{:S(2)}, u32[]{:S(2)}) collective-permute-start(bf16[128,640]{1,0:T(8,128)(2,1)S(1)} %convolution_convert_fusion.26), channel_id=1, source_target_pairs={{0,4},{4,0},{8,12},{12,8},{1,5},{5,1},{9,13},{13,9},{2,6},{6,2},{1... | collective-permute-start | bytes 491528 | tf_op jit(solution)/shard_map/ppermute | solution.py:33
  13.5 0.3 convolution_convert_fusion.13
  13.9 1.4 %collective-permute-start.10 = (bf16[128,1152]{1,0:T(8,128)(2,1)S(1)}, bf16[128,1152]{1,0:T(8,128)(2,1)S(1)}, u32[]{:S(2)}, u32[]{:S(2)}) collective-permute-start(bf16[128,1152]{1,0:T(8,128)(2,1)S(1)} %convolution_convert_fusion.13), channel_id=1, source_target_pairs={{0,2},{2,0},{1,3},{3,1},{4,6},{6,4},{5,7},{7,5},{8,10},{10,8},{9,1... | collective-permute-start | bytes 884744 | tf_op jit(solution)/shard_map/ppermute | solution.py:33
  15.5 2.6 %collective-permute-start.6 = (bf16[128,384]{1,0:T(8,128)(2,1)S(1)}, bf16[128,384]{1,0:T(8,128)(2,1)S(1)}, u32[]{:S(2)}, u32[]{:S(2)}) collective-permute-start(bf16[128,384]{1,0:T(8,128)(2,1)S(1)} %pad_maximum_fusion.13), channel_id=1, source_target_pairs={{0,8},{8,0},{4,12},{12,4},{1,9},{9,1},{5,13},{13,5},{2,10},{10,2},... | collective-permute-start | bytes 294920 | tf_op jit(solution)/shard_map/ppermute | solution.py:33
  18.5 1.6 %collective-permute-start.9 = (bf16[88,1152]{1,0:T(8,128)(2,1)S(1)}, bf16[88,1152]{1,0:T(8,128)(2,1)S(1)}, u32[]{:S(2)}, u32[]{:S(2)}) collective-permute-start(bf16[88,1152]{1,0:T(8,128)(2,1)S(1)} %convolution_convert_fusion.16), channel_id=1, source_target_pairs={{0,4},{4,0},{8,12},{12,8},{1,5},{5,1},{9,13},{13,9},{2,6},{6,2},{1... | collective-permute-start | bytes 608264 | tf_op jit(solution)/shard_map/ppermute | solution.py:33
  20.1 1.2 %collective-permute-done.6 = bf16[128,384]{1,0:T(8,128)(2,1)S(1)} collective-permute-done((bf16[128,384]{1,0:T(8,128)(2,1)S(1)}, bf16[128,384]{1,0:T(8,128)(2,1)S(1)}, u32[]{:S(2)}, u32[]{:S(2)}) %collective-permute-start.6) | collective-permute-done | bytes 98336 | tf_op jit(solution)/shard_map/ppermute | solution.py:33
  21.3 0.2 convolution_convert_fusion.12
  22.3 3.4 %collective-permute-start.15 = (bf16[80,640]{1,0:T(8,128)(2,1)S(1)}, bf16[80,640]{1,0:T(8,128)(2,1)S(1)}, u32[]{:S(2)}, u32[]{:S(2)}) collective-permute-start(bf16[80,640]{1,0:T(8,128)(2,1)S(1)} %convolution_convert_fusion.30), channel_id=1, source_target_pairs={{0,8},{8,0},{4,12},{12,4},{1,9},{9,1},{5,13},{13,5},{2,10},{10,2},... | collective-permute-start | bytes 307208 | tf_op jit(solution)/shard_map/ppermute | solution.py:33
  26.0 0.7 %collective-permute-start.13 = (bf16[128,896]{1,0:T(8,128)(2,1)S(1)}, bf16[128,896]{1,0:T(8,128)(2,1)S(1)}, u32[]{:S(2)}, u32[]{:S(2)}) collective-permute-start(bf16[128,896]{1,0:T(8,128)(2,1)S(1)} %convolution_convert_fusion.23), channel_id=1, source_target_pairs={{0,2},{2,0},{1,3},{3,1},{4,6},{6,4},{5,7},{7,5},{8,10},{10,8},{9,1... | collective-permute-start | bytes 688136 | tf_op jit(solution)/shard_map/ppermute | solution.py:33
  27.3 1.3 %collective-permute-start.16 = (bf16[88,1152]{1,0:T(8,128)(2,1)S(1)}, bf16[88,1152]{1,0:T(8,128)(2,1)S(1)}, u32[]{:S(2)}, u32[]{:S(2)}) collective-permute-start(bf16[88,1152]{1,0:T(8,128)(2,1)S(1)} %convolution_convert_fusion.15), channel_id=1, source_target_pairs={{0,4},{4,0},{8,12},{12,8},{1,5},{5,1},{9,13},{13,9},{2,6},{6,2},{1... | collective-permute-start | bytes 608264 | tf_op jit(solution)/shard_map/ppermute | solution.py:33
  28.6 1.0 %convolution_convert_fusion.10 = bf16[128,1152]{1,0:T(8,128)(2,1)} fusion(bf16[128,256]{1,0:T(8,128)(2,1)S(1)} %get-tuple-element.86, bf16[128,1152]{1,0:T(8,128)(2,1)S(1)} %collective-permute-done.10, bf16[128,1152]{1,0:T(8,128)(2,1)S(1)} %convolution_convert_fusion.13), kind=kOutput, calls=%fused_computation.35 | convolution fusion | flops 76824576 | bytes 950272 | tf_op jit(solution)/shard_map/dot_general | solution.py:222
  30.0 1.0 %convolution_convert_fusion.11 = bf16[128,1152]{1,0:T(8,128)(2,1)} fusion(bf16[128,256]{1,0:T(8,128)(2,1)S(1)} %slice_bitcast_fusion.7, bf16[88,1152]{1,0:T(8,128)(2,1)S(1)} %collective-permute-done.9, bf16[128,1152]{1,0:T(8,128)(2,1)S(1)} %convolution_convert_fusion.12), kind=kOutput, calls=%fused_computation.36 | convolution fusion | flops 77709312 | bytes 858112 | tf_op jit(solution)/shard_map/dot_general | solution.py:222
  31.0 2.0 %collective-permute-start.11 = (bf16[8,64]{1,0:T(8,128)(2,1)S(1)}, bf16[8,64]{1,0:T(8,128)(2,1)S(1)}, u32[]{:S(2)}, u32[]{:S(2)}) collective-permute-start(bf16[8,64]{1,0:T(8,128)(2,1)S(1)} %slice_maximum_fusion), channel_id=1, source_target_pairs={{0,2},{2,0},{1,3},{3,1},{4,6},{6,4},{5,7},{7,5},{8,10},{10,8},{9,1... | collective-permute-start | bytes 3080 | tf_op jit(solution)/shard_map/ppermute | solution.py:33
  32.9 1.0 %constant_dynamic-update-slice_fusion.3 = bf16[4096,128]{1,0:T(8,128)(2,1)} fusion(bf16[1,128,128]{2,1,0:T(8,128)(2,1)S(1)} %copy-done.6, bf16[128,256]{1,0:T(8,128)(2,1)S(1)} %slice-done, bf16[128,256]{1,0:T(8,128)(2,1)S(1)} %convolution_convert_fusion.33, bf16[3,128,256]{2,1,0:T(8,128)(2,1)S(1)} %get-tuple-element.66), kind=kOutput, calls=%fused_computation.166 | convolution fusion | flops 25493504 | bytes 294912 | tf_op jit(solution)/shard_map/ct,cp->tp/dot_general | solution.py:232
  34.6 1.3 %collective-permute-done.16 = bf16[88,1152]{1,0:T(8,128)(2,1)S(1)} collective-permute-done((bf16[88,1152]{1,0:T(8,128)(2,1)S(1)}, bf16[88,1152]{1,0:T(8,128)(2,1)S(1)}, u32[]{:S(2)}, u32[]{:S(2)}) %collective-permute-start.16) | collective-permute-done | bytes 202784 | tf_op jit(solution)/shard_map/ppermute | solution.py:33
  35.9 1.2 %convolution_convert_fusion.17 = bf16[80,1152]{1,0:T(8,128)(2,1)S(1)} fusion(bf16[88,1152]{1,0:T(8,128)(2,1)S(1)} %collective-permute-done.16, bf16[128,1152]{1,0:T(8,128)(2,1)} %convolution_convert_fusion.10, bf16[40,256]{1,0:T(8,128)(2,1)S(1)} %convolution_convert_fusion.39, bf16[40,256]{1,0:T(8,128)(2,1)S(1)} %convolution_convert_fusion.40), kind=kOutput, calls=%fused_computation.42 | convolution fusion | flops 49424384 | bytes 722944 | tf_op jit(solution)/shard_map/dot_general | solution.py:222
  37.1 1.7 %collective-permute-start.17 = (bf16[80,1152]{1,0:T(8,128)(2,1)S(1)}, bf16[80,1152]{1,0:T(8,128)(2,1)S(1)}, u32[]{:S(2)}, u32[]{:S(2)}) collective-permute-start(bf16[80,1152]{1,0:T(8,128)(2,1)S(1)} %convolution_convert_fusion.17), channel_id=1, source_target_pairs={{0,8},{8,0},{4,12},{12,4},{1,9},{9,1},{5,13},{13,5},{2,10},{10,2},... | collective-permute-start | bytes 552968 | tf_op jit(solution)/shard_map/ppermute | solution.py:33
  38.8 1.1 %constant_dynamic-update-slice_fusion.2 = bf16[4096,128]{1,0:T(8,128)(2,1)} fusion(bf16[4096,128]{1,0:T(8,128)(2,1)} %constant_dynamic-update-slice_fusion.3, bf16[1,128,128]{2,1,0:T(8,128)(2,1)S(1)} %copy-done.6, bf16[80,640]{1,0:T(8,128)(2,1)S(1)} %collective-permute-done.15, bf16[128,640]{1,0:T(8,128)(2,1)S(1)} %convolution_convert_fusion.25, ...), kind=kOutput, calls=%fused_computation.165 | convolution fusion | flops 64225280 | bytes 528384 | tf_op jit(solution)/shard_map/ct,cp->tp/dot_general | solution.py:232
  40.4 4.0 %collective-permute-start.18 = (bf16[80,896]{1,0:T(8,128)(2,1)S(1)}, bf16[80,896]{1,0:T(8,128)(2,1)S(1)}, u32[]{:S(2)}, u32[]{:S(2)}) collective-permute-start(bf16[80,896]{1,0:T(8,128)(2,1)S(1)} %convolution_convert_fusion.29), channel_id=1, source_target_pairs={{0,8},{8,0},{4,12},{12,4},{1,9},{9,1},{5,13},{13,5},{2,10},{10,2},... | collective-permute-start | bytes 430088 | tf_op jit(solution)/shard_map/ppermute | solution.py:33
  44.4 1.2 %constant_dynamic-update-slice_fusion.1 = bf16[4096,128]{1,0:T(8,128)(2,1)} fusion(bf16[4096,128]{1,0:T(8,128)(2,1)} %constant_dynamic-update-slice_fusion.2, bf16[1,128,128]{2,1,0:T(8,128)(2,1)S(1)} %copy-done.6, bf16[80,1152]{1,0:T(8,128)(2,1)S(1)} %collective-permute-done.12, bf16[128,1152]{1,0:T(8,128)(2,1)S(1)} %copy-done.8, ...), kind=kOutput, calls=%fused_computation.164 | convolution fusion | flops 115605504 | bytes 872448 | tf_op jit(solution)/shard_map/ct,cp->tp/dot_general | solution.py:232
  45.6 0.5 slice.183
  46.9 3.5 %collective-permute-done.17 = bf16[80,1152]{1,0:T(8,128)(2,1)S(1)} collective-permute-done((bf16[80,1152]{1,0:T(8,128)(2,1)S(1)}, bf16[80,1152]{1,0:T(8,128)(2,1)S(1)}, u32[]{:S(2)}, u32[]{:S(2)}) %collective-permute-start.17) | collective-permute-done | bytes 184352 | tf_op jit(solution)/shard_map/ppermute | solution.py:33
  50.4 1.2 %constant_dynamic-update-slice_fusion = bf16[4096,128]{1,0:T(8,128)(2,1)} fusion(bf16[4096,128]{1,0:T(8,128)(2,1)} %constant_dynamic-update-slice_fusion.1, bf16[1,128,128]{2,1,0:T(8,128)(2,1)S(1)} %copy-done.6, bf16[80,1152]{1,0:T(8,128)(2,1)S(1)} %collective-permute-done.17, bf16[128,1152]{1,0:T(8,128)(2,1)S(1)} %convolution_convert_fusion.7, ...), kind=kOutput, calls=%fused_computation.163 | convolution fusion | flops 115605504 | bytes 872448 | tf_op jit(solution)/shard_map/ct,cp->tp/dot_general | solution.py:232
  51.6 0.9 %collective-permute-done.18 = bf16[80,896]{1,0:T(8,128)(2,1)S(1)} collective-permute-done((bf16[80,896]{1,0:T(8,128)(2,1)S(1)}, bf16[80,896]{1,0:T(8,128)(2,1)S(1)}, u32[]{:S(2)}, u32[]{:S(2)}) %collective-permute-start.18) | collective-permute-done | bytes 143392 | tf_op jit(solution)/shard_map/ppermute | solution.py:33
  52.6 1.1 %fusion.20 = bf16[4096,128]{1,0:T(8,128)(2,1)} fusion(bf16[4096,128]{1,0:T(8,128)(2,1)} %constant_dynamic-update-slice_fusion, bf16[80,896]{1,0:T(8,128)(2,1)S(1)} %collective-permute-done.18, bf16[128,896]{1,0:T(8,128)(2,1)S(1)} %convolution_convert_fusion.21, bf16[2,128,256]{2,1,0:T(8,128)(2,1)S(1)} %get-tuple-element.76, ...), kind=kOutput, calls=%fused_computation.45 | convolution fusion | flops 89915392 | bytes 700416 | tf_op jit(solution)/shard_map/ct,cp->tp/dot_general | solution.py:232
  (64 shorter events, 4.5 us)
Async XLA Ops:
  0.0 4.6 %copy-start = (bf16[4096,128]{1,0:T(8,128)(2,1)S(1)}, bf16[4096,128]{1,0:T(8,128)(2,1)}, u32[]{:S(2)}) copy-start(bf16[4096,128]{1,0:T(8,128)(2,1)} %refs_1_.2) | copy-start | bytes 3145732
  0.0 4.6 %copy-start.2 = (bf16[1,128,128]{2,1,0:T(8,128)(2,1)S(1)}, bf16[1,128,128]{2,1,0:T(8,128)(2,1)}, u32[]{:S(2)}) copy-start(bf16[1,128,128]{2,1,0:T(8,128)(2,1)} %refs_0_.1) | copy-start | bytes 98308
  0.0 6.8 %copy-start.5 = (s32[1,3,64]{2,0,1:T(1,128)S(1)}, s32[1,3,64]{2,0,1:T(1,128)}, u32[]{:S(2)}) copy-start(s32[1,3,64]{2,0,1:T(1,128)} %param.9) | copy-start | bytes 2308
  0.0 6.8 %copy-start.4 = (bf16[1,3,64,128]{3,2,1,0:T(8,128)(2,1)S(1)}, bf16[1,3,64,128]{3,2,1,0:T(8,128)(2,1)}, u32[]{:S(2)}) copy-start(bf16[1,3,64,128]{3,2,1,0:T(8,128)(2,1)} %refs_1_.3) | copy-start | bytes 147460
  1.5 6.5 %collective-permute-start.3 = (bf16[128,256]{1,0:T(8,128)(2,1)S(1)}, bf16[128,256]{1,0:T(8,128)(2,1)S(1)}, u32[]{:S(2)}, u32[]{:S(2)}) collective-permute-start(bf16[128,256]{1,0:T(8,128)(2,1)S(1)} %get-tuple-element.63), channel_id=1, source_target_pairs={{0,2},{2,0},{1,3},{3,1},{4,6},{6,4},{5,7},{7,5},{8,10},{10,8},{9,1... | collective-permute-start | bytes 196616 | tf_op jit(solution)/shard_map/ppermute | solution.py:33
  4.5 7.1 %collective-permute-start.5 = (bf16[128,640]{1,0:T(8,128)(2,1)S(1)}, bf16[128,640]{1,0:T(8,128)(2,1)S(1)}, u32[]{:S(2)}, u32[]{:S(2)}) collective-permute-start(bf16[128,640]{1,0:T(8,128)(2,1)S(1)} %get-tuple-element.67), channel_id=1, source_target_pairs={{0,2},{2,0},{1,3},{3,1},{4,6},{6,4},{5,7},{7,5},{8,10},{10,8},{9,1... | collective-permute-start | bytes 491528 | tf_op jit(solution)/shard_map/ppermute | solution.py:33
  4.8 13.4 %collective-permute-start.7 = (bf16[128,1152]{1,0:T(8,128)(2,1)S(1)}, bf16[128,1152]{1,0:T(8,128)(2,1)S(1)}, u32[]{:S(2)}, u32[]{:S(2)}) collective-permute-start(bf16[128,1152]{1,0:T(8,128)(2,1)S(1)} %convolution_convert_fusion.14), channel_id=1, source_target_pairs={{0,2},{2,0},{1,3},{3,1},{4,6},{6,4},{5,7},{7,5},{8,10},{10,8},{9,1... | collective-permute-start | bytes 884744 | tf_op jit(solution)/shard_map/ppermute | solution.py:33
  8.2 5.6 %collective-permute-start.4 = (bf16[128,384]{1,0:T(8,128)(2,1)S(1)}, bf16[128,384]{1,0:T(8,128)(2,1)S(1)}, u32[]{:S(2)}, u32[]{:S(2)}) collective-permute-start(bf16[128,384]{1,0:T(8,128)(2,1)S(1)} %pad_maximum_fusion.12), channel_id=1, source_target_pairs={{0,4},{4,0},{8,12},{12,8},{1,5},{5,1},{9,13},{13,9},{2,6},{6,2},{1... | collective-permute-start | bytes 294920 | tf_op jit(solution)/shard_map/ppermute | solution.py:33
  11.8 9.8 %collective-permute-start.8 = (bf16[128,640]{1,0:T(8,128)(2,1)S(1)}, bf16[128,640]{1,0:T(8,128)(2,1)S(1)}, u32[]{:S(2)}, u32[]{:S(2)}) collective-permute-start(bf16[128,640]{1,0:T(8,128)(2,1)S(1)} %convolution_convert_fusion.26), channel_id=1, source_target_pairs={{0,4},{4,0},{8,12},{12,8},{1,5},{5,1},{9,13},{13,9},{2,6},{6,2},{1... | collective-permute-start | bytes 491528 | tf_op jit(solution)/shard_map/ppermute | solution.py:33
  13.9 13.2 %collective-permute-start.10 = (bf16[128,1152]{1,0:T(8,128)(2,1)S(1)}, bf16[128,1152]{1,0:T(8,128)(2,1)S(1)}, u32[]{:S(2)}, u32[]{:S(2)}) collective-permute-start(bf16[128,1152]{1,0:T(8,128)(2,1)S(1)} %convolution_convert_fusion.13), channel_id=1, source_target_pairs={{0,2},{2,0},{1,3},{3,1},{4,6},{6,4},{5,7},{7,5},{8,10},{10,8},{9,1... | collective-permute-start | bytes 884744 | tf_op jit(solution)/shard_map/ppermute | solution.py:33
  15.5 5.8 %collective-permute-start.6 = (bf16[128,384]{1,0:T(8,128)(2,1)S(1)}, bf16[128,384]{1,0:T(8,128)(2,1)S(1)}, u32[]{:S(2)}, u32[]{:S(2)}) collective-permute-start(bf16[128,384]{1,0:T(8,128)(2,1)S(1)} %pad_maximum_fusion.13), channel_id=1, source_target_pairs={{0,8},{8,0},{4,12},{12,4},{1,9},{9,1},{5,13},{13,5},{2,10},{10,2},... | collective-permute-start | bytes 294920 | tf_op jit(solution)/shard_map/ppermute | solution.py:33
  18.5 11.1 %collective-permute-start.9 = (bf16[88,1152]{1,0:T(8,128)(2,1)S(1)}, bf16[88,1152]{1,0:T(8,128)(2,1)S(1)}, u32[]{:S(2)}, u32[]{:S(2)}) collective-permute-start(bf16[88,1152]{1,0:T(8,128)(2,1)S(1)} %convolution_convert_fusion.16), channel_id=1, source_target_pairs={{0,4},{4,0},{8,12},{12,8},{1,5},{5,1},{9,13},{13,9},{2,6},{6,2},{1... | collective-permute-start | bytes 608264 | tf_op jit(solution)/shard_map/ppermute | solution.py:33
  21.3 8.7 %copy-start.3 = (bf16[128,384]{1,0:T(8,128)(2,1)}, bf16[128,384]{1,0:T(8,128)(2,1)S(1)}, u32[]{:S(2)}) copy-start(bf16[128,384]{1,0:T(8,128)(2,1)S(1)} %collective-permute-done.6) | copy-start | bytes 294916
  22.3 16.4 %collective-permute-start.15 = (bf16[80,640]{1,0:T(8,128)(2,1)S(1)}, bf16[80,640]{1,0:T(8,128)(2,1)S(1)}, u32[]{:S(2)}, u32[]{:S(2)}) collective-permute-start(bf16[80,640]{1,0:T(8,128)(2,1)S(1)} %convolution_convert_fusion.30), channel_id=1, source_target_pairs={{0,8},{8,0},{4,12},{12,4},{1,9},{9,1},{5,13},{13,5},{2,10},{10,2},... | collective-permute-start | bytes 307208 | tf_op jit(solution)/shard_map/ppermute | solution.py:33
  26.0 7.9 %collective-permute-start.13 = (bf16[128,896]{1,0:T(8,128)(2,1)S(1)}, bf16[128,896]{1,0:T(8,128)(2,1)S(1)}, u32[]{:S(2)}, u32[]{:S(2)}) collective-permute-start(bf16[128,896]{1,0:T(8,128)(2,1)S(1)} %convolution_convert_fusion.23), channel_id=1, source_target_pairs={{0,2},{2,0},{1,3},{3,1},{4,6},{6,4},{5,7},{7,5},{8,10},{10,8},{9,1... | collective-permute-start | bytes 688136 | tf_op jit(solution)/shard_map/ppermute | solution.py:33
  27.3 8.6 %collective-permute-start.16 = (bf16[88,1152]{1,0:T(8,128)(2,1)S(1)}, bf16[88,1152]{1,0:T(8,128)(2,1)S(1)}, u32[]{:S(2)}, u32[]{:S(2)}) collective-permute-start(bf16[88,1152]{1,0:T(8,128)(2,1)S(1)} %convolution_convert_fusion.15), channel_id=1, source_target_pairs={{0,4},{4,0},{8,12},{12,8},{1,5},{5,1},{9,13},{13,9},{2,6},{6,2},{1... | collective-permute-start | bytes 608264 | tf_op jit(solution)/shard_map/ppermute | solution.py:33
  29.8 14.6 %collective-permute-start.12 = (bf16[80,1152]{1,0:T(8,128)(2,1)S(1)}, bf16[80,1152]{1,0:T(8,128)(2,1)S(1)}, u32[]{:S(2)}, u32[]{:S(2)}) collective-permute-start(bf16[80,1152]{1,0:T(8,128)(2,1)S(1)} %convolution_convert_fusion.18), channel_id=1, source_target_pairs={{0,8},{8,0},{4,12},{12,4},{1,9},{9,1},{5,13},{13,5},{2,10},{10,2},... | collective-permute-start | bytes 552968 | tf_op jit(solution)/shard_map/ppermute | solution.py:33
  30.0 3.0 %slice-start = ((bf16[128,384]{1,0:T(8,128)(2,1)}), bf16[128,256]{1,0:T(8,128)(2,1)S(1)}, s32[]{:S(2)}) async-start(bf16[128,384]{1,0:T(8,128)(2,1)} %copy-done.3), calls=%async_computation | async-start | bytes 131072 | tf_op jit(solution)/shard_map/slice | solution.py:298
  30.0 3.0 %copy-start.6 = (bf16[1,128,128]{2,1,0:T(8,128)(2,1)S(1)}, bf16[1,128,128]{2,1,0:T(8,128)(2,1)}, u32[]{:S(2)}) copy-start(bf16[1,128,128]{2,1,0:T(8,128)(2,1)} %param.11) | copy-start | bytes 98308
  31.0 14.7 %collective-permute-start.11 = (bf16[8,64]{1,0:T(8,128)(2,1)S(1)}, bf16[8,64]{1,0:T(8,128)(2,1)S(1)}, u32[]{:S(2)}, u32[]{:S(2)}) collective-permute-start(bf16[8,64]{1,0:T(8,128)(2,1)S(1)} %slice_maximum_fusion), channel_id=1, source_target_pairs={{0,2},{2,0},{1,3},{3,1},{4,6},{6,4},{5,7},{7,5},{8,10},{10,8},{9,1... | collective-permute-start | bytes 3080 | tf_op jit(solution)/shard_map/ppermute | solution.py:33
  34.2 6.1 %collective-permute-start.14 = (bf16[88,896]{1,0:T(8,128)(2,1)S(1)}, bf16[88,896]{1,0:T(8,128)(2,1)S(1)}, u32[]{:S(2)}, u32[]{:S(2)}) collective-permute-start(bf16[88,896]{1,0:T(8,128)(2,1)S(1)} %convolution_convert_fusion.28), channel_id=1, source_target_pairs={{0,4},{4,0},{8,12},{12,8},{1,5},{5,1},{9,13},{13,9},{2,6},{6,2},{1... | collective-permute-start | bytes 473096 | tf_op jit(solution)/shard_map/ppermute | solution.py:33
  37.1 2.8 %copy-start.7 = (bf16[128,1152]{1,0:T(8,128)(2,1)S(1)}, bf16[128,1152]{1,0:T(8,128)(2,1)}, u32[]{:S(2)}) copy-start(bf16[128,1152]{1,0:T(8,128)(2,1)} %convolution_convert_fusion.10) | copy-start | bytes 884740
  37.1 13.3 %collective-permute-start.17 = (bf16[80,1152]{1,0:T(8,128)(2,1)S(1)}, bf16[80,1152]{1,0:T(8,128)(2,1)S(1)}, u32[]{:S(2)}, u32[]{:S(2)}) collective-permute-start(bf16[80,1152]{1,0:T(8,128)(2,1)S(1)} %convolution_convert_fusion.17), channel_id=1, source_target_pairs={{0,8},{8,0},{4,12},{12,4},{1,9},{9,1},{5,13},{13,5},{2,10},{10,2},... | collective-permute-start | bytes 552968 | tf_op jit(solution)/shard_map/ppermute | solution.py:33
  40.1 4.3 %copy-start.8 = (bf16[128,1152]{1,0:T(8,128)(2,1)S(1)}, bf16[128,1152]{1,0:T(8,128)(2,1)}, u32[]{:S(2)}) copy-start(bf16[128,1152]{1,0:T(8,128)(2,1)} %convolution_convert_fusion.11) | copy-start | bytes 884740
  40.4 12.1 %collective-permute-start.18 = (bf16[80,896]{1,0:T(8,128)(2,1)S(1)}, bf16[80,896]{1,0:T(8,128)(2,1)S(1)}, u32[]{:S(2)}, u32[]{:S(2)}) collective-permute-start(bf16[80,896]{1,0:T(8,128)(2,1)S(1)} %convolution_convert_fusion.29), channel_id=1, source_target_pairs={{0,8},{8,0},{4,12},{12,4},{1,9},{9,1},{5,13},{13,5},{2,10},{10,2},... | collective-permute-start | bytes 430088 | tf_op jit(solution)/shard_map/ppermute | solution.py:33

commit v19 on v18

--- a/solution.py
+++ b/solution.py
@@ -12,8 +12,8 @@
 COUNT_READ = 2
 LOOK = (3, -1)
 ORDER = (
-    (0, 0), (0, 1), (0, 2), (1, 0), (1, 1), (0, 3), (2, 0), (1, 2), LOOK, (2, 1), (0, 4), (1, 3),
-    (2, 2), (3, 0), (1, 4), (2, 3), (3, 1), (2, 4), (3, 2), (3, 3), (3, 4),
+    (0, 0), (0, 1), (0, 2), (1, 0), (1, 1), (0, 3), (2, 0), (1, 2), LOOK, (2, 1), (1, 3), (2, 2),
+    (0, 4), (3, 0), (1, 4), (2, 3), (3, 1), (2, 4), (3, 2), (3, 3), (3, 4),
 )
 KERNEL_VMEM = 16 * 1024 * 1024
 ROOM_SIXTEENTHS = (11, 10)
@@ -266,7 +266,7 @@
     unit = traces.shape[0] // sum(SHARES)
     pieces = len(SHARES)
     starts = [unit * sum(SHARES[:i]) for i in range(pieces + 1)]
-    coeffs = early(sampling, traces, starts[: EARLY_PIECES + 1])
+    coeffs = list(early(sampling, traces, starts[: EARLY_PIECES + 1]))
     full, small, extra = tables(after(skeleton, coeffs[0]), compress, wide, rooms)
     sampling, evaluation = sampling[0], evaluation[0]
     most_here = lax.broadcasted_iota(jnp.int32, extra.shape[1:], 1) >= rank
@@ -283,11 +283,11 @@
             continue
         count = starts[piece + 1] - starts[piece]
         if level == 0:
-            if piece < EARLY_PIECES:
-                own = coeffs[piece]
-            else:
-                block = traces[starts[piece] : starts[piece + 1]]
-                own = sampled(after(sampling, previous), block)
+            if piece == len(coeffs):
+                waiting = after(sampling, previous)
+                for late in (piece, piece + 1) if piece == pieces - 2 else (piece,):
+                    coeffs.append(sampled(waiting, traces[starts[late] : starts[late + 1]]))
+            own = coeffs[piece]
         else:
             arrived = after(partners[piece], previous)
             if level == levels:
@@ -311,7 +311,7 @@
                 most = jnp.maximum(most, after(counted, finished))
             continue
         if level == 0:
-            outgoing = own
+            outgoing = after(own, previous) if piece == pieces - 1 else own
         if piece == 0 and level >= wide:
             block = extra[level - wide]
             if known is not None:

time: 53.9 us -> 53.4 us (level)
  starting transfers between devices: 27.5 us -> 28.8 us
  waiting for transfers between devices: 8.87 us -> 7.86 us
  matrix products: 13.3 us -> 12.3 us
    ppermute x16, starting transfers between devices: 27.5 us -> 28.8 us  [from_partner(): return lax.ppermute(block, hop[0], route(*hop))]
    ppermute x16, waiting for transfers between devices: 8.87 us -> 7.86 us  [from_partner(): return lax.ppermute(block, hop[0], route(*hop))]
    dot_general x17, matrix products: 6.12 us -> 5.17 us  [times(): jnp.dot(matrix, value, preferred_element_type=jnp.float32)]
  transfers between devices with their start and end apart: 16 -> 16, of which waited for: 6 -> 5; matrix products, arithmetic and copies ran while one was open for 24% -> 22% of each run, Pallas kernels for 2% -> 2%
where the time goes in v19:
time: 53.4 us; the launch traced here: 53.3 us
  starting transfers between devices  28.8 us (54%)
  matrix products  12.3 us (23%)
  waiting for transfers between devices  7.86 us (15%)
  Pallas kernels  2.51 us (5%)
  between operations  0.99 us (2%)
  local copies, waits for them, and re-layouts  0.65 us (1%)
    ppermute x16, starting transfers between devices, from_partner(): return lax.ppermute(block, hop[0], route(*hop))  28.8 us
    ppermute x16, waiting for transfers between devices, from_partner(): return lax.ppermute(block, hop[0], route(*hop))  7.86 us
    dot_general x5, matrix products, evaluated(): jnp.einsum('ct,cp->tp', coeffs, evaluation, preferred_element_type=jnp.fl...  5.63 us
    dot_general x17, matrix products, times(): jnp.dot(matrix, value, preferred_element_type=jnp.float32)  5.17 us
    pallas_call x1, Pallas kernels, early(): pl.pallas_call(lambda *refs: early_kernel(starts, *refs), out_shape=[jax....  1.45 us
  transfers between devices with their start and end apart: 16, of which 5 were waited for; matrix products, arithmetic and copies ran while one was open for 22% of the time, Pallas kernels for 2%

profile of v19, /device:TPU:0, one launch (start us, length us, event | category | flops | bytes accessed | tf_op | source)
XLA Modules:
  0.0 53.3 jit_solution(9425529462031855066)
XLA Ops:
  0.0 1.4 %early.1 = (bf16[128,256]{1,0:T(8,128)(2,1)S(1)}, bf16[128,640]{1,0:T(8,128)(2,1)S(1)}) custom-call(bf16[1,128,128]{2,1,0:T(8,128)(2,1)} %refs_0_.1, bf16[4096,128]{1,0:T(8,128)(2,1)} %refs_1_.2), custom_call_target="tpu_custom_call" | custom-call | flops 29360128 | bytes 458752 | tf_op jit(solution)/shard_map/early/pallas_call | solution.py:69
  1.5 3.0 %collective-permute-start.3 = (bf16[128,256]{1,0:T(8,128)(2,1)S(1)}, bf16[128,256]{1,0:T(8,128)(2,1)S(1)}, u32[]{:S(2)}, u32[]{:S(2)}) collective-permute-start(bf16[128,256]{1,0:T(8,128)(2,1)S(1)} %get-tuple-element.63), channel_id=1, source_target_pairs={{0,2},{2,0},{1,3},{3,1},{4,6},{6,4},{5,7},{7,5},{8,10},{10,8},{9,1... | collective-permute-start | bytes 196616 | tf_op jit(solution)/shard_map/ppermute | solution.py:33
  4.6 0.3 convolution_convert_fusion.14
  4.8 2.0 %collective-permute-start.7 = (bf16[128,1152]{1,0:T(8,128)(2,1)S(1)}, bf16[128,1152]{1,0:T(8,128)(2,1)S(1)}, u32[]{:S(2)}, u32[]{:S(2)}) collective-permute-start(bf16[128,1152]{1,0:T(8,128)(2,1)S(1)} %convolution_convert_fusion.14), channel_id=1, source_target_pairs={{0,2},{2,0},{1,3},{3,1},{4,6},{6,4},{5,7},{7,5},{8,10},{10,8},{9,1... | collective-permute-start | bytes 884744 | tf_op jit(solution)/shard_map/ppermute | solution.py:33
  6.8 1.1 %tables.1 = (bf16[3,128,256]{2,1,0:T(8,128)(2,1)S(1)}, bf16[2,128,256]{2,1,0:T(8,128)(2,1)S(1)}, bf16[2,128,128]{2,1,0:T(8,128)(2,1)S(1)}) custom-call(s32[3,1,64]{2,1,0:T(1,128)S(1)} %bitcast.111, bf16[1,3,64,128]{3,2,1,0:T(8,128)(2,1)S(1)} %copy-done.4), custom_call_target="tpu_custom_call" | custom-call | flops 50000000 | bytes 600000 | tf_op jit(solution)/shard_map/tables/pallas_call | solution.py:155
  8.2 1.6 %collective-permute-start.4 = (bf16[128,384]{1,0:T(8,128)(2,1)S(1)}, bf16[128,384]{1,0:T(8,128)(2,1)S(1)}, u32[]{:S(2)}, u32[]{:S(2)}) collective-permute-start(bf16[128,384]{1,0:T(8,128)(2,1)S(1)} %pad_maximum_fusion.12), channel_id=1, source_target_pairs={{0,4},{4,0},{8,12},{12,8},{1,5},{5,1},{9,13},{13,9},{2,6},{6,2},{1... | collective-permute-start | bytes 294920 | tf_op jit(solution)/shard_map/ppermute | solution.py:33
  9.8 1.8 %collective-permute-done.5 = bf16[128,640]{1,0:T(8,128)(2,1)S(1)} collective-permute-done((bf16[128,640]{1,0:T(8,128)(2,1)S(1)}, bf16[128,640]{1,0:T(8,128)(2,1)S(1)}, u32[]{:S(2)}, u32[]{:S(2)}) %collective-permute-start.5) | collective-permute-done | bytes 163872 | tf_op jit(solution)/shard_map/ppermute | solution.py:33
  11.8 1.6 %collective-permute-start.8 = (bf16[128,640]{1,0:T(8,128)(2,1)S(1)}, bf16[128,640]{1,0:T(8,128)(2,1)S(1)}, u32[]{:S(2)}, u32[]{:S(2)}) collective-permute-start(bf16[128,640]{1,0:T(8,128)(2,1)S(1)} %convolution_convert_fusion.26), channel_id=1, source_target_pairs={{0,4},{4,0},{8,12},{12,8},{1,5},{5,1},{9,13},{13,9},{2,6},{6,2},{1... | collective-permute-start | bytes 491528 | tf_op jit(solution)/shard_map/ppermute | solution.py:33
  13.5 0.3 convolution_convert_fusion.13
  14.0 1.4 %collective-permute-start.10 = (bf16[128,1152]{1,0:T(8,128)(2,1)S(1)}, bf16[128,1152]{1,0:T(8,128)(2,1)S(1)}, u32[]{:S(2)}, u32[]{:S(2)}) collective-permute-start(bf16[128,1152]{1,0:T(8,128)(2,1)S(1)} %convolution_convert_fusion.13), channel_id=1, source_target_pairs={{0,2},{2,0},{1,3},{3,1},{4,6},{6,4},{5,7},{7,5},{8,10},{10,8},{9,1... | collective-permute-start | bytes 884744 | tf_op jit(solution)/shard_map/ppermute | solution.py:33
  15.6 2.6 %collective-permute-start.6 = (bf16[128,384]{1,0:T(8,128)(2,1)S(1)}, bf16[128,384]{1,0:T(8,128)(2,1)S(1)}, u32[]{:S(2)}, u32[]{:S(2)}) collective-permute-start(bf16[128,384]{1,0:T(8,128)(2,1)S(1)} %pad_maximum_fusion.13), channel_id=1, source_target_pairs={{0,8},{8,0},{4,12},{12,4},{1,9},{9,1},{5,13},{13,5},{2,10},{10,2},... | collective-permute-start | bytes 294920 | tf_op jit(solution)/shard_map/ppermute | solution.py:33
  18.3 0.2 convolution_convert_fusion.23
  18.8 1.6 %collective-permute-start.9 = (bf16[88,1152]{1,0:T(8,128)(2,1)S(1)}, bf16[88,1152]{1,0:T(8,128)(2,1)S(1)}, u32[]{:S(2)}, u32[]{:S(2)}) collective-permute-start(bf16[88,1152]{1,0:T(8,128)(2,1)S(1)} %convolution_convert_fusion.16), channel_id=1, source_target_pairs={{0,4},{4,0},{8,12},{12,8},{1,5},{5,1},{9,13},{13,9},{2,6},{6,2},{1... | collective-permute-start | bytes 608264 | tf_op jit(solution)/shard_map/ppermute | solution.py:33
  20.4 1.1 %collective-permute-done.6 = bf16[128,384]{1,0:T(8,128)(2,1)S(1)} collective-permute-done((bf16[128,384]{1,0:T(8,128)(2,1)S(1)}, bf16[128,384]{1,0:T(8,128)(2,1)S(1)}, u32[]{:S(2)}, u32[]{:S(2)}) %collective-permute-start.6) | collective-permute-done | bytes 98336 | tf_op jit(solution)/shard_map/ppermute | solution.py:33
  22.5 3.4 %collective-permute-start.15 = (bf16[80,640]{1,0:T(8,128)(2,1)S(1)}, bf16[80,640]{1,0:T(8,128)(2,1)S(1)}, u32[]{:S(2)}, u32[]{:S(2)}) collective-permute-start(bf16[80,640]{1,0:T(8,128)(2,1)S(1)} %convolution_convert_fusion.30), channel_id=1, source_target_pairs={{0,8},{8,0},{4,12},{12,4},{1,9},{9,1},{5,13},{13,5},{2,10},{10,2},... | collective-permute-start | bytes 307208 | tf_op jit(solution)/shard_map/ppermute | solution.py:33
  26.5 2.1 %collective-permute-start.16 = (bf16[88,1152]{1,0:T(8,128)(2,1)S(1)}, bf16[88,1152]{1,0:T(8,128)(2,1)S(1)}, u32[]{:S(2)}, u32[]{:S(2)}) collective-permute-start(bf16[88,1152]{1,0:T(8,128)(2,1)S(1)} %convolution_convert_fusion.15), channel_id=1, source_target_pairs={{0,4},{4,0},{8,12},{12,8},{1,5},{5,1},{9,13},{13,9},{2,6},{6,2},{1... | collective-permute-start | bytes 608264 | tf_op jit(solution)/shard_map/ppermute | solution.py:33
  29.2 0.3 collective-permute-start.13
  29.5 1.0 %convolution_convert_fusion.11 = bf16[128,1152]{1,0:T(8,128)(2,1)} fusion(bf16[128,256]{1,0:T(8,128)(2,1)S(1)} %slice_bitcast_fusion.7, bf16[88,1152]{1,0:T(8,128)(2,1)S(1)} %collective-permute-done.9, bf16[128,1152]{1,0:T(8,128)(2,1)S(1)} %convolution_convert_fusion.12), kind=kOutput, calls=%fused_computation.36 | convolution fusion | flops 77709312 | bytes 858112 | tf_op jit(solution)/shard_map/dot_general | solution.py:222
  30.5 1.7 %collective-permute-start.11 = (bf16[8,64]{1,0:T(8,128)(2,1)S(1)}, bf16[8,64]{1,0:T(8,128)(2,1)S(1)}, u32[]{:S(2)}, u32[]{:S(2)}) collective-permute-start(bf16[8,64]{1,0:T(8,128)(2,1)S(1)} %slice_maximum_fusion), channel_id=1, source_target_pairs={{0,2},{2,0},{1,3},{3,1},{4,6},{6,4},{5,7},{7,5},{8,10},{10,8},{9,1... | collective-permute-start | bytes 3080 | tf_op jit(solution)/shard_map/ppermute | solution.py:33
  32.2 1.0 %constant_dynamic-update-slice_fusion.3 = bf16[4096,128]{1,0:T(8,128)(2,1)} fusion(bf16[1,128,128]{2,1,0:T(8,128)(2,1)S(1)} %copy-done.6, bf16[128,256]{1,0:T(8,128)(2,1)S(1)} %slice-done, bf16[128,256]{1,0:T(8,128)(2,1)S(1)} %convolution_convert_fusion.33, bf16[3,128,256]{2,1,0:T(8,128)(2,1)S(1)} %get-tuple-element.66), kind=kOutput, calls=%fused_computation.166 | convolution fusion | flops 25493504 | bytes 294912 | tf_op jit(solution)/shard_map/ct,cp->tp/dot_general | solution.py:232
  33.2 2.0 %collective-permute-done.13 = bf16[128,896]{1,0:T(8,128)(2,1)S(1)} collective-permute-done((bf16[128,896]{1,0:T(8,128)(2,1)S(1)}, bf16[128,896]{1,0:T(8,128)(2,1)S(1)}, u32[]{:S(2)}, u32[]{:S(2)}) %collective-permute-start.13) | collective-permute-done | bytes 229408 | tf_op jit(solution)/shard_map/ppermute | solution.py:33
  35.5 1.2 %collective-permute-start.14 = (bf16[88,896]{1,0:T(8,128)(2,1)S(1)}, bf16[88,896]{1,0:T(8,128)(2,1)S(1)}, u32[]{:S(2)}, u32[]{:S(2)}) collective-permute-start(bf16[88,896]{1,0:T(8,128)(2,1)S(1)} %convolution_convert_fusion.28), channel_id=1, source_target_pairs={{0,4},{4,0},{8,12},{12,8},{1,5},{5,1},{9,13},{13,9},{2,6},{6,2},{1... | collective-permute-start | bytes 473096 | tf_op jit(solution)/shard_map/ppermute | solution.py:33
  36.9 1.9 %collective-permute-start.17 = (bf16[80,1152]{1,0:T(8,128)(2,1)S(1)}, bf16[80,1152]{1,0:T(8,128)(2,1)S(1)}, u32[]{:S(2)}, u32[]{:S(2)}) collective-permute-start(bf16[80,1152]{1,0:T(8,128)(2,1)S(1)} %convolution_convert_fusion.17), channel_id=1, source_target_pairs={{0,8},{8,0},{4,12},{12,4},{1,9},{9,1},{5,13},{13,5},{2,10},{10,2},... | collective-permute-start | bytes 552968 | tf_op jit(solution)/shard_map/ppermute | solution.py:33
  38.7 1.0 %convolution_convert_fusion.7 = bf16[128,1152]{1,0:T(8,128)(2,1)} fusion(bf16[128,256]{1,0:T(8,128)(2,1)S(1)} %slice_bitcast_fusion.7, bf16[88,1152]{1,0:T(8,128)(2,1)S(1)} %collective-permute-done.16, bf16[128,1152]{1,0:T(8,128)(2,1)S(1)} %convolution_convert_fusion.10), kind=kOutput, calls=%fused_computation.32 | convolution fusion | flops 77709312 | bytes 858112 | tf_op jit(solution)/shard_map/dot_general | solution.py:222
  39.7 1.1 %constant_dynamic-update-slice_fusion.2 = bf16[4096,128]{1,0:T(8,128)(2,1)} fusion(bf16[4096,128]{1,0:T(8,128)(2,1)} %constant_dynamic-update-slice_fusion.3, bf16[1,128,128]{2,1,0:T(8,128)(2,1)S(1)} %copy-done.6, bf16[80,640]{1,0:T(8,128)(2,1)S(1)} %collective-permute-done.15, bf16[128,640]{1,0:T(8,128)(2,1)S(1)} %convolution_convert_fusion.25, ...), kind=kOutput, calls=%fused_computation.165 | convolution fusion | flops 64225280 | bytes 528384 | tf_op jit(solution)/shard_map/ct,cp->tp/dot_general | solution.py:232
  41.3 4.0 %collective-permute-start.18 = (bf16[80,896]{1,0:T(8,128)(2,1)S(1)}, bf16[80,896]{1,0:T(8,128)(2,1)S(1)}, u32[]{:S(2)}, u32[]{:S(2)}) collective-permute-start(bf16[80,896]{1,0:T(8,128)(2,1)S(1)} %convolution_convert_fusion.29), channel_id=1, source_target_pairs={{0,8},{8,0},{4,12},{12,4},{1,9},{9,1},{5,13},{13,5},{2,10},{10,2},... | collective-permute-start | bytes 430088 | tf_op jit(solution)/shard_map/ppermute | solution.py:33
  45.3 1.2 %constant_dynamic-update-slice_fusion.1 = bf16[4096,128]{1,0:T(8,128)(2,1)} fusion(bf16[4096,128]{1,0:T(8,128)(2,1)} %constant_dynamic-update-slice_fusion.2, bf16[1,128,128]{2,1,0:T(8,128)(2,1)S(1)} %copy-done.6, bf16[80,1152]{1,0:T(8,128)(2,1)S(1)} %collective-permute-done.12, bf16[128,1152]{1,0:T(8,128)(2,1)S(1)} %copy-done.7, ...), kind=kOutput, calls=%fused_computation.164 | convolution fusion | flops 115605504 | bytes 872448 | tf_op jit(solution)/shard_map/ct,cp->tp/dot_general | solution.py:232
  46.5 0.6 %slice.183 = bf16[1,1]{1,0:T(2,128)(2,1)} slice(bf16[8,64]{1,0:T(8,128)(2,1)S(1)} %max.11), slice={[0:1], [0:1]} | slice | bytes 4 | tf_op jit(solution)/shard_map/slice | solution.py:330
  48.0 2.5 %collective-permute-done.17 = bf16[80,1152]{1,0:T(8,128)(2,1)S(1)} collective-permute-done((bf16[80,1152]{1,0:T(8,128)(2,1)S(1)}, bf16[80,1152]{1,0:T(8,128)(2,1)S(1)}, u32[]{:S(2)}, u32[]{:S(2)}) %collective-permute-start.17) | collective-permute-done | bytes 184352 | tf_op jit(solution)/shard_map/ppermute | solution.py:33
  50.5 1.2 %constant_dynamic-update-slice_fusion = bf16[4096,128]{1,0:T(8,128)(2,1)} fusion(bf16[4096,128]{1,0:T(8,128)(2,1)} %constant_dynamic-update-slice_fusion.1, bf16[1,128,128]{2,1,0:T(8,128)(2,1)S(1)} %copy-done.6, bf16[80,1152]{1,0:T(8,128)(2,1)S(1)} %collective-permute-done.17, bf16[128,1152]{1,0:T(8,128)(2,1)S(1)} %copy-done.8, ...), kind=kOutput, calls=%fused_computation.163 | convolution fusion | flops 115605504 | bytes 872448 | tf_op jit(solution)/shard_map/ct,cp->tp/dot_general | solution.py:232
  51.7 0.4 collective-permute-done.18
  52.1 1.1 %fusion.20 = bf16[4096,128]{1,0:T(8,128)(2,1)} fusion(bf16[4096,128]{1,0:T(8,128)(2,1)} %constant_dynamic-update-slice_fusion, bf16[80,896]{1,0:T(8,128)(2,1)S(1)} %collective-permute-done.18, bf16[128,896]{1,0:T(8,128)(2,1)S(1)} %convolution_convert_fusion.21, bf16[2,128,256]{2,1,0:T(8,128)(2,1)S(1)} %get-tuple-element.76, ...), kind=kOutput, calls=%fused_computation.45 | convolution fusion | flops 89915392 | bytes 700416 | tf_op jit(solution)/shard_map/ct,cp->tp/dot_general | solution.py:232
  (64 shorter events, 4.4 us)
Async XLA Ops:
  0.0 4.6 %copy-start = (bf16[4096,128]{1,0:T(8,128)(2,1)S(1)}, bf16[4096,128]{1,0:T(8,128)(2,1)}, u32[]{:S(2)}) copy-start(bf16[4096,128]{1,0:T(8,128)(2,1)} %refs_1_.2) | copy-start | bytes 3145732
  0.0 4.6 %copy-start.2 = (bf16[1,128,128]{2,1,0:T(8,128)(2,1)S(1)}, bf16[1,128,128]{2,1,0:T(8,128)(2,1)}, u32[]{:S(2)}) copy-start(bf16[1,128,128]{2,1,0:T(8,128)(2,1)} %refs_0_.1) | copy-start | bytes 98308
  0.0 6.8 %copy-start.5 = (s32[1,3,64]{2,0,1:T(1,128)S(1)}, s32[1,3,64]{2,0,1:T(1,128)}, u32[]{:S(2)}) copy-start(s32[1,3,64]{2,0,1:T(1,128)} %param.9) | copy-start | bytes 2308
  0.0 6.8 %copy-start.4 = (bf16[1,3,64,128]{3,2,1,0:T(8,128)(2,1)S(1)}, bf16[1,3,64,128]{3,2,1,0:T(8,128)(2,1)}, u32[]{:S(2)}) copy-start(bf16[1,3,64,128]{3,2,1,0:T(8,128)(2,1)} %refs_1_.3) | copy-start | bytes 147460
  1.5 6.5 %collective-permute-start.3 = (bf16[128,256]{1,0:T(8,128)(2,1)S(1)}, bf16[128,256]{1,0:T(8,128)(2,1)S(1)}, u32[]{:S(2)}, u32[]{:S(2)}) collective-permute-start(bf16[128,256]{1,0:T(8,128)(2,1)S(1)} %get-tuple-element.63), channel_id=1, source_target_pairs={{0,2},{2,0},{1,3},{3,1},{4,6},{6,4},{5,7},{7,5},{8,10},{10,8},{9,1... | collective-permute-start | bytes 196616 | tf_op jit(solution)/shard_map/ppermute | solution.py:33
  4.5 7.1 %collective-permute-start.5 = (bf16[128,640]{1,0:T(8,128)(2,1)S(1)}, bf16[128,640]{1,0:T(8,128)(2,1)S(1)}, u32[]{:S(2)}, u32[]{:S(2)}) collective-permute-start(bf16[128,640]{1,0:T(8,128)(2,1)S(1)} %get-tuple-element.67), channel_id=1, source_target_pairs={{0,2},{2,0},{1,3},{3,1},{4,6},{6,4},{5,7},{7,5},{8,10},{10,8},{9,1... | collective-permute-start | bytes 491528 | tf_op jit(solution)/shard_map/ppermute | solution.py:33
  4.8 13.7 %collective-permute-start.7 = (bf16[128,1152]{1,0:T(8,128)(2,1)S(1)}, bf16[128,1152]{1,0:T(8,128)(2,1)S(1)}, u32[]{:S(2)}, u32[]{:S(2)}) collective-permute-start(bf16[128,1152]{1,0:T(8,128)(2,1)S(1)} %convolution_convert_fusion.14), channel_id=1, source_target_pairs={{0,2},{2,0},{1,3},{3,1},{4,6},{6,4},{5,7},{7,5},{8,10},{10,8},{9,1... | collective-permute-start | bytes 884744 | tf_op jit(solution)/shard_map/ppermute | solution.py:33
  8.2 5.6 %collective-permute-start.4 = (bf16[128,384]{1,0:T(8,128)(2,1)S(1)}, bf16[128,384]{1,0:T(8,128)(2,1)S(1)}, u32[]{:S(2)}, u32[]{:S(2)}) collective-permute-start(bf16[128,384]{1,0:T(8,128)(2,1)S(1)} %pad_maximum_fusion.12), channel_id=1, source_target_pairs={{0,4},{4,0},{8,12},{12,8},{1,5},{5,1},{9,13},{13,9},{2,6},{6,2},{1... | collective-permute-start | bytes 294920 | tf_op jit(solution)/shard_map/ppermute | solution.py:33
  11.8 9.9 %collective-permute-start.8 = (bf16[128,640]{1,0:T(8,128)(2,1)S(1)}, bf16[128,640]{1,0:T(8,128)(2,1)S(1)}, u32[]{:S(2)}, u32[]{:S(2)}) collective-permute-start(bf16[128,640]{1,0:T(8,128)(2,1)S(1)} %convolution_convert_fusion.26), channel_id=1, source_target_pairs={{0,4},{4,0},{8,12},{12,8},{1,5},{5,1},{9,13},{13,9},{2,6},{6,2},{1... | collective-permute-start | bytes 491528 | tf_op jit(solution)/shard_map/ppermute | solution.py:33
  14.0 12.2 %collective-permute-start.10 = (bf16[128,1152]{1,0:T(8,128)(2,1)S(1)}, bf16[128,1152]{1,0:T(8,128)(2,1)S(1)}, u32[]{:S(2)}, u32[]{:S(2)}) collective-permute-start(bf16[128,1152]{1,0:T(8,128)(2,1)S(1)} %convolution_convert_fusion.13), channel_id=1, source_target_pairs={{0,2},{2,0},{1,3},{3,1},{4,6},{6,4},{5,7},{7,5},{8,10},{10,8},{9,1... | collective-permute-start | bytes 884744 | tf_op jit(solution)/shard_map/ppermute | solution.py:33
  15.6 5.8 %collective-permute-start.6 = (bf16[128,384]{1,0:T(8,128)(2,1)S(1)}, bf16[128,384]{1,0:T(8,128)(2,1)S(1)}, u32[]{:S(2)}, u32[]{:S(2)}) collective-permute-start(bf16[128,384]{1,0:T(8,128)(2,1)S(1)} %pad_maximum_fusion.13), channel_id=1, source_target_pairs={{0,8},{8,0},{4,12},{12,4},{1,9},{9,1},{5,13},{13,5},{2,10},{10,2},... | collective-permute-start | bytes 294920 | tf_op jit(solution)/shard_map/ppermute | solution.py:33
  18.8 10.1 %collective-permute-start.9 = (bf16[88,1152]{1,0:T(8,128)(2,1)S(1)}, bf16[88,1152]{1,0:T(8,128)(2,1)S(1)}, u32[]{:S(2)}, u32[]{:S(2)}) collective-permute-start(bf16[88,1152]{1,0:T(8,128)(2,1)S(1)} %convolution_convert_fusion.16), channel_id=1, source_target_pairs={{0,4},{4,0},{8,12},{12,8},{1,5},{5,1},{9,13},{13,9},{2,6},{6,2},{1... | collective-permute-start | bytes 608264 | tf_op jit(solution)/shard_map/ppermute | solution.py:33
  21.5 8.0 %copy-start.3 = (bf16[128,384]{1,0:T(8,128)(2,1)}, bf16[128,384]{1,0:T(8,128)(2,1)S(1)}, u32[]{:S(2)}) copy-start(bf16[128,384]{1,0:T(8,128)(2,1)S(1)} %collective-permute-done.6) | copy-start | bytes 294916
  22.5 17.2 %collective-permute-start.15 = (bf16[80,640]{1,0:T(8,128)(2,1)S(1)}, bf16[80,640]{1,0:T(8,128)(2,1)S(1)}, u32[]{:S(2)}, u32[]{:S(2)}) collective-permute-start(bf16[80,640]{1,0:T(8,128)(2,1)S(1)} %convolution_convert_fusion.30), channel_id=1, source_target_pairs={{0,8},{8,0},{4,12},{12,4},{1,9},{9,1},{5,13},{13,5},{2,10},{10,2},... | collective-permute-start | bytes 307208 | tf_op jit(solution)/shard_map/ppermute | solution.py:33
  26.5 10.2 %collective-permute-start.16 = (bf16[88,1152]{1,0:T(8,128)(2,1)S(1)}, bf16[88,1152]{1,0:T(8,128)(2,1)S(1)}, u32[]{:S(2)}, u32[]{:S(2)}) collective-permute-start(bf16[88,1152]{1,0:T(8,128)(2,1)S(1)} %convolution_convert_fusion.15), channel_id=1, source_target_pairs={{0,4},{4,0},{8,12},{12,8},{1,5},{5,1},{9,13},{13,9},{2,6},{6,2},{1... | collective-permute-start | bytes 608264 | tf_op jit(solution)/shard_map/ppermute | solution.py:33
  29.1 16.2 %collective-permute-start.12 = (bf16[80,1152]{1,0:T(8,128)(2,1)S(1)}, bf16[80,1152]{1,0:T(8,128)(2,1)S(1)}, u32[]{:S(2)}, u32[]{:S(2)}) collective-permute-start(bf16[80,1152]{1,0:T(8,128)(2,1)S(1)} %convolution_convert_fusion.18), channel_id=1, source_target_pairs={{0,8},{8,0},{4,12},{12,4},{1,9},{9,1},{5,13},{13,5},{2,10},{10,2},... | collective-permute-start | bytes 552968 | tf_op jit(solution)/shard_map/ppermute | solution.py:33
  29.2 6.1 %collective-permute-start.13 = (bf16[128,896]{1,0:T(8,128)(2,1)S(1)}, bf16[128,896]{1,0:T(8,128)(2,1)S(1)}, u32[]{:S(2)}, u32[]{:S(2)}) collective-permute-start(bf16[128,896]{1,0:T(8,128)(2,1)S(1)} %convolution_convert_fusion.23), channel_id=1, source_target_pairs={{0,2},{2,0},{1,3},{3,1},{4,6},{6,4},{5,7},{7,5},{8,10},{10,8},{9,1... | collective-permute-start | bytes 688136 | tf_op jit(solution)/shard_map/ppermute | solution.py:33
  29.5 2.7 %slice-start = ((bf16[128,384]{1,0:T(8,128)(2,1)}), bf16[128,256]{1,0:T(8,128)(2,1)S(1)}, s32[]{:S(2)}) async-start(bf16[128,384]{1,0:T(8,128)(2,1)} %copy-done.3), calls=%async_computation | async-start | bytes 131072 | tf_op jit(solution)/shard_map/slice | solution.py:298
  29.5 2.7 %copy-start.6 = (bf16[1,128,128]{2,1,0:T(8,128)(2,1)S(1)}, bf16[1,128,128]{2,1,0:T(8,128)(2,1)}, u32[]{:S(2)}) copy-start(bf16[1,128,128]{2,1,0:T(8,128)(2,1)} %param.11) | copy-start | bytes 98308
  30.5 16.0 %collective-permute-start.11 = (bf16[8,64]{1,0:T(8,128)(2,1)S(1)}, bf16[8,64]{1,0:T(8,128)(2,1)S(1)}, u32[]{:S(2)}, u32[]{:S(2)}) collective-permute-start(bf16[8,64]{1,0:T(8,128)(2,1)S(1)} %slice_maximum_fusion), channel_id=1, source_target_pairs={{0,2},{2,0},{1,3},{3,1},{4,6},{6,4},{5,7},{7,5},{8,10},{10,8},{9,1... | collective-permute-start | bytes 3080 | tf_op jit(solution)/shard_map/ppermute | solution.py:33
  35.5 5.6 %collective-permute-start.14 = (bf16[88,896]{1,0:T(8,128)(2,1)S(1)}, bf16[88,896]{1,0:T(8,128)(2,1)S(1)}, u32[]{:S(2)}, u32[]{:S(2)}) collective-permute-start(bf16[88,896]{1,0:T(8,128)(2,1)S(1)} %convolution_convert_fusion.28), channel_id=1, source_target_pairs={{0,4},{4,0},{8,12},{12,8},{1,5},{5,1},{9,13},{13,9},{2,6},{6,2},{1... | collective-permute-start | bytes 473096 | tf_op jit(solution)/shard_map/ppermute | solution.py:33
  36.9 13.6 %collective-permute-start.17 = (bf16[80,1152]{1,0:T(8,128)(2,1)S(1)}, bf16[80,1152]{1,0:T(8,128)(2,1)S(1)}, u32[]{:S(2)}, u32[]{:S(2)}) collective-permute-start(bf16[80,1152]{1,0:T(8,128)(2,1)S(1)} %convolution_convert_fusion.17), channel_id=1, source_target_pairs={{0,8},{8,0},{4,12},{12,4},{1,9},{9,1},{5,13},{13,5},{2,10},{10,2},... | collective-permute-start | bytes 552968 | tf_op jit(solution)/shard_map/ppermute | solution.py:33
  41.0 4.2 %copy-start.7 = (bf16[128,1152]{1,0:T(8,128)(2,1)S(1)}, bf16[128,1152]{1,0:T(8,128)(2,1)}, u32[]{:S(2)}) copy-start(bf16[128,1152]{1,0:T(8,128)(2,1)} %convolution_convert_fusion.11) | copy-start | bytes 884740
  41.3 10.9 %collective-permute-start.18 = (bf16[80,896]{1,0:T(8,128)(2,1)S(1)}, bf16[80,896]{1,0:T(8,128)(2,1)S(1)}, u32[]{:S(2)}, u32[]{:S(2)}) collective-permute-start(bf16[80,896]{1,0:T(8,128)(2,1)S(1)} %convolution_convert_fusion.29), channel_id=1, source_target_pairs={{0,8},{8,0},{4,12},{12,4},{1,9},{9,1},{5,13},{13,5},{2,10},{10,2},... | collective-permute-start | bytes 430088 | tf_op jit(solution)/shard_map/ppermute | solution.py:33
  46.5 4.0 %copy-start.8 = (bf16[128,1152]{1,0:T(8,128)(2,1)S(1)}, bf16[128,1152]{1,0:T(8,128)(2,1)}, u32[]{:S(2)}) copy-start(bf16[128,1152]{1,0:T(8,128)(2,1)} %convolution_convert_fusion.7) | copy-start | bytes 884740

commit v20 on v19

--- a/solution.py
+++ b/solution.py
@@ -11,8 +11,9 @@
 COUNT_PIECE = 2
 COUNT_READ = 2
 LOOK = (3, -1)
+MAKE = (0, -1)
 ORDER = (
-    (0, 0), (0, 1), (0, 2), (1, 0), (1, 1), (0, 3), (2, 0), (1, 2), LOOK, (2, 1), (1, 3), (2, 2),
+    (0, 0), (0, 1), (0, 2), (1, 0), (1, 1), MAKE, (2, 0), (0, 3), (1, 2), LOOK, (2, 1), (1, 3), (2, 2),
     (0, 4), (3, 0), (1, 4), (2, 3), (3, 1), (2, 4), (3, 2), (3, 3), (3, 4),
 )
 KERNEL_VMEM = 16 * 1024 * 1024
@@ -277,6 +278,11 @@
     inputs, partners, theirs, done = {}, {}, {}, [None] * pieces
     previous, finished, known = None, None, None
     for level, piece in ORDER:
+        if (level, piece) == MAKE:
+            waiting = after(sampling, previous)
+            coeffs.append(sampled(waiting, traces[starts[pieces - 2] : starts[pieces - 1]]))
+            previous = coeffs[-1]
+            continue
         if (level, piece) == LOOK:
             known = after(after(partners[0], previous), partners[1])[:, starts[1] :]
             theirs[levels - 1] = known[: rooms[levels - 1 - wide], :rank]
@@ -285,9 +291,10 @@
         if level == 0:
             if piece == len(coeffs):
                 waiting = after(sampling, previous)
-                for late in (piece, piece + 1) if piece == pieces - 2 else (piece,):
-                    coeffs.append(sampled(waiting, traces[starts[late] : starts[late + 1]]))
+                coeffs.append(sampled(waiting, traces[starts[piece] : starts[piece + 1]]))
             own = coeffs[piece]
+            if piece == pieces - 2:
+                coeffs.append(sampled(waiting, traces[starts[piece + 1] : starts[piece + 2]]))
         else:
             arrived = after(partners[piece], previous)
             if level == levels:
@@ -311,7 +318,7 @@
                 most = jnp.maximum(most, after(counted, finished))
             continue
         if level == 0:
-            outgoing = after(own, previous) if piece == pieces - 1 else own
+            outgoing = after(own, previous) if piece >= pieces - 2 else own
         if piece == 0 and level >= wide:
             block = extra[level - wide]
             if known is not None:

time: 53.4 us -> 52.5 us (0.983)
  starting transfers between devices: 28.8 us -> 22.9 us
  waiting for transfers between devices: 7.86 us -> 12.9 us
    ppermute x16, starting transfers between devices: 28.8 us -> 22.9 us  [from_partner(): return lax.ppermute(block, hop[0], route(*hop))]
    ppermute x16, waiting for transfers between devices: 7.86 us -> 12.9 us  [from_partner(): return lax.ppermute(block, hop[0], route(*hop))]
  transfers between devices with their start and end apart: 16 -> 16, of which waited for: 5 -> 7; matrix products, arithmetic and copies ran while one was open for 22% -> 23% of each run, Pallas kernels for 2% -> 2%
where the time goes in v20:
time: 52.5 us; the launch traced here: 52.3 us
  starting transfers between devices  22.9 us (44%)
  waiting for transfers between devices  12.9 us (25%)
  matrix products  12.3 us (23%)
  Pallas kernels  2.51 us (5%)
  between operations  0.98 us (2%)
  local copies, waits for them, and re-layouts  0.65 us (1%)
    ppermute x16, starting transfers between devices, from_partner(): return lax.ppermute(block, hop[0], route(*hop))  22.9 us
    ppermute x16, waiting for transfers between devices, from_partner(): return lax.ppermute(block, hop[0], route(*hop))  12.9 us
    dot_general x5, matrix products, evaluated(): jnp.einsum('ct,cp->tp', coeffs, evaluation, preferred_element_type=jnp.fl...  5.62 us
    dot_general x17, matrix products, times(): jnp.dot(matrix, value, preferred_element_type=jnp.float32)  5.17 us
    pallas_call x1, Pallas kernels, early(): pl.pallas_call(lambda *refs: early_kernel(starts, *refs), out_shape=[jax....  1.45 us
    pallas_call x1, Pallas kernels, tables(): pl.pallas_call(lambda *refs: tables_kernel(wide, rooms, *refs), out_shape...  1.06 us
  transfers between devices with their start and end apart: 16, of which 7 were waited for; matrix products, arithmetic and copies ran while one was open for 23% of the time, Pallas kernels for 2%

profile of v20, /device:TPU:0, one launch (start us, length us, event | category | flops | bytes accessed | tf_op | source)
XLA Modules:
  0.0 52.3 jit_solution(9885335178594628948)
XLA Ops:
  0.0 1.4 %early.1 = (bf16[128,256]{1,0:T(8,128)(2,1)S(1)}, bf16[128,640]{1,0:T(8,128)(2,1)S(1)}) custom-call(bf16[1,128,128]{2,1,0:T(8,128)(2,1)} %refs_0_.1, bf16[4096,128]{1,0:T(8,128)(2,1)} %refs_1_.2), custom_call_target="tpu_custom_call" | custom-call | flops 29360128 | bytes 458752 | tf_op jit(solution)/shard_map/early/pallas_call | solution.py:70
  1.5 3.0 %collective-permute-start.3 = (bf16[128,256]{1,0:T(8,128)(2,1)S(1)}, bf16[128,256]{1,0:T(8,128)(2,1)S(1)}, u32[]{:S(2)}, u32[]{:S(2)}) collective-permute-start(bf16[128,256]{1,0:T(8,128)(2,1)S(1)} %get-tuple-element.64), channel_id=1, source_target_pairs={{0,2},{2,0},{1,3},{3,1},{4,6},{6,4},{5,7},{7,5},{8,10},{10,8},{9,1... | collective-permute-start | bytes 196616 | tf_op jit(solution)/shard_map/ppermute | solution.py:34
  4.6 0.3 convolution_convert_fusion.14
  4.8 2.0 %collective-permute-start.7 = (bf16[128,1152]{1,0:T(8,128)(2,1)S(1)}, bf16[128,1152]{1,0:T(8,128)(2,1)S(1)}, u32[]{:S(2)}, u32[]{:S(2)}) collective-permute-start(bf16[128,1152]{1,0:T(8,128)(2,1)S(1)} %convolution_convert_fusion.14), channel_id=1, source_target_pairs={{0,2},{2,0},{1,3},{3,1},{4,6},{6,4},{5,7},{7,5},{8,10},{10,8},{9,1... | collective-permute-start | bytes 884744 | tf_op jit(solution)/shard_map/ppermute | solution.py:34
  6.8 1.1 %tables.1 = (bf16[3,128,256]{2,1,0:T(8,128)(2,1)S(1)}, bf16[2,128,256]{2,1,0:T(8,128)(2,1)S(1)}, bf16[2,128,128]{2,1,0:T(8,128)(2,1)S(1)}) custom-call(s32[3,1,64]{2,1,0:T(1,128)S(1)} %bitcast.111, bf16[1,3,64,128]{3,2,1,0:T(8,128)(2,1)S(1)} %copy-done.4), custom_call_target="tpu_custom_call" | custom-call | flops 50000000 | bytes 600000 | tf_op jit(solution)/shard_map/tables/pallas_call | solution.py:156
  8.2 1.6 %collective-permute-start.4 = (bf16[128,384]{1,0:T(8,128)(2,1)S(1)}, bf16[128,384]{1,0:T(8,128)(2,1)S(1)}, u32[]{:S(2)}, u32[]{:S(2)}) collective-permute-start(bf16[128,384]{1,0:T(8,128)(2,1)S(1)} %pad_maximum_fusion.12), channel_id=1, source_target_pairs={{0,4},{4,0},{8,12},{12,8},{1,5},{5,1},{9,13},{13,9},{2,6},{6,2},{1... | collective-permute-start | bytes 294920 | tf_op jit(solution)/shard_map/ppermute | solution.py:34
  9.8 1.8 %collective-permute-done.5 = bf16[128,640]{1,0:T(8,128)(2,1)S(1)} collective-permute-done((bf16[128,640]{1,0:T(8,128)(2,1)S(1)}, bf16[128,640]{1,0:T(8,128)(2,1)S(1)}, u32[]{:S(2)}, u32[]{:S(2)}) %collective-permute-start.5) | collective-permute-done | bytes 163872 | tf_op jit(solution)/shard_map/ppermute | solution.py:34
  11.8 1.6 %collective-permute-start.8 = (bf16[128,640]{1,0:T(8,128)(2,1)S(1)}, bf16[128,640]{1,0:T(8,128)(2,1)S(1)}, u32[]{:S(2)}, u32[]{:S(2)}) collective-permute-start(bf16[128,640]{1,0:T(8,128)(2,1)S(1)} %convolution_convert_fusion.26), channel_id=1, source_target_pairs={{0,4},{4,0},{8,12},{12,8},{1,5},{5,1},{9,13},{13,9},{2,6},{6,2},{1... | collective-permute-start | bytes 491528 | tf_op jit(solution)/shard_map/ppermute | solution.py:34
  14.2 2.7 %collective-permute-start.6 = (bf16[128,384]{1,0:T(8,128)(2,1)S(1)}, bf16[128,384]{1,0:T(8,128)(2,1)S(1)}, u32[]{:S(2)}, u32[]{:S(2)}) collective-permute-start(bf16[128,384]{1,0:T(8,128)(2,1)S(1)} %pad_maximum_fusion.13), channel_id=1, source_target_pairs={{0,8},{8,0},{4,12},{12,4},{1,9},{9,1},{5,13},{13,5},{2,10},{10,2},... | collective-permute-start | bytes 294920 | tf_op jit(solution)/shard_map/ppermute | solution.py:34
  16.9 1.4 %collective-permute-start.10 = (bf16[128,1152]{1,0:T(8,128)(2,1)S(1)}, bf16[128,1152]{1,0:T(8,128)(2,1)S(1)}, u32[]{:S(2)}, u32[]{:S(2)}) collective-permute-start(bf16[128,1152]{1,0:T(8,128)(2,1)S(1)} %convolution_convert_fusion.13), channel_id=1, source_target_pairs={{0,2},{2,0},{1,3},{3,1},{4,6},{6,4},{5,7},{7,5},{8,10},{10,8},{9,1... | collective-permute-start | bytes 884744 | tf_op jit(solution)/shard_map/ppermute | solution.py:34
  18.7 1.6 %collective-permute-start.9 = (bf16[88,1152]{1,0:T(8,128)(2,1)S(1)}, bf16[88,1152]{1,0:T(8,128)(2,1)S(1)}, u32[]{:S(2)}, u32[]{:S(2)}) collective-permute-start(bf16[88,1152]{1,0:T(8,128)(2,1)S(1)} %convolution_convert_fusion.16), channel_id=1, source_target_pairs={{0,4},{4,0},{8,12},{12,8},{1,5},{5,1},{9,13},{13,9},{2,6},{6,2},{1... | collective-permute-start | bytes 608264 | tf_op jit(solution)/shard_map/ppermute | solution.py:34
  20.3 0.6 %collective-permute-done.6 = bf16[128,384]{1,0:T(8,128)(2,1)S(1)} collective-permute-done((bf16[128,384]{1,0:T(8,128)(2,1)S(1)}, bf16[128,384]{1,0:T(8,128)(2,1)S(1)}, u32[]{:S(2)}, u32[]{:S(2)}) %collective-permute-start.6) | collective-permute-done | bytes 98336 | tf_op jit(solution)/shard_map/ppermute | solution.py:34
  21.9 2.2 %collective-permute-start.15 = (bf16[80,640]{1,0:T(8,128)(2,1)S(1)}, bf16[80,640]{1,0:T(8,128)(2,1)S(1)}, u32[]{:S(2)}, u32[]{:S(2)}) collective-permute-start(bf16[80,640]{1,0:T(8,128)(2,1)S(1)} %convolution_convert_fusion.30), channel_id=1, source_target_pairs={{0,8},{8,0},{4,12},{12,4},{1,9},{9,1},{5,13},{13,5},{2,10},{10,2},... | collective-permute-start | bytes 307208 | tf_op jit(solution)/shard_map/ppermute | solution.py:34
  24.7 0.6 %collective-permute-start.16 = (bf16[88,1152]{1,0:T(8,128)(2,1)S(1)}, bf16[88,1152]{1,0:T(8,128)(2,1)S(1)}, u32[]{:S(2)}, u32[]{:S(2)}) collective-permute-start(bf16[88,1152]{1,0:T(8,128)(2,1)S(1)} %convolution_convert_fusion.15), channel_id=1, source_target_pairs={{0,4},{4,0},{8,12},{12,8},{1,5},{5,1},{9,13},{13,9},{2,6},{6,2},{1... | collective-permute-start | bytes 608264 | tf_op jit(solution)/shard_map/ppermute | solution.py:34
  25.6 1.4 %collective-permute-done.9 = bf16[88,1152]{1,0:T(8,128)(2,1)S(1)} collective-permute-done((bf16[88,1152]{1,0:T(8,128)(2,1)S(1)}, bf16[88,1152]{1,0:T(8,128)(2,1)S(1)}, u32[]{:S(2)}, u32[]{:S(2)}) %collective-permute-start.9) | collective-permute-done | bytes 202784 | tf_op jit(solution)/shard_map/ppermute | solution.py:34
  27.2 1.2 %collective-permute-start.12 = (bf16[80,1152]{1,0:T(8,128)(2,1)S(1)}, bf16[80,1152]{1,0:T(8,128)(2,1)S(1)}, u32[]{:S(2)}, u32[]{:S(2)}) collective-permute-start(bf16[80,1152]{1,0:T(8,128)(2,1)S(1)} %convolution_convert_fusion.18), channel_id=1, source_target_pairs={{0,8},{8,0},{4,12},{12,4},{1,9},{9,1},{5,13},{13,5},{2,10},{10,2},... | collective-permute-start | bytes 552968 | tf_op jit(solution)/shard_map/ppermute | solution.py:34
  28.4 1.1 %collective-permute-start.13 = (bf16[128,896]{1,0:T(8,128)(2,1)S(1)}, bf16[128,896]{1,0:T(8,128)(2,1)S(1)}, u32[]{:S(2)}, u32[]{:S(2)}) collective-permute-start(bf16[128,896]{1,0:T(8,128)(2,1)S(1)} %convolution_convert_fusion.23), channel_id=1, source_target_pairs={{0,2},{2,0},{1,3},{3,1},{4,6},{6,4},{5,7},{7,5},{8,10},{10,8},{9,1... | collective-permute-start | bytes 688136 | tf_op jit(solution)/shard_map/ppermute | solution.py:34
  29.5 1.0 %convolution_convert_fusion.11 = bf16[128,1152]{1,0:T(8,128)(2,1)} fusion(bf16[128,256]{1,0:T(8,128)(2,1)S(1)} %slice_bitcast_fusion.7, bf16[88,1152]{1,0:T(8,128)(2,1)S(1)} %collective-permute-done.9, bf16[128,1152]{1,0:T(8,128)(2,1)S(1)} %convolution_convert_fusion.12), kind=kOutput, calls=%fused_computation.36 | convolution fusion | flops 77709312 | bytes 858112 | tf_op jit(solution)/shard_map/dot_general | solution.py:223
  30.5 1.0 %collective-permute-start.11 = (bf16[8,64]{1,0:T(8,128)(2,1)S(1)}, bf16[8,64]{1,0:T(8,128)(2,1)S(1)}, u32[]{:S(2)}, u32[]{:S(2)}) collective-permute-start(bf16[8,64]{1,0:T(8,128)(2,1)S(1)} %slice_maximum_fusion), channel_id=1, source_target_pairs={{0,2},{2,0},{1,3},{3,1},{4,6},{6,4},{5,7},{7,5},{8,10},{10,8},{9,1... | collective-permute-start | bytes 3080 | tf_op jit(solution)/shard_map/ppermute | solution.py:34
  31.4 1.0 %constant_dynamic-update-slice_fusion.3 = bf16[4096,128]{1,0:T(8,128)(2,1)} fusion(bf16[1,128,128]{2,1,0:T(8,128)(2,1)S(1)} %copy-done.6, bf16[128,256]{1,0:T(8,128)(2,1)S(1)} %slice-done, bf16[128,256]{1,0:T(8,128)(2,1)S(1)} %convolution_convert_fusion.33, bf16[3,128,256]{2,1,0:T(8,128)(2,1)S(1)} %get-tuple-element.67), kind=kOutput, calls=%fused_computation.166 | convolution fusion | flops 25493504 | bytes 294912 | tf_op jit(solution)/shard_map/ct,cp->tp/dot_general | solution.py:233
  32.4 2.2 %collective-permute-done.13 = bf16[128,896]{1,0:T(8,128)(2,1)S(1)} collective-permute-done((bf16[128,896]{1,0:T(8,128)(2,1)S(1)}, bf16[128,896]{1,0:T(8,128)(2,1)S(1)}, u32[]{:S(2)}, u32[]{:S(2)}) %collective-permute-start.13) | collective-permute-done | bytes 229408 | tf_op jit(solution)/shard_map/ppermute | solution.py:34
  34.9 0.7 %collective-permute-start.14 = (bf16[88,896]{1,0:T(8,128)(2,1)S(1)}, bf16[88,896]{1,0:T(8,128)(2,1)S(1)}, u32[]{:S(2)}, u32[]{:S(2)}) collective-permute-start(bf16[88,896]{1,0:T(8,128)(2,1)S(1)} %convolution_convert_fusion.28), channel_id=1, source_target_pairs={{0,4},{4,0},{8,12},{12,8},{1,5},{5,1},{9,13},{13,9},{2,6},{6,2},{1... | collective-permute-start | bytes 473096 | tf_op jit(solution)/shard_map/ppermute | solution.py:34
  35.9 1.9 %collective-permute-start.17 = (bf16[80,1152]{1,0:T(8,128)(2,1)S(1)}, bf16[80,1152]{1,0:T(8,128)(2,1)S(1)}, u32[]{:S(2)}, u32[]{:S(2)}) collective-permute-start(bf16[80,1152]{1,0:T(8,128)(2,1)S(1)} %convolution_convert_fusion.17), channel_id=1, source_target_pairs={{0,8},{8,0},{4,12},{12,4},{1,9},{9,1},{5,13},{13,5},{2,10},{10,2},... | collective-permute-start | bytes 552968 | tf_op jit(solution)/shard_map/ppermute | solution.py:34
  37.8 1.0 %convolution_convert_fusion.7 = bf16[128,1152]{1,0:T(8,128)(2,1)} fusion(bf16[128,256]{1,0:T(8,128)(2,1)S(1)} %slice_bitcast_fusion.7, bf16[88,1152]{1,0:T(8,128)(2,1)S(1)} %collective-permute-done.16, bf16[128,1152]{1,0:T(8,128)(2,1)S(1)} %convolution_convert_fusion.10), kind=kOutput, calls=%fused_computation.32 | convolution fusion | flops 77709312 | bytes 858112 | tf_op jit(solution)/shard_map/dot_general | solution.py:223
  38.8 1.1 %constant_dynamic-update-slice_fusion.2 = bf16[4096,128]{1,0:T(8,128)(2,1)} fusion(bf16[4096,128]{1,0:T(8,128)(2,1)} %constant_dynamic-update-slice_fusion.3, bf16[1,128,128]{2,1,0:T(8,128)(2,1)S(1)} %copy-done.6, bf16[80,640]{1,0:T(8,128)(2,1)S(1)} %collective-permute-done.15, bf16[128,640]{1,0:T(8,128)(2,1)S(1)} %convolution_convert_fusion.25, ...), kind=kOutput, calls=%fused_computation.165 | convolution fusion | flops 64225280 | bytes 528384 | tf_op jit(solution)/shard_map/ct,cp->tp/dot_general | solution.py:233
  40.1 2.0 %collective-permute-done.14 = bf16[88,896]{1,0:T(8,128)(2,1)S(1)} collective-permute-done((bf16[88,896]{1,0:T(8,128)(2,1)S(1)}, bf16[88,896]{1,0:T(8,128)(2,1)S(1)}, u32[]{:S(2)}, u32[]{:S(2)}) %collective-permute-start.14) | collective-permute-done | bytes 157728 | tf_op jit(solution)/shard_map/ppermute | solution.py:34
  42.4 1.2 %constant_dynamic-update-slice_fusion.1 = bf16[4096,128]{1,0:T(8,128)(2,1)} fusion(bf16[4096,128]{1,0:T(8,128)(2,1)} %constant_dynamic-update-slice_fusion.2, bf16[1,128,128]{2,1,0:T(8,128)(2,1)S(1)} %copy-done.6, bf16[80,1152]{1,0:T(8,128)(2,1)S(1)} %collective-permute-done.12, bf16[128,1152]{1,0:T(8,128)(2,1)S(1)} %copy-done.7, ...), kind=kOutput, calls=%fused_computation.164 | convolution fusion | flops 115605504 | bytes 872448 | tf_op jit(solution)/shard_map/ct,cp->tp/dot_general | solution.py:233
  43.6 0.6 %slice.183 = bf16[1,1]{1,0:T(2,128)(2,1)} slice(bf16[8,64]{1,0:T(8,128)(2,1)S(1)} %max.11), slice={[0:1], [0:1]} | slice | bytes 4 | tf_op jit(solution)/shard_map/slice | solution.py:337
  45.1 4.4 %collective-permute-done.17 = bf16[80,1152]{1,0:T(8,128)(2,1)S(1)} collective-permute-done((bf16[80,1152]{1,0:T(8,128)(2,1)S(1)}, bf16[80,1152]{1,0:T(8,128)(2,1)S(1)}, u32[]{:S(2)}, u32[]{:S(2)}) %collective-permute-start.17) | collective-permute-done | bytes 184352 | tf_op jit(solution)/shard_map/ppermute | solution.py:34
  49.5 1.2 %constant_dynamic-update-slice_fusion = bf16[4096,128]{1,0:T(8,128)(2,1)} fusion(bf16[4096,128]{1,0:T(8,128)(2,1)} %constant_dynamic-update-slice_fusion.1, bf16[1,128,128]{2,1,0:T(8,128)(2,1)S(1)} %copy-done.6, bf16[80,1152]{1,0:T(8,128)(2,1)S(1)} %collective-permute-done.17, bf16[128,1152]{1,0:T(8,128)(2,1)S(1)} %copy-done.8, ...), kind=kOutput, calls=%fused_computation.163 | convolution fusion | flops 115605504 | bytes 872448 | tf_op jit(solution)/shard_map/ct,cp->tp/dot_general | solution.py:233
  50.7 0.5 collective-permute-done.18
  51.2 1.1 %fusion.20 = bf16[4096,128]{1,0:T(8,128)(2,1)} fusion(bf16[4096,128]{1,0:T(8,128)(2,1)} %constant_dynamic-update-slice_fusion, bf16[80,896]{1,0:T(8,128)(2,1)S(1)} %collective-permute-done.18, bf16[128,896]{1,0:T(8,128)(2,1)S(1)} %convolution_convert_fusion.21, bf16[2,128,256]{2,1,0:T(8,128)(2,1)S(1)} %get-tuple-element.78, ...), kind=kOutput, calls=%fused_computation.45 | convolution fusion | flops 89915392 | bytes 700416 | tf_op jit(solution)/shard_map/ct,cp->tp/dot_general | solution.py:233
  (64 shorter events, 4.9 us)
Async XLA Ops:
  0.0 4.6 %copy-start = (bf16[4096,128]{1,0:T(8,128)(2,1)S(1)}, bf16[4096,128]{1,0:T(8,128)(2,1)}, u32[]{:S(2)}) copy-start(bf16[4096,128]{1,0:T(8,128)(2,1)} %refs_1_.2) | copy-start | bytes 3145732
  0.0 4.6 %copy-start.2 = (bf16[1,128,128]{2,1,0:T(8,128)(2,1)S(1)}, bf16[1,128,128]{2,1,0:T(8,128)(2,1)}, u32[]{:S(2)}) copy-start(bf16[1,128,128]{2,1,0:T(8,128)(2,1)} %refs_0_.1) | copy-start | bytes 98308
  0.0 6.8 %copy-start.5 = (s32[1,3,64]{2,0,1:T(1,128)S(1)}, s32[1,3,64]{2,0,1:T(1,128)}, u32[]{:S(2)}) copy-start(s32[1,3,64]{2,0,1:T(1,128)} %param.9) | copy-start | bytes 2308
  0.0 6.8 %copy-start.4 = (bf16[1,3,64,128]{3,2,1,0:T(8,128)(2,1)S(1)}, bf16[1,3,64,128]{3,2,1,0:T(8,128)(2,1)}, u32[]{:S(2)}) copy-start(bf16[1,3,64,128]{3,2,1,0:T(8,128)(2,1)} %refs_1_.3) | copy-start | bytes 147460
  1.5 6.5 %collective-permute-start.3 = (bf16[128,256]{1,0:T(8,128)(2,1)S(1)}, bf16[128,256]{1,0:T(8,128)(2,1)S(1)}, u32[]{:S(2)}, u32[]{:S(2)}) collective-permute-start(bf16[128,256]{1,0:T(8,128)(2,1)S(1)} %get-tuple-element.64), channel_id=1, source_target_pairs={{0,2},{2,0},{1,3},{3,1},{4,6},{6,4},{5,7},{7,5},{8,10},{10,8},{9,1... | collective-permute-start | bytes 196616 | tf_op jit(solution)/shard_map/ppermute | solution.py:34
  4.5 7.1 %collective-permute-start.5 = (bf16[128,640]{1,0:T(8,128)(2,1)S(1)}, bf16[128,640]{1,0:T(8,128)(2,1)S(1)}, u32[]{:S(2)}, u32[]{:S(2)}) collective-permute-start(bf16[128,640]{1,0:T(8,128)(2,1)S(1)} %get-tuple-element.68), channel_id=1, source_target_pairs={{0,2},{2,0},{1,3},{3,1},{4,6},{6,4},{5,7},{7,5},{8,10},{10,8},{9,1... | collective-permute-start | bytes 491528 | tf_op jit(solution)/shard_map/ppermute | solution.py:34
  4.8 13.7 %collective-permute-start.7 = (bf16[128,1152]{1,0:T(8,128)(2,1)S(1)}, bf16[128,1152]{1,0:T(8,128)(2,1)S(1)}, u32[]{:S(2)}, u32[]{:S(2)}) collective-permute-start(bf16[128,1152]{1,0:T(8,128)(2,1)S(1)} %convolution_convert_fusion.14), channel_id=1, source_target_pairs={{0,2},{2,0},{1,3},{3,1},{4,6},{6,4},{5,7},{7,5},{8,10},{10,8},{9,1... | collective-permute-start | bytes 884744 | tf_op jit(solution)/shard_map/ppermute | solution.py:34
  8.2 5.6 %collective-permute-start.4 = (bf16[128,384]{1,0:T(8,128)(2,1)S(1)}, bf16[128,384]{1,0:T(8,128)(2,1)S(1)}, u32[]{:S(2)}, u32[]{:S(2)}) collective-permute-start(bf16[128,384]{1,0:T(8,128)(2,1)S(1)} %pad_maximum_fusion.12), channel_id=1, source_target_pairs={{0,4},{4,0},{8,12},{12,8},{1,5},{5,1},{9,13},{13,9},{2,6},{6,2},{1... | collective-permute-start | bytes 294920 | tf_op jit(solution)/shard_map/ppermute | solution.py:34
  11.8 9.4 %collective-permute-start.8 = (bf16[128,640]{1,0:T(8,128)(2,1)S(1)}, bf16[128,640]{1,0:T(8,128)(2,1)S(1)}, u32[]{:S(2)}, u32[]{:S(2)}) collective-permute-start(bf16[128,640]{1,0:T(8,128)(2,1)S(1)} %convolution_convert_fusion.26), channel_id=1, source_target_pairs={{0,4},{4,0},{8,12},{12,8},{1,5},{5,1},{9,13},{13,9},{2,6},{6,2},{1... | collective-permute-start | bytes 491528 | tf_op jit(solution)/shard_map/ppermute | solution.py:34
  14.2 6.7 %collective-permute-start.6 = (bf16[128,384]{1,0:T(8,128)(2,1)S(1)}, bf16[128,384]{1,0:T(8,128)(2,1)S(1)}, u32[]{:S(2)}, u32[]{:S(2)}) collective-permute-start(bf16[128,384]{1,0:T(8,128)(2,1)S(1)} %pad_maximum_fusion.13), channel_id=1, source_target_pairs={{0,8},{8,0},{4,12},{12,4},{1,9},{9,1},{5,13},{13,5},{2,10},{10,2},... | collective-permute-start | bytes 294920 | tf_op jit(solution)/shard_map/ppermute | solution.py:34
  16.9 7.6 %collective-permute-start.10 = (bf16[128,1152]{1,0:T(8,128)(2,1)S(1)}, bf16[128,1152]{1,0:T(8,128)(2,1)S(1)}, u32[]{:S(2)}, u32[]{:S(2)}) collective-permute-start(bf16[128,1152]{1,0:T(8,128)(2,1)S(1)} %convolution_convert_fusion.13), channel_id=1, source_target_pairs={{0,2},{2,0},{1,3},{3,1},{4,6},{6,4},{5,7},{7,5},{8,10},{10,8},{9,1... | collective-permute-start | bytes 884744 | tf_op jit(solution)/shard_map/ppermute | solution.py:34
  18.7 8.2 %collective-permute-start.9 = (bf16[88,1152]{1,0:T(8,128)(2,1)S(1)}, bf16[88,1152]{1,0:T(8,128)(2,1)S(1)}, u32[]{:S(2)}, u32[]{:S(2)}) collective-permute-start(bf16[88,1152]{1,0:T(8,128)(2,1)S(1)} %convolution_convert_fusion.16), channel_id=1, source_target_pairs={{0,4},{4,0},{8,12},{12,8},{1,5},{5,1},{9,13},{13,9},{2,6},{6,2},{1... | collective-permute-start | bytes 608264 | tf_op jit(solution)/shard_map/ppermute | solution.py:34
  20.9 8.6 %copy-start.3 = (bf16[128,384]{1,0:T(8,128)(2,1)}, bf16[128,384]{1,0:T(8,128)(2,1)S(1)}, u32[]{:S(2)}) copy-start(bf16[128,384]{1,0:T(8,128)(2,1)S(1)} %collective-permute-done.6) | copy-start | bytes 294916
  21.9 16.8 %collective-permute-start.15 = (bf16[80,640]{1,0:T(8,128)(2,1)S(1)}, bf16[80,640]{1,0:T(8,128)(2,1)S(1)}, u32[]{:S(2)}, u32[]{:S(2)}) collective-permute-start(bf16[80,640]{1,0:T(8,128)(2,1)S(1)} %convolution_convert_fusion.30), channel_id=1, source_target_pairs={{0,8},{8,0},{4,12},{12,4},{1,9},{9,1},{5,13},{13,5},{2,10},{10,2},... | collective-permute-start | bytes 307208 | tf_op jit(solution)/shard_map/ppermute | solution.py:34
  24.7 10.9 %collective-permute-start.16 = (bf16[88,1152]{1,0:T(8,128)(2,1)S(1)}, bf16[88,1152]{1,0:T(8,128)(2,1)S(1)}, u32[]{:S(2)}, u32[]{:S(2)}) collective-permute-start(bf16[88,1152]{1,0:T(8,128)(2,1)S(1)} %convolution_convert_fusion.15), channel_id=1, source_target_pairs={{0,4},{4,0},{8,12},{12,8},{1,5},{5,1},{9,13},{13,9},{2,6},{6,2},{1... | collective-permute-start | bytes 608264 | tf_op jit(solution)/shard_map/ppermute | solution.py:34
  27.2 15.2 %collective-permute-start.12 = (bf16[80,1152]{1,0:T(8,128)(2,1)S(1)}, bf16[80,1152]{1,0:T(8,128)(2,1)S(1)}, u32[]{:S(2)}, u32[]{:S(2)}) collective-permute-start(bf16[80,1152]{1,0:T(8,128)(2,1)S(1)} %convolution_convert_fusion.18), channel_id=1, source_target_pairs={{0,8},{8,0},{4,12},{12,4},{1,9},{9,1},{5,13},{13,5},{2,10},{10,2},... | collective-permute-start | bytes 552968 | tf_op jit(solution)/shard_map/ppermute | solution.py:34
  28.4 6.2 %collective-permute-start.13 = (bf16[128,896]{1,0:T(8,128)(2,1)S(1)}, bf16[128,896]{1,0:T(8,128)(2,1)S(1)}, u32[]{:S(2)}, u32[]{:S(2)}) collective-permute-start(bf16[128,896]{1,0:T(8,128)(2,1)S(1)} %convolution_convert_fusion.23), channel_id=1, source_target_pairs={{0,2},{2,0},{1,3},{3,1},{4,6},{6,4},{5,7},{7,5},{8,10},{10,8},{9,1... | collective-permute-start | bytes 688136 | tf_op jit(solution)/shard_map/ppermute | solution.py:34
  29.5 1.9 %slice-start = ((bf16[128,384]{1,0:T(8,128)(2,1)}), bf16[128,256]{1,0:T(8,128)(2,1)S(1)}, s32[]{:S(2)}) async-start(bf16[128,384]{1,0:T(8,128)(2,1)} %copy-done.3), calls=%async_computation | async-start | bytes 131072 | tf_op jit(solution)/shard_map/slice | solution.py:305
  29.5 1.9 %copy-start.6 = (bf16[1,128,128]{2,1,0:T(8,128)(2,1)S(1)}, bf16[1,128,128]{2,1,0:T(8,128)(2,1)}, u32[]{:S(2)}) copy-start(bf16[1,128,128]{2,1,0:T(8,128)(2,1)} %param.11) | copy-start | bytes 98308
  30.5 13.1 %collective-permute-start.11 = (bf16[8,64]{1,0:T(8,128)(2,1)S(1)}, bf16[8,64]{1,0:T(8,128)(2,1)S(1)}, u32[]{:S(2)}, u32[]{:S(2)}) collective-permute-start(bf16[8,64]{1,0:T(8,128)(2,1)S(1)} %slice_maximum_fusion), channel_id=1, source_target_pairs={{0,2},{2,0},{1,3},{3,1},{4,6},{6,4},{5,7},{7,5},{8,10},{10,8},{9,1... | collective-permute-start | bytes 3080 | tf_op jit(solution)/shard_map/ppermute | solution.py:34
  34.9 7.1 %collective-permute-start.14 = (bf16[88,896]{1,0:T(8,128)(2,1)S(1)}, bf16[88,896]{1,0:T(8,128)(2,1)S(1)}, u32[]{:S(2)}, u32[]{:S(2)}) collective-permute-start(bf16[88,896]{1,0:T(8,128)(2,1)S(1)} %convolution_convert_fusion.28), channel_id=1, source_target_pairs={{0,4},{4,0},{8,12},{12,8},{1,5},{5,1},{9,13},{13,9},{2,6},{6,2},{1... | collective-permute-start | bytes 473096 | tf_op jit(solution)/shard_map/ppermute | solution.py:34
  35.9 13.6 %collective-permute-start.17 = (bf16[80,1152]{1,0:T(8,128)(2,1)S(1)}, bf16[80,1152]{1,0:T(8,128)(2,1)S(1)}, u32[]{:S(2)}, u32[]{:S(2)}) collective-permute-start(bf16[80,1152]{1,0:T(8,128)(2,1)S(1)} %convolution_convert_fusion.17), channel_id=1, source_target_pairs={{0,8},{8,0},{4,12},{12,4},{1,9},{9,1},{5,13},{13,5},{2,10},{10,2},... | collective-permute-start | bytes 552968 | tf_op jit(solution)/shard_map/ppermute | solution.py:34
  40.1 2.3 %copy-start.7 = (bf16[128,1152]{1,0:T(8,128)(2,1)S(1)}, bf16[128,1152]{1,0:T(8,128)(2,1)}, u32[]{:S(2)}) copy-start(bf16[128,1152]{1,0:T(8,128)(2,1)} %convolution_convert_fusion.11) | copy-start | bytes 884740
  42.3 8.9 %collective-permute-start.18 = (bf16[80,896]{1,0:T(8,128)(2,1)S(1)}, bf16[80,896]{1,0:T(8,128)(2,1)S(1)}, u32[]{:S(2)}, u32[]{:S(2)}) collective-permute-start(bf16[80,896]{1,0:T(8,128)(2,1)S(1)} %convolution_convert_fusion.29), channel_id=1, source_target_pairs={{0,8},{8,0},{4,12},{12,4},{1,9},{9,1},{5,13},{13,5},{2,10},{10,2},... | collective-permute-start | bytes 430088 | tf_op jit(solution)/shard_map/ppermute | solution.py:34
  43.6 5.9 %copy-start.8 = (bf16[128,1152]{1,0:T(8,128)(2,1)S(1)}, bf16[128,1152]{1,0:T(8,128)(2,1)}, u32[]{:S(2)}) copy-start(bf16[128,1152]{1,0:T(8,128)(2,1)} %convolution_convert_fusion.7) | copy-start | bytes 884740

commit v21 on v20

--- a/solution.py
+++ b/solution.py
@@ -5,7 +5,7 @@
 from jax.experimental.pallas import tpu as pltpu
 from jax.sharding import PartitionSpec as P
 
-SHARES = (2, 5, 9, 9, 7)
+SHARES = (1, 5, 9, 10, 7)
 FULL_PIECES = (2, 1)
 EARLY_PIECES = 2
 COUNT_PIECE = 2
@@ -13,7 +13,7 @@
 LOOK = (3, -1)
 MAKE = (0, -1)
 ORDER = (
-    (0, 0), (0, 1), (0, 2), (1, 0), (1, 1), MAKE, (2, 0), (0, 3), (1, 2), LOOK, (2, 1), (1, 3), (2, 2),
+    (0, 0), (0, 1), (1, 0), (0, 2), (1, 1), MAKE, (2, 0), (0, 3), (1, 2), LOOK, (2, 1), (1, 3), (2, 2),
     (0, 4), (3, 0), (1, 4), (2, 3), (3, 1), (2, 4), (3, 2), (3, 3), (3, 4),
 )
 KERNEL_VMEM = 16 * 1024 * 1024
@@ -284,7 +284,7 @@
             previous = coeffs[-1]
             continue
         if (level, piece) == LOOK:
-            known = after(after(partners[0], previous), partners[1])[:, starts[1] :]
+            known = after(partners[0], previous)[:, starts[1] :]
             theirs[levels - 1] = known[: rooms[levels - 1 - wide], :rank]
             continue
         count = starts[piece + 1] - starts[piece]

time: 52.5 us -> 55.5 us (1.057)
  waiting for transfers between devices: 12.9 us -> 14.6 us
  Pallas kernels: 2.51 us -> 3.18 us
  starting transfers between devices: 22.9 us -> 23.5 us
    ppermute x16, waiting for transfers between devices: 12.9 us -> 14.6 us  [from_partner(): return lax.ppermute(block, hop[0], route(*hop))]
    pallas_call x1, Pallas kernels: 1.06 us -> 1.8 us  [tables(): pl.pallas_call(lambda *refs: tables_kernel(wide, rooms, *refs), out_shape...]
    ppermute x16, starting transfers between devices: 22.9 us -> 23.5 us  [from_partner(): return lax.ppermute(block, hop[0], route(*hop))]
  transfers between devices with their start and end apart: 16 -> 16, of which waited for: 7 -> 7; matrix products, arithmetic and copies ran while one was open for 23% -> 21% of each run, Pallas kernels for 2% -> 3%
where the time goes in v21:
time: 55.5 us; the launch traced here: 55.4 us
  starting transfers between devices  23.5 us (42%)
  waiting for transfers between devices  14.6 us (26%)
  matrix products  12.3 us (22%)
  Pallas kernels  3.18 us (6%)
  between operations  0.99 us (2%)
  local copies, waits for them, and re-layouts  0.64 us (1%)
    ppermute x16, starting transfers between devices, from_partner(): return lax.ppermute(block, hop[0], route(*hop))  23.5 us
    ppermute x16, waiting for transfers between devices, from_partner(): return lax.ppermute(block, hop[0], route(*hop))  14.6 us
    dot_general x5, matrix products, evaluated(): jnp.einsum('ct,cp->tp', coeffs, evaluation, preferred_element_type=jnp.fl...  5.61 us
    dot_general x17, matrix products, times(): jnp.dot(matrix, value, preferred_element_type=jnp.float32)  5.16 us
    pallas_call x1, Pallas kernels, tables(): pl.pallas_call(lambda *refs: tables_kernel(wide, rooms, *refs), out_shape...  1.8 us
    pallas_call x1, Pallas kernels, early(): pl.pallas_call(lambda *refs: early_kernel(starts, *refs), out_shape=[jax....  1.37 us
  transfers between devices with their start and end apart: 16, of which 7 were waited for; matrix products, arithmetic and copies ran while one was open for 21% of the time, Pallas kernels for 3%

profile of v21, /device:TPU:0, one launch (start us, length us, event | category | flops | bytes accessed | tf_op | source)
XLA Modules:
  0.0 55.4 jit_solution(168837357804126540)
XLA Ops:
  0.0 1.4 %early.1 = (bf16[128,128]{1,0:T(8,128)(2,1)S(1)}, bf16[128,640]{1,0:T(8,128)(2,1)S(1)}) custom-call(bf16[1,128,128]{2,1,0:T(8,128)(2,1)} %refs_0_.1, bf16[4096,128]{1,0:T(8,128)(2,1)} %refs_1_.2), custom_call_target="tpu_custom_call" | custom-call | flops 25165824 | bytes 393216 | tf_op jit(solution)/shard_map/early/pallas_call | solution.py:70
  1.4 3.0 %collective-permute-start.3 = (bf16[128,128]{1,0:T(8,128)(2,1)S(1)}, bf16[128,128]{1,0:T(8,128)(2,1)S(1)}, u32[]{:S(2)}, u32[]{:S(2)}) collective-permute-start(bf16[128,128]{1,0:T(8,128)(2,1)S(1)} %get-tuple-element.63), channel_id=1, source_target_pairs={{0,2},{2,0},{1,3},{3,1},{4,6},{6,4},{5,7},{7,5},{8,10},{10,8},{9,1... | collective-permute-start | bytes 98312 | tf_op jit(solution)/shard_map/ppermute | solution.py:34
  4.5 1.8 %tables.1 = (bf16[3,128,256]{2,1,0:T(8,128)(2,1)S(1)}, bf16[2,128,256]{2,1,0:T(8,128)(2,1)S(1)}, bf16[2,128,128]{2,1,0:T(8,128)(2,1)S(1)}) custom-call(s32[3,1,64]{2,1,0:T(1,128)S(1)} %bitcast.111, bf16[1,3,64,128]{3,2,1,0:T(8,128)(2,1)} %refs_1_.3), custom_call_target="tpu_custom_call" | custom-call | flops 50000000 | bytes 600000 | tf_op jit(solution)/shard_map/tables/pallas_call | solution.py:156
  6.5 2.4 %collective-permute-start.4 = (bf16[128,256]{1,0:T(8,128)(2,1)S(1)}, bf16[128,256]{1,0:T(8,128)(2,1)S(1)}, u32[]{:S(2)}, u32[]{:S(2)}) collective-permute-start(bf16[128,256]{1,0:T(8,128)(2,1)S(1)} %pad_maximum_fusion.12), channel_id=1, source_target_pairs={{0,4},{4,0},{8,12},{12,8},{1,5},{5,1},{9,13},{13,9},{2,6},{6,2},{1... | collective-permute-start | bytes 196616 | tf_op jit(solution)/shard_map/ppermute | solution.py:34
  8.9 0.3 convolution_convert_fusion.14
  9.2 1.6 %collective-permute-start.7 = (bf16[128,1152]{1,0:T(8,128)(2,1)S(1)}, bf16[128,1152]{1,0:T(8,128)(2,1)S(1)}, u32[]{:S(2)}, u32[]{:S(2)}) collective-permute-start(bf16[128,1152]{1,0:T(8,128)(2,1)S(1)} %convolution_convert_fusion.14), channel_id=1, source_target_pairs={{0,2},{2,0},{1,3},{3,1},{4,6},{6,4},{5,7},{7,5},{8,10},{10,8},{9,1... | collective-permute-start | bytes 884744 | tf_op jit(solution)/shard_map/ppermute | solution.py:34
  11.0 2.2 %collective-permute-start.10 = (bf16[128,640]{1,0:T(8,128)(2,1)S(1)}, bf16[128,640]{1,0:T(8,128)(2,1)S(1)}, u32[]{:S(2)}, u32[]{:S(2)}) collective-permute-start(bf16[128,640]{1,0:T(8,128)(2,1)S(1)} %convolution_convert_fusion.26), channel_id=1, source_target_pairs={{0,4},{4,0},{8,12},{12,8},{1,5},{5,1},{9,13},{13,9},{2,6},{6,2},{1... | collective-permute-start | bytes 491528 | tf_op jit(solution)/shard_map/ppermute | solution.py:34
  13.2 0.3 convolution_convert_fusion.13
  13.9 2.5 %collective-permute-start.6 = (bf16[128,256]{1,0:T(8,128)(2,1)S(1)}, bf16[128,256]{1,0:T(8,128)(2,1)S(1)}, u32[]{:S(2)}, u32[]{:S(2)}) collective-permute-start(bf16[128,256]{1,0:T(8,128)(2,1)S(1)} %pad_maximum_fusion.13), channel_id=1, source_target_pairs={{0,8},{8,0},{4,12},{12,4},{1,9},{9,1},{5,13},{13,5},{2,10},{10,2},... | collective-permute-start | bytes 196616 | tf_op jit(solution)/shard_map/ppermute | solution.py:34
  16.4 0.3 collective-permute-start.9
  17.4 2.6 %collective-permute-done.6 = bf16[128,256]{1,0:T(8,128)(2,1)S(1)} collective-permute-done((bf16[128,256]{1,0:T(8,128)(2,1)S(1)}, bf16[128,256]{1,0:T(8,128)(2,1)S(1)}, u32[]{:S(2)}, u32[]{:S(2)}) %collective-permute-start.6) | collective-permute-done | bytes 65568 | tf_op jit(solution)/shard_map/ppermute | solution.py:34
  20.8 2.6 %collective-permute-start.15 = (bf16[80,640]{1,0:T(8,128)(2,1)S(1)}, bf16[80,640]{1,0:T(8,128)(2,1)S(1)}, u32[]{:S(2)}, u32[]{:S(2)}) collective-permute-start(bf16[80,640]{1,0:T(8,128)(2,1)S(1)} %convolution_convert_fusion.30), channel_id=1, source_target_pairs={{0,8},{8,0},{4,12},{12,4},{1,9},{9,1},{5,13},{13,5},{2,10},{10,2},... | collective-permute-start | bytes 307208 | tf_op jit(solution)/shard_map/ppermute | solution.py:34
  23.6 0.2 convolution_convert_fusion.12
  24.2 1.6 %collective-permute-start.16 = (bf16[88,1280]{1,0:T(8,128)(2,1)S(1)}, bf16[88,1280]{1,0:T(8,128)(2,1)S(1)}, u32[]{:S(2)}, u32[]{:S(2)}) collective-permute-start(bf16[88,1280]{1,0:T(8,128)(2,1)S(1)} %convolution_convert_fusion.15), channel_id=1, source_target_pairs={{0,4},{4,0},{8,12},{12,8},{1,5},{5,1},{9,13},{13,9},{2,6},{6,2},{1... | collective-permute-start | bytes 675848 | tf_op jit(solution)/shard_map/ppermute | solution.py:34
  25.8 0.3 convolution_convert_fusion.10
  26.1 3.8 %collective-permute-done.8 = bf16[88,1152]{1,0:T(8,128)(2,1)S(1)} collective-permute-done((bf16[88,1152]{1,0:T(8,128)(2,1)S(1)}, bf16[88,1152]{1,0:T(8,128)(2,1)S(1)}, u32[]{:S(2)}, u32[]{:S(2)}) %collective-permute-start.8) | collective-permute-done | bytes 202784 | tf_op jit(solution)/shard_map/ppermute | solution.py:34
  30.1 1.2 %collective-permute-start.13 = (bf16[128,896]{1,0:T(8,128)(2,1)S(1)}, bf16[128,896]{1,0:T(8,128)(2,1)S(1)}, u32[]{:S(2)}, u32[]{:S(2)}) collective-permute-start(bf16[128,896]{1,0:T(8,128)(2,1)S(1)} %convolution_convert_fusion.23), channel_id=1, source_target_pairs={{0,2},{2,0},{1,3},{3,1},{4,6},{6,4},{5,7},{7,5},{8,10},{10,8},{9,1... | collective-permute-start | bytes 688136 | tf_op jit(solution)/shard_map/ppermute | solution.py:34
  31.4 1.0 %convolution_convert_fusion.11 = bf16[128,1152]{1,0:T(8,128)(2,1)} fusion(bf16[128,256]{1,0:T(8,128)(2,1)S(1)} %slice_bitcast_fusion.7, bf16[88,1152]{1,0:T(8,128)(2,1)S(1)} %collective-permute-done.8, bf16[128,1152]{1,0:T(8,128)(2,1)S(1)} %convolution_convert_fusion.12), kind=kOutput, calls=%fused_computation.36 | convolution fusion | flops 77709312 | bytes 858112 | tf_op jit(solution)/shard_map/dot_general | solution.py:223
  32.3 0.9 %collective-permute-start.11 = (bf16[8,64]{1,0:T(8,128)(2,1)S(1)}, bf16[8,64]{1,0:T(8,128)(2,1)S(1)}, u32[]{:S(2)}, u32[]{:S(2)}) collective-permute-start(bf16[8,64]{1,0:T(8,128)(2,1)S(1)} %slice_maximum_fusion), channel_id=1, source_target_pairs={{0,2},{2,0},{1,3},{3,1},{4,6},{6,4},{5,7},{7,5},{8,10},{10,8},{9,1... | collective-permute-start | bytes 3080 | tf_op jit(solution)/shard_map/ppermute | solution.py:34
  33.2 1.0 %constant_dynamic-update-slice_fusion.3 = bf16[4096,128]{1,0:T(8,128)(2,1)} fusion(bf16[1,128,128]{2,1,0:T(8,128)(2,1)S(1)} %copy-done.5, bf16[128,128]{1,0:T(8,128)(2,1)S(1)} %slice.182, bf16[128,128]{1,0:T(8,128)(2,1)S(1)} %convolution_convert_fusion.33, bf16[3,128,256]{2,1,0:T(8,128)(2,1)S(1)} %get-tuple-element.66), kind=kOutput, calls=%fused_computation.168 | convolution fusion | flops 12746751 | bytes 196608 | tf_op jit(solution)/shard_map/ct,cp->tp/dot_general | solution.py:233
  34.2 2.1 %collective-permute-done.13 = bf16[128,896]{1,0:T(8,128)(2,1)S(1)} collective-permute-done((bf16[128,896]{1,0:T(8,128)(2,1)S(1)}, bf16[128,896]{1,0:T(8,128)(2,1)S(1)}, u32[]{:S(2)}, u32[]{:S(2)}) %collective-permute-start.13) | collective-permute-done | bytes 229408 | tf_op jit(solution)/shard_map/ppermute | solution.py:34
  36.8 2.9 %collective-permute-start.17 = (bf16[80,1280]{1,0:T(8,128)(2,1)S(1)}, bf16[80,1280]{1,0:T(8,128)(2,1)S(1)}, u32[]{:S(2)}, u32[]{:S(2)}) collective-permute-start(bf16[80,1280]{1,0:T(8,128)(2,1)S(1)} %convolution_convert_fusion.17), channel_id=1, source_target_pairs={{0,8},{8,0},{4,12},{12,4},{1,9},{9,1},{5,13},{13,5},{2,10},{10,2},... | collective-permute-start | bytes 614408 | tf_op jit(solution)/shard_map/ppermute | solution.py:34
  39.7 1.0 %convolution_convert_fusion.7 = bf16[128,1280]{1,0:T(8,128)(2,1)} fusion(bf16[128,256]{1,0:T(8,128)(2,1)S(1)} %slice_bitcast_fusion.7, bf16[88,1280]{1,0:T(8,128)(2,1)S(1)} %collective-permute-done.16, bf16[128,1280]{1,0:T(8,128)(2,1)S(1)} %convolution_convert_fusion.10), kind=kOutput, calls=%fused_computation.32 | convolution fusion | flops 86343680 | bytes 946176 | tf_op jit(solution)/shard_map/dot_general | solution.py:223
  40.7 1.1 %constant_dynamic-update-slice_fusion.2 = bf16[4096,128]{1,0:T(8,128)(2,1)} fusion(bf16[4096,128]{1,0:T(8,128)(2,1)} %constant_dynamic-update-slice_fusion.3, bf16[1,128,128]{2,1,0:T(8,128)(2,1)S(1)} %copy-done.5, bf16[80,640]{1,0:T(8,128)(2,1)S(1)} %collective-permute-done.15, bf16[128,640]{1,0:T(8,128)(2,1)S(1)} %convolution_convert_fusion.25, ...), kind=kOutput, calls=%fused_computation.167 | convolution fusion | flops 64225280 | bytes 528384 | tf_op jit(solution)/shard_map/ct,cp->tp/dot_general | solution.py:233
  42.0 1.6 %collective-permute-done.14 = bf16[88,896]{1,0:T(8,128)(2,1)S(1)} collective-permute-done((bf16[88,896]{1,0:T(8,128)(2,1)S(1)}, bf16[88,896]{1,0:T(8,128)(2,1)S(1)}, u32[]{:S(2)}, u32[]{:S(2)}) %collective-permute-start.14) | collective-permute-done | bytes 157728 | tf_op jit(solution)/shard_map/ppermute | solution.py:34
  43.8 2.1 %collective-permute-start.18 = (bf16[80,896]{1,0:T(8,128)(2,1)S(1)}, bf16[80,896]{1,0:T(8,128)(2,1)S(1)}, u32[]{:S(2)}, u32[]{:S(2)}) collective-permute-start(bf16[80,896]{1,0:T(8,128)(2,1)S(1)} %convolution_convert_fusion.29), channel_id=1, source_target_pairs={{0,8},{8,0},{4,12},{12,4},{1,9},{9,1},{5,13},{13,5},{2,10},{10,2},... | collective-permute-start | bytes 430088 | tf_op jit(solution)/shard_map/ppermute | solution.py:34
  45.9 1.2 %constant_dynamic-update-slice_fusion.1 = bf16[4096,128]{1,0:T(8,128)(2,1)} fusion(bf16[4096,128]{1,0:T(8,128)(2,1)} %constant_dynamic-update-slice_fusion.2, bf16[1,128,128]{2,1,0:T(8,128)(2,1)S(1)} %copy-done.5, bf16[80,1152]{1,0:T(8,128)(2,1)S(1)} %collective-permute-done.12, bf16[128,1152]{1,0:T(8,128)(2,1)S(1)} %copy-done.6, ...), kind=kOutput, calls=%fused_computation.166 | convolution fusion | flops 115605504 | bytes 872448 | tf_op jit(solution)/shard_map/ct,cp->tp/dot_general | solution.py:233
  47.1 0.6 %slice.183 = bf16[1,1]{1,0:T(2,128)(2,1)} slice(bf16[8,64]{1,0:T(8,128)(2,1)S(1)} %max.11), slice={[0:1], [0:1]} | slice | bytes 4 | tf_op jit(solution)/shard_map/slice | solution.py:337
  48.6 3.9 %collective-permute-done.17 = bf16[80,1280]{1,0:T(8,128)(2,1)S(1)} collective-permute-done((bf16[80,1280]{1,0:T(8,128)(2,1)S(1)}, bf16[80,1280]{1,0:T(8,128)(2,1)S(1)}, u32[]{:S(2)}, u32[]{:S(2)}) %collective-permute-start.17) | collective-permute-done | bytes 204832 | tf_op jit(solution)/shard_map/ppermute | solution.py:34
  52.6 1.2 %constant_dynamic-update-slice_fusion = bf16[4096,128]{1,0:T(8,128)(2,1)} fusion(bf16[4096,128]{1,0:T(8,128)(2,1)} %constant_dynamic-update-slice_fusion.1, bf16[1,128,128]{2,1,0:T(8,128)(2,1)S(1)} %copy-done.5, bf16[80,1280]{1,0:T(8,128)(2,1)S(1)} %collective-permute-done.17, bf16[128,1280]{1,0:T(8,128)(2,1)S(1)} %copy-done.7, ...), kind=kOutput, calls=%fused_computation.165 | convolution fusion | flops 128450560 | bytes 958464 | tf_op jit(solution)/shard_map/ct,cp->tp/dot_general | solution.py:233
  53.8 0.4 collective-permute-done.18
  54.2 1.1 %fusion.24 = bf16[4096,128]{1,0:T(8,128)(2,1)} fusion(bf16[4096,128]{1,0:T(8,128)(2,1)} %constant_dynamic-update-slice_fusion, bf16[80,896]{1,0:T(8,128)(2,1)S(1)} %collective-permute-done.18, bf16[128,896]{1,0:T(8,128)(2,1)S(1)} %convolution_convert_fusion.21, bf16[2,128,256]{2,1,0:T(8,128)(2,1)S(1)} %get-tuple-element.76, ...), kind=kOutput, calls=%fused_computation.51 | convolution fusion | flops 89915392 | bytes 700416 | tf_op jit(solution)/shard_map/ct,cp->tp/dot_general | solution.py:233
  (60 shorter events, 4.5 us)
Async XLA Ops:
  0.0 8.9 %copy-start = (bf16[4096,128]{1,0:T(8,128)(2,1)S(1)}, bf16[4096,128]{1,0:T(8,128)(2,1)}, u32[]{:S(2)}) copy-start(bf16[4096,128]{1,0:T(8,128)(2,1)} %refs_1_.2) | copy-start | bytes 3145732
  0.0 8.9 %copy-start.2 = (bf16[1,128,128]{2,1,0:T(8,128)(2,1)S(1)}, bf16[1,128,128]{2,1,0:T(8,128)(2,1)}, u32[]{:S(2)}) copy-start(bf16[1,128,128]{2,1,0:T(8,128)(2,1)} %refs_0_.1) | copy-start | bytes 98308
  0.0 4.5 %copy-start.4 = (s32[1,3,64]{2,0,1:T(1,128)S(1)}, s32[1,3,64]{2,0,1:T(1,128)}, u32[]{:S(2)}) copy-start(s32[1,3,64]{2,0,1:T(1,128)} %param.9) | copy-start | bytes 2308
  1.4 5.0 %collective-permute-start.3 = (bf16[128,128]{1,0:T(8,128)(2,1)S(1)}, bf16[128,128]{1,0:T(8,128)(2,1)S(1)}, u32[]{:S(2)}, u32[]{:S(2)}) collective-permute-start(bf16[128,128]{1,0:T(8,128)(2,1)S(1)} %get-tuple-element.63), channel_id=1, source_target_pairs={{0,2},{2,0},{1,3},{3,1},{4,6},{6,4},{5,7},{7,5},{8,10},{10,8},{9,1... | collective-permute-start | bytes 98312 | tf_op jit(solution)/shard_map/ppermute | solution.py:34
  4.4 6.4 %collective-permute-start.5 = (bf16[128,640]{1,0:T(8,128)(2,1)S(1)}, bf16[128,640]{1,0:T(8,128)(2,1)S(1)}, u32[]{:S(2)}, u32[]{:S(2)}) collective-permute-start(bf16[128,640]{1,0:T(8,128)(2,1)S(1)} %get-tuple-element.67), channel_id=1, source_target_pairs={{0,2},{2,0},{1,3},{3,1},{4,6},{6,4},{5,7},{7,5},{8,10},{10,8},{9,1... | collective-permute-start | bytes 491528 | tf_op jit(solution)/shard_map/ppermute | solution.py:34
  6.5 6.9 %collective-permute-start.4 = (bf16[128,256]{1,0:T(8,128)(2,1)S(1)}, bf16[128,256]{1,0:T(8,128)(2,1)S(1)}, u32[]{:S(2)}, u32[]{:S(2)}) collective-permute-start(bf16[128,256]{1,0:T(8,128)(2,1)S(1)} %pad_maximum_fusion.12), channel_id=1, source_target_pairs={{0,4},{4,0},{8,12},{12,8},{1,5},{5,1},{9,13},{13,9},{2,6},{6,2},{1... | collective-permute-start | bytes 196616 | tf_op jit(solution)/shard_map/ppermute | solution.py:34
  9.2 8.0 %collective-permute-start.7 = (bf16[128,1152]{1,0:T(8,128)(2,1)S(1)}, bf16[128,1152]{1,0:T(8,128)(2,1)S(1)}, u32[]{:S(2)}, u32[]{:S(2)}) collective-permute-start(bf16[128,1152]{1,0:T(8,128)(2,1)S(1)} %convolution_convert_fusion.14), channel_id=1, source_target_pairs={{0,2},{2,0},{1,3},{3,1},{4,6},{6,4},{5,7},{7,5},{8,10},{10,8},{9,1... | collective-permute-start | bytes 884744 | tf_op jit(solution)/shard_map/ppermute | solution.py:34
  11.0 9.5 %collective-permute-start.10 = (bf16[128,640]{1,0:T(8,128)(2,1)S(1)}, bf16[128,640]{1,0:T(8,128)(2,1)S(1)}, u32[]{:S(2)}, u32[]{:S(2)}) collective-permute-start(bf16[128,640]{1,0:T(8,128)(2,1)S(1)} %convolution_convert_fusion.26), channel_id=1, source_target_pairs={{0,4},{4,0},{8,12},{12,8},{1,5},{5,1},{9,13},{13,9},{2,6},{6,2},{1... | collective-permute-start | bytes 491528 | tf_op jit(solution)/shard_map/ppermute | solution.py:34
  13.9 6.0 %collective-permute-start.6 = (bf16[128,256]{1,0:T(8,128)(2,1)S(1)}, bf16[128,256]{1,0:T(8,128)(2,1)S(1)}, u32[]{:S(2)}, u32[]{:S(2)}) collective-permute-start(bf16[128,256]{1,0:T(8,128)(2,1)S(1)} %pad_maximum_fusion.13), channel_id=1, source_target_pairs={{0,8},{8,0},{4,12},{12,4},{1,9},{9,1},{5,13},{13,5},{2,10},{10,2},... | collective-permute-start | bytes 196616 | tf_op jit(solution)/shard_map/ppermute | solution.py:34
  16.4 7.5 %collective-permute-start.9 = (bf16[128,1280]{1,0:T(8,128)(2,1)S(1)}, bf16[128,1280]{1,0:T(8,128)(2,1)S(1)}, u32[]{:S(2)}, u32[]{:S(2)}) collective-permute-start(bf16[128,1280]{1,0:T(8,128)(2,1)S(1)} %convolution_convert_fusion.13), channel_id=1, source_target_pairs={{0,2},{2,0},{1,3},{3,1},{4,6},{6,4},{5,7},{7,5},{8,10},{10,8},{9,1... | collective-permute-start | bytes 983048 | tf_op jit(solution)/shard_map/ppermute | solution.py:34
  20.4 9.5 %collective-permute-start.8 = (bf16[88,1152]{1,0:T(8,128)(2,1)S(1)}, bf16[88,1152]{1,0:T(8,128)(2,1)S(1)}, u32[]{:S(2)}, u32[]{:S(2)}) collective-permute-start(bf16[88,1152]{1,0:T(8,128)(2,1)S(1)} %convolution_convert_fusion.16), channel_id=1, source_target_pairs={{0,4},{4,0},{8,12},{12,8},{1,5},{5,1},{9,13},{13,9},{2,6},{6,2},{1... | collective-permute-start | bytes 608264 | tf_op jit(solution)/shard_map/ppermute | solution.py:34
  20.8 19.9 %collective-permute-start.15 = (bf16[80,640]{1,0:T(8,128)(2,1)S(1)}, bf16[80,640]{1,0:T(8,128)(2,1)S(1)}, u32[]{:S(2)}, u32[]{:S(2)}) collective-permute-start(bf16[80,640]{1,0:T(8,128)(2,1)S(1)} %convolution_convert_fusion.30), channel_id=1, source_target_pairs={{0,8},{8,0},{4,12},{12,4},{1,9},{9,1},{5,13},{13,5},{2,10},{10,2},... | collective-permute-start | bytes 307208 | tf_op jit(solution)/shard_map/ppermute | solution.py:34
  24.2 12.4 %collective-permute-start.16 = (bf16[88,1280]{1,0:T(8,128)(2,1)S(1)}, bf16[88,1280]{1,0:T(8,128)(2,1)S(1)}, u32[]{:S(2)}, u32[]{:S(2)}) collective-permute-start(bf16[88,1280]{1,0:T(8,128)(2,1)S(1)} %convolution_convert_fusion.15), channel_id=1, source_target_pairs={{0,4},{4,0},{8,12},{12,8},{1,5},{5,1},{9,13},{13,9},{2,6},{6,2},{1... | collective-permute-start | bytes 675848 | tf_op jit(solution)/shard_map/ppermute | solution.py:34
  30.1 3.1 %copy-start.5 = (bf16[1,128,128]{2,1,0:T(8,128)(2,1)S(1)}, bf16[1,128,128]{2,1,0:T(8,128)(2,1)}, u32[]{:S(2)}) copy-start(bf16[1,128,128]{2,1,0:T(8,128)(2,1)} %param.11) | copy-start | bytes 98308
  30.1 15.8 %collective-permute-start.12 = (bf16[80,1152]{1,0:T(8,128)(2,1)S(1)}, bf16[80,1152]{1,0:T(8,128)(2,1)S(1)}, u32[]{:S(2)}, u32[]{:S(2)}) collective-permute-start(bf16[80,1152]{1,0:T(8,128)(2,1)S(1)} %convolution_convert_fusion.18), channel_id=1, source_target_pairs={{0,8},{8,0},{4,12},{12,4},{1,9},{9,1},{5,13},{13,5},{2,10},{10,2},... | collective-permute-start | bytes 552968 | tf_op jit(solution)/shard_map/ppermute | solution.py:34
  30.1 6.1 %collective-permute-start.13 = (bf16[128,896]{1,0:T(8,128)(2,1)S(1)}, bf16[128,896]{1,0:T(8,128)(2,1)S(1)}, u32[]{:S(2)}, u32[]{:S(2)}) collective-permute-start(bf16[128,896]{1,0:T(8,128)(2,1)S(1)} %convolution_convert_fusion.23), channel_id=1, source_target_pairs={{0,2},{2,0},{1,3},{3,1},{4,6},{6,4},{5,7},{7,5},{8,10},{10,8},{9,1... | collective-permute-start | bytes 688136 | tf_op jit(solution)/shard_map/ppermute | solution.py:34
  32.3 14.8 %collective-permute-start.11 = (bf16[8,64]{1,0:T(8,128)(2,1)S(1)}, bf16[8,64]{1,0:T(8,128)(2,1)S(1)}, u32[]{:S(2)}, u32[]{:S(2)}) collective-permute-start(bf16[8,64]{1,0:T(8,128)(2,1)S(1)} %slice_maximum_fusion), channel_id=1, source_target_pairs={{0,2},{2,0},{1,3},{3,1},{4,6},{6,4},{5,7},{7,5},{8,10},{10,8},{9,1... | collective-permute-start | bytes 3080 | tf_op jit(solution)/shard_map/ppermute | solution.py:34
  36.4 7.2 %collective-permute-start.14 = (bf16[88,896]{1,0:T(8,128)(2,1)S(1)}, bf16[88,896]{1,0:T(8,128)(2,1)S(1)}, u32[]{:S(2)}, u32[]{:S(2)}) collective-permute-start(bf16[88,896]{1,0:T(8,128)(2,1)S(1)} %convolution_convert_fusion.28), channel_id=1, source_target_pairs={{0,4},{4,0},{8,12},{12,8},{1,5},{5,1},{9,13},{13,9},{2,6},{6,2},{1... | collective-permute-start | bytes 473096 | tf_op jit(solution)/shard_map/ppermute | solution.py:34
  36.8 15.8 %collective-permute-start.17 = (bf16[80,1280]{1,0:T(8,128)(2,1)S(1)}, bf16[80,1280]{1,0:T(8,128)(2,1)S(1)}, u32[]{:S(2)}, u32[]{:S(2)}) collective-permute-start(bf16[80,1280]{1,0:T(8,128)(2,1)S(1)} %convolution_convert_fusion.17), channel_id=1, source_target_pairs={{0,8},{8,0},{4,12},{12,4},{1,9},{9,1},{5,13},{13,5},{2,10},{10,2},... | collective-permute-start | bytes 614408 | tf_op jit(solution)/shard_map/ppermute | solution.py:34
  42.0 3.9 %copy-start.6 = (bf16[128,1152]{1,0:T(8,128)(2,1)S(1)}, bf16[128,1152]{1,0:T(8,128)(2,1)}, u32[]{:S(2)}) copy-start(bf16[128,1152]{1,0:T(8,128)(2,1)} %convolution_convert_fusion.11) | copy-start | bytes 884740
  43.8 10.4 %collective-permute-start.18 = (bf16[80,896]{1,0:T(8,128)(2,1)S(1)}, bf16[80,896]{1,0:T(8,128)(2,1)S(1)}, u32[]{:S(2)}, u32[]{:S(2)}) collective-permute-start(bf16[80,896]{1,0:T(8,128)(2,1)S(1)} %convolution_convert_fusion.29), channel_id=1, source_target_pairs={{0,8},{8,0},{4,12},{12,4},{1,9},{9,1},{5,13},{13,5},{2,10},{10,2},... | collective-permute-start | bytes 430088 | tf_op jit(solution)/shard_map/ppermute | solution.py:34
  47.1 5.5 %copy-start.7 = (bf16[128,1280]{1,0:T(8,128)(2,1)S(1)}, bf16[128,1280]{1,0:T(8,128)(2,1)}, u32[]{:S(2)}) copy-start(bf16[128,1280]{1,0:T(8,128)(2,1)} %convolution_convert_fusion.7) | copy-start | bytes 983044
  53.8 1.6 %copy-start.3 = (bf16[1,3,64,128]{3,2,1,0:T(8,128)(2,1)S(1)}, bf16[1,3,64,128]{3,2,1,0:T(8,128)(2,1)}, u32[]{:S(2)}) copy-start(bf16[1,3,64,128]{3,2,1,0:T(8,128)(2,1)} %refs_1_.3) | copy-start | bytes 147460

commit v22 on v20

--- a/solution.py
+++ b/solution.py
@@ -5,7 +5,7 @@
 from jax.experimental.pallas import tpu as pltpu
 from jax.sharding import PartitionSpec as P
 
-SHARES = (2, 5, 9, 9, 7)
+SHARES = (2, 5, 7, 10, 8)
 FULL_PIECES = (2, 1)
 EARLY_PIECES = 2
 COUNT_PIECE = 2

time: 52.5 us -> 52.9 us (level)
  starting transfers between devices: 22.9 us -> 23.7 us
    ppermute x16, starting transfers between devices: 22.9 us -> 23.7 us  [from_partner(): return lax.ppermute(block, hop[0], route(*hop))]
  transfers between devices with their start and end apart: 16 -> 16, of which waited for: 7 -> 7; matrix products, arithmetic and copies ran while one was open for 23% -> 22% of each run, Pallas kernels for 2% -> 2%
where the time goes in v22:
time: 52.9 us; the launch traced here: 52.7 us
  starting transfers between devices  23.7 us (45%)
  waiting for transfers between devices  12.6 us (24%)
  matrix products  12.3 us (23%)
  Pallas kernels  2.51 us (5%)
  between operations  0.93 us (2%)
  local copies, waits for them, and re-layouts  0.62 us (1%)
    ppermute x16, starting transfers between devices, from_partner(): return lax.ppermute(block, hop[0], route(*hop))  23.7 us
    ppermute x16, waiting for transfers between devices, from_partner(): return lax.ppermute(block, hop[0], route(*hop))  12.6 us
    dot_general x5, matrix products, evaluated(): jnp.einsum('ct,cp->tp', coeffs, evaluation, preferred_element_type=jnp.fl...  5.63 us
    dot_general x17, matrix products, times(): jnp.dot(matrix, value, preferred_element_type=jnp.float32)  5.1 us
    pallas_call x1, Pallas kernels, early(): pl.pallas_call(lambda *refs: early_kernel(starts, *refs), out_shape=[jax....  1.45 us
    pallas_call x1, Pallas kernels, tables(): pl.pallas_call(lambda *refs: tables_kernel(wide, rooms, *refs), out_shape...  1.06 us
  transfers between devices with their start and end apart: 16, of which 7 were waited for; matrix products, arithmetic and copies ran while one was open for 22% of the time, Pallas kernels for 2%

profile of v22, /device:TPU:0, one launch (start us, length us, event | category | flops | bytes accessed | tf_op | source)
XLA Modules:
  0.0 52.7 jit_solution(3857338787007014860)
XLA Ops:
  0.0 1.4 %early.1 = (bf16[128,256]{1,0:T(8,128)(2,1)S(1)}, bf16[128,640]{1,0:T(8,128)(2,1)S(1)}) custom-call(bf16[1,128,128]{2,1,0:T(8,128)(2,1)} %refs_0_.1, bf16[4096,128]{1,0:T(8,128)(2,1)} %refs_1_.2), custom_call_target="tpu_custom_call" | custom-call | flops 29360128 | bytes 458752 | tf_op jit(solution)/shard_map/early/pallas_call | solution.py:70
  1.5 3.0 %collective-permute-start.3 = (bf16[128,256]{1,0:T(8,128)(2,1)S(1)}, bf16[128,256]{1,0:T(8,128)(2,1)S(1)}, u32[]{:S(2)}, u32[]{:S(2)}) collective-permute-start(bf16[128,256]{1,0:T(8,128)(2,1)S(1)} %get-tuple-element.64), channel_id=1, source_target_pairs={{0,2},{2,0},{1,3},{3,1},{4,6},{6,4},{5,7},{7,5},{8,10},{10,8},{9,1... | collective-permute-start | bytes 196616 | tf_op jit(solution)/shard_map/ppermute | solution.py:34
  4.8 2.0 %collective-permute-start.7 = (bf16[128,896]{1,0:T(8,128)(2,1)S(1)}, bf16[128,896]{1,0:T(8,128)(2,1)S(1)}, u32[]{:S(2)}, u32[]{:S(2)}) collective-permute-start(bf16[128,896]{1,0:T(8,128)(2,1)S(1)} %convolution_convert_fusion.21), channel_id=1, source_target_pairs={{0,2},{2,0},{1,3},{3,1},{4,6},{6,4},{5,7},{7,5},{8,10},{10,8},{9,1... | collective-permute-start | bytes 688136 | tf_op jit(solution)/shard_map/ppermute | solution.py:34
  6.8 1.1 %tables.1 = (bf16[3,128,256]{2,1,0:T(8,128)(2,1)S(1)}, bf16[2,128,256]{2,1,0:T(8,128)(2,1)S(1)}, bf16[2,128,128]{2,1,0:T(8,128)(2,1)S(1)}) custom-call(s32[3,1,64]{2,1,0:T(1,128)S(1)} %bitcast.111, bf16[1,3,64,128]{3,2,1,0:T(8,128)(2,1)S(1)} %copy-done.3), custom_call_target="tpu_custom_call" | custom-call | flops 50000000 | bytes 600000 | tf_op jit(solution)/shard_map/tables/pallas_call | solution.py:156
  8.2 1.6 %collective-permute-start.4 = (bf16[128,384]{1,0:T(8,128)(2,1)S(1)}, bf16[128,384]{1,0:T(8,128)(2,1)S(1)}, u32[]{:S(2)}, u32[]{:S(2)}) collective-permute-start(bf16[128,384]{1,0:T(8,128)(2,1)S(1)} %pad_maximum_fusion.12), channel_id=1, source_target_pairs={{0,4},{4,0},{8,12},{12,8},{1,5},{5,1},{9,13},{13,9},{2,6},{6,2},{1... | collective-permute-start | bytes 294920 | tf_op jit(solution)/shard_map/ppermute | solution.py:34
  9.8 1.8 %collective-permute-done.5 = bf16[128,640]{1,0:T(8,128)(2,1)S(1)} collective-permute-done((bf16[128,640]{1,0:T(8,128)(2,1)S(1)}, bf16[128,640]{1,0:T(8,128)(2,1)S(1)}, u32[]{:S(2)}, u32[]{:S(2)}) %collective-permute-start.5) | collective-permute-done | bytes 163872 | tf_op jit(solution)/shard_map/ppermute | solution.py:34
  11.8 1.6 %collective-permute-start.8 = (bf16[128,640]{1,0:T(8,128)(2,1)S(1)}, bf16[128,640]{1,0:T(8,128)(2,1)S(1)}, u32[]{:S(2)}, u32[]{:S(2)}) collective-permute-start(bf16[128,640]{1,0:T(8,128)(2,1)S(1)} %convolution_convert_fusion.26), channel_id=1, source_target_pairs={{0,4},{4,0},{8,12},{12,8},{1,5},{5,1},{9,13},{13,9},{2,6},{6,2},{1... | collective-permute-start | bytes 491528 | tf_op jit(solution)/shard_map/ppermute | solution.py:34
  13.5 0.3 convolution_convert_fusion.9
  14.3 2.7 %collective-permute-start.6 = (bf16[128,384]{1,0:T(8,128)(2,1)S(1)}, bf16[128,384]{1,0:T(8,128)(2,1)S(1)}, u32[]{:S(2)}, u32[]{:S(2)}) collective-permute-start(bf16[128,384]{1,0:T(8,128)(2,1)S(1)} %pad_maximum_fusion.13), channel_id=1, source_target_pairs={{0,8},{8,0},{4,12},{12,4},{1,9},{9,1},{5,13},{13,5},{2,10},{10,2},... | collective-permute-start | bytes 294920 | tf_op jit(solution)/shard_map/ppermute | solution.py:34
  17.0 1.4 %collective-permute-start.10 = (bf16[128,1280]{1,0:T(8,128)(2,1)S(1)}, bf16[128,1280]{1,0:T(8,128)(2,1)S(1)}, u32[]{:S(2)}, u32[]{:S(2)}) collective-permute-start(bf16[128,1280]{1,0:T(8,128)(2,1)S(1)} %convolution_convert_fusion.9), channel_id=1, source_target_pairs={{0,2},{2,0},{1,3},{3,1},{4,6},{6,4},{5,7},{7,5},{8,10},{10,8},{9,1... | collective-permute-start | bytes 983048 | tf_op jit(solution)/shard_map/ppermute | solution.py:34
  18.7 1.4 %collective-permute-start.9 = (bf16[88,896]{1,0:T(8,128)(2,1)S(1)}, bf16[88,896]{1,0:T(8,128)(2,1)S(1)}, u32[]{:S(2)}, u32[]{:S(2)}) collective-permute-start(bf16[88,896]{1,0:T(8,128)(2,1)S(1)} %convolution_convert_fusion.28), channel_id=1, source_target_pairs={{0,4},{4,0},{8,12},{12,8},{1,5},{5,1},{9,13},{13,9},{2,6},{6,2},{1... | collective-permute-start | bytes 473096 | tf_op jit(solution)/shard_map/ppermute | solution.py:34
  20.3 0.5 collective-permute-done.6
  21.5 2.9 %collective-permute-start.15 = (bf16[80,640]{1,0:T(8,128)(2,1)S(1)}, bf16[80,640]{1,0:T(8,128)(2,1)S(1)}, u32[]{:S(2)}, u32[]{:S(2)}) collective-permute-start(bf16[80,640]{1,0:T(8,128)(2,1)S(1)} %convolution_convert_fusion.30), channel_id=1, source_target_pairs={{0,8},{8,0},{4,12},{12,4},{1,9},{9,1},{5,13},{13,5},{2,10},{10,2},... | collective-permute-start | bytes 307208 | tf_op jit(solution)/shard_map/ppermute | solution.py:34
  24.9 0.3 collective-permute-start.16
  25.2 0.3 convolution_convert_fusion.8
  26.0 1.8 %collective-permute-start.12 = (bf16[80,896]{1,0:T(8,128)(2,1)S(1)}, bf16[80,896]{1,0:T(8,128)(2,1)S(1)}, u32[]{:S(2)}, u32[]{:S(2)}) collective-permute-start(bf16[80,896]{1,0:T(8,128)(2,1)S(1)} %convolution_convert_fusion.29), channel_id=1, source_target_pairs={{0,8},{8,0},{4,12},{12,4},{1,9},{9,1},{5,13},{13,5},{2,10},{10,2},... | collective-permute-start | bytes 430088 | tf_op jit(solution)/shard_map/ppermute | solution.py:34
  27.7 1.1 %collective-permute-start.13 = (bf16[128,1024]{1,0:T(8,128)(2,1)S(1)}, bf16[128,1024]{1,0:T(8,128)(2,1)S(1)}, u32[]{:S(2)}, u32[]{:S(2)}) collective-permute-start(bf16[128,1024]{1,0:T(8,128)(2,1)S(1)} %convolution_convert_fusion.16), channel_id=1, source_target_pairs={{0,2},{2,0},{1,3},{3,1},{4,6},{6,4},{5,7},{7,5},{8,10},{10,8},{9,1... | collective-permute-start | bytes 786440 | tf_op jit(solution)/shard_map/ppermute | solution.py:34
  28.8 0.9 %convolution_convert_fusion.19 = bf16[128,896]{1,0:T(8,128)(2,1)} fusion(bf16[128,256]{1,0:T(8,128)(2,1)S(1)} %slice_bitcast_fusion.7, bf16[88,896]{1,0:T(8,128)(2,1)S(1)} %collective-permute-done.9, bf16[128,896]{1,0:T(8,128)(2,1)S(1)} %convolution_convert_fusion.20), kind=kOutput, calls=%fused_computation.51 | convolution fusion | flops 60440576 | bytes 681984 | tf_op jit(solution)/shard_map/dot_general | solution.py:223
  29.7 1.0 %collective-permute-start.11 = (bf16[8,64]{1,0:T(8,128)(2,1)S(1)}, bf16[8,64]{1,0:T(8,128)(2,1)S(1)}, u32[]{:S(2)}, u32[]{:S(2)}) collective-permute-start(bf16[8,64]{1,0:T(8,128)(2,1)S(1)} %slice_maximum_fusion), channel_id=1, source_target_pairs={{0,2},{2,0},{1,3},{3,1},{4,6},{6,4},{5,7},{7,5},{8,10},{10,8},{9,1... | collective-permute-start | bytes 3080 | tf_op jit(solution)/shard_map/ppermute | solution.py:34
  30.7 1.0 %constant_dynamic-update-slice_fusion.3 = bf16[4096,128]{1,0:T(8,128)(2,1)} fusion(bf16[1,128,128]{2,1,0:T(8,128)(2,1)S(1)} %copy-done.5, bf16[128,256]{1,0:T(8,128)(2,1)S(1)} %slice.182, bf16[128,256]{1,0:T(8,128)(2,1)S(1)} %convolution_convert_fusion.33, bf16[3,128,256]{2,1,0:T(8,128)(2,1)S(1)} %get-tuple-element.67), kind=kOutput, calls=%fused_computation.168 | convolution fusion | flops 25493504 | bytes 294912 | tf_op jit(solution)/shard_map/ct,cp->tp/dot_general | solution.py:233
  31.7 2.4 %collective-permute-done.13 = bf16[128,1024]{1,0:T(8,128)(2,1)S(1)} collective-permute-done((bf16[128,1024]{1,0:T(8,128)(2,1)S(1)}, bf16[128,1024]{1,0:T(8,128)(2,1)S(1)}, u32[]{:S(2)}, u32[]{:S(2)}) %collective-permute-start.13) | collective-permute-done | bytes 262176 | tf_op jit(solution)/shard_map/ppermute | solution.py:34
  34.3 0.5 collective-permute-start.14
  35.1 2.4 %collective-permute-start.17 = (bf16[80,1280]{1,0:T(8,128)(2,1)S(1)}, bf16[80,1280]{1,0:T(8,128)(2,1)S(1)}, u32[]{:S(2)}, u32[]{:S(2)}) collective-permute-start(bf16[80,1280]{1,0:T(8,128)(2,1)S(1)} %convolution_convert_fusion.11), channel_id=1, source_target_pairs={{0,8},{8,0},{4,12},{12,4},{1,9},{9,1},{5,13},{13,5},{2,10},{10,2},... | collective-permute-start | bytes 614408 | tf_op jit(solution)/shard_map/ppermute | solution.py:34
  37.5 1.0 %convolution_convert_fusion.7 = bf16[128,1280]{1,0:T(8,128)(2,1)} fusion(bf16[128,256]{1,0:T(8,128)(2,1)S(1)} %slice_bitcast_fusion.7, bf16[88,1280]{1,0:T(8,128)(2,1)S(1)} %collective-permute-done.16, bf16[128,1280]{1,0:T(8,128)(2,1)S(1)} %convolution_convert_fusion.8), kind=kOutput, calls=%fused_computation.32 | convolution fusion | flops 86343680 | bytes 946176 | tf_op jit(solution)/shard_map/dot_general | solution.py:223
  38.5 1.1 %constant_dynamic-update-slice_fusion.2 = bf16[4096,128]{1,0:T(8,128)(2,1)} fusion(bf16[4096,128]{1,0:T(8,128)(2,1)} %constant_dynamic-update-slice_fusion.3, bf16[1,128,128]{2,1,0:T(8,128)(2,1)S(1)} %copy-done.5, bf16[80,640]{1,0:T(8,128)(2,1)S(1)} %collective-permute-done.15, bf16[128,640]{1,0:T(8,128)(2,1)S(1)} %convolution_convert_fusion.25, ...), kind=kOutput, calls=%fused_computation.167 | convolution fusion | flops 64225280 | bytes 528384 | tf_op jit(solution)/shard_map/ct,cp->tp/dot_general | solution.py:233
  39.8 2.0 %collective-permute-done.14 = bf16[88,1024]{1,0:T(8,128)(2,1)S(1)} collective-permute-done((bf16[88,1024]{1,0:T(8,128)(2,1)S(1)}, bf16[88,1024]{1,0:T(8,128)(2,1)S(1)}, u32[]{:S(2)}, u32[]{:S(2)}) %collective-permute-start.14) | collective-permute-done | bytes 180256 | tf_op jit(solution)/shard_map/ppermute | solution.py:34
  42.1 1.1 %constant_dynamic-update-slice_fusion.1 = bf16[4096,128]{1,0:T(8,128)(2,1)} fusion(bf16[4096,128]{1,0:T(8,128)(2,1)} %constant_dynamic-update-slice_fusion.2, bf16[1,128,128]{2,1,0:T(8,128)(2,1)S(1)} %copy-done.5, bf16[80,896]{1,0:T(8,128)(2,1)S(1)} %collective-permute-done.12, bf16[128,896]{1,0:T(8,128)(2,1)S(1)} %copy-done.6, ...), kind=kOutput, calls=%fused_computation.166 | convolution fusion | flops 89915392 | bytes 700416 | tf_op jit(solution)/shard_map/ct,cp->tp/dot_general | solution.py:233
  43.3 0.5 %slice.183 = bf16[1,1]{1,0:T(2,128)(2,1)} slice(bf16[8,64]{1,0:T(8,128)(2,1)S(1)} %max.11), slice={[0:1], [0:1]} | slice | bytes 4 | tf_op jit(solution)/shard_map/slice | solution.py:337
  44.7 4.6 %collective-permute-done.17 = bf16[80,1280]{1,0:T(8,128)(2,1)S(1)} collective-permute-done((bf16[80,1280]{1,0:T(8,128)(2,1)S(1)}, bf16[80,1280]{1,0:T(8,128)(2,1)S(1)}, u32[]{:S(2)}, u32[]{:S(2)}) %collective-permute-start.17) | collective-permute-done | bytes 204832 | tf_op jit(solution)/shard_map/ppermute | solution.py:34
  49.3 1.2 %constant_dynamic-update-slice_fusion = bf16[4096,128]{1,0:T(8,128)(2,1)} fusion(bf16[4096,128]{1,0:T(8,128)(2,1)} %constant_dynamic-update-slice_fusion.1, bf16[1,128,128]{2,1,0:T(8,128)(2,1)S(1)} %copy-done.5, bf16[80,1280]{1,0:T(8,128)(2,1)S(1)} %collective-permute-done.17, bf16[128,1280]{1,0:T(8,128)(2,1)S(1)} %copy-done.7, ...), kind=kOutput, calls=%fused_computation.165 | convolution fusion | flops 128450560 | bytes 958464 | tf_op jit(solution)/shard_map/ct,cp->tp/dot_general | solution.py:233
  50.6 1.0 %collective-permute-done.18 = bf16[80,1024]{1,0:T(8,128)(2,1)S(1)} collective-permute-done((bf16[80,1024]{1,0:T(8,128)(2,1)S(1)}, bf16[80,1024]{1,0:T(8,128)(2,1)S(1)}, u32[]{:S(2)}, u32[]{:S(2)}) %collective-permute-start.18) | collective-permute-done | bytes 163872 | tf_op jit(solution)/shard_map/ppermute | solution.py:34
  51.5 1.2 %fusion.24 = bf16[4096,128]{1,0:T(8,128)(2,1)} fusion(bf16[4096,128]{1,0:T(8,128)(2,1)} %constant_dynamic-update-slice_fusion, bf16[80,1024]{1,0:T(8,128)(2,1)S(1)} %collective-permute-done.18, bf16[128,1024]{1,0:T(8,128)(2,1)S(1)} %convolution_convert_fusion.14, bf16[2,128,256]{2,1,0:T(8,128)(2,1)S(1)} %get-tuple-element.78, ...), kind=kOutput, calls=%fused_computation.44 | convolution fusion | flops 102760448 | bytes 786432 | tf_op jit(solution)/shard_map/ct,cp->tp/dot_general | solution.py:233
  (61 shorter events, 4.8 us)
Async XLA Ops:
  0.0 4.6 %copy-start = (bf16[4096,128]{1,0:T(8,128)(2,1)S(1)}, bf16[4096,128]{1,0:T(8,128)(2,1)}, u32[]{:S(2)}) copy-start(bf16[4096,128]{1,0:T(8,128)(2,1)} %refs_1_.2) | copy-start | bytes 3145732
  0.0 4.6 %copy-start.2 = (bf16[1,128,128]{2,1,0:T(8,128)(2,1)S(1)}, bf16[1,128,128]{2,1,0:T(8,128)(2,1)}, u32[]{:S(2)}) copy-start(bf16[1,128,128]{2,1,0:T(8,128)(2,1)} %refs_0_.1) | copy-start | bytes 98308
  0.0 6.8 %copy-start.4 = (s32[1,3,64]{2,0,1:T(1,128)S(1)}, s32[1,3,64]{2,0,1:T(1,128)}, u32[]{:S(2)}) copy-start(s32[1,3,64]{2,0,1:T(1,128)} %param.9) | copy-start | bytes 2308
  0.0 6.8 %copy-start.3 = (bf16[1,3,64,128]{3,2,1,0:T(8,128)(2,1)S(1)}, bf16[1,3,64,128]{3,2,1,0:T(8,128)(2,1)}, u32[]{:S(2)}) copy-start(bf16[1,3,64,128]{3,2,1,0:T(8,128)(2,1)} %refs_1_.3) | copy-start | bytes 147460
  1.5 6.5 %collective-permute-start.3 = (bf16[128,256]{1,0:T(8,128)(2,1)S(1)}, bf16[128,256]{1,0:T(8,128)(2,1)S(1)}, u32[]{:S(2)}, u32[]{:S(2)}) collective-permute-start(bf16[128,256]{1,0:T(8,128)(2,1)S(1)} %get-tuple-element.64), channel_id=1, source_target_pairs={{0,2},{2,0},{1,3},{3,1},{4,6},{6,4},{5,7},{7,5},{8,10},{10,8},{9,1... | collective-permute-start | bytes 196616 | tf_op jit(solution)/shard_map/ppermute | solution.py:34
  4.5 7.1 %collective-permute-start.5 = (bf16[128,640]{1,0:T(8,128)(2,1)S(1)}, bf16[128,640]{1,0:T(8,128)(2,1)S(1)}, u32[]{:S(2)}, u32[]{:S(2)}) collective-permute-start(bf16[128,640]{1,0:T(8,128)(2,1)S(1)} %get-tuple-element.68), channel_id=1, source_target_pairs={{0,2},{2,0},{1,3},{3,1},{4,6},{6,4},{5,7},{7,5},{8,10},{10,8},{9,1... | collective-permute-start | bytes 491528 | tf_op jit(solution)/shard_map/ppermute | solution.py:34
  4.8 13.7 %collective-permute-start.7 = (bf16[128,896]{1,0:T(8,128)(2,1)S(1)}, bf16[128,896]{1,0:T(8,128)(2,1)S(1)}, u32[]{:S(2)}, u32[]{:S(2)}) collective-permute-start(bf16[128,896]{1,0:T(8,128)(2,1)S(1)} %convolution_convert_fusion.21), channel_id=1, source_target_pairs={{0,2},{2,0},{1,3},{3,1},{4,6},{6,4},{5,7},{7,5},{8,10},{10,8},{9,1... | collective-permute-start | bytes 688136 | tf_op jit(solution)/shard_map/ppermute | solution.py:34
  8.2 5.8 %collective-permute-start.4 = (bf16[128,384]{1,0:T(8,128)(2,1)S(1)}, bf16[128,384]{1,0:T(8,128)(2,1)S(1)}, u32[]{:S(2)}, u32[]{:S(2)}) collective-permute-start(bf16[128,384]{1,0:T(8,128)(2,1)S(1)} %pad_maximum_fusion.12), channel_id=1, source_target_pairs={{0,4},{4,0},{8,12},{12,8},{1,5},{5,1},{9,13},{13,9},{2,6},{6,2},{1... | collective-permute-start | bytes 294920 | tf_op jit(solution)/shard_map/ppermute | solution.py:34
  11.8 9.0 %collective-permute-start.8 = (bf16[128,640]{1,0:T(8,128)(2,1)S(1)}, bf16[128,640]{1,0:T(8,128)(2,1)S(1)}, u32[]{:S(2)}, u32[]{:S(2)}) collective-permute-start(bf16[128,640]{1,0:T(8,128)(2,1)S(1)} %convolution_convert_fusion.26), channel_id=1, source_target_pairs={{0,4},{4,0},{8,12},{12,8},{1,5},{5,1},{9,13},{13,9},{2,6},{6,2},{1... | collective-permute-start | bytes 491528 | tf_op jit(solution)/shard_map/ppermute | solution.py:34
  14.3 6.4 %collective-permute-start.6 = (bf16[128,384]{1,0:T(8,128)(2,1)S(1)}, bf16[128,384]{1,0:T(8,128)(2,1)S(1)}, u32[]{:S(2)}, u32[]{:S(2)}) collective-permute-start(bf16[128,384]{1,0:T(8,128)(2,1)S(1)} %pad_maximum_fusion.13), channel_id=1, source_target_pairs={{0,8},{8,0},{4,12},{12,4},{1,9},{9,1},{5,13},{13,5},{2,10},{10,2},... | collective-permute-start | bytes 294920 | tf_op jit(solution)/shard_map/ppermute | solution.py:34
  17.0 7.7 %collective-permute-start.10 = (bf16[128,1280]{1,0:T(8,128)(2,1)S(1)}, bf16[128,1280]{1,0:T(8,128)(2,1)S(1)}, u32[]{:S(2)}, u32[]{:S(2)}) collective-permute-start(bf16[128,1280]{1,0:T(8,128)(2,1)S(1)} %convolution_convert_fusion.9), channel_id=1, source_target_pairs={{0,2},{2,0},{1,3},{3,1},{4,6},{6,4},{5,7},{7,5},{8,10},{10,8},{9,1... | collective-permute-start | bytes 983048 | tf_op jit(solution)/shard_map/ppermute | solution.py:34
  18.7 7.0 %collective-permute-start.9 = (bf16[88,896]{1,0:T(8,128)(2,1)S(1)}, bf16[88,896]{1,0:T(8,128)(2,1)S(1)}, u32[]{:S(2)}, u32[]{:S(2)}) collective-permute-start(bf16[88,896]{1,0:T(8,128)(2,1)S(1)} %convolution_convert_fusion.28), channel_id=1, source_target_pairs={{0,4},{4,0},{8,12},{12,8},{1,5},{5,1},{9,13},{13,9},{2,6},{6,2},{1... | collective-permute-start | bytes 473096 | tf_op jit(solution)/shard_map/ppermute | solution.py:34
  21.5 17.0 %collective-permute-start.15 = (bf16[80,640]{1,0:T(8,128)(2,1)S(1)}, bf16[80,640]{1,0:T(8,128)(2,1)S(1)}, u32[]{:S(2)}, u32[]{:S(2)}) collective-permute-start(bf16[80,640]{1,0:T(8,128)(2,1)S(1)} %convolution_convert_fusion.30), channel_id=1, source_target_pairs={{0,8},{8,0},{4,12},{12,4},{1,9},{9,1},{5,13},{13,5},{2,10},{10,2},... | collective-permute-start | bytes 307208 | tf_op jit(solution)/shard_map/ppermute | solution.py:34
  24.9 9.9 %collective-permute-start.16 = (bf16[88,1280]{1,0:T(8,128)(2,1)S(1)}, bf16[88,1280]{1,0:T(8,128)(2,1)S(1)}, u32[]{:S(2)}, u32[]{:S(2)}) collective-permute-start(bf16[88,1280]{1,0:T(8,128)(2,1)S(1)} %convolution_convert_fusion.10), channel_id=1, source_target_pairs={{0,4},{4,0},{8,12},{12,8},{1,5},{5,1},{9,13},{13,9},{2,6},{6,2},{1... | collective-permute-start | bytes 675848 | tf_op jit(solution)/shard_map/ppermute | solution.py:34
  26.0 4.7 %copy-start.5 = (bf16[1,128,128]{2,1,0:T(8,128)(2,1)S(1)}, bf16[1,128,128]{2,1,0:T(8,128)(2,1)}, u32[]{:S(2)}) copy-start(bf16[1,128,128]{2,1,0:T(8,128)(2,1)} %param.11) | copy-start | bytes 98308
  26.0 16.2 %collective-permute-start.12 = (bf16[80,896]{1,0:T(8,128)(2,1)S(1)}, bf16[80,896]{1,0:T(8,128)(2,1)S(1)}, u32[]{:S(2)}, u32[]{:S(2)}) collective-permute-start(bf16[80,896]{1,0:T(8,128)(2,1)S(1)} %convolution_convert_fusion.29), channel_id=1, source_target_pairs={{0,8},{8,0},{4,12},{12,4},{1,9},{9,1},{5,13},{13,5},{2,10},{10,2},... | collective-permute-start | bytes 430088 | tf_op jit(solution)/shard_map/ppermute | solution.py:34
  27.7 6.4 %collective-permute-start.13 = (bf16[128,1024]{1,0:T(8,128)(2,1)S(1)}, bf16[128,1024]{1,0:T(8,128)(2,1)S(1)}, u32[]{:S(2)}, u32[]{:S(2)}) collective-permute-start(bf16[128,1024]{1,0:T(8,128)(2,1)S(1)} %convolution_convert_fusion.16), channel_id=1, source_target_pairs={{0,2},{2,0},{1,3},{3,1},{4,6},{6,4},{5,7},{7,5},{8,10},{10,8},{9,1... | collective-permute-start | bytes 786440 | tf_op jit(solution)/shard_map/ppermute | solution.py:34
  29.7 13.6 %collective-permute-start.11 = (bf16[8,64]{1,0:T(8,128)(2,1)S(1)}, bf16[8,64]{1,0:T(8,128)(2,1)S(1)}, u32[]{:S(2)}, u32[]{:S(2)}) collective-permute-start(bf16[8,64]{1,0:T(8,128)(2,1)S(1)} %slice_maximum_fusion), channel_id=1, source_target_pairs={{0,2},{2,0},{1,3},{3,1},{4,6},{6,4},{5,7},{7,5},{8,10},{10,8},{9,1... | collective-permute-start | bytes 3080 | tf_op jit(solution)/shard_map/ppermute | solution.py:34
  34.3 7.5 %collective-permute-start.14 = (bf16[88,1024]{1,0:T(8,128)(2,1)S(1)}, bf16[88,1024]{1,0:T(8,128)(2,1)S(1)}, u32[]{:S(2)}, u32[]{:S(2)}) collective-permute-start(bf16[88,1024]{1,0:T(8,128)(2,1)S(1)} %convolution_convert_fusion.22), channel_id=1, source_target_pairs={{0,4},{4,0},{8,12},{12,8},{1,5},{5,1},{9,13},{13,9},{2,6},{6,2},{1... | collective-permute-start | bytes 540680 | tf_op jit(solution)/shard_map/ppermute | solution.py:34
  35.1 14.2 %collective-permute-start.17 = (bf16[80,1280]{1,0:T(8,128)(2,1)S(1)}, bf16[80,1280]{1,0:T(8,128)(2,1)S(1)}, u32[]{:S(2)}, u32[]{:S(2)}) collective-permute-start(bf16[80,1280]{1,0:T(8,128)(2,1)S(1)} %convolution_convert_fusion.11), channel_id=1, source_target_pairs={{0,8},{8,0},{4,12},{12,4},{1,9},{9,1},{5,13},{13,5},{2,10},{10,2},... | collective-permute-start | bytes 614408 | tf_op jit(solution)/shard_map/ppermute | solution.py:34
  39.8 2.3 %copy-start.6 = (bf16[128,896]{1,0:T(8,128)(2,1)S(1)}, bf16[128,896]{1,0:T(8,128)(2,1)}, u32[]{:S(2)}) copy-start(bf16[128,896]{1,0:T(8,128)(2,1)} %convolution_convert_fusion.19) | copy-start | bytes 688132
  42.0 9.5 %collective-permute-start.18 = (bf16[80,1024]{1,0:T(8,128)(2,1)S(1)}, bf16[80,1024]{1,0:T(8,128)(2,1)S(1)}, u32[]{:S(2)}, u32[]{:S(2)}) collective-permute-start(bf16[80,1024]{1,0:T(8,128)(2,1)S(1)} %convolution_convert_fusion.23), channel_id=1, source_target_pairs={{0,8},{8,0},{4,12},{12,4},{1,9},{9,1},{5,13},{13,5},{2,10},{10,2},... | collective-permute-start | bytes 491528 | tf_op jit(solution)/shard_map/ppermute | solution.py:34
  44.5 4.9 %copy-start.7 = (bf16[128,1280]{1,0:T(8,128)(2,1)S(1)}, bf16[128,1280]{1,0:T(8,128)(2,1)}, u32[]{:S(2)}) copy-start(bf16[128,1280]{1,0:T(8,128)(2,1)} %convolution_convert_fusion.7) | copy-start | bytes 983044

commit v23 on v22

--- a/solution.py
+++ b/solution.py
@@ -5,7 +5,7 @@
 from jax.experimental.pallas import tpu as pltpu
 from jax.sharding import PartitionSpec as P
 
-SHARES = (2, 5, 7, 10, 8)
+SHARES = (1, 5, 8, 10, 8)
 FULL_PIECES = (2, 1)
 EARLY_PIECES = 2
 COUNT_PIECE = 2

time: 52.9 us -> 53.2 us (level)
  waiting for transfers between devices: 12.6 us -> 13.5 us
  starting transfers between devices: 23.7 us -> 23.1 us
    ppermute x16, waiting for transfers between devices: 12.6 us -> 13.5 us  [from_partner(): return lax.ppermute(block, hop[0], route(*hop))]
    ppermute x16, starting transfers between devices: 23.7 us -> 23.1 us  [from_partner(): return lax.ppermute(block, hop[0], route(*hop))]
  transfers between devices with their start and end apart: 16 -> 16, of which waited for: 7 -> 6; matrix products, arithmetic and copies ran while one was open for 22% -> 22% of each run, Pallas kernels for 2% -> 2%
where the time goes in v23:
time: 53.2 us; the launch traced here: 53 us
  starting transfers between devices  23.1 us (43%)
  waiting for transfers between devices  13.5 us (25%)
  matrix products  12.2 us (23%)
  Pallas kernels  2.42 us (5%)
  between operations  1.01 us (2%)
  local copies, waits for them, and re-layouts  0.64 us (1%)
    ppermute x16, starting transfers between devices, from_partner(): return lax.ppermute(block, hop[0], route(*hop))  23.1 us
    ppermute x16, waiting for transfers between devices, from_partner(): return lax.ppermute(block, hop[0], route(*hop))  13.5 us
    dot_general x5, matrix products, evaluated(): jnp.einsum('ct,cp->tp', coeffs, evaluation, preferred_element_type=jnp.fl...  5.63 us
    dot_general x17, matrix products, times(): jnp.dot(matrix, value, preferred_element_type=jnp.float32)  5.09 us
    pallas_call x1, Pallas kernels, early(): pl.pallas_call(lambda *refs: early_kernel(starts, *refs), out_shape=[jax....  1.35 us
  transfers between devices with their start and end apart: 16, of which 6 were waited for; matrix products, arithmetic and copies ran while one was open for 22% of the time, Pallas kernels for 2%

profile of v23, /device:TPU:0, one launch (start us, length us, event | category | flops | bytes accessed | tf_op | source)
XLA Modules:
  0.0 53.0 jit_solution(5747106928391859517)
XLA Ops:
  0.0 1.4 %early.1 = (bf16[128,128]{1,0:T(8,128)(2,1)S(1)}, bf16[128,640]{1,0:T(8,128)(2,1)S(1)}) custom-call(bf16[1,128,128]{2,1,0:T(8,128)(2,1)} %refs_0_.1, bf16[4096,128]{1,0:T(8,128)(2,1)} %refs_1_.2), custom_call_target="tpu_custom_call" | custom-call | flops 25165824 | bytes 393216 | tf_op jit(solution)/shard_map/early/pallas_call | solution.py:70
  1.4 3.0 %collective-permute-start.3 = (bf16[128,128]{1,0:T(8,128)(2,1)S(1)}, bf16[128,128]{1,0:T(8,128)(2,1)S(1)}, u32[]{:S(2)}, u32[]{:S(2)}) collective-permute-start(bf16[128,128]{1,0:T(8,128)(2,1)S(1)} %get-tuple-element.64), channel_id=1, source_target_pairs={{0,2},{2,0},{1,3},{3,1},{4,6},{6,4},{5,7},{7,5},{8,10},{10,8},{9,1... | collective-permute-start | bytes 98312 | tf_op jit(solution)/shard_map/ppermute | solution.py:34
  4.7 2.0 %collective-permute-start.7 = (bf16[128,1024]{1,0:T(8,128)(2,1)S(1)}, bf16[128,1024]{1,0:T(8,128)(2,1)S(1)}, u32[]{:S(2)}, u32[]{:S(2)}) collective-permute-start(bf16[128,1024]{1,0:T(8,128)(2,1)S(1)} %convolution_convert_fusion.21), channel_id=1, source_target_pairs={{0,2},{2,0},{1,3},{3,1},{4,6},{6,4},{5,7},{7,5},{8,10},{10,8},{9,1... | collective-permute-start | bytes 786440 | tf_op jit(solution)/shard_map/ppermute | solution.py:34
  6.7 1.1 %tables.1 = (bf16[3,128,256]{2,1,0:T(8,128)(2,1)S(1)}, bf16[2,128,256]{2,1,0:T(8,128)(2,1)S(1)}, bf16[2,128,128]{2,1,0:T(8,128)(2,1)S(1)}) custom-call(s32[3,1,64]{2,1,0:T(1,128)S(1)} %bitcast.111, bf16[1,3,64,128]{3,2,1,0:T(8,128)(2,1)S(1)} %copy-done.3), custom_call_target="tpu_custom_call" | custom-call | flops 50000000 | bytes 600000 | tf_op jit(solution)/shard_map/tables/pallas_call | solution.py:156
  8.1 1.6 %collective-permute-start.4 = (bf16[128,256]{1,0:T(8,128)(2,1)S(1)}, bf16[128,256]{1,0:T(8,128)(2,1)S(1)}, u32[]{:S(2)}, u32[]{:S(2)}) collective-permute-start(bf16[128,256]{1,0:T(8,128)(2,1)S(1)} %pad_maximum_fusion.12), channel_id=1, source_target_pairs={{0,4},{4,0},{8,12},{12,8},{1,5},{5,1},{9,13},{13,9},{2,6},{6,2},{1... | collective-permute-start | bytes 196616 | tf_op jit(solution)/shard_map/ppermute | solution.py:34
  9.7 1.8 %collective-permute-done.5 = bf16[128,640]{1,0:T(8,128)(2,1)S(1)} collective-permute-done((bf16[128,640]{1,0:T(8,128)(2,1)S(1)}, bf16[128,640]{1,0:T(8,128)(2,1)S(1)}, u32[]{:S(2)}, u32[]{:S(2)}) %collective-permute-start.5) | collective-permute-done | bytes 163872 | tf_op jit(solution)/shard_map/ppermute | solution.py:34
  11.7 1.6 %collective-permute-start.8 = (bf16[128,640]{1,0:T(8,128)(2,1)S(1)}, bf16[128,640]{1,0:T(8,128)(2,1)S(1)}, u32[]{:S(2)}, u32[]{:S(2)}) collective-permute-start(bf16[128,640]{1,0:T(8,128)(2,1)S(1)} %convolution_convert_fusion.28), channel_id=1, source_target_pairs={{0,4},{4,0},{8,12},{12,8},{1,5},{5,1},{9,13},{13,9},{2,6},{6,2},{1... | collective-permute-start | bytes 491528 | tf_op jit(solution)/shard_map/ppermute | solution.py:34
  13.4 0.3 convolution_convert_fusion.9
  14.1 2.6 %collective-permute-start.6 = (bf16[128,256]{1,0:T(8,128)(2,1)S(1)}, bf16[128,256]{1,0:T(8,128)(2,1)S(1)}, u32[]{:S(2)}, u32[]{:S(2)}) collective-permute-start(bf16[128,256]{1,0:T(8,128)(2,1)S(1)} %pad_maximum_fusion.13), channel_id=1, source_target_pairs={{0,8},{8,0},{4,12},{12,4},{1,9},{9,1},{5,13},{13,5},{2,10},{10,2},... | collective-permute-start | bytes 196616 | tf_op jit(solution)/shard_map/ppermute | solution.py:34
  16.7 0.7 %collective-permute-start.10 = (bf16[128,1280]{1,0:T(8,128)(2,1)S(1)}, bf16[128,1280]{1,0:T(8,128)(2,1)S(1)}, u32[]{:S(2)}, u32[]{:S(2)}) collective-permute-start(bf16[128,1280]{1,0:T(8,128)(2,1)S(1)} %convolution_convert_fusion.9), channel_id=1, source_target_pairs={{0,2},{2,0},{1,3},{3,1},{4,6},{6,4},{5,7},{7,5},{8,10},{10,8},{9,1... | collective-permute-start | bytes 983048 | tf_op jit(solution)/shard_map/ppermute | solution.py:34
  17.9 0.9 %collective-permute-start.9 = (bf16[88,1024]{1,0:T(8,128)(2,1)S(1)}, bf16[88,1024]{1,0:T(8,128)(2,1)S(1)}, u32[]{:S(2)}, u32[]{:S(2)}) collective-permute-start(bf16[88,1024]{1,0:T(8,128)(2,1)S(1)} %convolution_convert_fusion.23), channel_id=1, source_target_pairs={{0,4},{4,0},{8,12},{12,8},{1,5},{5,1},{9,13},{13,9},{2,6},{6,2},{1... | collective-permute-start | bytes 540680 | tf_op jit(solution)/shard_map/ppermute | solution.py:34
  18.8 1.4 %collective-permute-done.6 = bf16[128,256]{1,0:T(8,128)(2,1)S(1)} collective-permute-done((bf16[128,256]{1,0:T(8,128)(2,1)S(1)}, bf16[128,256]{1,0:T(8,128)(2,1)S(1)}, u32[]{:S(2)}, u32[]{:S(2)}) %collective-permute-start.6) | collective-permute-done | bytes 65568 | tf_op jit(solution)/shard_map/ppermute | solution.py:34
  21.1 2.5 %collective-permute-start.15 = (bf16[80,640]{1,0:T(8,128)(2,1)S(1)}, bf16[80,640]{1,0:T(8,128)(2,1)S(1)}, u32[]{:S(2)}, u32[]{:S(2)}) collective-permute-start(bf16[80,640]{1,0:T(8,128)(2,1)S(1)} %convolution_convert_fusion.30), channel_id=1, source_target_pairs={{0,8},{8,0},{4,12},{12,4},{1,9},{9,1},{5,13},{13,5},{2,10},{10,2},... | collective-permute-start | bytes 307208 | tf_op jit(solution)/shard_map/ppermute | solution.py:34
  24.2 0.6 %collective-permute-start.16 = (bf16[88,1280]{1,0:T(8,128)(2,1)S(1)}, bf16[88,1280]{1,0:T(8,128)(2,1)S(1)}, u32[]{:S(2)}, u32[]{:S(2)}) collective-permute-start(bf16[88,1280]{1,0:T(8,128)(2,1)S(1)} %convolution_convert_fusion.10), channel_id=1, source_target_pairs={{0,4},{4,0},{8,12},{12,8},{1,5},{5,1},{9,13},{13,9},{2,6},{6,2},{1... | collective-permute-start | bytes 675848 | tf_op jit(solution)/shard_map/ppermute | solution.py:34
  24.9 0.3 convolution_convert_fusion.8
  25.4 2.7 %collective-permute-start.12 = (bf16[80,1024]{1,0:T(8,128)(2,1)S(1)}, bf16[80,1024]{1,0:T(8,128)(2,1)S(1)}, u32[]{:S(2)}, u32[]{:S(2)}) collective-permute-start(bf16[80,1024]{1,0:T(8,128)(2,1)S(1)} %convolution_convert_fusion.27), channel_id=1, source_target_pairs={{0,8},{8,0},{4,12},{12,4},{1,9},{9,1},{5,13},{13,5},{2,10},{10,2},... | collective-permute-start | bytes 491528 | tf_op jit(solution)/shard_map/ppermute | solution.py:34
  28.0 0.7 %collective-permute-start.13 = (bf16[128,1024]{1,0:T(8,128)(2,1)S(1)}, bf16[128,1024]{1,0:T(8,128)(2,1)S(1)}, u32[]{:S(2)}, u32[]{:S(2)}) collective-permute-start(bf16[128,1024]{1,0:T(8,128)(2,1)S(1)} %convolution_convert_fusion.18), channel_id=1, source_target_pairs={{0,2},{2,0},{1,3},{3,1},{4,6},{6,4},{5,7},{7,5},{8,10},{10,8},{9,1... | collective-permute-start | bytes 786440 | tf_op jit(solution)/shard_map/ppermute | solution.py:34
  28.7 0.9 %convolution_convert_fusion.19 = bf16[128,1024]{1,0:T(8,128)(2,1)} fusion(bf16[128,256]{1,0:T(8,128)(2,1)S(1)} %slice_bitcast_fusion.7, bf16[88,1024]{1,0:T(8,128)(2,1)S(1)} %collective-permute-done.9, bf16[128,1024]{1,0:T(8,128)(2,1)S(1)} %convolution_convert_fusion.20), kind=kOutput, calls=%fused_computation.51 | convolution fusion | flops 69074944 | bytes 770048 | tf_op jit(solution)/shard_map/dot_general | solution.py:223
  29.7 1.3 %collective-permute-start.11 = (bf16[8,64]{1,0:T(8,128)(2,1)S(1)}, bf16[8,64]{1,0:T(8,128)(2,1)S(1)}, u32[]{:S(2)}, u32[]{:S(2)}) collective-permute-start(bf16[8,64]{1,0:T(8,128)(2,1)S(1)} %slice_maximum_fusion), channel_id=1, source_target_pairs={{0,2},{2,0},{1,3},{3,1},{4,6},{6,4},{5,7},{7,5},{8,10},{10,8},{9,1... | collective-permute-start | bytes 3080 | tf_op jit(solution)/shard_map/ppermute | solution.py:34
  31.0 1.0 %constant_dynamic-update-slice_fusion.3 = bf16[4096,128]{1,0:T(8,128)(2,1)} fusion(bf16[1,128,128]{2,1,0:T(8,128)(2,1)S(1)} %copy-done.5, bf16[128,128]{1,0:T(8,128)(2,1)S(1)} %slice.182, bf16[128,128]{1,0:T(8,128)(2,1)S(1)} %convolution_convert_fusion.33, bf16[3,128,256]{2,1,0:T(8,128)(2,1)S(1)} %get-tuple-element.67), kind=kOutput, calls=%fused_computation.166 | convolution fusion | flops 12746751 | bytes 196608 | tf_op jit(solution)/shard_map/ct,cp->tp/dot_general | solution.py:233
  31.9 2.6 %collective-permute-done.13 = bf16[128,1024]{1,0:T(8,128)(2,1)S(1)} collective-permute-done((bf16[128,1024]{1,0:T(8,128)(2,1)S(1)}, bf16[128,1024]{1,0:T(8,128)(2,1)S(1)}, u32[]{:S(2)}, u32[]{:S(2)}) %collective-permute-start.13) | collective-permute-done | bytes 262176 | tf_op jit(solution)/shard_map/ppermute | solution.py:34
  34.8 0.4 collective-permute-start.14
  35.4 2.2 %collective-permute-start.17 = (bf16[80,1280]{1,0:T(8,128)(2,1)S(1)}, bf16[80,1280]{1,0:T(8,128)(2,1)S(1)}, u32[]{:S(2)}, u32[]{:S(2)}) collective-permute-start(bf16[80,1280]{1,0:T(8,128)(2,1)S(1)} %convolution_convert_fusion.11), channel_id=1, source_target_pairs={{0,8},{8,0},{4,12},{12,4},{1,9},{9,1},{5,13},{13,5},{2,10},{10,2},... | collective-permute-start | bytes 614408 | tf_op jit(solution)/shard_map/ppermute | solution.py:34
  37.6 1.0 %convolution_convert_fusion.7 = bf16[128,1280]{1,0:T(8,128)(2,1)} fusion(bf16[128,256]{1,0:T(8,128)(2,1)S(1)} %slice_bitcast_fusion.7, bf16[88,1280]{1,0:T(8,128)(2,1)S(1)} %collective-permute-done.16, bf16[128,1280]{1,0:T(8,128)(2,1)S(1)} %convolution_convert_fusion.8), kind=kOutput, calls=%fused_computation.32 | convolution fusion | flops 86343680 | bytes 946176 | tf_op jit(solution)/shard_map/dot_general | solution.py:223
  38.6 1.1 %constant_dynamic-update-slice_fusion.2 = bf16[4096,128]{1,0:T(8,128)(2,1)} fusion(bf16[4096,128]{1,0:T(8,128)(2,1)} %constant_dynamic-update-slice_fusion.3, bf16[1,128,128]{2,1,0:T(8,128)(2,1)S(1)} %copy-done.5, bf16[80,640]{1,0:T(8,128)(2,1)S(1)} %collective-permute-done.15, bf16[128,640]{1,0:T(8,128)(2,1)S(1)} %convolution_convert_fusion.26, ...), kind=kOutput, calls=%fused_computation.165 | convolution fusion | flops 64225280 | bytes 528384 | tf_op jit(solution)/shard_map/ct,cp->tp/dot_general | solution.py:233
  39.9 2.3 %collective-permute-done.14 = bf16[88,1024]{1,0:T(8,128)(2,1)S(1)} collective-permute-done((bf16[88,1024]{1,0:T(8,128)(2,1)S(1)}, bf16[88,1024]{1,0:T(8,128)(2,1)S(1)}, u32[]{:S(2)}, u32[]{:S(2)}) %collective-permute-start.14) | collective-permute-done | bytes 180256 | tf_op jit(solution)/shard_map/ppermute | solution.py:34
  42.6 1.2 %constant_dynamic-update-slice_fusion.1 = bf16[4096,128]{1,0:T(8,128)(2,1)} fusion(bf16[4096,128]{1,0:T(8,128)(2,1)} %constant_dynamic-update-slice_fusion.2, bf16[1,128,128]{2,1,0:T(8,128)(2,1)S(1)} %copy-done.5, bf16[80,1024]{1,0:T(8,128)(2,1)S(1)} %collective-permute-done.12, bf16[128,1024]{1,0:T(8,128)(2,1)S(1)} %copy-done.6, ...), kind=kOutput, calls=%fused_computation.164 | convolution fusion | flops 102760448 | bytes 786432 | tf_op jit(solution)/shard_map/ct,cp->tp/dot_general | solution.py:233
  43.7 0.6 %slice.183 = bf16[1,1]{1,0:T(2,128)(2,1)} slice(bf16[8,64]{1,0:T(8,128)(2,1)S(1)} %max.11), slice={[0:1], [0:1]} | slice | bytes 4 | tf_op jit(solution)/shard_map/slice | solution.py:337
  45.3 4.2 %collective-permute-done.17 = bf16[80,1280]{1,0:T(8,128)(2,1)S(1)} collective-permute-done((bf16[80,1280]{1,0:T(8,128)(2,1)S(1)}, bf16[80,1280]{1,0:T(8,128)(2,1)S(1)}, u32[]{:S(2)}, u32[]{:S(2)}) %collective-permute-start.17) | collective-permute-done | bytes 204832 | tf_op jit(solution)/shard_map/ppermute | solution.py:34
  49.5 1.2 %constant_dynamic-update-slice_fusion = bf16[4096,128]{1,0:T(8,128)(2,1)} fusion(bf16[4096,128]{1,0:T(8,128)(2,1)} %constant_dynamic-update-slice_fusion.1, bf16[1,128,128]{2,1,0:T(8,128)(2,1)S(1)} %copy-done.5, bf16[80,1280]{1,0:T(8,128)(2,1)S(1)} %collective-permute-done.17, bf16[128,1280]{1,0:T(8,128)(2,1)S(1)} %copy-done.7, ...), kind=kOutput, calls=%fused_computation.163 | convolution fusion | flops 128450560 | bytes 958464 | tf_op jit(solution)/shard_map/ct,cp->tp/dot_general | solution.py:233
  50.7 1.1 %collective-permute-done.18 = bf16[80,1024]{1,0:T(8,128)(2,1)S(1)} collective-permute-done((bf16[80,1024]{1,0:T(8,128)(2,1)S(1)}, bf16[80,1024]{1,0:T(8,128)(2,1)S(1)}, u32[]{:S(2)}, u32[]{:S(2)}) %collective-permute-start.18) | collective-permute-done | bytes 163872 | tf_op jit(solution)/shard_map/ppermute | solution.py:34
  51.8 1.2 %fusion.24 = bf16[4096,128]{1,0:T(8,128)(2,1)} fusion(bf16[4096,128]{1,0:T(8,128)(2,1)} %constant_dynamic-update-slice_fusion, bf16[80,1024]{1,0:T(8,128)(2,1)S(1)} %collective-permute-done.18, bf16[128,1024]{1,0:T(8,128)(2,1)S(1)} %convolution_convert_fusion.14, bf16[2,128,256]{2,1,0:T(8,128)(2,1)S(1)} %get-tuple-element.78, ...), kind=kOutput, calls=%fused_computation.44 | convolution fusion | flops 102760448 | bytes 786432 | tf_op jit(solution)/shard_map/ct,cp->tp/dot_general | solution.py:233
  (60 shorter events, 4.5 us)
Async XLA Ops:
  0.0 4.5 %copy-start = (bf16[4096,128]{1,0:T(8,128)(2,1)S(1)}, bf16[4096,128]{1,0:T(8,128)(2,1)}, u32[]{:S(2)}) copy-start(bf16[4096,128]{1,0:T(8,128)(2,1)} %refs_1_.2) | copy-start | bytes 3145732
  0.0 4.5 %copy-start.2 = (bf16[1,128,128]{2,1,0:T(8,128)(2,1)S(1)}, bf16[1,128,128]{2,1,0:T(8,128)(2,1)}, u32[]{:S(2)}) copy-start(bf16[1,128,128]{2,1,0:T(8,128)(2,1)} %refs_0_.1) | copy-start | bytes 98308
  0.0 6.7 %copy-start.4 = (s32[1,3,64]{2,0,1:T(1,128)S(1)}, s32[1,3,64]{2,0,1:T(1,128)}, u32[]{:S(2)}) copy-start(s32[1,3,64]{2,0,1:T(1,128)} %param.9) | copy-start | bytes 2308
  0.0 6.7 %copy-start.3 = (bf16[1,3,64,128]{3,2,1,0:T(8,128)(2,1)S(1)}, bf16[1,3,64,128]{3,2,1,0:T(8,128)(2,1)}, u32[]{:S(2)}) copy-start(bf16[1,3,64,128]{3,2,1,0:T(8,128)(2,1)} %refs_1_.3) | copy-start | bytes 147460
  1.4 6.5 %collective-permute-start.3 = (bf16[128,128]{1,0:T(8,128)(2,1)S(1)}, bf16[128,128]{1,0:T(8,128)(2,1)S(1)}, u32[]{:S(2)}, u32[]{:S(2)}) collective-permute-start(bf16[128,128]{1,0:T(8,128)(2,1)S(1)} %get-tuple-element.64), channel_id=1, source_target_pairs={{0,2},{2,0},{1,3},{3,1},{4,6},{6,4},{5,7},{7,5},{8,10},{10,8},{9,1... | collective-permute-start | bytes 98312 | tf_op jit(solution)/shard_map/ppermute | solution.py:34
  4.4 7.1 %collective-permute-start.5 = (bf16[128,640]{1,0:T(8,128)(2,1)S(1)}, bf16[128,640]{1,0:T(8,128)(2,1)S(1)}, u32[]{:S(2)}, u32[]{:S(2)}) collective-permute-start(bf16[128,640]{1,0:T(8,128)(2,1)S(1)} %get-tuple-element.68), channel_id=1, source_target_pairs={{0,2},{2,0},{1,3},{3,1},{4,6},{6,4},{5,7},{7,5},{8,10},{10,8},{9,1... | collective-permute-start | bytes 491528 | tf_op jit(solution)/shard_map/ppermute | solution.py:34
  4.7 12.9 %collective-permute-start.7 = (bf16[128,1024]{1,0:T(8,128)(2,1)S(1)}, bf16[128,1024]{1,0:T(8,128)(2,1)S(1)}, u32[]{:S(2)}, u32[]{:S(2)}) collective-permute-start(bf16[128,1024]{1,0:T(8,128)(2,1)S(1)} %convolution_convert_fusion.21), channel_id=1, source_target_pairs={{0,2},{2,0},{1,3},{3,1},{4,6},{6,4},{5,7},{7,5},{8,10},{10,8},{9,1... | collective-permute-start | bytes 786440 | tf_op jit(solution)/shard_map/ppermute | solution.py:34
  8.1 5.6 %collective-permute-start.4 = (bf16[128,256]{1,0:T(8,128)(2,1)S(1)}, bf16[128,256]{1,0:T(8,128)(2,1)S(1)}, u32[]{:S(2)}, u32[]{:S(2)}) collective-permute-start(bf16[128,256]{1,0:T(8,128)(2,1)S(1)} %pad_maximum_fusion.12), channel_id=1, source_target_pairs={{0,4},{4,0},{8,12},{12,8},{1,5},{5,1},{9,13},{13,9},{2,6},{6,2},{1... | collective-permute-start | bytes 196616 | tf_op jit(solution)/shard_map/ppermute | solution.py:34
  11.7 8.7 %collective-permute-start.8 = (bf16[128,640]{1,0:T(8,128)(2,1)S(1)}, bf16[128,640]{1,0:T(8,128)(2,1)S(1)}, u32[]{:S(2)}, u32[]{:S(2)}) collective-permute-start(bf16[128,640]{1,0:T(8,128)(2,1)S(1)} %convolution_convert_fusion.28), channel_id=1, source_target_pairs={{0,4},{4,0},{8,12},{12,8},{1,5},{5,1},{9,13},{13,9},{2,6},{6,2},{1... | collective-permute-start | bytes 491528 | tf_op jit(solution)/shard_map/ppermute | solution.py:34
  14.1 6.0 %collective-permute-start.6 = (bf16[128,256]{1,0:T(8,128)(2,1)S(1)}, bf16[128,256]{1,0:T(8,128)(2,1)S(1)}, u32[]{:S(2)}, u32[]{:S(2)}) collective-permute-start(bf16[128,256]{1,0:T(8,128)(2,1)S(1)} %pad_maximum_fusion.13), channel_id=1, source_target_pairs={{0,8},{8,0},{4,12},{12,4},{1,9},{9,1},{5,13},{13,5},{2,10},{10,2},... | collective-permute-start | bytes 196616 | tf_op jit(solution)/shard_map/ppermute | solution.py:34
  16.7 7.2 %collective-permute-start.10 = (bf16[128,1280]{1,0:T(8,128)(2,1)S(1)}, bf16[128,1280]{1,0:T(8,128)(2,1)S(1)}, u32[]{:S(2)}, u32[]{:S(2)}) collective-permute-start(bf16[128,1280]{1,0:T(8,128)(2,1)S(1)} %convolution_convert_fusion.9), channel_id=1, source_target_pairs={{0,2},{2,0},{1,3},{3,1},{4,6},{6,4},{5,7},{7,5},{8,10},{10,8},{9,1... | collective-permute-start | bytes 983048 | tf_op jit(solution)/shard_map/ppermute | solution.py:34
  17.9 7.2 %collective-permute-start.9 = (bf16[88,1024]{1,0:T(8,128)(2,1)S(1)}, bf16[88,1024]{1,0:T(8,128)(2,1)S(1)}, u32[]{:S(2)}, u32[]{:S(2)}) collective-permute-start(bf16[88,1024]{1,0:T(8,128)(2,1)S(1)} %convolution_convert_fusion.23), channel_id=1, source_target_pairs={{0,4},{4,0},{8,12},{12,8},{1,5},{5,1},{9,13},{13,9},{2,6},{6,2},{1... | collective-permute-start | bytes 540680 | tf_op jit(solution)/shard_map/ppermute | solution.py:34
  21.1 17.4 %collective-permute-start.15 = (bf16[80,640]{1,0:T(8,128)(2,1)S(1)}, bf16[80,640]{1,0:T(8,128)(2,1)S(1)}, u32[]{:S(2)}, u32[]{:S(2)}) collective-permute-start(bf16[80,640]{1,0:T(8,128)(2,1)S(1)} %convolution_convert_fusion.30), channel_id=1, source_target_pairs={{0,8},{8,0},{4,12},{12,4},{1,9},{9,1},{5,13},{13,5},{2,10},{10,2},... | collective-permute-start | bytes 307208 | tf_op jit(solution)/shard_map/ppermute | solution.py:34
  24.2 10.9 %collective-permute-start.16 = (bf16[88,1280]{1,0:T(8,128)(2,1)S(1)}, bf16[88,1280]{1,0:T(8,128)(2,1)S(1)}, u32[]{:S(2)}, u32[]{:S(2)}) collective-permute-start(bf16[88,1280]{1,0:T(8,128)(2,1)S(1)} %convolution_convert_fusion.10), channel_id=1, source_target_pairs={{0,4},{4,0},{8,12},{12,8},{1,5},{5,1},{9,13},{13,9},{2,6},{6,2},{1... | collective-permute-start | bytes 675848 | tf_op jit(solution)/shard_map/ppermute | solution.py:34
  25.3 5.6 %copy-start.5 = (bf16[1,128,128]{2,1,0:T(8,128)(2,1)S(1)}, bf16[1,128,128]{2,1,0:T(8,128)(2,1)}, u32[]{:S(2)}) copy-start(bf16[1,128,128]{2,1,0:T(8,128)(2,1)} %param.11) | copy-start | bytes 98308
  25.4 17.2 %collective-permute-start.12 = (bf16[80,1024]{1,0:T(8,128)(2,1)S(1)}, bf16[80,1024]{1,0:T(8,128)(2,1)S(1)}, u32[]{:S(2)}, u32[]{:S(2)}) collective-permute-start(bf16[80,1024]{1,0:T(8,128)(2,1)S(1)} %convolution_convert_fusion.27), channel_id=1, source_target_pairs={{0,8},{8,0},{4,12},{12,4},{1,9},{9,1},{5,13},{13,5},{2,10},{10,2},... | collective-permute-start | bytes 491528 | tf_op jit(solution)/shard_map/ppermute | solution.py:34
  28.0 6.5 %collective-permute-start.13 = (bf16[128,1024]{1,0:T(8,128)(2,1)S(1)}, bf16[128,1024]{1,0:T(8,128)(2,1)S(1)}, u32[]{:S(2)}, u32[]{:S(2)}) collective-permute-start(bf16[128,1024]{1,0:T(8,128)(2,1)S(1)} %convolution_convert_fusion.18), channel_id=1, source_target_pairs={{0,2},{2,0},{1,3},{3,1},{4,6},{6,4},{5,7},{7,5},{8,10},{10,8},{9,1... | collective-permute-start | bytes 786440 | tf_op jit(solution)/shard_map/ppermute | solution.py:34
  29.7 14.1 %collective-permute-start.11 = (bf16[8,64]{1,0:T(8,128)(2,1)S(1)}, bf16[8,64]{1,0:T(8,128)(2,1)S(1)}, u32[]{:S(2)}, u32[]{:S(2)}) collective-permute-start(bf16[8,64]{1,0:T(8,128)(2,1)S(1)} %slice_maximum_fusion), channel_id=1, source_target_pairs={{0,2},{2,0},{1,3},{3,1},{4,6},{6,4},{5,7},{7,5},{8,10},{10,8},{9,1... | collective-permute-start | bytes 3080 | tf_op jit(solution)/shard_map/ppermute | solution.py:34
  34.8 7.5 %collective-permute-start.14 = (bf16[88,1024]{1,0:T(8,128)(2,1)S(1)}, bf16[88,1024]{1,0:T(8,128)(2,1)S(1)}, u32[]{:S(2)}, u32[]{:S(2)}) collective-permute-start(bf16[88,1024]{1,0:T(8,128)(2,1)S(1)} %convolution_convert_fusion.22), channel_id=1, source_target_pairs={{0,4},{4,0},{8,12},{12,8},{1,5},{5,1},{9,13},{13,9},{2,6},{6,2},{1... | collective-permute-start | bytes 540680 | tf_op jit(solution)/shard_map/ppermute | solution.py:34
  35.4 14.1 %collective-permute-start.17 = (bf16[80,1280]{1,0:T(8,128)(2,1)S(1)}, bf16[80,1280]{1,0:T(8,128)(2,1)S(1)}, u32[]{:S(2)}, u32[]{:S(2)}) collective-permute-start(bf16[80,1280]{1,0:T(8,128)(2,1)S(1)} %convolution_convert_fusion.11), channel_id=1, source_target_pairs={{0,8},{8,0},{4,12},{12,4},{1,9},{9,1},{5,13},{13,5},{2,10},{10,2},... | collective-permute-start | bytes 614408 | tf_op jit(solution)/shard_map/ppermute | solution.py:34
  39.9 2.7 %copy-start.6 = (bf16[128,1024]{1,0:T(8,128)(2,1)S(1)}, bf16[128,1024]{1,0:T(8,128)(2,1)}, u32[]{:S(2)}) copy-start(bf16[128,1024]{1,0:T(8,128)(2,1)} %convolution_convert_fusion.19) | copy-start | bytes 786436
  42.5 9.4 %collective-permute-start.18 = (bf16[80,1024]{1,0:T(8,128)(2,1)S(1)}, bf16[80,1024]{1,0:T(8,128)(2,1)S(1)}, u32[]{:S(2)}, u32[]{:S(2)}) collective-permute-start(bf16[80,1024]{1,0:T(8,128)(2,1)S(1)} %convolution_convert_fusion.24), channel_id=1, source_target_pairs={{0,8},{8,0},{4,12},{12,4},{1,9},{9,1},{5,13},{13,5},{2,10},{10,2},... | collective-permute-start | bytes 491528 | tf_op jit(solution)/shard_map/ppermute | solution.py:34
  45.0 4.5 %copy-start.7 = (bf16[128,1280]{1,0:T(8,128)(2,1)S(1)}, bf16[128,1280]{1,0:T(8,128)(2,1)}, u32[]{:S(2)}) copy-start(bf16[128,1280]{1,0:T(8,128)(2,1)} %convolution_convert_fusion.7) | copy-start | bytes 983044

commit v24 on v23

--- a/solution.py
+++ b/solution.py
@@ -5,7 +5,7 @@
 from jax.experimental.pallas import tpu as pltpu
 from jax.sharding import PartitionSpec as P
 
-SHARES = (1, 5, 8, 10, 8)
+SHARES = (1, 6, 7, 9, 9)
 FULL_PIECES = (2, 1)
 EARLY_PIECES = 2
 COUNT_PIECE = 2

time: 53.2 us -> 53.8 us (1.011)
  the two profiles are of different devices: /device:TPU:0 before, /device:TPU:2 now
where the time goes in v24:
time: 53.8 us; the launch traced here: 53.6 us
  starting transfers between devices  19.3 us (36%)
  waiting for transfers between devices  17.1 us (32%)
  matrix products  13 us (24%)
  Pallas kernels  2.44 us (5%)
  between operations  1.01 us (2%)
  local copies, waits for them, and re-layouts  0.65 us (1%)
    ppermute x16, starting transfers between devices, from_partner(): return lax.ppermute(block, hop[0], route(*hop))  19.3 us
    ppermute x16, waiting for transfers between devices, from_partner(): return lax.ppermute(block, hop[0], route(*hop))  17.1 us
    dot_general x17, matrix products, times(): jnp.dot(matrix, value, preferred_element_type=jnp.float32)  5.84 us
    dot_general x5, matrix products, evaluated(): jnp.einsum('ct,cp->tp', coeffs, evaluation, preferred_element_type=jnp.fl...  5.61 us
    pallas_call x1, Pallas kernels, early(): pl.pallas_call(lambda *refs: early_kernel(starts, *refs), out_shape=[jax....  1.38 us
  transfers between devices with their start and end apart: 16, of which 7 were waited for; matrix products, arithmetic and copies ran while one was open for 23% of the time, Pallas kernels for 2%

profile of v24, /device:TPU:2, one launch (start us, length us, event | category | flops | bytes accessed | tf_op | source)
XLA Modules:
  0.0 53.6 jit_solution(260634161604752369)
XLA Ops:
  0.0 1.4 %early.1 = (bf16[128,128]{1,0:T(8,128)(2,1)S(1)}, bf16[128,768]{1,0:T(8,128)(2,1)S(1)}) custom-call(bf16[1,128,128]{2,1,0:T(8,128)(2,1)} %refs_0_.1, bf16[4096,128]{1,0:T(8,128)(2,1)} %refs_1_.2), custom_call_target="tpu_custom_call" | custom-call | flops 29360128 | bytes 458752 | tf_op jit(solution)/shard_map/early/pallas_call | solution.py:70
  1.5 2.0 %collective-permute-start.5 = (bf16[128,768]{1,0:T(8,128)(2,1)S(1)}, bf16[128,768]{1,0:T(8,128)(2,1)S(1)}, u32[]{:S(2)}, u32[]{:S(2)}) collective-permute-start(bf16[128,768]{1,0:T(8,128)(2,1)S(1)} %get-tuple-element.68), channel_id=1, source_target_pairs={{0,2},{2,0},{1,3},{3,1},{4,6},{6,4},{5,7},{7,5},{8,10},{10,8},{9,1... | collective-permute-start | bytes 589832 | tf_op jit(solution)/shard_map/ppermute | solution.py:34
  3.9 1.1 %tables.1 = (bf16[3,128,256]{2,1,0:T(8,128)(2,1)S(1)}, bf16[2,128,256]{2,1,0:T(8,128)(2,1)S(1)}, bf16[2,128,128]{2,1,0:T(8,128)(2,1)S(1)}) custom-call(s32[3,1,64]{2,1,0:T(1,128)S(1)} %bitcast.111, bf16[1,3,64,128]{3,2,1,0:T(8,128)(2,1)S(1)} %copy-done.3), custom_call_target="tpu_custom_call" | custom-call | flops 50000000 | bytes 600000 | tf_op jit(solution)/shard_map/tables/pallas_call | solution.py:156
  5.0 0.7 %collective-permute-done.3 = bf16[128,128]{1,0:T(8,128)(2,1)S(1)} collective-permute-done((bf16[128,128]{1,0:T(8,128)(2,1)S(1)}, bf16[128,128]{1,0:T(8,128)(2,1)S(1)}, u32[]{:S(2)}, u32[]{:S(2)}) %collective-permute-start.3) | collective-permute-done | bytes 32800 | tf_op jit(solution)/shard_map/ppermute | solution.py:34
  5.9 1.6 %collective-permute-start.4 = (bf16[128,256]{1,0:T(8,128)(2,1)S(1)}, bf16[128,256]{1,0:T(8,128)(2,1)S(1)}, u32[]{:S(2)}, u32[]{:S(2)}) collective-permute-start(bf16[128,256]{1,0:T(8,128)(2,1)S(1)} %pad_maximum_fusion.12), channel_id=1, source_target_pairs={{0,4},{4,0},{8,12},{12,8},{1,5},{5,1},{9,13},{13,9},{2,6},{6,2},{1... | collective-permute-start | bytes 196616 | tf_op jit(solution)/shard_map/ppermute | solution.py:34
  7.6 2.4 %collective-permute-done.5 = bf16[128,768]{1,0:T(8,128)(2,1)S(1)} collective-permute-done((bf16[128,768]{1,0:T(8,128)(2,1)S(1)}, bf16[128,768]{1,0:T(8,128)(2,1)S(1)}, u32[]{:S(2)}, u32[]{:S(2)}) %collective-permute-start.5) | collective-permute-done | bytes 196640 | tf_op jit(solution)/shard_map/ppermute | solution.py:34
  10.2 1.6 %collective-permute-start.8 = (bf16[128,768]{1,0:T(8,128)(2,1)S(1)}, bf16[128,768]{1,0:T(8,128)(2,1)S(1)}, u32[]{:S(2)}, u32[]{:S(2)}) collective-permute-start(bf16[128,768]{1,0:T(8,128)(2,1)S(1)} %convolution_convert_fusion.27), channel_id=1, source_target_pairs={{0,4},{4,0},{8,12},{12,8},{1,5},{5,1},{9,13},{13,9},{2,6},{6,2},{1... | collective-permute-start | bytes 589832 | tf_op jit(solution)/shard_map/ppermute | solution.py:34
  11.8 0.3 convolution_convert_fusion.14
  12.1 0.3 convolution_convert_fusion.13
  12.7 2.7 %collective-permute-start.6 = (bf16[128,256]{1,0:T(8,128)(2,1)S(1)}, bf16[128,256]{1,0:T(8,128)(2,1)S(1)}, u32[]{:S(2)}, u32[]{:S(2)}) collective-permute-start(bf16[128,256]{1,0:T(8,128)(2,1)S(1)} %pad_maximum_fusion.13), channel_id=1, source_target_pairs={{0,8},{8,0},{4,12},{12,4},{1,9},{9,1},{5,13},{13,5},{2,10},{10,2},... | collective-permute-start | bytes 196616 | tf_op jit(solution)/shard_map/ppermute | solution.py:34
  15.3 1.4 %collective-permute-start.10 = (bf16[128,1152]{1,0:T(8,128)(2,1)S(1)}, bf16[128,1152]{1,0:T(8,128)(2,1)S(1)}, u32[]{:S(2)}, u32[]{:S(2)}) collective-permute-start(bf16[128,1152]{1,0:T(8,128)(2,1)S(1)} %convolution_convert_fusion.14), channel_id=1, source_target_pairs={{0,2},{2,0},{1,3},{3,1},{4,6},{6,4},{5,7},{7,5},{8,10},{10,8},{9,1... | collective-permute-start | bytes 884744 | tf_op jit(solution)/shard_map/ppermute | solution.py:34
  17.0 0.5 collective-permute-start.9
  17.8 0.3 collective-permute-done.6
  18.8 3.4 %collective-permute-start.15 = (bf16[80,768]{1,0:T(8,128)(2,1)S(1)}, bf16[80,768]{1,0:T(8,128)(2,1)S(1)}, u32[]{:S(2)}, u32[]{:S(2)}) collective-permute-start(bf16[80,768]{1,0:T(8,128)(2,1)S(1)} %convolution_convert_fusion.30), channel_id=1, source_target_pairs={{0,8},{8,0},{4,12},{12,4},{1,9},{9,1},{5,13},{13,5},{2,10},{10,2},... | collective-permute-start | bytes 368648 | tf_op jit(solution)/shard_map/ppermute | solution.py:34
  22.9 1.0 %convolution_convert_fusion.11 = bf16[128,1152]{1,0:T(8,128)(2,1)} fusion(bf16[128,256]{1,0:T(8,128)(2,1)S(1)} %get-tuple-element.88, bf16[128,1152]{1,0:T(8,128)(2,1)S(1)} %collective-permute-done.10, bf16[128,1152]{1,0:T(8,128)(2,1)S(1)} %convolution_convert_fusion.14), kind=kOutput, calls=%fused_computation.37 | convolution fusion | flops 76824576 | bytes 950272 | tf_op jit(solution)/shard_map/dot_general | solution.py:223
  23.9 1.4 %collective-permute-done.9 = bf16[88,896]{1,0:T(8,128)(2,1)S(1)} collective-permute-done((bf16[88,896]{1,0:T(8,128)(2,1)S(1)}, bf16[88,896]{1,0:T(8,128)(2,1)S(1)}, u32[]{:S(2)}, u32[]{:S(2)}) %collective-permute-start.9) | collective-permute-done | bytes 157728 | tf_op jit(solution)/shard_map/ppermute | solution.py:34
  25.5 0.3 collective-permute-start.12
  25.8 1.4 %collective-permute-start.13 = (bf16[128,1152]{1,0:T(8,128)(2,1)S(1)}, bf16[128,1152]{1,0:T(8,128)(2,1)S(1)}, u32[]{:S(2)}, u32[]{:S(2)}) collective-permute-start(bf16[128,1152]{1,0:T(8,128)(2,1)S(1)} %convolution_convert_fusion.13), channel_id=1, source_target_pairs={{0,2},{2,0},{1,3},{3,1},{4,6},{6,4},{5,7},{7,5},{8,10},{10,8},{9,1... | collective-permute-start | bytes 884744 | tf_op jit(solution)/shard_map/ppermute | solution.py:34
  27.2 0.9 %convolution_convert_fusion.21 = bf16[128,896]{1,0:T(8,128)(2,1)} fusion(bf16[128,256]{1,0:T(8,128)(2,1)S(1)} %slice_bitcast_fusion.7, bf16[88,896]{1,0:T(8,128)(2,1)S(1)} %collective-permute-done.9, bf16[128,896]{1,0:T(8,128)(2,1)S(1)} %convolution_convert_fusion.22), kind=kOutput, calls=%fused_computation.47 | convolution fusion | flops 60440576 | bytes 681984 | tf_op jit(solution)/shard_map/dot_general | solution.py:223
  28.2 0.6 %collective-permute-start.11 = (bf16[8,64]{1,0:T(8,128)(2,1)S(1)}, bf16[8,64]{1,0:T(8,128)(2,1)S(1)}, u32[]{:S(2)}, u32[]{:S(2)}) collective-permute-start(bf16[8,64]{1,0:T(8,128)(2,1)S(1)} %slice_maximum_fusion), channel_id=1, source_target_pairs={{0,2},{2,0},{1,3},{3,1},{4,6},{6,4},{5,7},{7,5},{8,10},{10,8},{9,1... | collective-permute-start | bytes 3080 | tf_op jit(solution)/shard_map/ppermute | solution.py:34
  28.8 1.0 %constant_dynamic-update-slice_fusion.3 = bf16[4096,128]{1,0:T(8,128)(2,1)} fusion(bf16[1,128,128]{2,1,0:T(8,128)(2,1)S(1)} %copy-done.5, bf16[128,128]{1,0:T(8,128)(2,1)S(1)} %slice.182, bf16[128,128]{1,0:T(8,128)(2,1)S(1)} %convolution_convert_fusion.33, bf16[3,128,256]{2,1,0:T(8,128)(2,1)S(1)} %get-tuple-element.67), kind=kOutput, calls=%fused_computation.166 | convolution fusion | flops 12746751 | bytes 196608 | tf_op jit(solution)/shard_map/ct,cp->tp/dot_general | solution.py:233
  29.7 2.8 %collective-permute-done.13 = bf16[128,1152]{1,0:T(8,128)(2,1)S(1)} collective-permute-done((bf16[128,1152]{1,0:T(8,128)(2,1)S(1)}, bf16[128,1152]{1,0:T(8,128)(2,1)S(1)}, u32[]{:S(2)}, u32[]{:S(2)}) %collective-permute-start.13) | collective-permute-done | bytes 294944 | tf_op jit(solution)/shard_map/ppermute | solution.py:34
  33.0 2.7 %collective-permute-start.17 = (bf16[80,1152]{1,0:T(8,128)(2,1)S(1)}, bf16[80,1152]{1,0:T(8,128)(2,1)S(1)}, u32[]{:S(2)}, u32[]{:S(2)}) collective-permute-start(bf16[80,1152]{1,0:T(8,128)(2,1)S(1)} %convolution_convert_fusion.18), channel_id=1, source_target_pairs={{0,8},{8,0},{4,12},{12,4},{1,9},{9,1},{5,13},{13,5},{2,10},{10,2},... | collective-permute-start | bytes 552968 | tf_op jit(solution)/shard_map/ppermute | solution.py:34
  35.8 0.6 %collective-permute-start.14 = (bf16[88,1152]{1,0:T(8,128)(2,1)S(1)}, bf16[88,1152]{1,0:T(8,128)(2,1)S(1)}, u32[]{:S(2)}, u32[]{:S(2)}) collective-permute-start(bf16[88,1152]{1,0:T(8,128)(2,1)S(1)} %convolution_convert_fusion.15), channel_id=1, source_target_pairs={{0,4},{4,0},{8,12},{12,8},{1,5},{5,1},{9,13},{13,9},{2,6},{6,2},{1... | collective-permute-start | bytes 608264 | tf_op jit(solution)/shard_map/ppermute | solution.py:34
  36.4 1.0 %convolution_convert_fusion.12 = bf16[128,1152]{1,0:T(8,128)(2,1)} fusion(bf16[128,256]{1,0:T(8,128)(2,1)S(1)} %get-tuple-element.88, bf16[128,1152]{1,0:T(8,128)(2,1)S(1)} %collective-permute-done.13, bf16[128,1152]{1,0:T(8,128)(2,1)S(1)} %convolution_convert_fusion.13), kind=kOutput, calls=%fused_computation.38 | convolution fusion | flops 76824576 | bytes 950272 | tf_op jit(solution)/shard_map/dot_general | solution.py:223
  37.4 1.1 %constant_dynamic-update-slice_fusion.2 = bf16[4096,128]{1,0:T(8,128)(2,1)} fusion(bf16[4096,128]{1,0:T(8,128)(2,1)} %constant_dynamic-update-slice_fusion.3, bf16[1,128,128]{2,1,0:T(8,128)(2,1)S(1)} %copy-done.5, bf16[80,768]{1,0:T(8,128)(2,1)S(1)} %collective-permute-done.15, bf16[128,768]{1,0:T(8,128)(2,1)S(1)} %convolution_convert_fusion.26, ...), kind=kOutput, calls=%fused_computation.165 | convolution fusion | flops 77070336 | bytes 614400 | tf_op jit(solution)/shard_map/ct,cp->tp/dot_general | solution.py:233
  38.7 5.0 %collective-permute-done.14 = bf16[88,1152]{1,0:T(8,128)(2,1)S(1)} collective-permute-done((bf16[88,1152]{1,0:T(8,128)(2,1)S(1)}, bf16[88,1152]{1,0:T(8,128)(2,1)S(1)}, u32[]{:S(2)}, u32[]{:S(2)}) %collective-permute-start.14) | collective-permute-done | bytes 202784 | tf_op jit(solution)/shard_map/ppermute | solution.py:34
  44.1 1.1 %constant_dynamic-update-slice_fusion.1 = bf16[4096,128]{1,0:T(8,128)(2,1)} fusion(bf16[4096,128]{1,0:T(8,128)(2,1)} %constant_dynamic-update-slice_fusion.2, bf16[1,128,128]{2,1,0:T(8,128)(2,1)S(1)} %copy-done.5, bf16[80,896]{1,0:T(8,128)(2,1)S(1)} %collective-permute-done.12, bf16[128,896]{1,0:T(8,128)(2,1)S(1)} %copy-done.8, ...), kind=kOutput, calls=%fused_computation.164 | convolution fusion | flops 89915392 | bytes 700416 | tf_op jit(solution)/shard_map/ct,cp->tp/dot_general | solution.py:233
  45.2 0.6 %slice.183 = bf16[1,1]{1,0:T(2,128)(2,1)} slice(bf16[8,64]{1,0:T(8,128)(2,1)S(1)} %max.11), slice={[0:1], [0:1]} | slice | bytes 4 | tf_op jit(solution)/shard_map/slice | solution.py:337
  46.5 1.2 %constant_dynamic-update-slice_fusion = bf16[4096,128]{1,0:T(8,128)(2,1)} fusion(bf16[4096,128]{1,0:T(8,128)(2,1)} %constant_dynamic-update-slice_fusion.1, bf16[1,128,128]{2,1,0:T(8,128)(2,1)S(1)} %copy-done.5, bf16[80,1152]{1,0:T(8,128)(2,1)S(1)} %collective-permute-done.17, bf16[128,1152]{1,0:T(8,128)(2,1)S(1)} %convolution_convert_fusion.10, ...), kind=kOutput, calls=%fused_computation.163 | convolution fusion | flops 115605504 | bytes 872448 | tf_op jit(solution)/shard_map/ct,cp->tp/dot_general | solution.py:233
  47.9 4.5 %collective-permute-done.18 = bf16[80,1152]{1,0:T(8,128)(2,1)S(1)} collective-permute-done((bf16[80,1152]{1,0:T(8,128)(2,1)S(1)}, bf16[80,1152]{1,0:T(8,128)(2,1)S(1)}, u32[]{:S(2)}, u32[]{:S(2)}) %collective-permute-start.18) | collective-permute-done | bytes 184352 | tf_op jit(solution)/shard_map/ppermute | solution.py:34
  52.4 1.2 %fusion.20 = bf16[4096,128]{1,0:T(8,128)(2,1)} fusion(bf16[4096,128]{1,0:T(8,128)(2,1)} %constant_dynamic-update-slice_fusion, bf16[80,1152]{1,0:T(8,128)(2,1)S(1)} %collective-permute-done.18, bf16[128,1152]{1,0:T(8,128)(2,1)S(1)} %convolution_convert_fusion.7, bf16[2,128,256]{2,1,0:T(8,128)(2,1)S(1)} %get-tuple-element.78, ...), kind=kOutput, calls=%fused_computation.31 | convolution fusion | flops 115605504 | bytes 872448 | tf_op jit(solution)/shard_map/ct,cp->tp/dot_general | solution.py:233
  (62 shorter events, 4.6 us)
Async XLA Ops:
  0.0 3.5 %copy-start = (bf16[4096,128]{1,0:T(8,128)(2,1)S(1)}, bf16[4096,128]{1,0:T(8,128)(2,1)}, u32[]{:S(2)}) copy-start(bf16[4096,128]{1,0:T(8,128)(2,1)} %refs_1_.2) | copy-start | bytes 3145732
  0.0 3.5 %copy-start.2 = (bf16[1,128,128]{2,1,0:T(8,128)(2,1)S(1)}, bf16[1,128,128]{2,1,0:T(8,128)(2,1)}, u32[]{:S(2)}) copy-start(bf16[1,128,128]{2,1,0:T(8,128)(2,1)} %refs_0_.1) | copy-start | bytes 98308
  0.0 3.9 %copy-start.4 = (s32[1,3,64]{2,0,1:T(1,128)S(1)}, s32[1,3,64]{2,0,1:T(1,128)}, u32[]{:S(2)}) copy-start(s32[1,3,64]{2,0,1:T(1,128)} %param.9) | copy-start | bytes 2308
  0.0 3.9 %copy-start.3 = (bf16[1,3,64,128]{3,2,1,0:T(8,128)(2,1)S(1)}, bf16[1,3,64,128]{3,2,1,0:T(8,128)(2,1)}, u32[]{:S(2)}) copy-start(bf16[1,3,64,128]{3,2,1,0:T(8,128)(2,1)} %refs_1_.3) | copy-start | bytes 147460
  1.4 4.3 %collective-permute-start.3 = (bf16[128,128]{1,0:T(8,128)(2,1)S(1)}, bf16[128,128]{1,0:T(8,128)(2,1)S(1)}, u32[]{:S(2)}, u32[]{:S(2)}) collective-permute-start(bf16[128,128]{1,0:T(8,128)(2,1)S(1)} %get-tuple-element.64), channel_id=1, source_target_pairs={{0,2},{2,0},{1,3},{3,1},{4,6},{6,4},{5,7},{7,5},{8,10},{10,8},{9,1... | collective-permute-start | bytes 98312 | tf_op jit(solution)/shard_map/ppermute | solution.py:34
  1.5 8.5 %collective-permute-start.5 = (bf16[128,768]{1,0:T(8,128)(2,1)S(1)}, bf16[128,768]{1,0:T(8,128)(2,1)S(1)}, u32[]{:S(2)}, u32[]{:S(2)}) collective-permute-start(bf16[128,768]{1,0:T(8,128)(2,1)S(1)} %get-tuple-element.68), channel_id=1, source_target_pairs={{0,2},{2,0},{1,3},{3,1},{4,6},{6,4},{5,7},{7,5},{8,10},{10,8},{9,1... | collective-permute-start | bytes 589832 | tf_op jit(solution)/shard_map/ppermute | solution.py:34
  3.8 13.1 %collective-permute-start.7 = (bf16[128,896]{1,0:T(8,128)(2,1)S(1)}, bf16[128,896]{1,0:T(8,128)(2,1)S(1)}, u32[]{:S(2)}, u32[]{:S(2)}) collective-permute-start(bf16[128,896]{1,0:T(8,128)(2,1)S(1)} %convolution_convert_fusion.23), channel_id=1, source_target_pairs={{0,2},{2,0},{1,3},{3,1},{4,6},{6,4},{5,7},{7,5},{8,10},{10,8},{9,1... | collective-permute-start | bytes 688136 | tf_op jit(solution)/shard_map/ppermute | solution.py:34
  5.9 6.4 %collective-permute-start.4 = (bf16[128,256]{1,0:T(8,128)(2,1)S(1)}, bf16[128,256]{1,0:T(8,128)(2,1)S(1)}, u32[]{:S(2)}, u32[]{:S(2)}) collective-permute-start(bf16[128,256]{1,0:T(8,128)(2,1)S(1)} %pad_maximum_fusion.12), channel_id=1, source_target_pairs={{0,4},{4,0},{8,12},{12,8},{1,5},{5,1},{9,13},{13,9},{2,6},{6,2},{1... | collective-permute-start | bytes 196616 | tf_op jit(solution)/shard_map/ppermute | solution.py:34
  10.2 7.9 %collective-permute-start.8 = (bf16[128,768]{1,0:T(8,128)(2,1)S(1)}, bf16[128,768]{1,0:T(8,128)(2,1)S(1)}, u32[]{:S(2)}, u32[]{:S(2)}) collective-permute-start(bf16[128,768]{1,0:T(8,128)(2,1)S(1)} %convolution_convert_fusion.27), channel_id=1, source_target_pairs={{0,4},{4,0},{8,12},{12,8},{1,5},{5,1},{9,13},{13,9},{2,6},{6,2},{1... | collective-permute-start | bytes 589832 | tf_op jit(solution)/shard_map/ppermute | solution.py:34
  12.7 5.4 %collective-permute-start.6 = (bf16[128,256]{1,0:T(8,128)(2,1)S(1)}, bf16[128,256]{1,0:T(8,128)(2,1)S(1)}, u32[]{:S(2)}, u32[]{:S(2)}) collective-permute-start(bf16[128,256]{1,0:T(8,128)(2,1)S(1)} %pad_maximum_fusion.13), channel_id=1, source_target_pairs={{0,8},{8,0},{4,12},{12,4},{1,9},{9,1},{5,13},{13,5},{2,10},{10,2},... | collective-permute-start | bytes 196616 | tf_op jit(solution)/shard_map/ppermute | solution.py:34
  15.3 7.3 %collective-permute-start.10 = (bf16[128,1152]{1,0:T(8,128)(2,1)S(1)}, bf16[128,1152]{1,0:T(8,128)(2,1)S(1)}, u32[]{:S(2)}, u32[]{:S(2)}) collective-permute-start(bf16[128,1152]{1,0:T(8,128)(2,1)S(1)} %convolution_convert_fusion.14), channel_id=1, source_target_pairs={{0,2},{2,0},{1,3},{3,1},{4,6},{6,4},{5,7},{7,5},{8,10},{10,8},{9,1... | collective-permute-start | bytes 884744 | tf_op jit(solution)/shard_map/ppermute | solution.py:34
  17.0 8.2 %collective-permute-start.9 = (bf16[88,896]{1,0:T(8,128)(2,1)S(1)}, bf16[88,896]{1,0:T(8,128)(2,1)S(1)}, u32[]{:S(2)}, u32[]{:S(2)}) collective-permute-start(bf16[88,896]{1,0:T(8,128)(2,1)S(1)} %convolution_convert_fusion.28), channel_id=1, source_target_pairs={{0,4},{4,0},{8,12},{12,8},{1,5},{5,1},{9,13},{13,9},{2,6},{6,2},{1... | collective-permute-start | bytes 473096 | tf_op jit(solution)/shard_map/ppermute | solution.py:34
  18.8 18.5 %collective-permute-start.15 = (bf16[80,768]{1,0:T(8,128)(2,1)S(1)}, bf16[80,768]{1,0:T(8,128)(2,1)S(1)}, u32[]{:S(2)}, u32[]{:S(2)}) collective-permute-start(bf16[80,768]{1,0:T(8,128)(2,1)S(1)} %convolution_convert_fusion.30), channel_id=1, source_target_pairs={{0,8},{8,0},{4,12},{12,4},{1,9},{9,1},{5,13},{13,5},{2,10},{10,2},... | collective-permute-start | bytes 368648 | tf_op jit(solution)/shard_map/ppermute | solution.py:34
  22.8 9.9 %collective-permute-start.16 = (bf16[88,1152]{1,0:T(8,128)(2,1)S(1)}, bf16[88,1152]{1,0:T(8,128)(2,1)S(1)}, u32[]{:S(2)}, u32[]{:S(2)}) collective-permute-start(bf16[88,1152]{1,0:T(8,128)(2,1)S(1)} %convolution_convert_fusion.16), channel_id=1, source_target_pairs={{0,4},{4,0},{8,12},{12,8},{1,5},{5,1},{9,13},{13,9},{2,6},{6,2},{1... | collective-permute-start | bytes 608264 | tf_op jit(solution)/shard_map/ppermute | solution.py:34
  25.5 3.3 %copy-start.5 = (bf16[1,128,128]{2,1,0:T(8,128)(2,1)S(1)}, bf16[1,128,128]{2,1,0:T(8,128)(2,1)}, u32[]{:S(2)}) copy-start(bf16[1,128,128]{2,1,0:T(8,128)(2,1)} %param.11) | copy-start | bytes 98308
  25.5 18.6 %collective-permute-start.12 = (bf16[80,896]{1,0:T(8,128)(2,1)S(1)}, bf16[80,896]{1,0:T(8,128)(2,1)S(1)}, u32[]{:S(2)}, u32[]{:S(2)}) collective-permute-start(bf16[80,896]{1,0:T(8,128)(2,1)S(1)} %convolution_convert_fusion.29), channel_id=1, source_target_pairs={{0,8},{8,0},{4,12},{12,4},{1,9},{9,1},{5,13},{13,5},{2,10},{10,2},... | collective-permute-start | bytes 430088 | tf_op jit(solution)/shard_map/ppermute | solution.py:34
  25.8 6.7 %collective-permute-start.13 = (bf16[128,1152]{1,0:T(8,128)(2,1)S(1)}, bf16[128,1152]{1,0:T(8,128)(2,1)S(1)}, u32[]{:S(2)}, u32[]{:S(2)}) collective-permute-start(bf16[128,1152]{1,0:T(8,128)(2,1)S(1)} %convolution_convert_fusion.13), channel_id=1, source_target_pairs={{0,2},{2,0},{1,3},{3,1},{4,6},{6,4},{5,7},{7,5},{8,10},{10,8},{9,1... | collective-permute-start | bytes 884744 | tf_op jit(solution)/shard_map/ppermute | solution.py:34
  28.2 4.6 %copy-start.6 = (bf16[128,1152]{1,0:T(8,128)(2,1)S(1)}, bf16[128,1152]{1,0:T(8,128)(2,1)}, u32[]{:S(2)}) copy-start(bf16[128,1152]{1,0:T(8,128)(2,1)} %convolution_convert_fusion.11) | copy-start | bytes 884740
  28.2 17.0 %collective-permute-start.11 = (bf16[8,64]{1,0:T(8,128)(2,1)S(1)}, bf16[8,64]{1,0:T(8,128)(2,1)S(1)}, u32[]{:S(2)}, u32[]{:S(2)}) collective-permute-start(bf16[8,64]{1,0:T(8,128)(2,1)S(1)} %slice_maximum_fusion), channel_id=1, source_target_pairs={{0,2},{2,0},{1,3},{3,1},{4,6},{6,4},{5,7},{7,5},{8,10},{10,8},{9,1... | collective-permute-start | bytes 3080 | tf_op jit(solution)/shard_map/ppermute | solution.py:34
  33.0 12.2 %collective-permute-start.17 = (bf16[80,1152]{1,0:T(8,128)(2,1)S(1)}, bf16[80,1152]{1,0:T(8,128)(2,1)S(1)}, u32[]{:S(2)}, u32[]{:S(2)}) collective-permute-start(bf16[80,1152]{1,0:T(8,128)(2,1)S(1)} %convolution_convert_fusion.18), channel_id=1, source_target_pairs={{0,8},{8,0},{4,12},{12,4},{1,9},{9,1},{5,13},{13,5},{2,10},{10,2},... | collective-permute-start | bytes 552968 | tf_op jit(solution)/shard_map/ppermute | solution.py:34
  35.8 8.0 %collective-permute-start.14 = (bf16[88,1152]{1,0:T(8,128)(2,1)S(1)}, bf16[88,1152]{1,0:T(8,128)(2,1)S(1)}, u32[]{:S(2)}, u32[]{:S(2)}) collective-permute-start(bf16[88,1152]{1,0:T(8,128)(2,1)S(1)} %convolution_convert_fusion.15), channel_id=1, source_target_pairs={{0,4},{4,0},{8,12},{12,8},{1,5},{5,1},{9,13},{13,9},{2,6},{6,2},{1... | collective-permute-start | bytes 608264 | tf_op jit(solution)/shard_map/ppermute | solution.py:34
  38.5 5.2 %copy-start.7 = (bf16[128,1152]{1,0:T(8,128)(2,1)S(1)}, bf16[128,1152]{1,0:T(8,128)(2,1)}, u32[]{:S(2)}) copy-start(bf16[128,1152]{1,0:T(8,128)(2,1)} %convolution_convert_fusion.12) | copy-start | bytes 884740
  38.7 5.3 %copy-start.8 = (bf16[128,896]{1,0:T(8,128)(2,1)S(1)}, bf16[128,896]{1,0:T(8,128)(2,1)}, u32[]{:S(2)}) copy-start(bf16[128,896]{1,0:T(8,128)(2,1)} %convolution_convert_fusion.21) | copy-start | bytes 688132
  44.0 8.5 %collective-permute-start.18 = (bf16[80,1152]{1,0:T(8,128)(2,1)S(1)}, bf16[80,1152]{1,0:T(8,128)(2,1)S(1)}, u32[]{:S(2)}, u32[]{:S(2)}) collective-permute-start(bf16[80,1152]{1,0:T(8,128)(2,1)S(1)} %convolution_convert_fusion.17), channel_id=1, source_target_pairs={{0,8},{8,0},{4,12},{12,4},{1,9},{9,1},{5,13},{13,5},{2,10},{10,2},... | collective-permute-start | bytes 552968 | tf_op jit(solution)/shard_map/ppermute | solution.py:34

commit v25 on v23

--- a/solution.py
+++ b/solution.py
@@ -18,6 +18,7 @@
 )
 KERNEL_VMEM = 16 * 1024 * 1024
 ROOM_SIXTEENTHS = (11, 10)
+MOST_ROW = 96
 
 
 def route(axis, apart):
@@ -142,12 +143,14 @@
         match = (match & jnp.logical_not(partner_column)) | (compacted & partner_column)
         imag = (imag_column & jnp.logical_not(partner_column)) | (slot_imag & partner_column)
         small_ref[high, :rank], small_ref[high, rank:] = halves(match, imag)
-        once = (k < rank) & from_partner_entry
-        places = across(one_hot(once & (slot == row)), one_hot(once & (entry - rank == row)))
-        extra_ref[high] = places.astype(jnp.bfloat16)
+        imag_entry = jnp.where(k < rank, 0, 1)
+        used = from_partner_entry & (slot < room)
+        to_slot = one_hot(used & (slot + room * imag_entry == row))
+        from_coefficient = one_hot(used & (entry - rank + rank * imag_entry == row))
+        extra_ref[high] = across(to_slot, from_coefficient).astype(jnp.bfloat16)
         most = jnp.maximum(most, jnp.sum(picked, axis=1, keepdims=True) * 0.5 - room)
     for high in range(levels - wide):
-        extra_ref[high] = jnp.where(k < rank, extra_ref[high].astype(f32), most).astype(jnp.bfloat16)
+        extra_ref[high] = jnp.where(row < MOST_ROW, extra_ref[high].astype(f32), most).astype(jnp.bfloat16)
 
 
 def tables(skeleton, compress, wide, rooms):
@@ -208,15 +211,6 @@
     rank = both.shape[1] // 2
     turned = jnp.concatenate([-both[:, rank:], both[:, :rank]], 1)
     return jnp.concatenate([both, turned], 2)
-
-
-def compact_rows(matrix, slot):
-    rank = slot.shape[1]
-    parts = [
-        jnp.dot(slot, half, preferred_element_type=jnp.float32)
-        for half in (matrix[:rank], matrix[rank:])
-    ]
-    return jnp.concatenate(parts, 0).astype(jnp.bfloat16)
 
 
 def times(matrix, value):
@@ -270,7 +264,7 @@
     coeffs = list(early(sampling, traces, starts[: EARLY_PIECES + 1]))
     full, small, extra = tables(after(skeleton, coeffs[0]), compress, wide, rooms)
     sampling, evaluation = sampling[0], evaluation[0]
-    most_here = lax.broadcasted_iota(jnp.int32, extra.shape[1:], 1) >= rank
+    most_here = lax.broadcasted_iota(jnp.int32, extra.shape[1:], 0) >= MOST_ROW
 
     def compact(level, piece):
         return level >= wide and piece >= FULL_PIECES[level - wide]
@@ -285,7 +279,7 @@
             continue
         if (level, piece) == LOOK:
             known = after(after(partners[0], previous), partners[1])[:, starts[1] :]
-            theirs[levels - 1] = known[: rooms[levels - 1 - wide], :rank]
+            theirs[levels - 1] = known[: 2 * rooms[levels - 1 - wide]]
             continue
         count = starts[piece + 1] - starts[piece]
         if level == 0:
@@ -301,14 +295,14 @@
                 arrived = after(arrived, finished)
             elif piece == 0 and level - 1 >= wide:
                 known = arrived[:, count:]
-                theirs[level - 1] = known[: rooms[level - 1 - wide], :rank]
+                theirs[level - 1] = known[: 2 * rooms[level - 1 - wide]]
             value = jnp.concatenate([inputs[piece], arrived[:, :count]], 0)
             matrix = full[level - 1]
             if compact(level - 1, piece):
                 value = jnp.pad(value, ((0, full.shape[2] - value.shape[0]), (0, 0)))
                 matrix = small[level - 1 - wide]
             if level < levels and compact(level, piece):
-                outgoing = times(compact_rows(matrix, theirs[level]), value)
+                outgoing = times(times(theirs[level], matrix), value)
                 own = times(after(matrix, outgoing), value)
             else:
                 own = outgoing = times(matrix, value)
@@ -328,7 +322,7 @@
         partners[piece] = from_partner(outgoing, hops[level])
         previous = outgoing
         if (level, piece) == (levels - 1, COUNT_PIECE):
-            most = after(jnp.maximum(extra[levels - 1 - wide], known)[:8, rank:], outgoing)
+            most = after(jnp.maximum(extra[levels - 1 - wide], known)[MOST_ROW : MOST_ROW + 8], outgoing)
             for hop in hops[: wide - 1]:
                 most = jnp.maximum(most, from_partner(most, hop))
             counted = from_partner(most, hops[wide - 1])

time: 53.2 us -> 53.2 us (level)
  starting transfers between devices: 23.1 us -> 22.3 us
  waiting for transfers between devices: 13.5 us -> 14.1 us
    dot_general x17 -> x19, matrix products: 5.09 us -> 6.19 us  [times(): jnp.dot(matrix, value, preferred_element_type=jnp.float32)]
    ppermute x16, starting transfers between devices: 23.1 us -> 22.3 us  [from_partner(): return lax.ppermute(block, hop[0], route(*hop))]
    dot_general x6 -> x0, matrix products: 0.77 us -> none  [compact_rows(): jnp.dot(slot, half, preferred_element_type=jnp.float32)]
    ppermute x16, waiting for transfers between devices: 13.5 us -> 14.1 us  [from_partner(): return lax.ppermute(block, hop[0], route(*hop))]
  transfers between devices with their start and end apart: 16 -> 16, of which waited for: 6 -> 7; matrix products, arithmetic and copies ran while one was open for 22% -> 23% of each run, Pallas kernels for 2% -> 2%
where the time goes in v25:
time: 53.2 us; the launch traced here: 53 us
  starting transfers between devices  22.3 us (42%)
  waiting for transfers between devices  14.1 us (27%)
  matrix products  12.6 us (24%)
  Pallas kernels  2.43 us (5%)
  between operations  0.89 us (2%)
  local copies, waits for them, and re-layouts  0.59 us (1%)
    ppermute x16, starting transfers between devices, from_partner(): return lax.ppermute(block, hop[0], route(*hop))  22.3 us
    ppermute x16, waiting for transfers between devices, from_partner(): return lax.ppermute(block, hop[0], route(*hop))  14.1 us
    dot_general x19, matrix products, times(): jnp.dot(matrix, value, preferred_element_type=jnp.float32)  6.19 us
    dot_general x5, matrix products, evaluated(): jnp.einsum('ct,cp->tp', coeffs, evaluation, preferred_element_type=jnp.fl...  5.63 us
    pallas_call x1, Pallas kernels, early(): pl.pallas_call(lambda *refs: early_kernel(starts, *refs), out_shape=[jax....  1.35 us
    pallas_call x1, Pallas kernels, tables(): pl.pallas_call(lambda *refs: tables_kernel(wide, rooms, *refs), out_shape...  1.07 us
  transfers between devices with their start and end apart: 16, of which 7 were waited for; matrix products, arithmetic and copies ran while one was open for 23% of the time, Pallas kernels for 2%

profile of v25, /device:TPU:0, one launch (start us, length us, event | category | flops | bytes accessed | tf_op | source)
XLA Modules:
  0.0 53.0 jit_solution(7556634586449790715)
XLA Ops:
  0.0 1.4 %early.1 = (bf16[128,128]{1,0:T(8,128)(2,1)S(1)}, bf16[128,640]{1,0:T(8,128)(2,1)S(1)}) custom-call(bf16[1,128,128]{2,1,0:T(8,128)(2,1)} %refs_0_.1, bf16[4096,128]{1,0:T(8,128)(2,1)} %refs_1_.2), custom_call_target="tpu_custom_call" | custom-call | flops 25165824 | bytes 393216 | tf_op jit(solution)/shard_map/early/pallas_call | solution.py:71
  1.4 3.0 %collective-permute-start.3 = (bf16[128,128]{1,0:T(8,128)(2,1)S(1)}, bf16[128,128]{1,0:T(8,128)(2,1)S(1)}, u32[]{:S(2)}, u32[]{:S(2)}) collective-permute-start(bf16[128,128]{1,0:T(8,128)(2,1)S(1)} %get-tuple-element.64), channel_id=1, source_target_pairs={{0,2},{2,0},{1,3},{3,1},{4,6},{6,4},{5,7},{7,5},{8,10},{10,8},{9,1... | collective-permute-start | bytes 98312 | tf_op jit(solution)/shard_map/ppermute | solution.py:35
  4.7 2.0 %collective-permute-start.7 = (bf16[128,1024]{1,0:T(8,128)(2,1)S(1)}, bf16[128,1024]{1,0:T(8,128)(2,1)S(1)}, u32[]{:S(2)}, u32[]{:S(2)}) collective-permute-start(bf16[128,1024]{1,0:T(8,128)(2,1)S(1)} %convolution_convert_fusion.21), channel_id=1, source_target_pairs={{0,2},{2,0},{1,3},{3,1},{4,6},{6,4},{5,7},{7,5},{8,10},{10,8},{9,1... | collective-permute-start | bytes 786440 | tf_op jit(solution)/shard_map/ppermute | solution.py:35
  6.7 1.1 %tables.1 = (bf16[3,128,256]{2,1,0:T(8,128)(2,1)S(1)}, bf16[2,128,256]{2,1,0:T(8,128)(2,1)S(1)}, bf16[2,128,128]{2,1,0:T(8,128)(2,1)S(1)}) custom-call(s32[3,1,64]{2,1,0:T(1,128)S(1)} %bitcast.103, bf16[1,3,64,128]{3,2,1,0:T(8,128)(2,1)S(1)} %copy-done.4), custom_call_target="tpu_custom_call" | custom-call | flops 50000000 | bytes 600000 | tf_op jit(solution)/shard_map/tables/pallas_call | solution.py:159
  8.1 1.6 %collective-permute-start.4 = (bf16[128,256]{1,0:T(8,128)(2,1)S(1)}, bf16[128,256]{1,0:T(8,128)(2,1)S(1)}, u32[]{:S(2)}, u32[]{:S(2)}) collective-permute-start(bf16[128,256]{1,0:T(8,128)(2,1)S(1)} %pad_maximum_fusion.12), channel_id=1, source_target_pairs={{0,4},{4,0},{8,12},{12,8},{1,5},{5,1},{9,13},{13,9},{2,6},{6,2},{1... | collective-permute-start | bytes 196616 | tf_op jit(solution)/shard_map/ppermute | solution.py:35
  9.7 1.8 %collective-permute-done.5 = bf16[128,640]{1,0:T(8,128)(2,1)S(1)} collective-permute-done((bf16[128,640]{1,0:T(8,128)(2,1)S(1)}, bf16[128,640]{1,0:T(8,128)(2,1)S(1)}, u32[]{:S(2)}, u32[]{:S(2)}) %collective-permute-start.5) | collective-permute-done | bytes 163872 | tf_op jit(solution)/shard_map/ppermute | solution.py:35
  11.7 1.6 %collective-permute-start.8 = (bf16[128,640]{1,0:T(8,128)(2,1)S(1)}, bf16[128,640]{1,0:T(8,128)(2,1)S(1)}, u32[]{:S(2)}, u32[]{:S(2)}) collective-permute-start(bf16[128,640]{1,0:T(8,128)(2,1)S(1)} %convolution_convert_fusion.28), channel_id=1, source_target_pairs={{0,4},{4,0},{8,12},{12,8},{1,5},{5,1},{9,13},{13,9},{2,6},{6,2},{1... | collective-permute-start | bytes 491528 | tf_op jit(solution)/shard_map/ppermute | solution.py:35
  14.1 2.6 %collective-permute-start.6 = (bf16[128,256]{1,0:T(8,128)(2,1)S(1)}, bf16[128,256]{1,0:T(8,128)(2,1)S(1)}, u32[]{:S(2)}, u32[]{:S(2)}) collective-permute-start(bf16[128,256]{1,0:T(8,128)(2,1)S(1)} %pad_maximum_fusion.13), channel_id=1, source_target_pairs={{0,8},{8,0},{4,12},{12,4},{1,9},{9,1},{5,13},{13,5},{2,10},{10,2},... | collective-permute-start | bytes 196616 | tf_op jit(solution)/shard_map/ppermute | solution.py:35
  16.7 0.7 %collective-permute-start.10 = (bf16[128,1280]{1,0:T(8,128)(2,1)S(1)}, bf16[128,1280]{1,0:T(8,128)(2,1)S(1)}, u32[]{:S(2)}, u32[]{:S(2)}) collective-permute-start(bf16[128,1280]{1,0:T(8,128)(2,1)S(1)} %convolution_convert_fusion.9), channel_id=1, source_target_pairs={{0,2},{2,0},{1,3},{3,1},{4,6},{6,4},{5,7},{7,5},{8,10},{10,8},{9,1... | collective-permute-start | bytes 983048 | tf_op jit(solution)/shard_map/ppermute | solution.py:35
  17.9 0.9 %collective-permute-start.9 = (bf16[88,1024]{1,0:T(8,128)(2,1)S(1)}, bf16[88,1024]{1,0:T(8,128)(2,1)S(1)}, u32[]{:S(2)}, u32[]{:S(2)}) collective-permute-start(bf16[88,1024]{1,0:T(8,128)(2,1)S(1)} %convolution_convert_fusion.23), channel_id=1, source_target_pairs={{0,4},{4,0},{8,12},{12,8},{1,5},{5,1},{9,13},{13,9},{2,6},{6,2},{1... | collective-permute-start | bytes 540680 | tf_op jit(solution)/shard_map/ppermute | solution.py:35
  18.7 1.4 %collective-permute-done.6 = bf16[128,256]{1,0:T(8,128)(2,1)S(1)} collective-permute-done((bf16[128,256]{1,0:T(8,128)(2,1)S(1)}, bf16[128,256]{1,0:T(8,128)(2,1)S(1)}, u32[]{:S(2)}, u32[]{:S(2)}) %collective-permute-start.6) | collective-permute-done | bytes 65568 | tf_op jit(solution)/shard_map/ppermute | solution.py:35
  20.1 0.9 %convolution_convert_fusion.20 = bf16[128,1024]{1,0:T(8,128)(2,1)} fusion(bf16[128,256]{1,0:T(8,128)(2,1)S(1)} %get-tuple-element.88, bf16[128,1024]{1,0:T(8,128)(2,1)S(1)} %collective-permute-done.7, bf16[128,1024]{1,0:T(8,128)(2,1)S(1)} %convolution_convert_fusion.21), kind=kOutput, calls=%fused_computation.52 | convolution fusion | flops 68288512 | bytes 851968 | tf_op jit(solution)/shard_map/dot_general | solution.py:217
  21.2 0.3 convolution_convert_fusion.30
  21.5 2.5 %collective-permute-start.15 = (bf16[80,640]{1,0:T(8,128)(2,1)S(1)}, bf16[80,640]{1,0:T(8,128)(2,1)S(1)}, u32[]{:S(2)}, u32[]{:S(2)}) collective-permute-start(bf16[80,640]{1,0:T(8,128)(2,1)S(1)} %convolution_convert_fusion.30), channel_id=1, source_target_pairs={{0,8},{8,0},{4,12},{12,4},{1,9},{9,1},{5,13},{13,5},{2,10},{10,2},... | collective-permute-start | bytes 307208 | tf_op jit(solution)/shard_map/ppermute | solution.py:35
  24.5 0.3 collective-permute-start.16
  25.3 2.4 %collective-permute-start.12 = (bf16[80,1024]{1,0:T(8,128)(2,1)S(1)}, bf16[80,1024]{1,0:T(8,128)(2,1)S(1)}, u32[]{:S(2)}, u32[]{:S(2)}) collective-permute-start(bf16[80,1024]{1,0:T(8,128)(2,1)S(1)} %convolution_convert_fusion.27), channel_id=1, source_target_pairs={{0,8},{8,0},{4,12},{12,4},{1,9},{9,1},{5,13},{13,5},{2,10},{10,2},... | collective-permute-start | bytes 491528 | tf_op jit(solution)/shard_map/ppermute | solution.py:35
  27.7 0.7 %collective-permute-start.13 = (bf16[128,1024]{1,0:T(8,128)(2,1)S(1)}, bf16[128,1024]{1,0:T(8,128)(2,1)S(1)}, u32[]{:S(2)}, u32[]{:S(2)}) collective-permute-start(bf16[128,1024]{1,0:T(8,128)(2,1)S(1)} %convolution_convert_fusion.18), channel_id=1, source_target_pairs={{0,2},{2,0},{1,3},{3,1},{4,6},{6,4},{5,7},{7,5},{8,10},{10,8},{9,1... | collective-permute-start | bytes 786440 | tf_op jit(solution)/shard_map/ppermute | solution.py:35
  28.5 0.9 %convolution_convert_fusion.19 = bf16[128,1024]{1,0:T(8,128)(2,1)} fusion(bf16[128,256]{1,0:T(8,128)(2,1)S(1)} %slice_bitcast_fusion.7, bf16[88,1024]{1,0:T(8,128)(2,1)S(1)} %collective-permute-done.9, bf16[128,1024]{1,0:T(8,128)(2,1)S(1)} %copy-done.8), kind=kOutput, calls=%fused_computation.51 | convolution fusion | flops 69074944 | bytes 770048 | tf_op jit(solution)/shard_map/dot_general | solution.py:217
  29.4 1.3 %collective-permute-start.11 = (bf16[8,128]{1,0:T(8,128)(2,1)S(1)}, bf16[8,128]{1,0:T(8,128)(2,1)S(1)}, u32[]{:S(2)}, u32[]{:S(2)}) collective-permute-start(bf16[8,128]{1,0:T(8,128)(2,1)S(1)} %slice_maximum_fusion), channel_id=1, source_target_pairs={{0,2},{2,0},{1,3},{3,1},{4,6},{6,4},{5,7},{7,5},{8,10},{10,8},{9,1... | collective-permute-start | bytes 6152 | tf_op jit(solution)/shard_map/ppermute | solution.py:35
  30.7 1.0 %constant_dynamic-update-slice_fusion.3 = bf16[4096,128]{1,0:T(8,128)(2,1)} fusion(bf16[1,128,128]{2,1,0:T(8,128)(2,1)S(1)} %copy-done.6, bf16[128,128]{1,0:T(8,128)(2,1)S(1)} %slice-done, bf16[128,128]{1,0:T(8,128)(2,1)S(1)} %convolution_convert_fusion.36, bf16[3,128,256]{2,1,0:T(8,128)(2,1)S(1)} %get-tuple-element.67), kind=kOutput, calls=%fused_computation.149 | convolution fusion | flops 12746751 | bytes 196608 | tf_op jit(solution)/shard_map/ct,cp->tp/dot_general | solution.py:227
  32.0 2.4 %collective-permute-done.13 = bf16[128,1024]{1,0:T(8,128)(2,1)S(1)} collective-permute-done((bf16[128,1024]{1,0:T(8,128)(2,1)S(1)}, bf16[128,1024]{1,0:T(8,128)(2,1)S(1)}, u32[]{:S(2)}, u32[]{:S(2)}) %collective-permute-start.13) | collective-permute-done | bytes 262176 | tf_op jit(solution)/shard_map/ppermute | solution.py:35
  34.6 0.4 collective-permute-start.14
  35.2 2.0 %collective-permute-start.17 = (bf16[80,1280]{1,0:T(8,128)(2,1)S(1)}, bf16[80,1280]{1,0:T(8,128)(2,1)S(1)}, u32[]{:S(2)}, u32[]{:S(2)}) collective-permute-start(bf16[80,1280]{1,0:T(8,128)(2,1)S(1)} %convolution_convert_fusion.11), channel_id=1, source_target_pairs={{0,8},{8,0},{4,12},{12,4},{1,9},{9,1},{5,13},{13,5},{2,10},{10,2},... | collective-permute-start | bytes 614408 | tf_op jit(solution)/shard_map/ppermute | solution.py:35
  37.2 1.0 %convolution_convert_fusion.7 = bf16[128,1280]{1,0:T(8,128)(2,1)} fusion(bf16[128,256]{1,0:T(8,128)(2,1)S(1)} %slice_bitcast_fusion.7, bf16[88,1280]{1,0:T(8,128)(2,1)S(1)} %collective-permute-done.16, bf16[128,1280]{1,0:T(8,128)(2,1)S(1)} %convolution_convert_fusion.8), kind=kOutput, calls=%fused_computation.32 | convolution fusion | flops 86343680 | bytes 946176 | tf_op jit(solution)/shard_map/dot_general | solution.py:217
  38.1 1.1 %constant_dynamic-update-slice_fusion.2 = bf16[4096,128]{1,0:T(8,128)(2,1)} fusion(bf16[4096,128]{1,0:T(8,128)(2,1)} %constant_dynamic-update-slice_fusion.3, bf16[1,128,128]{2,1,0:T(8,128)(2,1)S(1)} %copy-done.6, bf16[80,640]{1,0:T(8,128)(2,1)S(1)} %collective-permute-done.15, bf16[128,640]{1,0:T(8,128)(2,1)S(1)} %convolution_convert_fusion.26, ...), kind=kOutput, calls=%fused_computation.148 | convolution fusion | flops 64225280 | bytes 528384 | tf_op jit(solution)/shard_map/ct,cp->tp/dot_general | solution.py:227
  39.5 2.6 %collective-permute-done.14 = bf16[88,1024]{1,0:T(8,128)(2,1)S(1)} collective-permute-done((bf16[88,1024]{1,0:T(8,128)(2,1)S(1)}, bf16[88,1024]{1,0:T(8,128)(2,1)S(1)}, u32[]{:S(2)}, u32[]{:S(2)}) %collective-permute-start.14) | collective-permute-done | bytes 180256 | tf_op jit(solution)/shard_map/ppermute | solution.py:35
  42.4 1.2 %constant_dynamic-update-slice_fusion.1 = bf16[4096,128]{1,0:T(8,128)(2,1)} fusion(bf16[4096,128]{1,0:T(8,128)(2,1)} %constant_dynamic-update-slice_fusion.2, bf16[1,128,128]{2,1,0:T(8,128)(2,1)S(1)} %copy-done.6, bf16[80,1024]{1,0:T(8,128)(2,1)S(1)} %collective-permute-done.12, bf16[128,1024]{1,0:T(8,128)(2,1)S(1)} %copy-done.9, ...), kind=kOutput, calls=%fused_computation.147 | convolution fusion | flops 102760448 | bytes 786432 | tf_op jit(solution)/shard_map/ct,cp->tp/dot_general | solution.py:227
  43.6 0.5 slice.121
  44.9 4.7 %collective-permute-done.17 = bf16[80,1280]{1,0:T(8,128)(2,1)S(1)} collective-permute-done((bf16[80,1280]{1,0:T(8,128)(2,1)S(1)}, bf16[80,1280]{1,0:T(8,128)(2,1)S(1)}, u32[]{:S(2)}, u32[]{:S(2)}) %collective-permute-start.17) | collective-permute-done | bytes 204832 | tf_op jit(solution)/shard_map/ppermute | solution.py:35
  49.6 1.2 %constant_dynamic-update-slice_fusion = bf16[4096,128]{1,0:T(8,128)(2,1)} fusion(bf16[4096,128]{1,0:T(8,128)(2,1)} %constant_dynamic-update-slice_fusion.1, bf16[1,128,128]{2,1,0:T(8,128)(2,1)S(1)} %copy-done.6, bf16[80,1280]{1,0:T(8,128)(2,1)S(1)} %collective-permute-done.17, bf16[128,1280]{1,0:T(8,128)(2,1)S(1)} %copy-done.10, ...), kind=kOutput, calls=%fused_computation.146 | convolution fusion | flops 128450560 | bytes 958464 | tf_op jit(solution)/shard_map/ct,cp->tp/dot_general | solution.py:227
  50.8 1.1 %collective-permute-done.18 = bf16[80,1024]{1,0:T(8,128)(2,1)S(1)} collective-permute-done((bf16[80,1024]{1,0:T(8,128)(2,1)S(1)}, bf16[80,1024]{1,0:T(8,128)(2,1)S(1)}, u32[]{:S(2)}, u32[]{:S(2)}) %collective-permute-start.18) | collective-permute-done | bytes 163872 | tf_op jit(solution)/shard_map/ppermute | solution.py:35
  51.9 1.2 %fusion.24 = bf16[4096,128]{1,0:T(8,128)(2,1)} fusion(bf16[4096,128]{1,0:T(8,128)(2,1)} %constant_dynamic-update-slice_fusion, bf16[80,1024]{1,0:T(8,128)(2,1)S(1)} %collective-permute-done.18, bf16[128,1024]{1,0:T(8,128)(2,1)S(1)} %convolution_convert_fusion.14, bf16[2,128,256]{2,1,0:T(8,128)(2,1)S(1)} %get-tuple-element.78, ...), kind=kOutput, calls=%fused_computation.44 | convolution fusion | flops 102760448 | bytes 786432 | tf_op jit(solution)/shard_map/ct,cp->tp/dot_general | solution.py:227
  (63 shorter events, 4.4 us)
Async XLA Ops:
  0.0 4.5 %copy-start = (bf16[4096,128]{1,0:T(8,128)(2,1)S(1)}, bf16[4096,128]{1,0:T(8,128)(2,1)}, u32[]{:S(2)}) copy-start(bf16[4096,128]{1,0:T(8,128)(2,1)} %refs_1_.2) | copy-start | bytes 3145732
  0.0 4.5 %copy-start.2 = (bf16[1,128,128]{2,1,0:T(8,128)(2,1)S(1)}, bf16[1,128,128]{2,1,0:T(8,128)(2,1)}, u32[]{:S(2)}) copy-start(bf16[1,128,128]{2,1,0:T(8,128)(2,1)} %refs_0_.1) | copy-start | bytes 98308
  0.0 6.7 %copy-start.5 = (s32[1,3,64]{2,0,1:T(1,128)S(1)}, s32[1,3,64]{2,0,1:T(1,128)}, u32[]{:S(2)}) copy-start(s32[1,3,64]{2,0,1:T(1,128)} %param.9) | copy-start | bytes 2308
  0.0 6.7 %copy-start.4 = (bf16[1,3,64,128]{3,2,1,0:T(8,128)(2,1)S(1)}, bf16[1,3,64,128]{3,2,1,0:T(8,128)(2,1)}, u32[]{:S(2)}) copy-start(bf16[1,3,64,128]{3,2,1,0:T(8,128)(2,1)} %refs_1_.3) | copy-start | bytes 147460
  1.4 6.5 %collective-permute-start.3 = (bf16[128,128]{1,0:T(8,128)(2,1)S(1)}, bf16[128,128]{1,0:T(8,128)(2,1)S(1)}, u32[]{:S(2)}, u32[]{:S(2)}) collective-permute-start(bf16[128,128]{1,0:T(8,128)(2,1)S(1)} %get-tuple-element.64), channel_id=1, source_target_pairs={{0,2},{2,0},{1,3},{3,1},{4,6},{6,4},{5,7},{7,5},{8,10},{10,8},{9,1... | collective-permute-start | bytes 98312 | tf_op jit(solution)/shard_map/ppermute | solution.py:35
  4.4 7.1 %collective-permute-start.5 = (bf16[128,640]{1,0:T(8,128)(2,1)S(1)}, bf16[128,640]{1,0:T(8,128)(2,1)S(1)}, u32[]{:S(2)}, u32[]{:S(2)}) collective-permute-start(bf16[128,640]{1,0:T(8,128)(2,1)S(1)} %get-tuple-element.68), channel_id=1, source_target_pairs={{0,2},{2,0},{1,3},{3,1},{4,6},{6,4},{5,7},{7,5},{8,10},{10,8},{9,1... | collective-permute-start | bytes 491528 | tf_op jit(solution)/shard_map/ppermute | solution.py:35
  4.7 12.9 %collective-permute-start.7 = (bf16[128,1024]{1,0:T(8,128)(2,1)S(1)}, bf16[128,1024]{1,0:T(8,128)(2,1)S(1)}, u32[]{:S(2)}, u32[]{:S(2)}) collective-permute-start(bf16[128,1024]{1,0:T(8,128)(2,1)S(1)} %convolution_convert_fusion.21), channel_id=1, source_target_pairs={{0,2},{2,0},{1,3},{3,1},{4,6},{6,4},{5,7},{7,5},{8,10},{10,8},{9,1... | collective-permute-start | bytes 786440 | tf_op jit(solution)/shard_map/ppermute | solution.py:35
  8.1 5.6 %collective-permute-start.4 = (bf16[128,256]{1,0:T(8,128)(2,1)S(1)}, bf16[128,256]{1,0:T(8,128)(2,1)S(1)}, u32[]{:S(2)}, u32[]{:S(2)}) collective-permute-start(bf16[128,256]{1,0:T(8,128)(2,1)S(1)} %pad_maximum_fusion.12), channel_id=1, source_target_pairs={{0,4},{4,0},{8,12},{12,8},{1,5},{5,1},{9,13},{13,9},{2,6},{6,2},{1... | collective-permute-start | bytes 196616 | tf_op jit(solution)/shard_map/ppermute | solution.py:35
  11.7 9.3 %collective-permute-start.8 = (bf16[128,640]{1,0:T(8,128)(2,1)S(1)}, bf16[128,640]{1,0:T(8,128)(2,1)S(1)}, u32[]{:S(2)}, u32[]{:S(2)}) collective-permute-start(bf16[128,640]{1,0:T(8,128)(2,1)S(1)} %convolution_convert_fusion.28), channel_id=1, source_target_pairs={{0,4},{4,0},{8,12},{12,8},{1,5},{5,1},{9,13},{13,9},{2,6},{6,2},{1... | collective-permute-start | bytes 491528 | tf_op jit(solution)/shard_map/ppermute | solution.py:35
  14.1 6.0 %collective-permute-start.6 = (bf16[128,256]{1,0:T(8,128)(2,1)S(1)}, bf16[128,256]{1,0:T(8,128)(2,1)S(1)}, u32[]{:S(2)}, u32[]{:S(2)}) collective-permute-start(bf16[128,256]{1,0:T(8,128)(2,1)S(1)} %pad_maximum_fusion.13), channel_id=1, source_target_pairs={{0,8},{8,0},{4,12},{12,4},{1,9},{9,1},{5,13},{13,5},{2,10},{10,2},... | collective-permute-start | bytes 196616 | tf_op jit(solution)/shard_map/ppermute | solution.py:35
  16.7 7.6 %collective-permute-start.10 = (bf16[128,1280]{1,0:T(8,128)(2,1)S(1)}, bf16[128,1280]{1,0:T(8,128)(2,1)S(1)}, u32[]{:S(2)}, u32[]{:S(2)}) collective-permute-start(bf16[128,1280]{1,0:T(8,128)(2,1)S(1)} %convolution_convert_fusion.9), channel_id=1, source_target_pairs={{0,2},{2,0},{1,3},{3,1},{4,6},{6,4},{5,7},{7,5},{8,10},{10,8},{9,1... | collective-permute-start | bytes 983048 | tf_op jit(solution)/shard_map/ppermute | solution.py:35
  17.9 7.2 %collective-permute-start.9 = (bf16[88,1024]{1,0:T(8,128)(2,1)S(1)}, bf16[88,1024]{1,0:T(8,128)(2,1)S(1)}, u32[]{:S(2)}, u32[]{:S(2)}) collective-permute-start(bf16[88,1024]{1,0:T(8,128)(2,1)S(1)} %convolution_convert_fusion.23), channel_id=1, source_target_pairs={{0,4},{4,0},{8,12},{12,8},{1,5},{5,1},{9,13},{13,9},{2,6},{6,2},{1... | collective-permute-start | bytes 540680 | tf_op jit(solution)/shard_map/ppermute | solution.py:35
  20.1 8.4 %copy-start.3 = (bf16[128,256]{1,0:T(8,128)(2,1)}, bf16[128,256]{1,0:T(8,128)(2,1)S(1)}, u32[]{:S(2)}) copy-start(bf16[128,256]{1,0:T(8,128)(2,1)S(1)} %collective-permute-done.6) | copy-start | bytes 196612
  21.2 3.9 %copy-start.7 = (bf16[128,1024]{1,0:T(8,128)(2,1)S(1)}, bf16[128,1024]{1,0:T(8,128)(2,1)}, u32[]{:S(2)}) copy-start(bf16[128,1024]{1,0:T(8,128)(2,1)} %convolution_convert_fusion.20) | copy-start | bytes 786436
  21.5 16.6 %collective-permute-start.15 = (bf16[80,640]{1,0:T(8,128)(2,1)S(1)}, bf16[80,640]{1,0:T(8,128)(2,1)S(1)}, u32[]{:S(2)}, u32[]{:S(2)}) collective-permute-start(bf16[80,640]{1,0:T(8,128)(2,1)S(1)} %convolution_convert_fusion.30), channel_id=1, source_target_pairs={{0,8},{8,0},{4,12},{12,4},{1,9},{9,1},{5,13},{13,5},{2,10},{10,2},... | collective-permute-start | bytes 307208 | tf_op jit(solution)/shard_map/ppermute | solution.py:35
  24.5 3.9 %copy-start.8 = (bf16[128,1024]{1,0:T(8,128)(2,1)S(1)}, bf16[128,1024]{1,0:T(8,128)(2,1)}, u32[]{:S(2)}) copy-start(bf16[128,1024]{1,0:T(8,128)(2,1)} %convolution_convert_fusion.20) | copy-start | bytes 786436
  24.5 10.4 %collective-permute-start.16 = (bf16[88,1280]{1,0:T(8,128)(2,1)S(1)}, bf16[88,1280]{1,0:T(8,128)(2,1)S(1)}, u32[]{:S(2)}, u32[]{:S(2)}) collective-permute-start(bf16[88,1280]{1,0:T(8,128)(2,1)S(1)} %convolution_convert_fusion.10), channel_id=1, source_target_pairs={{0,4},{4,0},{8,12},{12,8},{1,5},{5,1},{9,13},{13,9},{2,6},{6,2},{1... | collective-permute-start | bytes 675848 | tf_op jit(solution)/shard_map/ppermute | solution.py:35
  25.3 17.0 %collective-permute-start.12 = (bf16[80,1024]{1,0:T(8,128)(2,1)S(1)}, bf16[80,1024]{1,0:T(8,128)(2,1)S(1)}, u32[]{:S(2)}, u32[]{:S(2)}) collective-permute-start(bf16[80,1024]{1,0:T(8,128)(2,1)S(1)} %convolution_convert_fusion.27), channel_id=1, source_target_pairs={{0,8},{8,0},{4,12},{12,4},{1,9},{9,1},{5,13},{13,5},{2,10},{10,2},... | collective-permute-start | bytes 491528 | tf_op jit(solution)/shard_map/ppermute | solution.py:35
  27.7 6.6 %collective-permute-start.13 = (bf16[128,1024]{1,0:T(8,128)(2,1)S(1)}, bf16[128,1024]{1,0:T(8,128)(2,1)S(1)}, u32[]{:S(2)}, u32[]{:S(2)}) collective-permute-start(bf16[128,1024]{1,0:T(8,128)(2,1)S(1)} %convolution_convert_fusion.18), channel_id=1, source_target_pairs={{0,2},{2,0},{1,3},{3,1},{4,6},{6,4},{5,7},{7,5},{8,10},{10,8},{9,1... | collective-permute-start | bytes 786440 | tf_op jit(solution)/shard_map/ppermute | solution.py:35
  28.5 2.3 %slice-start = ((bf16[128,256]{1,0:T(8,128)(2,1)}), bf16[128,128]{1,0:T(8,128)(2,1)S(1)}, s32[]{:S(2)}) async-start(bf16[128,256]{1,0:T(8,128)(2,1)} %copy-done.3), calls=%async_computation | async-start | bytes 65536 | tf_op jit(solution)/shard_map/slice | solution.py:299
  28.5 2.3 %copy-start.6 = (bf16[1,128,128]{2,1,0:T(8,128)(2,1)S(1)}, bf16[1,128,128]{2,1,0:T(8,128)(2,1)}, u32[]{:S(2)}) copy-start(bf16[1,128,128]{2,1,0:T(8,128)(2,1)} %param.11) | copy-start | bytes 98308
  29.4 14.1 %collective-permute-start.11 = (bf16[8,128]{1,0:T(8,128)(2,1)S(1)}, bf16[8,128]{1,0:T(8,128)(2,1)S(1)}, u32[]{:S(2)}, u32[]{:S(2)}) collective-permute-start(bf16[8,128]{1,0:T(8,128)(2,1)S(1)} %slice_maximum_fusion), channel_id=1, source_target_pairs={{0,2},{2,0},{1,3},{3,1},{4,6},{6,4},{5,7},{7,5},{8,10},{10,8},{9,1... | collective-permute-start | bytes 6152 | tf_op jit(solution)/shard_map/ppermute | solution.py:35
  34.6 7.5 %collective-permute-start.14 = (bf16[88,1024]{1,0:T(8,128)(2,1)S(1)}, bf16[88,1024]{1,0:T(8,128)(2,1)S(1)}, u32[]{:S(2)}, u32[]{:S(2)}) collective-permute-start(bf16[88,1024]{1,0:T(8,128)(2,1)S(1)} %convolution_convert_fusion.22), channel_id=1, source_target_pairs={{0,4},{4,0},{8,12},{12,8},{1,5},{5,1},{9,13},{13,9},{2,6},{6,2},{1... | collective-permute-start | bytes 540680 | tf_op jit(solution)/shard_map/ppermute | solution.py:35
  35.2 14.4 %collective-permute-start.17 = (bf16[80,1280]{1,0:T(8,128)(2,1)S(1)}, bf16[80,1280]{1,0:T(8,128)(2,1)S(1)}, u32[]{:S(2)}, u32[]{:S(2)}) collective-permute-start(bf16[80,1280]{1,0:T(8,128)(2,1)S(1)} %convolution_convert_fusion.11), channel_id=1, source_target_pairs={{0,8},{8,0},{4,12},{12,4},{1,9},{9,1},{5,13},{13,5},{2,10},{10,2},... | collective-permute-start | bytes 614408 | tf_op jit(solution)/shard_map/ppermute | solution.py:35
  39.5 2.9 %copy-start.9 = (bf16[128,1024]{1,0:T(8,128)(2,1)S(1)}, bf16[128,1024]{1,0:T(8,128)(2,1)}, u32[]{:S(2)}) copy-start(bf16[128,1024]{1,0:T(8,128)(2,1)} %convolution_convert_fusion.19) | copy-start | bytes 786436
  42.3 9.6 %collective-permute-start.18 = (bf16[80,1024]{1,0:T(8,128)(2,1)S(1)}, bf16[80,1024]{1,0:T(8,128)(2,1)S(1)}, u32[]{:S(2)}, u32[]{:S(2)}) collective-permute-start(bf16[80,1024]{1,0:T(8,128)(2,1)S(1)} %convolution_convert_fusion.24), channel_id=1, source_target_pairs={{0,8},{8,0},{4,12},{12,4},{1,9},{9,1},{5,13},{13,5},{2,10},{10,2},... | collective-permute-start | bytes 491528 | tf_op jit(solution)/shard_map/ppermute | solution.py:35
  44.6 4.9 %copy-start.10 = (bf16[128,1280]{1,0:T(8,128)(2,1)S(1)}, bf16[128,1280]{1,0:T(8,128)(2,1)}, u32[]{:S(2)}) copy-start(bf16[128,1280]{1,0:T(8,128)(2,1)} %convolution_convert_fusion.7) | copy-start | bytes 983044

commit v26 on v25

--- a/solution.py
+++ b/solution.py
@@ -10,10 +10,11 @@
 EARLY_PIECES = 2
 COUNT_PIECE = 2
 COUNT_READ = 2
+TELL = (1, -1)
 LOOK = (3, -1)
 MAKE = (0, -1)
 ORDER = (
-    (0, 0), (0, 1), (0, 2), (1, 0), (1, 1), MAKE, (2, 0), (0, 3), (1, 2), LOOK, (2, 1), (1, 3), (2, 2),
+    (0, 0), (0, 1), (0, 2), (1, 0), TELL, (1, 1), MAKE, (2, 0), (0, 3), (1, 2), LOOK, (2, 1), (1, 3), (2, 2),
     (0, 4), (3, 0), (1, 4), (2, 3), (3, 1), (2, 4), (3, 2), (3, 3), (3, 4),
 )
 KERNEL_VMEM = 16 * 1024 * 1024
@@ -264,22 +265,24 @@
     coeffs = list(early(sampling, traces, starts[: EARLY_PIECES + 1]))
     full, small, extra = tables(after(skeleton, coeffs[0]), compress, wide, rooms)
     sampling, evaluation = sampling[0], evaluation[0]
-    most_here = lax.broadcasted_iota(jnp.int32, extra.shape[1:], 0) >= MOST_ROW
 
     def compact(level, piece):
         return level >= wide and piece >= FULL_PIECES[level - wide]
 
     inputs, partners, theirs, done = {}, {}, {}, [None] * pieces
-    previous, finished, known = None, None, None
+    previous, finished = None, None
     for level, piece in ORDER:
+        if (level, piece) == TELL:
+            told = from_partner(after(extra[levels - 1 - wide], previous), hops[levels - 1])
+            continue
+        if (level, piece) == LOOK:
+            told = after(told, (previous, partners[1]))
+            theirs[levels - 1] = told[: 2 * rooms[levels - 1 - wide]]
+            continue
         if (level, piece) == MAKE:
             waiting = after(sampling, previous)
             coeffs.append(sampled(waiting, traces[starts[pieces - 2] : starts[pieces - 1]]))
             previous = coeffs[-1]
-            continue
-        if (level, piece) == LOOK:
-            known = after(after(partners[0], previous), partners[1])[:, starts[1] :]
-            theirs[levels - 1] = known[: 2 * rooms[levels - 1 - wide]]
             continue
         count = starts[piece + 1] - starts[piece]
         if level == 0:
@@ -294,8 +297,7 @@
             if level == levels:
                 arrived = after(arrived, finished)
             elif piece == 0 and level - 1 >= wide:
-                known = arrived[:, count:]
-                theirs[level - 1] = known[: 2 * rooms[level - 1 - wide]]
+                theirs[level - 1] = arrived[: 2 * rooms[level - 1 - wide], count:]
             value = jnp.concatenate([inputs[piece], arrived[:, :count]], 0)
             matrix = full[level - 1]
             if compact(level - 1, piece):
@@ -313,19 +315,17 @@
             continue
         if level == 0:
             outgoing = after(own, previous) if piece >= pieces - 2 else own
-        if piece == 0 and level >= wide:
-            block = extra[level - wide]
-            if known is not None:
-                block = jnp.where(most_here, jnp.maximum(block, known), block)
-            outgoing = jnp.concatenate([outgoing, block], 1)
+        if piece == 0 and wide <= level < levels - 1:
+            outgoing = jnp.concatenate([outgoing, extra[level - wide]], 1)
         inputs[piece] = own
         partners[piece] = from_partner(outgoing, hops[level])
         previous = outgoing
-        if (level, piece) == (levels - 1, COUNT_PIECE):
-            most = after(jnp.maximum(extra[levels - 1 - wide], known)[MOST_ROW : MOST_ROW + 8], outgoing)
-            for hop in hops[: wide - 1]:
-                most = jnp.maximum(most, from_partner(most, hop))
-            counted = from_partner(most, hops[wide - 1])
+        if level == levels - 1 and 0 <= piece - COUNT_PIECE < levels - 1:
+            if piece == COUNT_PIECE:
+                most = after(jnp.maximum(extra[levels - 1 - wide], told)[MOST_ROW : MOST_ROW + 8], outgoing)
+            else:
+                most = jnp.maximum(most, after(counted, outgoing))
+            counted = from_partner(most, hops[piece - COUNT_PIECE])
     quick = jnp.concatenate(done, 0)
     return lax.cond(
         most[0, 0] > 0,

time: 53.2 us -> 53.4 us (level)
  starting transfers between devices: 22.3 us -> 26 us
  waiting for transfers between devices: 14.1 us -> 10.7 us
    ppermute x16 -> x18, starting transfers between devices: 22.3 us -> 26 us  [from_partner(): return lax.ppermute(block, hop[0], route(*hop))]
    ppermute x16 -> x18, waiting for transfers between devices: 14.1 us -> 10.7 us  [from_partner(): return lax.ppermute(block, hop[0], route(*hop))]
  transfers between devices with their start and end apart: 16 -> 18, of which waited for: 7 -> 6; matrix products, arithmetic and copies ran while one was open for 23% -> 22% of each run, Pallas kernels for 2% -> 2%
where the time goes in v26:
time: 53.4 us; the launch traced here: 53.2 us
  starting transfers between devices  26 us (49%)
  matrix products  12.5 us (23%)
  waiting for transfers between devices  10.7 us (20%)
  Pallas kernels  2.43 us (5%)
  between operations  0.94 us (2%)
  local copies, waits for them, and re-layouts  0.61 us (1%)
    ppermute x18, starting transfers between devices, from_partner(): return lax.ppermute(block, hop[0], route(*hop))  26 us
    ppermute x18, waiting for transfers between devices, from_partner(): return lax.ppermute(block, hop[0], route(*hop))  10.7 us
    dot_general x19, matrix products, times(): jnp.dot(matrix, value, preferred_element_type=jnp.float32)  6.16 us
    dot_general x5, matrix products, evaluated(): jnp.einsum('ct,cp->tp', coeffs, evaluation, preferred_element_type=jnp.fl...  5.61 us
    pallas_call x1, Pallas kernels, early(): pl.pallas_call(lambda *refs: early_kernel(starts, *refs), out_shape=[jax....  1.35 us
    pallas_call x1, Pallas kernels, tables(): pl.pallas_call(lambda *refs: tables_kernel(wide, rooms, *refs), out_shape...  1.07 us
  transfers between devices with their start and end apart: 18, of which 6 were waited for; matrix products, arithmetic and copies ran while one was open for 22% of the time, Pallas kernels for 2%

profile of v26, /device:TPU:0, one launch (start us, length us, event | category | flops | bytes accessed | tf_op | source)
XLA Modules:
  0.0 53.2 jit_solution(7749721754953090845)
XLA Ops:
  0.0 1.4 %early.1 = (bf16[128,128]{1,0:T(8,128)(2,1)S(1)}, bf16[128,640]{1,0:T(8,128)(2,1)S(1)}) custom-call(bf16[1,128,128]{2,1,0:T(8,128)(2,1)} %refs_0_.1, bf16[4096,128]{1,0:T(8,128)(2,1)} %refs_1_.2), custom_call_target="tpu_custom_call" | custom-call | flops 25165824 | bytes 393216 | tf_op jit(solution)/shard_map/early/pallas_call | solution.py:72
  1.4 3.0 %collective-permute-start.3 = (bf16[128,128]{1,0:T(8,128)(2,1)S(1)}, bf16[128,128]{1,0:T(8,128)(2,1)S(1)}, u32[]{:S(2)}, u32[]{:S(2)}) collective-permute-start(bf16[128,128]{1,0:T(8,128)(2,1)S(1)} %get-tuple-element.65), channel_id=1, source_target_pairs={{0,2},{2,0},{1,3},{3,1},{4,6},{6,4},{5,7},{7,5},{8,10},{10,8},{9,1... | collective-permute-start | bytes 98312 | tf_op jit(solution)/shard_map/ppermute | solution.py:36
  4.7 2.0 %collective-permute-start.7 = (bf16[128,1024]{1,0:T(8,128)(2,1)S(1)}, bf16[128,1024]{1,0:T(8,128)(2,1)S(1)}, u32[]{:S(2)}, u32[]{:S(2)}) collective-permute-start(bf16[128,1024]{1,0:T(8,128)(2,1)S(1)} %convolution_convert_fusion.21), channel_id=1, source_target_pairs={{0,2},{2,0},{1,3},{3,1},{4,6},{6,4},{5,7},{7,5},{8,10},{10,8},{9,1... | collective-permute-start | bytes 786440 | tf_op jit(solution)/shard_map/ppermute | solution.py:36
  6.7 1.1 %tables.1 = (bf16[3,128,256]{2,1,0:T(8,128)(2,1)S(1)}, bf16[2,128,256]{2,1,0:T(8,128)(2,1)S(1)}, bf16[2,128,128]{2,1,0:T(8,128)(2,1)S(1)}) custom-call(s32[3,1,64]{2,1,0:T(1,128)S(1)} %bitcast.101, bf16[1,3,64,128]{3,2,1,0:T(8,128)(2,1)S(1)} %copy-done.3), custom_call_target="tpu_custom_call" | custom-call | flops 50000000 | bytes 600000 | tf_op jit(solution)/shard_map/tables/pallas_call | solution.py:160
  8.1 1.6 %collective-permute-start.5 = (bf16[128,256]{1,0:T(8,128)(2,1)S(1)}, bf16[128,256]{1,0:T(8,128)(2,1)S(1)}, u32[]{:S(2)}, u32[]{:S(2)}) collective-permute-start(bf16[128,256]{1,0:T(8,128)(2,1)S(1)} %pad_maximum_fusion.12), channel_id=1, source_target_pairs={{0,4},{4,0},{8,12},{12,8},{1,5},{5,1},{9,13},{13,9},{2,6},{6,2},{1... | collective-permute-start | bytes 196616 | tf_op jit(solution)/shard_map/ppermute | solution.py:36
  9.7 2.6 %collective-permute-start.4 = (bf16[128,128]{1,0:T(8,128)(2,1)S(1)}, bf16[128,128]{1,0:T(8,128)(2,1)S(1)}, u32[]{:S(2)}, u32[]{:S(2)}) collective-permute-start(bf16[128,128]{1,0:T(8,128)(2,1)S(1)} %get-tuple-element.72), channel_id=1, source_target_pairs={{0,8},{8,0},{4,12},{12,4},{1,9},{9,1},{5,13},{13,5},{2,10},{10,2},... | collective-permute-start | bytes 98312 | tf_op jit(solution)/shard_map/ppermute | solution.py:36
  12.5 0.9 %collective-permute-start.8 = (bf16[128,640]{1,0:T(8,128)(2,1)S(1)}, bf16[128,640]{1,0:T(8,128)(2,1)S(1)}, u32[]{:S(2)}, u32[]{:S(2)}) collective-permute-start(bf16[128,640]{1,0:T(8,128)(2,1)S(1)} %convolution_convert_fusion.28), channel_id=1, source_target_pairs={{0,4},{4,0},{8,12},{12,8},{1,5},{5,1},{9,13},{13,9},{2,6},{6,2},{1... | collective-permute-start | bytes 491528 | tf_op jit(solution)/shard_map/ppermute | solution.py:36
  14.0 2.6 %collective-permute-start.14 = (bf16[128,128]{1,0:T(8,128)(2,1)S(1)}, bf16[128,128]{1,0:T(8,128)(2,1)S(1)}, u32[]{:S(2)}, u32[]{:S(2)}) collective-permute-start(bf16[128,128]{1,0:T(8,128)(2,1)S(1)} %convolution_convert_fusion.36), channel_id=1, source_target_pairs={{0,8},{8,0},{4,12},{12,4},{1,9},{9,1},{5,13},{13,5},{2,10},{10,2},... | collective-permute-start | bytes 98312 | tf_op jit(solution)/shard_map/ppermute | solution.py:36
  16.6 0.7 %collective-permute-start.10 = (bf16[128,1280]{1,0:T(8,128)(2,1)S(1)}, bf16[128,1280]{1,0:T(8,128)(2,1)S(1)}, u32[]{:S(2)}, u32[]{:S(2)}) collective-permute-start(bf16[128,1280]{1,0:T(8,128)(2,1)S(1)} %convolution_convert_fusion.9), channel_id=1, source_target_pairs={{0,2},{2,0},{1,3},{3,1},{4,6},{6,4},{5,7},{7,5},{8,10},{10,8},{9,1... | collective-permute-start | bytes 983048 | tf_op jit(solution)/shard_map/ppermute | solution.py:36
  17.8 0.9 %collective-permute-start.9 = (bf16[88,1024]{1,0:T(8,128)(2,1)S(1)}, bf16[88,1024]{1,0:T(8,128)(2,1)S(1)}, u32[]{:S(2)}, u32[]{:S(2)}) collective-permute-start(bf16[88,1024]{1,0:T(8,128)(2,1)S(1)} %convolution_convert_fusion.23), channel_id=1, source_target_pairs={{0,4},{4,0},{8,12},{12,8},{1,5},{5,1},{9,13},{13,9},{2,6},{6,2},{1... | collective-permute-start | bytes 540680 | tf_op jit(solution)/shard_map/ppermute | solution.py:36
  18.6 0.9 %convolution_convert_fusion.20 = bf16[128,1024]{1,0:T(8,128)(2,1)} fusion(bf16[128,256]{1,0:T(8,128)(2,1)S(1)} %get-tuple-element.92, bf16[128,1024]{1,0:T(8,128)(2,1)S(1)} %collective-permute-done.7, bf16[128,1024]{1,0:T(8,128)(2,1)S(1)} %convolution_convert_fusion.21), kind=kOutput, calls=%fused_computation.52 | convolution fusion | flops 68288512 | bytes 851968 | tf_op jit(solution)/shard_map/dot_general | solution.py:218
  20.1 3.0 %collective-permute-start.18 = (bf16[80,640]{1,0:T(8,128)(2,1)S(1)}, bf16[80,640]{1,0:T(8,128)(2,1)S(1)}, u32[]{:S(2)}, u32[]{:S(2)}) collective-permute-start(bf16[80,640]{1,0:T(8,128)(2,1)S(1)} %convolution_convert_fusion.30), channel_id=1, source_target_pairs={{0,8},{8,0},{4,12},{12,4},{1,9},{9,1},{5,13},{13,5},{2,10},{10,2},... | collective-permute-start | bytes 307208 | tf_op jit(solution)/shard_map/ppermute | solution.py:36
  23.9 0.9 %collective-permute-start.12 = (bf16[88,1280]{1,0:T(8,128)(2,1)S(1)}, bf16[88,1280]{1,0:T(8,128)(2,1)S(1)}, u32[]{:S(2)}, u32[]{:S(2)}) collective-permute-start(bf16[88,1280]{1,0:T(8,128)(2,1)S(1)} %convolution_convert_fusion.10), channel_id=1, source_target_pairs={{0,4},{4,0},{8,12},{12,8},{1,5},{5,1},{9,13},{13,9},{2,6},{6,2},{1... | collective-permute-start | bytes 675848 | tf_op jit(solution)/shard_map/ppermute | solution.py:36
  24.9 0.9 %collective-permute-done.9 = bf16[88,1024]{1,0:T(8,128)(2,1)S(1)} collective-permute-done((bf16[88,1024]{1,0:T(8,128)(2,1)S(1)}, bf16[88,1024]{1,0:T(8,128)(2,1)S(1)}, u32[]{:S(2)}, u32[]{:S(2)}) %collective-permute-start.9) | collective-permute-done | bytes 180256 | tf_op jit(solution)/shard_map/ppermute | solution.py:36
  26.0 1.7 %collective-permute-start.16 = (bf16[80,1024]{1,0:T(8,128)(2,1)S(1)}, bf16[80,1024]{1,0:T(8,128)(2,1)S(1)}, u32[]{:S(2)}, u32[]{:S(2)}) collective-permute-start(bf16[80,1024]{1,0:T(8,128)(2,1)S(1)} %convolution_convert_fusion.27), channel_id=1, source_target_pairs={{0,8},{8,0},{4,12},{12,4},{1,9},{9,1},{5,13},{13,5},{2,10},{10,2},... | collective-permute-start | bytes 491528 | tf_op jit(solution)/shard_map/ppermute | solution.py:36
  27.7 0.9 %convolution_convert_fusion.18 = bf16[128,1024]{1,0:T(8,128)(2,1)} fusion(bf16[128,256]{1,0:T(8,128)(2,1)S(1)} %slice_bitcast_fusion.7, bf16[88,1024]{1,0:T(8,128)(2,1)S(1)} %collective-permute-done.9, bf16[128,1024]{1,0:T(8,128)(2,1)S(1)} %copy-done.6), kind=kOutput, calls=%fused_computation.50 | convolution fusion | flops 69074944 | bytes 770048 | tf_op jit(solution)/shard_map/dot_general | solution.py:218
  28.7 0.7 %collective-permute-start.13 = (bf16[128,1024]{1,0:T(8,128)(2,1)S(1)}, bf16[128,1024]{1,0:T(8,128)(2,1)S(1)}, u32[]{:S(2)}, u32[]{:S(2)}) collective-permute-start(bf16[128,1024]{1,0:T(8,128)(2,1)S(1)} %convolution_convert_fusion.19), channel_id=1, source_target_pairs={{0,2},{2,0},{1,3},{3,1},{4,6},{6,4},{5,7},{7,5},{8,10},{10,8},{9,1... | collective-permute-start | bytes 786440 | tf_op jit(solution)/shard_map/ppermute | solution.py:36
  29.4 1.3 %collective-permute-start.11 = (bf16[8,128]{1,0:T(8,128)(2,1)S(1)}, bf16[8,128]{1,0:T(8,128)(2,1)S(1)}, u32[]{:S(2)}, u32[]{:S(2)}) collective-permute-start(bf16[8,128]{1,0:T(8,128)(2,1)S(1)} %slice_maximum_fusion), channel_id=1, source_target_pairs={{0,2},{2,0},{1,3},{3,1},{4,6},{6,4},{5,7},{7,5},{8,10},{10,8},{9,1... | collective-permute-start | bytes 6152 | tf_op jit(solution)/shard_map/ppermute | solution.py:36
  30.7 1.0 %constant_dynamic-update-slice_fusion.3 = bf16[4096,128]{1,0:T(8,128)(2,1)} fusion(bf16[1,128,128]{2,1,0:T(8,128)(2,1)S(1)} %copy-done.5, bf16[128,128]{1,0:T(8,128)(2,1)S(1)} %collective-permute-done.14, bf16[128,128]{1,0:T(8,128)(2,1)S(1)} %convolution_convert_fusion.36, bf16[3,128,256]{2,1,0:T(8,128)(2,1)S(1)} %get-tuple-element.68), kind=kOutput, calls=%fused_computation.147 | convolution fusion | flops 12746751 | bytes 196608 | tf_op jit(solution)/shard_map/ct,cp->tp/dot_general | solution.py:228
  31.9 3.1 %collective-permute-done.13 = bf16[128,1024]{1,0:T(8,128)(2,1)S(1)} collective-permute-done((bf16[128,1024]{1,0:T(8,128)(2,1)S(1)}, bf16[128,1024]{1,0:T(8,128)(2,1)S(1)}, u32[]{:S(2)}, u32[]{:S(2)}) %collective-permute-start.13) | collective-permute-done | bytes 262176 | tf_op jit(solution)/shard_map/ppermute | solution.py:36
  35.3 0.5 collective-permute-start.17
  36.0 1.1 %collective-permute-start.19 = (bf16[80,1280]{1,0:T(8,128)(2,1)S(1)}, bf16[80,1280]{1,0:T(8,128)(2,1)S(1)}, u32[]{:S(2)}, u32[]{:S(2)}) collective-permute-start(bf16[80,1280]{1,0:T(8,128)(2,1)S(1)} %convolution_convert_fusion.11), channel_id=1, source_target_pairs={{0,8},{8,0},{4,12},{12,4},{1,9},{9,1},{5,13},{13,5},{2,10},{10,2},... | collective-permute-start | bytes 614408 | tf_op jit(solution)/shard_map/ppermute | solution.py:36
  37.2 1.0 %convolution_convert_fusion.7 = bf16[128,1280]{1,0:T(8,128)(2,1)} fusion(bf16[128,256]{1,0:T(8,128)(2,1)S(1)} %slice_bitcast_fusion.7, bf16[88,1280]{1,0:T(8,128)(2,1)S(1)} %collective-permute-done.12, bf16[128,1280]{1,0:T(8,128)(2,1)S(1)} %convolution_convert_fusion.8), kind=kOutput, calls=%fused_computation.32 | convolution fusion | flops 86343680 | bytes 946176 | tf_op jit(solution)/shard_map/dot_general | solution.py:218
  38.1 2.0 %collective-permute-start.15 = (bf16[8,128]{1,0:T(8,128)(2,1)S(1)}, bf16[8,128]{1,0:T(8,128)(2,1)S(1)}, u32[]{:S(2)}, u32[]{:S(2)}) collective-permute-start(bf16[8,128]{1,0:T(8,128)(2,1)S(1)} %max.10), channel_id=1, source_target_pairs={{0,4},{4,0},{8,12},{12,8},{1,5},{5,1},{9,13},{13,9},{2,6},{6,2},{1... | collective-permute-start | bytes 6152 | tf_op jit(solution)/shard_map/ppermute | solution.py:36
  40.1 1.1 %constant_dynamic-update-slice_fusion.2 = bf16[4096,128]{1,0:T(8,128)(2,1)} fusion(bf16[4096,128]{1,0:T(8,128)(2,1)} %constant_dynamic-update-slice_fusion.3, bf16[1,128,128]{2,1,0:T(8,128)(2,1)S(1)} %copy-done.5, bf16[80,640]{1,0:T(8,128)(2,1)S(1)} %collective-permute-done.18, bf16[128,640]{1,0:T(8,128)(2,1)S(1)} %convolution_convert_fusion.26, ...), kind=kOutput, calls=%fused_computation.146 | convolution fusion | flops 64225280 | bytes 528384 | tf_op jit(solution)/shard_map/ct,cp->tp/dot_general | solution.py:228
  41.5 1.3 %collective-permute-done.17 = bf16[88,1024]{1,0:T(8,128)(2,1)S(1)} collective-permute-done((bf16[88,1024]{1,0:T(8,128)(2,1)S(1)}, bf16[88,1024]{1,0:T(8,128)(2,1)S(1)}, u32[]{:S(2)}, u32[]{:S(2)}) %collective-permute-start.17) | collective-permute-done | bytes 180256 | tf_op jit(solution)/shard_map/ppermute | solution.py:36
  43.3 1.2 %constant_dynamic-update-slice_fusion.1 = bf16[4096,128]{1,0:T(8,128)(2,1)} fusion(bf16[4096,128]{1,0:T(8,128)(2,1)} %constant_dynamic-update-slice_fusion.2, bf16[1,128,128]{2,1,0:T(8,128)(2,1)S(1)} %copy-done.5, bf16[80,1024]{1,0:T(8,128)(2,1)S(1)} %collective-permute-done.16, bf16[128,1024]{1,0:T(8,128)(2,1)S(1)} %copy-done.7, ...), kind=kOutput, calls=%fused_computation.145 | convolution fusion | flops 102760448 | bytes 786432 | tf_op jit(solution)/shard_map/ct,cp->tp/dot_general | solution.py:228
  44.5 0.5 %slice.107 = bf16[1,1]{1,0:T(2,128)(2,1)} slice(bf16[8,128]{1,0:T(8,128)(2,1)S(1)} %max.11), slice={[0:1], [0:1]} | slice | bytes 4 | tf_op jit(solution)/shard_map/slice | solution.py:331
  45.9 3.8 %collective-permute-done.19 = bf16[80,1280]{1,0:T(8,128)(2,1)S(1)} collective-permute-done((bf16[80,1280]{1,0:T(8,128)(2,1)S(1)}, bf16[80,1280]{1,0:T(8,128)(2,1)S(1)}, u32[]{:S(2)}, u32[]{:S(2)}) %collective-permute-start.19) | collective-permute-done | bytes 204832 | tf_op jit(solution)/shard_map/ppermute | solution.py:36
  49.7 1.2 %constant_dynamic-update-slice_fusion = bf16[4096,128]{1,0:T(8,128)(2,1)} fusion(bf16[4096,128]{1,0:T(8,128)(2,1)} %constant_dynamic-update-slice_fusion.1, bf16[1,128,128]{2,1,0:T(8,128)(2,1)S(1)} %copy-done.5, bf16[80,1280]{1,0:T(8,128)(2,1)S(1)} %collective-permute-done.19, bf16[128,1280]{1,0:T(8,128)(2,1)S(1)} %copy-done.8, ...), kind=kOutput, calls=%fused_computation.144 | convolution fusion | flops 128450560 | bytes 958464 | tf_op jit(solution)/shard_map/ct,cp->tp/dot_general | solution.py:228
  51.0 1.1 %collective-permute-done.20 = bf16[80,1024]{1,0:T(8,128)(2,1)S(1)} collective-permute-done((bf16[80,1024]{1,0:T(8,128)(2,1)S(1)}, bf16[80,1024]{1,0:T(8,128)(2,1)S(1)}, u32[]{:S(2)}, u32[]{:S(2)}) %collective-permute-start.20) | collective-permute-done | bytes 163872 | tf_op jit(solution)/shard_map/ppermute | solution.py:36
  52.1 1.2 %fusion.24 = bf16[4096,128]{1,0:T(8,128)(2,1)} fusion(bf16[4096,128]{1,0:T(8,128)(2,1)} %constant_dynamic-update-slice_fusion, bf16[80,1024]{1,0:T(8,128)(2,1)S(1)} %collective-permute-done.20, bf16[128,1024]{1,0:T(8,128)(2,1)S(1)} %convolution_convert_fusion.14, bf16[2,128,256]{2,1,0:T(8,128)(2,1)S(1)} %get-tuple-element.79, ...), kind=kOutput, calls=%fused_computation.44 | convolution fusion | flops 102760448 | bytes 786432 | tf_op jit(solution)/shard_map/ct,cp->tp/dot_general | solution.py:228
  (59 shorter events, 4.9 us)
Async XLA Ops:
  0.0 4.5 %copy-start = (bf16[4096,128]{1,0:T(8,128)(2,1)S(1)}, bf16[4096,128]{1,0:T(8,128)(2,1)}, u32[]{:S(2)}) copy-start(bf16[4096,128]{1,0:T(8,128)(2,1)} %refs_1_.2) | copy-start | bytes 3145732
  0.0 4.5 %copy-start.2 = (bf16[1,128,128]{2,1,0:T(8,128)(2,1)S(1)}, bf16[1,128,128]{2,1,0:T(8,128)(2,1)}, u32[]{:S(2)}) copy-start(bf16[1,128,128]{2,1,0:T(8,128)(2,1)} %refs_0_.1) | copy-start | bytes 98308
  0.0 6.7 %copy-start.4 = (s32[1,3,64]{2,0,1:T(1,128)S(1)}, s32[1,3,64]{2,0,1:T(1,128)}, u32[]{:S(2)}) copy-start(s32[1,3,64]{2,0,1:T(1,128)} %param.9) | copy-start | bytes 2308
  0.0 6.7 %copy-start.3 = (bf16[1,3,64,128]{3,2,1,0:T(8,128)(2,1)S(1)}, bf16[1,3,64,128]{3,2,1,0:T(8,128)(2,1)}, u32[]{:S(2)}) copy-start(bf16[1,3,64,128]{3,2,1,0:T(8,128)(2,1)} %refs_1_.3) | copy-start | bytes 147460
  1.4 6.5 %collective-permute-start.3 = (bf16[128,128]{1,0:T(8,128)(2,1)S(1)}, bf16[128,128]{1,0:T(8,128)(2,1)S(1)}, u32[]{:S(2)}, u32[]{:S(2)}) collective-permute-start(bf16[128,128]{1,0:T(8,128)(2,1)S(1)} %get-tuple-element.65), channel_id=1, source_target_pairs={{0,2},{2,0},{1,3},{3,1},{4,6},{6,4},{5,7},{7,5},{8,10},{10,8},{9,1... | collective-permute-start | bytes 98312 | tf_op jit(solution)/shard_map/ppermute | solution.py:36
  4.4 7.9 %collective-permute-start.6 = (bf16[128,640]{1,0:T(8,128)(2,1)S(1)}, bf16[128,640]{1,0:T(8,128)(2,1)S(1)}, u32[]{:S(2)}, u32[]{:S(2)}) collective-permute-start(bf16[128,640]{1,0:T(8,128)(2,1)S(1)} %get-tuple-element.69), channel_id=1, source_target_pairs={{0,2},{2,0},{1,3},{3,1},{4,6},{6,4},{5,7},{7,5},{8,10},{10,8},{9,1... | collective-permute-start | bytes 491528 | tf_op jit(solution)/shard_map/ppermute | solution.py:36
  4.7 12.8 %collective-permute-start.7 = (bf16[128,1024]{1,0:T(8,128)(2,1)S(1)}, bf16[128,1024]{1,0:T(8,128)(2,1)S(1)}, u32[]{:S(2)}, u32[]{:S(2)}) collective-permute-start(bf16[128,1024]{1,0:T(8,128)(2,1)S(1)} %convolution_convert_fusion.21), channel_id=1, source_target_pairs={{0,2},{2,0},{1,3},{3,1},{4,6},{6,4},{5,7},{7,5},{8,10},{10,8},{9,1... | collective-permute-start | bytes 786440 | tf_op jit(solution)/shard_map/ppermute | solution.py:36
  8.1 5.6 %collective-permute-start.5 = (bf16[128,256]{1,0:T(8,128)(2,1)S(1)}, bf16[128,256]{1,0:T(8,128)(2,1)S(1)}, u32[]{:S(2)}, u32[]{:S(2)}) collective-permute-start(bf16[128,256]{1,0:T(8,128)(2,1)S(1)} %pad_maximum_fusion.12), channel_id=1, source_target_pairs={{0,4},{4,0},{8,12},{12,8},{1,5},{5,1},{9,13},{13,9},{2,6},{6,2},{1... | collective-permute-start | bytes 196616 | tf_op jit(solution)/shard_map/ppermute | solution.py:36
  9.7 9.9 %collective-permute-start.4 = (bf16[128,128]{1,0:T(8,128)(2,1)S(1)}, bf16[128,128]{1,0:T(8,128)(2,1)S(1)}, u32[]{:S(2)}, u32[]{:S(2)}) collective-permute-start(bf16[128,128]{1,0:T(8,128)(2,1)S(1)} %get-tuple-element.72), channel_id=1, source_target_pairs={{0,8},{8,0},{4,12},{12,4},{1,9},{9,1},{5,13},{13,5},{2,10},{10,2},... | collective-permute-start | bytes 98312 | tf_op jit(solution)/shard_map/ppermute | solution.py:36
  12.5 7.1 %collective-permute-start.8 = (bf16[128,640]{1,0:T(8,128)(2,1)S(1)}, bf16[128,640]{1,0:T(8,128)(2,1)S(1)}, u32[]{:S(2)}, u32[]{:S(2)}) collective-permute-start(bf16[128,640]{1,0:T(8,128)(2,1)S(1)} %convolution_convert_fusion.28), channel_id=1, source_target_pairs={{0,4},{4,0},{8,12},{12,8},{1,5},{5,1},{9,13},{13,9},{2,6},{6,2},{1... | collective-permute-start | bytes 491528 | tf_op jit(solution)/shard_map/ppermute | solution.py:36
  14.0 15.4 %collective-permute-start.14 = (bf16[128,128]{1,0:T(8,128)(2,1)S(1)}, bf16[128,128]{1,0:T(8,128)(2,1)S(1)}, u32[]{:S(2)}, u32[]{:S(2)}) collective-permute-start(bf16[128,128]{1,0:T(8,128)(2,1)S(1)} %convolution_convert_fusion.36), channel_id=1, source_target_pairs={{0,8},{8,0},{4,12},{12,4},{1,9},{9,1},{5,13},{13,5},{2,10},{10,2},... | collective-permute-start | bytes 98312 | tf_op jit(solution)/shard_map/ppermute | solution.py:36
  16.6 7.1 %collective-permute-start.10 = (bf16[128,1280]{1,0:T(8,128)(2,1)S(1)}, bf16[128,1280]{1,0:T(8,128)(2,1)S(1)}, u32[]{:S(2)}, u32[]{:S(2)}) collective-permute-start(bf16[128,1280]{1,0:T(8,128)(2,1)S(1)} %convolution_convert_fusion.9), channel_id=1, source_target_pairs={{0,2},{2,0},{1,3},{3,1},{4,6},{6,4},{5,7},{7,5},{8,10},{10,8},{9,1... | collective-permute-start | bytes 983048 | tf_op jit(solution)/shard_map/ppermute | solution.py:36
  17.8 8.0 %collective-permute-start.9 = (bf16[88,1024]{1,0:T(8,128)(2,1)S(1)}, bf16[88,1024]{1,0:T(8,128)(2,1)S(1)}, u32[]{:S(2)}, u32[]{:S(2)}) collective-permute-start(bf16[88,1024]{1,0:T(8,128)(2,1)S(1)} %convolution_convert_fusion.23), channel_id=1, source_target_pairs={{0,4},{4,0},{8,12},{12,8},{1,5},{5,1},{9,13},{13,9},{2,6},{6,2},{1... | collective-permute-start | bytes 540680 | tf_op jit(solution)/shard_map/ppermute | solution.py:36
  20.0 5.8 %copy-start.6 = (bf16[128,1024]{1,0:T(8,128)(2,1)S(1)}, bf16[128,1024]{1,0:T(8,128)(2,1)}, u32[]{:S(2)}) copy-start(bf16[128,1024]{1,0:T(8,128)(2,1)} %convolution_convert_fusion.20) | copy-start | bytes 786436
  20.1 18.1 %collective-permute-start.18 = (bf16[80,640]{1,0:T(8,128)(2,1)S(1)}, bf16[80,640]{1,0:T(8,128)(2,1)S(1)}, u32[]{:S(2)}, u32[]{:S(2)}) collective-permute-start(bf16[80,640]{1,0:T(8,128)(2,1)S(1)} %convolution_convert_fusion.30), channel_id=1, source_target_pairs={{0,8},{8,0},{4,12},{12,4},{1,9},{9,1},{5,13},{13,5},{2,10},{10,2},... | collective-permute-start | bytes 307208 | tf_op jit(solution)/shard_map/ppermute | solution.py:36
  23.9 11.8 %collective-permute-start.12 = (bf16[88,1280]{1,0:T(8,128)(2,1)S(1)}, bf16[88,1280]{1,0:T(8,128)(2,1)S(1)}, u32[]{:S(2)}, u32[]{:S(2)}) collective-permute-start(bf16[88,1280]{1,0:T(8,128)(2,1)S(1)} %convolution_convert_fusion.10), channel_id=1, source_target_pairs={{0,4},{4,0},{8,12},{12,8},{1,5},{5,1},{9,13},{13,9},{2,6},{6,2},{1... | collective-permute-start | bytes 675848 | tf_op jit(solution)/shard_map/ppermute | solution.py:36
  26.0 4.7 %copy-start.5 = (bf16[1,128,128]{2,1,0:T(8,128)(2,1)S(1)}, bf16[1,128,128]{2,1,0:T(8,128)(2,1)}, u32[]{:S(2)}) copy-start(bf16[1,128,128]{2,1,0:T(8,128)(2,1)} %param.11) | copy-start | bytes 98308
  26.0 17.3 %collective-permute-start.16 = (bf16[80,1024]{1,0:T(8,128)(2,1)S(1)}, bf16[80,1024]{1,0:T(8,128)(2,1)S(1)}, u32[]{:S(2)}, u32[]{:S(2)}) collective-permute-start(bf16[80,1024]{1,0:T(8,128)(2,1)S(1)} %convolution_convert_fusion.27), channel_id=1, source_target_pairs={{0,8},{8,0},{4,12},{12,4},{1,9},{9,1},{5,13},{13,5},{2,10},{10,2},... | collective-permute-start | bytes 491528 | tf_op jit(solution)/shard_map/ppermute | solution.py:36
  28.7 6.4 %collective-permute-start.13 = (bf16[128,1024]{1,0:T(8,128)(2,1)S(1)}, bf16[128,1024]{1,0:T(8,128)(2,1)S(1)}, u32[]{:S(2)}, u32[]{:S(2)}) collective-permute-start(bf16[128,1024]{1,0:T(8,128)(2,1)S(1)} %convolution_convert_fusion.19), channel_id=1, source_target_pairs={{0,2},{2,0},{1,3},{3,1},{4,6},{6,4},{5,7},{7,5},{8,10},{10,8},{9,1... | collective-permute-start | bytes 786440 | tf_op jit(solution)/shard_map/ppermute | solution.py:36
  29.4 8.8 %collective-permute-start.11 = (bf16[8,128]{1,0:T(8,128)(2,1)S(1)}, bf16[8,128]{1,0:T(8,128)(2,1)S(1)}, u32[]{:S(2)}, u32[]{:S(2)}) collective-permute-start(bf16[8,128]{1,0:T(8,128)(2,1)S(1)} %slice_maximum_fusion), channel_id=1, source_target_pairs={{0,2},{2,0},{1,3},{3,1},{4,6},{6,4},{5,7},{7,5},{8,10},{10,8},{9,1... | collective-permute-start | bytes 6152 | tf_op jit(solution)/shard_map/ppermute | solution.py:36
  35.3 7.5 %collective-permute-start.17 = (bf16[88,1024]{1,0:T(8,128)(2,1)S(1)}, bf16[88,1024]{1,0:T(8,128)(2,1)S(1)}, u32[]{:S(2)}, u32[]{:S(2)}) collective-permute-start(bf16[88,1024]{1,0:T(8,128)(2,1)S(1)} %convolution_convert_fusion.22), channel_id=1, source_target_pairs={{0,4},{4,0},{8,12},{12,8},{1,5},{5,1},{9,13},{13,9},{2,6},{6,2},{1... | collective-permute-start | bytes 540680 | tf_op jit(solution)/shard_map/ppermute | solution.py:36
  36.0 13.7 %collective-permute-start.19 = (bf16[80,1280]{1,0:T(8,128)(2,1)S(1)}, bf16[80,1280]{1,0:T(8,128)(2,1)S(1)}, u32[]{:S(2)}, u32[]{:S(2)}) collective-permute-start(bf16[80,1280]{1,0:T(8,128)(2,1)S(1)} %convolution_convert_fusion.11), channel_id=1, source_target_pairs={{0,8},{8,0},{4,12},{12,4},{1,9},{9,1},{5,13},{13,5},{2,10},{10,2},... | collective-permute-start | bytes 614408 | tf_op jit(solution)/shard_map/ppermute | solution.py:36
  38.1 6.3 %collective-permute-start.15 = (bf16[8,128]{1,0:T(8,128)(2,1)S(1)}, bf16[8,128]{1,0:T(8,128)(2,1)S(1)}, u32[]{:S(2)}, u32[]{:S(2)}) collective-permute-start(bf16[8,128]{1,0:T(8,128)(2,1)S(1)} %max.10), channel_id=1, source_target_pairs={{0,4},{4,0},{8,12},{12,8},{1,5},{5,1},{9,13},{13,9},{2,6},{6,2},{1... | collective-permute-start | bytes 6152 | tf_op jit(solution)/shard_map/ppermute | solution.py:36
  41.5 1.8 %copy-start.7 = (bf16[128,1024]{1,0:T(8,128)(2,1)S(1)}, bf16[128,1024]{1,0:T(8,128)(2,1)}, u32[]{:S(2)}) copy-start(bf16[128,1024]{1,0:T(8,128)(2,1)} %convolution_convert_fusion.18) | copy-start | bytes 786436
  43.0 9.0 %collective-permute-start.20 = (bf16[80,1024]{1,0:T(8,128)(2,1)S(1)}, bf16[80,1024]{1,0:T(8,128)(2,1)S(1)}, u32[]{:S(2)}, u32[]{:S(2)}) collective-permute-start(bf16[80,1024]{1,0:T(8,128)(2,1)S(1)} %convolution_convert_fusion.24), channel_id=1, source_target_pairs={{0,8},{8,0},{4,12},{12,4},{1,9},{9,1},{5,13},{13,5},{2,10},{10,2},... | collective-permute-start | bytes 491528 | tf_op jit(solution)/shard_map/ppermute | solution.py:36
  45.7 4.1 %copy-start.8 = (bf16[128,1280]{1,0:T(8,128)(2,1)S(1)}, bf16[128,1280]{1,0:T(8,128)(2,1)}, u32[]{:S(2)}) copy-start(bf16[128,1280]{1,0:T(8,128)(2,1)} %convolution_convert_fusion.7) | copy-start | bytes 983044

commit v27 on v20

--- a/solution.py
+++ b/solution.py
@@ -323,12 +323,13 @@
             block = extra[level - wide]
             if known is not None:
                 block = jnp.where(most_here, jnp.maximum(block, known), block)
+            so_far = block
             outgoing = jnp.concatenate([outgoing, block], 1)
         inputs[piece] = own
         partners[piece] = from_partner(outgoing, hops[level])
         previous = outgoing
         if (level, piece) == (levels - 1, COUNT_PIECE):
-            most = after(jnp.maximum(extra[levels - 1 - wide], known)[:8, rank:], outgoing)
+            most = after(jnp.maximum(so_far, known)[:8, rank:], outgoing)
             for hop in hops[: wide - 1]:
                 most = jnp.maximum(most, from_partner(most, hop))
             counted = from_partner(most, hops[wide - 1])

time: 52.5 us -> 52.4 us (level)
  no operation moved by 1% of the time
where the time goes in v27:
time: 52.4 us; the launch traced here: 52.2 us
  starting transfers between devices  23.3 us (44%)
  waiting for transfers between devices  12.5 us (24%)
  matrix products  12.3 us (23%)
  Pallas kernels  2.51 us (5%)
  between operations  0.91 us (2%)
  local copies, waits for them, and re-layouts  0.62 us (1%)
    ppermute x16, starting transfers between devices, from_partner(): return lax.ppermute(block, hop[0], route(*hop))  23.3 us
    ppermute x16, waiting for transfers between devices, from_partner(): return lax.ppermute(block, hop[0], route(*hop))  12.5 us
    dot_general x5, matrix products, evaluated(): jnp.einsum('ct,cp->tp', coeffs, evaluation, preferred_element_type=jnp.fl...  5.64 us
    dot_general x17, matrix products, times(): jnp.dot(matrix, value, preferred_element_type=jnp.float32)  5.15 us
    pallas_call x1, Pallas kernels, early(): pl.pallas_call(lambda *refs: early_kernel(starts, *refs), out_shape=[jax....  1.45 us
    pallas_call x1, Pallas kernels, tables(): pl.pallas_call(lambda *refs: tables_kernel(wide, rooms, *refs), out_shape...  1.06 us
  transfers between devices with their start and end apart: 16, of which 7 were waited for; matrix products, arithmetic and copies ran while one was open for 23% of the time, Pallas kernels for 2%

profile of v27, /device:TPU:0, one launch (start us, length us, event | category | flops | bytes accessed | tf_op | source)
XLA Modules:
  0.0 52.2 jit_solution(5194028390464026317)
XLA Ops:
  0.0 1.4 %early.1 = (bf16[128,256]{1,0:T(8,128)(2,1)S(1)}, bf16[128,640]{1,0:T(8,128)(2,1)S(1)}) custom-call(bf16[1,128,128]{2,1,0:T(8,128)(2,1)} %refs_0_.1, bf16[4096,128]{1,0:T(8,128)(2,1)} %refs_1_.2), custom_call_target="tpu_custom_call" | custom-call | flops 29360128 | bytes 458752 | tf_op jit(solution)/shard_map/early/pallas_call | solution.py:70
  1.5 3.0 %collective-permute-start.3 = (bf16[128,256]{1,0:T(8,128)(2,1)S(1)}, bf16[128,256]{1,0:T(8,128)(2,1)S(1)}, u32[]{:S(2)}, u32[]{:S(2)}) collective-permute-start(bf16[128,256]{1,0:T(8,128)(2,1)S(1)} %get-tuple-element.64), channel_id=1, source_target_pairs={{0,2},{2,0},{1,3},{3,1},{4,6},{6,4},{5,7},{7,5},{8,10},{10,8},{9,1... | collective-permute-start | bytes 196616 | tf_op jit(solution)/shard_map/ppermute | solution.py:34
  4.6 0.3 convolution_convert_fusion.14
  4.8 2.0 %collective-permute-start.7 = (bf16[128,1152]{1,0:T(8,128)(2,1)S(1)}, bf16[128,1152]{1,0:T(8,128)(2,1)S(1)}, u32[]{:S(2)}, u32[]{:S(2)}) collective-permute-start(bf16[128,1152]{1,0:T(8,128)(2,1)S(1)} %convolution_convert_fusion.14), channel_id=1, source_target_pairs={{0,2},{2,0},{1,3},{3,1},{4,6},{6,4},{5,7},{7,5},{8,10},{10,8},{9,1... | collective-permute-start | bytes 884744 | tf_op jit(solution)/shard_map/ppermute | solution.py:34
  6.8 1.1 %tables.1 = (bf16[3,128,256]{2,1,0:T(8,128)(2,1)S(1)}, bf16[2,128,256]{2,1,0:T(8,128)(2,1)S(1)}, bf16[2,128,128]{2,1,0:T(8,128)(2,1)S(1)}) custom-call(s32[3,1,64]{2,1,0:T(1,128)S(1)} %bitcast.109, bf16[1,3,64,128]{3,2,1,0:T(8,128)(2,1)S(1)} %copy-done.4), custom_call_target="tpu_custom_call" | custom-call | flops 50000000 | bytes 600000 | tf_op jit(solution)/shard_map/tables/pallas_call | solution.py:156
  8.2 1.6 %collective-permute-start.4 = (bf16[128,384]{1,0:T(8,128)(2,1)S(1)}, bf16[128,384]{1,0:T(8,128)(2,1)S(1)}, u32[]{:S(2)}, u32[]{:S(2)}) collective-permute-start(bf16[128,384]{1,0:T(8,128)(2,1)S(1)} %pad_maximum_fusion.12), channel_id=1, source_target_pairs={{0,4},{4,0},{8,12},{12,8},{1,5},{5,1},{9,13},{13,9},{2,6},{6,2},{1... | collective-permute-start | bytes 294920 | tf_op jit(solution)/shard_map/ppermute | solution.py:34
  9.8 1.8 %collective-permute-done.5 = bf16[128,640]{1,0:T(8,128)(2,1)S(1)} collective-permute-done((bf16[128,640]{1,0:T(8,128)(2,1)S(1)}, bf16[128,640]{1,0:T(8,128)(2,1)S(1)}, u32[]{:S(2)}, u32[]{:S(2)}) %collective-permute-start.5) | collective-permute-done | bytes 163872 | tf_op jit(solution)/shard_map/ppermute | solution.py:34
  11.8 1.6 %collective-permute-start.8 = (bf16[128,640]{1,0:T(8,128)(2,1)S(1)}, bf16[128,640]{1,0:T(8,128)(2,1)S(1)}, u32[]{:S(2)}, u32[]{:S(2)}) collective-permute-start(bf16[128,640]{1,0:T(8,128)(2,1)S(1)} %convolution_convert_fusion.26), channel_id=1, source_target_pairs={{0,4},{4,0},{8,12},{12,8},{1,5},{5,1},{9,13},{13,9},{2,6},{6,2},{1... | collective-permute-start | bytes 491528 | tf_op jit(solution)/shard_map/ppermute | solution.py:34
  14.2 2.7 %collective-permute-start.6 = (bf16[128,384]{1,0:T(8,128)(2,1)S(1)}, bf16[128,384]{1,0:T(8,128)(2,1)S(1)}, u32[]{:S(2)}, u32[]{:S(2)}) collective-permute-start(bf16[128,384]{1,0:T(8,128)(2,1)S(1)} %pad_maximum_fusion.13), channel_id=1, source_target_pairs={{0,8},{8,0},{4,12},{12,4},{1,9},{9,1},{5,13},{13,5},{2,10},{10,2},... | collective-permute-start | bytes 294920 | tf_op jit(solution)/shard_map/ppermute | solution.py:34
  16.9 1.4 %collective-permute-start.10 = (bf16[128,1152]{1,0:T(8,128)(2,1)S(1)}, bf16[128,1152]{1,0:T(8,128)(2,1)S(1)}, u32[]{:S(2)}, u32[]{:S(2)}) collective-permute-start(bf16[128,1152]{1,0:T(8,128)(2,1)S(1)} %convolution_convert_fusion.13), channel_id=1, source_target_pairs={{0,2},{2,0},{1,3},{3,1},{4,6},{6,4},{5,7},{7,5},{8,10},{10,8},{9,1... | collective-permute-start | bytes 884744 | tf_op jit(solution)/shard_map/ppermute | solution.py:34
  18.7 1.6 %collective-permute-start.9 = (bf16[88,1152]{1,0:T(8,128)(2,1)S(1)}, bf16[88,1152]{1,0:T(8,128)(2,1)S(1)}, u32[]{:S(2)}, u32[]{:S(2)}) collective-permute-start(bf16[88,1152]{1,0:T(8,128)(2,1)S(1)} %convolution_convert_fusion.16), channel_id=1, source_target_pairs={{0,4},{4,0},{8,12},{12,8},{1,5},{5,1},{9,13},{13,9},{2,6},{6,2},{1... | collective-permute-start | bytes 608264 | tf_op jit(solution)/shard_map/ppermute | solution.py:34
  20.3 0.6 %collective-permute-done.6 = bf16[128,384]{1,0:T(8,128)(2,1)S(1)} collective-permute-done((bf16[128,384]{1,0:T(8,128)(2,1)S(1)}, bf16[128,384]{1,0:T(8,128)(2,1)S(1)}, u32[]{:S(2)}, u32[]{:S(2)}) %collective-permute-start.6) | collective-permute-done | bytes 98336 | tf_op jit(solution)/shard_map/ppermute | solution.py:34
  22.0 2.2 %collective-permute-start.15 = (bf16[80,640]{1,0:T(8,128)(2,1)S(1)}, bf16[80,640]{1,0:T(8,128)(2,1)S(1)}, u32[]{:S(2)}, u32[]{:S(2)}) collective-permute-start(bf16[80,640]{1,0:T(8,128)(2,1)S(1)} %convolution_convert_fusion.30), channel_id=1, source_target_pairs={{0,8},{8,0},{4,12},{12,4},{1,9},{9,1},{5,13},{13,5},{2,10},{10,2},... | collective-permute-start | bytes 307208 | tf_op jit(solution)/shard_map/ppermute | solution.py:34
  24.7 0.6 %collective-permute-start.16 = (bf16[88,1152]{1,0:T(8,128)(2,1)S(1)}, bf16[88,1152]{1,0:T(8,128)(2,1)S(1)}, u32[]{:S(2)}, u32[]{:S(2)}) collective-permute-start(bf16[88,1152]{1,0:T(8,128)(2,1)S(1)} %convolution_convert_fusion.15), channel_id=1, source_target_pairs={{0,4},{4,0},{8,12},{12,8},{1,5},{5,1},{9,13},{13,9},{2,6},{6,2},{1... | collective-permute-start | bytes 608264 | tf_op jit(solution)/shard_map/ppermute | solution.py:34
  25.6 1.1 %collective-permute-done.9 = bf16[88,1152]{1,0:T(8,128)(2,1)S(1)} collective-permute-done((bf16[88,1152]{1,0:T(8,128)(2,1)S(1)}, bf16[88,1152]{1,0:T(8,128)(2,1)S(1)}, u32[]{:S(2)}, u32[]{:S(2)}) %collective-permute-start.9) | collective-permute-done | bytes 202784 | tf_op jit(solution)/shard_map/ppermute | solution.py:34
  26.9 1.6 %collective-permute-start.12 = (bf16[80,1152]{1,0:T(8,128)(2,1)S(1)}, bf16[80,1152]{1,0:T(8,128)(2,1)S(1)}, u32[]{:S(2)}, u32[]{:S(2)}) collective-permute-start(bf16[80,1152]{1,0:T(8,128)(2,1)S(1)} %convolution_convert_fusion.18), channel_id=1, source_target_pairs={{0,8},{8,0},{4,12},{12,4},{1,9},{9,1},{5,13},{13,5},{2,10},{10,2},... | collective-permute-start | bytes 552968 | tf_op jit(solution)/shard_map/ppermute | solution.py:34
  28.4 1.1 %collective-permute-start.13 = (bf16[128,896]{1,0:T(8,128)(2,1)S(1)}, bf16[128,896]{1,0:T(8,128)(2,1)S(1)}, u32[]{:S(2)}, u32[]{:S(2)}) collective-permute-start(bf16[128,896]{1,0:T(8,128)(2,1)S(1)} %convolution_convert_fusion.23), channel_id=1, source_target_pairs={{0,2},{2,0},{1,3},{3,1},{4,6},{6,4},{5,7},{7,5},{8,10},{10,8},{9,1... | collective-permute-start | bytes 688136 | tf_op jit(solution)/shard_map/ppermute | solution.py:34
  29.5 1.0 %convolution_convert_fusion.11 = bf16[128,1152]{1,0:T(8,128)(2,1)} fusion(bf16[128,256]{1,0:T(8,128)(2,1)S(1)} %slice_bitcast_fusion.7, bf16[88,1152]{1,0:T(8,128)(2,1)S(1)} %collective-permute-done.9, bf16[128,1152]{1,0:T(8,128)(2,1)S(1)} %convolution_convert_fusion.12), kind=kOutput, calls=%fused_computation.36 | convolution fusion | flops 77709312 | bytes 858112 | tf_op jit(solution)/shard_map/dot_general | solution.py:223
  30.5 1.0 %collective-permute-start.11 = (bf16[8,64]{1,0:T(8,128)(2,1)S(1)}, bf16[8,64]{1,0:T(8,128)(2,1)S(1)}, u32[]{:S(2)}, u32[]{:S(2)}) collective-permute-start(bf16[8,64]{1,0:T(8,128)(2,1)S(1)} %slice_maximum_fusion), channel_id=1, source_target_pairs={{0,2},{2,0},{1,3},{3,1},{4,6},{6,4},{5,7},{7,5},{8,10},{10,8},{9,1... | collective-permute-start | bytes 3080 | tf_op jit(solution)/shard_map/ppermute | solution.py:34
  31.4 1.0 %constant_dynamic-update-slice_fusion.3 = bf16[4096,128]{1,0:T(8,128)(2,1)} fusion(bf16[1,128,128]{2,1,0:T(8,128)(2,1)S(1)} %copy-done.6, bf16[128,256]{1,0:T(8,128)(2,1)S(1)} %slice-done, bf16[128,256]{1,0:T(8,128)(2,1)S(1)} %convolution_convert_fusion.33, bf16[3,128,256]{2,1,0:T(8,128)(2,1)S(1)} %get-tuple-element.67), kind=kOutput, calls=%fused_computation.165 | convolution fusion | flops 25493504 | bytes 294912 | tf_op jit(solution)/shard_map/ct,cp->tp/dot_general | solution.py:233
  32.4 2.2 %collective-permute-done.13 = bf16[128,896]{1,0:T(8,128)(2,1)S(1)} collective-permute-done((bf16[128,896]{1,0:T(8,128)(2,1)S(1)}, bf16[128,896]{1,0:T(8,128)(2,1)S(1)}, u32[]{:S(2)}, u32[]{:S(2)}) %collective-permute-start.13) | collective-permute-done | bytes 229408 | tf_op jit(solution)/shard_map/ppermute | solution.py:34
  34.9 0.7 %collective-permute-start.14 = (bf16[88,896]{1,0:T(8,128)(2,1)S(1)}, bf16[88,896]{1,0:T(8,128)(2,1)S(1)}, u32[]{:S(2)}, u32[]{:S(2)}) collective-permute-start(bf16[88,896]{1,0:T(8,128)(2,1)S(1)} %convolution_convert_fusion.28), channel_id=1, source_target_pairs={{0,4},{4,0},{8,12},{12,8},{1,5},{5,1},{9,13},{13,9},{2,6},{6,2},{1... | collective-permute-start | bytes 473096 | tf_op jit(solution)/shard_map/ppermute | solution.py:34
  35.9 1.9 %collective-permute-start.17 = (bf16[80,1152]{1,0:T(8,128)(2,1)S(1)}, bf16[80,1152]{1,0:T(8,128)(2,1)S(1)}, u32[]{:S(2)}, u32[]{:S(2)}) collective-permute-start(bf16[80,1152]{1,0:T(8,128)(2,1)S(1)} %convolution_convert_fusion.17), channel_id=1, source_target_pairs={{0,8},{8,0},{4,12},{12,4},{1,9},{9,1},{5,13},{13,5},{2,10},{10,2},... | collective-permute-start | bytes 552968 | tf_op jit(solution)/shard_map/ppermute | solution.py:34
  37.8 1.0 %convolution_convert_fusion.7 = bf16[128,1152]{1,0:T(8,128)(2,1)} fusion(bf16[128,256]{1,0:T(8,128)(2,1)S(1)} %slice_bitcast_fusion.7, bf16[88,1152]{1,0:T(8,128)(2,1)S(1)} %collective-permute-done.16, bf16[128,1152]{1,0:T(8,128)(2,1)S(1)} %convolution_convert_fusion.10), kind=kOutput, calls=%fused_computation.32 | convolution fusion | flops 77709312 | bytes 858112 | tf_op jit(solution)/shard_map/dot_general | solution.py:223
  38.8 1.1 %constant_dynamic-update-slice_fusion.2 = bf16[4096,128]{1,0:T(8,128)(2,1)} fusion(bf16[4096,128]{1,0:T(8,128)(2,1)} %constant_dynamic-update-slice_fusion.3, bf16[1,128,128]{2,1,0:T(8,128)(2,1)S(1)} %copy-done.6, bf16[80,640]{1,0:T(8,128)(2,1)S(1)} %collective-permute-done.15, bf16[128,640]{1,0:T(8,128)(2,1)S(1)} %convolution_convert_fusion.25, ...), kind=kOutput, calls=%fused_computation.164 | convolution fusion | flops 64225280 | bytes 528384 | tf_op jit(solution)/shard_map/ct,cp->tp/dot_general | solution.py:233
  40.1 1.9 %collective-permute-done.14 = bf16[88,896]{1,0:T(8,128)(2,1)S(1)} collective-permute-done((bf16[88,896]{1,0:T(8,128)(2,1)S(1)}, bf16[88,896]{1,0:T(8,128)(2,1)S(1)}, u32[]{:S(2)}, u32[]{:S(2)}) %collective-permute-start.14) | collective-permute-done | bytes 157728 | tf_op jit(solution)/shard_map/ppermute | solution.py:34
  42.4 1.2 %constant_dynamic-update-slice_fusion.1 = bf16[4096,128]{1,0:T(8,128)(2,1)} fusion(bf16[4096,128]{1,0:T(8,128)(2,1)} %constant_dynamic-update-slice_fusion.2, bf16[1,128,128]{2,1,0:T(8,128)(2,1)S(1)} %copy-done.6, bf16[80,1152]{1,0:T(8,128)(2,1)S(1)} %collective-permute-done.12, bf16[128,1152]{1,0:T(8,128)(2,1)S(1)} %copy-done.7, ...), kind=kOutput, calls=%fused_computation.163 | convolution fusion | flops 115605504 | bytes 872448 | tf_op jit(solution)/shard_map/ct,cp->tp/dot_general | solution.py:233
  43.6 0.5 %slice.182 = bf16[1,1]{1,0:T(2,128)(2,1)} slice(bf16[8,64]{1,0:T(8,128)(2,1)S(1)} %max.11), slice={[0:1], [0:1]} | slice | bytes 4 | tf_op jit(solution)/shard_map/slice | solution.py:338
  45.0 4.3 %collective-permute-done.17 = bf16[80,1152]{1,0:T(8,128)(2,1)S(1)} collective-permute-done((bf16[80,1152]{1,0:T(8,128)(2,1)S(1)}, bf16[80,1152]{1,0:T(8,128)(2,1)S(1)}, u32[]{:S(2)}, u32[]{:S(2)}) %collective-permute-start.17) | collective-permute-done | bytes 184352 | tf_op jit(solution)/shard_map/ppermute | solution.py:34
  49.3 1.2 %constant_dynamic-update-slice_fusion = bf16[4096,128]{1,0:T(8,128)(2,1)} fusion(bf16[4096,128]{1,0:T(8,128)(2,1)} %constant_dynamic-update-slice_fusion.1, bf16[1,128,128]{2,1,0:T(8,128)(2,1)S(1)} %copy-done.6, bf16[80,1152]{1,0:T(8,128)(2,1)S(1)} %collective-permute-done.17, bf16[128,1152]{1,0:T(8,128)(2,1)S(1)} %copy-done.8, ...), kind=kOutput, calls=%fused_computation.162 | convolution fusion | flops 115605504 | bytes 872448 | tf_op jit(solution)/shard_map/ct,cp->tp/dot_general | solution.py:233
  50.5 0.6 %collective-permute-done.18 = bf16[80,896]{1,0:T(8,128)(2,1)S(1)} collective-permute-done((bf16[80,896]{1,0:T(8,128)(2,1)S(1)}, bf16[80,896]{1,0:T(8,128)(2,1)S(1)}, u32[]{:S(2)}, u32[]{:S(2)}) %collective-permute-start.18) | collective-permute-done | bytes 143392 | tf_op jit(solution)/shard_map/ppermute | solution.py:34
  51.1 1.1 %fusion.20 = bf16[4096,128]{1,0:T(8,128)(2,1)} fusion(bf16[4096,128]{1,0:T(8,128)(2,1)} %constant_dynamic-update-slice_fusion, bf16[80,896]{1,0:T(8,128)(2,1)S(1)} %collective-permute-done.18, bf16[128,896]{1,0:T(8,128)(2,1)S(1)} %convolution_convert_fusion.21, bf16[2,128,256]{2,1,0:T(8,128)(2,1)S(1)} %get-tuple-element.78, ...), kind=kOutput, calls=%fused_computation.45 | convolution fusion | flops 89915392 | bytes 700416 | tf_op jit(solution)/shard_map/ct,cp->tp/dot_general | solution.py:233
  (64 shorter events, 5.0 us)
Async XLA Ops:
  0.0 4.6 %copy-start = (bf16[4096,128]{1,0:T(8,128)(2,1)S(1)}, bf16[4096,128]{1,0:T(8,128)(2,1)}, u32[]{:S(2)}) copy-start(bf16[4096,128]{1,0:T(8,128)(2,1)} %refs_1_.2) | copy-start | bytes 3145732
  0.0 4.6 %copy-start.2 = (bf16[1,128,128]{2,1,0:T(8,128)(2,1)S(1)}, bf16[1,128,128]{2,1,0:T(8,128)(2,1)}, u32[]{:S(2)}) copy-start(bf16[1,128,128]{2,1,0:T(8,128)(2,1)} %refs_0_.1) | copy-start | bytes 98308
  0.0 6.8 %copy-start.5 = (s32[1,3,64]{2,0,1:T(1,128)S(1)}, s32[1,3,64]{2,0,1:T(1,128)}, u32[]{:S(2)}) copy-start(s32[1,3,64]{2,0,1:T(1,128)} %param.9) | copy-start | bytes 2308
  0.0 6.8 %copy-start.4 = (bf16[1,3,64,128]{3,2,1,0:T(8,128)(2,1)S(1)}, bf16[1,3,64,128]{3,2,1,0:T(8,128)(2,1)}, u32[]{:S(2)}) copy-start(bf16[1,3,64,128]{3,2,1,0:T(8,128)(2,1)} %refs_1_.3) | copy-start | bytes 147460
  1.5 6.5 %collective-permute-start.3 = (bf16[128,256]{1,0:T(8,128)(2,1)S(1)}, bf16[128,256]{1,0:T(8,128)(2,1)S(1)}, u32[]{:S(2)}, u32[]{:S(2)}) collective-permute-start(bf16[128,256]{1,0:T(8,128)(2,1)S(1)} %get-tuple-element.64), channel_id=1, source_target_pairs={{0,2},{2,0},{1,3},{3,1},{4,6},{6,4},{5,7},{7,5},{8,10},{10,8},{9,1... | collective-permute-start | bytes 196616 | tf_op jit(solution)/shard_map/ppermute | solution.py:34
  4.5 7.1 %collective-permute-start.5 = (bf16[128,640]{1,0:T(8,128)(2,1)S(1)}, bf16[128,640]{1,0:T(8,128)(2,1)S(1)}, u32[]{:S(2)}, u32[]{:S(2)}) collective-permute-start(bf16[128,640]{1,0:T(8,128)(2,1)S(1)} %get-tuple-element.68), channel_id=1, source_target_pairs={{0,2},{2,0},{1,3},{3,1},{4,6},{6,4},{5,7},{7,5},{8,10},{10,8},{9,1... | collective-permute-start | bytes 491528 | tf_op jit(solution)/shard_map/ppermute | solution.py:34
  4.8 13.7 %collective-permute-start.7 = (bf16[128,1152]{1,0:T(8,128)(2,1)S(1)}, bf16[128,1152]{1,0:T(8,128)(2,1)S(1)}, u32[]{:S(2)}, u32[]{:S(2)}) collective-permute-start(bf16[128,1152]{1,0:T(8,128)(2,1)S(1)} %convolution_convert_fusion.14), channel_id=1, source_target_pairs={{0,2},{2,0},{1,3},{3,1},{4,6},{6,4},{5,7},{7,5},{8,10},{10,8},{9,1... | collective-permute-start | bytes 884744 | tf_op jit(solution)/shard_map/ppermute | solution.py:34
  8.2 5.6 %collective-permute-start.4 = (bf16[128,384]{1,0:T(8,128)(2,1)S(1)}, bf16[128,384]{1,0:T(8,128)(2,1)S(1)}, u32[]{:S(2)}, u32[]{:S(2)}) collective-permute-start(bf16[128,384]{1,0:T(8,128)(2,1)S(1)} %pad_maximum_fusion.12), channel_id=1, source_target_pairs={{0,4},{4,0},{8,12},{12,8},{1,5},{5,1},{9,13},{13,9},{2,6},{6,2},{1... | collective-permute-start | bytes 294920 | tf_op jit(solution)/shard_map/ppermute | solution.py:34
  11.8 9.4 %collective-permute-start.8 = (bf16[128,640]{1,0:T(8,128)(2,1)S(1)}, bf16[128,640]{1,0:T(8,128)(2,1)S(1)}, u32[]{:S(2)}, u32[]{:S(2)}) collective-permute-start(bf16[128,640]{1,0:T(8,128)(2,1)S(1)} %convolution_convert_fusion.26), channel_id=1, source_target_pairs={{0,4},{4,0},{8,12},{12,8},{1,5},{5,1},{9,13},{13,9},{2,6},{6,2},{1... | collective-permute-start | bytes 491528 | tf_op jit(solution)/shard_map/ppermute | solution.py:34
  14.2 6.7 %collective-permute-start.6 = (bf16[128,384]{1,0:T(8,128)(2,1)S(1)}, bf16[128,384]{1,0:T(8,128)(2,1)S(1)}, u32[]{:S(2)}, u32[]{:S(2)}) collective-permute-start(bf16[128,384]{1,0:T(8,128)(2,1)S(1)} %pad_maximum_fusion.13), channel_id=1, source_target_pairs={{0,8},{8,0},{4,12},{12,4},{1,9},{9,1},{5,13},{13,5},{2,10},{10,2},... | collective-permute-start | bytes 294920 | tf_op jit(solution)/shard_map/ppermute | solution.py:34
  16.9 7.6 %collective-permute-start.10 = (bf16[128,1152]{1,0:T(8,128)(2,1)S(1)}, bf16[128,1152]{1,0:T(8,128)(2,1)S(1)}, u32[]{:S(2)}, u32[]{:S(2)}) collective-permute-start(bf16[128,1152]{1,0:T(8,128)(2,1)S(1)} %convolution_convert_fusion.13), channel_id=1, source_target_pairs={{0,2},{2,0},{1,3},{3,1},{4,6},{6,4},{5,7},{7,5},{8,10},{10,8},{9,1... | collective-permute-start | bytes 884744 | tf_op jit(solution)/shard_map/ppermute | solution.py:34
  18.7 7.9 %collective-permute-start.9 = (bf16[88,1152]{1,0:T(8,128)(2,1)S(1)}, bf16[88,1152]{1,0:T(8,128)(2,1)S(1)}, u32[]{:S(2)}, u32[]{:S(2)}) collective-permute-start(bf16[88,1152]{1,0:T(8,128)(2,1)S(1)} %convolution_convert_fusion.16), channel_id=1, source_target_pairs={{0,4},{4,0},{8,12},{12,8},{1,5},{5,1},{9,13},{13,9},{2,6},{6,2},{1... | collective-permute-start | bytes 608264 | tf_op jit(solution)/shard_map/ppermute | solution.py:34
  20.9 8.6 %copy-start.3 = (bf16[128,384]{1,0:T(8,128)(2,1)}, bf16[128,384]{1,0:T(8,128)(2,1)S(1)}, u32[]{:S(2)}) copy-start(bf16[128,384]{1,0:T(8,128)(2,1)S(1)} %collective-permute-done.6) | copy-start | bytes 294916
  22.0 16.7 %collective-permute-start.15 = (bf16[80,640]{1,0:T(8,128)(2,1)S(1)}, bf16[80,640]{1,0:T(8,128)(2,1)S(1)}, u32[]{:S(2)}, u32[]{:S(2)}) collective-permute-start(bf16[80,640]{1,0:T(8,128)(2,1)S(1)} %convolution_convert_fusion.30), channel_id=1, source_target_pairs={{0,8},{8,0},{4,12},{12,4},{1,9},{9,1},{5,13},{13,5},{2,10},{10,2},... | collective-permute-start | bytes 307208 | tf_op jit(solution)/shard_map/ppermute | solution.py:34
  24.7 10.9 %collective-permute-start.16 = (bf16[88,1152]{1,0:T(8,128)(2,1)S(1)}, bf16[88,1152]{1,0:T(8,128)(2,1)S(1)}, u32[]{:S(2)}, u32[]{:S(2)}) collective-permute-start(bf16[88,1152]{1,0:T(8,128)(2,1)S(1)} %convolution_convert_fusion.15), channel_id=1, source_target_pairs={{0,4},{4,0},{8,12},{12,8},{1,5},{5,1},{9,13},{13,9},{2,6},{6,2},{1... | collective-permute-start | bytes 608264 | tf_op jit(solution)/shard_map/ppermute | solution.py:34
  26.9 15.5 %collective-permute-start.12 = (bf16[80,1152]{1,0:T(8,128)(2,1)S(1)}, bf16[80,1152]{1,0:T(8,128)(2,1)S(1)}, u32[]{:S(2)}, u32[]{:S(2)}) collective-permute-start(bf16[80,1152]{1,0:T(8,128)(2,1)S(1)} %convolution_convert_fusion.18), channel_id=1, source_target_pairs={{0,8},{8,0},{4,12},{12,4},{1,9},{9,1},{5,13},{13,5},{2,10},{10,2},... | collective-permute-start | bytes 552968 | tf_op jit(solution)/shard_map/ppermute | solution.py:34
  28.4 6.2 %collective-permute-start.13 = (bf16[128,896]{1,0:T(8,128)(2,1)S(1)}, bf16[128,896]{1,0:T(8,128)(2,1)S(1)}, u32[]{:S(2)}, u32[]{:S(2)}) collective-permute-start(bf16[128,896]{1,0:T(8,128)(2,1)S(1)} %convolution_convert_fusion.23), channel_id=1, source_target_pairs={{0,2},{2,0},{1,3},{3,1},{4,6},{6,4},{5,7},{7,5},{8,10},{10,8},{9,1... | collective-permute-start | bytes 688136 | tf_op jit(solution)/shard_map/ppermute | solution.py:34
  29.5 1.9 %slice-start = ((bf16[128,384]{1,0:T(8,128)(2,1)}), bf16[128,256]{1,0:T(8,128)(2,1)S(1)}, s32[]{:S(2)}) async-start(bf16[128,384]{1,0:T(8,128)(2,1)} %copy-done.3), calls=%async_computation | async-start | bytes 131072 | tf_op jit(solution)/shard_map/slice | solution.py:305
  29.5 1.9 %copy-start.6 = (bf16[1,128,128]{2,1,0:T(8,128)(2,1)S(1)}, bf16[1,128,128]{2,1,0:T(8,128)(2,1)}, u32[]{:S(2)}) copy-start(bf16[1,128,128]{2,1,0:T(8,128)(2,1)} %param.11) | copy-start | bytes 98308
  30.5 13.1 %collective-permute-start.11 = (bf16[8,64]{1,0:T(8,128)(2,1)S(1)}, bf16[8,64]{1,0:T(8,128)(2,1)S(1)}, u32[]{:S(2)}, u32[]{:S(2)}) collective-permute-start(bf16[8,64]{1,0:T(8,128)(2,1)S(1)} %slice_maximum_fusion), channel_id=1, source_target_pairs={{0,2},{2,0},{1,3},{3,1},{4,6},{6,4},{5,7},{7,5},{8,10},{10,8},{9,1... | collective-permute-start | bytes 3080 | tf_op jit(solution)/shard_map/ppermute | solution.py:34
  34.9 7.1 %collective-permute-start.14 = (bf16[88,896]{1,0:T(8,128)(2,1)S(1)}, bf16[88,896]{1,0:T(8,128)(2,1)S(1)}, u32[]{:S(2)}, u32[]{:S(2)}) collective-permute-start(bf16[88,896]{1,0:T(8,128)(2,1)S(1)} %convolution_convert_fusion.28), channel_id=1, source_target_pairs={{0,4},{4,0},{8,12},{12,8},{1,5},{5,1},{9,13},{13,9},{2,6},{6,2},{1... | collective-permute-start | bytes 473096 | tf_op jit(solution)/shard_map/ppermute | solution.py:34
  35.9 13.4 %collective-permute-start.17 = (bf16[80,1152]{1,0:T(8,128)(2,1)S(1)}, bf16[80,1152]{1,0:T(8,128)(2,1)S(1)}, u32[]{:S(2)}, u32[]{:S(2)}) collective-permute-start(bf16[80,1152]{1,0:T(8,128)(2,1)S(1)} %convolution_convert_fusion.17), channel_id=1, source_target_pairs={{0,8},{8,0},{4,12},{12,4},{1,9},{9,1},{5,13},{13,5},{2,10},{10,2},... | collective-permute-start | bytes 552968 | tf_op jit(solution)/shard_map/ppermute | solution.py:34
  40.1 2.3 %copy-start.7 = (bf16[128,1152]{1,0:T(8,128)(2,1)S(1)}, bf16[128,1152]{1,0:T(8,128)(2,1)}, u32[]{:S(2)}) copy-start(bf16[128,1152]{1,0:T(8,128)(2,1)} %convolution_convert_fusion.11) | copy-start | bytes 884740
  42.2 8.9 %collective-permute-start.18 = (bf16[80,896]{1,0:T(8,128)(2,1)S(1)}, bf16[80,896]{1,0:T(8,128)(2,1)S(1)}, u32[]{:S(2)}, u32[]{:S(2)}) collective-permute-start(bf16[80,896]{1,0:T(8,128)(2,1)S(1)} %convolution_convert_fusion.29), channel_id=1, source_target_pairs={{0,8},{8,0},{4,12},{12,4},{1,9},{9,1},{5,13},{13,5},{2,10},{10,2},... | collective-permute-start | bytes 430088 | tf_op jit(solution)/shard_map/ppermute | solution.py:34
  43.6 5.7 %copy-start.8 = (bf16[128,1152]{1,0:T(8,128)(2,1)S(1)}, bf16[128,1152]{1,0:T(8,128)(2,1)}, u32[]{:S(2)}) copy-start(bf16[128,1152]{1,0:T(8,128)(2,1)} %convolution_convert_fusion.7) | copy-start | bytes 884740

commit v28 on v27

--- a/solution.py
+++ b/solution.py
@@ -12,6 +12,7 @@
 COUNT_READ = 2
 LOOK = (3, -1)
 MAKE = (0, -1)
+LATE = (1, 2)
 ORDER = (
     (0, 0), (0, 1), (0, 2), (1, 0), (1, 1), MAKE, (2, 0), (0, 3), (1, 2), LOOK, (2, 1), (1, 3), (2, 2),
     (0, 4), (3, 0), (1, 4), (2, 3), (3, 1), (2, 4), (3, 2), (3, 3), (3, 4),
@@ -276,7 +277,7 @@
         return level >= wide and piece >= FULL_PIECES[level - wide]
 
     inputs, partners, theirs, done = {}, {}, {}, [None] * pieces
-    previous, finished, known = None, None, None
+    previous, finished, known, kept = None, None, None, None
     for level, piece in ORDER:
         if (level, piece) == MAKE:
             waiting = after(sampling, previous)
@@ -309,7 +310,10 @@
                 matrix = small[level - 1 - wide]
             if level < levels and compact(level, piece):
                 outgoing = times(compact_rows(matrix, theirs[level]), value)
-                own = times(after(matrix, outgoing), value)
+                if (level, piece) == LATE:
+                    own, kept = None, (matrix, value)
+                else:
+                    own = times(after(matrix, outgoing), value)
             else:
                 own = outgoing = times(matrix, value)
         if level == levels:
@@ -325,6 +329,8 @@
                 block = jnp.where(most_here, jnp.maximum(block, known), block)
             so_far = block
             outgoing = jnp.concatenate([outgoing, block], 1)
+        if kept is not None and own is not None:
+            inputs[LATE[1]], kept = times(after(kept[0], outgoing), kept[1]), None
         inputs[piece] = own
         partners[piece] = from_partner(outgoing, hops[level])
         previous = outgoing

time: 52.4 us -> 54.2 us (1.034)
  matrix products: 12.3 us -> 14 us
    dot_general x17, matrix products: 5.15 us -> 6.86 us  [times(): jnp.dot(matrix, value, preferred_element_type=jnp.float32)]
  transfers between devices with their start and end apart: 16 -> 16, of which waited for: 7 -> 7; matrix products, arithmetic and copies ran while one was open for 23% -> 25% of each run, Pallas kernels for 2% -> 2%
where the time goes in v28:
time: 54.2 us; the launch traced here: 54 us
  starting transfers between devices  23.8 us (44%)
  matrix products  14 us (26%)
  waiting for transfers between devices  12 us (22%)
  Pallas kernels  2.51 us (5%)
  between operations  0.96 us (2%)
  local copies, waits for them, and re-layouts  0.65 us (1%)
    ppermute x16, starting transfers between devices, from_partner(): return lax.ppermute(block, hop[0], route(*hop))  23.8 us
    ppermute x16, waiting for transfers between devices, from_partner(): return lax.ppermute(block, hop[0], route(*hop))  12 us
    dot_general x17, matrix products, times(): jnp.dot(matrix, value, preferred_element_type=jnp.float32)  6.86 us
    dot_general x5, matrix products, evaluated(): jnp.einsum('ct,cp->tp', coeffs, evaluation, preferred_element_type=jnp.fl...  5.62 us
    pallas_call x1, Pallas kernels, early(): pl.pallas_call(lambda *refs: early_kernel(starts, *refs), out_shape=[jax....  1.45 us
  transfers between devices with their start and end apart: 16, of which 7 were waited for; matrix products, arithmetic and copies ran while one was open for 25% of the time, Pallas kernels for 2%

profile of v28, /device:TPU:0, one launch (start us, length us, event | category | flops | bytes accessed | tf_op | source)
XLA Modules:
  0.0 54.0 jit_solution(14330686919847498491)
XLA Ops:
  0.0 1.4 %early.1 = (bf16[128,256]{1,0:T(8,128)(2,1)S(1)}, bf16[128,640]{1,0:T(8,128)(2,1)S(1)}) custom-call(bf16[1,128,128]{2,1,0:T(8,128)(2,1)} %refs_0_.1, bf16[4096,128]{1,0:T(8,128)(2,1)} %refs_1_.2), custom_call_target="tpu_custom_call" | custom-call | flops 29360128 | bytes 458752 | tf_op jit(solution)/shard_map/early/pallas_call | solution.py:71
  1.5 3.0 %collective-permute-start.3 = (bf16[128,256]{1,0:T(8,128)(2,1)S(1)}, bf16[128,256]{1,0:T(8,128)(2,1)S(1)}, u32[]{:S(2)}, u32[]{:S(2)}) collective-permute-start(bf16[128,256]{1,0:T(8,128)(2,1)S(1)} %get-tuple-element.64), channel_id=1, source_target_pairs={{0,2},{2,0},{1,3},{3,1},{4,6},{6,4},{5,7},{7,5},{8,10},{10,8},{9,1... | collective-permute-start | bytes 196616 | tf_op jit(solution)/shard_map/ppermute | solution.py:35
  4.8 2.0 %collective-permute-start.7 = (bf16[128,1152]{1,0:T(8,128)(2,1)S(1)}, bf16[128,1152]{1,0:T(8,128)(2,1)S(1)}, u32[]{:S(2)}, u32[]{:S(2)}) collective-permute-start(bf16[128,1152]{1,0:T(8,128)(2,1)S(1)} %convolution_convert_fusion.14), channel_id=1, source_target_pairs={{0,2},{2,0},{1,3},{3,1},{4,6},{6,4},{5,7},{7,5},{8,10},{10,8},{9,1... | collective-permute-start | bytes 884744 | tf_op jit(solution)/shard_map/ppermute | solution.py:35
  6.8 1.1 %tables.1 = (bf16[3,128,256]{2,1,0:T(8,128)(2,1)S(1)}, bf16[2,128,256]{2,1,0:T(8,128)(2,1)S(1)}, bf16[2,128,128]{2,1,0:T(8,128)(2,1)S(1)}) custom-call(s32[3,1,64]{2,1,0:T(1,128)S(1)} %bitcast.109, bf16[1,3,64,128]{3,2,1,0:T(8,128)(2,1)S(1)} %copy-done.4), custom_call_target="tpu_custom_call" | custom-call | flops 50000000 | bytes 600000 | tf_op jit(solution)/shard_map/tables/pallas_call | solution.py:157
  8.2 1.6 %collective-permute-start.4 = (bf16[128,384]{1,0:T(8,128)(2,1)S(1)}, bf16[128,384]{1,0:T(8,128)(2,1)S(1)}, u32[]{:S(2)}, u32[]{:S(2)}) collective-permute-start(bf16[128,384]{1,0:T(8,128)(2,1)S(1)} %pad_maximum_fusion.12), channel_id=1, source_target_pairs={{0,4},{4,0},{8,12},{12,8},{1,5},{5,1},{9,13},{13,9},{2,6},{6,2},{1... | collective-permute-start | bytes 294920 | tf_op jit(solution)/shard_map/ppermute | solution.py:35
  9.8 1.8 %collective-permute-done.5 = bf16[128,640]{1,0:T(8,128)(2,1)S(1)} collective-permute-done((bf16[128,640]{1,0:T(8,128)(2,1)S(1)}, bf16[128,640]{1,0:T(8,128)(2,1)S(1)}, u32[]{:S(2)}, u32[]{:S(2)}) %collective-permute-start.5) | collective-permute-done | bytes 163872 | tf_op jit(solution)/shard_map/ppermute | solution.py:35
  11.8 1.6 %collective-permute-start.8 = (bf16[128,640]{1,0:T(8,128)(2,1)S(1)}, bf16[128,640]{1,0:T(8,128)(2,1)S(1)}, u32[]{:S(2)}, u32[]{:S(2)}) collective-permute-start(bf16[128,640]{1,0:T(8,128)(2,1)S(1)} %convolution_convert_fusion.26), channel_id=1, source_target_pairs={{0,4},{4,0},{8,12},{12,8},{1,5},{5,1},{9,13},{13,9},{2,6},{6,2},{1... | collective-permute-start | bytes 491528 | tf_op jit(solution)/shard_map/ppermute | solution.py:35
  14.5 2.7 %collective-permute-start.6 = (bf16[128,384]{1,0:T(8,128)(2,1)S(1)}, bf16[128,384]{1,0:T(8,128)(2,1)S(1)}, u32[]{:S(2)}, u32[]{:S(2)}) collective-permute-start(bf16[128,384]{1,0:T(8,128)(2,1)S(1)} %pad_maximum_fusion.13), channel_id=1, source_target_pairs={{0,8},{8,0},{4,12},{12,4},{1,9},{9,1},{5,13},{13,5},{2,10},{10,2},... | collective-permute-start | bytes 294920 | tf_op jit(solution)/shard_map/ppermute | solution.py:35
  17.1 1.4 %collective-permute-start.10 = (bf16[128,1152]{1,0:T(8,128)(2,1)S(1)}, bf16[128,1152]{1,0:T(8,128)(2,1)S(1)}, u32[]{:S(2)}, u32[]{:S(2)}) collective-permute-start(bf16[128,1152]{1,0:T(8,128)(2,1)S(1)} %convolution_convert_fusion.13), channel_id=1, source_target_pairs={{0,2},{2,0},{1,3},{3,1},{4,6},{6,4},{5,7},{7,5},{8,10},{10,8},{9,1... | collective-permute-start | bytes 884744 | tf_op jit(solution)/shard_map/ppermute | solution.py:35
  18.7 1.4 %collective-permute-start.9 = (bf16[88,1152]{1,0:T(8,128)(2,1)S(1)}, bf16[88,1152]{1,0:T(8,128)(2,1)S(1)}, u32[]{:S(2)}, u32[]{:S(2)}) collective-permute-start(bf16[88,1152]{1,0:T(8,128)(2,1)S(1)} %convolution_convert_fusion.16), channel_id=1, source_target_pairs={{0,4},{4,0},{8,12},{12,8},{1,5},{5,1},{9,13},{13,9},{2,6},{6,2},{1... | collective-permute-start | bytes 608264 | tf_op jit(solution)/shard_map/ppermute | solution.py:35
  20.1 1.1 %collective-permute-done.6 = bf16[128,384]{1,0:T(8,128)(2,1)S(1)} collective-permute-done((bf16[128,384]{1,0:T(8,128)(2,1)S(1)}, bf16[128,384]{1,0:T(8,128)(2,1)S(1)}, u32[]{:S(2)}, u32[]{:S(2)}) %collective-permute-start.6) | collective-permute-done | bytes 98336 | tf_op jit(solution)/shard_map/ppermute | solution.py:35
  21.9 2.4 %collective-permute-start.15 = (bf16[80,640]{1,0:T(8,128)(2,1)S(1)}, bf16[80,640]{1,0:T(8,128)(2,1)S(1)}, u32[]{:S(2)}, u32[]{:S(2)}) collective-permute-start(bf16[80,640]{1,0:T(8,128)(2,1)S(1)} %convolution_convert_fusion.30), channel_id=1, source_target_pairs={{0,8},{8,0},{4,12},{12,4},{1,9},{9,1},{5,13},{13,5},{2,10},{10,2},... | collective-permute-start | bytes 307208 | tf_op jit(solution)/shard_map/ppermute | solution.py:35
  25.3 1.0 %convolution_convert_fusion.10 = bf16[128,1152]{1,0:T(8,128)(2,1)} fusion(bf16[128,256]{1,0:T(8,128)(2,1)S(1)} %get-tuple-element.88, bf16[128,1152]{1,0:T(8,128)(2,1)S(1)} %collective-permute-done.10, bf16[128,1152]{1,0:T(8,128)(2,1)S(1)} %convolution_convert_fusion.13), kind=kOutput, calls=%fused_computation.35 | convolution fusion | flops 76824576 | bytes 950272 | tf_op jit(solution)/shard_map/dot_general | solution.py:224
  26.3 0.7 %collective-permute-done.9 = bf16[88,1152]{1,0:T(8,128)(2,1)S(1)} collective-permute-done((bf16[88,1152]{1,0:T(8,128)(2,1)S(1)}, bf16[88,1152]{1,0:T(8,128)(2,1)S(1)}, u32[]{:S(2)}, u32[]{:S(2)}) %collective-permute-start.9) | collective-permute-done | bytes 202784 | tf_op jit(solution)/shard_map/ppermute | solution.py:35
  27.2 1.9 %collective-permute-start.12 = (bf16[80,1152]{1,0:T(8,128)(2,1)S(1)}, bf16[80,1152]{1,0:T(8,128)(2,1)S(1)}, u32[]{:S(2)}, u32[]{:S(2)}) collective-permute-start(bf16[80,1152]{1,0:T(8,128)(2,1)S(1)} %convolution_convert_fusion.18), channel_id=1, source_target_pairs={{0,8},{8,0},{4,12},{12,4},{1,9},{9,1},{5,13},{13,5},{2,10},{10,2},... | collective-permute-start | bytes 552968 | tf_op jit(solution)/shard_map/ppermute | solution.py:35
  29.2 1.1 %collective-permute-start.13 = (bf16[128,896]{1,0:T(8,128)(2,1)S(1)}, bf16[128,896]{1,0:T(8,128)(2,1)S(1)}, u32[]{:S(2)}, u32[]{:S(2)}) collective-permute-start(bf16[128,896]{1,0:T(8,128)(2,1)S(1)} %convolution_convert_fusion.23), channel_id=1, source_target_pairs={{0,2},{2,0},{1,3},{3,1},{4,6},{6,4},{5,7},{7,5},{8,10},{10,8},{9,1... | collective-permute-start | bytes 688136 | tf_op jit(solution)/shard_map/ppermute | solution.py:35
  30.2 1.0 %convolution_convert_fusion.11 = bf16[128,1152]{1,0:T(8,128)(2,1)} fusion(bf16[128,256]{1,0:T(8,128)(2,1)S(1)} %slice_bitcast_fusion.7, bf16[88,1152]{1,0:T(8,128)(2,1)S(1)} %collective-permute-done.9, bf16[128,1152]{1,0:T(8,128)(2,1)S(1)} %convolution_convert_fusion.12), kind=kOutput, calls=%fused_computation.36 | convolution fusion | flops 77709312 | bytes 858112 | tf_op jit(solution)/shard_map/dot_general | solution.py:224
  31.2 1.0 %collective-permute-start.11 = (bf16[8,64]{1,0:T(8,128)(2,1)S(1)}, bf16[8,64]{1,0:T(8,128)(2,1)S(1)}, u32[]{:S(2)}, u32[]{:S(2)}) collective-permute-start(bf16[8,64]{1,0:T(8,128)(2,1)S(1)} %slice_maximum_fusion), channel_id=1, source_target_pairs={{0,2},{2,0},{1,3},{3,1},{4,6},{6,4},{5,7},{7,5},{8,10},{10,8},{9,1... | collective-permute-start | bytes 3080 | tf_op jit(solution)/shard_map/ppermute | solution.py:35
  32.2 1.0 %constant_dynamic-update-slice_fusion.3 = bf16[4096,128]{1,0:T(8,128)(2,1)} fusion(bf16[1,128,128]{2,1,0:T(8,128)(2,1)S(1)} %copy-done.6, bf16[128,256]{1,0:T(8,128)(2,1)S(1)} %slice-done, bf16[128,256]{1,0:T(8,128)(2,1)S(1)} %convolution_convert_fusion.33, bf16[3,128,256]{2,1,0:T(8,128)(2,1)S(1)} %get-tuple-element.67), kind=kOutput, calls=%fused_computation.165 | convolution fusion | flops 25493504 | bytes 294912 | tf_op jit(solution)/shard_map/ct,cp->tp/dot_general | solution.py:234
  33.2 2.2 %collective-permute-done.13 = bf16[128,896]{1,0:T(8,128)(2,1)S(1)} collective-permute-done((bf16[128,896]{1,0:T(8,128)(2,1)S(1)}, bf16[128,896]{1,0:T(8,128)(2,1)S(1)}, u32[]{:S(2)}, u32[]{:S(2)}) %collective-permute-start.13) | collective-permute-done | bytes 229408 | tf_op jit(solution)/shard_map/ppermute | solution.py:35
  35.6 1.0 %collective-permute-start.14 = (bf16[88,896]{1,0:T(8,128)(2,1)S(1)}, bf16[88,896]{1,0:T(8,128)(2,1)S(1)}, u32[]{:S(2)}, u32[]{:S(2)}) collective-permute-start(bf16[88,896]{1,0:T(8,128)(2,1)S(1)} %convolution_convert_fusion.28), channel_id=1, source_target_pairs={{0,4},{4,0},{8,12},{12,8},{1,5},{5,1},{9,13},{13,9},{2,6},{6,2},{1... | collective-permute-start | bytes 473096 | tf_op jit(solution)/shard_map/ppermute | solution.py:35
  36.6 1.2 %convolution_convert_fusion.17 = bf16[80,1152]{1,0:T(8,128)(2,1)S(1)} fusion(bf16[88,1152]{1,0:T(8,128)(2,1)S(1)} %collective-permute-done.16, bf16[128,1152]{1,0:T(8,128)(2,1)} %convolution_convert_fusion.10, bf16[40,256]{1,0:T(8,128)(2,1)S(1)} %convolution_convert_fusion.39, bf16[40,256]{1,0:T(8,128)(2,1)S(1)} %convolution_convert_fusion.40), kind=kOutput, calls=%fused_computation.42 | convolution fusion | flops 49424384 | bytes 722944 | tf_op jit(solution)/shard_map/dot_general | solution.py:224
  37.8 1.2 %collective-permute-start.17 = (bf16[80,1152]{1,0:T(8,128)(2,1)S(1)}, bf16[80,1152]{1,0:T(8,128)(2,1)S(1)}, u32[]{:S(2)}, u32[]{:S(2)}) collective-permute-start(bf16[80,1152]{1,0:T(8,128)(2,1)S(1)} %convolution_convert_fusion.17), channel_id=1, source_target_pairs={{0,8},{8,0},{4,12},{12,4},{1,9},{9,1},{5,13},{13,5},{2,10},{10,2},... | collective-permute-start | bytes 552968 | tf_op jit(solution)/shard_map/ppermute | solution.py:35
  39.0 1.0 %convolution_convert_fusion.7 = bf16[128,1152]{1,0:T(8,128)(2,1)} fusion(bf16[128,256]{1,0:T(8,128)(2,1)S(1)} %slice_bitcast_fusion.7, bf16[88,1152]{1,0:T(8,128)(2,1)S(1)} %collective-permute-done.16, bf16[128,1152]{1,0:T(8,128)(2,1)S(1)} %copy-done.7), kind=kOutput, calls=%fused_computation.32 | convolution fusion | flops 77709312 | bytes 858112 | tf_op jit(solution)/shard_map/dot_general | solution.py:224
  40.0 1.1 %constant_dynamic-update-slice_fusion.2 = bf16[4096,128]{1,0:T(8,128)(2,1)} fusion(bf16[4096,128]{1,0:T(8,128)(2,1)} %constant_dynamic-update-slice_fusion.3, bf16[1,128,128]{2,1,0:T(8,128)(2,1)S(1)} %copy-done.6, bf16[80,640]{1,0:T(8,128)(2,1)S(1)} %collective-permute-done.15, bf16[128,640]{1,0:T(8,128)(2,1)S(1)} %convolution_convert_fusion.25, ...), kind=kOutput, calls=%fused_computation.164 | convolution fusion | flops 64225280 | bytes 528384 | tf_op jit(solution)/shard_map/ct,cp->tp/dot_general | solution.py:234
  41.3 0.9 %collective-permute-done.14 = bf16[88,896]{1,0:T(8,128)(2,1)S(1)} collective-permute-done((bf16[88,896]{1,0:T(8,128)(2,1)S(1)}, bf16[88,896]{1,0:T(8,128)(2,1)S(1)}, u32[]{:S(2)}, u32[]{:S(2)}) %collective-permute-start.14) | collective-permute-done | bytes 157728 | tf_op jit(solution)/shard_map/ppermute | solution.py:35
  42.4 1.3 %collective-permute-start.18 = (bf16[80,896]{1,0:T(8,128)(2,1)S(1)}, bf16[80,896]{1,0:T(8,128)(2,1)S(1)}, u32[]{:S(2)}, u32[]{:S(2)}) collective-permute-start(bf16[80,896]{1,0:T(8,128)(2,1)S(1)} %convolution_convert_fusion.29), channel_id=1, source_target_pairs={{0,8},{8,0},{4,12},{12,4},{1,9},{9,1},{5,13},{13,5},{2,10},{10,2},... | collective-permute-start | bytes 430088 | tf_op jit(solution)/shard_map/ppermute | solution.py:35
  43.7 1.2 %constant_dynamic-update-slice_fusion.1 = bf16[4096,128]{1,0:T(8,128)(2,1)} fusion(bf16[4096,128]{1,0:T(8,128)(2,1)} %constant_dynamic-update-slice_fusion.2, bf16[1,128,128]{2,1,0:T(8,128)(2,1)S(1)} %copy-done.6, bf16[80,1152]{1,0:T(8,128)(2,1)S(1)} %collective-permute-done.12, bf16[128,1152]{1,0:T(8,128)(2,1)S(1)} %copy-done.8, ...), kind=kOutput, calls=%fused_computation.163 | convolution fusion | flops 115605504 | bytes 872448 | tf_op jit(solution)/shard_map/ct,cp->tp/dot_general | solution.py:234
  45.0 0.6 %slice.182 = bf16[1,1]{1,0:T(2,128)(2,1)} slice(bf16[8,64]{1,0:T(8,128)(2,1)S(1)} %max.11), slice={[0:1], [0:1]} | slice | bytes 4 | tf_op jit(solution)/shard_map/slice | solution.py:344
  46.4 4.9 %collective-permute-done.17 = bf16[80,1152]{1,0:T(8,128)(2,1)S(1)} collective-permute-done((bf16[80,1152]{1,0:T(8,128)(2,1)S(1)}, bf16[80,1152]{1,0:T(8,128)(2,1)S(1)}, u32[]{:S(2)}, u32[]{:S(2)}) %collective-permute-start.17) | collective-permute-done | bytes 184352 | tf_op jit(solution)/shard_map/ppermute | solution.py:35
  51.4 1.2 %constant_dynamic-update-slice_fusion = bf16[4096,128]{1,0:T(8,128)(2,1)} fusion(bf16[4096,128]{1,0:T(8,128)(2,1)} %constant_dynamic-update-slice_fusion.1, bf16[1,128,128]{2,1,0:T(8,128)(2,1)S(1)} %copy-done.6, bf16[80,1152]{1,0:T(8,128)(2,1)S(1)} %collective-permute-done.17, bf16[128,1152]{1,0:T(8,128)(2,1)S(1)} %copy-done.9, ...), kind=kOutput, calls=%fused_computation.162 | convolution fusion | flops 115605504 | bytes 872448 | tf_op jit(solution)/shard_map/ct,cp->tp/dot_general | solution.py:234
  52.9 1.1 %fusion.20 = bf16[4096,128]{1,0:T(8,128)(2,1)} fusion(bf16[4096,128]{1,0:T(8,128)(2,1)} %constant_dynamic-update-slice_fusion, bf16[80,896]{1,0:T(8,128)(2,1)S(1)} %collective-permute-done.18, bf16[128,896]{1,0:T(8,128)(2,1)S(1)} %convolution_convert_fusion.21, bf16[2,128,256]{2,1,0:T(8,128)(2,1)S(1)} %get-tuple-element.78, ...), kind=kOutput, calls=%fused_computation.45 | convolution fusion | flops 89915392 | bytes 700416 | tf_op jit(solution)/shard_map/ct,cp->tp/dot_general | solution.py:234
  (66 shorter events, 5.1 us)
Async XLA Ops:
  0.0 4.6 %copy-start = (bf16[4096,128]{1,0:T(8,128)(2,1)S(1)}, bf16[4096,128]{1,0:T(8,128)(2,1)}, u32[]{:S(2)}) copy-start(bf16[4096,128]{1,0:T(8,128)(2,1)} %refs_1_.2) | copy-start | bytes 3145732
  0.0 4.6 %copy-start.2 = (bf16[1,128,128]{2,1,0:T(8,128)(2,1)S(1)}, bf16[1,128,128]{2,1,0:T(8,128)(2,1)}, u32[]{:S(2)}) copy-start(bf16[1,128,128]{2,1,0:T(8,128)(2,1)} %refs_0_.1) | copy-start | bytes 98308
  0.0 6.8 %copy-start.5 = (s32[1,3,64]{2,0,1:T(1,128)S(1)}, s32[1,3,64]{2,0,1:T(1,128)}, u32[]{:S(2)}) copy-start(s32[1,3,64]{2,0,1:T(1,128)} %param.9) | copy-start | bytes 2308
  0.0 6.8 %copy-start.4 = (bf16[1,3,64,128]{3,2,1,0:T(8,128)(2,1)S(1)}, bf16[1,3,64,128]{3,2,1,0:T(8,128)(2,1)}, u32[]{:S(2)}) copy-start(bf16[1,3,64,128]{3,2,1,0:T(8,128)(2,1)} %refs_1_.3) | copy-start | bytes 147460
  1.5 6.5 %collective-permute-start.3 = (bf16[128,256]{1,0:T(8,128)(2,1)S(1)}, bf16[128,256]{1,0:T(8,128)(2,1)S(1)}, u32[]{:S(2)}, u32[]{:S(2)}) collective-permute-start(bf16[128,256]{1,0:T(8,128)(2,1)S(1)} %get-tuple-element.64), channel_id=1, source_target_pairs={{0,2},{2,0},{1,3},{3,1},{4,6},{6,4},{5,7},{7,5},{8,10},{10,8},{9,1... | collective-permute-start | bytes 196616 | tf_op jit(solution)/shard_map/ppermute | solution.py:35
  4.5 7.1 %collective-permute-start.5 = (bf16[128,640]{1,0:T(8,128)(2,1)S(1)}, bf16[128,640]{1,0:T(8,128)(2,1)S(1)}, u32[]{:S(2)}, u32[]{:S(2)}) collective-permute-start(bf16[128,640]{1,0:T(8,128)(2,1)S(1)} %get-tuple-element.68), channel_id=1, source_target_pairs={{0,2},{2,0},{1,3},{3,1},{4,6},{6,4},{5,7},{7,5},{8,10},{10,8},{9,1... | collective-permute-start | bytes 491528 | tf_op jit(solution)/shard_map/ppermute | solution.py:35
  4.8 13.7 %collective-permute-start.7 = (bf16[128,1152]{1,0:T(8,128)(2,1)S(1)}, bf16[128,1152]{1,0:T(8,128)(2,1)S(1)}, u32[]{:S(2)}, u32[]{:S(2)}) collective-permute-start(bf16[128,1152]{1,0:T(8,128)(2,1)S(1)} %convolution_convert_fusion.14), channel_id=1, source_target_pairs={{0,2},{2,0},{1,3},{3,1},{4,6},{6,4},{5,7},{7,5},{8,10},{10,8},{9,1... | collective-permute-start | bytes 884744 | tf_op jit(solution)/shard_map/ppermute | solution.py:35
  8.2 5.8 %collective-permute-start.4 = (bf16[128,384]{1,0:T(8,128)(2,1)S(1)}, bf16[128,384]{1,0:T(8,128)(2,1)S(1)}, u32[]{:S(2)}, u32[]{:S(2)}) collective-permute-start(bf16[128,384]{1,0:T(8,128)(2,1)S(1)} %pad_maximum_fusion.12), channel_id=1, source_target_pairs={{0,4},{4,0},{8,12},{12,8},{1,5},{5,1},{9,13},{13,9},{2,6},{6,2},{1... | collective-permute-start | bytes 294920 | tf_op jit(solution)/shard_map/ppermute | solution.py:35
  11.8 9.4 %collective-permute-start.8 = (bf16[128,640]{1,0:T(8,128)(2,1)S(1)}, bf16[128,640]{1,0:T(8,128)(2,1)S(1)}, u32[]{:S(2)}, u32[]{:S(2)}) collective-permute-start(bf16[128,640]{1,0:T(8,128)(2,1)S(1)} %convolution_convert_fusion.26), channel_id=1, source_target_pairs={{0,4},{4,0},{8,12},{12,8},{1,5},{5,1},{9,13},{13,9},{2,6},{6,2},{1... | collective-permute-start | bytes 491528 | tf_op jit(solution)/shard_map/ppermute | solution.py:35
  14.5 6.7 %collective-permute-start.6 = (bf16[128,384]{1,0:T(8,128)(2,1)S(1)}, bf16[128,384]{1,0:T(8,128)(2,1)S(1)}, u32[]{:S(2)}, u32[]{:S(2)}) collective-permute-start(bf16[128,384]{1,0:T(8,128)(2,1)S(1)} %pad_maximum_fusion.13), channel_id=1, source_target_pairs={{0,8},{8,0},{4,12},{12,4},{1,9},{9,1},{5,13},{13,5},{2,10},{10,2},... | collective-permute-start | bytes 294920 | tf_op jit(solution)/shard_map/ppermute | solution.py:35
  17.1 7.8 %collective-permute-start.10 = (bf16[128,1152]{1,0:T(8,128)(2,1)S(1)}, bf16[128,1152]{1,0:T(8,128)(2,1)S(1)}, u32[]{:S(2)}, u32[]{:S(2)}) collective-permute-start(bf16[128,1152]{1,0:T(8,128)(2,1)S(1)} %convolution_convert_fusion.13), channel_id=1, source_target_pairs={{0,2},{2,0},{1,3},{3,1},{4,6},{6,4},{5,7},{7,5},{8,10},{10,8},{9,1... | collective-permute-start | bytes 884744 | tf_op jit(solution)/shard_map/ppermute | solution.py:35
  18.7 8.3 %collective-permute-start.9 = (bf16[88,1152]{1,0:T(8,128)(2,1)S(1)}, bf16[88,1152]{1,0:T(8,128)(2,1)S(1)}, u32[]{:S(2)}, u32[]{:S(2)}) collective-permute-start(bf16[88,1152]{1,0:T(8,128)(2,1)S(1)} %convolution_convert_fusion.16), channel_id=1, source_target_pairs={{0,4},{4,0},{8,12},{12,8},{1,5},{5,1},{9,13},{13,9},{2,6},{6,2},{1... | collective-permute-start | bytes 608264 | tf_op jit(solution)/shard_map/ppermute | solution.py:35
  21.2 9.0 %copy-start.3 = (bf16[128,384]{1,0:T(8,128)(2,1)}, bf16[128,384]{1,0:T(8,128)(2,1)S(1)}, u32[]{:S(2)}) copy-start(bf16[128,384]{1,0:T(8,128)(2,1)S(1)} %collective-permute-done.6) | copy-start | bytes 294916
  21.9 18.1 %collective-permute-start.15 = (bf16[80,640]{1,0:T(8,128)(2,1)S(1)}, bf16[80,640]{1,0:T(8,128)(2,1)S(1)}, u32[]{:S(2)}, u32[]{:S(2)}) collective-permute-start(bf16[80,640]{1,0:T(8,128)(2,1)S(1)} %convolution_convert_fusion.30), channel_id=1, source_target_pairs={{0,8},{8,0},{4,12},{12,4},{1,9},{9,1},{5,13},{13,5},{2,10},{10,2},... | collective-permute-start | bytes 307208 | tf_op jit(solution)/shard_map/ppermute | solution.py:35
  25.1 11.5 %collective-permute-start.16 = (bf16[88,1152]{1,0:T(8,128)(2,1)S(1)}, bf16[88,1152]{1,0:T(8,128)(2,1)S(1)}, u32[]{:S(2)}, u32[]{:S(2)}) collective-permute-start(bf16[88,1152]{1,0:T(8,128)(2,1)S(1)} %convolution_convert_fusion.15), channel_id=1, source_target_pairs={{0,4},{4,0},{8,12},{12,8},{1,5},{5,1},{9,13},{13,9},{2,6},{6,2},{1... | collective-permute-start | bytes 608264 | tf_op jit(solution)/shard_map/ppermute | solution.py:35
  27.2 16.5 %collective-permute-start.12 = (bf16[80,1152]{1,0:T(8,128)(2,1)S(1)}, bf16[80,1152]{1,0:T(8,128)(2,1)S(1)}, u32[]{:S(2)}, u32[]{:S(2)}) collective-permute-start(bf16[80,1152]{1,0:T(8,128)(2,1)S(1)} %convolution_convert_fusion.18), channel_id=1, source_target_pairs={{0,8},{8,0},{4,12},{12,4},{1,9},{9,1},{5,13},{13,5},{2,10},{10,2},... | collective-permute-start | bytes 552968 | tf_op jit(solution)/shard_map/ppermute | solution.py:35
  29.2 6.2 %collective-permute-start.13 = (bf16[128,896]{1,0:T(8,128)(2,1)S(1)}, bf16[128,896]{1,0:T(8,128)(2,1)S(1)}, u32[]{:S(2)}, u32[]{:S(2)}) collective-permute-start(bf16[128,896]{1,0:T(8,128)(2,1)S(1)} %convolution_convert_fusion.23), channel_id=1, source_target_pairs={{0,2},{2,0},{1,3},{3,1},{4,6},{6,4},{5,7},{7,5},{8,10},{10,8},{9,1... | collective-permute-start | bytes 688136 | tf_op jit(solution)/shard_map/ppermute | solution.py:35
  30.2 1.9 %slice-start = ((bf16[128,384]{1,0:T(8,128)(2,1)}), bf16[128,256]{1,0:T(8,128)(2,1)S(1)}, s32[]{:S(2)}) async-start(bf16[128,384]{1,0:T(8,128)(2,1)} %copy-done.3), calls=%async_computation | async-start | bytes 131072 | tf_op jit(solution)/shard_map/slice | solution.py:306
  30.2 1.9 %copy-start.6 = (bf16[1,128,128]{2,1,0:T(8,128)(2,1)S(1)}, bf16[1,128,128]{2,1,0:T(8,128)(2,1)}, u32[]{:S(2)}) copy-start(bf16[1,128,128]{2,1,0:T(8,128)(2,1)} %param.11) | copy-start | bytes 98308
  31.2 13.7 %collective-permute-start.11 = (bf16[8,64]{1,0:T(8,128)(2,1)S(1)}, bf16[8,64]{1,0:T(8,128)(2,1)S(1)}, u32[]{:S(2)}, u32[]{:S(2)}) collective-permute-start(bf16[8,64]{1,0:T(8,128)(2,1)S(1)} %slice_maximum_fusion), channel_id=1, source_target_pairs={{0,2},{2,0},{1,3},{3,1},{4,6},{6,4},{5,7},{7,5},{8,10},{10,8},{9,1... | collective-permute-start | bytes 3080 | tf_op jit(solution)/shard_map/ppermute | solution.py:35
  35.6 3.4 %copy-start.7 = (bf16[128,1152]{1,0:T(8,128)(2,1)S(1)}, bf16[128,1152]{1,0:T(8,128)(2,1)}, u32[]{:S(2)}) copy-start(bf16[128,1152]{1,0:T(8,128)(2,1)} %convolution_convert_fusion.10) | copy-start | bytes 884740
  35.6 6.6 %collective-permute-start.14 = (bf16[88,896]{1,0:T(8,128)(2,1)S(1)}, bf16[88,896]{1,0:T(8,128)(2,1)S(1)}, u32[]{:S(2)}, u32[]{:S(2)}) collective-permute-start(bf16[88,896]{1,0:T(8,128)(2,1)S(1)} %convolution_convert_fusion.28), channel_id=1, source_target_pairs={{0,4},{4,0},{8,12},{12,8},{1,5},{5,1},{9,13},{13,9},{2,6},{6,2},{1... | collective-permute-start | bytes 473096 | tf_op jit(solution)/shard_map/ppermute | solution.py:35
  37.8 13.5 %collective-permute-start.17 = (bf16[80,1152]{1,0:T(8,128)(2,1)S(1)}, bf16[80,1152]{1,0:T(8,128)(2,1)S(1)}, u32[]{:S(2)}, u32[]{:S(2)}) collective-permute-start(bf16[80,1152]{1,0:T(8,128)(2,1)S(1)} %convolution_convert_fusion.17), channel_id=1, source_target_pairs={{0,8},{8,0},{4,12},{12,4},{1,9},{9,1},{5,13},{13,5},{2,10},{10,2},... | collective-permute-start | bytes 552968 | tf_op jit(solution)/shard_map/ppermute | solution.py:35
  41.3 2.4 %copy-start.8 = (bf16[128,1152]{1,0:T(8,128)(2,1)S(1)}, bf16[128,1152]{1,0:T(8,128)(2,1)}, u32[]{:S(2)}) copy-start(bf16[128,1152]{1,0:T(8,128)(2,1)} %convolution_convert_fusion.11) | copy-start | bytes 884740
  42.4 10.5 %collective-permute-start.18 = (bf16[80,896]{1,0:T(8,128)(2,1)S(1)}, bf16[80,896]{1,0:T(8,128)(2,1)S(1)}, u32[]{:S(2)}, u32[]{:S(2)}) collective-permute-start(bf16[80,896]{1,0:T(8,128)(2,1)S(1)} %convolution_convert_fusion.29), channel_id=1, source_target_pairs={{0,8},{8,0},{4,12},{12,4},{1,9},{9,1},{5,13},{13,5},{2,10},{10,2},... | collective-permute-start | bytes 430088 | tf_op jit(solution)/shard_map/ppermute | solution.py:35
  44.9 6.4 %copy-start.9 = (bf16[128,1152]{1,0:T(8,128)(2,1)S(1)}, bf16[128,1152]{1,0:T(8,128)(2,1)}, u32[]{:S(2)}) copy-start(bf16[128,1152]{1,0:T(8,128)(2,1)} %convolution_convert_fusion.7) | copy-start | bytes 884740

commit v29 on v27

--- a/solution.py
+++ b/solution.py
@@ -5,7 +5,7 @@
 from jax.experimental.pallas import tpu as pltpu
 from jax.sharding import PartitionSpec as P
 
-SHARES = (2, 5, 9, 9, 7)
+SHARES = (2, 5, 8, 10, 7)
 FULL_PIECES = (2, 1)
 EARLY_PIECES = 2
 COUNT_PIECE = 2

time: 52.4 us -> 54 us (1.031)
  waiting for transfers between devices: 12.5 us -> 10 us
  starting transfers between devices: 23.3 us -> 25.7 us
  matrix products: 12.3 us -> 13.9 us
    ppermute x16, waiting for transfers between devices: 12.5 us -> 10 us  [from_partner(): return lax.ppermute(block, hop[0], route(*hop))]
    ppermute x16, starting transfers between devices: 23.3 us -> 25.7 us  [from_partner(): return lax.ppermute(block, hop[0], route(*hop))]
    dot_general x17, matrix products: 5.15 us -> 6.77 us  [times(): jnp.dot(matrix, value, preferred_element_type=jnp.float32)]
  transfers between devices with their start and end apart: 16 -> 16, of which waited for: 7 -> 6; matrix products, arithmetic and copies ran while one was open for 23% -> 25% of each run, Pallas kernels for 2% -> 2%
where the time goes in v29:
time: 54 us; the launch traced here: 53.8 us
  starting transfers between devices  25.7 us (48%)
  matrix products  13.9 us (26%)
  waiting for transfers between devices  10 us (19%)
  Pallas kernels  2.51 us (5%)
  between operations  0.94 us (2%)
  local copies, waits for them, and re-layouts  0.62 us (1%)
    ppermute x16, starting transfers between devices, from_partner(): return lax.ppermute(block, hop[0], route(*hop))  25.7 us
    ppermute x16, waiting for transfers between devices, from_partner(): return lax.ppermute(block, hop[0], route(*hop))  10 us
    dot_general x17, matrix products, times(): jnp.dot(matrix, value, preferred_element_type=jnp.float32)  6.77 us
    dot_general x5, matrix products, evaluated(): jnp.einsum('ct,cp->tp', coeffs, evaluation, preferred_element_type=jnp.fl...  5.64 us
    pallas_call x1, Pallas kernels, early(): pl.pallas_call(lambda *refs: early_kernel(starts, *refs), out_shape=[jax....  1.45 us
  transfers between devices with their start and end apart: 16, of which 6 were waited for; matrix products, arithmetic and copies ran while one was open for 25% of the time, Pallas kernels for 2%

profile of v29, /device:TPU:0, one launch (start us, length us, event | category | flops | bytes accessed | tf_op | source)
XLA Modules:
  0.0 53.8 jit_solution(10108611228395760880)
XLA Ops:
  0.0 1.4 %early.1 = (bf16[128,256]{1,0:T(8,128)(2,1)S(1)}, bf16[128,640]{1,0:T(8,128)(2,1)S(1)}) custom-call(bf16[1,128,128]{2,1,0:T(8,128)(2,1)} %refs_0_.1, bf16[4096,128]{1,0:T(8,128)(2,1)} %refs_1_.2), custom_call_target="tpu_custom_call" | custom-call | flops 29360128 | bytes 458752 | tf_op jit(solution)/shard_map/early/pallas_call | solution.py:70
  1.5 3.0 %collective-permute-start.3 = (bf16[128,256]{1,0:T(8,128)(2,1)S(1)}, bf16[128,256]{1,0:T(8,128)(2,1)S(1)}, u32[]{:S(2)}, u32[]{:S(2)}) collective-permute-start(bf16[128,256]{1,0:T(8,128)(2,1)S(1)} %get-tuple-element.64), channel_id=1, source_target_pairs={{0,2},{2,0},{1,3},{3,1},{4,6},{6,4},{5,7},{7,5},{8,10},{10,8},{9,1... | collective-permute-start | bytes 196616 | tf_op jit(solution)/shard_map/ppermute | solution.py:34
  4.8 2.0 %collective-permute-start.7 = (bf16[128,1024]{1,0:T(8,128)(2,1)S(1)}, bf16[128,1024]{1,0:T(8,128)(2,1)S(1)}, u32[]{:S(2)}, u32[]{:S(2)}) collective-permute-start(bf16[128,1024]{1,0:T(8,128)(2,1)S(1)} %convolution_convert_fusion.16), channel_id=1, source_target_pairs={{0,2},{2,0},{1,3},{3,1},{4,6},{6,4},{5,7},{7,5},{8,10},{10,8},{9,1... | collective-permute-start | bytes 786440 | tf_op jit(solution)/shard_map/ppermute | solution.py:34
  6.8 1.1 %tables.1 = (bf16[3,128,256]{2,1,0:T(8,128)(2,1)S(1)}, bf16[2,128,256]{2,1,0:T(8,128)(2,1)S(1)}, bf16[2,128,128]{2,1,0:T(8,128)(2,1)S(1)}) custom-call(s32[3,1,64]{2,1,0:T(1,128)S(1)} %bitcast.109, bf16[1,3,64,128]{3,2,1,0:T(8,128)(2,1)S(1)} %copy-done.4), custom_call_target="tpu_custom_call" | custom-call | flops 50000000 | bytes 600000 | tf_op jit(solution)/shard_map/tables/pallas_call | solution.py:156
  8.2 1.6 %collective-permute-start.4 = (bf16[128,384]{1,0:T(8,128)(2,1)S(1)}, bf16[128,384]{1,0:T(8,128)(2,1)S(1)}, u32[]{:S(2)}, u32[]{:S(2)}) collective-permute-start(bf16[128,384]{1,0:T(8,128)(2,1)S(1)} %pad_maximum_fusion.12), channel_id=1, source_target_pairs={{0,4},{4,0},{8,12},{12,8},{1,5},{5,1},{9,13},{13,9},{2,6},{6,2},{1... | collective-permute-start | bytes 294920 | tf_op jit(solution)/shard_map/ppermute | solution.py:34
  9.8 1.8 %collective-permute-done.5 = bf16[128,640]{1,0:T(8,128)(2,1)S(1)} collective-permute-done((bf16[128,640]{1,0:T(8,128)(2,1)S(1)}, bf16[128,640]{1,0:T(8,128)(2,1)S(1)}, u32[]{:S(2)}, u32[]{:S(2)}) %collective-permute-start.5) | collective-permute-done | bytes 163872 | tf_op jit(solution)/shard_map/ppermute | solution.py:34
  11.8 1.6 %collective-permute-start.8 = (bf16[128,640]{1,0:T(8,128)(2,1)S(1)}, bf16[128,640]{1,0:T(8,128)(2,1)S(1)}, u32[]{:S(2)}, u32[]{:S(2)}) collective-permute-start(bf16[128,640]{1,0:T(8,128)(2,1)S(1)} %convolution_convert_fusion.26), channel_id=1, source_target_pairs={{0,4},{4,0},{8,12},{12,8},{1,5},{5,1},{9,13},{13,9},{2,6},{6,2},{1... | collective-permute-start | bytes 491528 | tf_op jit(solution)/shard_map/ppermute | solution.py:34
  14.2 2.7 %collective-permute-start.6 = (bf16[128,384]{1,0:T(8,128)(2,1)S(1)}, bf16[128,384]{1,0:T(8,128)(2,1)S(1)}, u32[]{:S(2)}, u32[]{:S(2)}) collective-permute-start(bf16[128,384]{1,0:T(8,128)(2,1)S(1)} %pad_maximum_fusion.13), channel_id=1, source_target_pairs={{0,8},{8,0},{4,12},{12,4},{1,9},{9,1},{5,13},{13,5},{2,10},{10,2},... | collective-permute-start | bytes 294920 | tf_op jit(solution)/shard_map/ppermute | solution.py:34
  16.9 1.4 %collective-permute-start.10 = (bf16[128,1280]{1,0:T(8,128)(2,1)S(1)}, bf16[128,1280]{1,0:T(8,128)(2,1)S(1)}, u32[]{:S(2)}, u32[]{:S(2)}) collective-permute-start(bf16[128,1280]{1,0:T(8,128)(2,1)S(1)} %convolution_convert_fusion.9), channel_id=1, source_target_pairs={{0,2},{2,0},{1,3},{3,1},{4,6},{6,4},{5,7},{7,5},{8,10},{10,8},{9,1... | collective-permute-start | bytes 983048 | tf_op jit(solution)/shard_map/ppermute | solution.py:34
  18.7 1.6 %collective-permute-start.9 = (bf16[88,1024]{1,0:T(8,128)(2,1)S(1)}, bf16[88,1024]{1,0:T(8,128)(2,1)S(1)}, u32[]{:S(2)}, u32[]{:S(2)}) collective-permute-start(bf16[88,1024]{1,0:T(8,128)(2,1)S(1)} %convolution_convert_fusion.22), channel_id=1, source_target_pairs={{0,4},{4,0},{8,12},{12,8},{1,5},{5,1},{9,13},{13,9},{2,6},{6,2},{1... | collective-permute-start | bytes 540680 | tf_op jit(solution)/shard_map/ppermute | solution.py:34
  20.3 0.6 %collective-permute-done.6 = bf16[128,384]{1,0:T(8,128)(2,1)S(1)} collective-permute-done((bf16[128,384]{1,0:T(8,128)(2,1)S(1)}, bf16[128,384]{1,0:T(8,128)(2,1)S(1)}, u32[]{:S(2)}, u32[]{:S(2)}) %collective-permute-start.6) | collective-permute-done | bytes 98336 | tf_op jit(solution)/shard_map/ppermute | solution.py:34
  22.0 2.5 %collective-permute-start.15 = (bf16[80,640]{1,0:T(8,128)(2,1)S(1)}, bf16[80,640]{1,0:T(8,128)(2,1)S(1)}, u32[]{:S(2)}, u32[]{:S(2)}) collective-permute-start(bf16[80,640]{1,0:T(8,128)(2,1)S(1)} %convolution_convert_fusion.30), channel_id=1, source_target_pairs={{0,8},{8,0},{4,12},{12,4},{1,9},{9,1},{5,13},{13,5},{2,10},{10,2},... | collective-permute-start | bytes 307208 | tf_op jit(solution)/shard_map/ppermute | solution.py:34
  25.3 1.0 %convolution_convert_fusion.8 = bf16[128,1280]{1,0:T(8,128)(2,1)} fusion(bf16[128,256]{1,0:T(8,128)(2,1)S(1)} %get-tuple-element.88, bf16[128,1280]{1,0:T(8,128)(2,1)S(1)} %collective-permute-done.10, bf16[128,1280]{1,0:T(8,128)(2,1)S(1)} %convolution_convert_fusion.9), kind=kOutput, calls=%fused_computation.33 | convolution fusion | flops 85360640 | bytes 1048576 | tf_op jit(solution)/shard_map/dot_general | solution.py:223
  26.5 2.6 %collective-permute-start.12 = (bf16[80,1024]{1,0:T(8,128)(2,1)S(1)}, bf16[80,1024]{1,0:T(8,128)(2,1)S(1)}, u32[]{:S(2)}, u32[]{:S(2)}) collective-permute-start(bf16[80,1024]{1,0:T(8,128)(2,1)S(1)} %convolution_convert_fusion.25), channel_id=1, source_target_pairs={{0,8},{8,0},{4,12},{12,4},{1,9},{9,1},{5,13},{13,5},{2,10},{10,2},... | collective-permute-start | bytes 491528 | tf_op jit(solution)/shard_map/ppermute | solution.py:34
  29.1 1.1 %collective-permute-start.13 = (bf16[128,896]{1,0:T(8,128)(2,1)S(1)}, bf16[128,896]{1,0:T(8,128)(2,1)S(1)}, u32[]{:S(2)}, u32[]{:S(2)}) collective-permute-start(bf16[128,896]{1,0:T(8,128)(2,1)S(1)} %convolution_convert_fusion.21), channel_id=1, source_target_pairs={{0,2},{2,0},{1,3},{3,1},{4,6},{6,4},{5,7},{7,5},{8,10},{10,8},{9,1... | collective-permute-start | bytes 688136 | tf_op jit(solution)/shard_map/ppermute | solution.py:34
  30.2 0.9 %convolution_convert_fusion.14 = bf16[128,1024]{1,0:T(8,128)(2,1)} fusion(bf16[128,256]{1,0:T(8,128)(2,1)S(1)} %slice_bitcast_fusion.7, bf16[88,1024]{1,0:T(8,128)(2,1)S(1)} %collective-permute-done.9, bf16[128,1024]{1,0:T(8,128)(2,1)S(1)} %convolution_convert_fusion.15), kind=kOutput, calls=%fused_computation.45 | convolution fusion | flops 69074944 | bytes 770048 | tf_op jit(solution)/shard_map/dot_general | solution.py:223
  31.1 1.0 %collective-permute-start.11 = (bf16[8,64]{1,0:T(8,128)(2,1)S(1)}, bf16[8,64]{1,0:T(8,128)(2,1)S(1)}, u32[]{:S(2)}, u32[]{:S(2)}) collective-permute-start(bf16[8,64]{1,0:T(8,128)(2,1)S(1)} %slice_maximum_fusion), channel_id=1, source_target_pairs={{0,2},{2,0},{1,3},{3,1},{4,6},{6,4},{5,7},{7,5},{8,10},{10,8},{9,1... | collective-permute-start | bytes 3080 | tf_op jit(solution)/shard_map/ppermute | solution.py:34
  32.1 1.0 %constant_dynamic-update-slice_fusion.3 = bf16[4096,128]{1,0:T(8,128)(2,1)} fusion(bf16[1,128,128]{2,1,0:T(8,128)(2,1)S(1)} %copy-done.6, bf16[128,256]{1,0:T(8,128)(2,1)S(1)} %slice-done, bf16[128,256]{1,0:T(8,128)(2,1)S(1)} %convolution_convert_fusion.33, bf16[3,128,256]{2,1,0:T(8,128)(2,1)S(1)} %get-tuple-element.67), kind=kOutput, calls=%fused_computation.167 | convolution fusion | flops 25493504 | bytes 294912 | tf_op jit(solution)/shard_map/ct,cp->tp/dot_general | solution.py:233
  33.1 2.1 %collective-permute-done.13 = bf16[128,896]{1,0:T(8,128)(2,1)S(1)} collective-permute-done((bf16[128,896]{1,0:T(8,128)(2,1)S(1)}, bf16[128,896]{1,0:T(8,128)(2,1)S(1)}, u32[]{:S(2)}, u32[]{:S(2)}) %collective-permute-start.13) | collective-permute-done | bytes 229408 | tf_op jit(solution)/shard_map/ppermute | solution.py:34
  35.4 0.5 collective-permute-start.14
  35.9 1.2 %convolution_convert_fusion.11 = bf16[80,1280]{1,0:T(8,128)(2,1)S(1)} fusion(bf16[88,1280]{1,0:T(8,128)(2,1)S(1)} %collective-permute-done.16, bf16[128,1280]{1,0:T(8,128)(2,1)} %convolution_convert_fusion.8, bf16[40,256]{1,0:T(8,128)(2,1)S(1)} %convolution_convert_fusion.39, bf16[40,256]{1,0:T(8,128)(2,1)S(1)} %convolution_convert_fusion.40), kind=kOutput, calls=%fused_computation.36 | convolution fusion | flops 54906880 | bytes 798720 | tf_op jit(solution)/shard_map/dot_general | solution.py:223
  37.1 1.8 %collective-permute-start.17 = (bf16[80,1280]{1,0:T(8,128)(2,1)S(1)}, bf16[80,1280]{1,0:T(8,128)(2,1)S(1)}, u32[]{:S(2)}, u32[]{:S(2)}) collective-permute-start(bf16[80,1280]{1,0:T(8,128)(2,1)S(1)} %convolution_convert_fusion.11), channel_id=1, source_target_pairs={{0,8},{8,0},{4,12},{12,4},{1,9},{9,1},{5,13},{13,5},{2,10},{10,2},... | collective-permute-start | bytes 614408 | tf_op jit(solution)/shard_map/ppermute | solution.py:34
  38.9 1.0 %convolution_convert_fusion.7 = bf16[128,1280]{1,0:T(8,128)(2,1)} fusion(bf16[128,256]{1,0:T(8,128)(2,1)S(1)} %slice_bitcast_fusion.7, bf16[88,1280]{1,0:T(8,128)(2,1)S(1)} %collective-permute-done.16, bf16[128,1280]{1,0:T(8,128)(2,1)S(1)} %copy-done.7), kind=kOutput, calls=%fused_computation.32 | convolution fusion | flops 86343680 | bytes 946176 | tf_op jit(solution)/shard_map/dot_general | solution.py:223
  39.9 1.1 %constant_dynamic-update-slice_fusion.2 = bf16[4096,128]{1,0:T(8,128)(2,1)} fusion(bf16[4096,128]{1,0:T(8,128)(2,1)} %constant_dynamic-update-slice_fusion.3, bf16[1,128,128]{2,1,0:T(8,128)(2,1)S(1)} %copy-done.6, bf16[80,640]{1,0:T(8,128)(2,1)S(1)} %collective-permute-done.15, bf16[128,640]{1,0:T(8,128)(2,1)S(1)} %convolution_convert_fusion.24, ...), kind=kOutput, calls=%fused_computation.166 | convolution fusion | flops 64225280 | bytes 528384 | tf_op jit(solution)/shard_map/ct,cp->tp/dot_general | solution.py:233
  41.2 0.5 collective-permute-done.14
  41.9 1.9 %collective-permute-start.18 = (bf16[80,896]{1,0:T(8,128)(2,1)S(1)}, bf16[80,896]{1,0:T(8,128)(2,1)S(1)}, u32[]{:S(2)}, u32[]{:S(2)}) collective-permute-start(bf16[80,896]{1,0:T(8,128)(2,1)S(1)} %convolution_convert_fusion.29), channel_id=1, source_target_pairs={{0,8},{8,0},{4,12},{12,4},{1,9},{9,1},{5,13},{13,5},{2,10},{10,2},... | collective-permute-start | bytes 430088 | tf_op jit(solution)/shard_map/ppermute | solution.py:34
  43.8 1.2 %constant_dynamic-update-slice_fusion.1 = bf16[4096,128]{1,0:T(8,128)(2,1)} fusion(bf16[4096,128]{1,0:T(8,128)(2,1)} %constant_dynamic-update-slice_fusion.2, bf16[1,128,128]{2,1,0:T(8,128)(2,1)S(1)} %copy-done.6, bf16[80,1024]{1,0:T(8,128)(2,1)S(1)} %collective-permute-done.12, bf16[128,1024]{1,0:T(8,128)(2,1)S(1)} %copy-done.8, ...), kind=kOutput, calls=%fused_computation.165 | convolution fusion | flops 102760448 | bytes 786432 | tf_op jit(solution)/shard_map/ct,cp->tp/dot_general | solution.py:233
  45.0 0.5 %slice.182 = bf16[1,1]{1,0:T(2,128)(2,1)} slice(bf16[8,64]{1,0:T(8,128)(2,1)S(1)} %max.11), slice={[0:1], [0:1]} | slice | bytes 4 | tf_op jit(solution)/shard_map/slice | solution.py:338
  46.4 4.7 %collective-permute-done.17 = bf16[80,1280]{1,0:T(8,128)(2,1)S(1)} collective-permute-done((bf16[80,1280]{1,0:T(8,128)(2,1)S(1)}, bf16[80,1280]{1,0:T(8,128)(2,1)S(1)}, u32[]{:S(2)}, u32[]{:S(2)}) %collective-permute-start.17) | collective-permute-done | bytes 204832 | tf_op jit(solution)/shard_map/ppermute | solution.py:34
  51.2 1.2 %constant_dynamic-update-slice_fusion = bf16[4096,128]{1,0:T(8,128)(2,1)} fusion(bf16[4096,128]{1,0:T(8,128)(2,1)} %constant_dynamic-update-slice_fusion.1, bf16[1,128,128]{2,1,0:T(8,128)(2,1)S(1)} %copy-done.6, bf16[80,1280]{1,0:T(8,128)(2,1)S(1)} %collective-permute-done.17, bf16[128,1280]{1,0:T(8,128)(2,1)S(1)} %copy-done.9, ...), kind=kOutput, calls=%fused_computation.164 | convolution fusion | flops 128450560 | bytes 958464 | tf_op jit(solution)/shard_map/ct,cp->tp/dot_general | solution.py:233
  52.4 0.3 collective-permute-done.18
  52.7 1.1 %fusion.24 = bf16[4096,128]{1,0:T(8,128)(2,1)} fusion(bf16[4096,128]{1,0:T(8,128)(2,1)} %constant_dynamic-update-slice_fusion, bf16[80,896]{1,0:T(8,128)(2,1)S(1)} %collective-permute-done.18, bf16[128,896]{1,0:T(8,128)(2,1)S(1)} %convolution_convert_fusion.19, bf16[2,128,256]{2,1,0:T(8,128)(2,1)S(1)} %get-tuple-element.78, ...), kind=kOutput, calls=%fused_computation.49 | convolution fusion | flops 89915392 | bytes 700416 | tf_op jit(solution)/shard_map/ct,cp->tp/dot_general | solution.py:233
  (66 shorter events, 4.8 us)
Async XLA Ops:
  0.0 4.6 %copy-start = (bf16[4096,128]{1,0:T(8,128)(2,1)S(1)}, bf16[4096,128]{1,0:T(8,128)(2,1)}, u32[]{:S(2)}) copy-start(bf16[4096,128]{1,0:T(8,128)(2,1)} %refs_1_.2) | copy-start | bytes 3145732
  0.0 4.6 %copy-start.2 = (bf16[1,128,128]{2,1,0:T(8,128)(2,1)S(1)}, bf16[1,128,128]{2,1,0:T(8,128)(2,1)}, u32[]{:S(2)}) copy-start(bf16[1,128,128]{2,1,0:T(8,128)(2,1)} %refs_0_.1) | copy-start | bytes 98308
  0.0 6.8 %copy-start.5 = (s32[1,3,64]{2,0,1:T(1,128)S(1)}, s32[1,3,64]{2,0,1:T(1,128)}, u32[]{:S(2)}) copy-start(s32[1,3,64]{2,0,1:T(1,128)} %param.9) | copy-start | bytes 2308
  0.0 6.8 %copy-start.4 = (bf16[1,3,64,128]{3,2,1,0:T(8,128)(2,1)S(1)}, bf16[1,3,64,128]{3,2,1,0:T(8,128)(2,1)}, u32[]{:S(2)}) copy-start(bf16[1,3,64,128]{3,2,1,0:T(8,128)(2,1)} %refs_1_.3) | copy-start | bytes 147460
  1.5 6.5 %collective-permute-start.3 = (bf16[128,256]{1,0:T(8,128)(2,1)S(1)}, bf16[128,256]{1,0:T(8,128)(2,1)S(1)}, u32[]{:S(2)}, u32[]{:S(2)}) collective-permute-start(bf16[128,256]{1,0:T(8,128)(2,1)S(1)} %get-tuple-element.64), channel_id=1, source_target_pairs={{0,2},{2,0},{1,3},{3,1},{4,6},{6,4},{5,7},{7,5},{8,10},{10,8},{9,1... | collective-permute-start | bytes 196616 | tf_op jit(solution)/shard_map/ppermute | solution.py:34
  4.5 7.1 %collective-permute-start.5 = (bf16[128,640]{1,0:T(8,128)(2,1)S(1)}, bf16[128,640]{1,0:T(8,128)(2,1)S(1)}, u32[]{:S(2)}, u32[]{:S(2)}) collective-permute-start(bf16[128,640]{1,0:T(8,128)(2,1)S(1)} %get-tuple-element.68), channel_id=1, source_target_pairs={{0,2},{2,0},{1,3},{3,1},{4,6},{6,4},{5,7},{7,5},{8,10},{10,8},{9,1... | collective-permute-start | bytes 491528 | tf_op jit(solution)/shard_map/ppermute | solution.py:34
  4.8 13.7 %collective-permute-start.7 = (bf16[128,1024]{1,0:T(8,128)(2,1)S(1)}, bf16[128,1024]{1,0:T(8,128)(2,1)S(1)}, u32[]{:S(2)}, u32[]{:S(2)}) collective-permute-start(bf16[128,1024]{1,0:T(8,128)(2,1)S(1)} %convolution_convert_fusion.16), channel_id=1, source_target_pairs={{0,2},{2,0},{1,3},{3,1},{4,6},{6,4},{5,7},{7,5},{8,10},{10,8},{9,1... | collective-permute-start | bytes 786440 | tf_op jit(solution)/shard_map/ppermute | solution.py:34
  8.2 5.6 %collective-permute-start.4 = (bf16[128,384]{1,0:T(8,128)(2,1)S(1)}, bf16[128,384]{1,0:T(8,128)(2,1)S(1)}, u32[]{:S(2)}, u32[]{:S(2)}) collective-permute-start(bf16[128,384]{1,0:T(8,128)(2,1)S(1)} %pad_maximum_fusion.12), channel_id=1, source_target_pairs={{0,4},{4,0},{8,12},{12,8},{1,5},{5,1},{9,13},{13,9},{2,6},{6,2},{1... | collective-permute-start | bytes 294920 | tf_op jit(solution)/shard_map/ppermute | solution.py:34
  11.8 9.4 %collective-permute-start.8 = (bf16[128,640]{1,0:T(8,128)(2,1)S(1)}, bf16[128,640]{1,0:T(8,128)(2,1)S(1)}, u32[]{:S(2)}, u32[]{:S(2)}) collective-permute-start(bf16[128,640]{1,0:T(8,128)(2,1)S(1)} %convolution_convert_fusion.26), channel_id=1, source_target_pairs={{0,4},{4,0},{8,12},{12,8},{1,5},{5,1},{9,13},{13,9},{2,6},{6,2},{1... | collective-permute-start | bytes 491528 | tf_op jit(solution)/shard_map/ppermute | solution.py:34
  14.2 6.7 %collective-permute-start.6 = (bf16[128,384]{1,0:T(8,128)(2,1)S(1)}, bf16[128,384]{1,0:T(8,128)(2,1)S(1)}, u32[]{:S(2)}, u32[]{:S(2)}) collective-permute-start(bf16[128,384]{1,0:T(8,128)(2,1)S(1)} %pad_maximum_fusion.13), channel_id=1, source_target_pairs={{0,8},{8,0},{4,12},{12,4},{1,9},{9,1},{5,13},{13,5},{2,10},{10,2},... | collective-permute-start | bytes 294920 | tf_op jit(solution)/shard_map/ppermute | solution.py:34
  16.9 7.9 %collective-permute-start.10 = (bf16[128,1280]{1,0:T(8,128)(2,1)S(1)}, bf16[128,1280]{1,0:T(8,128)(2,1)S(1)}, u32[]{:S(2)}, u32[]{:S(2)}) collective-permute-start(bf16[128,1280]{1,0:T(8,128)(2,1)S(1)} %convolution_convert_fusion.9), channel_id=1, source_target_pairs={{0,2},{2,0},{1,3},{3,1},{4,6},{6,4},{5,7},{7,5},{8,10},{10,8},{9,1... | collective-permute-start | bytes 983048 | tf_op jit(solution)/shard_map/ppermute | solution.py:34
  18.7 7.6 %collective-permute-start.9 = (bf16[88,1024]{1,0:T(8,128)(2,1)S(1)}, bf16[88,1024]{1,0:T(8,128)(2,1)S(1)}, u32[]{:S(2)}, u32[]{:S(2)}) collective-permute-start(bf16[88,1024]{1,0:T(8,128)(2,1)S(1)} %convolution_convert_fusion.22), channel_id=1, source_target_pairs={{0,4},{4,0},{8,12},{12,8},{1,5},{5,1},{9,13},{13,9},{2,6},{6,2},{1... | collective-permute-start | bytes 540680 | tf_op jit(solution)/shard_map/ppermute | solution.py:34
  21.0 9.2 %copy-start.3 = (bf16[128,384]{1,0:T(8,128)(2,1)}, bf16[128,384]{1,0:T(8,128)(2,1)S(1)}, u32[]{:S(2)}) copy-start(bf16[128,384]{1,0:T(8,128)(2,1)S(1)} %collective-permute-done.6) | copy-start | bytes 294916
  22.0 17.9 %collective-permute-start.15 = (bf16[80,640]{1,0:T(8,128)(2,1)S(1)}, bf16[80,640]{1,0:T(8,128)(2,1)S(1)}, u32[]{:S(2)}, u32[]{:S(2)}) collective-permute-start(bf16[80,640]{1,0:T(8,128)(2,1)S(1)} %convolution_convert_fusion.30), channel_id=1, source_target_pairs={{0,8},{8,0},{4,12},{12,4},{1,9},{9,1},{5,13},{13,5},{2,10},{10,2},... | collective-permute-start | bytes 307208 | tf_op jit(solution)/shard_map/ppermute | solution.py:34
  25.0 10.9 %collective-permute-start.16 = (bf16[88,1280]{1,0:T(8,128)(2,1)S(1)}, bf16[88,1280]{1,0:T(8,128)(2,1)S(1)}, u32[]{:S(2)}, u32[]{:S(2)}) collective-permute-start(bf16[88,1280]{1,0:T(8,128)(2,1)S(1)} %convolution_convert_fusion.10), channel_id=1, source_target_pairs={{0,4},{4,0},{8,12},{12,8},{1,5},{5,1},{9,13},{13,9},{2,6},{6,2},{1... | collective-permute-start | bytes 675848 | tf_op jit(solution)/shard_map/ppermute | solution.py:34
  26.5 17.3 %collective-permute-start.12 = (bf16[80,1024]{1,0:T(8,128)(2,1)S(1)}, bf16[80,1024]{1,0:T(8,128)(2,1)S(1)}, u32[]{:S(2)}, u32[]{:S(2)}) collective-permute-start(bf16[80,1024]{1,0:T(8,128)(2,1)S(1)} %convolution_convert_fusion.25), channel_id=1, source_target_pairs={{0,8},{8,0},{4,12},{12,4},{1,9},{9,1},{5,13},{13,5},{2,10},{10,2},... | collective-permute-start | bytes 491528 | tf_op jit(solution)/shard_map/ppermute | solution.py:34
  29.1 6.0 %collective-permute-start.13 = (bf16[128,896]{1,0:T(8,128)(2,1)S(1)}, bf16[128,896]{1,0:T(8,128)(2,1)S(1)}, u32[]{:S(2)}, u32[]{:S(2)}) collective-permute-start(bf16[128,896]{1,0:T(8,128)(2,1)S(1)} %convolution_convert_fusion.21), channel_id=1, source_target_pairs={{0,2},{2,0},{1,3},{3,1},{4,6},{6,4},{5,7},{7,5},{8,10},{10,8},{9,1... | collective-permute-start | bytes 688136 | tf_op jit(solution)/shard_map/ppermute | solution.py:34
  30.2 1.9 %slice-start = ((bf16[128,384]{1,0:T(8,128)(2,1)}), bf16[128,256]{1,0:T(8,128)(2,1)S(1)}, s32[]{:S(2)}) async-start(bf16[128,384]{1,0:T(8,128)(2,1)} %copy-done.3), calls=%async_computation | async-start | bytes 131072 | tf_op jit(solution)/shard_map/slice | solution.py:305
  30.2 1.9 %copy-start.6 = (bf16[1,128,128]{2,1,0:T(8,128)(2,1)S(1)}, bf16[1,128,128]{2,1,0:T(8,128)(2,1)}, u32[]{:S(2)}) copy-start(bf16[1,128,128]{2,1,0:T(8,128)(2,1)} %param.11) | copy-start | bytes 98308
  31.1 13.9 %collective-permute-start.11 = (bf16[8,64]{1,0:T(8,128)(2,1)S(1)}, bf16[8,64]{1,0:T(8,128)(2,1)S(1)}, u32[]{:S(2)}, u32[]{:S(2)}) collective-permute-start(bf16[8,64]{1,0:T(8,128)(2,1)S(1)} %slice_maximum_fusion), channel_id=1, source_target_pairs={{0,2},{2,0},{1,3},{3,1},{4,6},{6,4},{5,7},{7,5},{8,10},{10,8},{9,1... | collective-permute-start | bytes 3080 | tf_op jit(solution)/shard_map/ppermute | solution.py:34
  35.4 3.5 %copy-start.7 = (bf16[128,1280]{1,0:T(8,128)(2,1)S(1)}, bf16[128,1280]{1,0:T(8,128)(2,1)}, u32[]{:S(2)}) copy-start(bf16[128,1280]{1,0:T(8,128)(2,1)} %convolution_convert_fusion.8) | copy-start | bytes 983044
  35.4 6.3 %collective-permute-start.14 = (bf16[88,896]{1,0:T(8,128)(2,1)S(1)}, bf16[88,896]{1,0:T(8,128)(2,1)S(1)}, u32[]{:S(2)}, u32[]{:S(2)}) collective-permute-start(bf16[88,896]{1,0:T(8,128)(2,1)S(1)} %convolution_convert_fusion.28), channel_id=1, source_target_pairs={{0,4},{4,0},{8,12},{12,8},{1,5},{5,1},{9,13},{13,9},{2,6},{6,2},{1... | collective-permute-start | bytes 473096 | tf_op jit(solution)/shard_map/ppermute | solution.py:34
  37.1 14.0 %collective-permute-start.17 = (bf16[80,1280]{1,0:T(8,128)(2,1)S(1)}, bf16[80,1280]{1,0:T(8,128)(2,1)S(1)}, u32[]{:S(2)}, u32[]{:S(2)}) collective-permute-start(bf16[80,1280]{1,0:T(8,128)(2,1)S(1)} %convolution_convert_fusion.11), channel_id=1, source_target_pairs={{0,8},{8,0},{4,12},{12,4},{1,9},{9,1},{5,13},{13,5},{2,10},{10,2},... | collective-permute-start | bytes 614408 | tf_op jit(solution)/shard_map/ppermute | solution.py:34
  41.2 2.6 %copy-start.8 = (bf16[128,1024]{1,0:T(8,128)(2,1)S(1)}, bf16[128,1024]{1,0:T(8,128)(2,1)}, u32[]{:S(2)}) copy-start(bf16[128,1024]{1,0:T(8,128)(2,1)} %convolution_convert_fusion.14) | copy-start | bytes 786436
  41.9 10.8 %collective-permute-start.18 = (bf16[80,896]{1,0:T(8,128)(2,1)S(1)}, bf16[80,896]{1,0:T(8,128)(2,1)S(1)}, u32[]{:S(2)}, u32[]{:S(2)}) collective-permute-start(bf16[80,896]{1,0:T(8,128)(2,1)S(1)} %convolution_convert_fusion.29), channel_id=1, source_target_pairs={{0,8},{8,0},{4,12},{12,4},{1,9},{9,1},{5,13},{13,5},{2,10},{10,2},... | collective-permute-start | bytes 430088 | tf_op jit(solution)/shard_map/ppermute | solution.py:34
  45.0 6.2 %copy-start.9 = (bf16[128,1280]{1,0:T(8,128)(2,1)S(1)}, bf16[128,1280]{1,0:T(8,128)(2,1)}, u32[]{:S(2)}) copy-start(bf16[128,1280]{1,0:T(8,128)(2,1)} %convolution_convert_fusion.7) | copy-start | bytes 983044
